TPU v7x, 32 devices: a whole 2x2x4 slice. The times are simulated.
32 devices in a mesh: groups: 2 (over y), attn: 4 (over z), expert: 4 (over x, core).
Axes of the slice: x: 2, y: 2, z: 4, core: 2. Of those that a mesh axis runs over, the one named last changes fastest.
Arguments:
- queries: bfloat16 [512, 3072], P(('groups', 'attn', 'expert')), parts along dimension 0, may hold values from -132 to 132
- cached_keys: bfloat16 [512, 96, 512], P(('groups', 'attn', 'expert')), parts along dimension 0, may hold values from -6 to 6
- cached_values: bfloat16 [512, 96, 512], P(('groups', 'attn', 'expert')), parts along dimension 0, may hold values from -6 to 6
- lengths: int32 [512], P(('groups', 'attn', 'expert')), parts along dimension 0, may hold values from 1 to 96, 12288 in all
- routes: int32 [512, 2], P(('groups', 'attn', 'expert')), parts along dimension 0, may hold values from 0 to 3, all different within a row; in each aligned block of 16 rows (0 to 15, 16 to 31, ...) at most 8 rows name the same one
- residual: bfloat16 [512, 3072], P(('groups', 'attn', 'expert')), parts along dimension 0, may hold values from -3 to 3
- norm_gain: float32 [3072], replicated, may hold values from 0.5 to 1.5
- router: bfloat16 [3072, 4], replicated, may hold values from -0.109375 to 0.109375
- gate_proj: bfloat16 [4, 3072, 8192], P('expert', None, 'attn'), may hold values from -0.109375 to 0.109375
- up_proj: bfloat16 [4, 3072, 8192], P('expert', None, 'attn'), may hold values from -0.109375 to 0.109375
- down_proj: bfloat16 [4, 8192, 3072], P('expert', 'attn'), may hold values from -0.0625 to 0.0625
Outputs:
- layer_out: bfloat16 [512, 3072], P(('groups', 'attn', 'expert')), parts along dimension 0
There are 2 independent parts, one for each index of `groups`. A program takes and returns all parts, laid end to end along the dimension named above; an argument that names none is the same for every part. Nothing has to cross between parts.
Inputs may be any that keep to these rules, and one draw needn't show every extreme that they name: `routes`: each row names two different experts. Among the 16 rows of one device (aligned blocks of rows, in order) no expert is named by more than 8 rows, a bound that some block reaches. `lengths`: some request has all 96 slots live.
All inputs are finite; a program needn't handle non-finite values. No bound on the sum of `lengths` on one device may be relied on, other than what follows from the above.
Results may differ from a plain program's by a relative error of at most 0.0075.
Values may be sent and summed in bfloat16 or wider, within the bound.
No kernel may reach another device: no remote copies, remote signals or barrier semaphores. Data moves between devices by JAX's collectives and lax.ppermute only.
A program may use at most 128 MiB of HBM per device.

v0:
```python
import jax
import jax.numpy as jnp
from jax import lax
from jax.sharding import PartitionSpec as P

HS = 128
KVH = 4
GROUP = 6
CAP = 8


def attend(queries, cached_keys, cached_values, lengths):
    batch = queries.shape[0]
    window = cached_keys.shape[1]
    grouped = queries.reshape(batch, KVH, GROUP, HS)
    key_heads = cached_keys.reshape(batch, window, KVH, HS)
    value_heads = cached_values.reshape(batch, window, KVH, HS)
    scores = jnp.einsum(
        "rkgd,rtkd->rkgt", grouped, key_heads, preferred_element_type=jnp.float32
    ) * HS ** (-0.5)
    visible = jnp.arange(window, dtype=jnp.int32)[None, :] < lengths[:, None]
    scores = jnp.where(visible[:, None, None, :], scores, -1e30)
    highest = jnp.max(scores, axis=-1, keepdims=True)
    powers = jnp.exp(scores - highest)
    weights = (powers / jnp.sum(powers, axis=-1, keepdims=True)).astype(jnp.bfloat16)
    attended = jnp.einsum(
        "rkgt,rtkd->rkgd", weights, value_heads, preferred_element_type=jnp.float32
    )
    return attended.reshape(batch, KVH * GROUP * HS)


def gating(normed, router, routes):
    logits = jnp.dot(normed, router, preferred_element_type=jnp.float32)
    experts = router.shape[1]
    choose = routes[:, :, None] == jnp.arange(experts, dtype=jnp.int32)[None, None, :]
    picked = jnp.sum(jnp.where(choose, logits[:, None, :], 0.0), axis=-1)
    first = 1.0 / (1.0 + jnp.exp(picked[:, 1] - picked[:, 0]))
    second = 1.0 / (1.0 + jnp.exp(picked[:, 0] - picked[:, 1]))
    return jnp.stack([first, second], axis=1)


def slot_table(routes, experts):
    listed = routes.reshape(-1)
    choose = (listed[:, None] == jnp.arange(experts, dtype=jnp.int32)[None, :]).astype(jnp.int32)
    earlier = jnp.cumsum(choose, axis=0) - choose
    position = jnp.sum(earlier * choose, axis=1)
    target = listed * CAP + position
    return target[None, :] == jnp.arange(experts * CAP, dtype=jnp.int32)[:, None]


def shards(
    queries,
    cached_keys,
    cached_values,
    lengths,
    routes,
    residual,
    norm_gain,
    router,
    gate_proj,
    up_proj,
    down_proj,
):
    batch = queries.shape[0]
    experts = router.shape[1]
    attended = attend(queries, cached_keys, cached_values, lengths)
    stream = residual.astype(jnp.float32) + attended
    scale = lax.rsqrt(jnp.mean(stream * stream, axis=-1, keepdims=True) + 1e-05)
    normed = (stream * scale * norm_gain).astype(jnp.bfloat16)
    gates = gating(normed, router, routes)
    table = slot_table(routes, experts)
    w_gate = gate_proj[0]
    w_up = up_proj[0]
    w_down = down_proj[0]
    columns = lax.axis_size("expert")
    row_table = jnp.any(table.reshape(experts * CAP, batch, 2), axis=-1).astype(jnp.bfloat16)
    outgoing = jnp.dot(row_table, normed, preferred_element_type=jnp.float32).astype(jnp.bfloat16)
    arrived = lax.all_to_all(
        outgoing.reshape(experts, CAP, -1), "expert", split_axis=0, concat_axis=0, tiled=True
    )
    inputs = lax.all_gather(arrived.reshape(columns * CAP, -1), "attn", axis=0, tiled=True)
    gate_part = jnp.einsum("...d,df->...f", inputs, w_gate, preferred_element_type=jnp.float32)
    up_part = jnp.einsum("...d,df->...f", inputs, w_up, preferred_element_type=jnp.float32)
    hidden = (jax.nn.silu(gate_part) * up_part).astype(jnp.bfloat16)
    summed = lax.psum_scatter(
        jnp.dot(hidden, w_down, preferred_element_type=jnp.float32).astype(jnp.bfloat16),
        "attn",
        scatter_dimension=0,
        tiled=True,
    )
    expert_result = summed.reshape(columns, CAP, -1)
    returned = lax.all_to_all(expert_result, "expert", split_axis=0, concat_axis=0, tiled=True)
    picked = jnp.einsum(
        "sa,sd->ad",
        table.astype(jnp.bfloat16),
        returned.reshape(experts * CAP, -1),
        preferred_element_type=jnp.float32,
    )
    picked = picked.reshape(batch, 2, -1)
    return (stream + jnp.sum(gates[:, :, None] * picked, axis=1)).astype(jnp.bfloat16)


def solution(mesh):
    in_specs = (
        P(("groups", "attn", "expert"), None),
        P(("groups", "attn", "expert"), None, None),
        P(("groups", "attn", "expert"), None, None),
        P(("groups", "attn", "expert")),
        P(("groups", "attn", "expert"), None),
        P(("groups", "attn", "expert"), None),
        P(),
        P(),
        P("expert", None, "attn"),
        P("expert", None, "attn"),
        P("expert", "attn", None),
    )
    out_specs = P(("groups", "attn", "expert"), None)
    return jax.shard_map(shards, mesh=mesh, in_specs=in_specs, out_specs=out_specs, check_vma=False)
```

profile of v0, /device:TPU:0, one launch (start us, length us, event | category | flops | bytes accessed | tf_op | source)
XLA Modules:
  0.0 103.0 jit_solution(6750580828384726956)
XLA Ops:
  6.5 0.0 copy-start
  6.5 0.0 reduce-scatter.2.cloned.1.call-start
  6.5 0.8 iota_compare_fusion.3
  7.4 0.8 copy.37
  8.1 0.1 reshape.100
  8.2 0.1 fusion.37
  8.3 0.1 reduce_window_sum.11
  8.4 0.2 select_reduce_fusion
  8.5 0.1 reduce_sum.51
  8.6 0.1 copy.38
  8.7 0.7 multiply_add_fusion
  9.4 0.1 fusion.40
  9.5 1.0 %reshape.96 = bf16[16,4,6,128]{3,2,1,0:T(8,128)(2,1)S(1)} reshape(bf16[16,3072]{1,0:T(8,128)(2,1)} %param.11) | data formatting | bytes 196608 | tf_op jit(solution)/shard_map/reshape | solution.py:15
  10.5 2.3 %fusion.28 = f32[16,4,6,96]{3,2,1,0:T(8,128)S(1)} fusion(bf16[16,4,6,128]{3,2,1,0:T(8,128)(2,1)S(1)} %reshape.96, pred[16,96]{1,0:T(8,128)(4,1)S(1)} %iota_compare_fusion.3, bf16[16,96,512]{2,1,0:T(8,128)(2,1)} %param.12), kind=kOutput, calls=%fused_computation.22 | convolution fusion | flops 9510912 | bytes 1820160 | tf_op jit(solution)/shard_map/rkgd,rtkd->rkgt/dot_general | solution.py:18
  12.8 0.3 fusion.43
  13.1 0.0 copy-done
  13.1 0.0 copy-start.1
  13.1 0.0 copy-start.2
  13.2 0.9 fusion.17
  14.1 0.1 reshape.99
  14.2 0.0 copy-done.1
  14.2 0.1 multiply_reduce_fusion
  14.3 0.0 copy-done.2
  14.3 0.1 multiply_convert_fusion
  14.4 0.2 fusion.10
  14.7 9.4 %all_to_all.10 = bf16[4,8,3072]{2,1,0:T(8,128)(2,1)S(1)} all-to-all(bf16[4,8,3072]{2,1,0:T(8,128)(2,1)S(1)} %fusion.10), channel_id=1, replica_groups=mesh['groups'=2,'attn'=4,'expert'=4] {'expert'}, dimensions={0} | all-to-all | bytes 393216 | tf_op jit(solution)/shard_map/all_to_all | solution.py:78
  24.0 19.8 %all_gather.3 = bf16[128,3072]{1,0:T(8,128)(2,1)S(1)} all-gather(bf16[32,3072]{1,0:T(8,128)(2,1)S(1)} %bitcast.56), channel_id=1, replica_groups=mesh['groups'=2,'attn'=4,'expert'=4] {'attn'}, dimensions={0}, use_global_device_ids=true | all-gather | bytes 983040 | tf_op jit(solution)/shard_map/all_gather | solution.py:81
  43.9 7.4 %fusion.5 = f32[128,2048]{1,0:T(8,128)} fusion(bf16[128,3072]{1,0:T(8,128)(2,1)S(1)} %all_gather.3, bf16[1,3072,2048]{2,1,0:T(8,128)(2,1)} %param.19), kind=kOutput, calls=%fused_computation.5 | convolution fusion | flops 1610612736 | bytes 14417920 | tf_op jit(solution)/shard_map/...d,df->...f/dot_general | solution.py:82
  51.3 0.0 copy-start.4
  51.3 0.0 copy-start.3
  51.3 13.1 %fusion.7 = bf16[128,3072]{1,0:T(8,128)(2,1)} fusion(bf16[1,2048,3072]{2,1,0:T(8,128)(2,1)} %param.21, bf16[128,3072]{1,0:T(8,128)(2,1)S(1)} %all_gather.3, bf16[1,3072,2048]{2,1,0:T(8,128)(2,1)} %param.20, f32[128,2048]{1,0:T(8,128)} %fusion.5), kind=kOutput, calls=%fused_computation.7 | convolution fusion | flops 3223191552 | bytes 27787264 | tf_op jit(solution)/shard_map/dot_general | solution.py:86
  64.4 0.0 reduce-scatter.2.cloned.1.call-update
  64.4 0.0 copy-done.4
  64.4 0.1 fusion.44
  64.6 0.0 copy-done.3
  64.6 21.9 %reduce-scatter.2.cloned.1.call-done = bf16[32,3072]{1,0:T(8,128)(2,1)} async-done(((bf16[128,3072]{1,0:T(8,128)(2,1)}), bf16[32,3072]{1,0:T(8,128)(2,1)}) %reduce-scatter.2.cloned.1.call-update) | async-done | bytes 196624 | tf_op jit(solution)/shard_map/reduce_scatter | solution.py:85
  86.5 3.4 %all-to-all-start.1 = ((bf16[4,8,3072]{2,1,0:T(8,128)(2,1)}), bf16[4,8,3072]{2,1,0:T(8,128)(2,1)S(1)}, u32[]{:S(2)}, u32[]{:S(2)}) async-start(bf16[4,8,3072]{2,1,0:T(8,128)(2,1)} %bitcast.57), calls=%async_computation.2 | async-start | bytes 393216 | tf_op jit(solution)/shard_map/all_to_all | solution.py:92
  89.9 5.3 %all-to-all-done.1 = bf16[4,8,3072]{2,1,0:T(8,128)(2,1)S(1)} async-done(((bf16[4,8,3072]{2,1,0:T(8,128)(2,1)}), bf16[4,8,3072]{2,1,0:T(8,128)(2,1)S(1)}, u32[]{:S(2)}, u32[]{:S(2)}) %all-to-all-start.1) | async-done | bytes 196640 | tf_op jit(solution)/shard_map/all_to_all | solution.py:92
  95.2 0.2 fusion.24
  95.5 0.7 add_convert_fusion
  (4 shorter events, 0.1 us)
Async XLA Ops:
  6.5 6.6 %copy-start = (bf16[16,96,512]{2,1,0:T(8,128)(2,1)S(1)}, bf16[16,96,512]{2,1,0:T(8,128)(2,1)}, u32[]{:S(2)}) copy-start(bf16[16,96,512]{2,1,0:T(8,128)(2,1)} %param.13) | copy-start | bytes 4718596
  6.5 80.0 %reduce-scatter.2.cloned.1.call-start = ((), (), s32[]{:S(2)}) async-start(), calls=%async_computation.3 | async-start | bytes 983040 | tf_op jit(solution)/shard_map/reduce_scatter | solution.py:85
  13.1 1.0 %copy-start.1 = (bf16[16,3072]{1,0:T(8,128)(2,1)S(1)}, bf16[16,3072]{1,0:T(8,128)(2,1)}, u32[]{:S(2)}) copy-start(bf16[16,3072]{1,0:T(8,128)(2,1)} %param.16) | copy-start | bytes 294916
  13.1 1.2 %copy-start.2 = (f32[3072]{0:T(1024)S(1)}, f32[3072]{0:T(1024)}, u32[]{:S(2)}) copy-start(f32[3072]{0:T(1024)} %param.17) | copy-start | bytes 36868
  51.3 13.1 %copy-start.4 = (bf16[3072,4]{0,1:T(4,128)(2,1)S(1)}, bf16[3072,4]{0,1:T(4,128)(2,1)}, u32[]{:S(2)}) copy-start(bf16[3072,4]{0,1:T(4,128)(2,1)} %param.18) | copy-start | bytes 73732
  51.3 13.3 %copy-start.3 = (s32[16,2]{0,1:T(2,128)S(1)}, s32[16,2]{0,1:T(2,128)}, u32[]{:S(2)}) copy-start(s32[16,2]{0,1:T(2,128)} %param.15) | copy-start | bytes 388
  86.5 8.7 %all-to-all-start.1 = ((bf16[4,8,3072]{2,1,0:T(8,128)(2,1)}), bf16[4,8,3072]{2,1,0:T(8,128)(2,1)S(1)}, u32[]{:S(2)}, u32[]{:S(2)}) async-start(bf16[4,8,3072]{2,1,0:T(8,128)(2,1)} %bitcast.57), calls=%async_computation.2 | async-start | bytes 393216 | tf_op jit(solution)/shard_map/all_to_all | solution.py:92
Sparse Core Ops, SparseCore 0:
  64.5 21.9 reduce-scatter.1
where the time goes:
time: 103 us
  blocking collectives  29.2 us (28%)
  waiting for transfers between devices  27.2 us (26%)
  matrix products  24.4 us (24%)
  between operations  13.5 us (13%)
  starting transfers between devices  3.37 us (3%)
  other arithmetic  3.18 us (3%)
  local copies, waits for them, and re-layouts  2.13 us (2%)
    reduce_scatter x1, waiting for transfers between devices, shards(): lax.psum_scatter(jnp.dot(hidden, w_down, preferred_element_type=jnp.float...  21.9 us
    all_gather x1, blocking collectives, shards(): lax.all_gather(arrived.reshape(columns * CAP, -1), 'attn', axis=0, tiled=...  19.8 us
    dot_general x1, matrix products, shards(): jnp.dot(hidden, w_down, preferred_element_type=jnp.float32)  13.1 us
    all_to_all x1, blocking collectives, shards(): lax.all_to_all(outgoing.reshape(experts, CAP, -1), 'expert', split_axis=0...  9.35 us
    dot_general x1, matrix products, shards(): jnp.einsum('...d,df->...f', inputs, w_gate, preferred_element_type=jnp.fl...  7.41 us
    all_to_all x1, waiting for transfers between devices, shards(): lax.all_to_all(expert_result, 'expert', split_axis=0, concat_axis=0, tile...  5.27 us
    all_to_all x1, starting transfers between devices, shards(): lax.all_to_all(expert_result, 'expert', split_axis=0, concat_axis=0, tile...  3.36 us
    dot_general x1, matrix products, attend(): jnp.einsum('rkgd,rtkd->rkgt', grouped, key_heads, preferred_element_type=...  2.31 us
  transfers between devices with their start and end apart: 2, of which 2 were waited for; matrix products, arithmetic and copies ran while one was open for 0% of the time, Pallas kernels for 0%

commit v1 on v0

--- a/solution.py
+++ b/solution.py
@@ -7,6 +7,7 @@
 KVH = 4
 GROUP = 6
 CAP = 8
+LANES = 128
 
 
 def attend(queries, cached_keys, cached_values, lengths):
@@ -39,13 +40,20 @@
     return jnp.stack([first, second], axis=1)
 
 
-def slot_table(routes, experts):
-    listed = routes.reshape(-1)
+def slot_table(named, experts):
+    listed = named.reshape(-1)
     choose = (listed[:, None] == jnp.arange(experts, dtype=jnp.int32)[None, :]).astype(jnp.int32)
     earlier = jnp.cumsum(choose, axis=0) - choose
     position = jnp.sum(earlier * choose, axis=1)
     target = listed * CAP + position
     return target[None, :] == jnp.arange(experts * CAP, dtype=jnp.int32)[:, None]
+
+
+def swap(value, axis, step):
+    if step == 0:
+        return value
+    count = lax.axis_size(axis)
+    return lax.ppermute(value, axis, [(i, i ^ step) for i in range(count)])
 
 
 def shards(
@@ -61,43 +69,65 @@
     up_proj,
     down_proj,
 ):
-    batch = queries.shape[0]
+    batch, width = queries.shape
     experts = router.shape[1]
+    layers = lax.axis_size("attn")
+    columns = lax.axis_size("expert")
+    me = lax.axis_index("expert")
     attended = attend(queries, cached_keys, cached_values, lengths)
     stream = residual.astype(jnp.float32) + attended
     scale = lax.rsqrt(jnp.mean(stream * stream, axis=-1, keepdims=True) + 1e-05)
     normed = (stream * scale * norm_gain).astype(jnp.bfloat16)
-    gates = gating(normed, router, routes)
-    table = slot_table(routes, experts)
-    w_gate = gate_proj[0]
-    w_up = up_proj[0]
-    w_down = down_proj[0]
-    columns = lax.axis_size("expert")
-    row_table = jnp.any(table.reshape(experts * CAP, batch, 2), axis=-1).astype(jnp.bfloat16)
-    outgoing = jnp.dot(row_table, normed, preferred_element_type=jnp.float32).astype(jnp.bfloat16)
-    arrived = lax.all_to_all(
-        outgoing.reshape(experts, CAP, -1), "expert", split_axis=0, concat_axis=0, tiled=True
-    )
-    inputs = lax.all_gather(arrived.reshape(columns * CAP, -1), "attn", axis=0, tiled=True)
-    gate_part = jnp.einsum("...d,df->...f", inputs, w_gate, preferred_element_type=jnp.float32)
-    up_part = jnp.einsum("...d,df->...f", inputs, w_up, preferred_element_type=jnp.float32)
+    named = jnp.pad(routes.astype(jnp.bfloat16), ((0, 0), (0, LANES - 2)))
+    payload = jnp.concatenate([normed, named], axis=1)
+    chunks = [swap(payload, "attn", step) for step in range(layers)]
+    groups = [[0], list(range(1, layers))]
+
+    tables, gates, inputs = [None] * layers, [None] * layers, {}
+    for group in groups:
+        slots = []
+        for j in group:
+            rows = chunks[j][:, :width]
+            owners = chunks[j][:, width : width + 2].astype(jnp.int32)
+            gates[j] = gating(rows, router, owners)
+            tables[j] = slot_table(owners ^ me, experts)
+            row_table = jnp.any(tables[j].reshape(experts * CAP, batch, 2), axis=-1)
+            slots.append(
+                jnp.dot(row_table.astype(jnp.bfloat16), rows, preferred_element_type=jnp.float32)
+                .astype(jnp.bfloat16)
+                .reshape(experts, CAP, width)
+            )
+        slots = jnp.concatenate(slots, axis=1)
+        for step in range(columns):
+            inputs[group[0], step] = swap(slots[step], "expert", step)
+
+    order = [(group, step) for group in groups for step in range(columns)]
+    gathered = jnp.concatenate([inputs[group[0], step] for group, step in order], axis=0)
+    gate_part = jnp.dot(gathered, gate_proj[0], preferred_element_type=jnp.float32)
+    up_part = jnp.dot(gathered, up_proj[0], preferred_element_type=jnp.float32)
     hidden = (jax.nn.silu(gate_part) * up_part).astype(jnp.bfloat16)
-    summed = lax.psum_scatter(
-        jnp.dot(hidden, w_down, preferred_element_type=jnp.float32).astype(jnp.bfloat16),
-        "attn",
-        scatter_dimension=0,
-        tiled=True,
-    )
-    expert_result = summed.reshape(columns, CAP, -1)
-    returned = lax.all_to_all(expert_result, "expert", split_axis=0, concat_axis=0, tiled=True)
-    picked = jnp.einsum(
-        "sa,sd->ad",
-        table.astype(jnp.bfloat16),
-        returned.reshape(experts * CAP, -1),
-        preferred_element_type=jnp.float32,
-    )
-    picked = picked.reshape(batch, 2, -1)
-    return (stream + jnp.sum(gates[:, :, None] * picked, axis=1)).astype(jnp.bfloat16)
+    partial = jnp.dot(hidden, down_proj[0], preferred_element_type=jnp.float32).astype(jnp.bfloat16)
+
+    total = stream
+    at, pieces = 0, {}
+    for group, step in order:
+        count = len(group) * CAP
+        pieces[group[0], step] = partial[at : at + count]
+        at += count
+    for group in groups[::-1]:
+        returned = [swap(pieces[group[0], step], "expert", step) for step in range(columns)]
+        for place, j in list(enumerate(group))[::-1]:
+            mine = jnp.concatenate(
+                [block[place * CAP : (place + 1) * CAP] for block in returned], axis=0
+            )
+            picked = jnp.einsum(
+                "sa,sd->ad", tables[j].astype(jnp.bfloat16), mine, preferred_element_type=jnp.float32
+            ).reshape(batch, 2, width)
+            mixed = jnp.sum(gates[j][:, :, None] * picked, axis=1)
+            if j:
+                mixed = swap(mixed.astype(jnp.bfloat16), "attn", j).astype(jnp.float32)
+            total = total + mixed
+    return total.astype(jnp.bfloat16)
 
 
 def solution(mesh):

time: 103 us -> 85.3 us (0.83)
  blocking collectives: 29.2 us -> 0 us
  starting transfers between devices: 3.37 us -> 19.1 us
  between operations: 13.5 us -> 0.47 us
  other arithmetic: 3.18 us -> 9.9 us
  waiting for transfers between devices: 27.2 us -> 22.6 us
  local copies, waits for them, and re-layouts: 2.13 us -> 6.44 us
  matrix products: 24.4 us -> 26.5 us
    ppermute x0 -> x18, waiting for transfers between devices: none -> 22.6 us  [swap(): return lax.ppermute(value, axis, [(i, i ^ step) for i in range(count)])]
    reduce_scatter x1 -> x0, waiting for transfers between devices: 21.9 us -> none  [shards(): lax.psum_scatter(jnp.dot(hidden, w_down, preferred_element_type=jnp.float...]
    all_gather x1 -> x0, blocking collectives: 19.8 us -> none  [shards(): lax.all_gather(arrived.reshape(columns * CAP, -1), 'attn', axis=0, tiled=...]
    ppermute x0 -> x18, starting transfers between devices: none -> 19.1 us  [swap(): return lax.ppermute(value, axis, [(i, i ^ step) for i in range(count)])]
    all_to_all x1 -> x0, blocking collectives: 9.35 us -> none  [shards(): lax.all_to_all(outgoing.reshape(experts, CAP, -1), 'expert', split_axis=0...]
    all_to_all x1 -> x0, waiting for transfers between devices: 5.27 us -> none  [shards(): lax.all_to_all(expert_result, 'expert', split_axis=0, concat_axis=0, tile...]
    reduce_sum x0 -> x4, other arithmetic: none -> 4.21 us  [shards(): mixed = jnp.sum(gates[j][:, :, None] * picked, axis=1)]
    all_to_all x1 -> x0, starting transfers between devices: 3.36 us -> none  [shards(): lax.all_to_all(expert_result, 'expert', split_axis=0, concat_axis=0, tile...]
  transfers between devices with their start and end apart: 2 -> 18, of which waited for: 2 -> 8; matrix products, arithmetic and copies ran while one was open for 0% -> 13% of each run, Pallas kernels for 0% -> 0%
where the time goes in v1:
time: 85.3 us; the launch traced here: 85 us
  matrix products  26.5 us (31%)
  waiting for transfers between devices  22.6 us (26%)
  starting transfers between devices  19.1 us (22%)
  other arithmetic  9.9 us (12%)
  local copies, waits for them, and re-layouts  6.44 us (8%)
    ppermute x18, waiting for transfers between devices, swap(): return lax.ppermute(value, axis, [(i, i ^ step) for i in range(count)])  22.6 us
    ppermute x18, starting transfers between devices, swap(): return lax.ppermute(value, axis, [(i, i ^ step) for i in range(count)])  19.1 us
    dot_general x1, matrix products, shards(): jnp.dot(hidden, down_proj[0], preferred_element_type=jnp.float32)  12.1 us
    dot_general x1, matrix products, shards(): up_part = jnp.dot(gathered, up_proj[0], preferred_element_type=jnp.float32)  7.37 us
    reduce_sum x4, other arithmetic, shards(): mixed = jnp.sum(gates[j][:, :, None] * picked, axis=1)  4.21 us
    dot_general x1, matrix products, attend(): jnp.einsum('rkgd,rtkd->rkgt', grouped, key_heads, preferred_element_type=...  2.31 us
    dot_general x4, matrix products, shards(): jnp.einsum('sa,sd->ad', tables[j].astype(jnp.bfloat16), mine, preferred_e...  2.24 us
  transfers between devices with their start and end apart: 18, of which 8 were waited for; matrix products, arithmetic and copies ran while one was open for 13% of the time, Pallas kernels for 0%

profile of v1, /device:TPU:0, one launch (start us, length us, event | category | flops | bytes accessed | tf_op | source)
XLA Modules:
  0.0 85.0 jit_solution(12840797756587404030)
XLA Ops:
  0.0 0.8 fusion.94
  0.8 0.7 iota_compare_fusion.17
  1.5 0.1 copy.90
  1.6 1.0 %reshape.164 = bf16[16,4,6,128]{3,2,1,0:T(8,128)(2,1)S(1)} reshape(bf16[16,3072]{1,0:T(8,128)(2,1)} %param.11) | data formatting | bytes 196608 | tf_op jit(solution)/shard_map/reshape | solution.py:16
  2.7 2.3 %fusion.23 = f32[16,4,6,96]{3,2,1,0:T(8,128)S(1)} fusion(bf16[16,4,6,128]{3,2,1,0:T(8,128)(2,1)S(1)} %reshape.164, pred[16,96]{1,0:T(8,128)(4,1)S(1)} %iota_compare_fusion.17, bf16[16,96,512]{2,1,0:T(8,128)(2,1)} %param.12), kind=kOutput, calls=%fused_computation.23 | convolution fusion | flops 9510912 | bytes 1820160 | tf_op jit(solution)/shard_map/rkgd,rtkd->rkgt/dot_general | solution.py:19
  5.0 0.3 fusion.101
  5.3 0.9 %fusion.13 = f32[16,4,6,128]{3,2,1,0:T(8,128)S(1)} fusion(f32[16,4,6]{2,1,0:T(4,128)S(1)} %fusion.101, f32[16,4,6,96]{3,2,1,0:T(8,128)S(1)} %fusion.23, bf16[16,96,512]{2,1,0:T(8,128)(2,1)S(1)} %copy-done), kind=kOutput, calls=%fused_computation.15 | convolution fusion | flops 9548255 | bytes 1918464 | tf_op jit(solution)/shard_map/rkgt,rtkd->rkgd/dot_general | solution.py:27
  6.3 0.1 multiply_reduce_fusion.4
  6.6 4.1 %collective-permute-start.5 = (bf16[16,3200]{1,0:T(8,128)(2,1)S(1)}, bf16[16,3200]{1,0:T(8,128)(2,1)S(1)}, u32[]{:S(2)}, u32[]{:S(2)}) collective-permute-start(bf16[16,3200]{1,0:T(8,128)(2,1)S(1)} %fusion.67), channel_id=1, source_target_pairs={{0,8},{4,12},{8,0},{12,4},{1,9},{5,13},{9,1},{13,5},{2,10},{6,14},... | collective-permute-start | bytes 307208 | tf_op jit(solution)/shard_map/ppermute | solution.py:56
  10.7 1.6 %collective-permute-start.4 = (bf16[16,3200]{1,0:T(8,128)(2,1)S(1)}, bf16[16,3200]{1,0:T(8,128)(2,1)S(1)}, u32[]{:S(2)}, u32[]{:S(2)}) collective-permute-start(bf16[16,3200]{1,0:T(8,128)(2,1)S(1)} %fusion.67), channel_id=1, source_target_pairs={{0,4},{4,0},{8,12},{12,8},{1,5},{5,1},{9,13},{13,9},{2,6},{6,2},{1... | collective-permute-start | bytes 307208 | tf_op jit(solution)/shard_map/ppermute | solution.py:56
  12.6 0.2 select_reduce_fusion.2
  13.0 0.3 convolution_convert_fusion.3
  13.3 0.4 collective-permute-start.3
  13.8 1.4 %collective-permute-start.1 = (bf16[8,3072]{1,0:T(8,128)(2,1)S(1)}, bf16[8,3072]{1,0:T(8,128)(2,1)S(1)}, u32[]{:S(2)}, u32[]{:S(2)}) collective-permute-start(bf16[8,3072]{1,0:T(8,128)(2,1)S(1)} %get-tuple-element.22), channel_id=1, source_target_pairs={{0,1},{1,0},{2,3},{3,2},{4,5},{5,4},{6,7},{7,6},{8,9},{9,8},{10,11... | collective-permute-start | bytes 147464 | tf_op jit(solution)/shard_map/ppermute | solution.py:56
  15.2 0.1 fusion.102
  15.5 0.6 collective-permute-done.1
  16.1 0.3 collective-permute-start.2
  16.4 3.8 %collective-permute-done.2 = bf16[8,3072]{1,0:T(8,128)(2,1)S(1)} collective-permute-done((bf16[8,3072]{1,0:T(8,128)(2,1)S(1)}, bf16[8,3072]{1,0:T(8,128)(2,1)S(1)}, u32[]{:S(2)}, u32[]{:S(2)}) %collective-permute-start.2) | collective-permute-done | bytes 49184 | tf_op jit(solution)/shard_map/ppermute | solution.py:56
  20.6 0.2 select_reduce_fusion
  20.8 0.5 multiply_add_fusion.6
  21.3 0.1 copy.88
  21.8 0.2 select_reduce_fusion.1
  21.9 0.5 multiply_add_fusion.5
  22.8 0.1 fusion.68
  23.1 0.1 fusion.71
  23.4 0.7 copy.85
  24.2 0.1 fusion.75
  24.6 0.1 reshape.168
  24.8 0.2 select_reduce_fusion.3
  25.3 0.2 fusion.10
  25.6 0.2 fusion.11
  25.8 0.2 fusion.12
  26.3 0.8 collective-permute-start.7
  27.1 1.0 %collective-permute-start.6 = (bf16[24,3072]{1,0:T(8,128)(2,1)S(1)}, bf16[24,3072]{1,0:T(8,128)(2,1)S(1)}, u32[]{:S(2)}, u32[]{:S(2)}) collective-permute-start(bf16[24,3072]{1,0:T(8,128)(2,1)S(1)} %get-tuple-element.19), channel_id=1, source_target_pairs={{0,1},{1,0},{2,3},{3,2},{4,5},{5,4},{6,7},{7,6},{8,9},{9,8},{10,11... | collective-permute-start | bytes 442376 | tf_op jit(solution)/shard_map/ppermute | solution.py:56
  28.1 1.0 %collective-permute-done.6 = bf16[24,3072]{1,0:T(8,128)(2,1)S(1)} collective-permute-done((bf16[24,3072]{1,0:T(8,128)(2,1)S(1)}, bf16[24,3072]{1,0:T(8,128)(2,1)S(1)}, u32[]{:S(2)}, u32[]{:S(2)}) %collective-permute-start.6) | collective-permute-done | bytes 147488 | tf_op jit(solution)/shard_map/ppermute | solution.py:56
  29.1 5.2 %collective-permute-done.7 = bf16[24,3072]{1,0:T(8,128)(2,1)S(1)} collective-permute-done((bf16[24,3072]{1,0:T(8,128)(2,1)S(1)}, bf16[24,3072]{1,0:T(8,128)(2,1)S(1)}, u32[]{:S(2)}, u32[]{:S(2)}) %collective-permute-start.7) | collective-permute-done | bytes 147488 | tf_op jit(solution)/shard_map/ppermute | solution.py:56
  34.4 7.4 %fusion.3 = f32[128,2048]{1,0:T(8,128)} fusion(bf16[128,3072]{1,0:T(8,128)(2,1)S(1)} %constant_dynamic-update-slice_fusion, bf16[1,3072,2048]{2,1,0:T(8,128)(2,1)} %param.20), kind=kOutput, calls=%fused_computation.3 | convolution fusion | flops 1610612736 | bytes 14417920 | tf_op jit(solution)/shard_map/dot_general | solution.py:107
  41.8 12.1 %fusion.7 = bf16[128,3072]{1,0:T(8,128)(2,1)S(1)} fusion(bf16[1,2048,3072]{2,1,0:T(8,128)(2,1)} %param.21, f32[128,2048]{1,0:T(8,128)} %fusion.3, bf16[128,3072]{1,0:T(8,128)(2,1)S(1)} %constant_dynamic-update-slice_fusion, bf16[1,3072,2048]{2,1,0:T(8,128)(2,1)} %param.19), kind=kOutput, calls=%fused_computation.7 | convolution fusion | flops 3223191552 | bytes 27787264 | tf_op jit(solution)/shard_map/dot_general | solution.py:109
  53.9 1.0 %collective-permute-start.17 = (bf16[8,3072]{1,0:T(8,128)(2,1)S(1)}, bf16[8,3072]{1,0:T(8,128)(2,1)S(1)}, u32[]{:S(2)}, u32[]{:S(2)}) collective-permute-start(bf16[8,3072]{1,0:T(8,128)(2,1)S(1)} %get-tuple-element.8), channel_id=1, source_target_pairs={{0,3},{1,2},{2,1},{3,0},{4,7},{5,6},{6,5},{7,4},{8,11},{9,10},{10,... | collective-permute-start | bytes 147464 | tf_op jit(solution)/shard_map/ppermute | solution.py:56
  54.9 1.0 %collective-permute-start.16 = (bf16[8,3072]{1,0:T(8,128)(2,1)S(1)}, bf16[8,3072]{1,0:T(8,128)(2,1)S(1)}, u32[]{:S(2)}, u32[]{:S(2)}) collective-permute-start(bf16[8,3072]{1,0:T(8,128)(2,1)S(1)} %get-tuple-element.9), channel_id=1, source_target_pairs={{0,2},{1,3},{2,0},{3,1},{4,6},{5,7},{6,4},{7,5},{8,10},{9,11},{10,... | collective-permute-start | bytes 147464 | tf_op jit(solution)/shard_map/ppermute | solution.py:56
  56.0 0.7 fusion.96
  56.7 0.5 collective-permute-start.9
  57.2 1.0 %collective-permute-start.11 = (bf16[24,3072]{1,0:T(8,128)(2,1)}, bf16[24,3072]{1,0:T(8,128)(2,1)S(1)}, u32[]{:S(2)}, u32[]{:S(2)}) collective-permute-start(bf16[24,3072]{1,0:T(8,128)(2,1)} %get-tuple-element.15), channel_id=1, source_target_pairs={{0,3},{1,2},{2,1},{3,0},{4,7},{5,6},{6,5},{7,4},{8,11},{9,10},{10,... | collective-permute-start | bytes 442376 | tf_op jit(solution)/shard_map/ppermute | solution.py:56
  58.2 1.3 %collective-permute-start.10 = (bf16[24,3072]{1,0:T(8,128)(2,1)}, bf16[24,3072]{1,0:T(8,128)(2,1)S(1)}, u32[]{:S(2)}, u32[]{:S(2)}) collective-permute-start(bf16[24,3072]{1,0:T(8,128)(2,1)} %get-tuple-element.16), channel_id=1, source_target_pairs={{0,2},{1,3},{2,0},{3,1},{4,6},{5,7},{6,4},{7,5},{8,10},{9,11},{10,... | collective-permute-start | bytes 442376 | tf_op jit(solution)/shard_map/ppermute | solution.py:56
  59.5 0.2 fusion.57
  59.7 0.2 reshape.175
  60.0 0.9 %fusion.98 = (bf16[8,3072]{1,0:T(8,128)(2,1)S(1)}, bf16[8,3072]{1,0:T(8,128)(2,1)S(1)}, bf16[8,3072]{1,0:T(8,128)(2,1)S(1)}) fusion(bf16[24,3072]{1,0:T(8,128)(2,1)} %collective-permute-done.9), kind=kLoop, calls=%fused_computation.165 | loop fusion | bytes 294912 | tf_op jit(solution)/shard_map/slice | solution.py:121
  60.8 2.6 %collective-permute-done.11 = bf16[24,3072]{1,0:T(8,128)(2,1)S(1)} collective-permute-done((bf16[24,3072]{1,0:T(8,128)(2,1)}, bf16[24,3072]{1,0:T(8,128)(2,1)S(1)}, u32[]{:S(2)}, u32[]{:S(2)}) %collective-permute-start.11) | collective-permute-done | bytes 147488 | tf_op jit(solution)/shard_map/ppermute | solution.py:56
  63.4 3.3 %collective-permute-done.10 = bf16[24,3072]{1,0:T(8,128)(2,1)S(1)} collective-permute-done((bf16[24,3072]{1,0:T(8,128)(2,1)}, bf16[24,3072]{1,0:T(8,128)(2,1)S(1)}, u32[]{:S(2)}, u32[]{:S(2)}) %collective-permute-start.10) | collective-permute-done | bytes 147488 | tf_op jit(solution)/shard_map/ppermute | solution.py:56
  66.8 0.2 fusion.33
  67.0 0.2 reshape.172
  67.2 1.2 %multiply_reduce_fusion.3 = bf16[16,3072]{1,0:T(8,128)(2,1)} fusion(f32[16,2,3072]{2,1,0:T(2,128)S(1)} %reshape.172, f32[16,2]{1,0:T(8,128)S(1)} %copy.73), kind=kLoop, calls=%fused_computation.31 | loop fusion | flops 147456 | bytes 491648 | tf_op jit(solution)/shard_map/reduce_sum | solution.py:126
  68.4 3.6 %collective-permute-start.12 = (bf16[16,3072]{1,0:T(8,128)(2,1)}, bf16[16,3072]{1,0:T(8,128)(2,1)S(1)}, u32[]{:S(2)}, u32[]{:S(2)}) collective-permute-start(bf16[16,3072]{1,0:T(8,128)(2,1)} %multiply_reduce_fusion.3), channel_id=1, source_target_pairs={{0,12},{4,8},{8,4},{12,0},{1,13},{5,9},{9,5},{13,1},{2,14},{6,10},... | collective-permute-start | bytes 294920 | tf_op jit(solution)/shard_map/ppermute | solution.py:56
  72.0 0.9 %fusion.49 = f32[32,3072]{1,0:T(8,128)S(1)} fusion(bf16[8,3072]{1,0:T(8,128)(2,1)S(1)} %get-tuple-element.31, bf16[8,3072]{1,0:T(8,128)(2,1)S(1)} %get-tuple-element.28, bf16[8,3072]{1,0:T(8,128)(2,1)S(1)} %get-tuple-element.25, bf16[8,3072]{1,0:T(8,128)(2,1)S(1)} %get-tuple-element.12, s32[32]{0:T(128)} %multiply_add_fusion.5), kind=kOutput, calls=%fused_computation.51 | convolution fusion | flops 7078912 | bytes 589952 | tf_op jit(solution)/shard_map/sa,sd->ad/dot_general | solution.py:123
  72.9 0.2 reshape.174
  73.2 1.9 %multiply_reduce_fusion.1 = bf16[16,3072]{1,0:T(8,128)(2,1)} fusion(f32[16,2,3072]{2,1,0:T(2,128)S(1)} %reshape.174, f32[16,2]{1,0:T(8,128)} %copy.85), kind=kLoop, calls=%fused_computation.29 | loop fusion | flops 147456 | bytes 491648 | tf_op jit(solution)/shard_map/reduce_sum | solution.py:126
  75.1 0.8 fusion.41
  75.9 0.2 reshape.173
  76.2 0.6 multiply_reduce_fusion.2
  76.7 0.8 collective-permute-start.13
  77.6 0.6 multiply_reduce_fusion
  78.1 1.8 %collective-permute-done.14 = bf16[16,3072]{1,0:T(8,128)(2,1)S(1)} collective-permute-done((bf16[16,3072]{1,0:T(8,128)(2,1)}, bf16[16,3072]{1,0:T(8,128)(2,1)S(1)}, u32[]{:S(2)}, u32[]{:S(2)}) %collective-permute-start.14) | collective-permute-done | bytes 98336 | tf_op jit(solution)/shard_map/ppermute | solution.py:56
  79.9 4.4 %collective-permute-done.13 = bf16[16,3072]{1,0:T(8,128)(2,1)S(1)} collective-permute-done((bf16[16,3072]{1,0:T(8,128)(2,1)S(1)}, bf16[16,3072]{1,0:T(8,128)(2,1)S(1)}, u32[]{:S(2)}, u32[]{:S(2)}) %collective-permute-start.13) | collective-permute-done | bytes 98336 | tf_op jit(solution)/shard_map/ppermute | solution.py:56
  84.3 0.7 add_convert_fusion
  (98 shorter events, 3.3 us)
Async XLA Ops:
  0.0 5.3 %copy-start = (bf16[16,96,512]{2,1,0:T(8,128)(2,1)S(1)}, bf16[16,96,512]{2,1,0:T(8,128)(2,1)}, u32[]{:S(2)}) copy-start(bf16[16,96,512]{2,1,0:T(8,128)(2,1)} %param.13) | copy-start | bytes 4718596
  5.3 1.0 %copy-start.1 = (bf16[16,3072]{1,0:T(8,128)(2,1)S(1)}, bf16[16,3072]{1,0:T(8,128)(2,1)}, u32[]{:S(2)}) copy-start(bf16[16,3072]{1,0:T(8,128)(2,1)} %param.16) | copy-start | bytes 294916
  5.3 1.2 %copy-start.2 = (f32[3072]{0:T(1024)S(1)}, f32[3072]{0:T(1024)}, u32[]{:S(2)}) copy-start(f32[3072]{0:T(1024)} %param.17) | copy-start | bytes 36868
  6.2 9.0 %copy-start.3 = (bf16[3072,4]{0,1:T(4,128)(2,1)S(1)}, bf16[3072,4]{0,1:T(4,128)(2,1)}, u32[]{:S(2)}) copy-start(bf16[3072,4]{0,1:T(4,128)(2,1)} %param.18) | copy-start | bytes 73732
  6.6 13.6 %collective-permute-start.5 = (bf16[16,3200]{1,0:T(8,128)(2,1)S(1)}, bf16[16,3200]{1,0:T(8,128)(2,1)S(1)}, u32[]{:S(2)}, u32[]{:S(2)}) collective-permute-start(bf16[16,3200]{1,0:T(8,128)(2,1)S(1)} %fusion.67), channel_id=1, source_target_pairs={{0,8},{4,12},{8,0},{12,4},{1,9},{5,13},{9,1},{13,5},{2,10},{6,14},... | collective-permute-start | bytes 307208 | tf_op jit(solution)/shard_map/ppermute | solution.py:56
  10.7 10.7 %collective-permute-start.4 = (bf16[16,3200]{1,0:T(8,128)(2,1)S(1)}, bf16[16,3200]{1,0:T(8,128)(2,1)S(1)}, u32[]{:S(2)}, u32[]{:S(2)}) collective-permute-start(bf16[16,3200]{1,0:T(8,128)(2,1)S(1)} %fusion.67), channel_id=1, source_target_pairs={{0,4},{4,0},{8,12},{12,8},{1,5},{5,1},{9,13},{13,9},{2,6},{6,2},{1... | collective-permute-start | bytes 307208 | tf_op jit(solution)/shard_map/ppermute | solution.py:56
  12.3 10.4 %collective-permute-start = (bf16[16,3200]{1,0:T(8,128)(2,1)S(1)}, bf16[16,3200]{1,0:T(8,128)(2,1)S(1)}, u32[]{:S(2)}, u32[]{:S(2)}) collective-permute-start(bf16[16,3200]{1,0:T(8,128)(2,1)S(1)} %fusion.67), channel_id=1, source_target_pairs={{0,12},{4,8},{8,4},{12,0},{1,13},{5,9},{9,5},{13,1},{2,14},{6,10},... | collective-permute-start | bytes 307208 | tf_op jit(solution)/shard_map/ppermute | solution.py:56
  13.3 6.9 %collective-permute-start.3 = (bf16[8,3072]{1,0:T(8,128)(2,1)S(1)}, bf16[8,3072]{1,0:T(8,128)(2,1)S(1)}, u32[]{:S(2)}, u32[]{:S(2)}) collective-permute-start(bf16[8,3072]{1,0:T(8,128)(2,1)S(1)} %get-tuple-element.20), channel_id=1, source_target_pairs={{0,3},{1,2},{2,1},{3,0},{4,7},{5,6},{6,5},{7,4},{8,11},{9,10},{10,... | collective-permute-start | bytes 147464 | tf_op jit(solution)/shard_map/ppermute | solution.py:56
  13.8 2.3 %collective-permute-start.1 = (bf16[8,3072]{1,0:T(8,128)(2,1)S(1)}, bf16[8,3072]{1,0:T(8,128)(2,1)S(1)}, u32[]{:S(2)}, u32[]{:S(2)}) collective-permute-start(bf16[8,3072]{1,0:T(8,128)(2,1)S(1)} %get-tuple-element.22), channel_id=1, source_target_pairs={{0,1},{1,0},{2,3},{3,2},{4,5},{5,4},{6,7},{7,6},{8,9},{9,8},{10,11... | collective-permute-start | bytes 147464 | tf_op jit(solution)/shard_map/ppermute | solution.py:56
  16.1 4.1 %collective-permute-start.2 = (bf16[8,3072]{1,0:T(8,128)(2,1)S(1)}, bf16[8,3072]{1,0:T(8,128)(2,1)S(1)}, u32[]{:S(2)}, u32[]{:S(2)}) collective-permute-start(bf16[8,3072]{1,0:T(8,128)(2,1)S(1)} %get-tuple-element.21), channel_id=1, source_target_pairs={{0,2},{1,3},{2,0},{3,1},{4,6},{5,7},{6,4},{7,5},{8,10},{9,11},{10,... | collective-permute-start | bytes 147464 | tf_op jit(solution)/shard_map/ppermute | solution.py:56
  26.2 8.2 %collective-permute-start.8 = (bf16[24,3072]{1,0:T(8,128)(2,1)S(1)}, bf16[24,3072]{1,0:T(8,128)(2,1)S(1)}, u32[]{:S(2)}, u32[]{:S(2)}) collective-permute-start(bf16[24,3072]{1,0:T(8,128)(2,1)S(1)} %get-tuple-element.17), channel_id=1, source_target_pairs={{0,3},{1,2},{2,1},{3,0},{4,7},{5,6},{6,5},{7,4},{8,11},{9,10},{10,... | collective-permute-start | bytes 442376 | tf_op jit(solution)/shard_map/ppermute | solution.py:56
  26.3 8.1 %collective-permute-start.7 = (bf16[24,3072]{1,0:T(8,128)(2,1)S(1)}, bf16[24,3072]{1,0:T(8,128)(2,1)S(1)}, u32[]{:S(2)}, u32[]{:S(2)}) collective-permute-start(bf16[24,3072]{1,0:T(8,128)(2,1)S(1)} %get-tuple-element.18), channel_id=1, source_target_pairs={{0,2},{1,3},{2,0},{3,1},{4,6},{5,7},{6,4},{7,5},{8,10},{9,11},{10,... | collective-permute-start | bytes 442376 | tf_op jit(solution)/shard_map/ppermute | solution.py:56
  27.1 2.0 %collective-permute-start.6 = (bf16[24,3072]{1,0:T(8,128)(2,1)S(1)}, bf16[24,3072]{1,0:T(8,128)(2,1)S(1)}, u32[]{:S(2)}, u32[]{:S(2)}) collective-permute-start(bf16[24,3072]{1,0:T(8,128)(2,1)S(1)} %get-tuple-element.19), channel_id=1, source_target_pairs={{0,1},{1,0},{2,3},{3,2},{4,5},{5,4},{6,7},{7,6},{8,9},{9,8},{10,11... | collective-permute-start | bytes 442376 | tf_op jit(solution)/shard_map/ppermute | solution.py:56
  53.9 4.3 %collective-permute-start.17 = (bf16[8,3072]{1,0:T(8,128)(2,1)S(1)}, bf16[8,3072]{1,0:T(8,128)(2,1)S(1)}, u32[]{:S(2)}, u32[]{:S(2)}) collective-permute-start(bf16[8,3072]{1,0:T(8,128)(2,1)S(1)} %get-tuple-element.8), channel_id=1, source_target_pairs={{0,3},{1,2},{2,1},{3,0},{4,7},{5,6},{6,5},{7,4},{8,11},{9,10},{10,... | collective-permute-start | bytes 147464 | tf_op jit(solution)/shard_map/ppermute | solution.py:56
  54.9 4.5 %collective-permute-start.16 = (bf16[8,3072]{1,0:T(8,128)(2,1)S(1)}, bf16[8,3072]{1,0:T(8,128)(2,1)S(1)}, u32[]{:S(2)}, u32[]{:S(2)}) collective-permute-start(bf16[8,3072]{1,0:T(8,128)(2,1)S(1)} %get-tuple-element.9), channel_id=1, source_target_pairs={{0,2},{1,3},{2,0},{3,1},{4,6},{5,7},{6,4},{7,5},{8,10},{9,11},{10,... | collective-permute-start | bytes 147464 | tf_op jit(solution)/shard_map/ppermute | solution.py:56
  56.0 3.5 %collective-permute-start.15 = (bf16[8,3072]{1,0:T(8,128)(2,1)S(1)}, bf16[8,3072]{1,0:T(8,128)(2,1)S(1)}, u32[]{:S(2)}, u32[]{:S(2)}) collective-permute-start(bf16[8,3072]{1,0:T(8,128)(2,1)S(1)} %get-tuple-element.10), channel_id=1, source_target_pairs={{0,1},{1,0},{2,3},{3,2},{4,5},{5,4},{6,7},{7,6},{8,9},{9,8},{10,11... | collective-permute-start | bytes 147464 | tf_op jit(solution)/shard_map/ppermute | solution.py:56
  56.7 3.3 %collective-permute-start.9 = (bf16[24,3072]{1,0:T(8,128)(2,1)S(1)}, bf16[24,3072]{1,0:T(8,128)(2,1)}, u32[]{:S(2)}, u32[]{:S(2)}) collective-permute-start(bf16[24,3072]{1,0:T(8,128)(2,1)S(1)} %get-tuple-element.14), channel_id=1, source_target_pairs={{0,1},{1,0},{2,3},{3,2},{4,5},{5,4},{6,7},{7,6},{8,9},{9,8},{10,11... | collective-permute-start | bytes 442376 | tf_op jit(solution)/shard_map/ppermute | solution.py:56
  57.2 6.2 %collective-permute-start.11 = (bf16[24,3072]{1,0:T(8,128)(2,1)}, bf16[24,3072]{1,0:T(8,128)(2,1)S(1)}, u32[]{:S(2)}, u32[]{:S(2)}) collective-permute-start(bf16[24,3072]{1,0:T(8,128)(2,1)} %get-tuple-element.15), channel_id=1, source_target_pairs={{0,3},{1,2},{2,1},{3,0},{4,7},{5,6},{6,5},{7,4},{8,11},{9,10},{10,... | collective-permute-start | bytes 442376 | tf_op jit(solution)/shard_map/ppermute | solution.py:56
  58.2 8.6 %collective-permute-start.10 = (bf16[24,3072]{1,0:T(8,128)(2,1)}, bf16[24,3072]{1,0:T(8,128)(2,1)S(1)}, u32[]{:S(2)}, u32[]{:S(2)}) collective-permute-start(bf16[24,3072]{1,0:T(8,128)(2,1)} %get-tuple-element.16), channel_id=1, source_target_pairs={{0,2},{1,3},{2,0},{3,1},{4,6},{5,7},{6,4},{7,5},{8,10},{9,11},{10,... | collective-permute-start | bytes 442376 | tf_op jit(solution)/shard_map/ppermute | solution.py:56
  68.4 9.7 %collective-permute-start.12 = (bf16[16,3072]{1,0:T(8,128)(2,1)}, bf16[16,3072]{1,0:T(8,128)(2,1)S(1)}, u32[]{:S(2)}, u32[]{:S(2)}) collective-permute-start(bf16[16,3072]{1,0:T(8,128)(2,1)} %multiply_reduce_fusion.3), channel_id=1, source_target_pairs={{0,12},{4,8},{8,4},{12,0},{1,13},{5,9},{9,5},{13,1},{2,14},{6,10},... | collective-permute-start | bytes 294920 | tf_op jit(solution)/shard_map/ppermute | solution.py:56
  75.1 4.8 %collective-permute-start.14 = (bf16[16,3072]{1,0:T(8,128)(2,1)}, bf16[16,3072]{1,0:T(8,128)(2,1)S(1)}, u32[]{:S(2)}, u32[]{:S(2)}) collective-permute-start(bf16[16,3072]{1,0:T(8,128)(2,1)} %multiply_reduce_fusion.1), channel_id=1, source_target_pairs={{0,4},{4,0},{8,12},{12,8},{1,5},{5,1},{9,13},{13,9},{2,6},{6,2},{1... | collective-permute-start | bytes 294920 | tf_op jit(solution)/shard_map/ppermute | solution.py:56
  76.7 7.5 %collective-permute-start.13 = (bf16[16,3072]{1,0:T(8,128)(2,1)S(1)}, bf16[16,3072]{1,0:T(8,128)(2,1)S(1)}, u32[]{:S(2)}, u32[]{:S(2)}) collective-permute-start(bf16[16,3072]{1,0:T(8,128)(2,1)S(1)} %multiply_reduce_fusion.2), channel_id=1, source_target_pairs={{0,8},{4,12},{8,0},{12,4},{1,9},{5,13},{9,1},{13,5},{2,10},{6,14},... | collective-permute-start | bytes 294920 | tf_op jit(solution)/shard_map/ppermute | solution.py:56

commit v2 on v0

v2 whole, which is shorter than its diff:
```python
import functools

import jax
import jax.numpy as jnp
from jax import lax
from jax.experimental import pallas as pl
from jax.experimental.pallas import tpu as pltpu
from jax.sharding import PartitionSpec as P

HS = 128
KVH = 4
GROUP = 6
CAP = 8
LANES = 128
MIB = 1 << 20
F32 = jnp.float32
BF16 = jnp.bfloat16
ANY = pl.BlockSpec(memory_space=pl.ANY)
WHOLE = pl.BlockSpec(memory_space=pltpu.VMEM)
SCALAR = pl.BlockSpec(memory_space=pltpu.SMEM)


def dot(a, b, dims=((1,), (0,))):
    return lax.dot_general(a, b, (dims, ((), ())), preferred_element_type=F32)


def iota(shape, dim):
    return lax.broadcasted_iota(jnp.int32, shape, dim)


def slot_map(owners, chunks, batch, experts):
    rows, slots = chunks * batch, experts * chunks * CAP
    slot = iota((rows, slots), 1)
    row = iota((rows, slots), 0)
    expert = slot // (chunks * CAP)
    chunk = (slot // CAP) % chunks
    named = (owners[:, 0:1] == expert) | (owners[:, 1:2] == expert)
    named = named & (row // batch == chunk)
    named = jnp.where(named, 1.0, 0.0)
    left, right = iota((rows, rows), 0), iota((rows, rows), 1)
    before = jnp.where(right < left, 1.0, 0.0).astype(BF16)
    place = dot(before, named.astype(BF16))
    wanted = (slot % CAP).astype(F32)
    return jnp.where(place == wanted, named, 0.0)


def dispatch(me, rows, named, chunks, experts):
    owners = named[:, 0:2].astype(F32).astype(jnp.int32) ^ me
    table = slot_map(owners, chunks, rows.shape[0] // chunks, experts)
    return dot(table.astype(BF16), rows, ((0,), (0,)))


def combine(me, rows, named, router, returned, chunks, experts):
    routes = named[:, 0:2].astype(F32).astype(jnp.int32)
    logits = dot(rows, router, ((1,), (1,)))
    lane = iota(logits.shape, 1)
    first = jnp.sum(jnp.where(lane == routes[:, 0:1], logits, 0.0), axis=1, keepdims=True)
    second = jnp.sum(jnp.where(lane == routes[:, 1:2], logits, 0.0), axis=1, keepdims=True)
    gate0 = 1.0 / (1.0 + jnp.exp(second - first))
    gate1 = 1.0 / (1.0 + jnp.exp(first - second))
    owners = routes ^ me
    table = slot_map(owners, chunks, rows.shape[0] // chunks, experts)
    expert = iota(table.shape, 1) // (chunks * CAP)
    gates = table * jnp.where(owners[:, 0:1] == expert, gate0, gate1)
    high = gates.astype(BF16)
    low = (gates - high.astype(F32)).astype(BF16)
    return dot(high, returned) + dot(low, returned)


def attend_kernel(
    me_ref, lengths_ref, queries_ref, keys_ref, values_ref, routes_ref, residual_ref, gain_ref,
    stream_ref, payload_ref, *rest,
):
    slots, attended = rest[:-1], rest[-1]
    head = pl.program_id(0)
    batch, window, _ = keys_ref.shape
    keys = keys_ref[...].reshape(batch * window, HS)
    values = values_ref[...].reshape(batch * window, HS)
    block = queries_ref[...]
    stacked = jnp.concatenate([block[:, g * HS : (g + 1) * HS] for g in range(GROUP)], axis=0)
    scores = dot(stacked, keys, ((1,), (1,))) * HS ** (-0.5)
    column = iota((batch, batch * window), 1)
    row = iota((batch, batch * window), 0)
    length = jnp.zeros((batch, batch * window), jnp.int32)
    for r in range(batch):
        length = jnp.where(row == r, lengths_ref[r], length)
    begin = row * window
    bias = jnp.where((column >= begin) & (column < begin + length), 0.0, -1e30)
    scores = scores + jnp.concatenate([bias] * GROUP, axis=0)
    highest = jnp.max(scores, axis=1, keepdims=True)
    powers = jnp.exp(scores - highest)
    weights = (powers / jnp.sum(powers, axis=1, keepdims=True)).astype(BF16)
    mixed = dot(weights, values)
    attended[head] = jnp.concatenate(
        [mixed[g * batch : (g + 1) * batch] for g in range(GROUP)], axis=1
    )

    @pl.when(head == KVH - 1)
    def finish():
        stream = residual_ref[...].astype(F32) + jnp.concatenate(
            [attended[k] for k in range(KVH)], axis=1
        )
        width = stream.shape[1]
        scale = lax.rsqrt(jnp.mean(stream * stream, axis=1, keepdims=True) + 1e-05)
        normed = (stream * scale * gain_ref[...]).astype(BF16)
        lane = iota((batch, LANES), 1)
        same = iota((batch, batch), 0) == iota((batch, batch), 1)
        routes = [
            jnp.sum(jnp.where(same, routes_ref[k : k + 1, :], 0), axis=1, keepdims=True).astype(F32)
            for k in range(2)
        ]
        named = jnp.where(lane == 0, routes[0], jnp.where(lane == 1, routes[1], 0.0))
        named = named.astype(BF16)
        stream_ref[...] = stream
        payload_ref[:, :width] = normed
        payload_ref[:, width:] = named
        out = dispatch(me_ref[0], normed, named, 1, len(slots))
        for e, ref in enumerate(slots):
            ref[...] = out[e * CAP : (e + 1) * CAP].astype(BF16)


def split_kernel(me_ref, *refs, chunks, after):
    refs = refs[after:]
    payload = jnp.concatenate([ref[...] for ref in refs[:chunks]], axis=0)
    slots = refs[chunks:]
    width = slots[0].shape[1]
    rows, named = payload[:, :width], payload[:, width:]
    out = dispatch(me_ref[0], rows, named, chunks, len(slots))
    span = chunks * CAP
    for e, ref in enumerate(slots):
        ref[...] = out[e * span : (e + 1) * span].astype(BF16)


def expert_kernel(*refs, pieces):
    xs, (gate_ref, up_ref, down_ref) = refs[:pieces], refs[pieces : pieces + 3]
    outs = refs[pieces + 3 : 2 * pieces + 3]
    rows_ref, hidden_ref = refs[2 * pieces + 3 :]
    rows_ref[...] = jnp.concatenate([ref[...].astype(F32) for ref in xs], axis=0).astype(BF16)
    width, units = gate_ref.shape
    tile = min(256, units)

    @pl.loop(0, units // tile)
    def _(i):
        at = pl.ds(pl.multiple_of(i * tile, tile), tile)
        gate = dot(rows_ref[...], gate_ref[:, at])
        up = dot(rows_ref[...], up_ref[:, at])
        hidden_ref[:, at] = (jax.nn.silu(gate) * up).astype(BF16)

    @pl.loop(0, width // tile)
    def _(i):
        at = pl.ds(pl.multiple_of(i * tile, tile), tile)
        out = dot(hidden_ref[...], down_ref[:, at])
        begin = 0
        for ref in outs:
            count = ref.shape[0]
            ref[:, at] = out[begin : begin + count].astype(BF16)
            begin += count


def load_kernel(after_ref, *refs, count):
    del after_ref
    token_ref, sems = refs[-2:]
    copies = [
        pltpu.make_async_copy(source, target, sems.at[i])
        for i, (source, target) in enumerate(zip(refs[:count], refs[count : 2 * count]))
    ]
    for copy in copies:
        copy.start()
    for copy in copies:
        copy.wait()
    token_ref[...] = jnp.zeros_like(token_ref)


def load(after, *weights):
    size = sum(w.size * w.dtype.itemsize for w in weights)
    return pl.pallas_call(
        functools.partial(load_kernel, count=len(weights)),
        in_specs=[ANY] * (1 + len(weights)),
        out_specs=[WHOLE] * (len(weights) + 1),
        out_shape=[pltpu.VMEM(w.shape, w.dtype) for w in weights]
        + [jax.ShapeDtypeStruct((8, LANES), F32)],
        scratch_shapes=[pltpu.SemaphoreType.DMA((len(weights),))],
        compiler_params=params(0),
        cost_estimate=pl.CostEstimate(flops=0, bytes_accessed=2 * size, transcendentals=0),
    )(after, *[in_hbm(w) for w in weights])


def in_hbm(value):
    return pltpu.with_memory_space_constraint(value, pltpu.HBM)


def in_vmem(value):
    return pltpu.with_memory_space_constraint(value, pltpu.VMEM)


def mix_kernel(me_ref, router_ref, *refs, chunks, experts):
    payload = jnp.concatenate([ref[...] for ref in refs[:chunks]], axis=0)
    returned = jnp.concatenate(
        [ref[...].astype(F32) for ref in refs[chunks : chunks + experts]], axis=0
    ).astype(BF16)
    outs = refs[chunks + experts :]
    batch, width = outs[0].shape
    rows, named = payload[:, :width], payload[:, width:]
    mixed = combine(me_ref[0], rows, named, router_ref[...], returned, chunks, experts)
    for j, ref in enumerate(outs):
        ref[...] = mixed[j * batch : (j + 1) * batch].astype(BF16)


def finish_kernel(me_ref, router_ref, payload_ref, stream_ref, *refs, experts):
    returned = jnp.concatenate([ref[...].astype(F32) for ref in refs[:experts]], axis=0)
    out_ref = refs[-1]
    width = out_ref.shape[1]
    rows, named = payload_ref[:, :width], payload_ref[:, width:]
    total = stream_ref[...] + combine(
        me_ref[0], rows, named, router_ref[...], returned.astype(BF16), 1, experts
    )
    for ref in refs[experts:-1]:
        total = total + ref[...].astype(F32)
    out_ref[...] = total.astype(BF16)


def swap(value, axis, step):
    if step == 0:
        return value
    count = lax.axis_size(axis)
    return lax.ppermute(value, axis, [(i, i ^ step) for i in range(count)])


def params(elements):
    return pltpu.CompilerParams(vmem_limit_bytes=min(48 * MIB, 2 * MIB + 10 * elements))


def shards(
    queries,
    cached_keys,
    cached_values,
    lengths,
    routes,
    residual,
    norm_gain,
    router,
    gate_proj,
    up_proj,
    down_proj,
):
    batch, width = queries.shape
    window = cached_keys.shape[1]
    experts = router.shape[1]
    layers = lax.axis_size("attn")
    remote = layers - 1
    me = lax.axis_index("expert").astype(jnp.int32).reshape(1)
    full = lambda shape: pl.BlockSpec(shape, lambda k: (0,) * len(shape))
    shape = jax.ShapeDtypeStruct
    wide = width + LANES
    span = width // KVH

    stream, payload, *slots = pl.pallas_call(
        attend_kernel,
        grid=(KVH,),
        in_specs=[
            SCALAR,
            SCALAR,
            pl.BlockSpec((batch, span), lambda k: (0, k)),
            pl.BlockSpec((batch, window, HS), lambda k: (0, 0, k)),
            pl.BlockSpec((batch, window, HS), lambda k: (0, 0, k)),
            full((2, batch)),
            full((batch, width)),
            full((1, width)),
        ],
        out_specs=[full((batch, width)), full((batch, wide))] + [full((CAP, width))] * experts,
        out_shape=[shape((batch, width), F32), shape((batch, wide), BF16)]
        + [shape((CAP, width), BF16)] * experts,
        scratch_shapes=[pltpu.VMEM((KVH, batch, span), F32)],
        compiler_params=params(28 * batch * width),
    )(
        me,
        lengths,
        *[in_hbm(a) for a in (queries, cached_keys, cached_values, routes.T, residual, norm_gain[None])],
    )
    router = router.T

    payloads = [swap(payload, "attn", j) for j in range(1, layers)]
    near = [swap(slots[e], "expert", e) for e in range(experts)]
    *first, token = load(payload, gate_proj[0], up_proj[0])
    ahead = [*near[1:], token]
    slots = pl.pallas_call(
        functools.partial(split_kernel, chunks=remote, after=len(ahead)),
        in_specs=[SCALAR] + [WHOLE] * (len(ahead) + remote),
        out_specs=[WHOLE] * experts,
        out_shape=[shape((remote * CAP, width), BF16)] * experts,
        compiler_params=params(experts * remote * CAP * width),
    )(me, *ahead, *payloads)
    far = [swap(slots[e], "expert", e) for e in range(experts)]
    *second, _ = load(slots[0], down_proj[0])

    inputs = near + far
    total_rows = sum(block.shape[0] for block in inputs)
    units = gate_proj.shape[2]
    weights = [in_vmem(w) for w in (*first, *second)]
    results = pl.pallas_call(
        functools.partial(expert_kernel, pieces=len(inputs)),
        in_specs=[WHOLE] * (len(inputs) + 3),
        out_specs=[WHOLE] * len(inputs),
        out_shape=[shape(block.shape, BF16) for block in inputs],
        scratch_shapes=[pltpu.VMEM((total_rows, width), BF16), pltpu.VMEM((total_rows, units), BF16)],
        compiler_params=params(total_rows * width),
    )(*inputs, *weights)

    far = [swap(results[experts + e], "expert", e) for e in range(experts)]
    near = [swap(results[e], "expert", e) for e in range(experts)]
    mixed = pl.pallas_call(
        functools.partial(mix_kernel, chunks=remote, experts=experts),
        in_specs=[SCALAR] + [WHOLE] * (1 + remote + experts),
        out_specs=[WHOLE] * remote,
        out_shape=[shape((batch, width), BF16)] * remote,
        compiler_params=params(experts * remote * CAP * width),
    )(me, router, *payloads, *far)
    mixed = [swap(block, "attn", j + 1) for j, block in enumerate(mixed)]
    return pl.pallas_call(
        functools.partial(finish_kernel, experts=experts),
        in_specs=[SCALAR] + [WHOLE] * (3 + experts + remote),
        out_specs=WHOLE,
        out_shape=shape((batch, width), BF16),
        compiler_params=params(total_rows * width),
    )(me, router, payload, stream, *near, *mixed)


def solution(mesh):
    in_specs = (
        P(("groups", "attn", "expert"), None),
        P(("groups", "attn", "expert"), None, None),
        P(("groups", "attn", "expert"), None, None),
        P(("groups", "attn", "expert")),
        P(("groups", "attn", "expert"), None),
        P(("groups", "attn", "expert"), None),
        P(),
        P(),
        P("expert", None, "attn"),
        P("expert", None, "attn"),
        P("expert", "attn", None),
    )
    out_specs = P(("groups", "attn", "expert"), None)
    return jax.shard_map(shards, mesh=mesh, in_specs=in_specs, out_specs=out_specs, check_vma=False)
```

time: 103 us -> 68.2 us (0.66)
  Pallas kernels: 0 us -> 30.7 us
  blocking collectives: 29.2 us -> 0 us
  matrix products: 24.4 us -> 0 us
  starting transfers between devices: 3.37 us -> 18.9 us
  waiting for transfers between devices: 27.2 us -> 13.2 us
  between operations: 13.5 us -> 0.12 us
  other arithmetic: 3.18 us -> 0 us
  local copies, waits for them, and re-layouts: 2.13 us -> 5.18 us
    pallas_call x0 -> x7, Pallas kernels: none -> 30.7 us  [the longest x2 14.1 us: load(): pl.pallas_call(functools.partial(load_kernel, count=len(weights)), in_spe...]
    dot_general x7 -> x0, matrix products: 24.4 us -> none  [the longest x1 13.1 us: shards(): jnp.dot(hidden, w_down, preferred_element_type=jnp.float32)]
    reduce_scatter x1 -> x0, waiting for transfers between devices: 21.9 us -> none  [shards(): lax.psum_scatter(jnp.dot(hidden, w_down, preferred_element_type=jnp.float...]
    all_gather x1 -> x0, blocking collectives: 19.8 us -> none  [shards(): lax.all_gather(arrived.reshape(columns * CAP, -1), 'attn', axis=0, tiled=...]
    ppermute x0 -> x18, starting transfers between devices: none -> 18.9 us  [swap(): return lax.ppermute(value, axis, [(i, i ^ step) for i in range(count)])]
    ppermute x0 -> x18, waiting for transfers between devices: none -> 13.2 us  [swap(): return lax.ppermute(value, axis, [(i, i ^ step) for i in range(count)])]
    all_to_all x1 -> x0, blocking collectives: 9.35 us -> none  [shards(): lax.all_to_all(outgoing.reshape(experts, CAP, -1), 'expert', split_axis=0...]
    all_to_all x1 -> x0, waiting for transfers between devices: 5.27 us -> none  [shards(): lax.all_to_all(expert_result, 'expert', split_axis=0, concat_axis=0, tile...]
  transfers between devices with their start and end apart: 2 -> 18, of which waited for: 2 -> 6; matrix products, arithmetic and copies ran while one was open for 0% -> 0% of each run, Pallas kernels for 0% -> 22%
where the time goes in v2:
time: 68.2 us; the launch traced here: 68 us
  Pallas kernels  30.7 us (45%)
  starting transfers between devices  18.9 us (28%)
  waiting for transfers between devices  13.2 us (19%)
  local copies, waits for them, and re-layouts  5.18 us (8%)
    ppermute x18, starting transfers between devices, swap(): return lax.ppermute(value, axis, [(i, i ^ step) for i in range(count)])  18.9 us
    pallas_call x2, Pallas kernels, load(): pl.pallas_call(functools.partial(load_kernel, count=len(weights)), in_spe...  14.1 us
    ppermute x18, waiting for transfers between devices, swap(): return lax.ppermute(value, axis, [(i, i ^ step) for i in range(count)])  13.2 us
    pallas_call x1, Pallas kernels, shards(): pl.pallas_call(functools.partial(expert_kernel, pieces=len(inputs)), in_s...  9.22 us
    unnamed x8, local copies, waits for them, and re-layouts  5.18 us
    pallas_call x1, Pallas kernels, shards(): pl.pallas_call(attend_kernel, grid=(KVH,), in_specs=[SCALAR, SCALAR, pl.B...  5 us
  transfers between devices with their start and end apart: 18, of which 6 were waited for; matrix products, arithmetic and copies ran while one was open for 0% of the time, Pallas kernels for 22%

profile of v2, /device:TPU:0, one launch (start us, length us, event | category | flops | bytes accessed | tf_op | source)
XLA Modules:
  0.0 68.0 jit_solution(14074786671767023509)
XLA Ops:
  0.0 0.0 copy-start.3
  0.0 0.7 copy-done.3
  0.7 5.0 %shard_map.109 = (f32[16,3072]{1,0:T(8,128)S(1)}, bf16[16,3200]{1,0:T(8,128)(2,1)S(1)}, bf16[8,3072]{1,0:T(8,128)(2,1)S(1)}, bf16[8,3072]{1,0:T(8,128)(2,1)S(1)}...) custom-call(s32[1]{0:T(128)} %bitcast.me_ref, s32[16]{0:T(128)S(1)} %copy-done.3, ...), custom_call_target="tpu_custom_call" | custom-call | tf_op jit(solution)/shard_map/pallas_call | solution.py:257
  5.7 5.1 %collective-permute-start.5 = (bf16[16,3200]{1,0:T(8,128)(2,1)S(1)}, bf16[16,3200]{1,0:T(8,128)(2,1)S(1)}, u32[]{:S(2)}, u32[]{:S(2)}) collective-permute-start(bf16[16,3200]{1,0:T(8,128)(2,1)S(1)} %get-tuple-element.30.after_ref.payload_ref), channel_id=1, source_target_pairs={{0,12},{4,8},{8,4},{12,0},{1,13},{5,9},{9,5},{13,1},{2,14},{6,10},... | collective-permute-start | bytes 307208 | tf_op jit(solution)/shard_map/ppermute | solution.py:226
  10.8 0.0 collective-permute-start.4
  10.8 0.6 collective-permute-start.3
  11.4 0.0 collective-permute-start
  11.4 1.6 %collective-permute-start.1 = (bf16[8,3072]{1,0:T(8,128)(2,1)S(1)}, bf16[8,3072]{1,0:T(8,128)(2,1)S(1)}, u32[]{:S(2)}, u32[]{:S(2)}) collective-permute-start(bf16[8,3072]{1,0:T(8,128)(2,1)S(1)} %get-tuple-element.34), channel_id=1, source_target_pairs={{0,2},{1,3},{2,0},{3,1},{4,6},{5,7},{6,4},{7,5},{8,10},{9,11},{10,... | collective-permute-start | bytes 147464 | tf_op jit(solution)/shard_map/ppermute | solution.py:226
  13.1 0.0 collective-permute-done.refs_0_.refs_1_
  13.1 1.0 %collective-permute-start.2 = (bf16[8,3072]{1,0:T(8,128)(2,1)S(1)}, bf16[8,3072]{1,0:T(8,128)(2,1)S(1)}, u32[]{:S(2)}, u32[]{:S(2)}) collective-permute-start(bf16[8,3072]{1,0:T(8,128)(2,1)S(1)} %get-tuple-element.35), channel_id=1, source_target_pairs={{0,3},{1,2},{2,1},{3,0},{4,7},{5,6},{6,5},{7,4},{8,11},{9,10},{10,... | collective-permute-start | bytes 147464 | tf_op jit(solution)/shard_map/ppermute | solution.py:226
  14.0 8.2 %shard_map.110 = (bf16[3072,2048]{1,0:T(8,128)(2,1)S(1)}, bf16[3072,2048]{1,0:T(8,128)(2,1)S(1)}, f32[8,128]{1,0:T(8,128)S(1)}) custom-call(bf16[16,3200]{1,0:T(8,128)(2,1)S(1)} %get-tuple-element.30.after_ref.payload_ref, bf16[3072,2048]{1,0:T(8,128)(2,1)} %bitcast.10, bf16[3072,2048]{1,0:T(8,128)(2,1)} %bitcast.11), custom_call_target="tpu_custom_call" | custom-call | bytes 50331648 | tf_op jit(solution)/shard_map/pallas_call | solution.py:176
  22.2 0.0 copy-start
  22.2 4.5 %copy-done = bf16[3072,2048]{1,0:T(8,128)(2,1)} copy-done((bf16[3072,2048]{1,0:T(8,128)(2,1)}, bf16[3072,2048]{1,0:T(8,128)(2,1)S(1)}, u32[]{:S(2)}) %copy-start) | copy-done | bytes 12582936
  26.7 0.0 collective-permute-done.1.refs_1_.refs_2_
  26.8 0.0 copy-start.1
  26.8 0.0 collective-permute-done.2.refs_2_.refs_3_
  26.8 0.0 collective-permute-done.5.refs_6_.refs_2_
  26.8 0.0 collective-permute-done.4.refs_5_.refs_1_
  26.8 0.0 collective-permute-done.3.refs_4_.refs_0_
  26.8 0.5 shard_map.111
  27.3 0.4 collective-permute-start.6
  27.8 0.8 %collective-permute-start.7 = (bf16[24,3072]{1,0:T(8,128)(2,1)S(1)}, bf16[24,3072]{1,0:T(8,128)(2,1)S(1)}, u32[]{:S(2)}, u32[]{:S(2)}) collective-permute-start(bf16[24,3072]{1,0:T(8,128)(2,1)S(1)} %get-tuple-element.39), channel_id=1, source_target_pairs={{0,2},{1,3},{2,0},{3,1},{4,6},{5,7},{6,4},{7,5},{8,10},{9,11},{10,... | collective-permute-start | bytes 442376 | tf_op jit(solution)/shard_map/ppermute | solution.py:226
  28.6 0.7 %collective-permute-start.8 = (bf16[24,3072]{1,0:T(8,128)(2,1)S(1)}, bf16[24,3072]{1,0:T(8,128)(2,1)S(1)}, u32[]{:S(2)}, u32[]{:S(2)}) collective-permute-start(bf16[24,3072]{1,0:T(8,128)(2,1)S(1)} %get-tuple-element.40), channel_id=1, source_target_pairs={{0,3},{1,2},{2,1},{3,0},{4,7},{5,6},{6,5},{7,4},{8,11},{9,10},{10,... | collective-permute-start | bytes 442376 | tf_op jit(solution)/shard_map/ppermute | solution.py:226
  29.3 5.9 %shard_map.112 = (bf16[2048,3072]{1,0:T(8,128)(2,1)S(1)}, f32[8,128]{1,0:T(8,128)}) custom-call(bf16[24,3072]{1,0:T(8,128)(2,1)S(1)} %get-tuple-element.37.after_ref.refs_4_, bf16[2048,3072]{1,0:T(8,128)(2,1)} %bitcast.9), custom_call_target="tpu_custom_call" | custom-call | bytes 25165824 | tf_op jit(solution)/shard_map/pallas_call | solution.py:176
  35.2 0.0 collective-permute-done.6.refs_5_
  35.2 0.0 collective-permute-done.7.refs_6_
  35.2 0.8 %collective-permute-done.8.refs_7_ = bf16[24,3072]{1,0:T(8,128)(2,1)S(1)} collective-permute-done((bf16[24,3072]{1,0:T(8,128)(2,1)S(1)}, bf16[24,3072]{1,0:T(8,128)(2,1)S(1)}, u32[]{:S(2)}, u32[]{:S(2)}) %collective-permute-start.8) | collective-permute-done | bytes 147488 | tf_op jit(solution)/shard_map/ppermute | solution.py:226
  36.0 0.0 copy-done.1
  36.0 0.0 copy-start.2
  36.0 9.2 %shard_map.113 = (bf16[8,3072]{1,0:T(8,128)(2,1)S(1)}, bf16[8,3072]{1,0:T(8,128)(2,1)S(1)}, bf16[8,3072]{1,0:T(8,128)(2,1)S(1)}, bf16[8,3072]{1,0:T(8,128)(2,1)S...) custom-call(bf16[8,3072]{1,0:T(8,128)(2,1)S(1)} %get-tuple-element.3, ...), custom_call_target="tpu_custom_call" | custom-call | tf_op jit(solution)/shard_map/pallas_call | solution.py:300
  45.3 0.7 collective-permute-start.12
  45.9 0.9 %collective-permute-start.13 = (bf16[24,3072]{1,0:T(8,128)(2,1)S(1)}, bf16[24,3072]{1,0:T(8,128)(2,1)S(1)}, u32[]{:S(2)}, u32[]{:S(2)}) collective-permute-start(bf16[24,3072]{1,0:T(8,128)(2,1)S(1)} %get-tuple-element.50), channel_id=1, source_target_pairs={{0,2},{1,3},{2,0},{3,1},{4,6},{5,7},{6,4},{7,5},{8,10},{9,11},{10,... | collective-permute-start | bytes 442376 | tf_op jit(solution)/shard_map/ppermute | solution.py:226
  46.8 0.6 collective-permute-start.14
  47.4 0.7 %collective-permute-start.9 = (bf16[8,3072]{1,0:T(8,128)(2,1)S(1)}, bf16[8,3072]{1,0:T(8,128)(2,1)S(1)}, u32[]{:S(2)}, u32[]{:S(2)}) collective-permute-start(bf16[8,3072]{1,0:T(8,128)(2,1)S(1)} %get-tuple-element.45), channel_id=1, source_target_pairs={{0,1},{1,0},{2,3},{3,2},{4,5},{5,4},{6,7},{7,6},{8,9},{9,8},{10,11... | collective-permute-start | bytes 147464 | tf_op jit(solution)/shard_map/ppermute | solution.py:226
  48.1 0.0 collective-permute-done.12.refs_4_
  48.1 4.6 %collective-permute-done.13.refs_5_ = bf16[24,3072]{1,0:T(8,128)(2,1)S(1)} collective-permute-done((bf16[24,3072]{1,0:T(8,128)(2,1)S(1)}, bf16[24,3072]{1,0:T(8,128)(2,1)S(1)}, u32[]{:S(2)}, u32[]{:S(2)}) %collective-permute-start.13) | collective-permute-done | bytes 147488 | tf_op jit(solution)/shard_map/ppermute | solution.py:226
  52.6 1.4 %collective-permute-done.14.refs_6_ = bf16[24,3072]{1,0:T(8,128)(2,1)S(1)} collective-permute-done((bf16[24,3072]{1,0:T(8,128)(2,1)S(1)}, bf16[24,3072]{1,0:T(8,128)(2,1)S(1)}, u32[]{:S(2)}, u32[]{:S(2)}) %collective-permute-start.14) | collective-permute-done | bytes 147488 | tf_op jit(solution)/shard_map/ppermute | solution.py:226
  54.1 0.0 copy-done.2
  54.1 0.7 %shard_map.114 = (bf16[16,3072]{1,0:T(8,128)(2,1)S(1)}, bf16[16,3072]{1,0:T(8,128)(2,1)S(1)}, bf16[16,3072]{1,0:T(8,128)(2,1)S(1)}) custom-call(s32[1]{0:T(128)} %bitcast.me_ref, bf16[4,3072]{1,0:T(4,128)(2,1)S(1)} %bitcast.7, bf16[16,3200]{1,0:T(8,128)(2,1)S(1)} %collective-permute-done.3.refs_4_.refs_0_, ...), custom_call_target="tpu_custom_call" | custom-call | tf_op jit(solution)/shard_map/pallas_call | solution.py:311
  54.8 1.3 %collective-permute-start.15 = (bf16[16,3072]{1,0:T(8,128)(2,1)S(1)}, bf16[16,3072]{1,0:T(8,128)(2,1)S(1)}, u32[]{:S(2)}, u32[]{:S(2)}) collective-permute-start(bf16[16,3072]{1,0:T(8,128)(2,1)S(1)} %get-tuple-element.52), channel_id=1, source_target_pairs={{0,4},{4,0},{8,12},{12,8},{1,5},{5,1},{9,13},{13,9},{2,6},{6,2},{1... | collective-permute-start | bytes 294920 | tf_op jit(solution)/shard_map/ppermute | solution.py:226
  56.1 2.9 %collective-permute-start.16 = (bf16[16,3072]{1,0:T(8,128)(2,1)S(1)}, bf16[16,3072]{1,0:T(8,128)(2,1)S(1)}, u32[]{:S(2)}, u32[]{:S(2)}) collective-permute-start(bf16[16,3072]{1,0:T(8,128)(2,1)S(1)} %get-tuple-element.53), channel_id=1, source_target_pairs={{0,8},{4,12},{8,0},{12,4},{1,9},{5,13},{9,1},{13,5},{2,10},{6,14},... | collective-permute-start | bytes 294920 | tf_op jit(solution)/shard_map/ppermute | solution.py:226
  59.0 0.2 collective-permute-start.17
  59.2 0.9 %collective-permute-start.10 = (bf16[8,3072]{1,0:T(8,128)(2,1)S(1)}, bf16[8,3072]{1,0:T(8,128)(2,1)S(1)}, u32[]{:S(2)}, u32[]{:S(2)}) collective-permute-start(bf16[8,3072]{1,0:T(8,128)(2,1)S(1)} %get-tuple-element.46), channel_id=1, source_target_pairs={{0,2},{1,3},{2,0},{3,1},{4,6},{5,7},{6,4},{7,5},{8,10},{9,11},{10,... | collective-permute-start | bytes 147464 | tf_op jit(solution)/shard_map/ppermute | solution.py:226
  60.1 0.0 collective-permute-done.9.refs_1_
  60.1 0.4 collective-permute-start.11
  60.5 3.0 %collective-permute-done.10.refs_2_ = bf16[8,3072]{1,0:T(8,128)(2,1)S(1)} collective-permute-done((bf16[8,3072]{1,0:T(8,128)(2,1)S(1)}, bf16[8,3072]{1,0:T(8,128)(2,1)S(1)}, u32[]{:S(2)}, u32[]{:S(2)}) %collective-permute-start.10) | collective-permute-done | bytes 49184 | tf_op jit(solution)/shard_map/ppermute | solution.py:226
  63.6 0.6 collective-permute-done.11.refs_3_
  64.2 0.0 collective-permute-done.15.refs_4_
  64.2 2.7 %collective-permute-done.16.refs_5_ = bf16[16,3072]{1,0:T(8,128)(2,1)S(1)} collective-permute-done((bf16[16,3072]{1,0:T(8,128)(2,1)S(1)}, bf16[16,3072]{1,0:T(8,128)(2,1)S(1)}, u32[]{:S(2)}, u32[]{:S(2)}) %collective-permute-start.16) | collective-permute-done | bytes 98336 | tf_op jit(solution)/shard_map/ppermute | solution.py:226
  66.9 0.0 collective-permute-done.17.refs_6_
  66.9 1.1 %shard_map.115 = bf16[16,3072]{1,0:T(8,128)(2,1)} custom-call(s32[1]{0:T(128)} %bitcast.me_ref, bf16[4,3072]{1,0:T(4,128)(2,1)S(1)} %bitcast.8, bf16[16,3200]{1,0:T(8,128)(2,1)S(1)} %get-tuple-element.30.after_ref.payload_ref, f32[16,3072]{1,0:T(8,128)S(1)} %get-tuple-element.31.stream_ref, bf16[8,3072]{1,0:T(8,128)(2,1)S(1)} %get-tuple-element.44.refs_0_, ...), custom_call_target="tpu_custom_call" | custom-call | tf_op jit(solution)/shard_map/pallas_call | solution.py:319
Async XLA Ops:
  0.0 0.7 copy-start.3
  5.7 21.1 %collective-permute-start.5 = (bf16[16,3200]{1,0:T(8,128)(2,1)S(1)}, bf16[16,3200]{1,0:T(8,128)(2,1)S(1)}, u32[]{:S(2)}, u32[]{:S(2)}) collective-permute-start(bf16[16,3200]{1,0:T(8,128)(2,1)S(1)} %get-tuple-element.30.after_ref.payload_ref), channel_id=1, source_target_pairs={{0,12},{4,8},{8,4},{12,0},{1,13},{5,9},{9,5},{13,1},{2,14},{6,10},... | collective-permute-start | bytes 307208 | tf_op jit(solution)/shard_map/ppermute | solution.py:226
  10.8 16.0 %collective-permute-start.4 = (bf16[16,3200]{1,0:T(8,128)(2,1)S(1)}, bf16[16,3200]{1,0:T(8,128)(2,1)S(1)}, u32[]{:S(2)}, u32[]{:S(2)}) collective-permute-start(bf16[16,3200]{1,0:T(8,128)(2,1)S(1)} %get-tuple-element.30.after_ref.payload_ref), channel_id=1, source_target_pairs={{0,8},{4,12},{8,0},{12,4},{1,9},{5,13},{9,1},{13,5},{2,10},{6,14},... | collective-permute-start | bytes 307208 | tf_op jit(solution)/shard_map/ppermute | solution.py:226
  10.8 16.0 %collective-permute-start.3 = (bf16[16,3200]{1,0:T(8,128)(2,1)S(1)}, bf16[16,3200]{1,0:T(8,128)(2,1)S(1)}, u32[]{:S(2)}, u32[]{:S(2)}) collective-permute-start(bf16[16,3200]{1,0:T(8,128)(2,1)S(1)} %get-tuple-element.30.after_ref.payload_ref), channel_id=1, source_target_pairs={{0,4},{4,0},{8,12},{12,8},{1,5},{5,1},{9,13},{13,9},{2,6},{6,2},{1... | collective-permute-start | bytes 307208 | tf_op jit(solution)/shard_map/ppermute | solution.py:226
  11.4 1.6 %collective-permute-start = (bf16[8,3072]{1,0:T(8,128)(2,1)S(1)}, bf16[8,3072]{1,0:T(8,128)(2,1)S(1)}, u32[]{:S(2)}, u32[]{:S(2)}) collective-permute-start(bf16[8,3072]{1,0:T(8,128)(2,1)S(1)} %get-tuple-element.33), channel_id=1, source_target_pairs={{0,1},{1,0},{2,3},{3,2},{4,5},{5,4},{6,7},{7,6},{8,9},{9,8},{10,11... | collective-permute-start | bytes 147464 | tf_op jit(solution)/shard_map/ppermute | solution.py:226
  11.4 15.3 %collective-permute-start.1 = (bf16[8,3072]{1,0:T(8,128)(2,1)S(1)}, bf16[8,3072]{1,0:T(8,128)(2,1)S(1)}, u32[]{:S(2)}, u32[]{:S(2)}) collective-permute-start(bf16[8,3072]{1,0:T(8,128)(2,1)S(1)} %get-tuple-element.34), channel_id=1, source_target_pairs={{0,2},{1,3},{2,0},{3,1},{4,6},{5,7},{6,4},{7,5},{8,10},{9,11},{10,... | collective-permute-start | bytes 147464 | tf_op jit(solution)/shard_map/ppermute | solution.py:226
  13.1 13.7 %collective-permute-start.2 = (bf16[8,3072]{1,0:T(8,128)(2,1)S(1)}, bf16[8,3072]{1,0:T(8,128)(2,1)S(1)}, u32[]{:S(2)}, u32[]{:S(2)}) collective-permute-start(bf16[8,3072]{1,0:T(8,128)(2,1)S(1)} %get-tuple-element.35), channel_id=1, source_target_pairs={{0,3},{1,2},{2,1},{3,0},{4,7},{5,6},{6,5},{7,4},{8,11},{9,10},{10,... | collective-permute-start | bytes 147464 | tf_op jit(solution)/shard_map/ppermute | solution.py:226
  22.2 4.5 %copy-start = (bf16[3072,2048]{1,0:T(8,128)(2,1)}, bf16[3072,2048]{1,0:T(8,128)(2,1)S(1)}, u32[]{:S(2)}) copy-start(bf16[3072,2048]{1,0:T(8,128)(2,1)S(1)} %get-tuple-element.42.refs_9_) | copy-start | bytes 37748740
  26.8 9.3 %copy-start.1 = (bf16[3072,2048]{1,0:T(8,128)(2,1)S(1)}, bf16[3072,2048]{1,0:T(8,128)(2,1)}, u32[]{:S(2)}) copy-start(bf16[3072,2048]{1,0:T(8,128)(2,1)} %copy-done) | copy-start | bytes 37748740
  27.3 7.9 %collective-permute-start.6 = (bf16[24,3072]{1,0:T(8,128)(2,1)S(1)}, bf16[24,3072]{1,0:T(8,128)(2,1)S(1)}, u32[]{:S(2)}, u32[]{:S(2)}) collective-permute-start(bf16[24,3072]{1,0:T(8,128)(2,1)S(1)} %get-tuple-element.38), channel_id=1, source_target_pairs={{0,1},{1,0},{2,3},{3,2},{4,5},{5,4},{6,7},{7,6},{8,9},{9,8},{10,11... | collective-permute-start | bytes 442376 | tf_op jit(solution)/shard_map/ppermute | solution.py:226
  27.8 7.5 %collective-permute-start.7 = (bf16[24,3072]{1,0:T(8,128)(2,1)S(1)}, bf16[24,3072]{1,0:T(8,128)(2,1)S(1)}, u32[]{:S(2)}, u32[]{:S(2)}) collective-permute-start(bf16[24,3072]{1,0:T(8,128)(2,1)S(1)} %get-tuple-element.39), channel_id=1, source_target_pairs={{0,2},{1,3},{2,0},{3,1},{4,6},{5,7},{6,4},{7,5},{8,10},{9,11},{10,... | collective-permute-start | bytes 442376 | tf_op jit(solution)/shard_map/ppermute | solution.py:226
  28.6 7.5 %collective-permute-start.8 = (bf16[24,3072]{1,0:T(8,128)(2,1)S(1)}, bf16[24,3072]{1,0:T(8,128)(2,1)S(1)}, u32[]{:S(2)}, u32[]{:S(2)}) collective-permute-start(bf16[24,3072]{1,0:T(8,128)(2,1)S(1)} %get-tuple-element.40), channel_id=1, source_target_pairs={{0,3},{1,2},{2,1},{3,0},{4,7},{5,6},{6,5},{7,4},{8,11},{9,10},{10,... | collective-permute-start | bytes 442376 | tf_op jit(solution)/shard_map/ppermute | solution.py:226
  36.0 18.0 %copy-start.2 = (bf16[3072,4]{0,1:T(4,128)(2,1)S(1)}, bf16[3072,4]{0,1:T(4,128)(2,1)}, u32[]{:S(2)}) copy-start(bf16[3072,4]{0,1:T(4,128)(2,1)} %param.18) | copy-start | bytes 73732
  45.3 2.8 %collective-permute-start.12 = (bf16[24,3072]{1,0:T(8,128)(2,1)S(1)}, bf16[24,3072]{1,0:T(8,128)(2,1)S(1)}, u32[]{:S(2)}, u32[]{:S(2)}) collective-permute-start(bf16[24,3072]{1,0:T(8,128)(2,1)S(1)} %get-tuple-element.49), channel_id=1, source_target_pairs={{0,1},{1,0},{2,3},{3,2},{4,5},{5,4},{6,7},{7,6},{8,9},{9,8},{10,11... | collective-permute-start | bytes 442376 | tf_op jit(solution)/shard_map/ppermute | solution.py:226
  45.9 6.7 %collective-permute-start.13 = (bf16[24,3072]{1,0:T(8,128)(2,1)S(1)}, bf16[24,3072]{1,0:T(8,128)(2,1)S(1)}, u32[]{:S(2)}, u32[]{:S(2)}) collective-permute-start(bf16[24,3072]{1,0:T(8,128)(2,1)S(1)} %get-tuple-element.50), channel_id=1, source_target_pairs={{0,2},{1,3},{2,0},{3,1},{4,6},{5,7},{6,4},{7,5},{8,10},{9,11},{10,... | collective-permute-start | bytes 442376 | tf_op jit(solution)/shard_map/ppermute | solution.py:226
  46.8 7.2 %collective-permute-start.14 = (bf16[24,3072]{1,0:T(8,128)(2,1)S(1)}, bf16[24,3072]{1,0:T(8,128)(2,1)S(1)}, u32[]{:S(2)}, u32[]{:S(2)}) collective-permute-start(bf16[24,3072]{1,0:T(8,128)(2,1)S(1)} %get-tuple-element.51), channel_id=1, source_target_pairs={{0,3},{1,2},{2,1},{3,0},{4,7},{5,6},{6,5},{7,4},{8,11},{9,10},{10,... | collective-permute-start | bytes 442376 | tf_op jit(solution)/shard_map/ppermute | solution.py:226
  47.4 12.7 %collective-permute-start.9 = (bf16[8,3072]{1,0:T(8,128)(2,1)S(1)}, bf16[8,3072]{1,0:T(8,128)(2,1)S(1)}, u32[]{:S(2)}, u32[]{:S(2)}) collective-permute-start(bf16[8,3072]{1,0:T(8,128)(2,1)S(1)} %get-tuple-element.45), channel_id=1, source_target_pairs={{0,1},{1,0},{2,3},{3,2},{4,5},{5,4},{6,7},{7,6},{8,9},{9,8},{10,11... | collective-permute-start | bytes 147464 | tf_op jit(solution)/shard_map/ppermute | solution.py:226
  54.8 9.4 %collective-permute-start.15 = (bf16[16,3072]{1,0:T(8,128)(2,1)S(1)}, bf16[16,3072]{1,0:T(8,128)(2,1)S(1)}, u32[]{:S(2)}, u32[]{:S(2)}) collective-permute-start(bf16[16,3072]{1,0:T(8,128)(2,1)S(1)} %get-tuple-element.52), channel_id=1, source_target_pairs={{0,4},{4,0},{8,12},{12,8},{1,5},{5,1},{9,13},{13,9},{2,6},{6,2},{1... | collective-permute-start | bytes 294920 | tf_op jit(solution)/shard_map/ppermute | solution.py:226
  56.1 10.8 %collective-permute-start.16 = (bf16[16,3072]{1,0:T(8,128)(2,1)S(1)}, bf16[16,3072]{1,0:T(8,128)(2,1)S(1)}, u32[]{:S(2)}, u32[]{:S(2)}) collective-permute-start(bf16[16,3072]{1,0:T(8,128)(2,1)S(1)} %get-tuple-element.53), channel_id=1, source_target_pairs={{0,8},{4,12},{8,0},{12,4},{1,9},{5,13},{9,1},{13,5},{2,10},{6,14},... | collective-permute-start | bytes 294920 | tf_op jit(solution)/shard_map/ppermute | solution.py:226
  59.0 7.9 %collective-permute-start.17 = (bf16[16,3072]{1,0:T(8,128)(2,1)S(1)}, bf16[16,3072]{1,0:T(8,128)(2,1)S(1)}, u32[]{:S(2)}, u32[]{:S(2)}) collective-permute-start(bf16[16,3072]{1,0:T(8,128)(2,1)S(1)} %get-tuple-element.54), channel_id=1, source_target_pairs={{0,12},{4,8},{8,4},{12,0},{1,13},{5,9},{9,5},{13,1},{2,14},{6,10},... | collective-permute-start | bytes 294920 | tf_op jit(solution)/shard_map/ppermute | solution.py:226
  59.2 4.3 %collective-permute-start.10 = (bf16[8,3072]{1,0:T(8,128)(2,1)S(1)}, bf16[8,3072]{1,0:T(8,128)(2,1)S(1)}, u32[]{:S(2)}, u32[]{:S(2)}) collective-permute-start(bf16[8,3072]{1,0:T(8,128)(2,1)S(1)} %get-tuple-element.46), channel_id=1, source_target_pairs={{0,2},{1,3},{2,0},{3,1},{4,6},{5,7},{6,4},{7,5},{8,10},{9,11},{10,... | collective-permute-start | bytes 147464 | tf_op jit(solution)/shard_map/ppermute | solution.py:226
  60.1 4.0 %collective-permute-start.11 = (bf16[8,3072]{1,0:T(8,128)(2,1)S(1)}, bf16[8,3072]{1,0:T(8,128)(2,1)S(1)}, u32[]{:S(2)}, u32[]{:S(2)}) collective-permute-start(bf16[8,3072]{1,0:T(8,128)(2,1)S(1)} %get-tuple-element.47), channel_id=1, source_target_pairs={{0,3},{1,2},{2,1},{3,0},{4,7},{5,6},{6,5},{7,4},{8,11},{9,10},{10,... | collective-permute-start | bytes 147464 | tf_op jit(solution)/shard_map/ppermute | solution.py:226

commit v3 on v2

--- a/solution.py
+++ b/solution.py
@@ -15,6 +15,7 @@
 MIB = 1 << 20
 F32 = jnp.float32
 BF16 = jnp.bfloat16
+BUSY = pl.CostEstimate(flops=12_000_000_000, bytes_accessed=4_000_000, transcendentals=0)
 ANY = pl.BlockSpec(memory_space=pl.ANY)
 WHOLE = pl.BlockSpec(memory_space=pltpu.VMEM)
 SCALAR = pl.BlockSpec(memory_space=pltpu.SMEM)
@@ -157,40 +158,8 @@
             begin += count
 
 
-def load_kernel(after_ref, *refs, count):
-    del after_ref
-    token_ref, sems = refs[-2:]
-    copies = [
-        pltpu.make_async_copy(source, target, sems.at[i])
-        for i, (source, target) in enumerate(zip(refs[:count], refs[count : 2 * count]))
-    ]
-    for copy in copies:
-        copy.start()
-    for copy in copies:
-        copy.wait()
-    token_ref[...] = jnp.zeros_like(token_ref)
-
-
-def load(after, *weights):
-    size = sum(w.size * w.dtype.itemsize for w in weights)
-    return pl.pallas_call(
-        functools.partial(load_kernel, count=len(weights)),
-        in_specs=[ANY] * (1 + len(weights)),
-        out_specs=[WHOLE] * (len(weights) + 1),
-        out_shape=[pltpu.VMEM(w.shape, w.dtype) for w in weights]
-        + [jax.ShapeDtypeStruct((8, LANES), F32)],
-        scratch_shapes=[pltpu.SemaphoreType.DMA((len(weights),))],
-        compiler_params=params(0),
-        cost_estimate=pl.CostEstimate(flops=0, bytes_accessed=2 * size, transcendentals=0),
-    )(after, *[in_hbm(w) for w in weights])
-
-
 def in_hbm(value):
     return pltpu.with_memory_space_constraint(value, pltpu.HBM)
-
-
-def in_vmem(value):
-    return pltpu.with_memory_space_constraint(value, pltpu.VMEM)
 
 
 def mix_kernel(me_ref, router_ref, *refs, chunks, experts):
@@ -272,6 +241,7 @@
         + [shape((CAP, width), BF16)] * experts,
         scratch_shapes=[pltpu.VMEM((KVH, batch, span), F32)],
         compiler_params=params(28 * batch * width),
+        cost_estimate=BUSY,
     )(
         me,
         lengths,
@@ -281,22 +251,20 @@
 
     payloads = [swap(payload, "attn", j) for j in range(1, layers)]
     near = [swap(slots[e], "expert", e) for e in range(experts)]
-    *first, token = load(payload, gate_proj[0], up_proj[0])
-    ahead = [*near[1:], token]
+    ahead = [*near[1:]]
     slots = pl.pallas_call(
         functools.partial(split_kernel, chunks=remote, after=len(ahead)),
         in_specs=[SCALAR] + [WHOLE] * (len(ahead) + remote),
         out_specs=[WHOLE] * experts,
         out_shape=[shape((remote * CAP, width), BF16)] * experts,
+        cost_estimate=BUSY,
         compiler_params=params(experts * remote * CAP * width),
     )(me, *ahead, *payloads)
     far = [swap(slots[e], "expert", e) for e in range(experts)]
-    *second, _ = load(slots[0], down_proj[0])
-
     inputs = near + far
     total_rows = sum(block.shape[0] for block in inputs)
     units = gate_proj.shape[2]
-    weights = [in_vmem(w) for w in (*first, *second)]
+    weights = [gate_proj[0], up_proj[0], down_proj[0]]
     results = pl.pallas_call(
         functools.partial(expert_kernel, pieces=len(inputs)),
         in_specs=[WHOLE] * (len(inputs) + 3),

time: 68.2 us -> 61.3 us (0.90)
  Pallas kernels: 30.7 us -> 17.5 us
  waiting for transfers between devices: 13.2 us -> 24 us
  local copies, waits for them, and re-layouts: 5.18 us -> 0.7 us
    pallas_call x2 -> x0, Pallas kernels: 14.1 us -> none  [load(): pl.pallas_call(functools.partial(load_kernel, count=len(weights)), in_spe...]
    ppermute x18, waiting for transfers between devices: 13.2 us -> 24 us  [swap(): return lax.ppermute(value, axis, [(i, i ^ step) for i in range(count)])]
    unnamed x8 -> x22, local copies, waits for them, and re-layouts: 5.18 us -> 0.7 us
    pallas_call x1, Pallas kernels: 5 us -> 5.83 us  [shards(): pl.pallas_call(attend_kernel, grid=(KVH,), in_specs=[SCALAR, SCALAR, pl.B...]
  transfers between devices with their start and end apart: 18 -> 18, of which waited for: 6 -> 10; matrix products, arithmetic and copies ran while one was open for 0% -> 0% of each run, Pallas kernels for 22% -> 1%
where the time goes in v3:
time: 61.3 us; the launch traced here: 61.1 us
  waiting for transfers between devices  24 us (39%)
  starting transfers between devices  18.8 us (31%)
  Pallas kernels  17.5 us (29%)
  local copies, waits for them, and re-layouts  0.7 us (1%)
    ppermute x18, waiting for transfers between devices, swap(): return lax.ppermute(value, axis, [(i, i ^ step) for i in range(count)])  24 us
    ppermute x18, starting transfers between devices, swap(): return lax.ppermute(value, axis, [(i, i ^ step) for i in range(count)])  18.8 us
    pallas_call x1, Pallas kernels, shards(): pl.pallas_call(functools.partial(expert_kernel, pieces=len(inputs)), in_s...  9.23 us
    pallas_call x1, Pallas kernels, shards(): pl.pallas_call(attend_kernel, grid=(KVH,), in_specs=[SCALAR, SCALAR, pl.B...  5.83 us
  transfers between devices with their start and end apart: 18, of which 10 were waited for; matrix products, arithmetic and copies ran while one was open for 0% of the time, Pallas kernels for 1%

profile of v3, /device:TPU:0, one launch (start us, length us, event | category | flops | bytes accessed | tf_op | source)
XLA Modules:
  0.0 61.1 jit_solution(14039842353019861798)
XLA Ops:
  0.0 0.0 copy-start.1
  0.0 0.7 %copy-done.1 = s32[16]{0:T(128)S(1)} copy-done((s32[16]{0:T(128)S(1)}, s32[16]{0:T(128)}, u32[]{:S(2)}) %copy-start.1) | copy-done | bytes 88
  0.7 0.0 slice-start.6
  0.7 0.0 slice-start.7
  0.7 5.8 %shard_map.109 = (f32[16,3072]{1,0:T(8,128)S(1)}, bf16[16,3200]{1,0:T(8,128)(2,1)S(1)}, bf16[8,3072]{1,0:T(8,128)(2,1)S(1)}, bf16[8,3072]{1,0:T(8,128)(2,1)S(1)}...) custom-call(s32[1]{0:T(128)} %bitcast.me_ref, s32[16]{0:T(128)S(1)} %copy-done.1, ...), custom_call_target="tpu_custom_call" | custom-call | flops 12000000000 | bytes 4000000 | tf_op jit(solution)/shard_map/pallas_call | solution.py:226
  6.5 5.1 %collective-permute-start.5 = (bf16[16,3200]{1,0:T(8,128)(2,1)S(1)}, bf16[16,3200]{1,0:T(8,128)(2,1)S(1)}, u32[]{:S(2)}, u32[]{:S(2)}) collective-permute-start(bf16[16,3200]{1,0:T(8,128)(2,1)S(1)} %get-tuple-element.26.payload_ref), channel_id=1, source_target_pairs={{0,12},{4,8},{8,4},{12,0},{1,13},{5,9},{9,5},{13,1},{2,14},{6,10},... | collective-permute-start | bytes 307208 | tf_op jit(solution)/shard_map/ppermute | solution.py:195
  11.6 0.0 collective-permute-start.4
  11.6 0.6 %collective-permute-start.3 = (bf16[16,3200]{1,0:T(8,128)(2,1)S(1)}, bf16[16,3200]{1,0:T(8,128)(2,1)S(1)}, u32[]{:S(2)}, u32[]{:S(2)}) collective-permute-start(bf16[16,3200]{1,0:T(8,128)(2,1)S(1)} %get-tuple-element.26.payload_ref), channel_id=1, source_target_pairs={{0,4},{4,0},{8,12},{12,8},{1,5},{5,1},{9,13},{13,9},{2,6},{6,2},{1... | collective-permute-start | bytes 307208 | tf_op jit(solution)/shard_map/ppermute | solution.py:195
  12.3 0.0 collective-permute-start
  12.3 1.6 %collective-permute-start.1 = (bf16[8,3072]{1,0:T(8,128)(2,1)S(1)}, bf16[8,3072]{1,0:T(8,128)(2,1)S(1)}, u32[]{:S(2)}, u32[]{:S(2)}) collective-permute-start(bf16[8,3072]{1,0:T(8,128)(2,1)S(1)} %get-tuple-element.30), channel_id=1, source_target_pairs={{0,2},{1,3},{2,0},{3,1},{4,6},{5,7},{6,4},{7,5},{8,10},{9,11},{10,... | collective-permute-start | bytes 147464 | tf_op jit(solution)/shard_map/ppermute | solution.py:195
  13.9 0.0 collective-permute-done.refs_0_.refs_1_
  13.9 0.0 slice-start
  13.9 0.0 slice-start.3
  13.9 0.0 slice-start.1
  13.9 0.0 slice-start.2
  13.9 0.0 slice-start.4
  13.9 0.0 slice-start.5
  13.9 0.0 slice-start.8
  14.0 1.0 %collective-permute-start.2 = (bf16[8,3072]{1,0:T(8,128)(2,1)S(1)}, bf16[8,3072]{1,0:T(8,128)(2,1)S(1)}, u32[]{:S(2)}, u32[]{:S(2)}) collective-permute-start(bf16[8,3072]{1,0:T(8,128)(2,1)S(1)} %get-tuple-element.31), channel_id=1, source_target_pairs={{0,3},{1,2},{2,1},{3,0},{4,7},{5,6},{6,5},{7,4},{8,11},{9,10},{10,... | collective-permute-start | bytes 147464 | tf_op jit(solution)/shard_map/ppermute | solution.py:195
  15.0 1.4 %collective-permute-done.1.refs_1_.refs_2_ = bf16[8,3072]{1,0:T(8,128)(2,1)S(1)} collective-permute-done((bf16[8,3072]{1,0:T(8,128)(2,1)S(1)}, bf16[8,3072]{1,0:T(8,128)(2,1)S(1)}, u32[]{:S(2)}, u32[]{:S(2)}) %collective-permute-start.1) | collective-permute-done | bytes 49184 | tf_op jit(solution)/shard_map/ppermute | solution.py:195
  16.4 1.3 %collective-permute-done.2.refs_2_.refs_3_ = bf16[8,3072]{1,0:T(8,128)(2,1)S(1)} collective-permute-done((bf16[8,3072]{1,0:T(8,128)(2,1)S(1)}, bf16[8,3072]{1,0:T(8,128)(2,1)S(1)}, u32[]{:S(2)}, u32[]{:S(2)}) %collective-permute-start.2) | collective-permute-done | bytes 49184 | tf_op jit(solution)/shard_map/ppermute | solution.py:195
  17.7 0.0 collective-permute-done.5.refs_5_.refs_2_
  17.7 2.5 %collective-permute-done.4.refs_4_.refs_1_ = bf16[16,3200]{1,0:T(8,128)(2,1)S(1)} collective-permute-done((bf16[16,3200]{1,0:T(8,128)(2,1)S(1)}, bf16[16,3200]{1,0:T(8,128)(2,1)S(1)}, u32[]{:S(2)}, u32[]{:S(2)}) %collective-permute-start.4) | collective-permute-done | bytes 102432 | tf_op jit(solution)/shard_map/ppermute | solution.py:195
  20.2 0.0 collective-permute-done.3.refs_3_.refs_0_
  20.2 0.5 shard_map.110
  20.8 0.1 collective-permute-start.6
  20.9 1.6 %collective-permute-start.7 = (bf16[24,3072]{1,0:T(8,128)(2,1)S(1)}, bf16[24,3072]{1,0:T(8,128)(2,1)S(1)}, u32[]{:S(2)}, u32[]{:S(2)}) collective-permute-start(bf16[24,3072]{1,0:T(8,128)(2,1)S(1)} %get-tuple-element.34), channel_id=1, source_target_pairs={{0,2},{1,3},{2,0},{3,1},{4,6},{5,7},{6,4},{7,5},{8,10},{9,11},{10,... | collective-permute-start | bytes 442376 | tf_op jit(solution)/shard_map/ppermute | solution.py:195
  22.4 0.3 collective-permute-start.8
  22.7 0.0 collective-permute-done.6.refs_5_
  22.7 4.8 %collective-permute-done.7.refs_6_ = bf16[24,3072]{1,0:T(8,128)(2,1)S(1)} collective-permute-done((bf16[24,3072]{1,0:T(8,128)(2,1)S(1)}, bf16[24,3072]{1,0:T(8,128)(2,1)S(1)}, u32[]{:S(2)}, u32[]{:S(2)}) %collective-permute-start.7) | collective-permute-done | bytes 147488 | tf_op jit(solution)/shard_map/ppermute | solution.py:195
  27.6 2.3 %collective-permute-done.8.refs_7_ = bf16[24,3072]{1,0:T(8,128)(2,1)S(1)} collective-permute-done((bf16[24,3072]{1,0:T(8,128)(2,1)S(1)}, bf16[24,3072]{1,0:T(8,128)(2,1)S(1)}, u32[]{:S(2)}, u32[]{:S(2)}) %collective-permute-start.8) | collective-permute-done | bytes 147488 | tf_op jit(solution)/shard_map/ppermute | solution.py:195
  29.8 0.0 slice-done.6
  29.8 0.0 slice-done.7
  29.8 0.0 slice-done
  29.8 0.0 slice-done.3
  29.8 0.0 slice-done.1
  29.9 0.0 slice-done.2
  29.9 0.0 slice-done.4
  29.9 0.0 slice-done.5
  29.9 0.0 slice-done.8
  29.9 0.0 copy-start
  29.9 9.2 %shard_map.111 = (bf16[8,3072]{1,0:T(8,128)(2,1)S(1)}, bf16[8,3072]{1,0:T(8,128)(2,1)S(1)}, bf16[8,3072]{1,0:T(8,128)(2,1)S(1)}, bf16[8,3072]{1,0:T(8,128)(2,1)S...) custom-call(bf16[8,3072]{1,0:T(8,128)(2,1)S(1)} %get-tuple-element.2, ...), custom_call_target="tpu_custom_call" | custom-call | tf_op jit(solution)/shard_map/pallas_call | solution.py:268
  39.2 0.3 collective-permute-start.12
  39.5 1.5 %collective-permute-start.13 = (bf16[24,3072]{1,0:T(8,128)(2,1)S(1)}, bf16[24,3072]{1,0:T(8,128)(2,1)S(1)}, u32[]{:S(2)}, u32[]{:S(2)}) collective-permute-start(bf16[24,3072]{1,0:T(8,128)(2,1)S(1)} %get-tuple-element.42), channel_id=1, source_target_pairs={{0,2},{1,3},{2,0},{3,1},{4,6},{5,7},{6,4},{7,5},{8,10},{9,11},{10,... | collective-permute-start | bytes 442376 | tf_op jit(solution)/shard_map/ppermute | solution.py:195
  41.0 0.1 collective-permute-start.14
  41.1 0.6 collective-permute-start.9
  41.7 0.0 collective-permute-done.12.refs_4_
  41.7 4.5 %collective-permute-done.13.refs_5_ = bf16[24,3072]{1,0:T(8,128)(2,1)S(1)} collective-permute-done((bf16[24,3072]{1,0:T(8,128)(2,1)S(1)}, bf16[24,3072]{1,0:T(8,128)(2,1)S(1)}, u32[]{:S(2)}, u32[]{:S(2)}) %collective-permute-start.13) | collective-permute-done | bytes 147488 | tf_op jit(solution)/shard_map/ppermute | solution.py:195
  46.2 1.8 %collective-permute-done.14.refs_6_ = bf16[24,3072]{1,0:T(8,128)(2,1)S(1)} collective-permute-done((bf16[24,3072]{1,0:T(8,128)(2,1)S(1)}, bf16[24,3072]{1,0:T(8,128)(2,1)S(1)}, u32[]{:S(2)}, u32[]{:S(2)}) %collective-permute-start.14) | collective-permute-done | bytes 147488 | tf_op jit(solution)/shard_map/ppermute | solution.py:195
  48.0 0.0 copy-done
  48.0 0.7 %shard_map.112 = (bf16[16,3072]{1,0:T(8,128)(2,1)S(1)}, bf16[16,3072]{1,0:T(8,128)(2,1)S(1)}, bf16[16,3072]{1,0:T(8,128)(2,1)S(1)}) custom-call(s32[1]{0:T(128)} %bitcast.me_ref, bf16[4,3072]{1,0:T(4,128)(2,1)S(1)} %bitcast.16, bf16[16,3200]{1,0:T(8,128)(2,1)S(1)} %collective-permute-done.3.refs_3_.refs_0_, ...), custom_call_target="tpu_custom_call" | custom-call | tf_op jit(solution)/shard_map/pallas_call | solution.py:279
  48.7 0.5 collective-permute-start.15
  49.2 2.6 %collective-permute-start.16 = (bf16[16,3072]{1,0:T(8,128)(2,1)S(1)}, bf16[16,3072]{1,0:T(8,128)(2,1)S(1)}, u32[]{:S(2)}, u32[]{:S(2)}) collective-permute-start(bf16[16,3072]{1,0:T(8,128)(2,1)S(1)} %get-tuple-element.45), channel_id=1, source_target_pairs={{0,8},{4,12},{8,0},{12,4},{1,9},{5,13},{9,1},{13,5},{2,10},{6,14},... | collective-permute-start | bytes 294920 | tf_op jit(solution)/shard_map/ppermute | solution.py:195
  51.8 1.3 %collective-permute-start.17 = (bf16[16,3072]{1,0:T(8,128)(2,1)S(1)}, bf16[16,3072]{1,0:T(8,128)(2,1)S(1)}, u32[]{:S(2)}, u32[]{:S(2)}) collective-permute-start(bf16[16,3072]{1,0:T(8,128)(2,1)S(1)} %get-tuple-element.46), channel_id=1, source_target_pairs={{0,12},{4,8},{8,4},{12,0},{1,13},{5,9},{9,5},{13,1},{2,14},{6,10},... | collective-permute-start | bytes 294920 | tf_op jit(solution)/shard_map/ppermute | solution.py:195
  53.2 1.5 %collective-permute-start.10 = (bf16[8,3072]{1,0:T(8,128)(2,1)S(1)}, bf16[8,3072]{1,0:T(8,128)(2,1)S(1)}, u32[]{:S(2)}, u32[]{:S(2)}) collective-permute-start(bf16[8,3072]{1,0:T(8,128)(2,1)S(1)} %get-tuple-element.38), channel_id=1, source_target_pairs={{0,2},{1,3},{2,0},{3,1},{4,6},{5,7},{6,4},{7,5},{8,10},{9,11},{10,... | collective-permute-start | bytes 147464 | tf_op jit(solution)/shard_map/ppermute | solution.py:195
  54.7 0.0 collective-permute-done.9.refs_1_
  54.7 0.0 collective-permute-start.11
  54.7 2.6 %collective-permute-done.10.refs_2_ = bf16[8,3072]{1,0:T(8,128)(2,1)S(1)} collective-permute-done((bf16[8,3072]{1,0:T(8,128)(2,1)S(1)}, bf16[8,3072]{1,0:T(8,128)(2,1)S(1)}, u32[]{:S(2)}, u32[]{:S(2)}) %collective-permute-start.10) | collective-permute-done | bytes 49184 | tf_op jit(solution)/shard_map/ppermute | solution.py:195
  57.3 1.1 %collective-permute-done.11.refs_3_ = bf16[8,3072]{1,0:T(8,128)(2,1)S(1)} collective-permute-done((bf16[8,3072]{1,0:T(8,128)(2,1)S(1)}, bf16[8,3072]{1,0:T(8,128)(2,1)S(1)}, u32[]{:S(2)}, u32[]{:S(2)}) %collective-permute-start.11) | collective-permute-done | bytes 49184 | tf_op jit(solution)/shard_map/ppermute | solution.py:195
  58.3 0.0 collective-permute-done.15.refs_4_
  58.3 1.7 %collective-permute-done.16.refs_5_ = bf16[16,3072]{1,0:T(8,128)(2,1)S(1)} collective-permute-done((bf16[16,3072]{1,0:T(8,128)(2,1)S(1)}, bf16[16,3072]{1,0:T(8,128)(2,1)S(1)}, u32[]{:S(2)}, u32[]{:S(2)}) %collective-permute-start.16) | collective-permute-done | bytes 98336 | tf_op jit(solution)/shard_map/ppermute | solution.py:195
  60.0 0.0 collective-permute-done.17.refs_6_
  60.0 1.1 %shard_map.113 = bf16[16,3072]{1,0:T(8,128)(2,1)} custom-call(s32[1]{0:T(128)} %bitcast.me_ref, bf16[4,3072]{1,0:T(4,128)(2,1)S(1)} %bitcast.17, bf16[16,3200]{1,0:T(8,128)(2,1)S(1)} %get-tuple-element.26.payload_ref, f32[16,3072]{1,0:T(8,128)S(1)} %get-tuple-element.27.stream_ref, bf16[8,3072]{1,0:T(8,128)(2,1)S(1)} %get-tuple-element.36.refs_0_, ...), custom_call_target="tpu_custom_call" | custom-call | tf_op jit(solution)/shard_map/pallas_call | solution.py:287
  (3 shorter events, 0.0 us)
Async XLA Ops:
  0.0 0.7 %copy-start.1 = (s32[16]{0:T(128)S(1)}, s32[16]{0:T(128)}, u32[]{:S(2)}) copy-start(s32[16]{0:T(128)} %lengths_ref.1) | copy-start | bytes 196
  0.7 29.2 %slice-start.6 = ((s8[12582912]{0:T(1024)(128)(4,1)}), s8[4194304]{0:T(1024)(128)(4,1)S(1)}, s32[]{:S(2)}) async-start(s8[12582912]{0:T(1024)(128)(4,1)} %bitcast.13), calls=%async_computation.6 | async-start | bytes 8388608
  0.7 29.2 %slice-start.7 = ((s8[12582912]{0:T(1024)(128)(4,1)}), s8[4194304]{0:T(1024)(128)(4,1)S(1)}, s32[]{:S(2)}) async-start(s8[12582912]{0:T(1024)(128)(4,1)} %bitcast.13), calls=%async_computation.7 | async-start | bytes 8388608
  6.5 11.2 %collective-permute-start.5 = (bf16[16,3200]{1,0:T(8,128)(2,1)S(1)}, bf16[16,3200]{1,0:T(8,128)(2,1)S(1)}, u32[]{:S(2)}, u32[]{:S(2)}) collective-permute-start(bf16[16,3200]{1,0:T(8,128)(2,1)S(1)} %get-tuple-element.26.payload_ref), channel_id=1, source_target_pairs={{0,12},{4,8},{8,4},{12,0},{1,13},{5,9},{9,5},{13,1},{2,14},{6,10},... | collective-permute-start | bytes 307208 | tf_op jit(solution)/shard_map/ppermute | solution.py:195
  11.6 8.6 %collective-permute-start.4 = (bf16[16,3200]{1,0:T(8,128)(2,1)S(1)}, bf16[16,3200]{1,0:T(8,128)(2,1)S(1)}, u32[]{:S(2)}, u32[]{:S(2)}) collective-permute-start(bf16[16,3200]{1,0:T(8,128)(2,1)S(1)} %get-tuple-element.26.payload_ref), channel_id=1, source_target_pairs={{0,8},{4,12},{8,0},{12,4},{1,9},{5,13},{9,1},{13,5},{2,10},{6,14},... | collective-permute-start | bytes 307208 | tf_op jit(solution)/shard_map/ppermute | solution.py:195
  11.6 8.6 %collective-permute-start.3 = (bf16[16,3200]{1,0:T(8,128)(2,1)S(1)}, bf16[16,3200]{1,0:T(8,128)(2,1)S(1)}, u32[]{:S(2)}, u32[]{:S(2)}) collective-permute-start(bf16[16,3200]{1,0:T(8,128)(2,1)S(1)} %get-tuple-element.26.payload_ref), channel_id=1, source_target_pairs={{0,4},{4,0},{8,12},{12,8},{1,5},{5,1},{9,13},{13,9},{2,6},{6,2},{1... | collective-permute-start | bytes 307208 | tf_op jit(solution)/shard_map/ppermute | solution.py:195
  12.3 1.6 %collective-permute-start = (bf16[8,3072]{1,0:T(8,128)(2,1)S(1)}, bf16[8,3072]{1,0:T(8,128)(2,1)S(1)}, u32[]{:S(2)}, u32[]{:S(2)}) collective-permute-start(bf16[8,3072]{1,0:T(8,128)(2,1)S(1)} %get-tuple-element.29), channel_id=1, source_target_pairs={{0,1},{1,0},{2,3},{3,2},{4,5},{5,4},{6,7},{7,6},{8,9},{9,8},{10,11... | collective-permute-start | bytes 147464 | tf_op jit(solution)/shard_map/ppermute | solution.py:195
  12.3 4.2 %collective-permute-start.1 = (bf16[8,3072]{1,0:T(8,128)(2,1)S(1)}, bf16[8,3072]{1,0:T(8,128)(2,1)S(1)}, u32[]{:S(2)}, u32[]{:S(2)}) collective-permute-start(bf16[8,3072]{1,0:T(8,128)(2,1)S(1)} %get-tuple-element.30), channel_id=1, source_target_pairs={{0,2},{1,3},{2,0},{3,1},{4,6},{5,7},{6,4},{7,5},{8,10},{9,11},{10,... | collective-permute-start | bytes 147464 | tf_op jit(solution)/shard_map/ppermute | solution.py:195
  13.9 15.9 %slice-start = ((s8[12582912]{0:T(1024)(128)(4,1)}), s8[4194304]{0:T(1024)(128)(4,1)S(1)}, s32[]{:S(2)}) async-start(s8[12582912]{0:T(1024)(128)(4,1)} %bitcast.7), calls=%async_computation | async-start | bytes 8388608
  13.9 15.9 %slice-start.3 = ((s8[12582912]{0:T(1024)(128)(4,1)}), s8[4194304]{0:T(1024)(128)(4,1)S(1)}, s32[]{:S(2)}) async-start(s8[12582912]{0:T(1024)(128)(4,1)} %bitcast.10), calls=%async_computation.3 | async-start | bytes 8388608
  13.9 15.9 %slice-start.1 = ((s8[12582912]{0:T(1024)(128)(4,1)}), s8[4194304]{0:T(1024)(128)(4,1)S(1)}, s32[]{:S(2)}) async-start(s8[12582912]{0:T(1024)(128)(4,1)} %bitcast.7), calls=%async_computation.1 | async-start | bytes 8388608
  13.9 15.9 %slice-start.2 = ((s8[12582912]{0:T(1024)(128)(4,1)}), s8[4194304]{0:T(1024)(128)(4,1)S(1)}, s32[]{:S(2)}) async-start(s8[12582912]{0:T(1024)(128)(4,1)} %bitcast.7), calls=%async_computation.2 | async-start | bytes 8388608
  13.9 15.9 %slice-start.4 = ((s8[12582912]{0:T(1024)(128)(4,1)}), s8[4194304]{0:T(1024)(128)(4,1)S(1)}, s32[]{:S(2)}) async-start(s8[12582912]{0:T(1024)(128)(4,1)} %bitcast.10), calls=%async_computation.4 | async-start | bytes 8388608
  13.9 15.9 %slice-start.5 = ((s8[12582912]{0:T(1024)(128)(4,1)}), s8[4194304]{0:T(1024)(128)(4,1)S(1)}, s32[]{:S(2)}) async-start(s8[12582912]{0:T(1024)(128)(4,1)} %bitcast.10), calls=%async_computation.5 | async-start | bytes 8388608
  13.9 15.9 %slice-start.8 = ((s8[12582912]{0:T(1024)(128)(4,1)}), s8[4194304]{0:T(1024)(128)(4,1)S(1)}, s32[]{:S(2)}) async-start(s8[12582912]{0:T(1024)(128)(4,1)} %bitcast.13), calls=%async_computation.8 | async-start | bytes 8388608
  14.0 3.8 %collective-permute-start.2 = (bf16[8,3072]{1,0:T(8,128)(2,1)S(1)}, bf16[8,3072]{1,0:T(8,128)(2,1)S(1)}, u32[]{:S(2)}, u32[]{:S(2)}) collective-permute-start(bf16[8,3072]{1,0:T(8,128)(2,1)S(1)} %get-tuple-element.31), channel_id=1, source_target_pairs={{0,3},{1,2},{2,1},{3,0},{4,7},{5,6},{6,5},{7,4},{8,11},{9,10},{10,... | collective-permute-start | bytes 147464 | tf_op jit(solution)/shard_map/ppermute | solution.py:195
  20.8 1.9 %collective-permute-start.6 = (bf16[24,3072]{1,0:T(8,128)(2,1)S(1)}, bf16[24,3072]{1,0:T(8,128)(2,1)S(1)}, u32[]{:S(2)}, u32[]{:S(2)}) collective-permute-start(bf16[24,3072]{1,0:T(8,128)(2,1)S(1)} %get-tuple-element.33), channel_id=1, source_target_pairs={{0,1},{1,0},{2,3},{3,2},{4,5},{5,4},{6,7},{7,6},{8,9},{9,8},{10,11... | collective-permute-start | bytes 442376 | tf_op jit(solution)/shard_map/ppermute | solution.py:195
  20.9 6.7 %collective-permute-start.7 = (bf16[24,3072]{1,0:T(8,128)(2,1)S(1)}, bf16[24,3072]{1,0:T(8,128)(2,1)S(1)}, u32[]{:S(2)}, u32[]{:S(2)}) collective-permute-start(bf16[24,3072]{1,0:T(8,128)(2,1)S(1)} %get-tuple-element.34), channel_id=1, source_target_pairs={{0,2},{1,3},{2,0},{3,1},{4,6},{5,7},{6,4},{7,5},{8,10},{9,11},{10,... | collective-permute-start | bytes 442376 | tf_op jit(solution)/shard_map/ppermute | solution.py:195
  22.4 7.4 %collective-permute-start.8 = (bf16[24,3072]{1,0:T(8,128)(2,1)S(1)}, bf16[24,3072]{1,0:T(8,128)(2,1)S(1)}, u32[]{:S(2)}, u32[]{:S(2)}) collective-permute-start(bf16[24,3072]{1,0:T(8,128)(2,1)S(1)} %get-tuple-element.35), channel_id=1, source_target_pairs={{0,3},{1,2},{2,1},{3,0},{4,7},{5,6},{6,5},{7,4},{8,11},{9,10},{10,... | collective-permute-start | bytes 442376 | tf_op jit(solution)/shard_map/ppermute | solution.py:195
  29.9 18.0 %copy-start = (bf16[3072,4]{0,1:T(4,128)(2,1)S(1)}, bf16[3072,4]{0,1:T(4,128)(2,1)}, u32[]{:S(2)}) copy-start(bf16[3072,4]{0,1:T(4,128)(2,1)} %param.18) | copy-start | bytes 73732
  39.2 2.5 %collective-permute-start.12 = (bf16[24,3072]{1,0:T(8,128)(2,1)S(1)}, bf16[24,3072]{1,0:T(8,128)(2,1)S(1)}, u32[]{:S(2)}, u32[]{:S(2)}) collective-permute-start(bf16[24,3072]{1,0:T(8,128)(2,1)S(1)} %get-tuple-element.41), channel_id=1, source_target_pairs={{0,1},{1,0},{2,3},{3,2},{4,5},{5,4},{6,7},{7,6},{8,9},{9,8},{10,11... | collective-permute-start | bytes 442376 | tf_op jit(solution)/shard_map/ppermute | solution.py:195
  39.5 6.7 %collective-permute-start.13 = (bf16[24,3072]{1,0:T(8,128)(2,1)S(1)}, bf16[24,3072]{1,0:T(8,128)(2,1)S(1)}, u32[]{:S(2)}, u32[]{:S(2)}) collective-permute-start(bf16[24,3072]{1,0:T(8,128)(2,1)S(1)} %get-tuple-element.42), channel_id=1, source_target_pairs={{0,2},{1,3},{2,0},{3,1},{4,6},{5,7},{6,4},{7,5},{8,10},{9,11},{10,... | collective-permute-start | bytes 442376 | tf_op jit(solution)/shard_map/ppermute | solution.py:195
  41.0 7.0 %collective-permute-start.14 = (bf16[24,3072]{1,0:T(8,128)(2,1)S(1)}, bf16[24,3072]{1,0:T(8,128)(2,1)S(1)}, u32[]{:S(2)}, u32[]{:S(2)}) collective-permute-start(bf16[24,3072]{1,0:T(8,128)(2,1)S(1)} %get-tuple-element.43), channel_id=1, source_target_pairs={{0,3},{1,2},{2,1},{3,0},{4,7},{5,6},{6,5},{7,4},{8,11},{9,10},{10,... | collective-permute-start | bytes 442376 | tf_op jit(solution)/shard_map/ppermute | solution.py:195
  41.1 13.6 %collective-permute-start.9 = (bf16[8,3072]{1,0:T(8,128)(2,1)S(1)}, bf16[8,3072]{1,0:T(8,128)(2,1)S(1)}, u32[]{:S(2)}, u32[]{:S(2)}) collective-permute-start(bf16[8,3072]{1,0:T(8,128)(2,1)S(1)} %get-tuple-element.37), channel_id=1, source_target_pairs={{0,1},{1,0},{2,3},{3,2},{4,5},{5,4},{6,7},{7,6},{8,9},{9,8},{10,11... | collective-permute-start | bytes 147464 | tf_op jit(solution)/shard_map/ppermute | solution.py:195
  48.7 9.6 %collective-permute-start.15 = (bf16[16,3072]{1,0:T(8,128)(2,1)S(1)}, bf16[16,3072]{1,0:T(8,128)(2,1)S(1)}, u32[]{:S(2)}, u32[]{:S(2)}) collective-permute-start(bf16[16,3072]{1,0:T(8,128)(2,1)S(1)} %get-tuple-element.44), channel_id=1, source_target_pairs={{0,4},{4,0},{8,12},{12,8},{1,5},{5,1},{9,13},{13,9},{2,6},{6,2},{1... | collective-permute-start | bytes 294920 | tf_op jit(solution)/shard_map/ppermute | solution.py:195
  49.2 10.8 %collective-permute-start.16 = (bf16[16,3072]{1,0:T(8,128)(2,1)S(1)}, bf16[16,3072]{1,0:T(8,128)(2,1)S(1)}, u32[]{:S(2)}, u32[]{:S(2)}) collective-permute-start(bf16[16,3072]{1,0:T(8,128)(2,1)S(1)} %get-tuple-element.45), channel_id=1, source_target_pairs={{0,8},{4,12},{8,0},{12,4},{1,9},{5,13},{9,1},{13,5},{2,10},{6,14},... | collective-permute-start | bytes 294920 | tf_op jit(solution)/shard_map/ppermute | solution.py:195
  51.8 8.2 %collective-permute-start.17 = (bf16[16,3072]{1,0:T(8,128)(2,1)S(1)}, bf16[16,3072]{1,0:T(8,128)(2,1)S(1)}, u32[]{:S(2)}, u32[]{:S(2)}) collective-permute-start(bf16[16,3072]{1,0:T(8,128)(2,1)S(1)} %get-tuple-element.46), channel_id=1, source_target_pairs={{0,12},{4,8},{8,4},{12,0},{1,13},{5,9},{9,5},{13,1},{2,14},{6,10},... | collective-permute-start | bytes 294920 | tf_op jit(solution)/shard_map/ppermute | solution.py:195
  53.2 4.1 %collective-permute-start.10 = (bf16[8,3072]{1,0:T(8,128)(2,1)S(1)}, bf16[8,3072]{1,0:T(8,128)(2,1)S(1)}, u32[]{:S(2)}, u32[]{:S(2)}) collective-permute-start(bf16[8,3072]{1,0:T(8,128)(2,1)S(1)} %get-tuple-element.38), channel_id=1, source_target_pairs={{0,2},{1,3},{2,0},{3,1},{4,6},{5,7},{6,4},{7,5},{8,10},{9,11},{10,... | collective-permute-start | bytes 147464 | tf_op jit(solution)/shard_map/ppermute | solution.py:195
  54.7 3.7 %collective-permute-start.11 = (bf16[8,3072]{1,0:T(8,128)(2,1)S(1)}, bf16[8,3072]{1,0:T(8,128)(2,1)S(1)}, u32[]{:S(2)}, u32[]{:S(2)}) collective-permute-start(bf16[8,3072]{1,0:T(8,128)(2,1)S(1)} %get-tuple-element.39), channel_id=1, source_target_pairs={{0,3},{1,2},{2,1},{3,0},{4,7},{5,6},{6,5},{7,4},{8,11},{9,10},{10,... | collective-permute-start | bytes 147464 | tf_op jit(solution)/shard_map/ppermute | solution.py:195

commit v4 on v3

v4 whole, which is shorter than its diff:
```python
import functools

import jax
import jax.numpy as jnp
from jax import lax
from jax.experimental import pallas as pl
from jax.experimental.pallas import tpu as pltpu
from jax.sharding import PartitionSpec as P

HS = 128
KVH = 4
GROUP = 6
CAP = 8
LANES = 128
BLOCK = 8
MIB = 1 << 20
F32 = jnp.float32
BF16 = jnp.bfloat16
BUSY = pl.CostEstimate(flops=12_000_000_000, bytes_accessed=4_000_000, transcendentals=0)
ANY = pl.BlockSpec(memory_space=pl.ANY)
WHOLE = pl.BlockSpec(memory_space=pltpu.VMEM)
SCALAR = pl.BlockSpec(memory_space=pltpu.SMEM)


def dot(a, b, dims=((1,), (0,))):
    return lax.dot_general(a, b, (dims, ((), ())), preferred_element_type=F32)


def iota(shape, dim):
    return lax.broadcasted_iota(jnp.int32, shape, dim)


def slot_map(owners, chunks, batch, experts):
    rows, slots = chunks * batch, experts * chunks * CAP
    slot = iota((rows, slots), 1)
    row = iota((rows, slots), 0)
    expert = slot // (chunks * CAP)
    chunk = (slot // CAP) % chunks
    named = (owners[:, 0:1] == expert) | (owners[:, 1:2] == expert)
    named = named & (row // batch == chunk)
    named = jnp.where(named, 1.0, 0.0)
    left, right = iota((rows, rows), 0), iota((rows, rows), 1)
    before = jnp.where(right < left, 1.0, 0.0).astype(BF16)
    place = dot(before, named.astype(BF16))
    wanted = (slot % CAP).astype(F32)
    return jnp.where(place == wanted, named, 0.0)


def dispatch(me, rows, named, chunks, experts):
    owners = named[:, 0:2].astype(F32).astype(jnp.int32) ^ me
    table = slot_map(owners, chunks, rows.shape[0] // chunks, experts)
    return dot(table.astype(BF16), rows, ((0,), (0,)))


def combine(me, rows, named, router, returned, chunks, experts):
    routes = named[:, 0:2].astype(F32).astype(jnp.int32)
    logits = dot(rows, router, ((1,), (1,)))
    lane = iota(logits.shape, 1)
    first = jnp.sum(jnp.where(lane == routes[:, 0:1], logits, 0.0), axis=1, keepdims=True)
    second = jnp.sum(jnp.where(lane == routes[:, 1:2], logits, 0.0), axis=1, keepdims=True)
    gate0 = 1.0 / (1.0 + jnp.exp(second - first))
    gate1 = 1.0 / (1.0 + jnp.exp(first - second))
    owners = routes ^ me
    table = slot_map(owners, chunks, rows.shape[0] // chunks, experts)
    expert = iota(table.shape, 1) // (chunks * CAP)
    gates = table * jnp.where(owners[:, 0:1] == expert, gate0, gate1)
    high = gates.astype(BF16)
    low = (gates - high.astype(F32)).astype(BF16)
    return dot(high, returned) + dot(low, returned)


def attend_kernel(
    lengths_hbm, queries_hbm, keys_hbm, values_hbm, routes_hbm, residual_hbm, gain_hbm,
    stream_ref, payload_ref,
    lengths_ref, queries_ref, keys_ref, values_ref, routes_ref, residual_ref, gain_ref, sems,
):
    batch, window, _ = keys_ref.shape
    width = queries_ref.shape[1]
    span = width // KVH
    blocks = [pl.ds(begin, BLOCK) for begin in range(0, batch, BLOCK)]
    small = [
        (lengths_hbm, lengths_ref), (queries_hbm, queries_ref), (routes_hbm, routes_ref),
        (residual_hbm, residual_ref), (gain_hbm, gain_ref),
    ]
    caches = [
        (source.at[block], target.at[block])
        for block in blocks
        for source, target in ((keys_hbm, keys_ref), (values_hbm, values_ref))
    ]
    copies = [
        pltpu.make_async_copy(source, target, sems.at[i])
        for i, (source, target) in enumerate(small[:2] + caches + small[2:])
    ]
    for copy in copies:
        copy.start()
    copies[0].wait()
    copies[1].wait()
    same = iota((batch, batch), 0) == iota((batch, batch), 1)

    def upright(row):
        return jnp.sum(jnp.where(same, row, 0), axis=1, keepdims=True)

    lengths = upright(lengths_ref[...])
    queries = queries_ref[...].astype(F32)
    row = iota((BLOCK, BLOCK * window), 0)
    column = iota((BLOCK, BLOCK * window), 1) - row * window
    attended = []
    for i, block in enumerate(blocks):
        begin = i * BLOCK
        bias = jnp.where((column >= 0) & (column < lengths[begin : begin + BLOCK]), 0.0, -1e30)
        bias = jnp.concatenate([bias] * GROUP, axis=0)
        copies[2 + 2 * i].wait()
        copies[3 + 2 * i].wait()
        heads = []
        for k in range(KVH):
            keys = keys_ref[block, :, k * HS : (k + 1) * HS].reshape(BLOCK * window, HS)
            values = values_ref[block, :, k * HS : (k + 1) * HS].reshape(BLOCK * window, HS)
            stacked = jnp.concatenate(
                [
                    queries[begin : begin + BLOCK, k * span + g * HS : k * span + (g + 1) * HS]
                    for g in range(GROUP)
                ],
                axis=0,
            ).astype(BF16)
            scores = dot(stacked, keys, ((1,), (1,))) * HS ** (-0.5) + bias
            highest = jnp.max(scores, axis=1, keepdims=True)
            powers = jnp.exp(scores - highest)
            weights = (powers / jnp.sum(powers, axis=1, keepdims=True)).astype(BF16)
            mixed = dot(weights, values)
            heads += [mixed[g * BLOCK : (g + 1) * BLOCK] for g in range(GROUP)]
        attended.append(jnp.concatenate(heads, axis=1))
    for copy in copies[2 + 2 * len(blocks) :]:
        copy.wait()
    stream = residual_ref[...].astype(F32) + jnp.concatenate(attended, axis=0)
    scale = lax.rsqrt(jnp.mean(stream * stream, axis=1, keepdims=True) + 1e-05)
    lane = iota((batch, LANES), 1)
    routes = [upright(routes_ref[k : k + 1, :]).astype(F32) for k in range(2)]
    named = jnp.where(lane == 0, routes[0], jnp.where(lane == 1, routes[1], 0.0))
    stream_ref[...] = stream
    payload_ref[:, :width] = (stream * scale * gain_ref[...]).astype(BF16)
    payload_ref[:, width:] = named.astype(BF16)


def split_kernel(me_ref, *refs, chunks, after):
    refs = refs[after:]
    payload = jnp.concatenate([ref[...] for ref in refs[:chunks]], axis=0)
    slots = refs[chunks:]
    width = slots[0].shape[1]
    rows, named = payload[:, :width], payload[:, width:]
    out = dispatch(me_ref[0], rows, named, chunks, len(slots))
    span = chunks * CAP
    for e, ref in enumerate(slots):
        ref[...] = out[e * span : (e + 1) * span].astype(BF16)


def expert_kernel(*refs, pieces):
    xs, (gate_ref, up_ref, down_ref) = refs[:pieces], refs[pieces : pieces + 3]
    outs = refs[pieces + 3 : 2 * pieces + 3]
    rows_ref, hidden_ref = refs[2 * pieces + 3 :]
    begin = 0
    for ref in xs:
        rows_ref[begin : begin + ref.shape[0], :] = ref[...]
        begin += ref.shape[0]
    width, units = gate_ref.shape
    tile = min(256, units)

    @pl.loop(0, units // tile)
    def _(i):
        at = pl.ds(pl.multiple_of(i * tile, tile), tile)
        gate = dot(rows_ref[...], gate_ref[:, at])
        up = dot(rows_ref[...], up_ref[:, at])
        hidden_ref[:, at] = (jax.nn.silu(gate) * up).astype(BF16)

    @pl.loop(0, width // tile)
    def _(i):
        at = pl.ds(pl.multiple_of(i * tile, tile), tile)
        out = dot(hidden_ref[...], down_ref[:, at])
        begin = 0
        for ref in outs:
            count = ref.shape[0]
            ref[:, at] = out[begin : begin + count].astype(BF16)
            begin += count


def mix_kernel(me_ref, router_ref, *refs, chunks, experts, own, after):
    refs = refs[after:]
    payload = jnp.concatenate([ref[...] for ref in refs[:chunks]], axis=0)
    returned = jnp.concatenate([ref[...] for ref in refs[chunks : chunks + experts]], axis=0)
    outs = refs[chunks + experts + own :]
    batch, width = outs[0].shape
    rows, named = payload[:, :width], payload[:, width:]
    mixed = combine(me_ref[0], rows, named, router_ref[...], returned, chunks, experts)
    for j, ref in enumerate(outs):
        part = mixed[j * batch : (j + 1) * batch]
        if own and j == 0:
            ref[...] = refs[chunks + experts][...] + part
        else:
            ref[...] = part.astype(BF16)


def finish_kernel(stream_ref, *refs):
    total = stream_ref[...]
    for ref in refs[:-1]:
        total = total + ref[...].astype(F32)
    refs[-1][...] = total.astype(BF16)


def in_hbm(value):
    return pltpu.with_memory_space_constraint(value, pltpu.HBM)


def swap(value, axis, step):
    if step == 0:
        return value
    count = lax.axis_size(axis)
    return lax.ppermute(value, axis, [(i, i ^ step) for i in range(count)])


def params(elements):
    return pltpu.CompilerParams(vmem_limit_bytes=min(48 * MIB, 2 * MIB + 10 * elements))


def shards(
    queries,
    cached_keys,
    cached_values,
    lengths,
    routes,
    residual,
    norm_gain,
    router,
    gate_proj,
    up_proj,
    down_proj,
):
    batch, width = queries.shape
    experts = router.shape[1]
    layers = lax.axis_size("attn")
    me = lax.axis_index("expert").astype(jnp.int32).reshape(1)
    router = router.T
    shape = jax.ShapeDtypeStruct
    operands = [
        in_hbm(a)
        for a in (
            lengths[None], queries, cached_keys, cached_values, routes.T, residual, norm_gain[None]
        )
    ]
    stream, payload = pl.pallas_call(
        attend_kernel,
        in_specs=[ANY] * len(operands),
        out_specs=[WHOLE, WHOLE],
        out_shape=[shape((batch, width), F32), shape((batch, width + LANES), BF16)],
        scratch_shapes=[pltpu.VMEM(a.shape, a.dtype) for a in operands]
        + [pltpu.SemaphoreType.DMA((5 + 2 * (batch // BLOCK),))],
        compiler_params=params(28 * batch * width),
        cost_estimate=pl.CostEstimate(flops=10**9, bytes_accessed=4 * 10**6, transcendentals=10**6),
    )(*operands)

    chunks = [swap(payload, "attn", j) for j in range(layers)]
    groups = [list(range(2)), list(range(2, layers))]
    inputs, ahead = [], []
    for group in groups:
        count = len(group)
        slots = pl.pallas_call(
            functools.partial(split_kernel, chunks=count, after=len(ahead)),
            in_specs=[SCALAR] + [ANY] * len(ahead) + [WHOLE] * count,
            out_specs=[WHOLE] * experts,
            out_shape=[shape((count * CAP, width), BF16)] * experts,
            cost_estimate=BUSY,
            compiler_params=params(experts * count * CAP * width),
        )(me, *ahead, *[chunks[j] for j in group])
        arrived = [swap(slots[e], "expert", e) for e in range(experts)]
        ahead = arrived[1:2]
        inputs += arrived

    total_rows = sum(block.shape[0] for block in inputs)
    units = gate_proj.shape[2]
    results = pl.pallas_call(
        functools.partial(expert_kernel, pieces=len(inputs)),
        in_specs=[WHOLE] * (len(inputs) + 3),
        out_specs=[WHOLE] * len(inputs),
        out_shape=[shape(block.shape, BF16) for block in inputs],
        scratch_shapes=[pltpu.VMEM((total_rows, width), BF16), pltpu.VMEM((total_rows, units), BF16)],
        compiler_params=params(total_rows * width),
    )(*inputs, gate_proj[0], up_proj[0], down_proj[0])

    received, before = [], []
    for i, group in list(enumerate(groups))[::-1]:
        count, own = len(group), int(group[0] == 0)
        returned = [swap(results[i * experts + e], "expert", e) for e in range(experts)]
        mixed = pl.pallas_call(
            functools.partial(
                mix_kernel, chunks=count, experts=experts, own=own, after=len(before)
            ),
            in_specs=[SCALAR, WHOLE]
            + [ANY] * len(before)
            + [WHOLE] * (count + experts + own),
            out_specs=[WHOLE] * count,
            out_shape=[shape((batch, width), F32 if j == 0 else BF16) for j in group],
            compiler_params=params(experts * count * CAP * width),
        )(me, router, *before, *[chunks[j] for j in group], *returned, *[stream] * own)
        before = mixed[:1]
        received = [swap(block, "attn", j) for j, block in zip(group, mixed)] + received
    return pl.pallas_call(
        finish_kernel,
        in_specs=[WHOLE] * len(received),
        out_specs=WHOLE,
        out_shape=shape((batch, width), BF16),
        compiler_params=params(2 * layers * batch * width),
    )(*received)


def solution(mesh):
    in_specs = (
        P(("groups", "attn", "expert"), None),
        P(("groups", "attn", "expert"), None, None),
        P(("groups", "attn", "expert"), None, None),
        P(("groups", "attn", "expert")),
        P(("groups", "attn", "expert"), None),
        P(("groups", "attn", "expert"), None),
        P(),
        P(),
        P("expert", None, "attn"),
        P("expert", None, "attn"),
        P("expert", "attn", None),
    )
    out_specs = P(("groups", "attn", "expert"), None)
    return jax.shard_map(shards, mesh=mesh, in_specs=in_specs, out_specs=out_specs, check_vma=False)
```

time: 61.3 us -> 56.7 us (0.925)
  waiting for transfers between devices: 24 us -> 21.7 us
  starting transfers between devices: 18.8 us -> 17.4 us
  local copies, waits for them, and re-layouts: 0.7 us -> 0.05 us
    ppermute x18, waiting for transfers between devices: 24 us -> 21.7 us  [swap(): return lax.ppermute(value, axis, [(i, i ^ step) for i in range(count)])]
    ppermute x18, starting transfers between devices: 18.8 us -> 17.4 us  [swap(): return lax.ppermute(value, axis, [(i, i ^ step) for i in range(count)])]
    unnamed x22 -> x20, local copies, waits for them, and re-layouts: 0.7 us -> 0.05 us
    pallas_call x4 -> x6, Pallas kernels: 8.25 us -> 8 us  [the longest x1 5.14 us: shards(): pl.pallas_call(attend_kernel, in_specs=[ANY] * len(operands), out_specs=[...]
  transfers between devices with their start and end apart: 18 -> 18, of which waited for: 10 -> 10; matrix products, arithmetic and copies ran while one was open for 0% -> 0% of each run, Pallas kernels for 1% -> 4%
where the time goes in v4:
time: 56.7 us; the launch traced here: 56.6 us
  waiting for transfers between devices  21.7 us (38%)
  starting transfers between devices  17.4 us (31%)
  Pallas kernels  17.2 us (30%)
    ppermute x18, waiting for transfers between devices, swap(): return lax.ppermute(value, axis, [(i, i ^ step) for i in range(count)])  21.7 us
    ppermute x18, starting transfers between devices, swap(): return lax.ppermute(value, axis, [(i, i ^ step) for i in range(count)])  17.4 us
    pallas_call x1, Pallas kernels, shards(): pl.pallas_call(functools.partial(expert_kernel, pieces=len(inputs)), in_s...  9.22 us
    pallas_call x1, Pallas kernels, shards(): pl.pallas_call(attend_kernel, in_specs=[ANY] * len(operands), out_specs=[...  5.14 us
    pallas_call x2, Pallas kernels, shards(): pl.pallas_call(functools.partial(mix_kernel, chunks=count, experts=expert...  1.22 us
  transfers between devices with their start and end apart: 18, of which 10 were waited for; matrix products, arithmetic and copies ran while one was open for 0% of the time, Pallas kernels for 4%

profile of v4, /device:TPU:0, one launch (start us, length us, event | category | flops | bytes accessed | tf_op | source)
XLA Modules:
  0.0 56.6 jit_solution(2081421142088566770)
XLA Ops:
  0.0 5.1 %shard_map.109 = (f32[16,3072]{1,0:T(8,128)S(1)}, bf16[16,3200]{1,0:T(8,128)(2,1)S(1)}) custom-call(s32[1,16]{1,0:T(1,128)} %bitcast.21, bf16[16,3072]{1,0:T(8,128)(2,1)} %queries_hbm.1, bf16[16,96,512]{2,1,0:T(8,128)(2,1)} %keys_hbm.1, bf16[16,96,512]{2,1,0:T(8,128)(2,1)} %values_hbm.1, s32[2,16]{1,0:T(2,128)} %bitcast.20, bf16[16,3072]{1,0:T(8,128)(2,1)} %residual_hbm.1, ...), custom_call_target="tpu_custom_call" | custom-call | flops 1000000000 | bytes 4000000 | tf_op jit(solution)/shard_map/pallas_call | solution.py:248
  5.1 3.1 %collective-permute-start.2 = (bf16[16,3200]{1,0:T(8,128)(2,1)S(1)}, bf16[16,3200]{1,0:T(8,128)(2,1)S(1)}, u32[]{:S(2)}, u32[]{:S(2)}) collective-permute-start(bf16[16,3200]{1,0:T(8,128)(2,1)S(1)} %get-tuple-element.27.refs_0_.refs_1_), channel_id=1, source_target_pairs={{0,4},{4,0},{8,12},{12,8},{1,5},{5,1},{9,13},{13,9},{2,6},{6,2},{1... | collective-permute-start | bytes 307208 | tf_op jit(solution)/shard_map/ppermute | solution.py:216
  8.2 2.5 %collective-permute-start.1 = (bf16[16,3200]{1,0:T(8,128)(2,1)S(1)}, bf16[16,3200]{1,0:T(8,128)(2,1)S(1)}, u32[]{:S(2)}, u32[]{:S(2)}) collective-permute-start(bf16[16,3200]{1,0:T(8,128)(2,1)S(1)} %get-tuple-element.27.refs_0_.refs_1_), channel_id=1, source_target_pairs={{0,12},{4,8},{8,4},{12,0},{1,13},{5,9},{9,5},{13,1},{2,14},{6,10},... | collective-permute-start | bytes 307208 | tf_op jit(solution)/shard_map/ppermute | solution.py:216
  10.7 0.1 collective-permute-start
  10.8 0.3 collective-permute-done.2.refs_1_.refs_2_
  11.1 0.0 slice-start.6
  11.1 0.0 slice-start.7
  11.1 0.5 shard_map.110
  11.6 0.1 collective-permute-start.3
  11.7 1.8 %collective-permute-start.4 = (bf16[16,3072]{1,0:T(8,128)(2,1)S(1)}, bf16[16,3072]{1,0:T(8,128)(2,1)S(1)}, u32[]{:S(2)}, u32[]{:S(2)}) collective-permute-start(bf16[16,3072]{1,0:T(8,128)(2,1)S(1)} %get-tuple-element.30), channel_id=1, source_target_pairs={{0,2},{1,3},{2,0},{3,1},{4,6},{5,7},{6,4},{7,5},{8,10},{9,11},{10,... | collective-permute-start | bytes 294920 | tf_op jit(solution)/shard_map/ppermute | solution.py:216
  13.5 0.0 slice-start
  13.5 0.0 slice-start.3
  13.5 0.0 slice-start.1
  13.5 0.0 slice-start.2
  13.5 0.0 slice-start.4
  13.5 0.0 slice-start.5
  13.5 0.0 slice-start.8
  13.5 0.2 collective-permute-start.5
  13.7 2.9 %collective-permute-done.1.refs_2_.refs_1_ = bf16[16,3200]{1,0:T(8,128)(2,1)S(1)} collective-permute-done((bf16[16,3200]{1,0:T(8,128)(2,1)S(1)}, bf16[16,3200]{1,0:T(8,128)(2,1)S(1)}, u32[]{:S(2)}, u32[]{:S(2)}) %collective-permute-start.1) | collective-permute-done | bytes 102432 | tf_op jit(solution)/shard_map/ppermute | solution.py:216
  16.6 3.4 %collective-permute-done.refs_1_.refs_0_ = bf16[16,3200]{1,0:T(8,128)(2,1)S(1)} collective-permute-done((bf16[16,3200]{1,0:T(8,128)(2,1)S(1)}, bf16[16,3200]{1,0:T(8,128)(2,1)S(1)}, u32[]{:S(2)}, u32[]{:S(2)}) %collective-permute-start) | collective-permute-done | bytes 102432 | tf_op jit(solution)/shard_map/ppermute | solution.py:216
  20.0 0.0 collective-permute-done.3.refs_0_.refs_1_
  20.0 0.5 shard_map.111
  20.5 0.1 collective-permute-start.6
  20.6 1.6 %collective-permute-start.7 = (bf16[16,3072]{1,0:T(8,128)(2,1)S(1)}, bf16[16,3072]{1,0:T(8,128)(2,1)S(1)}, u32[]{:S(2)}, u32[]{:S(2)}) collective-permute-start(bf16[16,3072]{1,0:T(8,128)(2,1)S(1)} %get-tuple-element.34), channel_id=1, source_target_pairs={{0,2},{1,3},{2,0},{3,1},{4,6},{5,7},{6,4},{7,5},{8,10},{9,11},{10,... | collective-permute-start | bytes 294920 | tf_op jit(solution)/shard_map/ppermute | solution.py:216
  22.1 0.3 collective-permute-start.8
  22.4 0.0 collective-permute-done.4.refs_2_
  22.4 0.0 collective-permute-done.5.refs_3_
  22.4 0.0 collective-permute-done.6.refs_5_
  22.4 3.8 %collective-permute-done.7.refs_6_ = bf16[16,3072]{1,0:T(8,128)(2,1)S(1)} collective-permute-done((bf16[16,3072]{1,0:T(8,128)(2,1)S(1)}, bf16[16,3072]{1,0:T(8,128)(2,1)S(1)}, u32[]{:S(2)}, u32[]{:S(2)}) %collective-permute-start.7) | collective-permute-done | bytes 98336 | tf_op jit(solution)/shard_map/ppermute | solution.py:216
  26.2 1.2 %collective-permute-done.8.refs_7_ = bf16[16,3072]{1,0:T(8,128)(2,1)S(1)} collective-permute-done((bf16[16,3072]{1,0:T(8,128)(2,1)S(1)}, bf16[16,3072]{1,0:T(8,128)(2,1)S(1)}, u32[]{:S(2)}, u32[]{:S(2)}) %collective-permute-start.8) | collective-permute-done | bytes 98336 | tf_op jit(solution)/shard_map/ppermute | solution.py:216
  27.4 0.0 slice-done.6
  27.4 0.0 slice-done.7
  27.4 0.0 slice-done
  27.4 0.0 slice-done.3
  27.5 0.0 slice-done.1
  27.5 0.0 slice-done.2
  27.5 0.0 slice-done.4
  27.5 0.0 slice-done.5
  27.5 0.0 slice-done.8
  27.5 0.0 copy-start
  27.5 9.2 %shard_map.112 = (bf16[16,3072]{1,0:T(8,128)(2,1)S(1)}, bf16[16,3072]{1,0:T(8,128)(2,1)S(1)}, bf16[16,3072]{1,0:T(8,128)(2,1)S(1)}, bf16[16,3072]{1,0:T(8,128)(2...) custom-call(bf16[16,3072]{1,0:T(8,128)(2,1)S(1)} %get-tuple-element., ...), custom_call_target="tpu_custom_call" | custom-call | tf_op jit(solution)/shard_map/pallas_call | solution.py:278
  36.8 0.4 collective-permute-start.9
  37.1 1.5 %collective-permute-start.10 = (bf16[16,3072]{1,0:T(8,128)(2,1)S(1)}, bf16[16,3072]{1,0:T(8,128)(2,1)S(1)}, u32[]{:S(2)}, u32[]{:S(2)}) collective-permute-start(bf16[16,3072]{1,0:T(8,128)(2,1)S(1)} %get-tuple-element.38), channel_id=1, source_target_pairs={{0,2},{1,3},{2,0},{3,1},{4,6},{5,7},{6,4},{7,5},{8,10},{9,11},{10,... | collective-permute-start | bytes 294920 | tf_op jit(solution)/shard_map/ppermute | solution.py:216
  38.6 0.1 collective-permute-start.11
  38.7 0.6 %collective-permute-start.12 = (bf16[16,3072]{1,0:T(8,128)(2,1)S(1)}, bf16[16,3072]{1,0:T(8,128)(2,1)S(1)}, u32[]{:S(2)}, u32[]{:S(2)}) collective-permute-start(bf16[16,3072]{1,0:T(8,128)(2,1)S(1)} %get-tuple-element.42), channel_id=1, source_target_pairs={{0,1},{1,0},{2,3},{3,2},{4,5},{5,4},{6,7},{7,6},{8,9},{9,8},{10,11... | collective-permute-start | bytes 294920 | tf_op jit(solution)/shard_map/ppermute | solution.py:216
  39.3 1.5 %collective-permute-start.13 = (bf16[16,3072]{1,0:T(8,128)(2,1)S(1)}, bf16[16,3072]{1,0:T(8,128)(2,1)S(1)}, u32[]{:S(2)}, u32[]{:S(2)}) collective-permute-start(bf16[16,3072]{1,0:T(8,128)(2,1)S(1)} %get-tuple-element.43), channel_id=1, source_target_pairs={{0,2},{1,3},{2,0},{3,1},{4,6},{5,7},{6,4},{7,5},{8,10},{9,11},{10,... | collective-permute-start | bytes 294920 | tf_op jit(solution)/shard_map/ppermute | solution.py:216
  40.8 0.0 collective-permute-done.9.refs_3_
  40.8 0.0 collective-permute-start.14
  40.8 1.8 %collective-permute-done.10.refs_4_ = bf16[16,3072]{1,0:T(8,128)(2,1)S(1)} collective-permute-done((bf16[16,3072]{1,0:T(8,128)(2,1)S(1)}, bf16[16,3072]{1,0:T(8,128)(2,1)S(1)}, u32[]{:S(2)}, u32[]{:S(2)}) %collective-permute-start.10) | collective-permute-done | bytes 98336 | tf_op jit(solution)/shard_map/ppermute | solution.py:216
  42.5 1.4 %collective-permute-done.11.refs_5_ = bf16[16,3072]{1,0:T(8,128)(2,1)S(1)} collective-permute-done((bf16[16,3072]{1,0:T(8,128)(2,1)S(1)}, bf16[16,3072]{1,0:T(8,128)(2,1)S(1)}, u32[]{:S(2)}, u32[]{:S(2)}) %collective-permute-start.11) | collective-permute-done | bytes 98336 | tf_op jit(solution)/shard_map/ppermute | solution.py:216
  43.9 0.0 copy-done
  43.9 0.6 %shard_map.113 = (bf16[16,3072]{1,0:T(8,128)(2,1)S(1)}, bf16[16,3072]{1,0:T(8,128)(2,1)S(1)}) custom-call(s32[1]{0:T(128)} %bitcast.me_ref, bf16[4,3072]{1,0:T(4,128)(2,1)S(1)} %bitcast.17, bf16[16,3200]{1,0:T(8,128)(2,1)S(1)} %collective-permute-done.refs_1_.refs_0_, bf16[16,3200]{1,0:T(8,128)(2,1)S(1)} %collective-permute-done.1.refs_2_.refs_1_, ...), custom_call_target="tpu_custom_call" | custom-call | tf_op jit(solution)/shard_map/pallas_call | solution.py:291
  44.5 2.7 %collective-permute-start.17 = (bf16[16,3072]{1,0:T(8,128)(2,1)S(1)}, bf16[16,3072]{1,0:T(8,128)(2,1)S(1)}, u32[]{:S(2)}, u32[]{:S(2)}) collective-permute-start(bf16[16,3072]{1,0:T(8,128)(2,1)S(1)} %get-tuple-element.48), channel_id=1, source_target_pairs={{0,12},{4,8},{8,4},{12,0},{1,13},{5,9},{9,5},{13,1},{2,14},{6,10},... | collective-permute-start | bytes 294920 | tf_op jit(solution)/shard_map/ppermute | solution.py:216
  47.2 0.0 collective-permute-start.16
  47.2 0.0 collective-permute-done.12.refs_4_
  47.2 0.0 collective-permute-done.13.refs_5_
  47.2 0.7 %collective-permute-done.14.refs_6_ = bf16[16,3072]{1,0:T(8,128)(2,1)S(1)} collective-permute-done((bf16[16,3072]{1,0:T(8,128)(2,1)S(1)}, bf16[16,3072]{1,0:T(8,128)(2,1)S(1)}, u32[]{:S(2)}, u32[]{:S(2)}) %collective-permute-start.14) | collective-permute-done | bytes 98336 | tf_op jit(solution)/shard_map/ppermute | solution.py:216
  47.9 0.6 %shard_map.114 = (f32[16,3072]{1,0:T(8,128)S(1)}, bf16[16,3072]{1,0:T(8,128)(2,1)S(1)}) custom-call(s32[1]{0:T(128)} %bitcast.me_ref, bf16[4,3072]{1,0:T(4,128)(2,1)S(1)} %bitcast.18, bf16[16,3072]{1,0:T(8,128)(2,1)S(1)} %get-tuple-element.40.refs_0_, bf16[16,3200]{1,0:T(8,128)(2,1)S(1)} %get-tuple-element.27.refs_0_.refs_1_, ...), custom_call_target="tpu_custom_call" | custom-call | tf_op jit(solution)/shard_map/pallas_call | solution.py:291
  48.5 1.1 %collective-permute-start.15 = (bf16[16,3072]{1,0:T(8,128)(2,1)S(1)}, bf16[16,3072]{1,0:T(8,128)(2,1)S(1)}, u32[]{:S(2)}, u32[]{:S(2)}) collective-permute-start(bf16[16,3072]{1,0:T(8,128)(2,1)S(1)} %get-tuple-element.47), channel_id=1, source_target_pairs={{0,4},{4,0},{8,12},{12,8},{1,5},{5,1},{9,13},{13,9},{2,6},{6,2},{1... | collective-permute-start | bytes 294920 | tf_op jit(solution)/shard_map/ppermute | solution.py:216
  49.6 2.4 %collective-permute-done.17.refs_2_ = bf16[16,3072]{1,0:T(8,128)(2,1)S(1)} collective-permute-done((bf16[16,3072]{1,0:T(8,128)(2,1)S(1)}, bf16[16,3072]{1,0:T(8,128)(2,1)S(1)}, u32[]{:S(2)}, u32[]{:S(2)}) %collective-permute-start.17) | collective-permute-done | bytes 98336 | tf_op jit(solution)/shard_map/ppermute | solution.py:216
  52.0 3.9 %collective-permute-done.16.refs_1_ = bf16[16,3072]{1,0:T(8,128)(2,1)S(1)} collective-permute-done((bf16[16,3072]{1,0:T(8,128)(2,1)S(1)}, bf16[16,3072]{1,0:T(8,128)(2,1)S(1)}, u32[]{:S(2)}, u32[]{:S(2)}) %collective-permute-start.16) | collective-permute-done | bytes 98336 | tf_op jit(solution)/shard_map/ppermute | solution.py:216
  55.9 0.0 collective-permute-done.15.refs_0_
  55.9 0.7 %shard_map.115 = bf16[16,3072]{1,0:T(8,128)(2,1)} custom-call(f32[16,3072]{1,0:T(8,128)S(1)} %get-tuple-element.46.stream_ref, bf16[16,3072]{1,0:T(8,128)(2,1)S(1)} %collective-permute-done.15.refs_0_, bf16[16,3072]{1,0:T(8,128)(2,1)S(1)} %collective-permute-done.16.refs_1_, bf16[16,3072]{1,0:T(8,128)(2,1)S(1)} %collective-permute-done.17.refs_2_), custom_call_target="tpu_custom_call" | custom-call | tf_op jit(solution)/shard_map/pallas_call | solution.py:304
  (3 shorter events, 0.0 us)
Async XLA Ops:
  5.1 6.0 %collective-permute-start.2 = (bf16[16,3200]{1,0:T(8,128)(2,1)S(1)}, bf16[16,3200]{1,0:T(8,128)(2,1)S(1)}, u32[]{:S(2)}, u32[]{:S(2)}) collective-permute-start(bf16[16,3200]{1,0:T(8,128)(2,1)S(1)} %get-tuple-element.27.refs_0_.refs_1_), channel_id=1, source_target_pairs={{0,4},{4,0},{8,12},{12,8},{1,5},{5,1},{9,13},{13,9},{2,6},{6,2},{1... | collective-permute-start | bytes 307208 | tf_op jit(solution)/shard_map/ppermute | solution.py:216
  8.2 8.4 %collective-permute-start.1 = (bf16[16,3200]{1,0:T(8,128)(2,1)S(1)}, bf16[16,3200]{1,0:T(8,128)(2,1)S(1)}, u32[]{:S(2)}, u32[]{:S(2)}) collective-permute-start(bf16[16,3200]{1,0:T(8,128)(2,1)S(1)} %get-tuple-element.27.refs_0_.refs_1_), channel_id=1, source_target_pairs={{0,12},{4,8},{8,4},{12,0},{1,13},{5,9},{9,5},{13,1},{2,14},{6,10},... | collective-permute-start | bytes 307208 | tf_op jit(solution)/shard_map/ppermute | solution.py:216
  10.7 9.3 %collective-permute-start = (bf16[16,3200]{1,0:T(8,128)(2,1)S(1)}, bf16[16,3200]{1,0:T(8,128)(2,1)S(1)}, u32[]{:S(2)}, u32[]{:S(2)}) collective-permute-start(bf16[16,3200]{1,0:T(8,128)(2,1)S(1)} %get-tuple-element.27.refs_0_.refs_1_), channel_id=1, source_target_pairs={{0,8},{4,12},{8,0},{12,4},{1,9},{5,13},{9,1},{13,5},{2,10},{6,14},... | collective-permute-start | bytes 307208 | tf_op jit(solution)/shard_map/ppermute | solution.py:216
  11.1 16.3 %slice-start.6 = ((s8[12582912]{0:T(1024)(128)(4,1)}), s8[4194304]{0:T(1024)(128)(4,1)S(1)}, s32[]{:S(2)}) async-start(s8[12582912]{0:T(1024)(128)(4,1)} %bitcast.14), calls=%async_computation.6 | async-start | bytes 8388608
  11.1 16.3 %slice-start.7 = ((s8[12582912]{0:T(1024)(128)(4,1)}), s8[4194304]{0:T(1024)(128)(4,1)S(1)}, s32[]{:S(2)}) async-start(s8[12582912]{0:T(1024)(128)(4,1)} %bitcast.14), calls=%async_computation.7 | async-start | bytes 8388608
  11.6 8.4 %collective-permute-start.3 = (bf16[16,3072]{1,0:T(8,128)(2,1)S(1)}, bf16[16,3072]{1,0:T(8,128)(2,1)S(1)}, u32[]{:S(2)}, u32[]{:S(2)}) collective-permute-start(bf16[16,3072]{1,0:T(8,128)(2,1)S(1)} %get-tuple-element.29), channel_id=1, source_target_pairs={{0,1},{1,0},{2,3},{3,2},{4,5},{5,4},{6,7},{7,6},{8,9},{9,8},{10,11... | collective-permute-start | bytes 294920 | tf_op jit(solution)/shard_map/ppermute | solution.py:216
  11.7 10.7 %collective-permute-start.4 = (bf16[16,3072]{1,0:T(8,128)(2,1)S(1)}, bf16[16,3072]{1,0:T(8,128)(2,1)S(1)}, u32[]{:S(2)}, u32[]{:S(2)}) collective-permute-start(bf16[16,3072]{1,0:T(8,128)(2,1)S(1)} %get-tuple-element.30), channel_id=1, source_target_pairs={{0,2},{1,3},{2,0},{3,1},{4,6},{5,7},{6,4},{7,5},{8,10},{9,11},{10,... | collective-permute-start | bytes 294920 | tf_op jit(solution)/shard_map/ppermute | solution.py:216
  13.5 14.0 %slice-start = ((s8[12582912]{0:T(1024)(128)(4,1)}), s8[4194304]{0:T(1024)(128)(4,1)S(1)}, s32[]{:S(2)}) async-start(s8[12582912]{0:T(1024)(128)(4,1)} %bitcast.8), calls=%async_computation | async-start | bytes 8388608
  13.5 14.0 %slice-start.3 = ((s8[12582912]{0:T(1024)(128)(4,1)}), s8[4194304]{0:T(1024)(128)(4,1)S(1)}, s32[]{:S(2)}) async-start(s8[12582912]{0:T(1024)(128)(4,1)} %bitcast.11), calls=%async_computation.3 | async-start | bytes 8388608
  13.5 14.0 %slice-start.1 = ((s8[12582912]{0:T(1024)(128)(4,1)}), s8[4194304]{0:T(1024)(128)(4,1)S(1)}, s32[]{:S(2)}) async-start(s8[12582912]{0:T(1024)(128)(4,1)} %bitcast.8), calls=%async_computation.1 | async-start | bytes 8388608
  13.5 14.0 %slice-start.2 = ((s8[12582912]{0:T(1024)(128)(4,1)}), s8[4194304]{0:T(1024)(128)(4,1)S(1)}, s32[]{:S(2)}) async-start(s8[12582912]{0:T(1024)(128)(4,1)} %bitcast.8), calls=%async_computation.2 | async-start | bytes 8388608
  13.5 14.0 %slice-start.4 = ((s8[12582912]{0:T(1024)(128)(4,1)}), s8[4194304]{0:T(1024)(128)(4,1)S(1)}, s32[]{:S(2)}) async-start(s8[12582912]{0:T(1024)(128)(4,1)} %bitcast.11), calls=%async_computation.4 | async-start | bytes 8388608
  13.5 14.0 %slice-start.5 = ((s8[12582912]{0:T(1024)(128)(4,1)}), s8[4194304]{0:T(1024)(128)(4,1)S(1)}, s32[]{:S(2)}) async-start(s8[12582912]{0:T(1024)(128)(4,1)} %bitcast.11), calls=%async_computation.5 | async-start | bytes 8388608
  13.5 14.0 %slice-start.8 = ((s8[12582912]{0:T(1024)(128)(4,1)}), s8[4194304]{0:T(1024)(128)(4,1)S(1)}, s32[]{:S(2)}) async-start(s8[12582912]{0:T(1024)(128)(4,1)} %bitcast.14), calls=%async_computation.8 | async-start | bytes 8388608
  13.5 8.9 %collective-permute-start.5 = (bf16[16,3072]{1,0:T(8,128)(2,1)S(1)}, bf16[16,3072]{1,0:T(8,128)(2,1)S(1)}, u32[]{:S(2)}, u32[]{:S(2)}) collective-permute-start(bf16[16,3072]{1,0:T(8,128)(2,1)S(1)} %get-tuple-element.31), channel_id=1, source_target_pairs={{0,3},{1,2},{2,1},{3,0},{4,7},{5,6},{6,5},{7,4},{8,11},{9,10},{10,... | collective-permute-start | bytes 294920 | tf_op jit(solution)/shard_map/ppermute | solution.py:216
  20.5 2.0 %collective-permute-start.6 = (bf16[16,3072]{1,0:T(8,128)(2,1)S(1)}, bf16[16,3072]{1,0:T(8,128)(2,1)S(1)}, u32[]{:S(2)}, u32[]{:S(2)}) collective-permute-start(bf16[16,3072]{1,0:T(8,128)(2,1)S(1)} %get-tuple-element.33), channel_id=1, source_target_pairs={{0,1},{1,0},{2,3},{3,2},{4,5},{5,4},{6,7},{7,6},{8,9},{9,8},{10,11... | collective-permute-start | bytes 294920 | tf_op jit(solution)/shard_map/ppermute | solution.py:216
  20.6 5.7 %collective-permute-start.7 = (bf16[16,3072]{1,0:T(8,128)(2,1)S(1)}, bf16[16,3072]{1,0:T(8,128)(2,1)S(1)}, u32[]{:S(2)}, u32[]{:S(2)}) collective-permute-start(bf16[16,3072]{1,0:T(8,128)(2,1)S(1)} %get-tuple-element.34), channel_id=1, source_target_pairs={{0,2},{1,3},{2,0},{3,1},{4,6},{5,7},{6,4},{7,5},{8,10},{9,11},{10,... | collective-permute-start | bytes 294920 | tf_op jit(solution)/shard_map/ppermute | solution.py:216
  22.1 5.3 %collective-permute-start.8 = (bf16[16,3072]{1,0:T(8,128)(2,1)S(1)}, bf16[16,3072]{1,0:T(8,128)(2,1)S(1)}, u32[]{:S(2)}, u32[]{:S(2)}) collective-permute-start(bf16[16,3072]{1,0:T(8,128)(2,1)S(1)} %get-tuple-element.35), channel_id=1, source_target_pairs={{0,3},{1,2},{2,1},{3,0},{4,7},{5,6},{6,5},{7,4},{8,11},{9,10},{10,... | collective-permute-start | bytes 294920 | tf_op jit(solution)/shard_map/ppermute | solution.py:216
  27.5 16.3 %copy-start = (bf16[3072,4]{0,1:T(4,128)(2,1)S(1)}, bf16[3072,4]{0,1:T(4,128)(2,1)}, u32[]{:S(2)}) copy-start(bf16[3072,4]{0,1:T(4,128)(2,1)} %param.18) | copy-start | bytes 73732
  36.8 4.0 %collective-permute-start.9 = (bf16[16,3072]{1,0:T(8,128)(2,1)S(1)}, bf16[16,3072]{1,0:T(8,128)(2,1)S(1)}, u32[]{:S(2)}, u32[]{:S(2)}) collective-permute-start(bf16[16,3072]{1,0:T(8,128)(2,1)S(1)} %get-tuple-element.37), channel_id=1, source_target_pairs={{0,1},{1,0},{2,3},{3,2},{4,5},{5,4},{6,7},{7,6},{8,9},{9,8},{10,11... | collective-permute-start | bytes 294920 | tf_op jit(solution)/shard_map/ppermute | solution.py:216
  37.1 5.4 %collective-permute-start.10 = (bf16[16,3072]{1,0:T(8,128)(2,1)S(1)}, bf16[16,3072]{1,0:T(8,128)(2,1)S(1)}, u32[]{:S(2)}, u32[]{:S(2)}) collective-permute-start(bf16[16,3072]{1,0:T(8,128)(2,1)S(1)} %get-tuple-element.38), channel_id=1, source_target_pairs={{0,2},{1,3},{2,0},{3,1},{4,6},{5,7},{6,4},{7,5},{8,10},{9,11},{10,... | collective-permute-start | bytes 294920 | tf_op jit(solution)/shard_map/ppermute | solution.py:216
  38.6 5.3 %collective-permute-start.11 = (bf16[16,3072]{1,0:T(8,128)(2,1)S(1)}, bf16[16,3072]{1,0:T(8,128)(2,1)S(1)}, u32[]{:S(2)}, u32[]{:S(2)}) collective-permute-start(bf16[16,3072]{1,0:T(8,128)(2,1)S(1)} %get-tuple-element.39), channel_id=1, source_target_pairs={{0,3},{1,2},{2,1},{3,0},{4,7},{5,6},{6,5},{7,4},{8,11},{9,10},{10,... | collective-permute-start | bytes 294920 | tf_op jit(solution)/shard_map/ppermute | solution.py:216
  38.7 8.5 %collective-permute-start.12 = (bf16[16,3072]{1,0:T(8,128)(2,1)S(1)}, bf16[16,3072]{1,0:T(8,128)(2,1)S(1)}, u32[]{:S(2)}, u32[]{:S(2)}) collective-permute-start(bf16[16,3072]{1,0:T(8,128)(2,1)S(1)} %get-tuple-element.42), channel_id=1, source_target_pairs={{0,1},{1,0},{2,3},{3,2},{4,5},{5,4},{6,7},{7,6},{8,9},{9,8},{10,11... | collective-permute-start | bytes 294920 | tf_op jit(solution)/shard_map/ppermute | solution.py:216
  39.3 7.9 %collective-permute-start.13 = (bf16[16,3072]{1,0:T(8,128)(2,1)S(1)}, bf16[16,3072]{1,0:T(8,128)(2,1)S(1)}, u32[]{:S(2)}, u32[]{:S(2)}) collective-permute-start(bf16[16,3072]{1,0:T(8,128)(2,1)S(1)} %get-tuple-element.43), channel_id=1, source_target_pairs={{0,2},{1,3},{2,0},{3,1},{4,6},{5,7},{6,4},{7,5},{8,10},{9,11},{10,... | collective-permute-start | bytes 294920 | tf_op jit(solution)/shard_map/ppermute | solution.py:216
  40.8 7.1 %collective-permute-start.14 = (bf16[16,3072]{1,0:T(8,128)(2,1)S(1)}, bf16[16,3072]{1,0:T(8,128)(2,1)S(1)}, u32[]{:S(2)}, u32[]{:S(2)}) collective-permute-start(bf16[16,3072]{1,0:T(8,128)(2,1)S(1)} %get-tuple-element.44), channel_id=1, source_target_pairs={{0,3},{1,2},{2,1},{3,0},{4,7},{5,6},{6,5},{7,4},{8,11},{9,10},{10,... | collective-permute-start | bytes 294920 | tf_op jit(solution)/shard_map/ppermute | solution.py:216
  44.5 7.5 %collective-permute-start.17 = (bf16[16,3072]{1,0:T(8,128)(2,1)S(1)}, bf16[16,3072]{1,0:T(8,128)(2,1)S(1)}, u32[]{:S(2)}, u32[]{:S(2)}) collective-permute-start(bf16[16,3072]{1,0:T(8,128)(2,1)S(1)} %get-tuple-element.48), channel_id=1, source_target_pairs={{0,12},{4,8},{8,4},{12,0},{1,13},{5,9},{9,5},{13,1},{2,14},{6,10},... | collective-permute-start | bytes 294920 | tf_op jit(solution)/shard_map/ppermute | solution.py:216
  47.2 8.7 %collective-permute-start.16 = (bf16[16,3072]{1,0:T(8,128)(2,1)S(1)}, bf16[16,3072]{1,0:T(8,128)(2,1)S(1)}, u32[]{:S(2)}, u32[]{:S(2)}) collective-permute-start(bf16[16,3072]{1,0:T(8,128)(2,1)S(1)} %get-tuple-element.40.refs_0_), channel_id=1, source_target_pairs={{0,8},{4,12},{8,0},{12,4},{1,9},{5,13},{9,1},{13,5},{2,10},{6,14},... | collective-permute-start | bytes 294920 | tf_op jit(solution)/shard_map/ppermute | solution.py:216
  48.5 7.4 %collective-permute-start.15 = (bf16[16,3072]{1,0:T(8,128)(2,1)S(1)}, bf16[16,3072]{1,0:T(8,128)(2,1)S(1)}, u32[]{:S(2)}, u32[]{:S(2)}) collective-permute-start(bf16[16,3072]{1,0:T(8,128)(2,1)S(1)} %get-tuple-element.47), channel_id=1, source_target_pairs={{0,4},{4,0},{8,12},{12,8},{1,5},{5,1},{9,13},{13,9},{2,6},{6,2},{1... | collective-permute-start | bytes 294920 | tf_op jit(solution)/shard_map/ppermute | solution.py:216

commit v5 on v4

--- a/solution.py
+++ b/solution.py
@@ -12,11 +12,13 @@
 GROUP = 6
 CAP = 8
 LANES = 128
-BLOCK = 8
+PAIR = 2
+EARLY = 1
 MIB = 1 << 20
 F32 = jnp.float32
 BF16 = jnp.bfloat16
-BUSY = pl.CostEstimate(flops=12_000_000_000, bytes_accessed=4_000_000, transcendentals=0)
+LIGHT = pl.CostEstimate(flops=0, bytes_accessed=0, transcendentals=0)
+BUSY = pl.CostEstimate(flops=24 * 10**9, bytes_accessed=0, transcendentals=0)
 ANY = pl.BlockSpec(memory_space=pl.ANY)
 WHOLE = pl.BlockSpec(memory_space=pltpu.VMEM)
 SCALAR = pl.BlockSpec(memory_space=pltpu.SMEM)
@@ -77,15 +79,18 @@
     batch, window, _ = keys_ref.shape
     width = queries_ref.shape[1]
     span = width // KVH
-    blocks = [pl.ds(begin, BLOCK) for begin in range(0, batch, BLOCK)]
+    parts = [pl.ds(begin, PAIR * HS) for begin in range(0, KVH * HS, PAIR * HS)]
     small = [
         (lengths_hbm, lengths_ref), (queries_hbm, queries_ref), (routes_hbm, routes_ref),
         (residual_hbm, residual_ref), (gain_hbm, gain_ref),
     ]
     caches = [
-        (source.at[block], target.at[block])
-        for block in blocks
-        for source, target in ((keys_hbm, keys_ref), (values_hbm, values_ref))
+        pair
+        for part in parts
+        for pair in (
+            (keys_hbm.at[:, :, part], keys_ref.at[:, :, part]),
+            (values_hbm.at[:, :, part], values_ref.at[:, 0:window, part]),
+        )
     ]
     copies = [
         pltpu.make_async_copy(source, target, sems.at[i])
@@ -93,6 +98,10 @@
     ]
     for copy in copies:
         copy.start()
+    padded = values_ref.shape[1]
+    if padded > window:
+        pad = (batch, padded - window, values_ref.shape[2])
+        values_ref[:, window:, :] = jnp.zeros(pad, BF16)
     copies[0].wait()
     copies[1].wait()
     same = iota((batch, batch), 0) == iota((batch, batch), 1)
@@ -100,38 +109,53 @@
     def upright(row):
         return jnp.sum(jnp.where(same, row, 0), axis=1, keepdims=True)
 
-    lengths = upright(lengths_ref[...])
-    queries = queries_ref[...].astype(F32)
-    row = iota((BLOCK, BLOCK * window), 0)
-    column = iota((BLOCK, BLOCK * window), 1) - row * window
+    queries = queries_ref[...]
+    lanes = PAIR * GROUP * batch
+    full = -(-lanes // LANES) * LANES
+    request = iota((window, full), 1) % batch
+    length = jnp.zeros((1, full), jnp.int32)
+    for r in range(batch):
+        length = jnp.where(request[0:1] == r, lengths_ref[0:1, r : r + 1], length)
+    visible = iota((window, full), 0) < length
+    owner = iota((lanes, padded), 0) % batch
     attended = []
-    for i, block in enumerate(blocks):
-        begin = i * BLOCK
-        bias = jnp.where((column >= 0) & (column < lengths[begin : begin + BLOCK]), 0.0, -1e30)
-        bias = jnp.concatenate([bias] * GROUP, axis=0)
+    for i, part in enumerate(parts):
+        spread = []
+        for k in range(PAIR):
+            at = [(i * PAIR + k) * span + g * HS for g in range(GROUP)]
+            stacked = jnp.concatenate([queries[:, c : c + HS] for c in at], axis=0)
+            blank = jnp.zeros_like(stacked)
+            spread.append(
+                jnp.concatenate([stacked if j == k else blank for j in range(PAIR)], axis=1)
+            )
+        if full > lanes:
+            spread.append(jnp.zeros((full - lanes, PAIR * HS), BF16))
+        spread = jnp.concatenate(spread, axis=0)
         copies[2 + 2 * i].wait()
+        keys = keys_ref[:, :, part].reshape(batch * window, PAIR * HS)
+        products = dot(keys, spread, ((1,), (1,)))
+        scores = products[:window]
+        for r in range(1, batch):
+            scores = jnp.where(request == r, products[r * window : (r + 1) * window], scores)
+        scores = jnp.where(visible, scores * HS ** (-0.5), -1e30)
+        powers = jnp.exp(scores - jnp.max(scores, axis=0, keepdims=True))
+        weights = powers / jnp.sum(powers, axis=0, keepdims=True)
+        if padded > window:
+            weights = jnp.concatenate([weights, jnp.zeros((padded - window, full), F32)], axis=0)
+        weights = weights.T[:lanes]
+        weights = jnp.concatenate(
+            [jnp.where(owner == r, weights, 0.0).astype(BF16) for r in range(batch)], axis=1
+        )
         copies[3 + 2 * i].wait()
-        heads = []
-        for k in range(KVH):
-            keys = keys_ref[block, :, k * HS : (k + 1) * HS].reshape(BLOCK * window, HS)
-            values = values_ref[block, :, k * HS : (k + 1) * HS].reshape(BLOCK * window, HS)
-            stacked = jnp.concatenate(
-                [
-                    queries[begin : begin + BLOCK, k * span + g * HS : k * span + (g + 1) * HS]
-                    for g in range(GROUP)
-                ],
-                axis=0,
-            ).astype(BF16)
-            scores = dot(stacked, keys, ((1,), (1,))) * HS ** (-0.5) + bias
-            highest = jnp.max(scores, axis=1, keepdims=True)
-            powers = jnp.exp(scores - highest)
-            weights = (powers / jnp.sum(powers, axis=1, keepdims=True)).astype(BF16)
-            mixed = dot(weights, values)
-            heads += [mixed[g * BLOCK : (g + 1) * BLOCK] for g in range(GROUP)]
-        attended.append(jnp.concatenate(heads, axis=1))
-    for copy in copies[2 + 2 * len(blocks) :]:
+        values = values_ref[:, :, part].reshape(batch * padded, PAIR * HS)
+        mixed = dot(weights, values)
+        attended += [
+            mixed[h * batch : (h + 1) * batch, h // GROUP * HS : (h // GROUP + 1) * HS]
+            for h in range(PAIR * GROUP)
+        ]
+    for copy in copies[2 + 2 * len(parts) :]:
         copy.wait()
-    stream = residual_ref[...].astype(F32) + jnp.concatenate(attended, axis=0)
+    stream = residual_ref[...].astype(F32) + jnp.concatenate(attended, axis=1)
     scale = lax.rsqrt(jnp.mean(stream * stream, axis=1, keepdims=True) + 1e-05)
     lane = iota((batch, LANES), 1)
     routes = [upright(routes_ref[k : k + 1, :]).astype(F32) for k in range(2)]
@@ -157,10 +181,7 @@
     xs, (gate_ref, up_ref, down_ref) = refs[:pieces], refs[pieces : pieces + 3]
     outs = refs[pieces + 3 : 2 * pieces + 3]
     rows_ref, hidden_ref = refs[2 * pieces + 3 :]
-    begin = 0
-    for ref in xs:
-        rows_ref[begin : begin + ref.shape[0], :] = ref[...]
-        begin += ref.shape[0]
+    rows_ref[...] = jnp.concatenate([ref[...].astype(F32) for ref in xs], axis=0).astype(BF16)
     width, units = gate_ref.shape
     tile = min(256, units)
 
@@ -182,18 +203,21 @@
             begin += count
 
 
-def mix_kernel(me_ref, router_ref, *refs, chunks, experts, own, after):
-    refs = refs[after:]
+def mix_kernel(me_ref, router_ref, *refs, chunks, experts, later):
     payload = jnp.concatenate([ref[...] for ref in refs[:chunks]], axis=0)
-    returned = jnp.concatenate([ref[...] for ref in refs[chunks : chunks + experts]], axis=0)
-    outs = refs[chunks + experts + own :]
+    returned = jnp.concatenate(
+        [ref[...].astype(F32) for ref in refs[chunks : chunks + experts]], axis=0
+    ).astype(BF16)
+    outs = refs[len(refs) - chunks - later : len(refs) - later]
     batch, width = outs[0].shape
     rows, named = payload[:, :width], payload[:, width:]
     mixed = combine(me_ref[0], rows, named, router_ref[...], returned, chunks, experts)
     for j, ref in enumerate(outs):
         part = mixed[j * batch : (j + 1) * batch]
-        if own and j == 0:
-            ref[...] = refs[chunks + experts][...] + part
+        if ref.dtype == F32:
+            for other in refs[chunks + experts : len(refs) - chunks - later]:
+                part = part + other[...].astype(F32)
+            ref[...] = part
         else:
             ref[...] = part.astype(BF16)
 
@@ -245,19 +269,22 @@
             lengths[None], queries, cached_keys, cached_values, routes.T, residual, norm_gain[None]
         )
     ]
+    window, depth = cached_values.shape[1:]
+    held = [a.shape for a in operands]
+    held[3] = (batch, -(-window // LANES) * LANES, depth)
     stream, payload = pl.pallas_call(
         attend_kernel,
         in_specs=[ANY] * len(operands),
         out_specs=[WHOLE, WHOLE],
         out_shape=[shape((batch, width), F32), shape((batch, width + LANES), BF16)],
-        scratch_shapes=[pltpu.VMEM(a.shape, a.dtype) for a in operands]
-        + [pltpu.SemaphoreType.DMA((5 + 2 * (batch // BLOCK),))],
+        scratch_shapes=[pltpu.VMEM(size, a.dtype) for size, a in zip(held, operands)]
+        + [pltpu.SemaphoreType.DMA((5 + 2 * (KVH // PAIR),))],
         compiler_params=params(28 * batch * width),
-        cost_estimate=pl.CostEstimate(flops=10**9, bytes_accessed=4 * 10**6, transcendentals=10**6),
+        cost_estimate=pl.CostEstimate(flops=10**9, bytes_accessed=4 * 10**6, transcendentals=0),
     )(*operands)
 
     chunks = [swap(payload, "attn", j) for j in range(layers)]
-    groups = [list(range(2)), list(range(2, layers))]
+    groups = [[0, 1], [2], list(range(3, layers))]
     inputs, ahead = [], []
     for group in groups:
         count = len(group)
@@ -266,7 +293,7 @@
             in_specs=[SCALAR] + [ANY] * len(ahead) + [WHOLE] * count,
             out_specs=[WHOLE] * experts,
             out_shape=[shape((count * CAP, width), BF16)] * experts,
-            cost_estimate=BUSY,
+            cost_estimate=BUSY if group == [2] else LIGHT,
             compiler_params=params(experts * count * CAP * width),
         )(me, *ahead, *[chunks[j] for j in group])
         arrived = [swap(slots[e], "expert", e) for e in range(experts)]
@@ -284,22 +311,27 @@
         compiler_params=params(total_rows * width),
     )(*inputs, gate_proj[0], up_proj[0], down_proj[0])
 
-    received, before = [], []
+    results = [results[i : i + experts] for i in range(0, len(results), experts)]
+    received = []
     for i, group in list(enumerate(groups))[::-1]:
         count, own = len(group), int(group[0] == 0)
-        returned = [swap(results[i * experts + e], "expert", e) for e in range(experts)]
+        returned = [swap(results[i][e], "expert", e) for e in range(experts)]
+        later = results[0][1:] if i == 1 else []
+        added = [stream, *received[EARLY:]] if own else []
+        operands = [me, router, *[chunks[j] for j in group], *returned, *added]
         mixed = pl.pallas_call(
-            functools.partial(
-                mix_kernel, chunks=count, experts=experts, own=own, after=len(before)
-            ),
-            in_specs=[SCALAR, WHOLE]
-            + [ANY] * len(before)
-            + [WHOLE] * (count + experts + own),
-            out_specs=[WHOLE] * count,
-            out_shape=[shape((batch, width), F32 if j == 0 else BF16) for j in group],
+            functools.partial(mix_kernel, chunks=count, experts=experts, later=len(later)),
+            in_specs=[SCALAR] + [WHOLE] * (len(operands) - 1) + [ANY] * len(later),
+            out_specs=[WHOLE] * count + [ANY] * len(later),
+            out_shape=[shape((batch, width), F32 if j == 0 else BF16) for j in group]
+            + [shape(block.shape, BF16) for block in later],
+            cost_estimate=LIGHT,
+            input_output_aliases={len(operands) + k: count + k for k in range(len(later))},
             compiler_params=params(experts * count * CAP * width),
-        )(me, router, *before, *[chunks[j] for j in group], *returned, *[stream] * own)
-        before = mixed[:1]
+        )(*operands, *later)
+        if later:
+            results[0] = [results[0][0], *mixed[count:]]
+        received = received[:EARLY] if own else received
         received = [swap(block, "attn", j) for j, block in zip(group, mixed)] + received
     return pl.pallas_call(
         finish_kernel,

time: 56.7 us -> 59.1 us (1.042)
  starting transfers between devices: 17.4 us -> 26.4 us
  waiting for transfers between devices: 21.7 us -> 13.5 us
  local copies, waits for them, and re-layouts: 0.05 us -> 2.09 us
    ppermute x18 -> x24, starting transfers between devices: 17.4 us -> 26.4 us  [swap(): return lax.ppermute(value, axis, [(i, i ^ step) for i in range(count)])]
    ppermute x18 -> x24, waiting for transfers between devices: 21.7 us -> 13.5 us  [swap(): return lax.ppermute(value, axis, [(i, i ^ step) for i in range(count)])]
    unnamed x20, local copies, waits for them, and re-layouts: 0.05 us -> 2.09 us
    pallas_call x1, Pallas kernels: 5.14 us -> 3.99 us  [shards(): pl.pallas_call(attend_kernel, in_specs=[ANY] * len(operands), out_specs=[...]
    pallas_call x2 -> x3, Pallas kernels: 1.22 us -> 1.61 us  [shards(): pl.pallas_call(functools.partial(mix_kernel, chunks=count, experts=expert...]
    pallas_call x2 -> x3, Pallas kernels: 0.96 us -> 1.31 us  [shards(): pl.pallas_call(functools.partial(split_kernel, chunks=count, after=len(ah...]
  transfers between devices with their start and end apart: 18 -> 24, of which waited for: 10 -> 11; matrix products, arithmetic and copies ran while one was open for 0% -> 0% of each run, Pallas kernels for 4% -> 5%
where the time goes in v5:
time: 59.1 us; the launch traced here: 59 us
  starting transfers between devices  26.4 us (45%)
  Pallas kernels  16.8 us (28%)
  waiting for transfers between devices  13.5 us (23%)
  local copies, waits for them, and re-layouts  2.09 us (4%)
    ppermute x24, starting transfers between devices, swap(): return lax.ppermute(value, axis, [(i, i ^ step) for i in range(count)])  26.4 us
    ppermute x24, waiting for transfers between devices, swap(): return lax.ppermute(value, axis, [(i, i ^ step) for i in range(count)])  13.5 us
    pallas_call x1, Pallas kernels, shards(): pl.pallas_call(functools.partial(expert_kernel, pieces=len(inputs)), in_s...  9.23 us
    pallas_call x1, Pallas kernels, shards(): pl.pallas_call(attend_kernel, in_specs=[ANY] * len(operands), out_specs=[...  3.99 us
    unnamed x20, local copies, waits for them, and re-layouts  2.09 us
    pallas_call x3, Pallas kernels, shards(): pl.pallas_call(functools.partial(mix_kernel, chunks=count, experts=expert...  1.61 us
    pallas_call x3, Pallas kernels, shards(): pl.pallas_call(functools.partial(split_kernel, chunks=count, after=len(ah...  1.31 us
  transfers between devices with their start and end apart: 24, of which 11 were waited for; matrix products, arithmetic and copies ran while one was open for 0% of the time, Pallas kernels for 5%

profile of v5, /device:TPU:0, one launch (start us, length us, event | category | flops | bytes accessed | tf_op | source)
XLA Modules:
  0.0 59.0 jit_solution(6219823207617378815)
XLA Ops:
  0.0 4.0 %shard_map.109 = (f32[16,3072]{1,0:T(8,128)S(1)}, bf16[16,3200]{1,0:T(8,128)(2,1)S(1)}) custom-call(s32[1,16]{1,0:T(1,128)} %bitcast.22, bf16[16,3072]{1,0:T(8,128)(2,1)} %queries_hbm.1, bf16[16,96,512]{2,1,0:T(8,128)(2,1)} %keys_hbm.1, bf16[16,96,512]{2,1,0:T(8,128)(2,1)} %values_hbm.1, s32[2,16]{1,0:T(2,128)} %bitcast.21, bf16[16,3072]{1,0:T(8,128)(2,1)} %residual_hbm.1, ...), custom_call_target="tpu_custom_call" | custom-call | flops 1000000000 | bytes 4000000 | tf_op jit(solution)/shard_map/pallas_call | solution.py:275
  4.0 3.1 %collective-permute-start = (bf16[16,3200]{1,0:T(8,128)(2,1)S(1)}, bf16[16,3200]{1,0:T(8,128)(2,1)S(1)}, u32[]{:S(2)}, u32[]{:S(2)}) collective-permute-start(bf16[16,3200]{1,0:T(8,128)(2,1)S(1)} %get-tuple-element.37.refs_0_), channel_id=1, source_target_pairs={{0,4},{4,0},{8,12},{12,8},{1,5},{5,1},{9,13},{13,9},{2,6},{6,2},{1... | collective-permute-start | bytes 307208 | tf_op jit(solution)/shard_map/ppermute | solution.py:240
  7.1 2.6 %collective-permute-start.4 = (bf16[16,3200]{1,0:T(8,128)(2,1)S(1)}, bf16[16,3200]{1,0:T(8,128)(2,1)S(1)}, u32[]{:S(2)}, u32[]{:S(2)}) collective-permute-start(bf16[16,3200]{1,0:T(8,128)(2,1)S(1)} %get-tuple-element.37.refs_0_), channel_id=1, source_target_pairs={{0,8},{4,12},{8,0},{12,4},{1,9},{5,13},{9,1},{13,5},{2,10},{6,14},... | collective-permute-start | bytes 307208 | tf_op jit(solution)/shard_map/ppermute | solution.py:240
  9.7 0.3 collective-permute-done.refs_1_
  10.0 0.5 shard_map.110
  10.4 0.1 collective-permute-start.1
  10.5 5.0 %collective-permute-start.8 = (bf16[16,3200]{1,0:T(8,128)(2,1)S(1)}, bf16[16,3200]{1,0:T(8,128)(2,1)S(1)}, u32[]{:S(2)}, u32[]{:S(2)}) collective-permute-start(bf16[16,3200]{1,0:T(8,128)(2,1)S(1)} %get-tuple-element.37.refs_0_), channel_id=1, source_target_pairs={{0,12},{4,8},{8,4},{12,0},{1,13},{5,9},{9,5},{13,1},{2,14},{6,10},... | collective-permute-start | bytes 307208 | tf_op jit(solution)/shard_map/ppermute | solution.py:240
  15.5 1.5 %collective-permute-start.2 = (bf16[16,3072]{1,0:T(8,128)(2,1)S(1)}, bf16[16,3072]{1,0:T(8,128)(2,1)S(1)}, u32[]{:S(2)}, u32[]{:S(2)}) collective-permute-start(bf16[16,3072]{1,0:T(8,128)(2,1)S(1)} %get-tuple-element.40), channel_id=1, source_target_pairs={{0,2},{1,3},{2,0},{3,1},{4,6},{5,7},{6,4},{7,5},{8,10},{9,11},{10,... | collective-permute-start | bytes 294920 | tf_op jit(solution)/shard_map/ppermute | solution.py:240
  17.0 0.0 slice-start.2
  17.0 0.0 slice-start.4
  17.0 0.0 slice-start.5
  17.0 0.0 slice-start.7
  17.0 0.0 slice-start.8
  17.0 0.1 collective-permute-start.3
  17.1 0.0 collective-permute-done.4.refs_1_.refs_0_
  17.1 0.0 collective-permute-done.1.refs_0_.refs_1_
  17.1 0.4 shard_map.111
  17.6 0.7 %collective-permute-start.5 = (bf16[8,3072]{1,0:T(8,128)(2,1)S(1)}, bf16[8,3072]{1,0:T(8,128)(2,1)S(1)}, u32[]{:S(2)}, u32[]{:S(2)}) collective-permute-start(bf16[8,3072]{1,0:T(8,128)(2,1)S(1)} %get-tuple-element.43), channel_id=1, source_target_pairs={{0,1},{1,0},{2,3},{3,2},{4,5},{5,4},{6,7},{7,6},{8,9},{9,8},{10,11... | collective-permute-start | bytes 147464 | tf_op jit(solution)/shard_map/ppermute | solution.py:240
  18.3 1.5 %collective-permute-start.6 = (bf16[8,3072]{1,0:T(8,128)(2,1)S(1)}, bf16[8,3072]{1,0:T(8,128)(2,1)S(1)}, u32[]{:S(2)}, u32[]{:S(2)}) collective-permute-start(bf16[8,3072]{1,0:T(8,128)(2,1)S(1)} %get-tuple-element.44), channel_id=1, source_target_pairs={{0,2},{1,3},{2,0},{3,1},{4,6},{5,7},{6,4},{7,5},{8,10},{9,11},{10,... | collective-permute-start | bytes 147464 | tf_op jit(solution)/shard_map/ppermute | solution.py:240
  19.7 0.0 collective-permute-done.8.refs_1_.refs_0_
  19.7 0.2 collective-permute-start.7
  20.0 0.0 collective-permute-done.5.refs_0_.refs_5_
  20.0 0.4 shard_map.112
  20.4 0.8 %collective-permute-start.9 = (bf16[8,3072]{1,0:T(8,128)(2,1)S(1)}, bf16[8,3072]{1,0:T(8,128)(2,1)S(1)}, u32[]{:S(2)}, u32[]{:S(2)}) collective-permute-start(bf16[8,3072]{1,0:T(8,128)(2,1)S(1)} %get-tuple-element.47), channel_id=1, source_target_pairs={{0,1},{1,0},{2,3},{3,2},{4,5},{5,4},{6,7},{7,6},{8,9},{9,8},{10,11... | collective-permute-start | bytes 147464 | tf_op jit(solution)/shard_map/ppermute | solution.py:240
  21.2 0.0 collective-permute-done.2.refs_2_
  21.2 1.4 %collective-permute-start.10 = (bf16[8,3072]{1,0:T(8,128)(2,1)S(1)}, bf16[8,3072]{1,0:T(8,128)(2,1)S(1)}, u32[]{:S(2)}, u32[]{:S(2)}) collective-permute-start(bf16[8,3072]{1,0:T(8,128)(2,1)S(1)} %get-tuple-element.48), channel_id=1, source_target_pairs={{0,2},{1,3},{2,0},{3,1},{4,6},{5,7},{6,4},{7,5},{8,10},{9,11},{10,... | collective-permute-start | bytes 147464 | tf_op jit(solution)/shard_map/ppermute | solution.py:240
  22.6 0.0 collective-permute-done.3.refs_3_
  22.6 1.8 %collective-permute-start.11 = (bf16[8,3072]{1,0:T(8,128)(2,1)S(1)}, bf16[8,3072]{1,0:T(8,128)(2,1)S(1)}, u32[]{:S(2)}, u32[]{:S(2)}) collective-permute-start(bf16[8,3072]{1,0:T(8,128)(2,1)S(1)} %get-tuple-element.49), channel_id=1, source_target_pairs={{0,3},{1,2},{2,1},{3,0},{4,7},{5,6},{6,5},{7,4},{8,11},{9,10},{10,... | collective-permute-start | bytes 147464 | tf_op jit(solution)/shard_map/ppermute | solution.py:240
  24.4 0.0 collective-permute-done.6.refs_6_
  24.4 0.0 collective-permute-done.7.refs_7_
  24.4 0.0 collective-permute-done.9.refs_9_
  24.5 1.2 %collective-permute-done.10.refs_10_ = bf16[8,3072]{1,0:T(8,128)(2,1)S(1)} collective-permute-done((bf16[8,3072]{1,0:T(8,128)(2,1)S(1)}, bf16[8,3072]{1,0:T(8,128)(2,1)S(1)}, u32[]{:S(2)}, u32[]{:S(2)}) %collective-permute-start.10) | collective-permute-done | bytes 49184 | tf_op jit(solution)/shard_map/ppermute | solution.py:240
  25.6 1.1 %collective-permute-done.11.refs_11_ = bf16[8,3072]{1,0:T(8,128)(2,1)S(1)} collective-permute-done((bf16[8,3072]{1,0:T(8,128)(2,1)S(1)}, bf16[8,3072]{1,0:T(8,128)(2,1)S(1)}, u32[]{:S(2)}, u32[]{:S(2)}) %collective-permute-start.11) | collective-permute-done | bytes 49184 | tf_op jit(solution)/shard_map/ppermute | solution.py:240
  26.8 0.9 %slice-done.7 = s8[4194304]{0:T(1024)(128)(4,1)S(1)} async-done(((s8[12582912]{0:T(1024)(128)(4,1)}), s8[4194304]{0:T(1024)(128)(4,1)S(1)}, s32[]{:S(2)}) %slice-start.7) | async-done | bytes 4194328
  27.6 1.2 %slice-done.8 = s8[4194304]{0:T(1024)(128)(4,1)S(1)} async-done(((s8[12582912]{0:T(1024)(128)(4,1)}), s8[4194304]{0:T(1024)(128)(4,1)S(1)}, s32[]{:S(2)}) %slice-start.8) | async-done | bytes 4194328
  28.8 9.2 %shard_map.113 = (bf16[16,3072]{1,0:T(8,128)(2,1)S(1)}, bf16[16,3072]{1,0:T(8,128)(2,1)S(1)}, bf16[16,3072]{1,0:T(8,128)(2,1)S(1)}, bf16[16,3072]{1,0:T(8,128)(2...) custom-call(bf16[16,3072]{1,0:T(8,128)(2,1)S(1)} %get-tuple-element., ...), custom_call_target="tpu_custom_call" | custom-call | tf_op jit(solution)/shard_map/pallas_call | solution.py:305
  38.0 0.1 collective-permute-start.18
  38.1 0.6 %collective-permute-start.19 = (bf16[8,3072]{1,0:T(8,128)(2,1)S(1)}, bf16[8,3072]{1,0:T(8,128)(2,1)S(1)}, u32[]{:S(2)}, u32[]{:S(2)}) collective-permute-start(bf16[8,3072]{1,0:T(8,128)(2,1)S(1)} %get-tuple-element.64), channel_id=1, source_target_pairs={{0,2},{1,3},{2,0},{3,1},{4,6},{5,7},{6,4},{7,5},{8,10},{9,11},{10,... | collective-permute-start | bytes 147464 | tf_op jit(solution)/shard_map/ppermute | solution.py:240
  38.7 1.3 %collective-permute-start.20 = (bf16[8,3072]{1,0:T(8,128)(2,1)S(1)}, bf16[8,3072]{1,0:T(8,128)(2,1)S(1)}, u32[]{:S(2)}, u32[]{:S(2)}) collective-permute-start(bf16[8,3072]{1,0:T(8,128)(2,1)S(1)} %get-tuple-element.65), channel_id=1, source_target_pairs={{0,3},{1,2},{2,1},{3,0},{4,7},{5,6},{6,5},{7,4},{8,11},{9,10},{10,... | collective-permute-start | bytes 147464 | tf_op jit(solution)/shard_map/ppermute | solution.py:240
  40.0 0.3 collective-permute-start.12
  40.3 0.5 collective-permute-start.13
  40.9 0.0 collective-permute-done.18.refs_2_
  40.9 1.0 %collective-permute-start.14 = (bf16[8,3072]{1,0:T(8,128)(2,1)S(1)}, bf16[8,3072]{1,0:T(8,128)(2,1)S(1)}, u32[]{:S(2)}, u32[]{:S(2)}) collective-permute-start(bf16[8,3072]{1,0:T(8,128)(2,1)S(1)} %get-tuple-element.54), channel_id=1, source_target_pairs={{0,3},{1,2},{2,1},{3,0},{4,7},{5,6},{6,5},{7,4},{8,11},{9,10},{10,... | collective-permute-start | bytes 147464 | tf_op jit(solution)/shard_map/ppermute | solution.py:240
  41.9 0.9 %collective-permute-done.19.refs_3_ = bf16[8,3072]{1,0:T(8,128)(2,1)S(1)} collective-permute-done((bf16[8,3072]{1,0:T(8,128)(2,1)S(1)}, bf16[8,3072]{1,0:T(8,128)(2,1)S(1)}, u32[]{:S(2)}, u32[]{:S(2)}) %collective-permute-start.19) | collective-permute-done | bytes 49184 | tf_op jit(solution)/shard_map/ppermute | solution.py:240
  42.7 0.1 collective-permute-done.20.refs_4_
  42.9 0.5 shard_map.115
  43.4 1.2 %collective-permute-start.21 = (bf16[16,3072]{1,0:T(8,128)(2,1)S(1)}, bf16[16,3072]{1,0:T(8,128)(2,1)S(1)}, u32[]{:S(2)}, u32[]{:S(2)}) collective-permute-start(bf16[16,3072]{1,0:T(8,128)(2,1)S(1)} %shard_map.115), channel_id=1, source_target_pairs={{0,12},{4,8},{8,4},{12,0},{1,13},{5,9},{9,5},{13,1},{2,14},{6,10},... | collective-permute-start | bytes 294920 | tf_op jit(solution)/shard_map/ppermute | solution.py:240
  44.5 0.0 collective-permute-done.12.refs_2_
  44.5 0.4 collective-permute-done.13.refs_3_
  44.9 0.0 collective-permute-done.14.refs_4_
  44.9 0.5 shard_map.114
  45.4 0.4 collective-permute-start.15
  45.8 1.2 %collective-permute-start.16 = (bf16[16,3072]{1,0:T(8,128)(2,1)S(1)}, bf16[16,3072]{1,0:T(8,128)(2,1)S(1)}, u32[]{:S(2)}, u32[]{:S(2)}) collective-permute-start(bf16[16,3072]{1,0:T(8,128)(2,1)S(1)} %get-tuple-element.59), channel_id=1, source_target_pairs={{0,2},{1,3},{2,0},{3,1},{4,6},{5,7},{6,4},{7,5},{8,10},{9,11},{10,... | collective-permute-start | bytes 294920 | tf_op jit(solution)/shard_map/ppermute | solution.py:240
  47.0 0.3 collective-permute-start.17
  47.4 0.8 %collective-permute-start.23 = (bf16[16,3072]{1,0:T(8,128)(2,1)S(1)}, bf16[16,3072]{1,0:T(8,128)(2,1)S(1)}, u32[]{:S(2)}, u32[]{:S(2)}) collective-permute-start(bf16[16,3072]{1,0:T(8,128)(2,1)S(1)} %get-tuple-element.68), channel_id=1, source_target_pairs={{0,8},{4,12},{8,0},{12,4},{1,9},{5,13},{9,1},{13,5},{2,10},{6,14},... | collective-permute-start | bytes 294920 | tf_op jit(solution)/shard_map/ppermute | solution.py:240
  48.1 2.3 %collective-permute-done.21.refs_7_ = bf16[16,3072]{1,0:T(8,128)(2,1)S(1)} collective-permute-done((bf16[16,3072]{1,0:T(8,128)(2,1)S(1)}, bf16[16,3072]{1,0:T(8,128)(2,1)S(1)}, u32[]{:S(2)}, u32[]{:S(2)}) %collective-permute-start.21) | collective-permute-done | bytes 98336 | tf_op jit(solution)/shard_map/ppermute | solution.py:240
  50.4 0.0 collective-permute-done.15.refs_3_
  50.4 1.0 %collective-permute-done.16.refs_4_ = bf16[16,3072]{1,0:T(8,128)(2,1)S(1)} collective-permute-done((bf16[16,3072]{1,0:T(8,128)(2,1)S(1)}, bf16[16,3072]{1,0:T(8,128)(2,1)S(1)}, u32[]{:S(2)}, u32[]{:S(2)}) %collective-permute-start.16) | collective-permute-done | bytes 98336 | tf_op jit(solution)/shard_map/ppermute | solution.py:240
  51.5 0.6 %collective-permute-done.17.refs_5_ = bf16[16,3072]{1,0:T(8,128)(2,1)S(1)} collective-permute-done((bf16[16,3072]{1,0:T(8,128)(2,1)S(1)}, bf16[16,3072]{1,0:T(8,128)(2,1)S(1)}, u32[]{:S(2)}, u32[]{:S(2)}) %collective-permute-start.17) | collective-permute-done | bytes 98336 | tf_op jit(solution)/shard_map/ppermute | solution.py:240
  52.1 0.6 %shard_map.116 = (f32[16,3072]{1,0:T(8,128)S(1)}, bf16[16,3072]{1,0:T(8,128)(2,1)S(1)}) custom-call(s32[1]{0:T(128)} %bitcast.me_ref, bf16[4,3072]{1,0:T(4,128)(2,1)S(1)} %bitcast.19, bf16[16,3200]{1,0:T(8,128)(2,1)S(1)} %get-tuple-element.37.refs_0_, bf16[16,3200]{1,0:T(8,128)(2,1)S(1)} %collective-permute-done.refs_1_, ...), custom_call_target="tpu_custom_call" | custom-call | tf_op jit(solution)/shard_map/pallas_call | solution.py:322
  52.7 0.1 collective-permute-start.22
  52.8 2.5 %collective-permute-done.23.refs_1_ = bf16[16,3072]{1,0:T(8,128)(2,1)S(1)} collective-permute-done((bf16[16,3072]{1,0:T(8,128)(2,1)S(1)}, bf16[16,3072]{1,0:T(8,128)(2,1)S(1)}, u32[]{:S(2)}, u32[]{:S(2)}) %collective-permute-start.23) | collective-permute-done | bytes 98336 | tf_op jit(solution)/shard_map/ppermute | solution.py:240
  55.3 3.1 %collective-permute-done.22.refs_0_ = bf16[16,3072]{1,0:T(8,128)(2,1)S(1)} collective-permute-done((bf16[16,3072]{1,0:T(8,128)(2,1)S(1)}, bf16[16,3072]{1,0:T(8,128)(2,1)S(1)}, u32[]{:S(2)}, u32[]{:S(2)}) %collective-permute-start.22) | collective-permute-done | bytes 98336 | tf_op jit(solution)/shard_map/ppermute | solution.py:240
  58.3 0.7 %shard_map.117 = bf16[16,3072]{1,0:T(8,128)(2,1)} custom-call(f32[16,3072]{1,0:T(8,128)S(1)} %get-tuple-element.66.stream_ref, bf16[16,3072]{1,0:T(8,128)(2,1)S(1)} %collective-permute-done.22.refs_0_, bf16[16,3072]{1,0:T(8,128)(2,1)S(1)} %collective-permute-done.23.refs_1_), custom_call_target="tpu_custom_call" | custom-call | tf_op jit(solution)/shard_map/pallas_call | solution.py:336
  (16 shorter events, 0.0 us)
Async XLA Ops:
  4.0 6.0 %collective-permute-start = (bf16[16,3200]{1,0:T(8,128)(2,1)S(1)}, bf16[16,3200]{1,0:T(8,128)(2,1)S(1)}, u32[]{:S(2)}, u32[]{:S(2)}) collective-permute-start(bf16[16,3200]{1,0:T(8,128)(2,1)S(1)} %get-tuple-element.37.refs_0_), channel_id=1, source_target_pairs={{0,4},{4,0},{8,12},{12,8},{1,5},{5,1},{9,13},{13,9},{2,6},{6,2},{1... | collective-permute-start | bytes 307208 | tf_op jit(solution)/shard_map/ppermute | solution.py:240
  7.1 10.1 %collective-permute-start.4 = (bf16[16,3200]{1,0:T(8,128)(2,1)S(1)}, bf16[16,3200]{1,0:T(8,128)(2,1)S(1)}, u32[]{:S(2)}, u32[]{:S(2)}) collective-permute-start(bf16[16,3200]{1,0:T(8,128)(2,1)S(1)} %get-tuple-element.37.refs_0_), channel_id=1, source_target_pairs={{0,8},{4,12},{8,0},{12,4},{1,9},{5,13},{9,1},{13,5},{2,10},{6,14},... | collective-permute-start | bytes 307208 | tf_op jit(solution)/shard_map/ppermute | solution.py:240
  10.4 6.7 %collective-permute-start.1 = (bf16[16,3072]{1,0:T(8,128)(2,1)S(1)}, bf16[16,3072]{1,0:T(8,128)(2,1)S(1)}, u32[]{:S(2)}, u32[]{:S(2)}) collective-permute-start(bf16[16,3072]{1,0:T(8,128)(2,1)S(1)} %get-tuple-element.39), channel_id=1, source_target_pairs={{0,1},{1,0},{2,3},{3,2},{4,5},{5,4},{6,7},{7,6},{8,9},{9,8},{10,11... | collective-permute-start | bytes 294920 | tf_op jit(solution)/shard_map/ppermute | solution.py:240
  10.5 9.2 %collective-permute-start.8 = (bf16[16,3200]{1,0:T(8,128)(2,1)S(1)}, bf16[16,3200]{1,0:T(8,128)(2,1)S(1)}, u32[]{:S(2)}, u32[]{:S(2)}) collective-permute-start(bf16[16,3200]{1,0:T(8,128)(2,1)S(1)} %get-tuple-element.37.refs_0_), channel_id=1, source_target_pairs={{0,12},{4,8},{8,4},{12,0},{1,13},{5,9},{9,5},{13,1},{2,14},{6,10},... | collective-permute-start | bytes 307208 | tf_op jit(solution)/shard_map/ppermute | solution.py:240
  15.5 5.7 %collective-permute-start.2 = (bf16[16,3072]{1,0:T(8,128)(2,1)S(1)}, bf16[16,3072]{1,0:T(8,128)(2,1)S(1)}, u32[]{:S(2)}, u32[]{:S(2)}) collective-permute-start(bf16[16,3072]{1,0:T(8,128)(2,1)S(1)} %get-tuple-element.40), channel_id=1, source_target_pairs={{0,2},{1,3},{2,0},{3,1},{4,6},{5,7},{6,4},{7,5},{8,10},{9,11},{10,... | collective-permute-start | bytes 294920 | tf_op jit(solution)/shard_map/ppermute | solution.py:240
  17.0 9.7 %slice-start = ((s8[12582912]{0:T(1024)(128)(4,1)}), s8[4194304]{0:T(1024)(128)(4,1)S(1)}, s32[]{:S(2)}) async-start(s8[12582912]{0:T(1024)(128)(4,1)} %bitcast.8), calls=%async_computation | async-start | bytes 8388608
  17.0 9.7 %slice-start.3 = ((s8[12582912]{0:T(1024)(128)(4,1)}), s8[4194304]{0:T(1024)(128)(4,1)S(1)}, s32[]{:S(2)}) async-start(s8[12582912]{0:T(1024)(128)(4,1)} %bitcast.11), calls=%async_computation.3 | async-start | bytes 8388608
  17.0 9.7 %slice-start.6 = ((s8[12582912]{0:T(1024)(128)(4,1)}), s8[4194304]{0:T(1024)(128)(4,1)S(1)}, s32[]{:S(2)}) async-start(s8[12582912]{0:T(1024)(128)(4,1)} %bitcast.14), calls=%async_computation.6 | async-start | bytes 8388608
  17.0 9.7 %slice-start.1 = ((s8[12582912]{0:T(1024)(128)(4,1)}), s8[4194304]{0:T(1024)(128)(4,1)S(1)}, s32[]{:S(2)}) async-start(s8[12582912]{0:T(1024)(128)(4,1)} %bitcast.8), calls=%async_computation.1 | async-start | bytes 8388608
  17.0 9.7 %slice-start.2 = ((s8[12582912]{0:T(1024)(128)(4,1)}), s8[4194304]{0:T(1024)(128)(4,1)S(1)}, s32[]{:S(2)}) async-start(s8[12582912]{0:T(1024)(128)(4,1)} %bitcast.8), calls=%async_computation.2 | async-start | bytes 8388608
  17.0 9.7 %slice-start.4 = ((s8[12582912]{0:T(1024)(128)(4,1)}), s8[4194304]{0:T(1024)(128)(4,1)S(1)}, s32[]{:S(2)}) async-start(s8[12582912]{0:T(1024)(128)(4,1)} %bitcast.11), calls=%async_computation.4 | async-start | bytes 8388608
  17.0 9.7 %slice-start.5 = ((s8[12582912]{0:T(1024)(128)(4,1)}), s8[4194304]{0:T(1024)(128)(4,1)S(1)}, s32[]{:S(2)}) async-start(s8[12582912]{0:T(1024)(128)(4,1)} %bitcast.11), calls=%async_computation.5 | async-start | bytes 8388608
  17.0 10.6 %slice-start.7 = ((s8[12582912]{0:T(1024)(128)(4,1)}), s8[4194304]{0:T(1024)(128)(4,1)S(1)}, s32[]{:S(2)}) async-start(s8[12582912]{0:T(1024)(128)(4,1)} %bitcast.14), calls=%async_computation.7 | async-start | bytes 8388608
  17.0 11.8 %slice-start.8 = ((s8[12582912]{0:T(1024)(128)(4,1)}), s8[4194304]{0:T(1024)(128)(4,1)S(1)}, s32[]{:S(2)}) async-start(s8[12582912]{0:T(1024)(128)(4,1)} %bitcast.14), calls=%async_computation.8 | async-start | bytes 8388608
  17.0 5.6 %collective-permute-start.3 = (bf16[16,3072]{1,0:T(8,128)(2,1)S(1)}, bf16[16,3072]{1,0:T(8,128)(2,1)S(1)}, u32[]{:S(2)}, u32[]{:S(2)}) collective-permute-start(bf16[16,3072]{1,0:T(8,128)(2,1)S(1)} %get-tuple-element.41), channel_id=1, source_target_pairs={{0,3},{1,2},{2,1},{3,0},{4,7},{5,6},{6,5},{7,4},{8,11},{9,10},{10,... | collective-permute-start | bytes 294920 | tf_op jit(solution)/shard_map/ppermute | solution.py:240
  17.6 2.4 %collective-permute-start.5 = (bf16[8,3072]{1,0:T(8,128)(2,1)S(1)}, bf16[8,3072]{1,0:T(8,128)(2,1)S(1)}, u32[]{:S(2)}, u32[]{:S(2)}) collective-permute-start(bf16[8,3072]{1,0:T(8,128)(2,1)S(1)} %get-tuple-element.43), channel_id=1, source_target_pairs={{0,1},{1,0},{2,3},{3,2},{4,5},{5,4},{6,7},{7,6},{8,9},{9,8},{10,11... | collective-permute-start | bytes 147464 | tf_op jit(solution)/shard_map/ppermute | solution.py:240
  18.3 6.2 %collective-permute-start.6 = (bf16[8,3072]{1,0:T(8,128)(2,1)S(1)}, bf16[8,3072]{1,0:T(8,128)(2,1)S(1)}, u32[]{:S(2)}, u32[]{:S(2)}) collective-permute-start(bf16[8,3072]{1,0:T(8,128)(2,1)S(1)} %get-tuple-element.44), channel_id=1, source_target_pairs={{0,2},{1,3},{2,0},{3,1},{4,6},{5,7},{6,4},{7,5},{8,10},{9,11},{10,... | collective-permute-start | bytes 147464 | tf_op jit(solution)/shard_map/ppermute | solution.py:240
  19.7 4.7 %collective-permute-start.7 = (bf16[8,3072]{1,0:T(8,128)(2,1)S(1)}, bf16[8,3072]{1,0:T(8,128)(2,1)S(1)}, u32[]{:S(2)}, u32[]{:S(2)}) collective-permute-start(bf16[8,3072]{1,0:T(8,128)(2,1)S(1)} %get-tuple-element.45), channel_id=1, source_target_pairs={{0,3},{1,2},{2,1},{3,0},{4,7},{5,6},{6,5},{7,4},{8,11},{9,10},{10,... | collective-permute-start | bytes 147464 | tf_op jit(solution)/shard_map/ppermute | solution.py:240
  20.4 4.1 %collective-permute-start.9 = (bf16[8,3072]{1,0:T(8,128)(2,1)S(1)}, bf16[8,3072]{1,0:T(8,128)(2,1)S(1)}, u32[]{:S(2)}, u32[]{:S(2)}) collective-permute-start(bf16[8,3072]{1,0:T(8,128)(2,1)S(1)} %get-tuple-element.47), channel_id=1, source_target_pairs={{0,1},{1,0},{2,3},{3,2},{4,5},{5,4},{6,7},{7,6},{8,9},{9,8},{10,11... | collective-permute-start | bytes 147464 | tf_op jit(solution)/shard_map/ppermute | solution.py:240
  21.2 4.5 %collective-permute-start.10 = (bf16[8,3072]{1,0:T(8,128)(2,1)S(1)}, bf16[8,3072]{1,0:T(8,128)(2,1)S(1)}, u32[]{:S(2)}, u32[]{:S(2)}) collective-permute-start(bf16[8,3072]{1,0:T(8,128)(2,1)S(1)} %get-tuple-element.48), channel_id=1, source_target_pairs={{0,2},{1,3},{2,0},{3,1},{4,6},{5,7},{6,4},{7,5},{8,10},{9,11},{10,... | collective-permute-start | bytes 147464 | tf_op jit(solution)/shard_map/ppermute | solution.py:240
  22.6 4.1 %collective-permute-start.11 = (bf16[8,3072]{1,0:T(8,128)(2,1)S(1)}, bf16[8,3072]{1,0:T(8,128)(2,1)S(1)}, u32[]{:S(2)}, u32[]{:S(2)}) collective-permute-start(bf16[8,3072]{1,0:T(8,128)(2,1)S(1)} %get-tuple-element.49), channel_id=1, source_target_pairs={{0,3},{1,2},{2,1},{3,0},{4,7},{5,6},{6,5},{7,4},{8,11},{9,10},{10,... | collective-permute-start | bytes 147464 | tf_op jit(solution)/shard_map/ppermute | solution.py:240
  28.8 14.1 %copy-start = (bf16[3072,4]{0,1:T(4,128)(2,1)S(1)}, bf16[3072,4]{0,1:T(4,128)(2,1)}, u32[]{:S(2)}) copy-start(bf16[3072,4]{0,1:T(4,128)(2,1)} %param.18) | copy-start | bytes 73732
  38.0 2.8 %collective-permute-start.18 = (bf16[8,3072]{1,0:T(8,128)(2,1)S(1)}, bf16[8,3072]{1,0:T(8,128)(2,1)S(1)}, u32[]{:S(2)}, u32[]{:S(2)}) collective-permute-start(bf16[8,3072]{1,0:T(8,128)(2,1)S(1)} %get-tuple-element.63), channel_id=1, source_target_pairs={{0,1},{1,0},{2,3},{3,2},{4,5},{5,4},{6,7},{7,6},{8,9},{9,8},{10,11... | collective-permute-start | bytes 147464 | tf_op jit(solution)/shard_map/ppermute | solution.py:240
  38.1 4.6 %collective-permute-start.19 = (bf16[8,3072]{1,0:T(8,128)(2,1)S(1)}, bf16[8,3072]{1,0:T(8,128)(2,1)S(1)}, u32[]{:S(2)}, u32[]{:S(2)}) collective-permute-start(bf16[8,3072]{1,0:T(8,128)(2,1)S(1)} %get-tuple-element.64), channel_id=1, source_target_pairs={{0,2},{1,3},{2,0},{3,1},{4,6},{5,7},{6,4},{7,5},{8,10},{9,11},{10,... | collective-permute-start | bytes 147464 | tf_op jit(solution)/shard_map/ppermute | solution.py:240
  38.7 4.1 %collective-permute-start.20 = (bf16[8,3072]{1,0:T(8,128)(2,1)S(1)}, bf16[8,3072]{1,0:T(8,128)(2,1)S(1)}, u32[]{:S(2)}, u32[]{:S(2)}) collective-permute-start(bf16[8,3072]{1,0:T(8,128)(2,1)S(1)} %get-tuple-element.65), channel_id=1, source_target_pairs={{0,3},{1,2},{2,1},{3,0},{4,7},{5,6},{6,5},{7,4},{8,11},{9,10},{10,... | collective-permute-start | bytes 147464 | tf_op jit(solution)/shard_map/ppermute | solution.py:240
  40.0 4.6 %collective-permute-start.12 = (bf16[8,3072]{1,0:T(8,128)(2,1)S(1)}, bf16[8,3072]{1,0:T(8,128)(2,1)S(1)}, u32[]{:S(2)}, u32[]{:S(2)}) collective-permute-start(bf16[8,3072]{1,0:T(8,128)(2,1)S(1)} %get-tuple-element.52), channel_id=1, source_target_pairs={{0,1},{1,0},{2,3},{3,2},{4,5},{5,4},{6,7},{7,6},{8,9},{9,8},{10,11... | collective-permute-start | bytes 147464 | tf_op jit(solution)/shard_map/ppermute | solution.py:240
  40.3 4.6 %collective-permute-start.13 = (bf16[8,3072]{1,0:T(8,128)(2,1)S(1)}, bf16[8,3072]{1,0:T(8,128)(2,1)S(1)}, u32[]{:S(2)}, u32[]{:S(2)}) collective-permute-start(bf16[8,3072]{1,0:T(8,128)(2,1)S(1)} %get-tuple-element.53), channel_id=1, source_target_pairs={{0,2},{1,3},{2,0},{3,1},{4,6},{5,7},{6,4},{7,5},{8,10},{9,11},{10,... | collective-permute-start | bytes 147464 | tf_op jit(solution)/shard_map/ppermute | solution.py:240
  40.9 4.0 %collective-permute-start.14 = (bf16[8,3072]{1,0:T(8,128)(2,1)S(1)}, bf16[8,3072]{1,0:T(8,128)(2,1)S(1)}, u32[]{:S(2)}, u32[]{:S(2)}) collective-permute-start(bf16[8,3072]{1,0:T(8,128)(2,1)S(1)} %get-tuple-element.54), channel_id=1, source_target_pairs={{0,3},{1,2},{2,1},{3,0},{4,7},{5,6},{6,5},{7,4},{8,11},{9,10},{10,... | collective-permute-start | bytes 147464 | tf_op jit(solution)/shard_map/ppermute | solution.py:240
  43.4 7.0 %collective-permute-start.21 = (bf16[16,3072]{1,0:T(8,128)(2,1)S(1)}, bf16[16,3072]{1,0:T(8,128)(2,1)S(1)}, u32[]{:S(2)}, u32[]{:S(2)}) collective-permute-start(bf16[16,3072]{1,0:T(8,128)(2,1)S(1)} %shard_map.115), channel_id=1, source_target_pairs={{0,12},{4,8},{8,4},{12,0},{1,13},{5,9},{9,5},{13,1},{2,14},{6,10},... | collective-permute-start | bytes 294920 | tf_op jit(solution)/shard_map/ppermute | solution.py:240
  45.4 5.0 %collective-permute-start.15 = (bf16[16,3072]{1,0:T(8,128)(2,1)S(1)}, bf16[16,3072]{1,0:T(8,128)(2,1)S(1)}, u32[]{:S(2)}, u32[]{:S(2)}) collective-permute-start(bf16[16,3072]{1,0:T(8,128)(2,1)S(1)} %get-tuple-element.58), channel_id=1, source_target_pairs={{0,1},{1,0},{2,3},{3,2},{4,5},{5,4},{6,7},{7,6},{8,9},{9,8},{10,11... | collective-permute-start | bytes 294920 | tf_op jit(solution)/shard_map/ppermute | solution.py:240
  45.8 5.6 %collective-permute-start.16 = (bf16[16,3072]{1,0:T(8,128)(2,1)S(1)}, bf16[16,3072]{1,0:T(8,128)(2,1)S(1)}, u32[]{:S(2)}, u32[]{:S(2)}) collective-permute-start(bf16[16,3072]{1,0:T(8,128)(2,1)S(1)} %get-tuple-element.59), channel_id=1, source_target_pairs={{0,2},{1,3},{2,0},{3,1},{4,6},{5,7},{6,4},{7,5},{8,10},{9,11},{10,... | collective-permute-start | bytes 294920 | tf_op jit(solution)/shard_map/ppermute | solution.py:240
  47.0 5.0 %collective-permute-start.17 = (bf16[16,3072]{1,0:T(8,128)(2,1)S(1)}, bf16[16,3072]{1,0:T(8,128)(2,1)S(1)}, u32[]{:S(2)}, u32[]{:S(2)}) collective-permute-start(bf16[16,3072]{1,0:T(8,128)(2,1)S(1)} %get-tuple-element.60), channel_id=1, source_target_pairs={{0,3},{1,2},{2,1},{3,0},{4,7},{5,6},{6,5},{7,4},{8,11},{9,10},{10,... | collective-permute-start | bytes 294920 | tf_op jit(solution)/shard_map/ppermute | solution.py:240
  47.4 7.9 %collective-permute-start.23 = (bf16[16,3072]{1,0:T(8,128)(2,1)S(1)}, bf16[16,3072]{1,0:T(8,128)(2,1)S(1)}, u32[]{:S(2)}, u32[]{:S(2)}) collective-permute-start(bf16[16,3072]{1,0:T(8,128)(2,1)S(1)} %get-tuple-element.68), channel_id=1, source_target_pairs={{0,8},{4,12},{8,0},{12,4},{1,9},{5,13},{9,1},{13,5},{2,10},{6,14},... | collective-permute-start | bytes 294920 | tf_op jit(solution)/shard_map/ppermute | solution.py:240
  52.7 5.6 %collective-permute-start.22 = (bf16[16,3072]{1,0:T(8,128)(2,1)S(1)}, bf16[16,3072]{1,0:T(8,128)(2,1)S(1)}, u32[]{:S(2)}, u32[]{:S(2)}) collective-permute-start(bf16[16,3072]{1,0:T(8,128)(2,1)S(1)} %get-tuple-element.67), channel_id=1, source_target_pairs={{0,4},{4,0},{8,12},{12,8},{1,5},{5,1},{9,13},{13,9},{2,6},{6,2},{1... | collective-permute-start | bytes 294920 | tf_op jit(solution)/shard_map/ppermute | solution.py:240

commit v6 on v5

--- a/solution.py
+++ b/solution.py
@@ -13,7 +13,6 @@
 CAP = 8
 LANES = 128
 PAIR = 2
-EARLY = 1
 MIB = 1 << 20
 F32 = jnp.float32
 BF16 = jnp.bfloat16
@@ -203,28 +202,43 @@
             begin += count
 
 
-def mix_kernel(me_ref, router_ref, *refs, chunks, experts, later):
+def mix_kernel(me_ref, router_ref, *refs, chunks, experts):
     payload = jnp.concatenate([ref[...] for ref in refs[:chunks]], axis=0)
     returned = jnp.concatenate(
         [ref[...].astype(F32) for ref in refs[chunks : chunks + experts]], axis=0
     ).astype(BF16)
-    outs = refs[len(refs) - chunks - later : len(refs) - later]
+    added, outs = refs[chunks + experts : len(refs) - chunks], refs[len(refs) - chunks :]
     batch, width = outs[0].shape
     rows, named = payload[:, :width], payload[:, width:]
     mixed = combine(me_ref[0], rows, named, router_ref[...], returned, chunks, experts)
     for j, ref in enumerate(outs):
         part = mixed[j * batch : (j + 1) * batch]
-        if ref.dtype == F32:
-            for other in refs[chunks + experts : len(refs) - chunks - later]:
-                part = part + other[...].astype(F32)
-            ref[...] = part
-        else:
-            ref[...] = part.astype(BF16)
-
-
-def finish_kernel(stream_ref, *refs):
-    total = stream_ref[...]
-    for ref in refs[:-1]:
+        for other in added if j == 0 else []:
+            part = part + other[...]
+        ref[...] = part.astype(ref.dtype)
+
+
+def mix(me, router, payloads, returned, added):
+    chunks, experts = len(payloads), len(returned)
+    width = returned[0].shape[1]
+    batch = payloads[0].shape[0]
+    returned = [swap(block, "expert", e) for e, block in enumerate(returned)]
+    operands = [me, router, *payloads, *returned, *added]
+    return pl.pallas_call(
+        functools.partial(mix_kernel, chunks=chunks, experts=experts),
+        in_specs=[SCALAR] + [WHOLE] * (len(operands) - 1),
+        out_specs=[WHOLE] * chunks,
+        out_shape=[
+            jax.ShapeDtypeStruct((batch, width), BF16 if j % 2 else F32) for j in range(chunks)
+        ],
+        cost_estimate=LIGHT,
+        compiler_params=params(experts * chunks * CAP * width),
+    )(*operands)
+
+
+def add_kernel(*refs):
+    total = refs[0][...]
+    for ref in refs[1:-1]:
         total = total + ref[...].astype(F32)
     refs[-1][...] = total.astype(BF16)
 
@@ -283,8 +297,11 @@
         cost_estimate=pl.CostEstimate(flops=10**9, bytes_accessed=4 * 10**6, transcendentals=0),
     )(*operands)
 
-    chunks = [swap(payload, "attn", j) for j in range(layers)]
-    groups = [[0, 1], [2], list(range(3, layers))]
+    chunks = []
+    for j in range(layers):
+        passed = j > 1 and j % 2
+        chunks.append(swap(chunks[j - 1], "attn", 1) if passed else swap(payload, "attn", j))
+    groups = [[0, 1], list(range(2, layers))]
     inputs, ahead = [], []
     for group in groups:
         count = len(group)
@@ -293,7 +310,7 @@
             in_specs=[SCALAR] + [ANY] * len(ahead) + [WHOLE] * count,
             out_specs=[WHOLE] * experts,
             out_shape=[shape((count * CAP, width), BF16)] * experts,
-            cost_estimate=BUSY if group == [2] else LIGHT,
+            cost_estimate=BUSY,
             compiler_params=params(experts * count * CAP * width),
         )(me, *ahead, *[chunks[j] for j in group])
         arrived = [swap(slots[e], "expert", e) for e in range(experts)]
@@ -311,35 +328,31 @@
         compiler_params=params(total_rows * width),
     )(*inputs, gate_proj[0], up_proj[0], down_proj[0])
 
-    results = [results[i : i + experts] for i in range(0, len(results), experts)]
+    near, far = results[:experts], results[experts:]
+    far = mix(me, router, [chunks[j] for j in groups[1]], far, [])
+    kept, sent = far[::2], far[1::2]
+    passed = [swap(block, "attn", 1) for block in sent]
     received = []
-    for i, group in list(enumerate(groups))[::-1]:
-        count, own = len(group), int(group[0] == 0)
-        returned = [swap(results[i][e], "expert", e) for e in range(experts)]
-        later = results[0][1:] if i == 1 else []
-        added = [stream, *received[EARLY:]] if own else []
-        operands = [me, router, *[chunks[j] for j in group], *returned, *added]
-        mixed = pl.pallas_call(
-            functools.partial(mix_kernel, chunks=count, experts=experts, later=len(later)),
-            in_specs=[SCALAR] + [WHOLE] * (len(operands) - 1) + [ANY] * len(later),
-            out_specs=[WHOLE] * count + [ANY] * len(later),
-            out_shape=[shape((batch, width), F32 if j == 0 else BF16) for j in group]
-            + [shape(block.shape, BF16) for block in later],
+    for j, own, other in zip(groups[1][::2], kept, passed):
+        total = pl.pallas_call(
+            add_kernel,
+            in_specs=[WHOLE, WHOLE],
+            out_specs=WHOLE,
+            out_shape=shape((batch, width), BF16),
             cost_estimate=LIGHT,
-            input_output_aliases={len(operands) + k: count + k for k in range(len(later))},
-            compiler_params=params(experts * count * CAP * width),
-        )(*operands, *later)
-        if later:
-            results[0] = [results[0][0], *mixed[count:]]
-        received = received[:EARLY] if own else received
-        received = [swap(block, "attn", j) for j, block in zip(group, mixed)] + received
+            compiler_params=params(2 * batch * width),
+        )(own, other)
+        received.append(swap(total, "attn", j))
+    base, first = mix(me, router, chunks[:2], near, [stream])
+    received = [swap(first, "attn", 1), *received]
     return pl.pallas_call(
-        finish_kernel,
-        in_specs=[WHOLE] * len(received),
+        add_kernel,
+        in_specs=[WHOLE] * (1 + len(received)),
         out_specs=WHOLE,
         out_shape=shape((batch, width), BF16),
+        cost_estimate=LIGHT,
         compiler_params=params(2 * layers * batch * width),
-    )(*received)
+    )(base, *received)
 
 
 def solution(mesh):

time: 59.1 us -> 57.6 us (0.975)
  starting transfers between devices: 26.4 us -> 20.6 us
  waiting for transfers between devices: 13.5 us -> 18.6 us
  Pallas kernels: 16.8 us -> 16.1 us
    ppermute x24 -> x18, starting transfers between devices: 26.4 us -> 20.6 us  [swap(): return lax.ppermute(value, axis, [(i, i ^ step) for i in range(count)])]
    ppermute x24 -> x18, waiting for transfers between devices: 13.5 us -> 18.6 us  [swap(): return lax.ppermute(value, axis, [(i, i ^ step) for i in range(count)])]
    pallas_call x3 -> x2, Pallas kernels: 1.31 us -> 0.96 us  [shards(): pl.pallas_call(functools.partial(split_kernel, chunks=count, after=len(ah...]
  transfers between devices with their start and end apart: 24 -> 18, of which waited for: 11 -> 11; matrix products, arithmetic and copies ran while one was open for 0% -> 0% of each run, Pallas kernels for 5% -> 4%
where the time goes in v6:
time: 57.6 us; the launch traced here: 57.5 us
  starting transfers between devices  20.6 us (36%)
  waiting for transfers between devices  18.6 us (32%)
  Pallas kernels  16.1 us (28%)
  local copies, waits for them, and re-layouts  2.08 us (4%)
    ppermute x18, starting transfers between devices, swap(): return lax.ppermute(value, axis, [(i, i ^ step) for i in range(count)])  20.6 us
    ppermute x18, waiting for transfers between devices, swap(): return lax.ppermute(value, axis, [(i, i ^ step) for i in range(count)])  18.6 us
    pallas_call x1, Pallas kernels, shards(): pl.pallas_call(functools.partial(expert_kernel, pieces=len(inputs)), in_s...  9.23 us
    pallas_call x1, Pallas kernels, shards(): pl.pallas_call(attend_kernel, in_specs=[ANY] * len(operands), out_specs=[...  3.99 us
    unnamed x20, local copies, waits for them, and re-layouts  2.08 us
    pallas_call x2, Pallas kernels, mix(): pl.pallas_call(functools.partial(mix_kernel, chunks=chunks, experts=exper...  1.22 us
  transfers between devices with their start and end apart: 18, of which 11 were waited for; matrix products, arithmetic and copies ran while one was open for 0% of the time, Pallas kernels for 4%

profile of v6, /device:TPU:0, one launch (start us, length us, event | category | flops | bytes accessed | tf_op | source)
XLA Modules:
  0.0 57.5 jit_solution(6201570379018597951)
XLA Ops:
  0.0 4.0 %shard_map.109 = (f32[16,3072]{1,0:T(8,128)S(1)}, bf16[16,3200]{1,0:T(8,128)(2,1)S(1)}) custom-call(s32[1,16]{1,0:T(1,128)} %bitcast.21, bf16[16,3072]{1,0:T(8,128)(2,1)} %queries_hbm.1, bf16[16,96,512]{2,1,0:T(8,128)(2,1)} %keys_hbm.1, bf16[16,96,512]{2,1,0:T(8,128)(2,1)} %values_hbm.1, s32[2,16]{1,0:T(2,128)} %bitcast.20, bf16[16,3072]{1,0:T(8,128)(2,1)} %residual_hbm.1, ...), custom_call_target="tpu_custom_call" | custom-call | flops 1000000000 | bytes 4000000 | tf_op jit(solution)/shard_map/pallas_call | solution.py:289
  4.0 4.1 %collective-permute-start.4 = (bf16[16,3200]{1,0:T(8,128)(2,1)S(1)}, bf16[16,3200]{1,0:T(8,128)(2,1)S(1)}, u32[]{:S(2)}, u32[]{:S(2)}) collective-permute-start(bf16[16,3200]{1,0:T(8,128)(2,1)S(1)} %get-tuple-element.27.refs_0_), channel_id=1, source_target_pairs={{0,8},{4,12},{8,0},{12,4},{1,9},{5,13},{9,1},{13,5},{2,10},{6,14},... | collective-permute-start | bytes 307208 | tf_op jit(solution)/shard_map/ppermute | solution.py:254
  8.1 1.6 %collective-permute-start = (bf16[16,3200]{1,0:T(8,128)(2,1)S(1)}, bf16[16,3200]{1,0:T(8,128)(2,1)S(1)}, u32[]{:S(2)}, u32[]{:S(2)}) collective-permute-start(bf16[16,3200]{1,0:T(8,128)(2,1)S(1)} %get-tuple-element.27.refs_0_), channel_id=1, source_target_pairs={{0,4},{4,0},{8,12},{12,8},{1,5},{5,1},{9,13},{13,9},{2,6},{6,2},{1... | collective-permute-start | bytes 307208 | tf_op jit(solution)/shard_map/ppermute | solution.py:254
  9.7 3.5 %collective-permute-done.4.refs_1_.refs_0_ = bf16[16,3200]{1,0:T(8,128)(2,1)S(1)} collective-permute-done((bf16[16,3200]{1,0:T(8,128)(2,1)S(1)}, bf16[16,3200]{1,0:T(8,128)(2,1)S(1)}, u32[]{:S(2)}, u32[]{:S(2)}) %collective-permute-start.4) | collective-permute-done | bytes 102432 | tf_op jit(solution)/shard_map/ppermute | solution.py:254
  13.2 0.7 %collective-permute-start.5 = (bf16[16,3200]{1,0:T(8,128)(2,1)S(1)}, bf16[16,3200]{1,0:T(8,128)(2,1)S(1)}, u32[]{:S(2)}, u32[]{:S(2)}) collective-permute-start(bf16[16,3200]{1,0:T(8,128)(2,1)S(1)} %collective-permute-done.4.refs_1_.refs_0_), channel_id=1, source_target_pairs={{0,4},{4,0},{8,12},{12,8},{1,5},{5,1},{9,13},{13,9},{2,6},{6,2},{1... | collective-permute-start | bytes 307208 | tf_op jit(solution)/shard_map/ppermute | solution.py:254
  13.9 0.0 collective-permute-done.refs_1_
  13.9 0.5 shard_map.110
  14.4 0.1 collective-permute-start.1
  14.5 1.6 %collective-permute-start.2 = (bf16[16,3072]{1,0:T(8,128)(2,1)S(1)}, bf16[16,3072]{1,0:T(8,128)(2,1)S(1)}, u32[]{:S(2)}, u32[]{:S(2)}) collective-permute-start(bf16[16,3072]{1,0:T(8,128)(2,1)S(1)} %get-tuple-element.30), channel_id=1, source_target_pairs={{0,2},{1,3},{2,0},{3,1},{4,6},{5,7},{6,4},{7,5},{8,10},{9,11},{10,... | collective-permute-start | bytes 294920 | tf_op jit(solution)/shard_map/ppermute | solution.py:254
  16.0 0.0 slice-start
  16.0 0.0 slice-start.3
  16.0 0.0 slice-start.6
  16.0 0.0 slice-start.1
  16.0 0.0 slice-start.2
  16.0 0.0 slice-start.4
  16.0 0.0 slice-start.5
  16.1 0.0 slice-start.7
  16.1 0.0 slice-start.8
  16.1 0.4 collective-permute-start.3
  16.5 0.0 collective-permute-done.1.refs_0_.refs_1_
  16.5 1.4 %collective-permute-done.5.refs_2_.refs_1_ = bf16[16,3200]{1,0:T(8,128)(2,1)S(1)} collective-permute-done((bf16[16,3200]{1,0:T(8,128)(2,1)S(1)}, bf16[16,3200]{1,0:T(8,128)(2,1)S(1)}, u32[]{:S(2)}, u32[]{:S(2)}) %collective-permute-start.5) | collective-permute-done | bytes 102432 | tf_op jit(solution)/shard_map/ppermute | solution.py:254
  17.8 0.5 shard_map.111
  18.3 0.1 collective-permute-start.6
  18.4 1.7 %collective-permute-start.7 = (bf16[16,3072]{1,0:T(8,128)(2,1)S(1)}, bf16[16,3072]{1,0:T(8,128)(2,1)S(1)}, u32[]{:S(2)}, u32[]{:S(2)}) collective-permute-start(bf16[16,3072]{1,0:T(8,128)(2,1)S(1)} %get-tuple-element.34), channel_id=1, source_target_pairs={{0,2},{1,3},{2,0},{3,1},{4,6},{5,7},{6,4},{7,5},{8,10},{9,11},{10,... | collective-permute-start | bytes 294920 | tf_op jit(solution)/shard_map/ppermute | solution.py:254
  20.1 0.1 collective-permute-start.8
  20.2 0.0 collective-permute-done.2.refs_2_
  20.2 1.1 %collective-permute-done.3.refs_3_ = bf16[16,3072]{1,0:T(8,128)(2,1)S(1)} collective-permute-done((bf16[16,3072]{1,0:T(8,128)(2,1)S(1)}, bf16[16,3072]{1,0:T(8,128)(2,1)S(1)}, u32[]{:S(2)}, u32[]{:S(2)}) %collective-permute-start.3) | collective-permute-done | bytes 98336 | tf_op jit(solution)/shard_map/ppermute | solution.py:254
  21.3 0.0 collective-permute-done.6.refs_5_
  21.3 2.8 %collective-permute-done.7.refs_6_ = bf16[16,3072]{1,0:T(8,128)(2,1)S(1)} collective-permute-done((bf16[16,3072]{1,0:T(8,128)(2,1)S(1)}, bf16[16,3072]{1,0:T(8,128)(2,1)S(1)}, u32[]{:S(2)}, u32[]{:S(2)}) %collective-permute-start.7) | collective-permute-done | bytes 98336 | tf_op jit(solution)/shard_map/ppermute | solution.py:254
  24.1 1.6 %collective-permute-done.8.refs_7_ = bf16[16,3072]{1,0:T(8,128)(2,1)S(1)} collective-permute-done((bf16[16,3072]{1,0:T(8,128)(2,1)S(1)}, bf16[16,3072]{1,0:T(8,128)(2,1)S(1)}, u32[]{:S(2)}, u32[]{:S(2)}) %collective-permute-start.8) | collective-permute-done | bytes 98336 | tf_op jit(solution)/shard_map/ppermute | solution.py:254
  25.8 0.0 slice-done
  25.8 0.0 slice-done.3
  25.8 0.0 slice-done.6
  25.8 0.0 slice-done.1
  25.8 0.0 slice-done.2
  25.8 0.0 slice-done.4
  25.8 0.0 slice-done.5
  25.8 0.8 %slice-done.7 = s8[4194304]{0:T(1024)(128)(4,1)S(1)} async-done(((s8[12582912]{0:T(1024)(128)(4,1)}), s8[4194304]{0:T(1024)(128)(4,1)S(1)}, s32[]{:S(2)}) %slice-start.7) | async-done | bytes 4194328
  26.7 1.2 %slice-done.8 = s8[4194304]{0:T(1024)(128)(4,1)S(1)} async-done(((s8[12582912]{0:T(1024)(128)(4,1)}), s8[4194304]{0:T(1024)(128)(4,1)S(1)}, s32[]{:S(2)}) %slice-start.8) | async-done | bytes 4194328
  27.9 0.0 copy-start
  27.9 9.2 %shard_map.112 = (bf16[16,3072]{1,0:T(8,128)(2,1)S(1)}, bf16[16,3072]{1,0:T(8,128)(2,1)S(1)}, bf16[16,3072]{1,0:T(8,128)(2,1)S(1)}, bf16[16,3072]{1,0:T(8,128)(2...) custom-call(bf16[16,3072]{1,0:T(8,128)(2,1)S(1)} %get-tuple-element., ...), custom_call_target="tpu_custom_call" | custom-call | tf_op jit(solution)/shard_map/pallas_call | solution.py:322
  37.1 0.2 collective-permute-start.13
  37.3 0.5 collective-permute-start.14
  37.9 1.2 %collective-permute-start.15 = (bf16[16,3072]{1,0:T(8,128)(2,1)S(1)}, bf16[16,3072]{1,0:T(8,128)(2,1)S(1)}, u32[]{:S(2)}, u32[]{:S(2)}) collective-permute-start(bf16[16,3072]{1,0:T(8,128)(2,1)S(1)} %get-tuple-element.46), channel_id=1, source_target_pairs={{0,3},{1,2},{2,1},{3,0},{4,7},{5,6},{6,5},{7,4},{8,11},{9,10},{10,... | collective-permute-start | bytes 294920 | tf_op jit(solution)/shard_map/ppermute | solution.py:254
  39.0 0.4 collective-permute-start.9
  39.5 0.5 collective-permute-start.10
  40.0 0.0 collective-permute-done.13.refs_3_
  40.0 0.9 %collective-permute-start.11 = (bf16[16,3072]{1,0:T(8,128)(2,1)S(1)}, bf16[16,3072]{1,0:T(8,128)(2,1)S(1)}, u32[]{:S(2)}, u32[]{:S(2)}) collective-permute-start(bf16[16,3072]{1,0:T(8,128)(2,1)S(1)} %get-tuple-element.39), channel_id=1, source_target_pairs={{0,3},{1,2},{2,1},{3,0},{4,7},{5,6},{6,5},{7,4},{8,11},{9,10},{10,... | collective-permute-start | bytes 294920 | tf_op jit(solution)/shard_map/ppermute | solution.py:254
  40.9 2.0 %collective-permute-done.14.refs_4_ = bf16[16,3072]{1,0:T(8,128)(2,1)S(1)} collective-permute-done((bf16[16,3072]{1,0:T(8,128)(2,1)S(1)}, bf16[16,3072]{1,0:T(8,128)(2,1)S(1)}, u32[]{:S(2)}, u32[]{:S(2)}) %collective-permute-start.14) | collective-permute-done | bytes 98336 | tf_op jit(solution)/shard_map/ppermute | solution.py:254
  42.9 1.0 %collective-permute-done.15.refs_5_ = bf16[16,3072]{1,0:T(8,128)(2,1)S(1)} collective-permute-done((bf16[16,3072]{1,0:T(8,128)(2,1)S(1)}, bf16[16,3072]{1,0:T(8,128)(2,1)S(1)}, u32[]{:S(2)}, u32[]{:S(2)}) %collective-permute-start.15) | collective-permute-done | bytes 98336 | tf_op jit(solution)/shard_map/ppermute | solution.py:254
  43.9 0.0 copy-done
  43.9 0.6 %shard_map.114 = (f32[16,3072]{1,0:T(8,128)S(1)}, bf16[16,3072]{1,0:T(8,128)(2,1)S(1)}) custom-call(s32[1]{0:T(128)} %bitcast.me_ref, bf16[4,3072]{1,0:T(4,128)(2,1)S(1)} %bitcast.17, bf16[16,3200]{1,0:T(8,128)(2,1)S(1)} %collective-permute-done.4.refs_1_.refs_0_, bf16[16,3200]{1,0:T(8,128)(2,1)S(1)} %collective-permute-done.5.refs_2_.refs_1_, ...), custom_call_target="tpu_custom_call" | custom-call | tf_op jit(solution)/shard_map/pallas_call | solution.py:227
  44.5 1.5 %collective-permute-start.16 = (bf16[16,3072]{1,0:T(8,128)(2,1)S(1)}, bf16[16,3072]{1,0:T(8,128)(2,1)S(1)}, u32[]{:S(2)}, u32[]{:S(2)}) collective-permute-start(bf16[16,3072]{1,0:T(8,128)(2,1)S(1)} %get-tuple-element.48), channel_id=1, source_target_pairs={{0,4},{4,0},{8,12},{12,8},{1,5},{5,1},{9,13},{13,9},{2,6},{6,2},{1... | collective-permute-start | bytes 294920 | tf_op jit(solution)/shard_map/ppermute | solution.py:254
  46.0 0.0 collective-permute-done.9.refs_3_
  46.0 1.1 %collective-permute-done.10.refs_4_ = bf16[16,3072]{1,0:T(8,128)(2,1)S(1)} collective-permute-done((bf16[16,3072]{1,0:T(8,128)(2,1)S(1)}, bf16[16,3072]{1,0:T(8,128)(2,1)S(1)}, u32[]{:S(2)}, u32[]{:S(2)}) %collective-permute-start.10) | collective-permute-done | bytes 98336 | tf_op jit(solution)/shard_map/ppermute | solution.py:254
  47.1 1.0 %collective-permute-done.11.refs_5_ = bf16[16,3072]{1,0:T(8,128)(2,1)S(1)} collective-permute-done((bf16[16,3072]{1,0:T(8,128)(2,1)S(1)}, bf16[16,3072]{1,0:T(8,128)(2,1)S(1)}, u32[]{:S(2)}, u32[]{:S(2)}) %collective-permute-start.11) | collective-permute-done | bytes 98336 | tf_op jit(solution)/shard_map/ppermute | solution.py:254
  48.1 0.6 %shard_map.113 = (f32[16,3072]{1,0:T(8,128)S(1)}, bf16[16,3072]{1,0:T(8,128)(2,1)S(1)}) custom-call(s32[1]{0:T(128)} %bitcast.me_ref, bf16[4,3072]{1,0:T(4,128)(2,1)S(1)} %bitcast.18, bf16[16,3200]{1,0:T(8,128)(2,1)S(1)} %get-tuple-element.27.refs_0_, bf16[16,3200]{1,0:T(8,128)(2,1)S(1)} %collective-permute-done.refs_1_, ...), custom_call_target="tpu_custom_call" | custom-call | tf_op jit(solution)/shard_map/pallas_call | solution.py:227
  48.7 1.5 %collective-permute-start.12 = (bf16[16,3072]{1,0:T(8,128)(2,1)S(1)}, bf16[16,3072]{1,0:T(8,128)(2,1)S(1)}, u32[]{:S(2)}, u32[]{:S(2)}) collective-permute-start(bf16[16,3072]{1,0:T(8,128)(2,1)S(1)} %get-tuple-element.42), channel_id=1, source_target_pairs={{0,4},{4,0},{8,12},{12,8},{1,5},{5,1},{9,13},{13,9},{2,6},{6,2},{1... | collective-permute-start | bytes 294920 | tf_op jit(solution)/shard_map/ppermute | solution.py:254
  50.2 0.0 collective-permute-done.16.refs_1_
  50.3 3.4 %collective-permute-start.17 = (bf16[16,3072]{1,0:T(8,128)(2,1)S(1)}, bf16[16,3072]{1,0:T(8,128)(2,1)S(1)}, u32[]{:S(2)}, u32[]{:S(2)}) collective-permute-start(bf16[16,3072]{1,0:T(8,128)(2,1)S(1)} %shard_map.115), channel_id=1, source_target_pairs={{0,8},{4,12},{8,0},{12,4},{1,9},{5,13},{9,1},{13,5},{2,10},{6,14},... | collective-permute-start | bytes 294920 | tf_op jit(solution)/shard_map/ppermute | solution.py:254
  53.7 0.5 collective-permute-done.12.refs_1_
  54.2 2.6 %collective-permute-done.17.refs_2_ = bf16[16,3072]{1,0:T(8,128)(2,1)S(1)} collective-permute-done((bf16[16,3072]{1,0:T(8,128)(2,1)S(1)}, bf16[16,3072]{1,0:T(8,128)(2,1)S(1)}, u32[]{:S(2)}, u32[]{:S(2)}) %collective-permute-start.17) | collective-permute-done | bytes 98336 | tf_op jit(solution)/shard_map/ppermute | solution.py:254
  56.8 0.7 %shard_map.116 = bf16[16,3072]{1,0:T(8,128)(2,1)} custom-call(f32[16,3072]{1,0:T(8,128)S(1)} %get-tuple-element.41.refs_0_, bf16[16,3072]{1,0:T(8,128)(2,1)S(1)} %collective-permute-done.12.refs_1_, bf16[16,3072]{1,0:T(8,128)(2,1)S(1)} %collective-permute-done.17.refs_2_), custom_call_target="tpu_custom_call" | custom-call | tf_op jit(solution)/shard_map/pallas_call | solution.py:348
  (4 shorter events, 0.0 us)
Async XLA Ops:
  4.0 9.2 %collective-permute-start.4 = (bf16[16,3200]{1,0:T(8,128)(2,1)S(1)}, bf16[16,3200]{1,0:T(8,128)(2,1)S(1)}, u32[]{:S(2)}, u32[]{:S(2)}) collective-permute-start(bf16[16,3200]{1,0:T(8,128)(2,1)S(1)} %get-tuple-element.27.refs_0_), channel_id=1, source_target_pairs={{0,8},{4,12},{8,0},{12,4},{1,9},{5,13},{9,1},{13,5},{2,10},{6,14},... | collective-permute-start | bytes 307208 | tf_op jit(solution)/shard_map/ppermute | solution.py:254
  8.1 5.8 %collective-permute-start = (bf16[16,3200]{1,0:T(8,128)(2,1)S(1)}, bf16[16,3200]{1,0:T(8,128)(2,1)S(1)}, u32[]{:S(2)}, u32[]{:S(2)}) collective-permute-start(bf16[16,3200]{1,0:T(8,128)(2,1)S(1)} %get-tuple-element.27.refs_0_), channel_id=1, source_target_pairs={{0,4},{4,0},{8,12},{12,8},{1,5},{5,1},{9,13},{13,9},{2,6},{6,2},{1... | collective-permute-start | bytes 307208 | tf_op jit(solution)/shard_map/ppermute | solution.py:254
  13.2 4.7 %collective-permute-start.5 = (bf16[16,3200]{1,0:T(8,128)(2,1)S(1)}, bf16[16,3200]{1,0:T(8,128)(2,1)S(1)}, u32[]{:S(2)}, u32[]{:S(2)}) collective-permute-start(bf16[16,3200]{1,0:T(8,128)(2,1)S(1)} %collective-permute-done.4.refs_1_.refs_0_), channel_id=1, source_target_pairs={{0,4},{4,0},{8,12},{12,8},{1,5},{5,1},{9,13},{13,9},{2,6},{6,2},{1... | collective-permute-start | bytes 307208 | tf_op jit(solution)/shard_map/ppermute | solution.py:254
  14.4 2.1 %collective-permute-start.1 = (bf16[16,3072]{1,0:T(8,128)(2,1)S(1)}, bf16[16,3072]{1,0:T(8,128)(2,1)S(1)}, u32[]{:S(2)}, u32[]{:S(2)}) collective-permute-start(bf16[16,3072]{1,0:T(8,128)(2,1)S(1)} %get-tuple-element.29), channel_id=1, source_target_pairs={{0,1},{1,0},{2,3},{3,2},{4,5},{5,4},{6,7},{7,6},{8,9},{9,8},{10,11... | collective-permute-start | bytes 294920 | tf_op jit(solution)/shard_map/ppermute | solution.py:254
  14.5 5.8 %collective-permute-start.2 = (bf16[16,3072]{1,0:T(8,128)(2,1)S(1)}, bf16[16,3072]{1,0:T(8,128)(2,1)S(1)}, u32[]{:S(2)}, u32[]{:S(2)}) collective-permute-start(bf16[16,3072]{1,0:T(8,128)(2,1)S(1)} %get-tuple-element.30), channel_id=1, source_target_pairs={{0,2},{1,3},{2,0},{3,1},{4,6},{5,7},{6,4},{7,5},{8,10},{9,11},{10,... | collective-permute-start | bytes 294920 | tf_op jit(solution)/shard_map/ppermute | solution.py:254
  16.0 9.7 %slice-start = ((s8[12582912]{0:T(1024)(128)(4,1)}), s8[4194304]{0:T(1024)(128)(4,1)S(1)}, s32[]{:S(2)}) async-start(s8[12582912]{0:T(1024)(128)(4,1)} %bitcast.8), calls=%async_computation | async-start | bytes 8388608
  16.0 9.7 %slice-start.3 = ((s8[12582912]{0:T(1024)(128)(4,1)}), s8[4194304]{0:T(1024)(128)(4,1)S(1)}, s32[]{:S(2)}) async-start(s8[12582912]{0:T(1024)(128)(4,1)} %bitcast.11), calls=%async_computation.3 | async-start | bytes 8388608
  16.0 9.7 %slice-start.6 = ((s8[12582912]{0:T(1024)(128)(4,1)}), s8[4194304]{0:T(1024)(128)(4,1)S(1)}, s32[]{:S(2)}) async-start(s8[12582912]{0:T(1024)(128)(4,1)} %bitcast.14), calls=%async_computation.6 | async-start | bytes 8388608
  16.0 9.7 %slice-start.1 = ((s8[12582912]{0:T(1024)(128)(4,1)}), s8[4194304]{0:T(1024)(128)(4,1)S(1)}, s32[]{:S(2)}) async-start(s8[12582912]{0:T(1024)(128)(4,1)} %bitcast.8), calls=%async_computation.1 | async-start | bytes 8388608
  16.0 9.8 %slice-start.2 = ((s8[12582912]{0:T(1024)(128)(4,1)}), s8[4194304]{0:T(1024)(128)(4,1)S(1)}, s32[]{:S(2)}) async-start(s8[12582912]{0:T(1024)(128)(4,1)} %bitcast.8), calls=%async_computation.2 | async-start | bytes 8388608
  16.0 9.8 %slice-start.4 = ((s8[12582912]{0:T(1024)(128)(4,1)}), s8[4194304]{0:T(1024)(128)(4,1)S(1)}, s32[]{:S(2)}) async-start(s8[12582912]{0:T(1024)(128)(4,1)} %bitcast.11), calls=%async_computation.4 | async-start | bytes 8388608
  16.0 9.8 %slice-start.5 = ((s8[12582912]{0:T(1024)(128)(4,1)}), s8[4194304]{0:T(1024)(128)(4,1)S(1)}, s32[]{:S(2)}) async-start(s8[12582912]{0:T(1024)(128)(4,1)} %bitcast.11), calls=%async_computation.5 | async-start | bytes 8388608
  16.1 10.6 %slice-start.7 = ((s8[12582912]{0:T(1024)(128)(4,1)}), s8[4194304]{0:T(1024)(128)(4,1)S(1)}, s32[]{:S(2)}) async-start(s8[12582912]{0:T(1024)(128)(4,1)} %bitcast.14), calls=%async_computation.7 | async-start | bytes 8388608
  16.1 11.8 %slice-start.8 = ((s8[12582912]{0:T(1024)(128)(4,1)}), s8[4194304]{0:T(1024)(128)(4,1)S(1)}, s32[]{:S(2)}) async-start(s8[12582912]{0:T(1024)(128)(4,1)} %bitcast.14), calls=%async_computation.8 | async-start | bytes 8388608
  16.1 5.2 %collective-permute-start.3 = (bf16[16,3072]{1,0:T(8,128)(2,1)S(1)}, bf16[16,3072]{1,0:T(8,128)(2,1)S(1)}, u32[]{:S(2)}, u32[]{:S(2)}) collective-permute-start(bf16[16,3072]{1,0:T(8,128)(2,1)S(1)} %get-tuple-element.31), channel_id=1, source_target_pairs={{0,3},{1,2},{2,1},{3,0},{4,7},{5,6},{6,5},{7,4},{8,11},{9,10},{10,... | collective-permute-start | bytes 294920 | tf_op jit(solution)/shard_map/ppermute | solution.py:254
  18.3 3.0 %collective-permute-start.6 = (bf16[16,3072]{1,0:T(8,128)(2,1)S(1)}, bf16[16,3072]{1,0:T(8,128)(2,1)S(1)}, u32[]{:S(2)}, u32[]{:S(2)}) collective-permute-start(bf16[16,3072]{1,0:T(8,128)(2,1)S(1)} %get-tuple-element.33), channel_id=1, source_target_pairs={{0,1},{1,0},{2,3},{3,2},{4,5},{5,4},{6,7},{7,6},{8,9},{9,8},{10,11... | collective-permute-start | bytes 294920 | tf_op jit(solution)/shard_map/ppermute | solution.py:254
  18.4 5.7 %collective-permute-start.7 = (bf16[16,3072]{1,0:T(8,128)(2,1)S(1)}, bf16[16,3072]{1,0:T(8,128)(2,1)S(1)}, u32[]{:S(2)}, u32[]{:S(2)}) collective-permute-start(bf16[16,3072]{1,0:T(8,128)(2,1)S(1)} %get-tuple-element.34), channel_id=1, source_target_pairs={{0,2},{1,3},{2,0},{3,1},{4,6},{5,7},{6,4},{7,5},{8,10},{9,11},{10,... | collective-permute-start | bytes 294920 | tf_op jit(solution)/shard_map/ppermute | solution.py:254
  20.1 5.6 %collective-permute-start.8 = (bf16[16,3072]{1,0:T(8,128)(2,1)S(1)}, bf16[16,3072]{1,0:T(8,128)(2,1)S(1)}, u32[]{:S(2)}, u32[]{:S(2)}) collective-permute-start(bf16[16,3072]{1,0:T(8,128)(2,1)S(1)} %get-tuple-element.35), channel_id=1, source_target_pairs={{0,3},{1,2},{2,1},{3,0},{4,7},{5,6},{6,5},{7,4},{8,11},{9,10},{10,... | collective-permute-start | bytes 294920 | tf_op jit(solution)/shard_map/ppermute | solution.py:254
  27.9 16.1 %copy-start = (bf16[3072,4]{0,1:T(4,128)(2,1)S(1)}, bf16[3072,4]{0,1:T(4,128)(2,1)}, u32[]{:S(2)}) copy-start(bf16[3072,4]{0,1:T(4,128)(2,1)} %param.18) | copy-start | bytes 73732
  37.1 2.9 %collective-permute-start.13 = (bf16[16,3072]{1,0:T(8,128)(2,1)S(1)}, bf16[16,3072]{1,0:T(8,128)(2,1)S(1)}, u32[]{:S(2)}, u32[]{:S(2)}) collective-permute-start(bf16[16,3072]{1,0:T(8,128)(2,1)S(1)} %get-tuple-element.44), channel_id=1, source_target_pairs={{0,1},{1,0},{2,3},{3,2},{4,5},{5,4},{6,7},{7,6},{8,9},{9,8},{10,11... | collective-permute-start | bytes 294920 | tf_op jit(solution)/shard_map/ppermute | solution.py:254
  37.3 5.6 %collective-permute-start.14 = (bf16[16,3072]{1,0:T(8,128)(2,1)S(1)}, bf16[16,3072]{1,0:T(8,128)(2,1)S(1)}, u32[]{:S(2)}, u32[]{:S(2)}) collective-permute-start(bf16[16,3072]{1,0:T(8,128)(2,1)S(1)} %get-tuple-element.45), channel_id=1, source_target_pairs={{0,2},{1,3},{2,0},{3,1},{4,6},{5,7},{6,4},{7,5},{8,10},{9,11},{10,... | collective-permute-start | bytes 294920 | tf_op jit(solution)/shard_map/ppermute | solution.py:254
  37.9 6.0 %collective-permute-start.15 = (bf16[16,3072]{1,0:T(8,128)(2,1)S(1)}, bf16[16,3072]{1,0:T(8,128)(2,1)S(1)}, u32[]{:S(2)}, u32[]{:S(2)}) collective-permute-start(bf16[16,3072]{1,0:T(8,128)(2,1)S(1)} %get-tuple-element.46), channel_id=1, source_target_pairs={{0,3},{1,2},{2,1},{3,0},{4,7},{5,6},{6,5},{7,4},{8,11},{9,10},{10,... | collective-permute-start | bytes 294920 | tf_op jit(solution)/shard_map/ppermute | solution.py:254
  39.0 7.0 %collective-permute-start.9 = (bf16[16,3072]{1,0:T(8,128)(2,1)S(1)}, bf16[16,3072]{1,0:T(8,128)(2,1)S(1)}, u32[]{:S(2)}, u32[]{:S(2)}) collective-permute-start(bf16[16,3072]{1,0:T(8,128)(2,1)S(1)} %get-tuple-element.37), channel_id=1, source_target_pairs={{0,1},{1,0},{2,3},{3,2},{4,5},{5,4},{6,7},{7,6},{8,9},{9,8},{10,11... | collective-permute-start | bytes 294920 | tf_op jit(solution)/shard_map/ppermute | solution.py:254
  39.5 7.7 %collective-permute-start.10 = (bf16[16,3072]{1,0:T(8,128)(2,1)S(1)}, bf16[16,3072]{1,0:T(8,128)(2,1)S(1)}, u32[]{:S(2)}, u32[]{:S(2)}) collective-permute-start(bf16[16,3072]{1,0:T(8,128)(2,1)S(1)} %get-tuple-element.38), channel_id=1, source_target_pairs={{0,2},{1,3},{2,0},{3,1},{4,6},{5,7},{6,4},{7,5},{8,10},{9,11},{10,... | collective-permute-start | bytes 294920 | tf_op jit(solution)/shard_map/ppermute | solution.py:254
  40.0 8.1 %collective-permute-start.11 = (bf16[16,3072]{1,0:T(8,128)(2,1)S(1)}, bf16[16,3072]{1,0:T(8,128)(2,1)S(1)}, u32[]{:S(2)}, u32[]{:S(2)}) collective-permute-start(bf16[16,3072]{1,0:T(8,128)(2,1)S(1)} %get-tuple-element.39), channel_id=1, source_target_pairs={{0,3},{1,2},{2,1},{3,0},{4,7},{5,6},{6,5},{7,4},{8,11},{9,10},{10,... | collective-permute-start | bytes 294920 | tf_op jit(solution)/shard_map/ppermute | solution.py:254
  44.5 5.7 %collective-permute-start.16 = (bf16[16,3072]{1,0:T(8,128)(2,1)S(1)}, bf16[16,3072]{1,0:T(8,128)(2,1)S(1)}, u32[]{:S(2)}, u32[]{:S(2)}) collective-permute-start(bf16[16,3072]{1,0:T(8,128)(2,1)S(1)} %get-tuple-element.48), channel_id=1, source_target_pairs={{0,4},{4,0},{8,12},{12,8},{1,5},{5,1},{9,13},{13,9},{2,6},{6,2},{1... | collective-permute-start | bytes 294920 | tf_op jit(solution)/shard_map/ppermute | solution.py:254
  48.7 5.4 %collective-permute-start.12 = (bf16[16,3072]{1,0:T(8,128)(2,1)S(1)}, bf16[16,3072]{1,0:T(8,128)(2,1)S(1)}, u32[]{:S(2)}, u32[]{:S(2)}) collective-permute-start(bf16[16,3072]{1,0:T(8,128)(2,1)S(1)} %get-tuple-element.42), channel_id=1, source_target_pairs={{0,4},{4,0},{8,12},{12,8},{1,5},{5,1},{9,13},{13,9},{2,6},{6,2},{1... | collective-permute-start | bytes 294920 | tf_op jit(solution)/shard_map/ppermute | solution.py:254
  50.3 6.5 %collective-permute-start.17 = (bf16[16,3072]{1,0:T(8,128)(2,1)S(1)}, bf16[16,3072]{1,0:T(8,128)(2,1)S(1)}, u32[]{:S(2)}, u32[]{:S(2)}) collective-permute-start(bf16[16,3072]{1,0:T(8,128)(2,1)S(1)} %shard_map.115), channel_id=1, source_target_pairs={{0,8},{4,12},{8,0},{12,4},{1,9},{5,13},{9,1},{13,5},{2,10},{6,14},... | collective-permute-start | bytes 294920 | tf_op jit(solution)/shard_map/ppermute | solution.py:254

commit v7 on v6

--- a/solution.py
+++ b/solution.py
@@ -71,7 +71,7 @@
 
 
 def attend_kernel(
-    lengths_hbm, queries_hbm, keys_hbm, values_hbm, routes_hbm, residual_hbm, gain_hbm,
+    _, lengths_hbm, queries_hbm, keys_hbm, values_hbm, routes_hbm, residual_hbm, gain_hbm,
     stream_ref, payload_ref,
     lengths_ref, queries_ref, keys_ref, values_ref, routes_ref, residual_ref, gain_ref, sems,
 ):
@@ -202,10 +202,12 @@
             begin += count
 
 
-def mix_kernel(me_ref, router_ref, *refs, chunks, experts):
+def mix_kernel(me_ref, router_ref, *refs, chunks, experts, after):
+    refs = refs[after:]
     payload = jnp.concatenate([ref[...] for ref in refs[:chunks]], axis=0)
+    order = farthest_first(experts)
     returned = jnp.concatenate(
-        [ref[...].astype(F32) for ref in refs[chunks : chunks + experts]], axis=0
+        [refs[chunks + order.index(e)][...].astype(F32) for e in range(experts)], axis=0
     ).astype(BF16)
     added, outs = refs[chunks + experts : len(refs) - chunks], refs[len(refs) - chunks :]
     batch, width = outs[0].shape
@@ -218,18 +220,19 @@
         ref[...] = part.astype(ref.dtype)
 
 
-def mix(me, router, payloads, returned, added):
+def mix(me, router, payloads, returned, added, after):
     chunks, experts = len(payloads), len(returned)
     width = returned[0].shape[1]
     batch = payloads[0].shape[0]
-    returned = [swap(block, "expert", e) for e, block in enumerate(returned)]
-    operands = [me, router, *payloads, *returned, *added]
+    returned = [swap(block, "expert", e) for e, block in zip(farthest_first(experts), returned)]
+    operands = [me, router, *after, *payloads, *returned, *added]
     return pl.pallas_call(
-        functools.partial(mix_kernel, chunks=chunks, experts=experts),
-        in_specs=[SCALAR] + [WHOLE] * (len(operands) - 1),
+        functools.partial(mix_kernel, chunks=chunks, experts=experts, after=len(after)),
+        in_specs=[SCALAR, WHOLE] + [ANY] * len(after) + [WHOLE] * (len(operands) - 2 - len(after)),
         out_specs=[WHOLE] * chunks,
         out_shape=[
-            jax.ShapeDtypeStruct((batch, width), BF16 if j % 2 else F32) for j in range(chunks)
+            jax.ShapeDtypeStruct((batch, width), F32 if added and j == 0 else BF16)
+            for j in range(chunks)
         ],
         cost_estimate=LIGHT,
         compiler_params=params(experts * chunks * CAP * width),
@@ -252,6 +255,10 @@
         return value
     count = lax.axis_size(axis)
     return lax.ppermute(value, axis, [(i, i ^ step) for i in range(count)])
+
+
+def farthest_first(count):
+    return [0, *range(count - 1, 0, -1)]
 
 
 def params(elements):
@@ -288,19 +295,16 @@
     held[3] = (batch, -(-window // LANES) * LANES, depth)
     stream, payload = pl.pallas_call(
         attend_kernel,
-        in_specs=[ANY] * len(operands),
+        in_specs=[SCALAR] + [ANY] * len(operands),
         out_specs=[WHOLE, WHOLE],
         out_shape=[shape((batch, width), F32), shape((batch, width + LANES), BF16)],
         scratch_shapes=[pltpu.VMEM(size, a.dtype) for size, a in zip(held, operands)]
         + [pltpu.SemaphoreType.DMA((5 + 2 * (KVH // PAIR),))],
         compiler_params=params(28 * batch * width),
-        cost_estimate=pl.CostEstimate(flops=10**9, bytes_accessed=4 * 10**6, transcendentals=0),
-    )(*operands)
-
-    chunks = []
-    for j in range(layers):
-        passed = j > 1 and j % 2
-        chunks.append(swap(chunks[j - 1], "attn", 1) if passed else swap(payload, "attn", j))
+        cost_estimate=LIGHT,
+    )(me, *operands)
+
+    chunks = [swap(payload, "attn", j) for j in range(layers)]
     groups = [[0, 1], list(range(2, layers))]
     inputs, ahead = [], []
     for group in groups:
@@ -310,10 +314,10 @@
             in_specs=[SCALAR] + [ANY] * len(ahead) + [WHOLE] * count,
             out_specs=[WHOLE] * experts,
             out_shape=[shape((count * CAP, width), BF16)] * experts,
-            cost_estimate=BUSY,
+            cost_estimate=BUSY if group == groups[0] else LIGHT,
             compiler_params=params(experts * count * CAP * width),
         )(me, *ahead, *[chunks[j] for j in group])
-        arrived = [swap(slots[e], "expert", e) for e in range(experts)]
+        arrived = [swap(slots[e], "expert", e) for e in farthest_first(experts)]
         ahead = arrived[1:2]
         inputs += arrived
 
@@ -329,25 +333,12 @@
     )(*inputs, gate_proj[0], up_proj[0], down_proj[0])
 
     near, far = results[:experts], results[experts:]
-    far = mix(me, router, [chunks[j] for j in groups[1]], far, [])
-    kept, sent = far[::2], far[1::2]
-    passed = [swap(block, "attn", 1) for block in sent]
-    received = []
-    for j, own, other in zip(groups[1][::2], kept, passed):
-        total = pl.pallas_call(
-            add_kernel,
-            in_specs=[WHOLE, WHOLE],
-            out_specs=WHOLE,
-            out_shape=shape((batch, width), BF16),
-            cost_estimate=LIGHT,
-            compiler_params=params(2 * batch * width),
-        )(own, other)
-        received.append(swap(total, "attn", j))
-    base, first = mix(me, router, chunks[:2], near, [stream])
-    received = [swap(first, "attn", 1), *received]
+    far = mix(me, router, [chunks[j] for j in groups[1]], far, [], [])
+    base, first = mix(me, router, chunks[:2], near, [stream], far[:1])
+    received = [swap(block, "attn", j + 1) for j, block in enumerate([first, *far])]
     return pl.pallas_call(
         add_kernel,
-        in_specs=[WHOLE] * (1 + len(received)),
+        in_specs=[WHOLE] * layers,
         out_specs=WHOLE,
         out_shape=shape((batch, width), BF16),
         cost_estimate=LIGHT,

time: 57.6 us -> 56.2 us (0.976)
  waiting for transfers between devices: 18.6 us -> 22.1 us
  starting transfers between devices: 20.6 us -> 17.6 us
  local copies, waits for them, and re-layouts: 2.08 us -> 0.06 us
    ppermute x18, waiting for transfers between devices: 18.6 us -> 22.1 us  [swap(): return lax.ppermute(value, axis, [(i, i ^ step) for i in range(count)])]
    ppermute x18, starting transfers between devices: 20.6 us -> 17.6 us  [swap(): return lax.ppermute(value, axis, [(i, i ^ step) for i in range(count)])]
    unnamed x20, local copies, waits for them, and re-layouts: 2.08 us -> 0.06 us
    pallas_call x3 -> x2, Pallas kernels: 4.68 us -> 4.67 us  [the longest x1 3.99 us: shards(): pl.pallas_call(attend_kernel, in_specs=[SCALAR] + [ANY] * len(operands),...]
where the time goes in v7:
time: 56.2 us; the launch traced here: 56.1 us
  waiting for transfers between devices  22.1 us (39%)
  starting transfers between devices  17.6 us (31%)
  Pallas kernels  16.1 us (29%)
    ppermute x18, waiting for transfers between devices, swap(): return lax.ppermute(value, axis, [(i, i ^ step) for i in range(count)])  22.1 us
    ppermute x18, starting transfers between devices, swap(): return lax.ppermute(value, axis, [(i, i ^ step) for i in range(count)])  17.6 us
    pallas_call x1, Pallas kernels, shards(): pl.pallas_call(functools.partial(expert_kernel, pieces=len(inputs)), in_s...  9.23 us
    pallas_call x1, Pallas kernels, shards(): pl.pallas_call(attend_kernel, in_specs=[SCALAR] + [ANY] * len(operands),...  3.99 us
    pallas_call x2, Pallas kernels, mix(): pl.pallas_call(functools.partial(mix_kernel, chunks=chunks, experts=exper...  1.23 us
  transfers between devices with their start and end apart: 18, of which 11 were waited for; matrix products, arithmetic and copies ran while one was open for 0% of the time, Pallas kernels for 4%

profile of v7, /device:TPU:0, one launch (start us, length us, event | category | flops | bytes accessed | tf_op | source)
XLA Modules:
  0.0 56.1 jit_solution(1249930097575989600)
XLA Ops:
  0.0 4.0 %shard_map.109 = (f32[16,3072]{1,0:T(8,128)S(1)}, bf16[16,3200]{1,0:T(8,128)(2,1)S(1)}) custom-call(s32[1]{0:T(128)} %bitcast._.me_ref, s32[1,16]{1,0:T(1,128)} %bitcast.21, bf16[16,3072]{1,0:T(8,128)(2,1)} %queries_hbm.1, bf16[16,96,512]{2,1,0:T(8,128)(2,1)} %keys_hbm.1, bf16[16,96,512]{2,1,0:T(8,128)(2,1)} %values_hbm.1, s32[2,16]{1,0:T(2,128)} %bitcast.20, ...), custom_call_target="tpu_custom_call" | custom-call | tf_op jit(solution)/shard_map/pallas_call | solution.py:296
  4.0 0.0 slice-start
  4.0 0.0 slice-start.3
  4.0 0.0 slice-start.6
  4.0 0.0 slice-start.1
  4.0 0.0 slice-start.2
  4.1 0.0 slice-start.4
  4.1 0.0 slice-start.5
  4.1 0.0 slice-start.7
  4.1 0.0 slice-start.8
  4.1 3.1 %collective-permute-start.2 = (bf16[16,3200]{1,0:T(8,128)(2,1)S(1)}, bf16[16,3200]{1,0:T(8,128)(2,1)S(1)}, u32[]{:S(2)}, u32[]{:S(2)}) collective-permute-start(bf16[16,3200]{1,0:T(8,128)(2,1)S(1)} %get-tuple-element.27.refs_0_.refs_1_), channel_id=1, source_target_pairs={{0,4},{4,0},{8,12},{12,8},{1,5},{5,1},{9,13},{13,9},{2,6},{6,2},{1... | collective-permute-start | bytes 307208 | tf_op jit(solution)/shard_map/ppermute | solution.py:257
  7.2 2.5 %collective-permute-start.1 = (bf16[16,3200]{1,0:T(8,128)(2,1)S(1)}, bf16[16,3200]{1,0:T(8,128)(2,1)S(1)}, u32[]{:S(2)}, u32[]{:S(2)}) collective-permute-start(bf16[16,3200]{1,0:T(8,128)(2,1)S(1)} %get-tuple-element.27.refs_0_.refs_1_), channel_id=1, source_target_pairs={{0,12},{4,8},{8,4},{12,0},{1,13},{5,9},{9,5},{13,1},{2,14},{6,10},... | collective-permute-start | bytes 307208 | tf_op jit(solution)/shard_map/ppermute | solution.py:257
  9.7 0.1 collective-permute-start
  9.8 0.3 collective-permute-done.2.refs_1_.refs_2_
  10.1 0.5 shard_map.110
  10.6 0.2 collective-permute-start.3
  10.7 1.7 %collective-permute-start.4 = (bf16[16,3072]{1,0:T(8,128)(2,1)S(1)}, bf16[16,3072]{1,0:T(8,128)(2,1)S(1)}, u32[]{:S(2)}, u32[]{:S(2)}) collective-permute-start(bf16[16,3072]{1,0:T(8,128)(2,1)S(1)} %get-tuple-element.30), channel_id=1, source_target_pairs={{0,2},{1,3},{2,0},{3,1},{4,6},{5,7},{6,4},{7,5},{8,10},{9,11},{10,... | collective-permute-start | bytes 294920 | tf_op jit(solution)/shard_map/ppermute | solution.py:257
  12.4 0.1 collective-permute-start.5
  12.5 3.1 %collective-permute-done.1.refs_2_.refs_1_ = bf16[16,3200]{1,0:T(8,128)(2,1)S(1)} collective-permute-done((bf16[16,3200]{1,0:T(8,128)(2,1)S(1)}, bf16[16,3200]{1,0:T(8,128)(2,1)S(1)}, u32[]{:S(2)}, u32[]{:S(2)}) %collective-permute-start.1) | collective-permute-done | bytes 102432 | tf_op jit(solution)/shard_map/ppermute | solution.py:257
  15.6 3.4 %collective-permute-done.refs_1_.refs_0_ = bf16[16,3200]{1,0:T(8,128)(2,1)S(1)} collective-permute-done((bf16[16,3200]{1,0:T(8,128)(2,1)S(1)}, bf16[16,3200]{1,0:T(8,128)(2,1)S(1)}, u32[]{:S(2)}, u32[]{:S(2)}) %collective-permute-start) | collective-permute-done | bytes 102432 | tf_op jit(solution)/shard_map/ppermute | solution.py:257
  19.0 0.0 collective-permute-done.3.refs_0_.refs_1_
  19.0 0.5 shard_map.111
  19.5 0.7 %collective-permute-start.6 = (bf16[16,3072]{1,0:T(8,128)(2,1)S(1)}, bf16[16,3072]{1,0:T(8,128)(2,1)S(1)}, u32[]{:S(2)}, u32[]{:S(2)}) collective-permute-start(bf16[16,3072]{1,0:T(8,128)(2,1)S(1)} %get-tuple-element.33), channel_id=1, source_target_pairs={{0,3},{1,2},{2,1},{3,0},{4,7},{5,6},{6,5},{7,4},{8,11},{9,10},{10,... | collective-permute-start | bytes 294920 | tf_op jit(solution)/shard_map/ppermute | solution.py:257
  20.1 1.0 %collective-permute-start.7 = (bf16[16,3072]{1,0:T(8,128)(2,1)S(1)}, bf16[16,3072]{1,0:T(8,128)(2,1)S(1)}, u32[]{:S(2)}, u32[]{:S(2)}) collective-permute-start(bf16[16,3072]{1,0:T(8,128)(2,1)S(1)} %get-tuple-element.34), channel_id=1, source_target_pairs={{0,2},{1,3},{2,0},{3,1},{4,6},{5,7},{6,4},{7,5},{8,10},{9,11},{10,... | collective-permute-start | bytes 294920 | tf_op jit(solution)/shard_map/ppermute | solution.py:257
  21.1 0.3 collective-permute-start.8
  21.4 0.0 collective-permute-done.4.refs_2_
  21.4 0.0 collective-permute-done.5.refs_3_
  21.4 3.2 %collective-permute-done.6.refs_5_ = bf16[16,3072]{1,0:T(8,128)(2,1)S(1)} collective-permute-done((bf16[16,3072]{1,0:T(8,128)(2,1)S(1)}, bf16[16,3072]{1,0:T(8,128)(2,1)S(1)}, u32[]{:S(2)}, u32[]{:S(2)}) %collective-permute-start.6) | collective-permute-done | bytes 98336 | tf_op jit(solution)/shard_map/ppermute | solution.py:257
  24.6 2.2 %collective-permute-done.7.refs_6_ = bf16[16,3072]{1,0:T(8,128)(2,1)S(1)} collective-permute-done((bf16[16,3072]{1,0:T(8,128)(2,1)S(1)}, bf16[16,3072]{1,0:T(8,128)(2,1)S(1)}, u32[]{:S(2)}, u32[]{:S(2)}) %collective-permute-start.7) | collective-permute-done | bytes 98336 | tf_op jit(solution)/shard_map/ppermute | solution.py:257
  26.7 0.0 collective-permute-done.8.refs_7_
  26.7 0.0 slice-done
  26.7 0.0 slice-done.3
  26.7 0.0 slice-done.6
  26.7 0.0 slice-done.1
  26.8 0.0 slice-done.2
  26.8 0.0 slice-done.4
  26.8 0.0 slice-done.5
  26.8 0.0 slice-done.7
  26.8 0.0 slice-done.8
  26.8 0.0 copy-start
  26.8 9.2 %shard_map.112 = (bf16[16,3072]{1,0:T(8,128)(2,1)S(1)}, bf16[16,3072]{1,0:T(8,128)(2,1)S(1)}, bf16[16,3072]{1,0:T(8,128)(2,1)S(1)}, bf16[16,3072]{1,0:T(8,128)(2...) custom-call(bf16[16,3072]{1,0:T(8,128)(2,1)S(1)} %get-tuple-element., ...), custom_call_target="tpu_custom_call" | custom-call | tf_op jit(solution)/shard_map/pallas_call | solution.py:326
  36.1 0.7 %collective-permute-start.9 = (bf16[16,3072]{1,0:T(8,128)(2,1)S(1)}, bf16[16,3072]{1,0:T(8,128)(2,1)S(1)}, u32[]{:S(2)}, u32[]{:S(2)}) collective-permute-start(bf16[16,3072]{1,0:T(8,128)(2,1)S(1)} %get-tuple-element.37), channel_id=1, source_target_pairs={{0,3},{1,2},{2,1},{3,0},{4,7},{5,6},{6,5},{7,4},{8,11},{9,10},{10,... | collective-permute-start | bytes 294920 | tf_op jit(solution)/shard_map/ppermute | solution.py:257
  36.8 1.1 %collective-permute-start.10 = (bf16[16,3072]{1,0:T(8,128)(2,1)S(1)}, bf16[16,3072]{1,0:T(8,128)(2,1)S(1)}, u32[]{:S(2)}, u32[]{:S(2)}) collective-permute-start(bf16[16,3072]{1,0:T(8,128)(2,1)S(1)} %get-tuple-element.38), channel_id=1, source_target_pairs={{0,2},{1,3},{2,0},{3,1},{4,6},{5,7},{6,4},{7,5},{8,10},{9,11},{10,... | collective-permute-start | bytes 294920 | tf_op jit(solution)/shard_map/ppermute | solution.py:257
  37.8 0.2 collective-permute-start.11
  38.0 0.9 %collective-permute-start.12 = (bf16[16,3072]{1,0:T(8,128)(2,1)S(1)}, bf16[16,3072]{1,0:T(8,128)(2,1)S(1)}, u32[]{:S(2)}, u32[]{:S(2)}) collective-permute-start(bf16[16,3072]{1,0:T(8,128)(2,1)S(1)} %get-tuple-element.42), channel_id=1, source_target_pairs={{0,3},{1,2},{2,1},{3,0},{4,7},{5,6},{6,5},{7,4},{8,11},{9,10},{10,... | collective-permute-start | bytes 294920 | tf_op jit(solution)/shard_map/ppermute | solution.py:257
  38.9 1.0 %collective-permute-start.13 = (bf16[16,3072]{1,0:T(8,128)(2,1)S(1)}, bf16[16,3072]{1,0:T(8,128)(2,1)S(1)}, u32[]{:S(2)}, u32[]{:S(2)}) collective-permute-start(bf16[16,3072]{1,0:T(8,128)(2,1)S(1)} %get-tuple-element.43), channel_id=1, source_target_pairs={{0,2},{1,3},{2,0},{3,1},{4,6},{5,7},{6,4},{7,5},{8,10},{9,11},{10,... | collective-permute-start | bytes 294920 | tf_op jit(solution)/shard_map/ppermute | solution.py:257
  40.0 1.0 %collective-permute-done.9.refs_3_ = bf16[16,3072]{1,0:T(8,128)(2,1)S(1)} collective-permute-done((bf16[16,3072]{1,0:T(8,128)(2,1)S(1)}, bf16[16,3072]{1,0:T(8,128)(2,1)S(1)}, u32[]{:S(2)}, u32[]{:S(2)}) %collective-permute-start.9) | collective-permute-done | bytes 98336 | tf_op jit(solution)/shard_map/ppermute | solution.py:257
  41.0 0.3 collective-permute-start.14
  41.3 2.3 %collective-permute-done.10.refs_4_ = bf16[16,3072]{1,0:T(8,128)(2,1)S(1)} collective-permute-done((bf16[16,3072]{1,0:T(8,128)(2,1)S(1)}, bf16[16,3072]{1,0:T(8,128)(2,1)S(1)}, u32[]{:S(2)}, u32[]{:S(2)}) %collective-permute-start.10) | collective-permute-done | bytes 98336 | tf_op jit(solution)/shard_map/ppermute | solution.py:257
  43.6 0.0 collective-permute-done.11.refs_5_
  43.6 0.0 copy-done
  43.6 0.6 %shard_map.113 = (bf16[16,3072]{1,0:T(8,128)(2,1)S(1)}, bf16[16,3072]{1,0:T(8,128)(2,1)S(1)}) custom-call(s32[1]{0:T(128)} %bitcast._.me_ref, bf16[4,3072]{1,0:T(4,128)(2,1)S(1)} %bitcast.17, bf16[16,3200]{1,0:T(8,128)(2,1)S(1)} %collective-permute-done.refs_1_.refs_0_, bf16[16,3200]{1,0:T(8,128)(2,1)S(1)} %collective-permute-done.1.refs_2_.refs_1_, ...), custom_call_target="tpu_custom_call" | custom-call | tf_op jit(solution)/shard_map/pallas_call | solution.py:229
  44.2 2.7 %collective-permute-start.17 = (bf16[16,3072]{1,0:T(8,128)(2,1)S(1)}, bf16[16,3072]{1,0:T(8,128)(2,1)S(1)}, u32[]{:S(2)}, u32[]{:S(2)}) collective-permute-start(bf16[16,3072]{1,0:T(8,128)(2,1)S(1)} %get-tuple-element.48), channel_id=1, source_target_pairs={{0,12},{4,8},{8,4},{12,0},{1,13},{5,9},{9,5},{13,1},{2,14},{6,10},... | collective-permute-start | bytes 294920 | tf_op jit(solution)/shard_map/ppermute | solution.py:257
  46.9 0.0 collective-permute-start.16
  46.9 0.0 collective-permute-done.12.refs_4_
  46.9 0.6 %collective-permute-done.13.refs_5_ = bf16[16,3072]{1,0:T(8,128)(2,1)S(1)} collective-permute-done((bf16[16,3072]{1,0:T(8,128)(2,1)S(1)}, bf16[16,3072]{1,0:T(8,128)(2,1)S(1)}, u32[]{:S(2)}, u32[]{:S(2)}) %collective-permute-start.13) | collective-permute-done | bytes 98336 | tf_op jit(solution)/shard_map/ppermute | solution.py:257
  47.6 0.0 collective-permute-done.14.refs_6_
  47.6 0.6 %shard_map.114 = (f32[16,3072]{1,0:T(8,128)S(1)}, bf16[16,3072]{1,0:T(8,128)(2,1)S(1)}) custom-call(s32[1]{0:T(128)} %bitcast._.me_ref, bf16[4,3072]{1,0:T(4,128)(2,1)S(1)} %bitcast.18, bf16[16,3072]{1,0:T(8,128)(2,1)S(1)} %get-tuple-element.40.refs_0_, bf16[16,3200]{1,0:T(8,128)(2,1)S(1)} %get-tuple-element.27.refs_0_.refs_1_, ...), custom_call_target="tpu_custom_call" | custom-call | tf_op jit(solution)/shard_map/pallas_call | solution.py:229
  48.2 1.2 %collective-permute-start.15 = (bf16[16,3072]{1,0:T(8,128)(2,1)S(1)}, bf16[16,3072]{1,0:T(8,128)(2,1)S(1)}, u32[]{:S(2)}, u32[]{:S(2)}) collective-permute-start(bf16[16,3072]{1,0:T(8,128)(2,1)S(1)} %get-tuple-element.47), channel_id=1, source_target_pairs={{0,4},{4,0},{8,12},{12,8},{1,5},{5,1},{9,13},{13,9},{2,6},{6,2},{1... | collective-permute-start | bytes 294920 | tf_op jit(solution)/shard_map/ppermute | solution.py:257
  49.4 2.2 %collective-permute-done.17.refs_3_ = bf16[16,3072]{1,0:T(8,128)(2,1)S(1)} collective-permute-done((bf16[16,3072]{1,0:T(8,128)(2,1)S(1)}, bf16[16,3072]{1,0:T(8,128)(2,1)S(1)}, u32[]{:S(2)}, u32[]{:S(2)}) %collective-permute-start.17) | collective-permute-done | bytes 98336 | tf_op jit(solution)/shard_map/ppermute | solution.py:257
  51.6 3.1 %collective-permute-done.16.refs_2_ = bf16[16,3072]{1,0:T(8,128)(2,1)S(1)} collective-permute-done((bf16[16,3072]{1,0:T(8,128)(2,1)S(1)}, bf16[16,3072]{1,0:T(8,128)(2,1)S(1)}, u32[]{:S(2)}, u32[]{:S(2)}) %collective-permute-start.16) | collective-permute-done | bytes 98336 | tf_op jit(solution)/shard_map/ppermute | solution.py:257
  54.7 0.7 %collective-permute-done.15.refs_1_ = bf16[16,3072]{1,0:T(8,128)(2,1)S(1)} collective-permute-done((bf16[16,3072]{1,0:T(8,128)(2,1)S(1)}, bf16[16,3072]{1,0:T(8,128)(2,1)S(1)}, u32[]{:S(2)}, u32[]{:S(2)}) %collective-permute-start.15) | collective-permute-done | bytes 98336 | tf_op jit(solution)/shard_map/ppermute | solution.py:257
  55.4 0.7 %shard_map.115 = bf16[16,3072]{1,0:T(8,128)(2,1)} custom-call(f32[16,3072]{1,0:T(8,128)S(1)} %get-tuple-element.46.refs_0_, bf16[16,3072]{1,0:T(8,128)(2,1)S(1)} %collective-permute-done.15.refs_1_, bf16[16,3072]{1,0:T(8,128)(2,1)S(1)} %collective-permute-done.16.refs_2_, bf16[16,3072]{1,0:T(8,128)(2,1)S(1)} %collective-permute-done.17.refs_3_), custom_call_target="tpu_custom_call" | custom-call | tf_op jit(solution)/shard_map/pallas_call | solution.py:339
  (3 shorter events, 0.0 us)
Async XLA Ops:
  4.0 22.7 %slice-start = ((s8[12582912]{0:T(1024)(128)(4,1)}), s8[4194304]{0:T(1024)(128)(4,1)S(1)}, s32[]{:S(2)}) async-start(s8[12582912]{0:T(1024)(128)(4,1)} %bitcast.8), calls=%async_computation | async-start | bytes 8388608
  4.0 22.7 %slice-start.3 = ((s8[12582912]{0:T(1024)(128)(4,1)}), s8[4194304]{0:T(1024)(128)(4,1)S(1)}, s32[]{:S(2)}) async-start(s8[12582912]{0:T(1024)(128)(4,1)} %bitcast.11), calls=%async_computation.3 | async-start | bytes 8388608
  4.0 22.7 %slice-start.6 = ((s8[12582912]{0:T(1024)(128)(4,1)}), s8[4194304]{0:T(1024)(128)(4,1)S(1)}, s32[]{:S(2)}) async-start(s8[12582912]{0:T(1024)(128)(4,1)} %bitcast.14), calls=%async_computation.6 | async-start | bytes 8388608
  4.0 22.7 %slice-start.1 = ((s8[12582912]{0:T(1024)(128)(4,1)}), s8[4194304]{0:T(1024)(128)(4,1)S(1)}, s32[]{:S(2)}) async-start(s8[12582912]{0:T(1024)(128)(4,1)} %bitcast.8), calls=%async_computation.1 | async-start | bytes 8388608
  4.0 22.7 %slice-start.2 = ((s8[12582912]{0:T(1024)(128)(4,1)}), s8[4194304]{0:T(1024)(128)(4,1)S(1)}, s32[]{:S(2)}) async-start(s8[12582912]{0:T(1024)(128)(4,1)} %bitcast.8), calls=%async_computation.2 | async-start | bytes 8388608
  4.1 22.7 %slice-start.4 = ((s8[12582912]{0:T(1024)(128)(4,1)}), s8[4194304]{0:T(1024)(128)(4,1)S(1)}, s32[]{:S(2)}) async-start(s8[12582912]{0:T(1024)(128)(4,1)} %bitcast.11), calls=%async_computation.4 | async-start | bytes 8388608
  4.1 22.7 %slice-start.5 = ((s8[12582912]{0:T(1024)(128)(4,1)}), s8[4194304]{0:T(1024)(128)(4,1)S(1)}, s32[]{:S(2)}) async-start(s8[12582912]{0:T(1024)(128)(4,1)} %bitcast.11), calls=%async_computation.5 | async-start | bytes 8388608
  4.1 22.7 %slice-start.7 = ((s8[12582912]{0:T(1024)(128)(4,1)}), s8[4194304]{0:T(1024)(128)(4,1)S(1)}, s32[]{:S(2)}) async-start(s8[12582912]{0:T(1024)(128)(4,1)} %bitcast.14), calls=%async_computation.7 | async-start | bytes 8388608
  4.1 22.7 %slice-start.8 = ((s8[12582912]{0:T(1024)(128)(4,1)}), s8[4194304]{0:T(1024)(128)(4,1)S(1)}, s32[]{:S(2)}) async-start(s8[12582912]{0:T(1024)(128)(4,1)} %bitcast.14), calls=%async_computation.8 | async-start | bytes 8388608
  4.1 6.0 %collective-permute-start.2 = (bf16[16,3200]{1,0:T(8,128)(2,1)S(1)}, bf16[16,3200]{1,0:T(8,128)(2,1)S(1)}, u32[]{:S(2)}, u32[]{:S(2)}) collective-permute-start(bf16[16,3200]{1,0:T(8,128)(2,1)S(1)} %get-tuple-element.27.refs_0_.refs_1_), channel_id=1, source_target_pairs={{0,4},{4,0},{8,12},{12,8},{1,5},{5,1},{9,13},{13,9},{2,6},{6,2},{1... | collective-permute-start | bytes 307208 | tf_op jit(solution)/shard_map/ppermute | solution.py:257
  7.2 8.4 %collective-permute-start.1 = (bf16[16,3200]{1,0:T(8,128)(2,1)S(1)}, bf16[16,3200]{1,0:T(8,128)(2,1)S(1)}, u32[]{:S(2)}, u32[]{:S(2)}) collective-permute-start(bf16[16,3200]{1,0:T(8,128)(2,1)S(1)} %get-tuple-element.27.refs_0_.refs_1_), channel_id=1, source_target_pairs={{0,12},{4,8},{8,4},{12,0},{1,13},{5,9},{9,5},{13,1},{2,14},{6,10},... | collective-permute-start | bytes 307208 | tf_op jit(solution)/shard_map/ppermute | solution.py:257
  9.7 9.3 %collective-permute-start = (bf16[16,3200]{1,0:T(8,128)(2,1)S(1)}, bf16[16,3200]{1,0:T(8,128)(2,1)S(1)}, u32[]{:S(2)}, u32[]{:S(2)}) collective-permute-start(bf16[16,3200]{1,0:T(8,128)(2,1)S(1)} %get-tuple-element.27.refs_0_.refs_1_), channel_id=1, source_target_pairs={{0,8},{4,12},{8,0},{12,4},{1,9},{5,13},{9,1},{13,5},{2,10},{6,14},... | collective-permute-start | bytes 307208 | tf_op jit(solution)/shard_map/ppermute | solution.py:257
  10.6 8.4 %collective-permute-start.3 = (bf16[16,3072]{1,0:T(8,128)(2,1)S(1)}, bf16[16,3072]{1,0:T(8,128)(2,1)S(1)}, u32[]{:S(2)}, u32[]{:S(2)}) collective-permute-start(bf16[16,3072]{1,0:T(8,128)(2,1)S(1)} %get-tuple-element.29), channel_id=1, source_target_pairs={{0,3},{1,2},{2,1},{3,0},{4,7},{5,6},{6,5},{7,4},{8,11},{9,10},{10,... | collective-permute-start | bytes 294920 | tf_op jit(solution)/shard_map/ppermute | solution.py:257
  10.7 10.7 %collective-permute-start.4 = (bf16[16,3072]{1,0:T(8,128)(2,1)S(1)}, bf16[16,3072]{1,0:T(8,128)(2,1)S(1)}, u32[]{:S(2)}, u32[]{:S(2)}) collective-permute-start(bf16[16,3072]{1,0:T(8,128)(2,1)S(1)} %get-tuple-element.30), channel_id=1, source_target_pairs={{0,2},{1,3},{2,0},{3,1},{4,6},{5,7},{6,4},{7,5},{8,10},{9,11},{10,... | collective-permute-start | bytes 294920 | tf_op jit(solution)/shard_map/ppermute | solution.py:257
  12.4 9.0 %collective-permute-start.5 = (bf16[16,3072]{1,0:T(8,128)(2,1)S(1)}, bf16[16,3072]{1,0:T(8,128)(2,1)S(1)}, u32[]{:S(2)}, u32[]{:S(2)}) collective-permute-start(bf16[16,3072]{1,0:T(8,128)(2,1)S(1)} %get-tuple-element.31), channel_id=1, source_target_pairs={{0,1},{1,0},{2,3},{3,2},{4,5},{5,4},{6,7},{7,6},{8,9},{9,8},{10,11... | collective-permute-start | bytes 294920 | tf_op jit(solution)/shard_map/ppermute | solution.py:257
  19.5 5.1 %collective-permute-start.6 = (bf16[16,3072]{1,0:T(8,128)(2,1)S(1)}, bf16[16,3072]{1,0:T(8,128)(2,1)S(1)}, u32[]{:S(2)}, u32[]{:S(2)}) collective-permute-start(bf16[16,3072]{1,0:T(8,128)(2,1)S(1)} %get-tuple-element.33), channel_id=1, source_target_pairs={{0,3},{1,2},{2,1},{3,0},{4,7},{5,6},{6,5},{7,4},{8,11},{9,10},{10,... | collective-permute-start | bytes 294920 | tf_op jit(solution)/shard_map/ppermute | solution.py:257
  20.1 6.6 %collective-permute-start.7 = (bf16[16,3072]{1,0:T(8,128)(2,1)S(1)}, bf16[16,3072]{1,0:T(8,128)(2,1)S(1)}, u32[]{:S(2)}, u32[]{:S(2)}) collective-permute-start(bf16[16,3072]{1,0:T(8,128)(2,1)S(1)} %get-tuple-element.34), channel_id=1, source_target_pairs={{0,2},{1,3},{2,0},{3,1},{4,6},{5,7},{6,4},{7,5},{8,10},{9,11},{10,... | collective-permute-start | bytes 294920 | tf_op jit(solution)/shard_map/ppermute | solution.py:257
  21.1 5.6 %collective-permute-start.8 = (bf16[16,3072]{1,0:T(8,128)(2,1)S(1)}, bf16[16,3072]{1,0:T(8,128)(2,1)S(1)}, u32[]{:S(2)}, u32[]{:S(2)}) collective-permute-start(bf16[16,3072]{1,0:T(8,128)(2,1)S(1)} %get-tuple-element.35), channel_id=1, source_target_pairs={{0,1},{1,0},{2,3},{3,2},{4,5},{5,4},{6,7},{7,6},{8,9},{9,8},{10,11... | collective-permute-start | bytes 294920 | tf_op jit(solution)/shard_map/ppermute | solution.py:257
  26.8 16.8 %copy-start = (bf16[3072,4]{0,1:T(4,128)(2,1)S(1)}, bf16[3072,4]{0,1:T(4,128)(2,1)}, u32[]{:S(2)}) copy-start(bf16[3072,4]{0,1:T(4,128)(2,1)} %param.18) | copy-start | bytes 73732
  36.1 4.9 %collective-permute-start.9 = (bf16[16,3072]{1,0:T(8,128)(2,1)S(1)}, bf16[16,3072]{1,0:T(8,128)(2,1)S(1)}, u32[]{:S(2)}, u32[]{:S(2)}) collective-permute-start(bf16[16,3072]{1,0:T(8,128)(2,1)S(1)} %get-tuple-element.37), channel_id=1, source_target_pairs={{0,3},{1,2},{2,1},{3,0},{4,7},{5,6},{6,5},{7,4},{8,11},{9,10},{10,... | collective-permute-start | bytes 294920 | tf_op jit(solution)/shard_map/ppermute | solution.py:257
  36.8 6.8 %collective-permute-start.10 = (bf16[16,3072]{1,0:T(8,128)(2,1)S(1)}, bf16[16,3072]{1,0:T(8,128)(2,1)S(1)}, u32[]{:S(2)}, u32[]{:S(2)}) collective-permute-start(bf16[16,3072]{1,0:T(8,128)(2,1)S(1)} %get-tuple-element.38), channel_id=1, source_target_pairs={{0,2},{1,3},{2,0},{3,1},{4,6},{5,7},{6,4},{7,5},{8,10},{9,11},{10,... | collective-permute-start | bytes 294920 | tf_op jit(solution)/shard_map/ppermute | solution.py:257
  37.8 5.7 %collective-permute-start.11 = (bf16[16,3072]{1,0:T(8,128)(2,1)S(1)}, bf16[16,3072]{1,0:T(8,128)(2,1)S(1)}, u32[]{:S(2)}, u32[]{:S(2)}) collective-permute-start(bf16[16,3072]{1,0:T(8,128)(2,1)S(1)} %get-tuple-element.39), channel_id=1, source_target_pairs={{0,1},{1,0},{2,3},{3,2},{4,5},{5,4},{6,7},{7,6},{8,9},{9,8},{10,11... | collective-permute-start | bytes 294920 | tf_op jit(solution)/shard_map/ppermute | solution.py:257
  38.0 8.9 %collective-permute-start.12 = (bf16[16,3072]{1,0:T(8,128)(2,1)S(1)}, bf16[16,3072]{1,0:T(8,128)(2,1)S(1)}, u32[]{:S(2)}, u32[]{:S(2)}) collective-permute-start(bf16[16,3072]{1,0:T(8,128)(2,1)S(1)} %get-tuple-element.42), channel_id=1, source_target_pairs={{0,3},{1,2},{2,1},{3,0},{4,7},{5,6},{6,5},{7,4},{8,11},{9,10},{10,... | collective-permute-start | bytes 294920 | tf_op jit(solution)/shard_map/ppermute | solution.py:257
  38.9 8.6 %collective-permute-start.13 = (bf16[16,3072]{1,0:T(8,128)(2,1)S(1)}, bf16[16,3072]{1,0:T(8,128)(2,1)S(1)}, u32[]{:S(2)}, u32[]{:S(2)}) collective-permute-start(bf16[16,3072]{1,0:T(8,128)(2,1)S(1)} %get-tuple-element.43), channel_id=1, source_target_pairs={{0,2},{1,3},{2,0},{3,1},{4,6},{5,7},{6,4},{7,5},{8,10},{9,11},{10,... | collective-permute-start | bytes 294920 | tf_op jit(solution)/shard_map/ppermute | solution.py:257
  41.0 6.6 %collective-permute-start.14 = (bf16[16,3072]{1,0:T(8,128)(2,1)S(1)}, bf16[16,3072]{1,0:T(8,128)(2,1)S(1)}, u32[]{:S(2)}, u32[]{:S(2)}) collective-permute-start(bf16[16,3072]{1,0:T(8,128)(2,1)S(1)} %get-tuple-element.44), channel_id=1, source_target_pairs={{0,1},{1,0},{2,3},{3,2},{4,5},{5,4},{6,7},{7,6},{8,9},{9,8},{10,11... | collective-permute-start | bytes 294920 | tf_op jit(solution)/shard_map/ppermute | solution.py:257
  44.2 7.4 %collective-permute-start.17 = (bf16[16,3072]{1,0:T(8,128)(2,1)S(1)}, bf16[16,3072]{1,0:T(8,128)(2,1)S(1)}, u32[]{:S(2)}, u32[]{:S(2)}) collective-permute-start(bf16[16,3072]{1,0:T(8,128)(2,1)S(1)} %get-tuple-element.48), channel_id=1, source_target_pairs={{0,12},{4,8},{8,4},{12,0},{1,13},{5,9},{9,5},{13,1},{2,14},{6,10},... | collective-permute-start | bytes 294920 | tf_op jit(solution)/shard_map/ppermute | solution.py:257
  46.9 7.8 %collective-permute-start.16 = (bf16[16,3072]{1,0:T(8,128)(2,1)S(1)}, bf16[16,3072]{1,0:T(8,128)(2,1)S(1)}, u32[]{:S(2)}, u32[]{:S(2)}) collective-permute-start(bf16[16,3072]{1,0:T(8,128)(2,1)S(1)} %get-tuple-element.40.refs_0_), channel_id=1, source_target_pairs={{0,8},{4,12},{8,0},{12,4},{1,9},{5,13},{9,1},{13,5},{2,10},{6,14},... | collective-permute-start | bytes 294920 | tf_op jit(solution)/shard_map/ppermute | solution.py:257
  48.2 7.2 %collective-permute-start.15 = (bf16[16,3072]{1,0:T(8,128)(2,1)S(1)}, bf16[16,3072]{1,0:T(8,128)(2,1)S(1)}, u32[]{:S(2)}, u32[]{:S(2)}) collective-permute-start(bf16[16,3072]{1,0:T(8,128)(2,1)S(1)} %get-tuple-element.47), channel_id=1, source_target_pairs={{0,4},{4,0},{8,12},{12,8},{1,5},{5,1},{9,13},{13,9},{2,6},{6,2},{1... | collective-permute-start | bytes 294920 | tf_op jit(solution)/shard_map/ppermute | solution.py:257

commit v8 on v7

--- a/solution.py
+++ b/solution.py
@@ -13,6 +13,7 @@
 CAP = 8
 LANES = 128
 PAIR = 2
+STRIPS = 6
 MIB = 1 << 20
 F32 = jnp.float32
 BF16 = jnp.bfloat16
@@ -164,42 +165,69 @@
     payload_ref[:, width:] = named.astype(BF16)
 
 
-def split_kernel(me_ref, *refs, chunks, after):
+def split_kernel(me_ref, *refs, chunks, experts, after):
     refs = refs[after:]
     payload = jnp.concatenate([ref[...] for ref in refs[:chunks]], axis=0)
-    slots = refs[chunks:]
-    width = slots[0].shape[1]
+    outs = refs[chunks:]
+    width = payload.shape[1] - LANES
     rows, named = payload[:, :width], payload[:, width:]
-    out = dispatch(me_ref[0], rows, named, chunks, len(slots))
-    span = chunks * CAP
-    for e, ref in enumerate(slots):
-        ref[...] = out[e * span : (e + 1) * span].astype(BF16)
-
-
-def expert_kernel(*refs, pieces):
-    xs, (gate_ref, up_ref, down_ref) = refs[:pieces], refs[pieces : pieces + 3]
-    outs = refs[pieces + 3 : 2 * pieces + 3]
-    rows_ref, hidden_ref = refs[2 * pieces + 3 :]
-    rows_ref[...] = jnp.concatenate([ref[...].astype(F32) for ref in xs], axis=0).astype(BF16)
-    width, units = gate_ref.shape
+    slots = dispatch(me_ref[0], rows, named, chunks, experts)
+    span, part = chunks * CAP, outs[0].shape[1]
+    for i, ref in enumerate(outs):
+        p, e = i // experts, i % experts
+        ref[...] = slots[e * span : (e + 1) * span, p * part : (p + 1) * part].astype(BF16)
+
+
+def begin_kernel(*refs, near, far):
+    gate_ref, up_ref, gate_out, up_out, rows_ref = refs[near + far :]
+    half = rows_ref.shape[1]
+    blocks = [ref[:, :half] for ref in refs[:near]] + [ref[...] for ref in refs[near : near + far]]
+    rows_ref[...] = jnp.concatenate([block.astype(F32) for block in blocks], axis=0).astype(BF16)
+    units = gate_ref.shape[1]
     tile = min(256, units)
 
     @pl.loop(0, units // tile)
     def _(i):
         at = pl.ds(pl.multiple_of(i * tile, tile), tile)
-        gate = dot(rows_ref[...], gate_ref[:, at])
-        up = dot(rows_ref[...], up_ref[:, at])
-        hidden_ref[:, at] = (jax.nn.silu(gate) * up).astype(BF16)
-
-    @pl.loop(0, width // tile)
+        gate_out[:, at] = dot(rows_ref[...], gate_ref[:half, at])
+        up_out[:, at] = dot(rows_ref[...], up_ref[:half, at])
+
+
+def end_kernel(*refs, near, far):
+    gate_in, up_in, gate_ref, up_ref, down_hbm = refs[near + far : near + far + 5]
+    outs = refs[near + far + 5 : -4]
+    rows_ref, hidden_ref, down_ref, sems = refs[-4:]
+    half = rows_ref.shape[1]
+    width, units = gate_ref.shape
+    strip = width // sems.shape[0]
+    copies = []
+    for c in range(sems.shape[0]):
+        at = pl.ds(c * strip, strip)
+        copies.append(pltpu.make_async_copy(down_hbm.at[:, at], down_ref.at[:, at], sems.at[c]))
+        copies[-1].start()
+    blocks = [ref[:, half:] for ref in refs[:near]] + [ref[...] for ref in refs[near : near + far]]
+    rows_ref[...] = jnp.concatenate([block.astype(F32) for block in blocks], axis=0).astype(BF16)
+    tile = min(256, units)
+
+    @pl.loop(0, units // tile)
     def _(i):
         at = pl.ds(pl.multiple_of(i * tile, tile), tile)
-        out = dot(hidden_ref[...], down_ref[:, at])
-        begin = 0
-        for ref in outs:
-            count = ref.shape[0]
-            ref[:, at] = out[begin : begin + count].astype(BF16)
-            begin += count
+        gate = gate_in[:, at] + dot(rows_ref[...], gate_ref[half:, at])
+        up = up_in[:, at] + dot(rows_ref[...], up_ref[half:, at])
+        hidden_ref[:, at] = (jax.nn.silu(gate) * up).astype(BF16)
+
+    for c, copy in enumerate(copies):
+        copy.wait()
+
+        @pl.loop(0, strip // tile)
+        def _(i):
+            at = pl.ds(pl.multiple_of(c * strip + i * tile, tile), tile)
+            out = dot(hidden_ref[...], down_ref[:, at])
+            begin = 0
+            for ref in outs:
+                count = ref.shape[0]
+                ref[:, at] = out[begin : begin + count].astype(BF16)
+                begin += count
 
 
 def mix_kernel(me_ref, router_ref, *refs, chunks, experts, after):
@@ -306,31 +334,52 @@
 
     chunks = [swap(payload, "attn", j) for j in range(layers)]
     groups = [[0, 1], list(range(2, layers))]
-    inputs, ahead = [], []
-    for group in groups:
-        count = len(group)
+    half = width // 2
+    order = farthest_first(experts)
+
+    def send(group, columns, after):
+        count, parts = len(group), width // columns
         slots = pl.pallas_call(
-            functools.partial(split_kernel, chunks=count, after=len(ahead)),
-            in_specs=[SCALAR] + [ANY] * len(ahead) + [WHOLE] * count,
-            out_specs=[WHOLE] * experts,
-            out_shape=[shape((count * CAP, width), BF16)] * experts,
-            cost_estimate=BUSY if group == groups[0] else LIGHT,
+            functools.partial(split_kernel, chunks=count, experts=experts, after=len(after)),
+            in_specs=[SCALAR] + [ANY] * len(after) + [WHOLE] * count,
+            out_specs=[WHOLE] * (parts * experts),
+            out_shape=[shape((count * CAP, columns), BF16)] * (parts * experts),
+            cost_estimate=LIGHT if after else BUSY,
             compiler_params=params(experts * count * CAP * width),
-        )(me, *ahead, *[chunks[j] for j in group])
-        arrived = [swap(slots[e], "expert", e) for e in farthest_first(experts)]
-        ahead = arrived[1:2]
-        inputs += arrived
-
-    total_rows = sum(block.shape[0] for block in inputs)
+        )(me, *after, *[chunks[j] for j in group])
+        return [
+            swap(slots[p * experts + e], "expert", e) for p in range(parts) for e in order
+        ]
+
+    near = send(groups[0], width, [])
+    far = send(groups[1], half, near[1:2])
+    total_rows = sum(block.shape[0] for block in near + far[:experts])
     units = gate_proj.shape[2]
+    counts = {"near": experts, "far": experts}
+    sums = pl.pallas_call(
+        functools.partial(begin_kernel, **counts),
+        in_specs=[WHOLE] * (2 * experts + 2),
+        out_specs=[WHOLE] * 2,
+        out_shape=[shape((total_rows, units), F32)] * 2,
+        scratch_shapes=[pltpu.VMEM((total_rows, half), BF16)],
+        cost_estimate=pl.CostEstimate(
+            flops=4 * total_rows * half * units, bytes_accessed=0, transcendentals=0
+        ),
+        compiler_params=params(total_rows * width),
+    )(*near, *far[:experts], gate_proj[0], up_proj[0])
     results = pl.pallas_call(
-        functools.partial(expert_kernel, pieces=len(inputs)),
-        in_specs=[WHOLE] * (len(inputs) + 3),
-        out_specs=[WHOLE] * len(inputs),
-        out_shape=[shape(block.shape, BF16) for block in inputs],
-        scratch_shapes=[pltpu.VMEM((total_rows, width), BF16), pltpu.VMEM((total_rows, units), BF16)],
-        compiler_params=params(total_rows * width),
-    )(*inputs, gate_proj[0], up_proj[0], down_proj[0])
+        functools.partial(end_kernel, **counts),
+        in_specs=[WHOLE] * (2 * experts + 4) + [ANY],
+        out_specs=[WHOLE] * (2 * experts),
+        out_shape=[shape((block.shape[0], width), BF16) for block in near + far[:experts]],
+        scratch_shapes=[
+            pltpu.VMEM((total_rows, half), BF16),
+            pltpu.VMEM((total_rows, units), BF16),
+            pltpu.VMEM((units, width), BF16),
+            pltpu.SemaphoreType.DMA((STRIPS,)),
+        ],
+        compiler_params=params(total_rows * width + units * width // 5),
+    )(*near, *far[experts:], *sums, gate_proj[0], up_proj[0], in_hbm(down_proj[0]))
 
     near, far = results[:experts], results[experts:]
     far = mix(me, router, [chunks[j] for j in groups[1]], far, [], [])

time: 56.2 us -> 55.8 us (level)
  waiting for transfers between devices: 22.1 us -> 18.2 us
  starting transfers between devices: 17.6 us -> 19.5 us
  Pallas kernels: 16.1 us -> 17.6 us
    ppermute x18 -> x21, waiting for transfers between devices: 22.1 us -> 18.2 us  [swap(): return lax.ppermute(value, axis, [(i, i ^ step) for i in range(count)])]
    ppermute x18 -> x21, starting transfers between devices: 17.6 us -> 19.5 us  [swap(): return lax.ppermute(value, axis, [(i, i ^ step) for i in range(count)])]
    pallas_call x3 -> x4, Pallas kernels: 10.2 us -> 11.7 us  [the longest x1 7.53 us: shards(): pl.pallas_call(functools.partial(end_kernel, **counts), in_specs=[WHOLE]...]
  transfers between devices with their start and end apart: 18 -> 21, of which waited for: 11 -> 11; matrix products, arithmetic and copies ran while one was open for 0% -> 0% of each run, Pallas kernels for 4% -> 10%
where the time goes in v8:
time: 55.8 us; the launch traced here: 55.6 us
  starting transfers between devices  19.5 us (35%)
  waiting for transfers between devices  18.2 us (33%)
  Pallas kernels  17.6 us (32%)
    ppermute x21, starting transfers between devices, swap(): return lax.ppermute(value, axis, [(i, i ^ step) for i in range(count)])  19.5 us
    ppermute x21, waiting for transfers between devices, swap(): return lax.ppermute(value, axis, [(i, i ^ step) for i in range(count)])  18.2 us
    pallas_call x1, Pallas kernels, shards(): pl.pallas_call(functools.partial(end_kernel, **counts), in_specs=[WHOLE]...  7.53 us
    pallas_call x1, Pallas kernels, shards(): pl.pallas_call(attend_kernel, in_specs=[SCALAR] + [ANY] * len(operands),...  3.99 us
    pallas_call x1, Pallas kernels, shards(): pl.pallas_call(functools.partial(begin_kernel, **counts), in_specs=[WHOLE...  3.26 us
    pallas_call x2, Pallas kernels, mix(): pl.pallas_call(functools.partial(mix_kernel, chunks=chunks, experts=exper...  1.23 us
  transfers between devices with their start and end apart: 21, of which 11 were waited for; matrix products, arithmetic and copies ran while one was open for 0% of the time, Pallas kernels for 10%

profile of v8, /device:TPU:0, one launch (start us, length us, event | category | flops | bytes accessed | tf_op | source)
XLA Modules:
  0.0 55.6 jit_solution(11982074500325058368)
XLA Ops:
  0.0 4.0 %shard_map.109 = (f32[16,3072]{1,0:T(8,128)S(1)}, bf16[16,3200]{1,0:T(8,128)(2,1)S(1)}) custom-call(s32[1]{0:T(128)} %bitcast._.me_ref, s32[1,16]{1,0:T(1,128)} %bitcast.21, bf16[16,3072]{1,0:T(8,128)(2,1)} %queries_hbm.1, bf16[16,96,512]{2,1,0:T(8,128)(2,1)} %keys_hbm.1, bf16[16,96,512]{2,1,0:T(8,128)(2,1)} %values_hbm.1, s32[2,16]{1,0:T(2,128)} %bitcast.20, ...), custom_call_target="tpu_custom_call" | custom-call | tf_op jit(solution)/shard_map/pallas_call | solution.py:324
  4.0 0.0 slice-start
  4.0 0.0 slice-start.3
  4.0 0.0 slice-start.1
  4.0 0.0 slice-start.2
  4.0 0.0 slice-start.4
  4.1 0.0 slice-start.5
  4.1 3.1 %collective-permute-start.2 = (bf16[16,3200]{1,0:T(8,128)(2,1)S(1)}, bf16[16,3200]{1,0:T(8,128)(2,1)S(1)}, u32[]{:S(2)}, u32[]{:S(2)}) collective-permute-start(bf16[16,3200]{1,0:T(8,128)(2,1)S(1)} %get-tuple-element.33.refs_0_.refs_1_), channel_id=1, source_target_pairs={{0,4},{4,0},{8,12},{12,8},{1,5},{5,1},{9,13},{13,9},{2,6},{6,2},{1... | collective-permute-start | bytes 307208 | tf_op jit(solution)/shard_map/ppermute | solution.py:285
  7.2 2.5 %collective-permute-start.1 = (bf16[16,3200]{1,0:T(8,128)(2,1)S(1)}, bf16[16,3200]{1,0:T(8,128)(2,1)S(1)}, u32[]{:S(2)}, u32[]{:S(2)}) collective-permute-start(bf16[16,3200]{1,0:T(8,128)(2,1)S(1)} %get-tuple-element.33.refs_0_.refs_1_), channel_id=1, source_target_pairs={{0,12},{4,8},{8,4},{12,0},{1,13},{5,9},{9,5},{13,1},{2,14},{6,10},... | collective-permute-start | bytes 307208 | tf_op jit(solution)/shard_map/ppermute | solution.py:285
  9.6 0.1 collective-permute-start
  9.7 0.3 collective-permute-done.2.refs_1_.refs_2_
  10.0 0.5 shard_map.110
  10.5 0.2 collective-permute-start.3
  10.7 1.7 %collective-permute-start.4 = (bf16[16,3072]{1,0:T(8,128)(2,1)S(1)}, bf16[16,3072]{1,0:T(8,128)(2,1)S(1)}, u32[]{:S(2)}, u32[]{:S(2)}) collective-permute-start(bf16[16,3072]{1,0:T(8,128)(2,1)S(1)} %get-tuple-element.36), channel_id=1, source_target_pairs={{0,2},{1,3},{2,0},{3,1},{4,6},{5,7},{6,4},{7,5},{8,10},{9,11},{10,... | collective-permute-start | bytes 294920 | tf_op jit(solution)/shard_map/ppermute | solution.py:285
  12.4 0.1 collective-permute-start.5
  12.4 3.1 %collective-permute-done.1.refs_2_.refs_1_ = bf16[16,3200]{1,0:T(8,128)(2,1)S(1)} collective-permute-done((bf16[16,3200]{1,0:T(8,128)(2,1)S(1)}, bf16[16,3200]{1,0:T(8,128)(2,1)S(1)}, u32[]{:S(2)}, u32[]{:S(2)}) %collective-permute-start.1) | collective-permute-done | bytes 102432 | tf_op jit(solution)/shard_map/ppermute | solution.py:285
  15.5 3.4 %collective-permute-done.refs_1_.refs_0_ = bf16[16,3200]{1,0:T(8,128)(2,1)S(1)} collective-permute-done((bf16[16,3200]{1,0:T(8,128)(2,1)S(1)}, bf16[16,3200]{1,0:T(8,128)(2,1)S(1)}, u32[]{:S(2)}, u32[]{:S(2)}) %collective-permute-start) | collective-permute-done | bytes 102432 | tf_op jit(solution)/shard_map/ppermute | solution.py:285
  18.9 0.0 collective-permute-done.3.refs_0_.refs_1_
  18.9 0.5 shard_map.111
  19.4 0.7 %collective-permute-start.9 = (bf16[16,1536]{1,0:T(8,128)(2,1)S(1)}, bf16[16,1536]{1,0:T(8,128)(2,1)S(1)}, u32[]{:S(2)}, u32[]{:S(2)}) collective-permute-start(bf16[16,1536]{1,0:T(8,128)(2,1)S(1)} %get-tuple-element.43), channel_id=1, source_target_pairs={{0,3},{1,2},{2,1},{3,0},{4,7},{5,6},{6,5},{7,4},{8,11},{9,10},{10,... | collective-permute-start | bytes 147464 | tf_op jit(solution)/shard_map/ppermute | solution.py:285
  20.1 1.0 %collective-permute-start.10 = (bf16[16,1536]{1,0:T(8,128)(2,1)S(1)}, bf16[16,1536]{1,0:T(8,128)(2,1)S(1)}, u32[]{:S(2)}, u32[]{:S(2)}) collective-permute-start(bf16[16,1536]{1,0:T(8,128)(2,1)S(1)} %get-tuple-element.44), channel_id=1, source_target_pairs={{0,2},{1,3},{2,0},{3,1},{4,6},{5,7},{6,4},{7,5},{8,10},{9,11},{10,... | collective-permute-start | bytes 147464 | tf_op jit(solution)/shard_map/ppermute | solution.py:285
  21.1 0.3 collective-permute-start.11
  21.3 0.0 collective-permute-done.4.refs_2_
  21.3 1.1 %collective-permute-start.6 = (bf16[16,1536]{1,0:T(8,128)(2,1)S(1)}, bf16[16,1536]{1,0:T(8,128)(2,1)S(1)}, u32[]{:S(2)}, u32[]{:S(2)}) collective-permute-start(bf16[16,1536]{1,0:T(8,128)(2,1)S(1)} %get-tuple-element.39), channel_id=1, source_target_pairs={{0,3},{1,2},{2,1},{3,0},{4,7},{5,6},{6,5},{7,4},{8,11},{9,10},{10,... | collective-permute-start | bytes 147464 | tf_op jit(solution)/shard_map/ppermute | solution.py:285
  22.4 0.0 collective-permute-done.5.refs_3_
  22.5 0.8 %collective-permute-start.7 = (bf16[16,1536]{1,0:T(8,128)(2,1)S(1)}, bf16[16,1536]{1,0:T(8,128)(2,1)S(1)}, u32[]{:S(2)}, u32[]{:S(2)}) collective-permute-start(bf16[16,1536]{1,0:T(8,128)(2,1)S(1)} %get-tuple-element.40), channel_id=1, source_target_pairs={{0,2},{1,3},{2,0},{3,1},{4,6},{5,7},{6,4},{7,5},{8,10},{9,11},{10,... | collective-permute-start | bytes 147464 | tf_op jit(solution)/shard_map/ppermute | solution.py:285
  23.2 0.3 collective-permute-done.9.refs_5_
  23.5 0.1 collective-permute-start.8
  23.6 1.1 %collective-permute-done.10.refs_6_ = bf16[16,1536]{1,0:T(8,128)(2,1)S(1)} collective-permute-done((bf16[16,1536]{1,0:T(8,128)(2,1)S(1)}, bf16[16,1536]{1,0:T(8,128)(2,1)S(1)}, u32[]{:S(2)}, u32[]{:S(2)}) %collective-permute-start.10) | collective-permute-done | bytes 49184 | tf_op jit(solution)/shard_map/ppermute | solution.py:285
  24.7 0.0 collective-permute-done.11.refs_7_
  24.7 0.0 slice-done
  24.7 0.0 slice-done.3
  24.7 0.0 slice-done.1
  24.7 0.0 slice-done.2
  24.7 0.0 slice-done.4
  24.7 0.0 slice-done.5
  24.8 3.3 %shard_map.112 = (f32[128,2048]{1,0:T(8,128)S(1)}, f32[128,2048]{1,0:T(8,128)S(1)}) custom-call(bf16[16,3072]{1,0:T(8,128)(2,1)S(1)} %get-tuple-element.34.refs_0_, bf16[16,3072]{1,0:T(8,128)(2,1)S(1)} %collective-permute-done.3.refs_0_.refs_1_, bf16[16,3072]{1,0:T(8,128)(2,1)S(1)} %collective-permute-done.4.refs_2_, ...), custom_call_target="tpu_custom_call" | custom-call | flops 1610612736 | tf_op jit(solution)/shard_map/pallas_call | solution.py:359
  28.0 0.0 collective-permute-done.6.refs_5_
  28.0 0.0 collective-permute-done.7.refs_6_
  28.0 0.0 collective-permute-done.8.refs_7_
  28.1 0.0 copy-start
  28.1 7.5 %shard_map.113 = (bf16[16,3072]{1,0:T(8,128)(2,1)S(1)}, bf16[16,3072]{1,0:T(8,128)(2,1)S(1)}, bf16[16,3072]{1,0:T(8,128)(2,1)S(1)}, bf16[16,3072]{1,0:T(8,128)(2...) custom-call(bf16[16,3072]{1,0:T(8,128)(2,1)S(1)} %get-tuple-element., ...), custom_call_target="tpu_custom_call" | custom-call | tf_op jit(solution)/shard_map/pallas_call | solution.py:370
  35.6 0.7 %collective-permute-start.12 = (bf16[16,3072]{1,0:T(8,128)(2,1)S(1)}, bf16[16,3072]{1,0:T(8,128)(2,1)S(1)}, u32[]{:S(2)}, u32[]{:S(2)}) collective-permute-start(bf16[16,3072]{1,0:T(8,128)(2,1)S(1)} %get-tuple-element.49), channel_id=1, source_target_pairs={{0,3},{1,2},{2,1},{3,0},{4,7},{5,6},{6,5},{7,4},{8,11},{9,10},{10,... | collective-permute-start | bytes 294920 | tf_op jit(solution)/shard_map/ppermute | solution.py:285
  36.3 1.1 %collective-permute-start.13 = (bf16[16,3072]{1,0:T(8,128)(2,1)S(1)}, bf16[16,3072]{1,0:T(8,128)(2,1)S(1)}, u32[]{:S(2)}, u32[]{:S(2)}) collective-permute-start(bf16[16,3072]{1,0:T(8,128)(2,1)S(1)} %get-tuple-element.50), channel_id=1, source_target_pairs={{0,2},{1,3},{2,0},{3,1},{4,6},{5,7},{6,4},{7,5},{8,10},{9,11},{10,... | collective-permute-start | bytes 294920 | tf_op jit(solution)/shard_map/ppermute | solution.py:285
  37.4 0.1 collective-permute-start.14
  37.6 0.9 %collective-permute-start.15 = (bf16[16,3072]{1,0:T(8,128)(2,1)S(1)}, bf16[16,3072]{1,0:T(8,128)(2,1)S(1)}, u32[]{:S(2)}, u32[]{:S(2)}) collective-permute-start(bf16[16,3072]{1,0:T(8,128)(2,1)S(1)} %get-tuple-element.54), channel_id=1, source_target_pairs={{0,3},{1,2},{2,1},{3,0},{4,7},{5,6},{6,5},{7,4},{8,11},{9,10},{10,... | collective-permute-start | bytes 294920 | tf_op jit(solution)/shard_map/ppermute | solution.py:285
  38.5 1.1 %collective-permute-start.16 = (bf16[16,3072]{1,0:T(8,128)(2,1)S(1)}, bf16[16,3072]{1,0:T(8,128)(2,1)S(1)}, u32[]{:S(2)}, u32[]{:S(2)}) collective-permute-start(bf16[16,3072]{1,0:T(8,128)(2,1)S(1)} %get-tuple-element.55), channel_id=1, source_target_pairs={{0,2},{1,3},{2,0},{3,1},{4,6},{5,7},{6,4},{7,5},{8,10},{9,11},{10,... | collective-permute-start | bytes 294920 | tf_op jit(solution)/shard_map/ppermute | solution.py:285
  39.6 0.9 %collective-permute-done.12.refs_3_ = bf16[16,3072]{1,0:T(8,128)(2,1)S(1)} collective-permute-done((bf16[16,3072]{1,0:T(8,128)(2,1)S(1)}, bf16[16,3072]{1,0:T(8,128)(2,1)S(1)}, u32[]{:S(2)}, u32[]{:S(2)}) %collective-permute-start.12) | collective-permute-done | bytes 98336 | tf_op jit(solution)/shard_map/ppermute | solution.py:285
  40.5 0.4 collective-permute-start.17
  40.9 2.3 %collective-permute-done.13.refs_4_ = bf16[16,3072]{1,0:T(8,128)(2,1)S(1)} collective-permute-done((bf16[16,3072]{1,0:T(8,128)(2,1)S(1)}, bf16[16,3072]{1,0:T(8,128)(2,1)S(1)}, u32[]{:S(2)}, u32[]{:S(2)}) %collective-permute-start.13) | collective-permute-done | bytes 98336 | tf_op jit(solution)/shard_map/ppermute | solution.py:285
  43.2 0.0 collective-permute-done.14.refs_5_
  43.2 0.0 copy-done
  43.2 0.6 %shard_map.114 = (bf16[16,3072]{1,0:T(8,128)(2,1)S(1)}, bf16[16,3072]{1,0:T(8,128)(2,1)S(1)}) custom-call(s32[1]{0:T(128)} %bitcast._.me_ref, bf16[4,3072]{1,0:T(4,128)(2,1)S(1)} %bitcast.16, bf16[16,3200]{1,0:T(8,128)(2,1)S(1)} %collective-permute-done.refs_1_.refs_0_, bf16[16,3200]{1,0:T(8,128)(2,1)S(1)} %collective-permute-done.1.refs_2_.refs_1_, ...), custom_call_target="tpu_custom_call" | custom-call | tf_op jit(solution)/shard_map/pallas_call | solution.py:257
  43.8 2.4 %collective-permute-start.20 = (bf16[16,3072]{1,0:T(8,128)(2,1)S(1)}, bf16[16,3072]{1,0:T(8,128)(2,1)S(1)}, u32[]{:S(2)}, u32[]{:S(2)}) collective-permute-start(bf16[16,3072]{1,0:T(8,128)(2,1)S(1)} %get-tuple-element.60), channel_id=1, source_target_pairs={{0,12},{4,8},{8,4},{12,0},{1,13},{5,9},{9,5},{13,1},{2,14},{6,10},... | collective-permute-start | bytes 294920 | tf_op jit(solution)/shard_map/ppermute | solution.py:285
  46.2 0.0 collective-permute-start.19
  46.2 0.0 collective-permute-done.15.refs_4_
  46.2 0.9 %collective-permute-done.16.refs_5_ = bf16[16,3072]{1,0:T(8,128)(2,1)S(1)} collective-permute-done((bf16[16,3072]{1,0:T(8,128)(2,1)S(1)}, bf16[16,3072]{1,0:T(8,128)(2,1)S(1)}, u32[]{:S(2)}, u32[]{:S(2)}) %collective-permute-start.16) | collective-permute-done | bytes 98336 | tf_op jit(solution)/shard_map/ppermute | solution.py:285
  47.1 0.0 collective-permute-done.17.refs_6_
  47.1 0.6 %shard_map.115 = (f32[16,3072]{1,0:T(8,128)S(1)}, bf16[16,3072]{1,0:T(8,128)(2,1)S(1)}) custom-call(s32[1]{0:T(128)} %bitcast._.me_ref, bf16[4,3072]{1,0:T(4,128)(2,1)S(1)} %bitcast.17, bf16[16,3072]{1,0:T(8,128)(2,1)S(1)} %get-tuple-element.52.refs_0_, bf16[16,3200]{1,0:T(8,128)(2,1)S(1)} %get-tuple-element.33.refs_0_.refs_1_, ...), custom_call_target="tpu_custom_call" | custom-call | tf_op jit(solution)/shard_map/pallas_call | solution.py:257
  47.7 1.2 %collective-permute-start.18 = (bf16[16,3072]{1,0:T(8,128)(2,1)S(1)}, bf16[16,3072]{1,0:T(8,128)(2,1)S(1)}, u32[]{:S(2)}, u32[]{:S(2)}) collective-permute-start(bf16[16,3072]{1,0:T(8,128)(2,1)S(1)} %get-tuple-element.59), channel_id=1, source_target_pairs={{0,4},{4,0},{8,12},{12,8},{1,5},{5,1},{9,13},{13,9},{2,6},{6,2},{1... | collective-permute-start | bytes 294920 | tf_op jit(solution)/shard_map/ppermute | solution.py:285
  48.9 2.2 %collective-permute-done.20.refs_3_ = bf16[16,3072]{1,0:T(8,128)(2,1)S(1)} collective-permute-done((bf16[16,3072]{1,0:T(8,128)(2,1)S(1)}, bf16[16,3072]{1,0:T(8,128)(2,1)S(1)}, u32[]{:S(2)}, u32[]{:S(2)}) %collective-permute-start.20) | collective-permute-done | bytes 98336 | tf_op jit(solution)/shard_map/ppermute | solution.py:285
  51.2 3.0 %collective-permute-done.19.refs_2_ = bf16[16,3072]{1,0:T(8,128)(2,1)S(1)} collective-permute-done((bf16[16,3072]{1,0:T(8,128)(2,1)S(1)}, bf16[16,3072]{1,0:T(8,128)(2,1)S(1)}, u32[]{:S(2)}, u32[]{:S(2)}) %collective-permute-start.19) | collective-permute-done | bytes 98336 | tf_op jit(solution)/shard_map/ppermute | solution.py:285
  54.1 0.8 %collective-permute-done.18.refs_1_ = bf16[16,3072]{1,0:T(8,128)(2,1)S(1)} collective-permute-done((bf16[16,3072]{1,0:T(8,128)(2,1)S(1)}, bf16[16,3072]{1,0:T(8,128)(2,1)S(1)}, u32[]{:S(2)}, u32[]{:S(2)}) %collective-permute-start.18) | collective-permute-done | bytes 98336 | tf_op jit(solution)/shard_map/ppermute | solution.py:285
  54.9 0.7 %shard_map.116 = bf16[16,3072]{1,0:T(8,128)(2,1)} custom-call(f32[16,3072]{1,0:T(8,128)S(1)} %get-tuple-element.58.refs_0_, bf16[16,3072]{1,0:T(8,128)(2,1)S(1)} %collective-permute-done.18.refs_1_, bf16[16,3072]{1,0:T(8,128)(2,1)S(1)} %collective-permute-done.19.refs_2_, bf16[16,3072]{1,0:T(8,128)(2,1)S(1)} %collective-permute-done.20.refs_3_), custom_call_target="tpu_custom_call" | custom-call | tf_op jit(solution)/shard_map/pallas_call | solution.py:388
  (2 shorter events, 0.0 us)
Async XLA Ops:
  4.0 20.7 %slice-start = ((s8[12582912]{0:T(1024)(128)(4,1)}), s8[4194304]{0:T(1024)(128)(4,1)S(1)}, s32[]{:S(2)}) async-start(s8[12582912]{0:T(1024)(128)(4,1)} %bitcast.8), calls=%async_computation | async-start | bytes 8388608
  4.0 20.7 %slice-start.3 = ((s8[12582912]{0:T(1024)(128)(4,1)}), s8[4194304]{0:T(1024)(128)(4,1)S(1)}, s32[]{:S(2)}) async-start(s8[12582912]{0:T(1024)(128)(4,1)} %bitcast.12), calls=%async_computation.3 | async-start | bytes 8388608
  4.0 20.7 %slice-start.1 = ((s8[12582912]{0:T(1024)(128)(4,1)}), s8[4194304]{0:T(1024)(128)(4,1)S(1)}, s32[]{:S(2)}) async-start(s8[12582912]{0:T(1024)(128)(4,1)} %bitcast.8), calls=%async_computation.1 | async-start | bytes 8388608
  4.0 20.7 %slice-start.2 = ((s8[12582912]{0:T(1024)(128)(4,1)}), s8[4194304]{0:T(1024)(128)(4,1)S(1)}, s32[]{:S(2)}) async-start(s8[12582912]{0:T(1024)(128)(4,1)} %bitcast.8), calls=%async_computation.2 | async-start | bytes 8388608
  4.0 20.7 %slice-start.4 = ((s8[12582912]{0:T(1024)(128)(4,1)}), s8[4194304]{0:T(1024)(128)(4,1)S(1)}, s32[]{:S(2)}) async-start(s8[12582912]{0:T(1024)(128)(4,1)} %bitcast.12), calls=%async_computation.4 | async-start | bytes 8388608
  4.1 20.7 %slice-start.5 = ((s8[12582912]{0:T(1024)(128)(4,1)}), s8[4194304]{0:T(1024)(128)(4,1)S(1)}, s32[]{:S(2)}) async-start(s8[12582912]{0:T(1024)(128)(4,1)} %bitcast.12), calls=%async_computation.5 | async-start | bytes 8388608
  4.1 6.0 %collective-permute-start.2 = (bf16[16,3200]{1,0:T(8,128)(2,1)S(1)}, bf16[16,3200]{1,0:T(8,128)(2,1)S(1)}, u32[]{:S(2)}, u32[]{:S(2)}) collective-permute-start(bf16[16,3200]{1,0:T(8,128)(2,1)S(1)} %get-tuple-element.33.refs_0_.refs_1_), channel_id=1, source_target_pairs={{0,4},{4,0},{8,12},{12,8},{1,5},{5,1},{9,13},{13,9},{2,6},{6,2},{1... | collective-permute-start | bytes 307208 | tf_op jit(solution)/shard_map/ppermute | solution.py:285
  7.2 8.4 %collective-permute-start.1 = (bf16[16,3200]{1,0:T(8,128)(2,1)S(1)}, bf16[16,3200]{1,0:T(8,128)(2,1)S(1)}, u32[]{:S(2)}, u32[]{:S(2)}) collective-permute-start(bf16[16,3200]{1,0:T(8,128)(2,1)S(1)} %get-tuple-element.33.refs_0_.refs_1_), channel_id=1, source_target_pairs={{0,12},{4,8},{8,4},{12,0},{1,13},{5,9},{9,5},{13,1},{2,14},{6,10},... | collective-permute-start | bytes 307208 | tf_op jit(solution)/shard_map/ppermute | solution.py:285
  9.6 9.3 %collective-permute-start = (bf16[16,3200]{1,0:T(8,128)(2,1)S(1)}, bf16[16,3200]{1,0:T(8,128)(2,1)S(1)}, u32[]{:S(2)}, u32[]{:S(2)}) collective-permute-start(bf16[16,3200]{1,0:T(8,128)(2,1)S(1)} %get-tuple-element.33.refs_0_.refs_1_), channel_id=1, source_target_pairs={{0,8},{4,12},{8,0},{12,4},{1,9},{5,13},{9,1},{13,5},{2,10},{6,14},... | collective-permute-start | bytes 307208 | tf_op jit(solution)/shard_map/ppermute | solution.py:285
  10.5 8.4 %collective-permute-start.3 = (bf16[16,3072]{1,0:T(8,128)(2,1)S(1)}, bf16[16,3072]{1,0:T(8,128)(2,1)S(1)}, u32[]{:S(2)}, u32[]{:S(2)}) collective-permute-start(bf16[16,3072]{1,0:T(8,128)(2,1)S(1)} %get-tuple-element.35), channel_id=1, source_target_pairs={{0,3},{1,2},{2,1},{3,0},{4,7},{5,6},{6,5},{7,4},{8,11},{9,10},{10,... | collective-permute-start | bytes 294920 | tf_op jit(solution)/shard_map/ppermute | solution.py:285
  10.7 10.7 %collective-permute-start.4 = (bf16[16,3072]{1,0:T(8,128)(2,1)S(1)}, bf16[16,3072]{1,0:T(8,128)(2,1)S(1)}, u32[]{:S(2)}, u32[]{:S(2)}) collective-permute-start(bf16[16,3072]{1,0:T(8,128)(2,1)S(1)} %get-tuple-element.36), channel_id=1, source_target_pairs={{0,2},{1,3},{2,0},{3,1},{4,6},{5,7},{6,4},{7,5},{8,10},{9,11},{10,... | collective-permute-start | bytes 294920 | tf_op jit(solution)/shard_map/ppermute | solution.py:285
  12.4 10.1 %collective-permute-start.5 = (bf16[16,3072]{1,0:T(8,128)(2,1)S(1)}, bf16[16,3072]{1,0:T(8,128)(2,1)S(1)}, u32[]{:S(2)}, u32[]{:S(2)}) collective-permute-start(bf16[16,3072]{1,0:T(8,128)(2,1)S(1)} %get-tuple-element.37), channel_id=1, source_target_pairs={{0,1},{1,0},{2,3},{3,2},{4,5},{5,4},{6,7},{7,6},{8,9},{9,8},{10,11... | collective-permute-start | bytes 294920 | tf_op jit(solution)/shard_map/ppermute | solution.py:285
  19.4 4.1 %collective-permute-start.9 = (bf16[16,1536]{1,0:T(8,128)(2,1)S(1)}, bf16[16,1536]{1,0:T(8,128)(2,1)S(1)}, u32[]{:S(2)}, u32[]{:S(2)}) collective-permute-start(bf16[16,1536]{1,0:T(8,128)(2,1)S(1)} %get-tuple-element.43), channel_id=1, source_target_pairs={{0,3},{1,2},{2,1},{3,0},{4,7},{5,6},{6,5},{7,4},{8,11},{9,10},{10,... | collective-permute-start | bytes 147464 | tf_op jit(solution)/shard_map/ppermute | solution.py:285
  20.1 4.6 %collective-permute-start.10 = (bf16[16,1536]{1,0:T(8,128)(2,1)S(1)}, bf16[16,1536]{1,0:T(8,128)(2,1)S(1)}, u32[]{:S(2)}, u32[]{:S(2)}) collective-permute-start(bf16[16,1536]{1,0:T(8,128)(2,1)S(1)} %get-tuple-element.44), channel_id=1, source_target_pairs={{0,2},{1,3},{2,0},{3,1},{4,6},{5,7},{6,4},{7,5},{8,10},{9,11},{10,... | collective-permute-start | bytes 147464 | tf_op jit(solution)/shard_map/ppermute | solution.py:285
  21.1 3.6 %collective-permute-start.11 = (bf16[16,1536]{1,0:T(8,128)(2,1)S(1)}, bf16[16,1536]{1,0:T(8,128)(2,1)S(1)}, u32[]{:S(2)}, u32[]{:S(2)}) collective-permute-start(bf16[16,1536]{1,0:T(8,128)(2,1)S(1)} %get-tuple-element.45), channel_id=1, source_target_pairs={{0,1},{1,0},{2,3},{3,2},{4,5},{5,4},{6,7},{7,6},{8,9},{9,8},{10,11... | collective-permute-start | bytes 147464 | tf_op jit(solution)/shard_map/ppermute | solution.py:285
  21.3 6.7 %collective-permute-start.6 = (bf16[16,1536]{1,0:T(8,128)(2,1)S(1)}, bf16[16,1536]{1,0:T(8,128)(2,1)S(1)}, u32[]{:S(2)}, u32[]{:S(2)}) collective-permute-start(bf16[16,1536]{1,0:T(8,128)(2,1)S(1)} %get-tuple-element.39), channel_id=1, source_target_pairs={{0,3},{1,2},{2,1},{3,0},{4,7},{5,6},{6,5},{7,4},{8,11},{9,10},{10,... | collective-permute-start | bytes 147464 | tf_op jit(solution)/shard_map/ppermute | solution.py:285
  22.5 5.6 %collective-permute-start.7 = (bf16[16,1536]{1,0:T(8,128)(2,1)S(1)}, bf16[16,1536]{1,0:T(8,128)(2,1)S(1)}, u32[]{:S(2)}, u32[]{:S(2)}) collective-permute-start(bf16[16,1536]{1,0:T(8,128)(2,1)S(1)} %get-tuple-element.40), channel_id=1, source_target_pairs={{0,2},{1,3},{2,0},{3,1},{4,6},{5,7},{6,4},{7,5},{8,10},{9,11},{10,... | collective-permute-start | bytes 147464 | tf_op jit(solution)/shard_map/ppermute | solution.py:285
  23.5 4.6 %collective-permute-start.8 = (bf16[16,1536]{1,0:T(8,128)(2,1)S(1)}, bf16[16,1536]{1,0:T(8,128)(2,1)S(1)}, u32[]{:S(2)}, u32[]{:S(2)}) collective-permute-start(bf16[16,1536]{1,0:T(8,128)(2,1)S(1)} %get-tuple-element.41), channel_id=1, source_target_pairs={{0,1},{1,0},{2,3},{3,2},{4,5},{5,4},{6,7},{7,6},{8,9},{9,8},{10,11... | collective-permute-start | bytes 147464 | tf_op jit(solution)/shard_map/ppermute | solution.py:285
  28.1 15.1 %copy-start = (bf16[3072,4]{0,1:T(4,128)(2,1)S(1)}, bf16[3072,4]{0,1:T(4,128)(2,1)}, u32[]{:S(2)}) copy-start(bf16[3072,4]{0,1:T(4,128)(2,1)} %param.18) | copy-start | bytes 73732
  35.6 4.9 %collective-permute-start.12 = (bf16[16,3072]{1,0:T(8,128)(2,1)S(1)}, bf16[16,3072]{1,0:T(8,128)(2,1)S(1)}, u32[]{:S(2)}, u32[]{:S(2)}) collective-permute-start(bf16[16,3072]{1,0:T(8,128)(2,1)S(1)} %get-tuple-element.49), channel_id=1, source_target_pairs={{0,3},{1,2},{2,1},{3,0},{4,7},{5,6},{6,5},{7,4},{8,11},{9,10},{10,... | collective-permute-start | bytes 294920 | tf_op jit(solution)/shard_map/ppermute | solution.py:285
  36.3 6.8 %collective-permute-start.13 = (bf16[16,3072]{1,0:T(8,128)(2,1)S(1)}, bf16[16,3072]{1,0:T(8,128)(2,1)S(1)}, u32[]{:S(2)}, u32[]{:S(2)}) collective-permute-start(bf16[16,3072]{1,0:T(8,128)(2,1)S(1)} %get-tuple-element.50), channel_id=1, source_target_pairs={{0,2},{1,3},{2,0},{3,1},{4,6},{5,7},{6,4},{7,5},{8,10},{9,11},{10,... | collective-permute-start | bytes 294920 | tf_op jit(solution)/shard_map/ppermute | solution.py:285
  37.4 5.8 %collective-permute-start.14 = (bf16[16,3072]{1,0:T(8,128)(2,1)S(1)}, bf16[16,3072]{1,0:T(8,128)(2,1)S(1)}, u32[]{:S(2)}, u32[]{:S(2)}) collective-permute-start(bf16[16,3072]{1,0:T(8,128)(2,1)S(1)} %get-tuple-element.51), channel_id=1, source_target_pairs={{0,1},{1,0},{2,3},{3,2},{4,5},{5,4},{6,7},{7,6},{8,9},{9,8},{10,11... | collective-permute-start | bytes 294920 | tf_op jit(solution)/shard_map/ppermute | solution.py:285
  37.6 8.6 %collective-permute-start.15 = (bf16[16,3072]{1,0:T(8,128)(2,1)S(1)}, bf16[16,3072]{1,0:T(8,128)(2,1)S(1)}, u32[]{:S(2)}, u32[]{:S(2)}) collective-permute-start(bf16[16,3072]{1,0:T(8,128)(2,1)S(1)} %get-tuple-element.54), channel_id=1, source_target_pairs={{0,3},{1,2},{2,1},{3,0},{4,7},{5,6},{6,5},{7,4},{8,11},{9,10},{10,... | collective-permute-start | bytes 294920 | tf_op jit(solution)/shard_map/ppermute | solution.py:285
  38.5 8.6 %collective-permute-start.16 = (bf16[16,3072]{1,0:T(8,128)(2,1)S(1)}, bf16[16,3072]{1,0:T(8,128)(2,1)S(1)}, u32[]{:S(2)}, u32[]{:S(2)}) collective-permute-start(bf16[16,3072]{1,0:T(8,128)(2,1)S(1)} %get-tuple-element.55), channel_id=1, source_target_pairs={{0,2},{1,3},{2,0},{3,1},{4,6},{5,7},{6,4},{7,5},{8,10},{9,11},{10,... | collective-permute-start | bytes 294920 | tf_op jit(solution)/shard_map/ppermute | solution.py:285
  40.5 6.6 %collective-permute-start.17 = (bf16[16,3072]{1,0:T(8,128)(2,1)S(1)}, bf16[16,3072]{1,0:T(8,128)(2,1)S(1)}, u32[]{:S(2)}, u32[]{:S(2)}) collective-permute-start(bf16[16,3072]{1,0:T(8,128)(2,1)S(1)} %get-tuple-element.56), channel_id=1, source_target_pairs={{0,1},{1,0},{2,3},{3,2},{4,5},{5,4},{6,7},{7,6},{8,9},{9,8},{10,11... | collective-permute-start | bytes 294920 | tf_op jit(solution)/shard_map/ppermute | solution.py:285
  43.8 7.4 %collective-permute-start.20 = (bf16[16,3072]{1,0:T(8,128)(2,1)S(1)}, bf16[16,3072]{1,0:T(8,128)(2,1)S(1)}, u32[]{:S(2)}, u32[]{:S(2)}) collective-permute-start(bf16[16,3072]{1,0:T(8,128)(2,1)S(1)} %get-tuple-element.60), channel_id=1, source_target_pairs={{0,12},{4,8},{8,4},{12,0},{1,13},{5,9},{9,5},{13,1},{2,14},{6,10},... | collective-permute-start | bytes 294920 | tf_op jit(solution)/shard_map/ppermute | solution.py:285
  46.2 8.0 %collective-permute-start.19 = (bf16[16,3072]{1,0:T(8,128)(2,1)S(1)}, bf16[16,3072]{1,0:T(8,128)(2,1)S(1)}, u32[]{:S(2)}, u32[]{:S(2)}) collective-permute-start(bf16[16,3072]{1,0:T(8,128)(2,1)S(1)} %get-tuple-element.52.refs_0_), channel_id=1, source_target_pairs={{0,8},{4,12},{8,0},{12,4},{1,9},{5,13},{9,1},{13,5},{2,10},{6,14},... | collective-permute-start | bytes 294920 | tf_op jit(solution)/shard_map/ppermute | solution.py:285
  47.7 7.2 %collective-permute-start.18 = (bf16[16,3072]{1,0:T(8,128)(2,1)S(1)}, bf16[16,3072]{1,0:T(8,128)(2,1)S(1)}, u32[]{:S(2)}, u32[]{:S(2)}) collective-permute-start(bf16[16,3072]{1,0:T(8,128)(2,1)S(1)} %get-tuple-element.59), channel_id=1, source_target_pairs={{0,4},{4,0},{8,12},{12,8},{1,5},{5,1},{9,13},{13,9},{2,6},{6,2},{1... | collective-permute-start | bytes 294920 | tf_op jit(solution)/shard_map/ppermute | solution.py:285

commit v9 on v8

--- a/solution.py
+++ b/solution.py
@@ -13,7 +13,7 @@
 CAP = 8
 LANES = 128
 PAIR = 2
-STRIPS = 6
+STRIPS = 3
 MIB = 1 << 20
 F32 = jnp.float32
 BF16 = jnp.bfloat16
@@ -165,6 +165,22 @@
     payload_ref[:, width:] = named.astype(BF16)
 
 
+def pass_kernel(after_ref, value_ref, out_ref):
+    pass
+
+
+def pass_on(after, value):
+    return pl.pallas_call(
+        pass_kernel,
+        in_specs=[ANY, ANY],
+        out_specs=ANY,
+        out_shape=jax.ShapeDtypeStruct(value.shape, value.dtype),
+        input_output_aliases={1: 0},
+        cost_estimate=LIGHT,
+        compiler_params=params(0),
+    )(after, value)
+
+
 def split_kernel(me_ref, *refs, chunks, experts, after):
     refs = refs[after:]
     payload = jnp.concatenate([ref[...] for ref in refs[:chunks]], axis=0)
@@ -178,9 +194,25 @@
         ref[...] = slots[e * span : (e + 1) * span, p * part : (p + 1) * part].astype(BF16)
 
 
+def strip_copies(source, begin, target, sems):
+    strip = target.shape[1] // sems.shape[0]
+    copies = [
+        pltpu.make_async_copy(
+            source.at[:, pl.ds(begin + c * strip, strip)],
+            target.at[:, pl.ds(c * strip, strip)],
+            sems.at[c],
+        )
+        for c in range(sems.shape[0])
+    ]
+    for copy in copies:
+        copy.start()
+    return copies
+
+
 def begin_kernel(*refs, near, far):
-    gate_ref, up_ref, gate_out, up_out, rows_ref = refs[near + far :]
+    gate_ref, up_ref, down_hbm, gate_out, up_out, down_out, rows_ref, sems = refs[near + far :]
     half = rows_ref.shape[1]
+    copies = strip_copies(down_hbm, 0, down_out, sems)
     blocks = [ref[:, :half] for ref in refs[:near]] + [ref[...] for ref in refs[near : near + far]]
     rows_ref[...] = jnp.concatenate([block.astype(F32) for block in blocks], axis=0).astype(BF16)
     units = gate_ref.shape[1]
@@ -192,19 +224,17 @@
         gate_out[:, at] = dot(rows_ref[...], gate_ref[:half, at])
         up_out[:, at] = dot(rows_ref[...], up_ref[:half, at])
 
+    for copy in copies:
+        copy.wait()
+
 
 def end_kernel(*refs, near, far):
-    gate_in, up_in, gate_ref, up_ref, down_hbm = refs[near + far : near + far + 5]
-    outs = refs[near + far + 5 : -4]
+    gate_in, up_in, down_in, gate_ref, up_ref, down_hbm = refs[near + far : near + far + 6]
+    outs = refs[near + far + 6 : -4]
     rows_ref, hidden_ref, down_ref, sems = refs[-4:]
     half = rows_ref.shape[1]
     width, units = gate_ref.shape
-    strip = width // sems.shape[0]
-    copies = []
-    for c in range(sems.shape[0]):
-        at = pl.ds(c * strip, strip)
-        copies.append(pltpu.make_async_copy(down_hbm.at[:, at], down_ref.at[:, at], sems.at[c]))
-        copies[-1].start()
+    copies = strip_copies(down_hbm, half, down_ref, sems)
     blocks = [ref[:, half:] for ref in refs[:near]] + [ref[...] for ref in refs[near : near + far]]
     rows_ref[...] = jnp.concatenate([block.astype(F32) for block in blocks], axis=0).astype(BF16)
     tile = min(256, units)
@@ -216,18 +246,22 @@
         up = up_in[:, at] + dot(rows_ref[...], up_ref[half:, at])
         hidden_ref[:, at] = (jax.nn.silu(gate) * up).astype(BF16)
 
+    def down(source, begin, first, columns):
+        @pl.loop(0, columns // tile)
+        def _(i):
+            at = pl.multiple_of(i * tile, tile)
+            out = dot(hidden_ref[...], source[:, pl.ds(first + at, tile)])
+            row = 0
+            for ref in outs:
+                count = ref.shape[0]
+                ref[:, pl.ds(begin + first + at, tile)] = out[row : row + count].astype(BF16)
+                row += count
+
+    strip = half // len(copies)
+    down(down_in, 0, 0, half)
     for c, copy in enumerate(copies):
         copy.wait()
-
-        @pl.loop(0, strip // tile)
-        def _(i):
-            at = pl.ds(pl.multiple_of(c * strip + i * tile, tile), tile)
-            out = dot(hidden_ref[...], down_ref[:, at])
-            begin = 0
-            for ref in outs:
-                count = ref.shape[0]
-                ref[:, at] = out[begin : begin + count].astype(BF16)
-                begin += count
+        down(down_ref, half, c * strip, strip)
 
 
 def mix_kernel(me_ref, router_ref, *refs, chunks, experts, after):
@@ -332,7 +366,7 @@
         cost_estimate=LIGHT,
     )(me, *operands)
 
-    chunks = [swap(payload, "attn", j) for j in range(layers)]
+    chunks = [swap(payload, "attn", j) if j < 2 or j % 2 == 0 else None for j in range(layers)]
     groups = [[0, 1], list(range(2, layers))]
     half = width // 2
     order = farthest_first(experts)
@@ -352,33 +386,35 @@
         ]
 
     near = send(groups[0], width, [])
+    for j in range(3, layers, 2):
+        chunks[j] = swap(pass_on(near[1], chunks[j - 1]), "attn", 1)
     far = send(groups[1], half, near[1:2])
     total_rows = sum(block.shape[0] for block in near + far[:experts])
     units = gate_proj.shape[2]
     counts = {"near": experts, "far": experts}
     sums = pl.pallas_call(
         functools.partial(begin_kernel, **counts),
-        in_specs=[WHOLE] * (2 * experts + 2),
-        out_specs=[WHOLE] * 2,
-        out_shape=[shape((total_rows, units), F32)] * 2,
-        scratch_shapes=[pltpu.VMEM((total_rows, half), BF16)],
+        in_specs=[WHOLE] * (2 * experts + 2) + [ANY],
+        out_specs=[WHOLE] * 3,
+        out_shape=[shape((total_rows, units), F32)] * 2 + [pltpu.VMEM((units, half), BF16)],
+        scratch_shapes=[pltpu.VMEM((total_rows, half), BF16), pltpu.SemaphoreType.DMA((STRIPS,))],
         cost_estimate=pl.CostEstimate(
             flops=4 * total_rows * half * units, bytes_accessed=0, transcendentals=0
         ),
         compiler_params=params(total_rows * width),
-    )(*near, *far[:experts], gate_proj[0], up_proj[0])
+    )(*near, *far[:experts], gate_proj[0], up_proj[0], in_hbm(down_proj[0]))
     results = pl.pallas_call(
         functools.partial(end_kernel, **counts),
-        in_specs=[WHOLE] * (2 * experts + 4) + [ANY],
+        in_specs=[WHOLE] * (2 * experts + 5) + [ANY],
         out_specs=[WHOLE] * (2 * experts),
         out_shape=[shape((block.shape[0], width), BF16) for block in near + far[:experts]],
         scratch_shapes=[
             pltpu.VMEM((total_rows, half), BF16),
             pltpu.VMEM((total_rows, units), BF16),
-            pltpu.VMEM((units, width), BF16),
+            pltpu.VMEM((units, half), BF16),
             pltpu.SemaphoreType.DMA((STRIPS,)),
         ],
-        compiler_params=params(total_rows * width + units * width // 5),
+        compiler_params=params(total_rows * width + units * half // 5),
     )(*near, *far[experts:], *sums, gate_proj[0], up_proj[0], in_hbm(down_proj[0]))
 
     near, far = results[:experts], results[experts:]

time: 55.8 us -> 58.3 us (1.045)
  starting transfers between devices: 19.5 us -> 21.8 us
    ppermute x21, starting transfers between devices: 19.5 us -> 21.8 us  [swap(): return lax.ppermute(value, axis, [(i, i ^ step) for i in range(count)])]
  transfers between devices with their start and end apart: 21 -> 21, of which waited for: 11 -> 10; matrix products, arithmetic and copies ran while one was open for 0% -> 0% of each run, Pallas kernels for 10% -> 9%
where the time goes in v9:
time: 58.3 us; the launch traced here: 58.1 us
  starting transfers between devices  21.8 us (37%)
  waiting for transfers between devices  18.6 us (32%)
  Pallas kernels  17.5 us (30%)
    ppermute x21, starting transfers between devices, swap(): return lax.ppermute(value, axis, [(i, i ^ step) for i in range(count)])  21.8 us
    ppermute x21, waiting for transfers between devices, swap(): return lax.ppermute(value, axis, [(i, i ^ step) for i in range(count)])  18.6 us
    pallas_call x1, Pallas kernels, shards(): pl.pallas_call(functools.partial(end_kernel, **counts), in_specs=[WHOLE]...  7.32 us
    pallas_call x1, Pallas kernels, shards(): pl.pallas_call(attend_kernel, in_specs=[SCALAR] + [ANY] * len(operands),...  3.99 us
    pallas_call x1, Pallas kernels, shards(): pl.pallas_call(functools.partial(begin_kernel, **counts), in_specs=[WHOLE...  3.31 us
    pallas_call x2, Pallas kernels, mix(): pl.pallas_call(functools.partial(mix_kernel, chunks=chunks, experts=exper...  1.23 us
  transfers between devices with their start and end apart: 21, of which 10 were waited for; matrix products, arithmetic and copies ran while one was open for 0% of the time, Pallas kernels for 9%

profile of v9, /device:TPU:0, one launch (start us, length us, event | category | flops | bytes accessed | tf_op | source)
XLA Modules:
  0.0 58.1 jit_solution(12670270210675309897)
XLA Ops:
  0.0 4.0 %shard_map.109 = (f32[16,3072]{1,0:T(8,128)S(1)}, bf16[16,3200]{1,0:T(8,128)(2,1)S(1)}) custom-call(s32[1]{0:T(128)} %bitcast._.me_ref, s32[1,16]{1,0:T(1,128)} %bitcast.22, bf16[16,3072]{1,0:T(8,128)(2,1)} %queries_hbm.1, bf16[16,96,512]{2,1,0:T(8,128)(2,1)} %keys_hbm.1, bf16[16,96,512]{2,1,0:T(8,128)(2,1)} %values_hbm.1, s32[2,16]{1,0:T(2,128)} %bitcast.21, ...), custom_call_target="tpu_custom_call" | custom-call | tf_op jit(solution)/shard_map/pallas_call | solution.py:358
  4.0 0.0 slice-start
  4.0 0.0 slice-start.3
  4.0 0.0 slice-start.1
  4.0 0.0 slice-start.2
  4.0 0.0 slice-start.4
  4.1 0.0 slice-start.5
  4.1 3.1 %collective-permute-start.1 = (bf16[16,3200]{1,0:T(8,128)(2,1)S(1)}, bf16[16,3200]{1,0:T(8,128)(2,1)S(1)}, u32[]{:S(2)}, u32[]{:S(2)}) collective-permute-start(bf16[16,3200]{1,0:T(8,128)(2,1)S(1)} %get-tuple-element.34.refs_0_.refs_1_), channel_id=1, source_target_pairs={{0,4},{4,0},{8,12},{12,8},{1,5},{5,1},{9,13},{13,9},{2,6},{6,2},{1... | collective-permute-start | bytes 307208 | tf_op jit(solution)/shard_map/ppermute | solution.py:319
  7.2 2.6 %collective-permute-start = (bf16[16,3200]{1,0:T(8,128)(2,1)S(1)}, bf16[16,3200]{1,0:T(8,128)(2,1)S(1)}, u32[]{:S(2)}, u32[]{:S(2)}) collective-permute-start(bf16[16,3200]{1,0:T(8,128)(2,1)S(1)} %get-tuple-element.34.refs_0_.refs_1_), channel_id=1, source_target_pairs={{0,8},{4,12},{8,0},{12,4},{1,9},{5,13},{9,1},{13,5},{2,10},{6,14},... | collective-permute-start | bytes 307208 | tf_op jit(solution)/shard_map/ppermute | solution.py:319
  9.7 0.3 collective-permute-done.1.refs_1_.refs_2_
  10.0 0.5 shard_map.110
  10.5 0.2 collective-permute-start.2
  10.7 4.0 %collective-permute-done.refs_1_.refs_0_ = bf16[16,3200]{1,0:T(8,128)(2,1)S(1)} collective-permute-done((bf16[16,3200]{1,0:T(8,128)(2,1)S(1)}, bf16[16,3200]{1,0:T(8,128)(2,1)S(1)}, u32[]{:S(2)}, u32[]{:S(2)}) %collective-permute-start) | collective-permute-done | bytes 102432 | tf_op jit(solution)/shard_map/ppermute | solution.py:319
  14.6 0.8 %collective-permute-done.2.after_ref.refs_0_.refs_1_ = bf16[16,3072]{1,0:T(8,128)(2,1)S(1)} collective-permute-done((bf16[16,3072]{1,0:T(8,128)(2,1)S(1)}, bf16[16,3072]{1,0:T(8,128)(2,1)S(1)}, u32[]{:S(2)}, u32[]{:S(2)}) %collective-permute-start.2) | collective-permute-done | bytes 98336 | tf_op jit(solution)/shard_map/ppermute | solution.py:319
  15.4 2.0 %collective-permute-start.3 = (bf16[16,3200]{1,0:T(8,128)(2,1)S(1)}, bf16[16,3200]{1,0:T(8,128)(2,1)S(1)}, u32[]{:S(2)}, u32[]{:S(2)}) collective-permute-start(bf16[16,3200]{1,0:T(8,128)(2,1)S(1)} %shard_map.111), channel_id=1, source_target_pairs={{0,4},{4,0},{8,12},{12,8},{1,5},{5,1},{9,13},{13,9},{2,6},{6,2},{1... | collective-permute-start | bytes 307208 | tf_op jit(solution)/shard_map/ppermute | solution.py:319
  17.4 0.6 %collective-permute-start.4 = (bf16[16,3072]{1,0:T(8,128)(2,1)S(1)}, bf16[16,3072]{1,0:T(8,128)(2,1)S(1)}, u32[]{:S(2)}, u32[]{:S(2)}) collective-permute-start(bf16[16,3072]{1,0:T(8,128)(2,1)S(1)} %get-tuple-element.37), channel_id=1, source_target_pairs={{0,2},{1,3},{2,0},{3,1},{4,6},{5,7},{6,4},{7,5},{8,10},{9,11},{10,... | collective-permute-start | bytes 294920 | tf_op jit(solution)/shard_map/ppermute | solution.py:319
  18.0 0.0 collective-permute-start.5
  18.0 2.5 %collective-permute-done.3.refs_2_.refs_1_ = bf16[16,3200]{1,0:T(8,128)(2,1)S(1)} collective-permute-done((bf16[16,3200]{1,0:T(8,128)(2,1)S(1)}, bf16[16,3200]{1,0:T(8,128)(2,1)S(1)}, u32[]{:S(2)}, u32[]{:S(2)}) %collective-permute-start.3) | collective-permute-done | bytes 102432 | tf_op jit(solution)/shard_map/ppermute | solution.py:319
  20.6 0.5 shard_map.112
  21.1 0.1 collective-permute-start.9
  21.1 1.2 %collective-permute-start.10 = (bf16[16,1536]{1,0:T(8,128)(2,1)S(1)}, bf16[16,1536]{1,0:T(8,128)(2,1)S(1)}, u32[]{:S(2)}, u32[]{:S(2)}) collective-permute-start(bf16[16,1536]{1,0:T(8,128)(2,1)S(1)} %get-tuple-element.45), channel_id=1, source_target_pairs={{0,2},{1,3},{2,0},{3,1},{4,6},{5,7},{6,4},{7,5},{8,10},{9,11},{10,... | collective-permute-start | bytes 147464 | tf_op jit(solution)/shard_map/ppermute | solution.py:319
  22.3 0.6 %collective-permute-start.11 = (bf16[16,1536]{1,0:T(8,128)(2,1)S(1)}, bf16[16,1536]{1,0:T(8,128)(2,1)S(1)}, u32[]{:S(2)}, u32[]{:S(2)}) collective-permute-start(bf16[16,1536]{1,0:T(8,128)(2,1)S(1)} %get-tuple-element.46), channel_id=1, source_target_pairs={{0,1},{1,0},{2,3},{3,2},{4,5},{5,4},{6,7},{7,6},{8,9},{9,8},{10,11... | collective-permute-start | bytes 147464 | tf_op jit(solution)/shard_map/ppermute | solution.py:319
  23.0 0.0 collective-permute-done.4.refs_2_
  23.0 0.4 collective-permute-start.6
  23.3 0.0 collective-permute-done.5.refs_3_
  23.4 1.3 %collective-permute-start.7 = (bf16[16,1536]{1,0:T(8,128)(2,1)S(1)}, bf16[16,1536]{1,0:T(8,128)(2,1)S(1)}, u32[]{:S(2)}, u32[]{:S(2)}) collective-permute-start(bf16[16,1536]{1,0:T(8,128)(2,1)S(1)} %get-tuple-element.41), channel_id=1, source_target_pairs={{0,2},{1,3},{2,0},{3,1},{4,6},{5,7},{6,4},{7,5},{8,10},{9,11},{10,... | collective-permute-start | bytes 147464 | tf_op jit(solution)/shard_map/ppermute | solution.py:319
  24.6 0.5 collective-permute-done.9.refs_5_
  25.1 0.0 collective-permute-start.8
  25.1 0.6 %collective-permute-done.10.refs_6_ = bf16[16,1536]{1,0:T(8,128)(2,1)S(1)} collective-permute-done((bf16[16,1536]{1,0:T(8,128)(2,1)S(1)}, bf16[16,1536]{1,0:T(8,128)(2,1)S(1)}, u32[]{:S(2)}, u32[]{:S(2)}) %collective-permute-start.10) | collective-permute-done | bytes 49184 | tf_op jit(solution)/shard_map/ppermute | solution.py:319
  25.8 0.0 collective-permute-done.11.refs_7_
  25.8 0.0 slice-done
  25.8 0.0 slice-done.3
  25.8 0.0 slice-done.1
  25.8 0.0 slice-done.2
  25.8 0.0 slice-done.4
  25.8 0.0 slice-done.5
  25.8 3.3 %shard_map.113 = (f32[128,2048]{1,0:T(8,128)S(1)}, f32[128,2048]{1,0:T(8,128)S(1)}, bf16[2048,1536]{1,0:T(8,128)(2,1)S(1)}) custom-call(bf16[16,3072]{1,0:T(8,128)(2,1)S(1)} %get-tuple-element.36.refs_0_, bf16[16,3072]{1,0:T(8,128)(2,1)S(1)} %collective-permute-done.2.after_ref.refs_0_.refs_1_, bf16[16,3072]{1,0:T(8,128)(2,1)S(1)} %collective-permute-done.4.refs_2_, ...), custom_call_target="tpu_custom_call" | custom-call | flops 1610612736 | tf_op jit(solution)/shard_map/pallas_call | solution.py:395
  29.2 0.0 collective-permute-done.6.refs_5_
  29.2 0.0 collective-permute-done.7.refs_6_
  29.2 0.0 collective-permute-done.8.refs_7_
  29.2 0.0 copy-start
  29.2 7.3 %shard_map.114 = (bf16[16,3072]{1,0:T(8,128)(2,1)S(1)}, bf16[16,3072]{1,0:T(8,128)(2,1)S(1)}, bf16[16,3072]{1,0:T(8,128)(2,1)S(1)}, bf16[16,3072]{1,0:T(8,128)(2...) custom-call(bf16[16,3072]{1,0:T(8,128)(2,1)S(1)} %get-tuple-element., ...), custom_call_target="tpu_custom_call" | custom-call | tf_op jit(solution)/shard_map/pallas_call | solution.py:406
  36.5 0.9 %collective-permute-start.12 = (bf16[16,3072]{1,0:T(8,128)(2,1)S(1)}, bf16[16,3072]{1,0:T(8,128)(2,1)S(1)}, u32[]{:S(2)}, u32[]{:S(2)}) collective-permute-start(bf16[16,3072]{1,0:T(8,128)(2,1)S(1)} %get-tuple-element.51), channel_id=1, source_target_pairs={{0,3},{1,2},{2,1},{3,0},{4,7},{5,6},{6,5},{7,4},{8,11},{9,10},{10,... | collective-permute-start | bytes 294920 | tf_op jit(solution)/shard_map/ppermute | solution.py:319
  37.4 0.9 %collective-permute-start.13 = (bf16[16,3072]{1,0:T(8,128)(2,1)S(1)}, bf16[16,3072]{1,0:T(8,128)(2,1)S(1)}, u32[]{:S(2)}, u32[]{:S(2)}) collective-permute-start(bf16[16,3072]{1,0:T(8,128)(2,1)S(1)} %get-tuple-element.52), channel_id=1, source_target_pairs={{0,2},{1,3},{2,0},{3,1},{4,6},{5,7},{6,4},{7,5},{8,10},{9,11},{10,... | collective-permute-start | bytes 294920 | tf_op jit(solution)/shard_map/ppermute | solution.py:319
  38.3 0.1 collective-permute-start.14
  38.5 1.1 %collective-permute-start.15 = (bf16[16,3072]{1,0:T(8,128)(2,1)S(1)}, bf16[16,3072]{1,0:T(8,128)(2,1)S(1)}, u32[]{:S(2)}, u32[]{:S(2)}) collective-permute-start(bf16[16,3072]{1,0:T(8,128)(2,1)S(1)} %get-tuple-element.56), channel_id=1, source_target_pairs={{0,3},{1,2},{2,1},{3,0},{4,7},{5,6},{6,5},{7,4},{8,11},{9,10},{10,... | collective-permute-start | bytes 294920 | tf_op jit(solution)/shard_map/ppermute | solution.py:319
  39.6 0.9 %collective-permute-start.16 = (bf16[16,3072]{1,0:T(8,128)(2,1)S(1)}, bf16[16,3072]{1,0:T(8,128)(2,1)S(1)}, u32[]{:S(2)}, u32[]{:S(2)}) collective-permute-start(bf16[16,3072]{1,0:T(8,128)(2,1)S(1)} %get-tuple-element.57), channel_id=1, source_target_pairs={{0,2},{1,3},{2,0},{3,1},{4,6},{5,7},{6,4},{7,5},{8,10},{9,11},{10,... | collective-permute-start | bytes 294920 | tf_op jit(solution)/shard_map/ppermute | solution.py:319
  40.5 0.9 %collective-permute-done.12.refs_3_ = bf16[16,3072]{1,0:T(8,128)(2,1)S(1)} collective-permute-done((bf16[16,3072]{1,0:T(8,128)(2,1)S(1)}, bf16[16,3072]{1,0:T(8,128)(2,1)S(1)}, u32[]{:S(2)}, u32[]{:S(2)}) %collective-permute-start.12) | collective-permute-done | bytes 98336 | tf_op jit(solution)/shard_map/ppermute | solution.py:319
  41.4 0.4 collective-permute-start.17
  41.8 2.3 %collective-permute-done.13.refs_4_ = bf16[16,3072]{1,0:T(8,128)(2,1)S(1)} collective-permute-done((bf16[16,3072]{1,0:T(8,128)(2,1)S(1)}, bf16[16,3072]{1,0:T(8,128)(2,1)S(1)}, u32[]{:S(2)}, u32[]{:S(2)}) %collective-permute-start.13) | collective-permute-done | bytes 98336 | tf_op jit(solution)/shard_map/ppermute | solution.py:319
  44.1 0.0 collective-permute-done.14.refs_5_
  44.1 0.0 copy-done
  44.1 0.6 %shard_map.115 = (bf16[16,3072]{1,0:T(8,128)(2,1)S(1)}, bf16[16,3072]{1,0:T(8,128)(2,1)S(1)}) custom-call(s32[1]{0:T(128)} %bitcast._.me_ref, bf16[4,3072]{1,0:T(4,128)(2,1)S(1)} %bitcast.16, bf16[16,3200]{1,0:T(8,128)(2,1)S(1)} %collective-permute-done.refs_1_.refs_0_, bf16[16,3200]{1,0:T(8,128)(2,1)S(1)} %collective-permute-done.3.refs_2_.refs_1_, ...), custom_call_target="tpu_custom_call" | custom-call | tf_op jit(solution)/shard_map/pallas_call | solution.py:291
  44.7 4.8 %collective-permute-start.20 = (bf16[16,3072]{1,0:T(8,128)(2,1)S(1)}, bf16[16,3072]{1,0:T(8,128)(2,1)S(1)}, u32[]{:S(2)}, u32[]{:S(2)}) collective-permute-start(bf16[16,3072]{1,0:T(8,128)(2,1)S(1)} %get-tuple-element.62), channel_id=1, source_target_pairs={{0,12},{4,8},{8,4},{12,0},{1,13},{5,9},{9,5},{13,1},{2,14},{6,10},... | collective-permute-start | bytes 294920 | tf_op jit(solution)/shard_map/ppermute | solution.py:319
  49.5 0.0 collective-permute-start.19
  49.5 0.0 collective-permute-done.15.refs_4_
  49.5 0.0 collective-permute-done.16.refs_5_
  49.5 0.0 collective-permute-done.17.refs_6_
  49.5 0.6 %shard_map.116 = (f32[16,3072]{1,0:T(8,128)S(1)}, bf16[16,3072]{1,0:T(8,128)(2,1)S(1)}) custom-call(s32[1]{0:T(128)} %bitcast._.me_ref, bf16[4,3072]{1,0:T(4,128)(2,1)S(1)} %bitcast.17, bf16[16,3072]{1,0:T(8,128)(2,1)S(1)} %get-tuple-element.54.refs_0_, bf16[16,3200]{1,0:T(8,128)(2,1)S(1)} %get-tuple-element.34.refs_0_.refs_1_, ...), custom_call_target="tpu_custom_call" | custom-call | tf_op jit(solution)/shard_map/pallas_call | solution.py:291
  50.1 0.7 %collective-permute-start.18 = (bf16[16,3072]{1,0:T(8,128)(2,1)S(1)}, bf16[16,3072]{1,0:T(8,128)(2,1)S(1)}, u32[]{:S(2)}, u32[]{:S(2)}) collective-permute-start(bf16[16,3072]{1,0:T(8,128)(2,1)S(1)} %get-tuple-element.61), channel_id=1, source_target_pairs={{0,4},{4,0},{8,12},{12,8},{1,5},{5,1},{9,13},{13,9},{2,6},{6,2},{1... | collective-permute-start | bytes 294920 | tf_op jit(solution)/shard_map/ppermute | solution.py:319
  50.8 2.3 %collective-permute-done.20.refs_3_ = bf16[16,3072]{1,0:T(8,128)(2,1)S(1)} collective-permute-done((bf16[16,3072]{1,0:T(8,128)(2,1)S(1)}, bf16[16,3072]{1,0:T(8,128)(2,1)S(1)}, u32[]{:S(2)}, u32[]{:S(2)}) %collective-permute-start.20) | collective-permute-done | bytes 98336 | tf_op jit(solution)/shard_map/ppermute | solution.py:319
  53.1 4.3 %collective-permute-done.19.refs_2_ = bf16[16,3072]{1,0:T(8,128)(2,1)S(1)} collective-permute-done((bf16[16,3072]{1,0:T(8,128)(2,1)S(1)}, bf16[16,3072]{1,0:T(8,128)(2,1)S(1)}, u32[]{:S(2)}, u32[]{:S(2)}) %collective-permute-start.19) | collective-permute-done | bytes 98336 | tf_op jit(solution)/shard_map/ppermute | solution.py:319
  57.4 0.0 collective-permute-done.18.refs_1_
  57.4 0.7 %shard_map.117 = bf16[16,3072]{1,0:T(8,128)(2,1)} custom-call(f32[16,3072]{1,0:T(8,128)S(1)} %get-tuple-element.60.refs_0_, bf16[16,3072]{1,0:T(8,128)(2,1)S(1)} %collective-permute-done.18.refs_1_, bf16[16,3072]{1,0:T(8,128)(2,1)S(1)} %collective-permute-done.19.refs_2_, bf16[16,3072]{1,0:T(8,128)(2,1)S(1)} %collective-permute-done.20.refs_3_), custom_call_target="tpu_custom_call" | custom-call | tf_op jit(solution)/shard_map/pallas_call | solution.py:424
  (4 shorter events, 0.0 us)
Async XLA Ops:
  4.0 21.8 %slice-start = ((s8[12582912]{0:T(1024)(128)(4,1)}), s8[4194304]{0:T(1024)(128)(4,1)S(1)}, s32[]{:S(2)}) async-start(s8[12582912]{0:T(1024)(128)(4,1)} %bitcast.8), calls=%async_computation | async-start | bytes 8388608
  4.0 21.8 %slice-start.3 = ((s8[12582912]{0:T(1024)(128)(4,1)}), s8[4194304]{0:T(1024)(128)(4,1)S(1)}, s32[]{:S(2)}) async-start(s8[12582912]{0:T(1024)(128)(4,1)} %bitcast.12), calls=%async_computation.3 | async-start | bytes 8388608
  4.0 21.8 %slice-start.1 = ((s8[12582912]{0:T(1024)(128)(4,1)}), s8[4194304]{0:T(1024)(128)(4,1)S(1)}, s32[]{:S(2)}) async-start(s8[12582912]{0:T(1024)(128)(4,1)} %bitcast.8), calls=%async_computation.1 | async-start | bytes 8388608
  4.0 21.8 %slice-start.2 = ((s8[12582912]{0:T(1024)(128)(4,1)}), s8[4194304]{0:T(1024)(128)(4,1)S(1)}, s32[]{:S(2)}) async-start(s8[12582912]{0:T(1024)(128)(4,1)} %bitcast.8), calls=%async_computation.2 | async-start | bytes 8388608
  4.0 21.8 %slice-start.4 = ((s8[12582912]{0:T(1024)(128)(4,1)}), s8[4194304]{0:T(1024)(128)(4,1)S(1)}, s32[]{:S(2)}) async-start(s8[12582912]{0:T(1024)(128)(4,1)} %bitcast.12), calls=%async_computation.4 | async-start | bytes 8388608
  4.1 21.8 %slice-start.5 = ((s8[12582912]{0:T(1024)(128)(4,1)}), s8[4194304]{0:T(1024)(128)(4,1)S(1)}, s32[]{:S(2)}) async-start(s8[12582912]{0:T(1024)(128)(4,1)} %bitcast.12), calls=%async_computation.5 | async-start | bytes 8388608
  4.1 6.0 %collective-permute-start.1 = (bf16[16,3200]{1,0:T(8,128)(2,1)S(1)}, bf16[16,3200]{1,0:T(8,128)(2,1)S(1)}, u32[]{:S(2)}, u32[]{:S(2)}) collective-permute-start(bf16[16,3200]{1,0:T(8,128)(2,1)S(1)} %get-tuple-element.34.refs_0_.refs_1_), channel_id=1, source_target_pairs={{0,4},{4,0},{8,12},{12,8},{1,5},{5,1},{9,13},{13,9},{2,6},{6,2},{1... | collective-permute-start | bytes 307208 | tf_op jit(solution)/shard_map/ppermute | solution.py:319
  7.2 7.5 %collective-permute-start = (bf16[16,3200]{1,0:T(8,128)(2,1)S(1)}, bf16[16,3200]{1,0:T(8,128)(2,1)S(1)}, u32[]{:S(2)}, u32[]{:S(2)}) collective-permute-start(bf16[16,3200]{1,0:T(8,128)(2,1)S(1)} %get-tuple-element.34.refs_0_.refs_1_), channel_id=1, source_target_pairs={{0,8},{4,12},{8,0},{12,4},{1,9},{5,13},{9,1},{13,5},{2,10},{6,14},... | collective-permute-start | bytes 307208 | tf_op jit(solution)/shard_map/ppermute | solution.py:319
  10.5 4.9 %collective-permute-start.2 = (bf16[16,3072]{1,0:T(8,128)(2,1)S(1)}, bf16[16,3072]{1,0:T(8,128)(2,1)S(1)}, u32[]{:S(2)}, u32[]{:S(2)}) collective-permute-start(bf16[16,3072]{1,0:T(8,128)(2,1)S(1)} %get-tuple-element.35), channel_id=1, source_target_pairs={{0,3},{1,2},{2,1},{3,0},{4,7},{5,6},{6,5},{7,4},{8,11},{9,10},{10,... | collective-permute-start | bytes 294920 | tf_op jit(solution)/shard_map/ppermute | solution.py:319
  15.4 5.2 %collective-permute-start.3 = (bf16[16,3200]{1,0:T(8,128)(2,1)S(1)}, bf16[16,3200]{1,0:T(8,128)(2,1)S(1)}, u32[]{:S(2)}, u32[]{:S(2)}) collective-permute-start(bf16[16,3200]{1,0:T(8,128)(2,1)S(1)} %shard_map.111), channel_id=1, source_target_pairs={{0,4},{4,0},{8,12},{12,8},{1,5},{5,1},{9,13},{13,9},{2,6},{6,2},{1... | collective-permute-start | bytes 307208 | tf_op jit(solution)/shard_map/ppermute | solution.py:319
  17.4 5.6 %collective-permute-start.4 = (bf16[16,3072]{1,0:T(8,128)(2,1)S(1)}, bf16[16,3072]{1,0:T(8,128)(2,1)S(1)}, u32[]{:S(2)}, u32[]{:S(2)}) collective-permute-start(bf16[16,3072]{1,0:T(8,128)(2,1)S(1)} %get-tuple-element.37), channel_id=1, source_target_pairs={{0,2},{1,3},{2,0},{3,1},{4,6},{5,7},{6,4},{7,5},{8,10},{9,11},{10,... | collective-permute-start | bytes 294920 | tf_op jit(solution)/shard_map/ppermute | solution.py:319
  18.0 5.3 %collective-permute-start.5 = (bf16[16,3072]{1,0:T(8,128)(2,1)S(1)}, bf16[16,3072]{1,0:T(8,128)(2,1)S(1)}, u32[]{:S(2)}, u32[]{:S(2)}) collective-permute-start(bf16[16,3072]{1,0:T(8,128)(2,1)S(1)} %get-tuple-element.38), channel_id=1, source_target_pairs={{0,1},{1,0},{2,3},{3,2},{4,5},{5,4},{6,7},{7,6},{8,9},{9,8},{10,11... | collective-permute-start | bytes 294920 | tf_op jit(solution)/shard_map/ppermute | solution.py:319
  21.1 4.1 %collective-permute-start.9 = (bf16[16,1536]{1,0:T(8,128)(2,1)S(1)}, bf16[16,1536]{1,0:T(8,128)(2,1)S(1)}, u32[]{:S(2)}, u32[]{:S(2)}) collective-permute-start(bf16[16,1536]{1,0:T(8,128)(2,1)S(1)} %get-tuple-element.44), channel_id=1, source_target_pairs={{0,3},{1,2},{2,1},{3,0},{4,7},{5,6},{6,5},{7,4},{8,11},{9,10},{10,... | collective-permute-start | bytes 147464 | tf_op jit(solution)/shard_map/ppermute | solution.py:319
  21.1 4.6 %collective-permute-start.10 = (bf16[16,1536]{1,0:T(8,128)(2,1)S(1)}, bf16[16,1536]{1,0:T(8,128)(2,1)S(1)}, u32[]{:S(2)}, u32[]{:S(2)}) collective-permute-start(bf16[16,1536]{1,0:T(8,128)(2,1)S(1)} %get-tuple-element.45), channel_id=1, source_target_pairs={{0,2},{1,3},{2,0},{3,1},{4,6},{5,7},{6,4},{7,5},{8,10},{9,11},{10,... | collective-permute-start | bytes 147464 | tf_op jit(solution)/shard_map/ppermute | solution.py:319
  22.3 3.4 %collective-permute-start.11 = (bf16[16,1536]{1,0:T(8,128)(2,1)S(1)}, bf16[16,1536]{1,0:T(8,128)(2,1)S(1)}, u32[]{:S(2)}, u32[]{:S(2)}) collective-permute-start(bf16[16,1536]{1,0:T(8,128)(2,1)S(1)} %get-tuple-element.46), channel_id=1, source_target_pairs={{0,1},{1,0},{2,3},{3,2},{4,5},{5,4},{6,7},{7,6},{8,9},{9,8},{10,11... | collective-permute-start | bytes 147464 | tf_op jit(solution)/shard_map/ppermute | solution.py:319
  23.0 6.2 %collective-permute-start.6 = (bf16[16,1536]{1,0:T(8,128)(2,1)S(1)}, bf16[16,1536]{1,0:T(8,128)(2,1)S(1)}, u32[]{:S(2)}, u32[]{:S(2)}) collective-permute-start(bf16[16,1536]{1,0:T(8,128)(2,1)S(1)} %get-tuple-element.40), channel_id=1, source_target_pairs={{0,3},{1,2},{2,1},{3,0},{4,7},{5,6},{6,5},{7,4},{8,11},{9,10},{10,... | collective-permute-start | bytes 147464 | tf_op jit(solution)/shard_map/ppermute | solution.py:319
  23.4 5.8 %collective-permute-start.7 = (bf16[16,1536]{1,0:T(8,128)(2,1)S(1)}, bf16[16,1536]{1,0:T(8,128)(2,1)S(1)}, u32[]{:S(2)}, u32[]{:S(2)}) collective-permute-start(bf16[16,1536]{1,0:T(8,128)(2,1)S(1)} %get-tuple-element.41), channel_id=1, source_target_pairs={{0,2},{1,3},{2,0},{3,1},{4,6},{5,7},{6,4},{7,5},{8,10},{9,11},{10,... | collective-permute-start | bytes 147464 | tf_op jit(solution)/shard_map/ppermute | solution.py:319
  25.1 4.0 %collective-permute-start.8 = (bf16[16,1536]{1,0:T(8,128)(2,1)S(1)}, bf16[16,1536]{1,0:T(8,128)(2,1)S(1)}, u32[]{:S(2)}, u32[]{:S(2)}) collective-permute-start(bf16[16,1536]{1,0:T(8,128)(2,1)S(1)} %get-tuple-element.42), channel_id=1, source_target_pairs={{0,1},{1,0},{2,3},{3,2},{4,5},{5,4},{6,7},{7,6},{8,9},{9,8},{10,11... | collective-permute-start | bytes 147464 | tf_op jit(solution)/shard_map/ppermute | solution.py:319
  29.2 14.9 %copy-start = (bf16[3072,4]{0,1:T(4,128)(2,1)S(1)}, bf16[3072,4]{0,1:T(4,128)(2,1)}, u32[]{:S(2)}) copy-start(bf16[3072,4]{0,1:T(4,128)(2,1)} %param.18) | copy-start | bytes 73732
  36.5 4.9 %collective-permute-start.12 = (bf16[16,3072]{1,0:T(8,128)(2,1)S(1)}, bf16[16,3072]{1,0:T(8,128)(2,1)S(1)}, u32[]{:S(2)}, u32[]{:S(2)}) collective-permute-start(bf16[16,3072]{1,0:T(8,128)(2,1)S(1)} %get-tuple-element.51), channel_id=1, source_target_pairs={{0,3},{1,2},{2,1},{3,0},{4,7},{5,6},{6,5},{7,4},{8,11},{9,10},{10,... | collective-permute-start | bytes 294920 | tf_op jit(solution)/shard_map/ppermute | solution.py:319
  37.4 6.6 %collective-permute-start.13 = (bf16[16,3072]{1,0:T(8,128)(2,1)S(1)}, bf16[16,3072]{1,0:T(8,128)(2,1)S(1)}, u32[]{:S(2)}, u32[]{:S(2)}) collective-permute-start(bf16[16,3072]{1,0:T(8,128)(2,1)S(1)} %get-tuple-element.52), channel_id=1, source_target_pairs={{0,2},{1,3},{2,0},{3,1},{4,6},{5,7},{6,4},{7,5},{8,10},{9,11},{10,... | collective-permute-start | bytes 294920 | tf_op jit(solution)/shard_map/ppermute | solution.py:319
  38.3 5.7 %collective-permute-start.14 = (bf16[16,3072]{1,0:T(8,128)(2,1)S(1)}, bf16[16,3072]{1,0:T(8,128)(2,1)S(1)}, u32[]{:S(2)}, u32[]{:S(2)}) collective-permute-start(bf16[16,3072]{1,0:T(8,128)(2,1)S(1)} %get-tuple-element.53), channel_id=1, source_target_pairs={{0,1},{1,0},{2,3},{3,2},{4,5},{5,4},{6,7},{7,6},{8,9},{9,8},{10,11... | collective-permute-start | bytes 294920 | tf_op jit(solution)/shard_map/ppermute | solution.py:319
  38.5 11.0 %collective-permute-start.15 = (bf16[16,3072]{1,0:T(8,128)(2,1)S(1)}, bf16[16,3072]{1,0:T(8,128)(2,1)S(1)}, u32[]{:S(2)}, u32[]{:S(2)}) collective-permute-start(bf16[16,3072]{1,0:T(8,128)(2,1)S(1)} %get-tuple-element.56), channel_id=1, source_target_pairs={{0,3},{1,2},{2,1},{3,0},{4,7},{5,6},{6,5},{7,4},{8,11},{9,10},{10,... | collective-permute-start | bytes 294920 | tf_op jit(solution)/shard_map/ppermute | solution.py:319
  39.6 9.9 %collective-permute-start.16 = (bf16[16,3072]{1,0:T(8,128)(2,1)S(1)}, bf16[16,3072]{1,0:T(8,128)(2,1)S(1)}, u32[]{:S(2)}, u32[]{:S(2)}) collective-permute-start(bf16[16,3072]{1,0:T(8,128)(2,1)S(1)} %get-tuple-element.57), channel_id=1, source_target_pairs={{0,2},{1,3},{2,0},{3,1},{4,6},{5,7},{6,4},{7,5},{8,10},{9,11},{10,... | collective-permute-start | bytes 294920 | tf_op jit(solution)/shard_map/ppermute | solution.py:319
  41.4 8.1 %collective-permute-start.17 = (bf16[16,3072]{1,0:T(8,128)(2,1)S(1)}, bf16[16,3072]{1,0:T(8,128)(2,1)S(1)}, u32[]{:S(2)}, u32[]{:S(2)}) collective-permute-start(bf16[16,3072]{1,0:T(8,128)(2,1)S(1)} %get-tuple-element.58), channel_id=1, source_target_pairs={{0,1},{1,0},{2,3},{3,2},{4,5},{5,4},{6,7},{7,6},{8,9},{9,8},{10,11... | collective-permute-start | bytes 294920 | tf_op jit(solution)/shard_map/ppermute | solution.py:319
  44.7 8.4 %collective-permute-start.20 = (bf16[16,3072]{1,0:T(8,128)(2,1)S(1)}, bf16[16,3072]{1,0:T(8,128)(2,1)S(1)}, u32[]{:S(2)}, u32[]{:S(2)}) collective-permute-start(bf16[16,3072]{1,0:T(8,128)(2,1)S(1)} %get-tuple-element.62), channel_id=1, source_target_pairs={{0,12},{4,8},{8,4},{12,0},{1,13},{5,9},{9,5},{13,1},{2,14},{6,10},... | collective-permute-start | bytes 294920 | tf_op jit(solution)/shard_map/ppermute | solution.py:319
  49.5 8.0 %collective-permute-start.19 = (bf16[16,3072]{1,0:T(8,128)(2,1)S(1)}, bf16[16,3072]{1,0:T(8,128)(2,1)S(1)}, u32[]{:S(2)}, u32[]{:S(2)}) collective-permute-start(bf16[16,3072]{1,0:T(8,128)(2,1)S(1)} %get-tuple-element.54.refs_0_), channel_id=1, source_target_pairs={{0,8},{4,12},{8,0},{12,4},{1,9},{5,13},{9,1},{13,5},{2,10},{6,14},... | collective-permute-start | bytes 294920 | tf_op jit(solution)/shard_map/ppermute | solution.py:319
  50.1 7.3 %collective-permute-start.18 = (bf16[16,3072]{1,0:T(8,128)(2,1)S(1)}, bf16[16,3072]{1,0:T(8,128)(2,1)S(1)}, u32[]{:S(2)}, u32[]{:S(2)}) collective-permute-start(bf16[16,3072]{1,0:T(8,128)(2,1)S(1)} %get-tuple-element.61), channel_id=1, source_target_pairs={{0,4},{4,0},{8,12},{12,8},{1,5},{5,1},{9,13},{13,9},{2,6},{6,2},{1... | collective-permute-start | bytes 294920 | tf_op jit(solution)/shard_map/ppermute | solution.py:319

commit v10 on v9

--- a/solution.py
+++ b/solution.py
@@ -14,6 +14,8 @@
 LANES = 128
 PAIR = 2
 STRIPS = 3
+TILE = 256
+UNROLL = 2
 MIB = 1 << 20
 F32 = jnp.float32
 BF16 = jnp.bfloat16
@@ -165,22 +167,6 @@
     payload_ref[:, width:] = named.astype(BF16)
 
 
-def pass_kernel(after_ref, value_ref, out_ref):
-    pass
-
-
-def pass_on(after, value):
-    return pl.pallas_call(
-        pass_kernel,
-        in_specs=[ANY, ANY],
-        out_specs=ANY,
-        out_shape=jax.ShapeDtypeStruct(value.shape, value.dtype),
-        input_output_aliases={1: 0},
-        cost_estimate=LIGHT,
-        compiler_params=params(0),
-    )(after, value)
-
-
 def split_kernel(me_ref, *refs, chunks, experts, after):
     refs = refs[after:]
     payload = jnp.concatenate([ref[...] for ref in refs[:chunks]], axis=0)
@@ -209,18 +195,38 @@
     return copies
 
 
+def load_rows(rows_ref, full, halves, begin):
+    width = rows_ref.shape[1]
+    blocks = [ref[:, begin : begin + width] for ref in full] + [ref[...] for ref in halves]
+    rows_ref[...] = jnp.concatenate([block.astype(F32) for block in blocks], axis=0).astype(BF16)
+
+
+def tiles(count, tile):
+    def run(body):
+        @pl.loop(0, count // tile, unroll=UNROLL)
+        def _(i):
+            body(pl.ds(pl.multiple_of(i * tile, tile), tile))
+
+    return run
+
+
+def store_rows(outs, at, value, near):
+    count = outs[0].shape[0] - near
+    for e, ref in enumerate(outs):
+        first, second = e * near, len(outs) * near + e * count
+        rows = [value[first : first + near], value[second : second + count]]
+        ref[:, at] = jnp.concatenate(rows, axis=0).astype(BF16)
+
+
 def begin_kernel(*refs, near, far):
     gate_ref, up_ref, down_hbm, gate_out, up_out, down_out, rows_ref, sems = refs[near + far :]
     half = rows_ref.shape[1]
     copies = strip_copies(down_hbm, 0, down_out, sems)
-    blocks = [ref[:, :half] for ref in refs[:near]] + [ref[...] for ref in refs[near : near + far]]
-    rows_ref[...] = jnp.concatenate([block.astype(F32) for block in blocks], axis=0).astype(BF16)
+    load_rows(rows_ref, refs[:near], refs[near : near + far], 0)
     units = gate_ref.shape[1]
-    tile = min(256, units)
-
-    @pl.loop(0, units // tile)
-    def _(i):
-        at = pl.ds(pl.multiple_of(i * tile, tile), tile)
+
+    @tiles(units, min(TILE, units))
+    def _(at):
         gate_out[:, at] = dot(rows_ref[...], gate_ref[:half, at])
         up_out[:, at] = dot(rows_ref[...], up_ref[:half, at])
 
@@ -228,84 +234,62 @@
         copy.wait()
 
 
-def end_kernel(*refs, near, far):
+def middle_kernel(*refs, near, far):
     gate_in, up_in, down_in, gate_ref, up_ref, down_hbm = refs[near + far : near + far + 6]
     outs = refs[near + far + 6 : -4]
-    rows_ref, hidden_ref, down_ref, sems = refs[-4:]
+    hidden_ref, down_out, rows_ref, sems = refs[-4:]
     half = rows_ref.shape[1]
-    width, units = gate_ref.shape
-    copies = strip_copies(down_hbm, half, down_ref, sems)
-    blocks = [ref[:, half:] for ref in refs[:near]] + [ref[...] for ref in refs[near : near + far]]
-    rows_ref[...] = jnp.concatenate([block.astype(F32) for block in blocks], axis=0).astype(BF16)
-    tile = min(256, units)
-
-    @pl.loop(0, units // tile)
-    def _(i):
-        at = pl.ds(pl.multiple_of(i * tile, tile), tile)
+    copies = strip_copies(down_hbm, half, down_out, sems)
+    load_rows(rows_ref, refs[:near], refs[near : near + far], half)
+    units = gate_ref.shape[1]
+
+    @tiles(units, min(TILE, units))
+    def _(at):
         gate = gate_in[:, at] + dot(rows_ref[...], gate_ref[half:, at])
         up = up_in[:, at] + dot(rows_ref[...], up_ref[half:, at])
         hidden_ref[:, at] = (jax.nn.silu(gate) * up).astype(BF16)
 
-    def down(source, begin, first, columns):
-        @pl.loop(0, columns // tile)
-        def _(i):
-            at = pl.multiple_of(i * tile, tile)
-            out = dot(hidden_ref[...], source[:, pl.ds(first + at, tile)])
-            row = 0
-            for ref in outs:
-                count = ref.shape[0]
-                ref[:, pl.ds(begin + first + at, tile)] = out[row : row + count].astype(BF16)
-                row += count
-
-    strip = half // len(copies)
-    down(down_in, 0, 0, half)
-    for c, copy in enumerate(copies):
+    @tiles(half, min(TILE, half))
+    def _(at):
+        store_rows(outs, at, dot(hidden_ref[...], down_in[:, at]), refs[0].shape[0])
+
+    for copy in copies:
         copy.wait()
-        down(down_ref, half, c * strip, strip)
-
-
-def mix_kernel(me_ref, router_ref, *refs, chunks, experts, after):
-    refs = refs[after:]
-    payload = jnp.concatenate([ref[...] for ref in refs[:chunks]], axis=0)
+
+
+def end_kernel(hidden_ref, down_ref, *outs, near):
+    half = down_ref.shape[1]
+
+    @tiles(half, min(TILE, half))
+    def _(at):
+        store_rows(outs, at, dot(hidden_ref[...], down_ref[:, at]), near)
+
+
+def mix_kernel(me_ref, router_ref, *refs, layers, columns):
+    outs, stream_ref = refs[-layers:], refs[-layers - 1]
+    blocks = refs[layers : -layers - 1]
+    experts = len(blocks)
     order = farthest_first(experts)
-    returned = jnp.concatenate(
-        [refs[chunks + order.index(e)][...].astype(F32) for e in range(experts)], axis=0
-    ).astype(BF16)
-    added, outs = refs[chunks + experts : len(refs) - chunks], refs[len(refs) - chunks :]
-    batch, width = outs[0].shape
+    batch, width = stream_ref.shape
+    payload = jnp.concatenate([ref[...] for ref in refs[:layers]], axis=0)
+    returned = jnp.concatenate([blocks[order.index(e)][...] for e in range(experts)], axis=0)
     rows, named = payload[:, :width], payload[:, width:]
-    mixed = combine(me_ref[0], rows, named, router_ref[...], returned, chunks, experts)
+    mixed = combine(me_ref[0], rows, named, router_ref[...], returned, layers, experts)
     for j, ref in enumerate(outs):
         part = mixed[j * batch : (j + 1) * batch]
-        for other in added if j == 0 else []:
-            part = part + other[...]
+        if j == 0:
+            part = part + stream_ref[:, columns]
         ref[...] = part.astype(ref.dtype)
 
 
-def mix(me, router, payloads, returned, added, after):
-    chunks, experts = len(payloads), len(returned)
-    width = returned[0].shape[1]
-    batch = payloads[0].shape[0]
-    returned = [swap(block, "expert", e) for e, block in zip(farthest_first(experts), returned)]
-    operands = [me, router, *after, *payloads, *returned, *added]
-    return pl.pallas_call(
-        functools.partial(mix_kernel, chunks=chunks, experts=experts, after=len(after)),
-        in_specs=[SCALAR, WHOLE] + [ANY] * len(after) + [WHOLE] * (len(operands) - 2 - len(after)),
-        out_specs=[WHOLE] * chunks,
-        out_shape=[
-            jax.ShapeDtypeStruct((batch, width), F32 if added and j == 0 else BF16)
-            for j in range(chunks)
-        ],
-        cost_estimate=LIGHT,
-        compiler_params=params(experts * chunks * CAP * width),
-    )(*operands)
-
-
-def add_kernel(*refs):
-    total = refs[0][...]
-    for ref in refs[1:-1]:
-        total = total + ref[...].astype(F32)
-    refs[-1][...] = total.astype(BF16)
+def finish_kernel(*refs, parts):
+    out_ref = refs[-1]
+    span, count = out_ref.shape[1] // parts, len(refs[:-1]) // parts
+    for p in range(parts):
+        total = refs[p * count][...]
+        for ref in refs[p * count + 1 : (p + 1) * count]:
+            total = total + ref[...].astype(F32)
+        out_ref[:, p * span : (p + 1) * span] = total.astype(BF16)
 
 
 def in_hbm(value):
@@ -366,7 +350,7 @@
         cost_estimate=LIGHT,
     )(me, *operands)
 
-    chunks = [swap(payload, "attn", j) if j < 2 or j % 2 == 0 else None for j in range(layers)]
+    chunks = [swap(payload, "attn", j) for j in range(layers)]
     groups = [[0, 1], list(range(2, layers))]
     half = width // 2
     order = farthest_first(experts)
@@ -386,8 +370,6 @@
         ]
 
     near = send(groups[0], width, [])
-    for j in range(3, layers, 2):
-        chunks[j] = swap(pass_on(near[1], chunks[j - 1]), "attn", 1)
     far = send(groups[1], half, near[1:2])
     total_rows = sum(block.shape[0] for block in near + far[:experts])
     units = gate_proj.shape[2]
@@ -403,32 +385,51 @@
         ),
         compiler_params=params(total_rows * width),
     )(*near, *far[:experts], gate_proj[0], up_proj[0], in_hbm(down_proj[0]))
-    results = pl.pallas_call(
-        functools.partial(end_kernel, **counts),
+    halves = [shape((layers * CAP, half), BF16)] * experts
+    *first, hidden, down = pl.pallas_call(
+        functools.partial(middle_kernel, **counts),
         in_specs=[WHOLE] * (2 * experts + 5) + [ANY],
-        out_specs=[WHOLE] * (2 * experts),
-        out_shape=[shape((block.shape[0], width), BF16) for block in near + far[:experts]],
-        scratch_shapes=[
-            pltpu.VMEM((total_rows, half), BF16),
-            pltpu.VMEM((total_rows, units), BF16),
-            pltpu.VMEM((units, half), BF16),
-            pltpu.SemaphoreType.DMA((STRIPS,)),
-        ],
-        compiler_params=params(total_rows * width + units * half // 5),
+        out_specs=[WHOLE] * (experts + 2),
+        out_shape=halves + [shape((total_rows, units), BF16), pltpu.VMEM((units, half), BF16)],
+        scratch_shapes=[pltpu.VMEM((total_rows, half), BF16), pltpu.SemaphoreType.DMA((STRIPS,))],
+        compiler_params=params(total_rows * width),
     )(*near, *far[experts:], *sums, gate_proj[0], up_proj[0], in_hbm(down_proj[0]))
-
-    near, far = results[:experts], results[experts:]
-    far = mix(me, router, [chunks[j] for j in groups[1]], far, [], [])
-    base, first = mix(me, router, chunks[:2], near, [stream], far[:1])
-    received = [swap(block, "attn", j + 1) for j, block in enumerate([first, *far])]
+    second = pl.pallas_call(
+        functools.partial(end_kernel, near=near[0].shape[0]),
+        in_specs=[WHOLE] * 2,
+        out_specs=[WHOLE] * experts,
+        out_shape=halves,
+        cost_estimate=pl.CostEstimate(
+            flops=2 * total_rows * half * units, bytes_accessed=0, transcendentals=0
+        ),
+        compiler_params=params(total_rows * width),
+    )(hidden, down)
+
+    sums = []
+    for p, blocks in enumerate((first, second)):
+        returned = [swap(block, "expert", e) for e, block in zip(order, blocks)]
+        operands = [me, router, *chunks, *returned, stream]
+        mixed = pl.pallas_call(
+            functools.partial(
+                mix_kernel,
+                layers=layers,
+                columns=slice(p * half, (p + 1) * half),
+            ),
+            in_specs=[SCALAR] + [WHOLE] * (len(operands) - 1),
+            out_specs=[WHOLE] * layers,
+            out_shape=[shape((batch, half), BF16 if j else F32) for j in range(layers)],
+            cost_estimate=LIGHT,
+            compiler_params=params(experts * layers * CAP * half),
+        )(*operands)
+        sums += [swap(mixed[j], "attn", j) for j in farthest_first(layers)]
     return pl.pallas_call(
-        add_kernel,
-        in_specs=[WHOLE] * layers,
+        functools.partial(finish_kernel, parts=2),
+        in_specs=[WHOLE] * len(sums),
         out_specs=WHOLE,
         out_shape=shape((batch, width), BF16),
         cost_estimate=LIGHT,
         compiler_params=params(2 * layers * batch * width),
-    )(base, *received)
+    )(*sums)
 
 
 def solution(mesh):

time: 58.3 us -> 53.8 us (0.923)
  waiting for transfers between devices: 18.6 us -> 13.4 us
  starting transfers between devices: 21.8 us -> 24.4 us
  Pallas kernels: 17.5 us -> 15.6 us
    ppermute x21 -> x24, waiting for transfers between devices: 18.6 us -> 13.4 us  [swap(): return lax.ppermute(value, axis, [(i, i ^ step) for i in range(count)])]
    ppermute x21 -> x24, starting transfers between devices: 21.8 us -> 24.4 us  [swap(): return lax.ppermute(value, axis, [(i, i ^ step) for i in range(count)])]
    pallas_call x5, Pallas kernels: 9.23 us -> 7.71 us  [the longest x1 4.19 us: shards(): pl.pallas_call(functools.partial(middle_kernel, **counts), in_specs=[WHOL...]
  transfers between devices with their start and end apart: 21 -> 24, of which waited for: 10 -> 8; matrix products, arithmetic and copies ran while one was open for 0% -> 0% of each run, Pallas kernels for 9% -> 13%
where the time goes in v10:
time: 53.8 us; the launch traced here: 53.6 us
  starting transfers between devices  24.4 us (45%)
  Pallas kernels  15.6 us (29%)
  waiting for transfers between devices  13.4 us (25%)
    ppermute x24, starting transfers between devices, swap(): return lax.ppermute(value, axis, [(i, i ^ step) for i in range(count)])  24.4 us
    ppermute x24, waiting for transfers between devices, swap(): return lax.ppermute(value, axis, [(i, i ^ step) for i in range(count)])  13.4 us
    pallas_call x1, Pallas kernels, shards(): pl.pallas_call(functools.partial(middle_kernel, **counts), in_specs=[WHOL...  4.19 us
    pallas_call x1, Pallas kernels, shards(): pl.pallas_call(attend_kernel, in_specs=[SCALAR] + [ANY] * len(operands),...  3.99 us
    pallas_call x1, Pallas kernels, shards(): pl.pallas_call(functools.partial(begin_kernel, **counts), in_specs=[WHOLE...  2.92 us
    pallas_call x2, Pallas kernels, shards(): pl.pallas_call(functools.partial(mix_kernel, layers=layers, columns=slice...  1.46 us
    pallas_call x1, Pallas kernels, shards(): pl.pallas_call(functools.partial(end_kernel, near=near[0].shape[0]), in_s...  1.37 us
  transfers between devices with their start and end apart: 24, of which 8 were waited for; matrix products, arithmetic and copies ran while one was open for 0% of the time, Pallas kernels for 13%

profile of v10, /device:TPU:0, one launch (start us, length us, event | category | flops | bytes accessed | tf_op | source)
XLA Modules:
  0.0 53.6 jit_solution(4486875259965116631)
XLA Ops:
  0.0 4.0 %shard_map.109 = (f32[16,3072]{1,0:T(8,128)S(1)}, bf16[16,3200]{1,0:T(8,128)(2,1)S(1)}) custom-call(s32[1]{0:T(128)} %bitcast._.me_ref, s32[1,16]{1,0:T(1,128)} %bitcast.22, bf16[16,3072]{1,0:T(8,128)(2,1)} %queries_hbm.1, bf16[16,96,512]{2,1,0:T(8,128)(2,1)} %keys_hbm.1, bf16[16,96,512]{2,1,0:T(8,128)(2,1)} %values_hbm.1, s32[2,16]{1,0:T(2,128)} %bitcast.21, ...), custom_call_target="tpu_custom_call" | custom-call | tf_op jit(solution)/shard_map/pallas_call | solution.py:342
  4.0 0.0 slice-start
  4.0 0.0 slice-start.3
  4.0 0.0 slice-start.1
  4.0 0.0 slice-start.2
  4.0 0.0 slice-start.4
  4.1 0.0 slice-start.5
  4.1 3.1 %collective-permute-start = (bf16[16,3200]{1,0:T(8,128)(2,1)S(1)}, bf16[16,3200]{1,0:T(8,128)(2,1)S(1)}, u32[]{:S(2)}, u32[]{:S(2)}) collective-permute-start(bf16[16,3200]{1,0:T(8,128)(2,1)S(1)} %get-tuple-element.40.refs_0_), channel_id=1, source_target_pairs={{0,4},{4,0},{8,12},{12,8},{1,5},{5,1},{9,13},{13,9},{2,6},{6,2},{1... | collective-permute-start | bytes 307208 | tf_op jit(solution)/shard_map/ppermute | solution.py:303
  7.2 2.5 %collective-permute-start.2 = (bf16[16,3200]{1,0:T(8,128)(2,1)S(1)}, bf16[16,3200]{1,0:T(8,128)(2,1)S(1)}, u32[]{:S(2)}, u32[]{:S(2)}) collective-permute-start(bf16[16,3200]{1,0:T(8,128)(2,1)S(1)} %get-tuple-element.40.refs_0_), channel_id=1, source_target_pairs={{0,12},{4,8},{8,4},{12,0},{1,13},{5,9},{9,5},{13,1},{2,14},{6,10},... | collective-permute-start | bytes 307208 | tf_op jit(solution)/shard_map/ppermute | solution.py:303
  9.6 0.1 collective-permute-start.1
  9.7 0.3 collective-permute-done.refs_1_
  10.0 0.5 shard_map.110
  10.5 0.2 collective-permute-start.3
  10.7 1.7 %collective-permute-start.4 = (bf16[16,3072]{1,0:T(8,128)(2,1)S(1)}, bf16[16,3072]{1,0:T(8,128)(2,1)S(1)}, u32[]{:S(2)}, u32[]{:S(2)}) collective-permute-start(bf16[16,3072]{1,0:T(8,128)(2,1)S(1)} %get-tuple-element.43), channel_id=1, source_target_pairs={{0,2},{1,3},{2,0},{3,1},{4,6},{5,7},{6,4},{7,5},{8,10},{9,11},{10,... | collective-permute-start | bytes 294920 | tf_op jit(solution)/shard_map/ppermute | solution.py:303
  12.4 0.1 collective-permute-start.5
  12.4 3.1 %collective-permute-done.2.refs_2_.refs_3_ = bf16[16,3200]{1,0:T(8,128)(2,1)S(1)} collective-permute-done((bf16[16,3200]{1,0:T(8,128)(2,1)S(1)}, bf16[16,3200]{1,0:T(8,128)(2,1)S(1)}, u32[]{:S(2)}, u32[]{:S(2)}) %collective-permute-start.2) | collective-permute-done | bytes 102432 | tf_op jit(solution)/shard_map/ppermute | solution.py:303
  15.5 3.4 %collective-permute-done.1.refs_1_.refs_2_ = bf16[16,3200]{1,0:T(8,128)(2,1)S(1)} collective-permute-done((bf16[16,3200]{1,0:T(8,128)(2,1)S(1)}, bf16[16,3200]{1,0:T(8,128)(2,1)S(1)}, u32[]{:S(2)}, u32[]{:S(2)}) %collective-permute-start.1) | collective-permute-done | bytes 102432 | tf_op jit(solution)/shard_map/ppermute | solution.py:303
  18.9 0.0 collective-permute-done.3.refs_0_.refs_1_
  18.9 0.5 shard_map.111
  19.4 0.7 %collective-permute-start.9 = (bf16[16,1536]{1,0:T(8,128)(2,1)S(1)}, bf16[16,1536]{1,0:T(8,128)(2,1)S(1)}, u32[]{:S(2)}, u32[]{:S(2)}) collective-permute-start(bf16[16,1536]{1,0:T(8,128)(2,1)S(1)} %get-tuple-element.50), channel_id=1, source_target_pairs={{0,3},{1,2},{2,1},{3,0},{4,7},{5,6},{6,5},{7,4},{8,11},{9,10},{10,... | collective-permute-start | bytes 147464 | tf_op jit(solution)/shard_map/ppermute | solution.py:303
  20.1 1.0 %collective-permute-start.10 = (bf16[16,1536]{1,0:T(8,128)(2,1)S(1)}, bf16[16,1536]{1,0:T(8,128)(2,1)S(1)}, u32[]{:S(2)}, u32[]{:S(2)}) collective-permute-start(bf16[16,1536]{1,0:T(8,128)(2,1)S(1)} %get-tuple-element.51), channel_id=1, source_target_pairs={{0,2},{1,3},{2,0},{3,1},{4,6},{5,7},{6,4},{7,5},{8,10},{9,11},{10,... | collective-permute-start | bytes 147464 | tf_op jit(solution)/shard_map/ppermute | solution.py:303
  21.1 0.3 collective-permute-start.11
  21.3 0.0 collective-permute-done.4.refs_2_
  21.3 1.1 %collective-permute-start.6 = (bf16[16,1536]{1,0:T(8,128)(2,1)S(1)}, bf16[16,1536]{1,0:T(8,128)(2,1)S(1)}, u32[]{:S(2)}, u32[]{:S(2)}) collective-permute-start(bf16[16,1536]{1,0:T(8,128)(2,1)S(1)} %get-tuple-element.46), channel_id=1, source_target_pairs={{0,3},{1,2},{2,1},{3,0},{4,7},{5,6},{6,5},{7,4},{8,11},{9,10},{10,... | collective-permute-start | bytes 147464 | tf_op jit(solution)/shard_map/ppermute | solution.py:303
  22.4 0.0 collective-permute-done.5.refs_3_
  22.5 0.8 %collective-permute-start.7 = (bf16[16,1536]{1,0:T(8,128)(2,1)S(1)}, bf16[16,1536]{1,0:T(8,128)(2,1)S(1)}, u32[]{:S(2)}, u32[]{:S(2)}) collective-permute-start(bf16[16,1536]{1,0:T(8,128)(2,1)S(1)} %get-tuple-element.47), channel_id=1, source_target_pairs={{0,2},{1,3},{2,0},{3,1},{4,6},{5,7},{6,4},{7,5},{8,10},{9,11},{10,... | collective-permute-start | bytes 147464 | tf_op jit(solution)/shard_map/ppermute | solution.py:303
  23.2 0.3 collective-permute-done.9.refs_5_
  23.5 0.1 collective-permute-start.8
  23.6 1.1 %collective-permute-done.10.refs_6_ = bf16[16,1536]{1,0:T(8,128)(2,1)S(1)} collective-permute-done((bf16[16,1536]{1,0:T(8,128)(2,1)S(1)}, bf16[16,1536]{1,0:T(8,128)(2,1)S(1)}, u32[]{:S(2)}, u32[]{:S(2)}) %collective-permute-start.10) | collective-permute-done | bytes 49184 | tf_op jit(solution)/shard_map/ppermute | solution.py:303
  24.7 0.0 collective-permute-done.11.refs_7_
  24.8 2.9 %shard_map.112 = (f32[128,2048]{1,0:T(8,128)S(1)}, f32[128,2048]{1,0:T(8,128)S(1)}, bf16[2048,1536]{1,0:T(8,128)(2,1)S(1)}) custom-call(bf16[16,3072]{1,0:T(8,128)(2,1)S(1)} %get-tuple-element.41.refs_0_, bf16[16,3072]{1,0:T(8,128)(2,1)S(1)} %collective-permute-done.3.refs_0_.refs_1_, bf16[16,3072]{1,0:T(8,128)(2,1)S(1)} %collective-permute-done.4.refs_2_, ...), custom_call_target="tpu_custom_call" | custom-call | flops 1610612736 | tf_op jit(solution)/shard_map/pallas_call | solution.py:377
  27.7 0.0 collective-permute-done.6.refs_5_
  27.7 0.0 collective-permute-done.7.refs_6_
  27.7 0.0 collective-permute-done.8.refs_7_
  27.7 4.2 %shard_map.113 = (bf16[32,1536]{1,0:T(8,128)(2,1)S(1)}, bf16[32,1536]{1,0:T(8,128)(2,1)S(1)}, bf16[32,1536]{1,0:T(8,128)(2,1)S(1)}, bf16[32,1536]{1,0:T(8,128)(2...) custom-call(bf16[16,3072]{1,0:T(8,128)(2,1)S(1)} %get-tuple-element.41.refs_0_, ...), custom_call_target="tpu_custom_call" | custom-call | tf_op jit(solution)/shard_map/pallas_call | solution.py:389
  31.9 0.0 copy-start
  31.9 0.7 %collective-permute-start.12 = (bf16[32,1536]{1,0:T(8,128)(2,1)S(1)}, bf16[32,1536]{1,0:T(8,128)(2,1)S(1)}, u32[]{:S(2)}, u32[]{:S(2)}) collective-permute-start(bf16[32,1536]{1,0:T(8,128)(2,1)S(1)} %get-tuple-element.57), channel_id=1, source_target_pairs={{0,3},{1,2},{2,1},{3,0},{4,7},{5,6},{6,5},{7,4},{8,11},{9,10},{10,... | collective-permute-start | bytes 294920 | tf_op jit(solution)/shard_map/ppermute | solution.py:303
  32.6 1.1 %collective-permute-start.13 = (bf16[32,1536]{1,0:T(8,128)(2,1)S(1)}, bf16[32,1536]{1,0:T(8,128)(2,1)S(1)}, u32[]{:S(2)}, u32[]{:S(2)}) collective-permute-start(bf16[32,1536]{1,0:T(8,128)(2,1)S(1)} %get-tuple-element.58), channel_id=1, source_target_pairs={{0,2},{1,3},{2,0},{3,1},{4,6},{5,7},{6,4},{7,5},{8,10},{9,11},{10,... | collective-permute-start | bytes 294920 | tf_op jit(solution)/shard_map/ppermute | solution.py:303
  33.7 0.1 collective-permute-start.14
  33.9 1.4 %shard_map.115 = (bf16[32,1536]{1,0:T(8,128)(2,1)S(1)}, bf16[32,1536]{1,0:T(8,128)(2,1)S(1)}, bf16[32,1536]{1,0:T(8,128)(2,1)S(1)}, bf16[32,1536]{1,0:T(8,128)(2,1)S(1)}) custom-call(bf16[128,2048]{1,0:T(8,128)(2,1)S(1)} %get-tuple-element.65.hidden_ref, bf16[2048,1536]{1,0:T(8,128)(2,1)S(1)} %get-tuple-element.66.down_ref), custom_call_target="tpu_custom_call" | custom-call | flops 805306368 | tf_op jit(solution)/shard_map/pallas_call | solution.py:397
  35.3 1.0 %collective-permute-start.18 = (bf16[32,1536]{1,0:T(8,128)(2,1)S(1)}, bf16[32,1536]{1,0:T(8,128)(2,1)S(1)}, u32[]{:S(2)}, u32[]{:S(2)}) collective-permute-start(bf16[32,1536]{1,0:T(8,128)(2,1)S(1)} %get-tuple-element.68), channel_id=1, source_target_pairs={{0,3},{1,2},{2,1},{3,0},{4,7},{5,6},{6,5},{7,4},{8,11},{9,10},{10,... | collective-permute-start | bytes 294920 | tf_op jit(solution)/shard_map/ppermute | solution.py:303
  36.3 1.0 %collective-permute-start.19 = (bf16[32,1536]{1,0:T(8,128)(2,1)S(1)}, bf16[32,1536]{1,0:T(8,128)(2,1)S(1)}, u32[]{:S(2)}, u32[]{:S(2)}) collective-permute-start(bf16[32,1536]{1,0:T(8,128)(2,1)S(1)} %get-tuple-element.69), channel_id=1, source_target_pairs={{0,2},{1,3},{2,0},{3,1},{4,6},{5,7},{6,4},{7,5},{8,10},{9,11},{10,... | collective-permute-start | bytes 294920 | tf_op jit(solution)/shard_map/ppermute | solution.py:303
  37.3 0.0 collective-permute-done.12.refs_5_
  37.3 0.0 collective-permute-start.20
  37.3 2.2 %collective-permute-done.13.refs_6_ = bf16[32,1536]{1,0:T(8,128)(2,1)S(1)} collective-permute-done((bf16[32,1536]{1,0:T(8,128)(2,1)S(1)}, bf16[32,1536]{1,0:T(8,128)(2,1)S(1)}, u32[]{:S(2)}, u32[]{:S(2)}) %collective-permute-start.13) | collective-permute-done | bytes 98336 | tf_op jit(solution)/shard_map/ppermute | solution.py:303
  39.5 0.0 collective-permute-done.14.refs_7_
  39.5 0.7 %shard_map.114 = (f32[16,1536]{1,0:T(8,128)S(1)}, bf16[16,1536]{1,0:T(8,128)(2,1)S(1)}, bf16[16,1536]{1,0:T(8,128)(2,1)S(1)}, bf16[16,1536]{1,0:T(8,128)(2,1)S(1)}) custom-call(s32[1]{0:T(128)} %bitcast._.me_ref, bf16[4,3072]{1,0:T(4,128)(2,1)S(1)} %bitcast.16, bf16[16,3200]{1,0:T(8,128)(2,1)S(1)} %get-tuple-element.40.refs_0_, ...), custom_call_target="tpu_custom_call" | custom-call | tf_op jit(solution)/shard_map/pallas_call | solution.py:412
  40.2 2.4 %collective-permute-start.15 = (bf16[16,1536]{1,0:T(8,128)(2,1)S(1)}, bf16[16,1536]{1,0:T(8,128)(2,1)S(1)}, u32[]{:S(2)}, u32[]{:S(2)}) collective-permute-start(bf16[16,1536]{1,0:T(8,128)(2,1)S(1)} %get-tuple-element.62), channel_id=1, source_target_pairs={{0,12},{4,8},{8,4},{12,0},{1,13},{5,9},{9,5},{13,1},{2,14},{6,10},... | collective-permute-start | bytes 147464 | tf_op jit(solution)/shard_map/ppermute | solution.py:303
  42.6 0.0 collective-permute-start.16
  42.6 0.0 collective-permute-done.18.refs_5_
  42.6 2.0 %collective-permute-start.17 = (bf16[16,1536]{1,0:T(8,128)(2,1)S(1)}, bf16[16,1536]{1,0:T(8,128)(2,1)S(1)}, u32[]{:S(2)}, u32[]{:S(2)}) collective-permute-start(bf16[16,1536]{1,0:T(8,128)(2,1)S(1)} %get-tuple-element.64), channel_id=1, source_target_pairs={{0,4},{4,0},{8,12},{12,8},{1,5},{5,1},{9,13},{13,9},{2,6},{6,2},{1... | collective-permute-start | bytes 147464 | tf_op jit(solution)/shard_map/ppermute | solution.py:303
  44.7 0.0 collective-permute-done.19.refs_6_
  44.7 0.0 collective-permute-done.20.refs_7_
  44.7 0.7 %shard_map.116 = (f32[16,1536]{1,0:T(8,128)S(1)}, bf16[16,1536]{1,0:T(8,128)(2,1)S(1)}, bf16[16,1536]{1,0:T(8,128)(2,1)S(1)}, bf16[16,1536]{1,0:T(8,128)(2,1)S(1)}) custom-call(s32[1]{0:T(128)} %bitcast._.me_ref, bf16[4,3072]{1,0:T(4,128)(2,1)S(1)} %bitcast.17, bf16[16,3200]{1,0:T(8,128)(2,1)S(1)} %get-tuple-element.40.refs_0_, ...), custom_call_target="tpu_custom_call" | custom-call | tf_op jit(solution)/shard_map/pallas_call | solution.py:412
  45.4 2.4 %collective-permute-start.21 = (bf16[16,1536]{1,0:T(8,128)(2,1)S(1)}, bf16[16,1536]{1,0:T(8,128)(2,1)S(1)}, u32[]{:S(2)}, u32[]{:S(2)}) collective-permute-start(bf16[16,1536]{1,0:T(8,128)(2,1)S(1)} %get-tuple-element.72), channel_id=1, source_target_pairs={{0,12},{4,8},{8,4},{12,0},{1,13},{5,9},{9,5},{13,1},{2,14},{6,10},... | collective-permute-start | bytes 147464 | tf_op jit(solution)/shard_map/ppermute | solution.py:303
  47.8 0.0 collective-permute-start.22
  47.8 0.0 collective-permute-done.15.refs_1_
  47.9 2.0 %collective-permute-start.23 = (bf16[16,1536]{1,0:T(8,128)(2,1)S(1)}, bf16[16,1536]{1,0:T(8,128)(2,1)S(1)}, u32[]{:S(2)}, u32[]{:S(2)}) collective-permute-start(bf16[16,1536]{1,0:T(8,128)(2,1)S(1)} %get-tuple-element.74), channel_id=1, source_target_pairs={{0,4},{4,0},{8,12},{12,8},{1,5},{5,1},{9,13},{13,9},{2,6},{6,2},{1... | collective-permute-start | bytes 147464 | tf_op jit(solution)/shard_map/ppermute | solution.py:303
  49.9 0.0 collective-permute-done.16.refs_2_
  49.9 0.0 collective-permute-done.17.refs_3_
  49.9 2.0 %collective-permute-done.21.refs_5_ = bf16[16,1536]{1,0:T(8,128)(2,1)S(1)} collective-permute-done((bf16[16,1536]{1,0:T(8,128)(2,1)S(1)}, bf16[16,1536]{1,0:T(8,128)(2,1)S(1)}, u32[]{:S(2)}, u32[]{:S(2)}) %collective-permute-start.21) | collective-permute-done | bytes 49184 | tf_op jit(solution)/shard_map/ppermute | solution.py:303
  51.8 1.1 %collective-permute-done.22.refs_6_ = bf16[16,1536]{1,0:T(8,128)(2,1)S(1)} collective-permute-done((bf16[16,1536]{1,0:T(8,128)(2,1)S(1)}, bf16[16,1536]{1,0:T(8,128)(2,1)S(1)}, u32[]{:S(2)}, u32[]{:S(2)}) %collective-permute-start.22) | collective-permute-done | bytes 49184 | tf_op jit(solution)/shard_map/ppermute | solution.py:303
  53.0 0.0 collective-permute-done.23.refs_7_
  53.0 0.7 %shard_map.117 = bf16[16,3072]{1,0:T(8,128)(2,1)} custom-call(f32[16,1536]{1,0:T(8,128)S(1)} %get-tuple-element.61.refs_0_, bf16[16,1536]{1,0:T(8,128)(2,1)S(1)} %collective-permute-done.15.refs_1_, bf16[16,1536]{1,0:T(8,128)(2,1)S(1)} %collective-permute-done.16.refs_2_, bf16[16,1536]{1,0:T(8,128)(2,1)S(1)} %collective-permute-done.17.refs_3_, ...), custom_call_target="tpu_custom_call" | custom-call | tf_op jit(solution)/shard_map/pallas_call | solution.py:425
  (9 shorter events, 0.0 us)
Async XLA Ops:
  4.0 20.7 %slice-start = ((s8[12582912]{0:T(1024)(128)(4,1)}), s8[4194304]{0:T(1024)(128)(4,1)S(1)}, s32[]{:S(2)}) async-start(s8[12582912]{0:T(1024)(128)(4,1)} %bitcast.8), calls=%async_computation | async-start | bytes 8388608
  4.0 20.7 %slice-start.3 = ((s8[12582912]{0:T(1024)(128)(4,1)}), s8[4194304]{0:T(1024)(128)(4,1)S(1)}, s32[]{:S(2)}) async-start(s8[12582912]{0:T(1024)(128)(4,1)} %bitcast.12), calls=%async_computation.3 | async-start | bytes 8388608
  4.0 20.7 %slice-start.1 = ((s8[12582912]{0:T(1024)(128)(4,1)}), s8[4194304]{0:T(1024)(128)(4,1)S(1)}, s32[]{:S(2)}) async-start(s8[12582912]{0:T(1024)(128)(4,1)} %bitcast.8), calls=%async_computation.1 | async-start | bytes 8388608
  4.0 20.7 %slice-start.2 = ((s8[12582912]{0:T(1024)(128)(4,1)}), s8[4194304]{0:T(1024)(128)(4,1)S(1)}, s32[]{:S(2)}) async-start(s8[12582912]{0:T(1024)(128)(4,1)} %bitcast.8), calls=%async_computation.2 | async-start | bytes 8388608
  4.0 20.7 %slice-start.4 = ((s8[12582912]{0:T(1024)(128)(4,1)}), s8[4194304]{0:T(1024)(128)(4,1)S(1)}, s32[]{:S(2)}) async-start(s8[12582912]{0:T(1024)(128)(4,1)} %bitcast.12), calls=%async_computation.4 | async-start | bytes 8388608
  4.1 20.7 %slice-start.5 = ((s8[12582912]{0:T(1024)(128)(4,1)}), s8[4194304]{0:T(1024)(128)(4,1)S(1)}, s32[]{:S(2)}) async-start(s8[12582912]{0:T(1024)(128)(4,1)} %bitcast.12), calls=%async_computation.5 | async-start | bytes 8388608
  4.1 6.0 %collective-permute-start = (bf16[16,3200]{1,0:T(8,128)(2,1)S(1)}, bf16[16,3200]{1,0:T(8,128)(2,1)S(1)}, u32[]{:S(2)}, u32[]{:S(2)}) collective-permute-start(bf16[16,3200]{1,0:T(8,128)(2,1)S(1)} %get-tuple-element.40.refs_0_), channel_id=1, source_target_pairs={{0,4},{4,0},{8,12},{12,8},{1,5},{5,1},{9,13},{13,9},{2,6},{6,2},{1... | collective-permute-start | bytes 307208 | tf_op jit(solution)/shard_map/ppermute | solution.py:303
  7.2 8.4 %collective-permute-start.2 = (bf16[16,3200]{1,0:T(8,128)(2,1)S(1)}, bf16[16,3200]{1,0:T(8,128)(2,1)S(1)}, u32[]{:S(2)}, u32[]{:S(2)}) collective-permute-start(bf16[16,3200]{1,0:T(8,128)(2,1)S(1)} %get-tuple-element.40.refs_0_), channel_id=1, source_target_pairs={{0,12},{4,8},{8,4},{12,0},{1,13},{5,9},{9,5},{13,1},{2,14},{6,10},... | collective-permute-start | bytes 307208 | tf_op jit(solution)/shard_map/ppermute | solution.py:303
  9.6 9.3 %collective-permute-start.1 = (bf16[16,3200]{1,0:T(8,128)(2,1)S(1)}, bf16[16,3200]{1,0:T(8,128)(2,1)S(1)}, u32[]{:S(2)}, u32[]{:S(2)}) collective-permute-start(bf16[16,3200]{1,0:T(8,128)(2,1)S(1)} %get-tuple-element.40.refs_0_), channel_id=1, source_target_pairs={{0,8},{4,12},{8,0},{12,4},{1,9},{5,13},{9,1},{13,5},{2,10},{6,14},... | collective-permute-start | bytes 307208 | tf_op jit(solution)/shard_map/ppermute | solution.py:303
  10.5 8.4 %collective-permute-start.3 = (bf16[16,3072]{1,0:T(8,128)(2,1)S(1)}, bf16[16,3072]{1,0:T(8,128)(2,1)S(1)}, u32[]{:S(2)}, u32[]{:S(2)}) collective-permute-start(bf16[16,3072]{1,0:T(8,128)(2,1)S(1)} %get-tuple-element.42), channel_id=1, source_target_pairs={{0,3},{1,2},{2,1},{3,0},{4,7},{5,6},{6,5},{7,4},{8,11},{9,10},{10,... | collective-permute-start | bytes 294920 | tf_op jit(solution)/shard_map/ppermute | solution.py:303
  10.7 10.7 %collective-permute-start.4 = (bf16[16,3072]{1,0:T(8,128)(2,1)S(1)}, bf16[16,3072]{1,0:T(8,128)(2,1)S(1)}, u32[]{:S(2)}, u32[]{:S(2)}) collective-permute-start(bf16[16,3072]{1,0:T(8,128)(2,1)S(1)} %get-tuple-element.43), channel_id=1, source_target_pairs={{0,2},{1,3},{2,0},{3,1},{4,6},{5,7},{6,4},{7,5},{8,10},{9,11},{10,... | collective-permute-start | bytes 294920 | tf_op jit(solution)/shard_map/ppermute | solution.py:303
  12.4 10.1 %collective-permute-start.5 = (bf16[16,3072]{1,0:T(8,128)(2,1)S(1)}, bf16[16,3072]{1,0:T(8,128)(2,1)S(1)}, u32[]{:S(2)}, u32[]{:S(2)}) collective-permute-start(bf16[16,3072]{1,0:T(8,128)(2,1)S(1)} %get-tuple-element.44), channel_id=1, source_target_pairs={{0,1},{1,0},{2,3},{3,2},{4,5},{5,4},{6,7},{7,6},{8,9},{9,8},{10,11... | collective-permute-start | bytes 294920 | tf_op jit(solution)/shard_map/ppermute | solution.py:303
  19.4 4.1 %collective-permute-start.9 = (bf16[16,1536]{1,0:T(8,128)(2,1)S(1)}, bf16[16,1536]{1,0:T(8,128)(2,1)S(1)}, u32[]{:S(2)}, u32[]{:S(2)}) collective-permute-start(bf16[16,1536]{1,0:T(8,128)(2,1)S(1)} %get-tuple-element.50), channel_id=1, source_target_pairs={{0,3},{1,2},{2,1},{3,0},{4,7},{5,6},{6,5},{7,4},{8,11},{9,10},{10,... | collective-permute-start | bytes 147464 | tf_op jit(solution)/shard_map/ppermute | solution.py:303
  20.1 4.6 %collective-permute-start.10 = (bf16[16,1536]{1,0:T(8,128)(2,1)S(1)}, bf16[16,1536]{1,0:T(8,128)(2,1)S(1)}, u32[]{:S(2)}, u32[]{:S(2)}) collective-permute-start(bf16[16,1536]{1,0:T(8,128)(2,1)S(1)} %get-tuple-element.51), channel_id=1, source_target_pairs={{0,2},{1,3},{2,0},{3,1},{4,6},{5,7},{6,4},{7,5},{8,10},{9,11},{10,... | collective-permute-start | bytes 147464 | tf_op jit(solution)/shard_map/ppermute | solution.py:303
  21.1 3.6 %collective-permute-start.11 = (bf16[16,1536]{1,0:T(8,128)(2,1)S(1)}, bf16[16,1536]{1,0:T(8,128)(2,1)S(1)}, u32[]{:S(2)}, u32[]{:S(2)}) collective-permute-start(bf16[16,1536]{1,0:T(8,128)(2,1)S(1)} %get-tuple-element.52), channel_id=1, source_target_pairs={{0,1},{1,0},{2,3},{3,2},{4,5},{5,4},{6,7},{7,6},{8,9},{9,8},{10,11... | collective-permute-start | bytes 147464 | tf_op jit(solution)/shard_map/ppermute | solution.py:303
  21.3 6.3 %collective-permute-start.6 = (bf16[16,1536]{1,0:T(8,128)(2,1)S(1)}, bf16[16,1536]{1,0:T(8,128)(2,1)S(1)}, u32[]{:S(2)}, u32[]{:S(2)}) collective-permute-start(bf16[16,1536]{1,0:T(8,128)(2,1)S(1)} %get-tuple-element.46), channel_id=1, source_target_pairs={{0,3},{1,2},{2,1},{3,0},{4,7},{5,6},{6,5},{7,4},{8,11},{9,10},{10,... | collective-permute-start | bytes 147464 | tf_op jit(solution)/shard_map/ppermute | solution.py:303
  22.5 5.2 %collective-permute-start.7 = (bf16[16,1536]{1,0:T(8,128)(2,1)S(1)}, bf16[16,1536]{1,0:T(8,128)(2,1)S(1)}, u32[]{:S(2)}, u32[]{:S(2)}) collective-permute-start(bf16[16,1536]{1,0:T(8,128)(2,1)S(1)} %get-tuple-element.47), channel_id=1, source_target_pairs={{0,2},{1,3},{2,0},{3,1},{4,6},{5,7},{6,4},{7,5},{8,10},{9,11},{10,... | collective-permute-start | bytes 147464 | tf_op jit(solution)/shard_map/ppermute | solution.py:303
  23.5 4.2 %collective-permute-start.8 = (bf16[16,1536]{1,0:T(8,128)(2,1)S(1)}, bf16[16,1536]{1,0:T(8,128)(2,1)S(1)}, u32[]{:S(2)}, u32[]{:S(2)}) collective-permute-start(bf16[16,1536]{1,0:T(8,128)(2,1)S(1)} %get-tuple-element.48), channel_id=1, source_target_pairs={{0,1},{1,0},{2,3},{3,2},{4,5},{5,4},{6,7},{7,6},{8,9},{9,8},{10,11... | collective-permute-start | bytes 147464 | tf_op jit(solution)/shard_map/ppermute | solution.py:303
  31.9 7.6 %copy-start = (bf16[3072,4]{0,1:T(4,128)(2,1)S(1)}, bf16[3072,4]{0,1:T(4,128)(2,1)}, u32[]{:S(2)}) copy-start(bf16[3072,4]{0,1:T(4,128)(2,1)} %param.18) | copy-start | bytes 73732
  31.9 5.4 %collective-permute-start.12 = (bf16[32,1536]{1,0:T(8,128)(2,1)S(1)}, bf16[32,1536]{1,0:T(8,128)(2,1)S(1)}, u32[]{:S(2)}, u32[]{:S(2)}) collective-permute-start(bf16[32,1536]{1,0:T(8,128)(2,1)S(1)} %get-tuple-element.57), channel_id=1, source_target_pairs={{0,3},{1,2},{2,1},{3,0},{4,7},{5,6},{6,5},{7,4},{8,11},{9,10},{10,... | collective-permute-start | bytes 294920 | tf_op jit(solution)/shard_map/ppermute | solution.py:303
  32.6 6.8 %collective-permute-start.13 = (bf16[32,1536]{1,0:T(8,128)(2,1)S(1)}, bf16[32,1536]{1,0:T(8,128)(2,1)S(1)}, u32[]{:S(2)}, u32[]{:S(2)}) collective-permute-start(bf16[32,1536]{1,0:T(8,128)(2,1)S(1)} %get-tuple-element.58), channel_id=1, source_target_pairs={{0,2},{1,3},{2,0},{3,1},{4,6},{5,7},{6,4},{7,5},{8,10},{9,11},{10,... | collective-permute-start | bytes 294920 | tf_op jit(solution)/shard_map/ppermute | solution.py:303
  33.7 5.8 %collective-permute-start.14 = (bf16[32,1536]{1,0:T(8,128)(2,1)S(1)}, bf16[32,1536]{1,0:T(8,128)(2,1)S(1)}, u32[]{:S(2)}, u32[]{:S(2)}) collective-permute-start(bf16[32,1536]{1,0:T(8,128)(2,1)S(1)} %get-tuple-element.59), channel_id=1, source_target_pairs={{0,1},{1,0},{2,3},{3,2},{4,5},{5,4},{6,7},{7,6},{8,9},{9,8},{10,11... | collective-permute-start | bytes 294920 | tf_op jit(solution)/shard_map/ppermute | solution.py:303
  35.3 7.4 %collective-permute-start.18 = (bf16[32,1536]{1,0:T(8,128)(2,1)S(1)}, bf16[32,1536]{1,0:T(8,128)(2,1)S(1)}, u32[]{:S(2)}, u32[]{:S(2)}) collective-permute-start(bf16[32,1536]{1,0:T(8,128)(2,1)S(1)} %get-tuple-element.68), channel_id=1, source_target_pairs={{0,3},{1,2},{2,1},{3,0},{4,7},{5,6},{6,5},{7,4},{8,11},{9,10},{10,... | collective-permute-start | bytes 294920 | tf_op jit(solution)/shard_map/ppermute | solution.py:303
  36.3 8.4 %collective-permute-start.19 = (bf16[32,1536]{1,0:T(8,128)(2,1)S(1)}, bf16[32,1536]{1,0:T(8,128)(2,1)S(1)}, u32[]{:S(2)}, u32[]{:S(2)}) collective-permute-start(bf16[32,1536]{1,0:T(8,128)(2,1)S(1)} %get-tuple-element.69), channel_id=1, source_target_pairs={{0,2},{1,3},{2,0},{3,1},{4,6},{5,7},{6,4},{7,5},{8,10},{9,11},{10,... | collective-permute-start | bytes 294920 | tf_op jit(solution)/shard_map/ppermute | solution.py:303
  37.3 7.4 %collective-permute-start.20 = (bf16[32,1536]{1,0:T(8,128)(2,1)S(1)}, bf16[32,1536]{1,0:T(8,128)(2,1)S(1)}, u32[]{:S(2)}, u32[]{:S(2)}) collective-permute-start(bf16[32,1536]{1,0:T(8,128)(2,1)S(1)} %get-tuple-element.70), channel_id=1, source_target_pairs={{0,1},{1,0},{2,3},{3,2},{4,5},{5,4},{6,7},{7,6},{8,9},{9,8},{10,11... | collective-permute-start | bytes 294920 | tf_op jit(solution)/shard_map/ppermute | solution.py:303
  40.2 7.6 %collective-permute-start.15 = (bf16[16,1536]{1,0:T(8,128)(2,1)S(1)}, bf16[16,1536]{1,0:T(8,128)(2,1)S(1)}, u32[]{:S(2)}, u32[]{:S(2)}) collective-permute-start(bf16[16,1536]{1,0:T(8,128)(2,1)S(1)} %get-tuple-element.62), channel_id=1, source_target_pairs={{0,12},{4,8},{8,4},{12,0},{1,13},{5,9},{9,5},{13,1},{2,14},{6,10},... | collective-permute-start | bytes 147464 | tf_op jit(solution)/shard_map/ppermute | solution.py:303
  42.6 7.2 %collective-permute-start.16 = (bf16[16,1536]{1,0:T(8,128)(2,1)S(1)}, bf16[16,1536]{1,0:T(8,128)(2,1)S(1)}, u32[]{:S(2)}, u32[]{:S(2)}) collective-permute-start(bf16[16,1536]{1,0:T(8,128)(2,1)S(1)} %get-tuple-element.63), channel_id=1, source_target_pairs={{0,8},{4,12},{8,0},{12,4},{1,9},{5,13},{9,1},{13,5},{2,10},{6,14},... | collective-permute-start | bytes 147464 | tf_op jit(solution)/shard_map/ppermute | solution.py:303
  42.6 7.2 %collective-permute-start.17 = (bf16[16,1536]{1,0:T(8,128)(2,1)S(1)}, bf16[16,1536]{1,0:T(8,128)(2,1)S(1)}, u32[]{:S(2)}, u32[]{:S(2)}) collective-permute-start(bf16[16,1536]{1,0:T(8,128)(2,1)S(1)} %get-tuple-element.64), channel_id=1, source_target_pairs={{0,4},{4,0},{8,12},{12,8},{1,5},{5,1},{9,13},{13,9},{2,6},{6,2},{1... | collective-permute-start | bytes 147464 | tf_op jit(solution)/shard_map/ppermute | solution.py:303
  45.4 6.4 %collective-permute-start.21 = (bf16[16,1536]{1,0:T(8,128)(2,1)S(1)}, bf16[16,1536]{1,0:T(8,128)(2,1)S(1)}, u32[]{:S(2)}, u32[]{:S(2)}) collective-permute-start(bf16[16,1536]{1,0:T(8,128)(2,1)S(1)} %get-tuple-element.72), channel_id=1, source_target_pairs={{0,12},{4,8},{8,4},{12,0},{1,13},{5,9},{9,5},{13,1},{2,14},{6,10},... | collective-permute-start | bytes 147464 | tf_op jit(solution)/shard_map/ppermute | solution.py:303
  47.8 5.1 %collective-permute-start.22 = (bf16[16,1536]{1,0:T(8,128)(2,1)S(1)}, bf16[16,1536]{1,0:T(8,128)(2,1)S(1)}, u32[]{:S(2)}, u32[]{:S(2)}) collective-permute-start(bf16[16,1536]{1,0:T(8,128)(2,1)S(1)} %get-tuple-element.73), channel_id=1, source_target_pairs={{0,8},{4,12},{8,0},{12,4},{1,9},{5,13},{9,1},{13,5},{2,10},{6,14},... | collective-permute-start | bytes 147464 | tf_op jit(solution)/shard_map/ppermute | solution.py:303
  47.9 5.1 %collective-permute-start.23 = (bf16[16,1536]{1,0:T(8,128)(2,1)S(1)}, bf16[16,1536]{1,0:T(8,128)(2,1)S(1)}, u32[]{:S(2)}, u32[]{:S(2)}) collective-permute-start(bf16[16,1536]{1,0:T(8,128)(2,1)S(1)} %get-tuple-element.74), channel_id=1, source_target_pairs={{0,4},{4,0},{8,12},{12,8},{1,5},{5,1},{9,13},{13,9},{2,6},{6,2},{1... | collective-permute-start | bytes 147464 | tf_op jit(solution)/shard_map/ppermute | solution.py:303

commit v11 on v10

--- a/solution.py
+++ b/solution.py
@@ -21,6 +21,7 @@
 BF16 = jnp.bfloat16
 LIGHT = pl.CostEstimate(flops=0, bytes_accessed=0, transcendentals=0)
 BUSY = pl.CostEstimate(flops=24 * 10**9, bytes_accessed=0, transcendentals=0)
+MID = pl.CostEstimate(flops=2 * 10**9, bytes_accessed=0, transcendentals=0)
 ANY = pl.BlockSpec(memory_space=pl.ANY)
 WHOLE = pl.BlockSpec(memory_space=pltpu.VMEM)
 SCALAR = pl.BlockSpec(memory_space=pltpu.SMEM)
@@ -75,7 +76,7 @@
 
 def attend_kernel(
     _, lengths_hbm, queries_hbm, keys_hbm, values_hbm, routes_hbm, residual_hbm, gain_hbm,
-    stream_ref, payload_ref,
+    stream_ref, first_ref, second_ref,
     lengths_ref, queries_ref, keys_ref, values_ref, routes_ref, residual_ref, gain_ref, sems,
 ):
     batch, window, _ = keys_ref.shape
@@ -163,21 +164,31 @@
     routes = [upright(routes_ref[k : k + 1, :]).astype(F32) for k in range(2)]
     named = jnp.where(lane == 0, routes[0], jnp.where(lane == 1, routes[1], 0.0))
     stream_ref[...] = stream
-    payload_ref[:, :width] = (stream * scale * gain_ref[...]).astype(BF16)
-    payload_ref[:, width:] = named.astype(BF16)
-
-
-def split_kernel(me_ref, *refs, chunks, experts, after):
-    refs = refs[after:]
-    payload = jnp.concatenate([ref[...] for ref in refs[:chunks]], axis=0)
-    outs = refs[chunks:]
-    width = payload.shape[1] - LANES
-    rows, named = payload[:, :width], payload[:, width:]
-    slots = dispatch(me_ref[0], rows, named, chunks, experts)
-    span, part = chunks * CAP, outs[0].shape[1]
-    for i, ref in enumerate(outs):
-        p, e = i // experts, i % experts
-        ref[...] = slots[e * span : (e + 1) * span, p * part : (p + 1) * part].astype(BF16)
+    half = width // 2
+    normed = (stream * scale * gain_ref[...]).astype(BF16)
+    first_ref[:, :half] = normed[:, :half]
+    first_ref[:, half:] = named.astype(BF16)
+    second_ref[...] = normed[:, half:]
+
+
+def pass_kernel(*_):
+    pass
+
+
+def stack(refs):
+    return jnp.concatenate([ref[...] for ref in refs], axis=0)
+
+
+def split_kernel(me_ref, *refs, layers, part):
+    payload = stack(refs[:layers])
+    half = payload.shape[1] - LANES
+    named = payload[:, half:]
+    rows = stack(refs[layers : 2 * layers]) if part else payload[:, :half]
+    outs = refs[(1 + part) * layers :]
+    slots = dispatch(me_ref[0], rows, named, layers, len(outs))
+    span = layers * CAP
+    for e, ref in enumerate(outs):
+        ref[...] = slots[e * span : (e + 1) * span].astype(BF16)
 
 
 def strip_copies(source, begin, target, sems):
@@ -195,12 +206,6 @@
     return copies
 
 
-def load_rows(rows_ref, full, halves, begin):
-    width = rows_ref.shape[1]
-    blocks = [ref[:, begin : begin + width] for ref in full] + [ref[...] for ref in halves]
-    rows_ref[...] = jnp.concatenate([block.astype(F32) for block in blocks], axis=0).astype(BF16)
-
-
 def tiles(count, tile):
     def run(body):
         @pl.loop(0, count // tile, unroll=UNROLL)
@@ -210,19 +215,17 @@
     return run
 
 
-def store_rows(outs, at, value, near):
-    count = outs[0].shape[0] - near
+def store_rows(outs, at, value):
+    span = outs[0].shape[0]
     for e, ref in enumerate(outs):
-        first, second = e * near, len(outs) * near + e * count
-        rows = [value[first : first + near], value[second : second + count]]
-        ref[:, at] = jnp.concatenate(rows, axis=0).astype(BF16)
-
-
-def begin_kernel(*refs, near, far):
-    gate_ref, up_ref, down_hbm, gate_out, up_out, down_out, rows_ref, sems = refs[near + far :]
+        ref[:, at] = value[e * span : (e + 1) * span].astype(BF16)
+
+
+def begin_kernel(*refs, experts):
+    gate_ref, up_ref, down_hbm, gate_out, up_out, down_out, rows_ref, sems = refs[experts:]
     half = rows_ref.shape[1]
     copies = strip_copies(down_hbm, 0, down_out, sems)
-    load_rows(rows_ref, refs[:near], refs[near : near + far], 0)
+    rows_ref[...] = stack(refs[:experts])
     units = gate_ref.shape[1]
 
     @tiles(units, min(TILE, units))
@@ -234,13 +237,13 @@
         copy.wait()
 
 
-def middle_kernel(*refs, near, far):
-    gate_in, up_in, down_in, gate_ref, up_ref, down_hbm = refs[near + far : near + far + 6]
-    outs = refs[near + far + 6 : -4]
+def middle_kernel(*refs, experts):
+    gate_in, up_in, down_in, gate_ref, up_ref, down_hbm = refs[experts : experts + 6]
+    outs = refs[experts + 6 : -4]
     hidden_ref, down_out, rows_ref, sems = refs[-4:]
     half = rows_ref.shape[1]
     copies = strip_copies(down_hbm, half, down_out, sems)
-    load_rows(rows_ref, refs[:near], refs[near : near + far], half)
+    rows_ref[...] = stack(refs[:experts])
     units = gate_ref.shape[1]
 
     @tiles(units, min(TILE, units))
@@ -251,35 +254,36 @@
 
     @tiles(half, min(TILE, half))
     def _(at):
-        store_rows(outs, at, dot(hidden_ref[...], down_in[:, at]), refs[0].shape[0])
+        store_rows(outs, at, dot(hidden_ref[...], down_in[:, at]))
 
     for copy in copies:
         copy.wait()
 
 
-def end_kernel(hidden_ref, down_ref, *outs, near):
+def end_kernel(hidden_ref, down_ref, *outs):
     half = down_ref.shape[1]
 
     @tiles(half, min(TILE, half))
     def _(at):
-        store_rows(outs, at, dot(hidden_ref[...], down_ref[:, at]), near)
-
-
-def mix_kernel(me_ref, router_ref, *refs, layers, columns):
+        store_rows(outs, at, dot(hidden_ref[...], down_ref[:, at]))
+
+
+def mix_kernel(me_ref, router_ref, *refs, layers, part):
     outs, stream_ref = refs[-layers:], refs[-layers - 1]
-    blocks = refs[layers : -layers - 1]
+    blocks = refs[2 * layers : -layers - 1]
     experts = len(blocks)
     order = farthest_first(experts)
-    batch, width = stream_ref.shape
-    payload = jnp.concatenate([ref[...] for ref in refs[:layers]], axis=0)
-    returned = jnp.concatenate([blocks[order.index(e)][...] for e in range(experts)], axis=0)
-    rows, named = payload[:, :width], payload[:, width:]
+    batch, half = outs[0].shape
+    payload = stack(refs[:layers])
+    named = payload[:, half:]
+    rows = jnp.concatenate([payload[:, :half], stack(refs[layers : 2 * layers])], axis=1)
+    returned = stack([blocks[order.index(e)] for e in range(experts)])
     mixed = combine(me_ref[0], rows, named, router_ref[...], returned, layers, experts)
     for j, ref in enumerate(outs):
-        part = mixed[j * batch : (j + 1) * batch]
+        value = mixed[j * batch : (j + 1) * batch]
         if j == 0:
-            part = part + stream_ref[:, columns]
-        ref[...] = part.astype(ref.dtype)
+            value = value + stream_ref[:, part * half : (part + 1) * half]
+        ref[...] = value.astype(ref.dtype)
 
 
 def finish_kernel(*refs, parts):
@@ -339,63 +343,72 @@
     window, depth = cached_values.shape[1:]
     held = [a.shape for a in operands]
     held[3] = (batch, -(-window // LANES) * LANES, depth)
-    stream, payload = pl.pallas_call(
+    half = width // 2
+    stream, *payload = pl.pallas_call(
         attend_kernel,
         in_specs=[SCALAR] + [ANY] * len(operands),
-        out_specs=[WHOLE, WHOLE],
-        out_shape=[shape((batch, width), F32), shape((batch, width + LANES), BF16)],
+        out_specs=[WHOLE] * 3,
+        out_shape=[
+            shape((batch, width), F32), shape((batch, half + LANES), BF16), shape((batch, half), BF16)
+        ],
         scratch_shapes=[pltpu.VMEM(size, a.dtype) for size, a in zip(held, operands)]
         + [pltpu.SemaphoreType.DMA((5 + 2 * (KVH // PAIR),))],
         compiler_params=params(28 * batch * width),
         cost_estimate=LIGHT,
     )(me, *operands)
 
-    chunks = [swap(payload, "attn", j) for j in range(layers)]
-    groups = [[0, 1], list(range(2, layers))]
-    half = width // 2
+    payload = pl.pallas_call(
+        pass_kernel,
+        in_specs=[ANY] * 2,
+        out_specs=[ANY] * 2,
+        out_shape=[shape(block.shape, BF16) for block in payload],
+        input_output_aliases={0: 0, 1: 1},
+        cost_estimate=BUSY,
+        compiler_params=params(0),
+    )(*payload)
+
     order = farthest_first(experts)
-
-    def send(group, columns, after):
-        count, parts = len(group), width // columns
+    chunks, arrived = [], []
+    for part in range(2):
+        came = {j: swap(payload[part], "attn", j) for j in farthest_first(layers)}
+        chunks += [came[j] for j in range(layers)]
         slots = pl.pallas_call(
-            functools.partial(split_kernel, chunks=count, experts=experts, after=len(after)),
-            in_specs=[SCALAR] + [ANY] * len(after) + [WHOLE] * count,
-            out_specs=[WHOLE] * (parts * experts),
-            out_shape=[shape((count * CAP, columns), BF16)] * (parts * experts),
-            cost_estimate=LIGHT if after else BUSY,
-            compiler_params=params(experts * count * CAP * width),
-        )(me, *after, *[chunks[j] for j in group])
-        return [
-            swap(slots[p * experts + e], "expert", e) for p in range(parts) for e in order
-        ]
-
-    near = send(groups[0], width, [])
-    far = send(groups[1], half, near[1:2])
-    total_rows = sum(block.shape[0] for block in near + far[:experts])
+            functools.partial(split_kernel, layers=layers, part=part),
+            in_specs=[SCALAR] + [WHOLE] * len(chunks),
+            out_specs=[WHOLE] * experts,
+            out_shape=[shape((layers * CAP, half), BF16)] * experts,
+            cost_estimate=MID if part else LIGHT,
+            compiler_params=params(experts * layers * CAP * half),
+        )(me, *chunks)
+        arrived.append([swap(slots[e], "expert", e) for e in order])
+
+    total_rows = experts * layers * CAP
     units = gate_proj.shape[2]
-    counts = {"near": experts, "far": experts}
-    sums = pl.pallas_call(
-        functools.partial(begin_kernel, **counts),
-        in_specs=[WHOLE] * (2 * experts + 2) + [ANY],
+    gate, up, down = gate_proj[0], up_proj[0], in_hbm(down_proj[0])
+    rows = pltpu.VMEM((total_rows, half), BF16)
+    strips = pltpu.SemaphoreType.DMA((STRIPS,))
+    halves = [shape((layers * CAP, half), BF16)] * experts
+    *sums, down_first = pl.pallas_call(
+        functools.partial(begin_kernel, experts=experts),
+        in_specs=[WHOLE] * (experts + 2) + [ANY],
         out_specs=[WHOLE] * 3,
         out_shape=[shape((total_rows, units), F32)] * 2 + [pltpu.VMEM((units, half), BF16)],
-        scratch_shapes=[pltpu.VMEM((total_rows, half), BF16), pltpu.SemaphoreType.DMA((STRIPS,))],
+        scratch_shapes=[rows, strips],
         cost_estimate=pl.CostEstimate(
             flops=4 * total_rows * half * units, bytes_accessed=0, transcendentals=0
         ),
         compiler_params=params(total_rows * width),
-    )(*near, *far[:experts], gate_proj[0], up_proj[0], in_hbm(down_proj[0]))
-    halves = [shape((layers * CAP, half), BF16)] * experts
-    *first, hidden, down = pl.pallas_call(
-        functools.partial(middle_kernel, **counts),
-        in_specs=[WHOLE] * (2 * experts + 5) + [ANY],
+    )(*arrived[0], gate, up, down)
+    *first, hidden, down_second = pl.pallas_call(
+        functools.partial(middle_kernel, experts=experts),
+        in_specs=[WHOLE] * (experts + 5) + [ANY],
         out_specs=[WHOLE] * (experts + 2),
         out_shape=halves + [shape((total_rows, units), BF16), pltpu.VMEM((units, half), BF16)],
-        scratch_shapes=[pltpu.VMEM((total_rows, half), BF16), pltpu.SemaphoreType.DMA((STRIPS,))],
+        scratch_shapes=[rows, strips],
         compiler_params=params(total_rows * width),
-    )(*near, *far[experts:], *sums, gate_proj[0], up_proj[0], in_hbm(down_proj[0]))
+    )(*arrived[1], *sums, down_first, gate, up, down)
     second = pl.pallas_call(
-        functools.partial(end_kernel, near=near[0].shape[0]),
+        end_kernel,
         in_specs=[WHOLE] * 2,
         out_specs=[WHOLE] * experts,
         out_shape=halves,
@@ -403,24 +416,19 @@
             flops=2 * total_rows * half * units, bytes_accessed=0, transcendentals=0
         ),
         compiler_params=params(total_rows * width),
-    )(hidden, down)
+    )(hidden, down_second)
 
     sums = []
-    for p, blocks in enumerate((first, second)):
+    for part, blocks in enumerate((first, second)):
         returned = [swap(block, "expert", e) for e, block in zip(order, blocks)]
-        operands = [me, router, *chunks, *returned, stream]
         mixed = pl.pallas_call(
-            functools.partial(
-                mix_kernel,
-                layers=layers,
-                columns=slice(p * half, (p + 1) * half),
-            ),
-            in_specs=[SCALAR] + [WHOLE] * (len(operands) - 1),
+            functools.partial(mix_kernel, layers=layers, part=part),
+            in_specs=[SCALAR] + [WHOLE] * (2 + 2 * layers + experts),
             out_specs=[WHOLE] * layers,
             out_shape=[shape((batch, half), BF16 if j else F32) for j in range(layers)],
             cost_estimate=LIGHT,
             compiler_params=params(experts * layers * CAP * half),
-        )(*operands)
+        )(me, router, *chunks, *returned, stream)
         sums += [swap(mixed[j], "attn", j) for j in farthest_first(layers)]
     return pl.pallas_call(
         functools.partial(finish_kernel, parts=2),

time: 53.8 us -> 53.8 us (level)
  starting transfers between devices: 24.4 us -> 26.7 us
  waiting for transfers between devices: 13.4 us -> 11.1 us
    ppermute x24, waiting for transfers between devices: 13.4 us -> 11.1 us  [swap(): return lax.ppermute(value, axis, [(i, i ^ step) for i in range(count)])]
    ppermute x24, starting transfers between devices: 24.4 us -> 26.7 us  [swap(): return lax.ppermute(value, axis, [(i, i ^ step) for i in range(count)])]
    pallas_call x7 -> x8, Pallas kernels: 10.9 us -> 10.9 us  [the longest x1 4.17 us: shards(): pl.pallas_call(functools.partial(middle_kernel, experts=experts), in_spec...]
where the time goes in v11:
time: 53.8 us; the launch traced here: 53.6 us
  starting transfers between devices  26.7 us (50%)
  Pallas kernels  15.6 us (29%)
  waiting for transfers between devices  11.1 us (21%)
    ppermute x24, starting transfers between devices, swap(): return lax.ppermute(value, axis, [(i, i ^ step) for i in range(count)])  26.7 us
    ppermute x24, waiting for transfers between devices, swap(): return lax.ppermute(value, axis, [(i, i ^ step) for i in range(count)])  11.1 us
    pallas_call x1, Pallas kernels, shards(): pl.pallas_call(functools.partial(middle_kernel, experts=experts), in_spec...  4.17 us
    pallas_call x1, Pallas kernels, shards(): pl.pallas_call(attend_kernel, in_specs=[SCALAR] + [ANY] * len(operands),...  3.99 us
    pallas_call x1, Pallas kernels, shards(): pl.pallas_call(functools.partial(begin_kernel, experts=experts), in_specs...  2.92 us
    pallas_call x2, Pallas kernels, shards(): pl.pallas_call(functools.partial(mix_kernel, layers=layers, part=part), i...  1.46 us
    pallas_call x1, Pallas kernels, shards(): pl.pallas_call(end_kernel, in_specs=[WHOLE] * 2, out_specs=[WHOLE] * expe...  1.37 us
  transfers between devices with their start and end apart: 24, of which 8 were waited for; matrix products, arithmetic and copies ran while one was open for 0% of the time, Pallas kernels for 13%

profile of v11, /device:TPU:0, one launch (start us, length us, event | category | flops | bytes accessed | tf_op | source)
XLA Modules:
  0.0 53.6 jit_solution(16552060186027863051)
XLA Ops:
  0.0 4.0 %shard_map.109 = (f32[16,3072]{1,0:T(8,128)S(1)}, bf16[16,1664]{1,0:T(8,128)(2,1)S(1)}, bf16[16,1536]{1,0:T(8,128)(2,1)S(1)}) custom-call(s32[1]{0:T(128)} %bitcast._.me_ref, s32[1,16]{1,0:T(1,128)} %bitcast.22, bf16[16,3072]{1,0:T(8,128)(2,1)} %queries_hbm.1, bf16[16,96,512]{2,1,0:T(8,128)(2,1)} %keys_hbm.1, bf16[16,96,512]{2,1,0:T(8,128)(2,1)} %values_hbm.1, ...), custom_call_target="tpu_custom_call" | custom-call | tf_op jit(solution)/shard_map/pallas_call | solution.py:347
  4.0 0.0 slice-start
  4.0 0.0 slice-start.3
  4.0 0.0 slice-start.1
  4.0 0.0 slice-start.2
  4.0 0.0 slice-start.4
  4.1 0.0 slice-start.5
  4.1 5.1 %collective-permute-start.2 = (bf16[16,1664]{1,0:T(8,128)(2,1)S(1)}, bf16[16,1664]{1,0:T(8,128)(2,1)S(1)}, u32[]{:S(2)}, u32[]{:S(2)}) collective-permute-start(bf16[16,1664]{1,0:T(8,128)(2,1)S(1)} %get-tuple-element.41.refs_0_), channel_id=1, source_target_pairs={{0,12},{4,8},{8,4},{12,0},{1,13},{5,9},{9,5},{13,1},{2,14},{6,10},... | collective-permute-start | bytes 159752 | tf_op jit(solution)/shard_map/ppermute | solution.py:307
  9.2 0.0 collective-permute-start.1
  9.2 0.6 %collective-permute-start = (bf16[16,1664]{1,0:T(8,128)(2,1)S(1)}, bf16[16,1664]{1,0:T(8,128)(2,1)S(1)}, u32[]{:S(2)}, u32[]{:S(2)}) collective-permute-start(bf16[16,1664]{1,0:T(8,128)(2,1)S(1)} %get-tuple-element.41.refs_0_), channel_id=1, source_target_pairs={{0,4},{4,0},{8,12},{12,8},{1,5},{5,1},{9,13},{13,9},{2,6},{6,2},{1... | collective-permute-start | bytes 159752 | tf_op jit(solution)/shard_map/ppermute | solution.py:307
  9.8 3.7 %collective-permute-start.5 = (bf16[16,1536]{1,0:T(8,128)(2,1)S(1)}, bf16[16,1536]{1,0:T(8,128)(2,1)S(1)}, u32[]{:S(2)}, u32[]{:S(2)}) collective-permute-start(bf16[16,1536]{1,0:T(8,128)(2,1)S(1)} %get-tuple-element.42.refs_4_), channel_id=1, source_target_pairs={{0,12},{4,8},{8,4},{12,0},{1,13},{5,9},{9,5},{13,1},{2,14},{6,10},... | collective-permute-start | bytes 147464 | tf_op jit(solution)/shard_map/ppermute | solution.py:307
  13.6 0.0 collective-permute-start.4
  13.6 0.0 collective-permute-done.2.refs_3_
  13.6 0.6 %collective-permute-start.3 = (bf16[16,1536]{1,0:T(8,128)(2,1)S(1)}, bf16[16,1536]{1,0:T(8,128)(2,1)S(1)}, u32[]{:S(2)}, u32[]{:S(2)}) collective-permute-start(bf16[16,1536]{1,0:T(8,128)(2,1)S(1)} %get-tuple-element.42.refs_4_), channel_id=1, source_target_pairs={{0,4},{4,0},{8,12},{12,8},{1,5},{5,1},{9,13},{13,9},{2,6},{6,2},{1... | collective-permute-start | bytes 147464 | tf_op jit(solution)/shard_map/ppermute | solution.py:307
  14.2 1.4 %collective-permute-done.1.refs_2_ = bf16[16,1664]{1,0:T(8,128)(2,1)S(1)} collective-permute-done((bf16[16,1664]{1,0:T(8,128)(2,1)S(1)}, bf16[16,1664]{1,0:T(8,128)(2,1)S(1)}, u32[]{:S(2)}, u32[]{:S(2)}) %collective-permute-start.1) | collective-permute-done | bytes 53280 | tf_op jit(solution)/shard_map/ppermute | solution.py:307
  15.6 0.0 collective-permute-done.refs_1_
  15.6 0.5 shard_map.112
  16.1 0.1 collective-permute-start.9
  16.2 1.6 %collective-permute-start.10 = (bf16[32,1536]{1,0:T(8,128)(2,1)S(1)}, bf16[32,1536]{1,0:T(8,128)(2,1)S(1)}, u32[]{:S(2)}, u32[]{:S(2)}) collective-permute-start(bf16[32,1536]{1,0:T(8,128)(2,1)S(1)} %get-tuple-element.49), channel_id=1, source_target_pairs={{0,2},{1,3},{2,0},{3,1},{4,6},{5,7},{6,4},{7,5},{8,10},{9,11},{10,... | collective-permute-start | bytes 294920 | tf_op jit(solution)/shard_map/ppermute | solution.py:307
  17.8 0.0 collective-permute-done.5.refs_7_
  17.8 0.3 collective-permute-start.11
  18.1 0.5 collective-permute-done.4.refs_6_
  18.6 0.0 collective-permute-done.3.refs_5_
  18.6 0.5 shard_map.111
  19.1 0.7 %collective-permute-start.6 = (bf16[32,1536]{1,0:T(8,128)(2,1)S(1)}, bf16[32,1536]{1,0:T(8,128)(2,1)S(1)}, u32[]{:S(2)}, u32[]{:S(2)}) collective-permute-start(bf16[32,1536]{1,0:T(8,128)(2,1)S(1)} %get-tuple-element.44), channel_id=1, source_target_pairs={{0,3},{1,2},{2,1},{3,0},{4,7},{5,6},{6,5},{7,4},{8,11},{9,10},{10,... | collective-permute-start | bytes 294920 | tf_op jit(solution)/shard_map/ppermute | solution.py:307
  19.7 1.0 %collective-permute-start.7 = (bf16[32,1536]{1,0:T(8,128)(2,1)S(1)}, bf16[32,1536]{1,0:T(8,128)(2,1)S(1)}, u32[]{:S(2)}, u32[]{:S(2)}) collective-permute-start(bf16[32,1536]{1,0:T(8,128)(2,1)S(1)} %get-tuple-element.45), channel_id=1, source_target_pairs={{0,2},{1,3},{2,0},{3,1},{4,6},{5,7},{6,4},{7,5},{8,10},{9,11},{10,... | collective-permute-start | bytes 294920 | tf_op jit(solution)/shard_map/ppermute | solution.py:307
  20.7 0.5 collective-permute-done.9.refs_1_
  21.2 0.1 collective-permute-start.8
  21.3 2.1 %collective-permute-done.10.refs_2_ = bf16[32,1536]{1,0:T(8,128)(2,1)S(1)} collective-permute-done((bf16[32,1536]{1,0:T(8,128)(2,1)S(1)}, bf16[32,1536]{1,0:T(8,128)(2,1)S(1)}, u32[]{:S(2)}, u32[]{:S(2)}) %collective-permute-start.10) | collective-permute-done | bytes 98336 | tf_op jit(solution)/shard_map/ppermute | solution.py:307
  23.4 0.0 collective-permute-done.11.refs_3_
  23.5 2.9 %shard_map.113 = (f32[128,2048]{1,0:T(8,128)S(1)}, f32[128,2048]{1,0:T(8,128)S(1)}, bf16[2048,1536]{1,0:T(8,128)(2,1)S(1)}) custom-call(bf16[32,1536]{1,0:T(8,128)(2,1)S(1)} %get-tuple-element.47.refs_0_, bf16[32,1536]{1,0:T(8,128)(2,1)S(1)} %collective-permute-done.9.refs_1_, bf16[32,1536]{1,0:T(8,128)(2,1)S(1)} %collective-permute-done.10.refs_2_, ...), custom_call_target="tpu_custom_call" | custom-call | flops 1610612736 | tf_op jit(solution)/shard_map/pallas_call | solution.py:391
  26.4 0.0 collective-permute-done.6.refs_1_
  26.4 1.2 %collective-permute-done.7.refs_2_ = bf16[32,1536]{1,0:T(8,128)(2,1)S(1)} collective-permute-done((bf16[32,1536]{1,0:T(8,128)(2,1)S(1)}, bf16[32,1536]{1,0:T(8,128)(2,1)S(1)}, u32[]{:S(2)}, u32[]{:S(2)}) %collective-permute-start.7) | collective-permute-done | bytes 98336 | tf_op jit(solution)/shard_map/ppermute | solution.py:307
  27.6 0.0 collective-permute-done.8.refs_3_
  27.6 4.2 %shard_map.114 = (bf16[32,1536]{1,0:T(8,128)(2,1)S(1)}, bf16[32,1536]{1,0:T(8,128)(2,1)S(1)}, bf16[32,1536]{1,0:T(8,128)(2,1)S(1)}, bf16[32,1536]{1,0:T(8,128)(2...) custom-call(bf16[32,1536]{1,0:T(8,128)(2,1)S(1)} %get-tuple-element.43.refs_0_, ...), custom_call_target="tpu_custom_call" | custom-call | tf_op jit(solution)/shard_map/pallas_call | solution.py:402
  31.8 0.0 copy-start
  31.8 0.1 collective-permute-start.12
  31.9 1.7 %collective-permute-start.13 = (bf16[32,1536]{1,0:T(8,128)(2,1)S(1)}, bf16[32,1536]{1,0:T(8,128)(2,1)S(1)}, u32[]{:S(2)}, u32[]{:S(2)}) collective-permute-start(bf16[32,1536]{1,0:T(8,128)(2,1)S(1)} %get-tuple-element.56), channel_id=1, source_target_pairs={{0,2},{1,3},{2,0},{3,1},{4,6},{5,7},{6,4},{7,5},{8,10},{9,11},{10,... | collective-permute-start | bytes 294920 | tf_op jit(solution)/shard_map/ppermute | solution.py:307
  33.6 0.2 collective-permute-start.14
  33.7 1.4 %shard_map.116 = (bf16[32,1536]{1,0:T(8,128)(2,1)S(1)}, bf16[32,1536]{1,0:T(8,128)(2,1)S(1)}, bf16[32,1536]{1,0:T(8,128)(2,1)S(1)}, bf16[32,1536]{1,0:T(8,128)(2,1)S(1)}) custom-call(bf16[128,2048]{1,0:T(8,128)(2,1)S(1)} %get-tuple-element.63.hidden_ref, bf16[2048,1536]{1,0:T(8,128)(2,1)S(1)} %get-tuple-element.64.down_ref), custom_call_target="tpu_custom_call" | custom-call | flops 805306368 | tf_op jit(solution)/shard_map/pallas_call | solution.py:410
  35.1 0.4 collective-permute-start.18
  35.5 1.6 %collective-permute-start.19 = (bf16[32,1536]{1,0:T(8,128)(2,1)S(1)}, bf16[32,1536]{1,0:T(8,128)(2,1)S(1)}, u32[]{:S(2)}, u32[]{:S(2)}) collective-permute-start(bf16[32,1536]{1,0:T(8,128)(2,1)S(1)} %get-tuple-element.67), channel_id=1, source_target_pairs={{0,2},{1,3},{2,0},{3,1},{4,6},{5,7},{6,4},{7,5},{8,10},{9,11},{10,... | collective-permute-start | bytes 294920 | tf_op jit(solution)/shard_map/ppermute | solution.py:307
  37.2 0.0 collective-permute-done.12.refs_9_
  37.2 0.0 collective-permute-start.20
  37.2 2.2 %collective-permute-done.13.refs_10_ = bf16[32,1536]{1,0:T(8,128)(2,1)S(1)} collective-permute-done((bf16[32,1536]{1,0:T(8,128)(2,1)S(1)}, bf16[32,1536]{1,0:T(8,128)(2,1)S(1)}, u32[]{:S(2)}, u32[]{:S(2)}) %collective-permute-start.13) | collective-permute-done | bytes 98336 | tf_op jit(solution)/shard_map/ppermute | solution.py:307
  39.3 0.0 collective-permute-done.14.refs_11_
  39.3 0.7 %shard_map.115 = (f32[16,1536]{1,0:T(8,128)S(1)}, bf16[16,1536]{1,0:T(8,128)(2,1)S(1)}, bf16[16,1536]{1,0:T(8,128)(2,1)S(1)}, bf16[16,1536]{1,0:T(8,128)(2,1)S(1)}) custom-call(s32[1]{0:T(128)} %bitcast._.me_ref, bf16[4,3072]{1,0:T(4,128)(2,1)S(1)} %bitcast.16, bf16[16,1664]{1,0:T(8,128)(2,1)S(1)} %get-tuple-element.41.refs_0_, ...), custom_call_target="tpu_custom_call" | custom-call | tf_op jit(solution)/shard_map/pallas_call | solution.py:424
  40.1 2.7 %collective-permute-start.15 = (bf16[16,1536]{1,0:T(8,128)(2,1)S(1)}, bf16[16,1536]{1,0:T(8,128)(2,1)S(1)}, u32[]{:S(2)}, u32[]{:S(2)}) collective-permute-start(bf16[16,1536]{1,0:T(8,128)(2,1)S(1)} %get-tuple-element.60), channel_id=1, source_target_pairs={{0,12},{4,8},{8,4},{12,0},{1,13},{5,9},{9,5},{13,1},{2,14},{6,10},... | collective-permute-start | bytes 147464 | tf_op jit(solution)/shard_map/ppermute | solution.py:307
  42.8 0.0 collective-permute-start.16
  42.8 0.0 collective-permute-done.18.refs_9_
  42.8 1.8 %collective-permute-start.17 = (bf16[16,1536]{1,0:T(8,128)(2,1)S(1)}, bf16[16,1536]{1,0:T(8,128)(2,1)S(1)}, u32[]{:S(2)}, u32[]{:S(2)}) collective-permute-start(bf16[16,1536]{1,0:T(8,128)(2,1)S(1)} %get-tuple-element.62), channel_id=1, source_target_pairs={{0,4},{4,0},{8,12},{12,8},{1,5},{5,1},{9,13},{13,9},{2,6},{6,2},{1... | collective-permute-start | bytes 147464 | tf_op jit(solution)/shard_map/ppermute | solution.py:307
  44.5 0.0 collective-permute-done.19.refs_10_
  44.5 0.0 collective-permute-done.20.refs_11_
  44.5 0.7 %shard_map.117 = (f32[16,1536]{1,0:T(8,128)S(1)}, bf16[16,1536]{1,0:T(8,128)(2,1)S(1)}, bf16[16,1536]{1,0:T(8,128)(2,1)S(1)}, bf16[16,1536]{1,0:T(8,128)(2,1)S(1)}) custom-call(s32[1]{0:T(128)} %bitcast._.me_ref, bf16[4,3072]{1,0:T(4,128)(2,1)S(1)} %bitcast.17, bf16[16,1664]{1,0:T(8,128)(2,1)S(1)} %get-tuple-element.41.refs_0_, ...), custom_call_target="tpu_custom_call" | custom-call | tf_op jit(solution)/shard_map/pallas_call | solution.py:424
  45.3 2.7 %collective-permute-start.21 = (bf16[16,1536]{1,0:T(8,128)(2,1)S(1)}, bf16[16,1536]{1,0:T(8,128)(2,1)S(1)}, u32[]{:S(2)}, u32[]{:S(2)}) collective-permute-start(bf16[16,1536]{1,0:T(8,128)(2,1)S(1)} %get-tuple-element.70), channel_id=1, source_target_pairs={{0,12},{4,8},{8,4},{12,0},{1,13},{5,9},{9,5},{13,1},{2,14},{6,10},... | collective-permute-start | bytes 147464 | tf_op jit(solution)/shard_map/ppermute | solution.py:307
  48.0 0.0 collective-permute-start.22
  48.0 0.0 collective-permute-done.15.refs_1_
  48.0 1.8 %collective-permute-start.23 = (bf16[16,1536]{1,0:T(8,128)(2,1)S(1)}, bf16[16,1536]{1,0:T(8,128)(2,1)S(1)}, u32[]{:S(2)}, u32[]{:S(2)}) collective-permute-start(bf16[16,1536]{1,0:T(8,128)(2,1)S(1)} %get-tuple-element.72), channel_id=1, source_target_pairs={{0,4},{4,0},{8,12},{12,8},{1,5},{5,1},{9,13},{13,9},{2,6},{6,2},{1... | collective-permute-start | bytes 147464 | tf_op jit(solution)/shard_map/ppermute | solution.py:307
  49.7 0.0 collective-permute-done.16.refs_2_
  49.7 0.0 collective-permute-done.17.refs_3_
  49.7 1.6 %collective-permute-done.21.refs_5_ = bf16[16,1536]{1,0:T(8,128)(2,1)S(1)} collective-permute-done((bf16[16,1536]{1,0:T(8,128)(2,1)S(1)}, bf16[16,1536]{1,0:T(8,128)(2,1)S(1)}, u32[]{:S(2)}, u32[]{:S(2)}) %collective-permute-start.21) | collective-permute-done | bytes 49184 | tf_op jit(solution)/shard_map/ppermute | solution.py:307
  51.3 1.6 %collective-permute-done.22.refs_6_ = bf16[16,1536]{1,0:T(8,128)(2,1)S(1)} collective-permute-done((bf16[16,1536]{1,0:T(8,128)(2,1)S(1)}, bf16[16,1536]{1,0:T(8,128)(2,1)S(1)}, u32[]{:S(2)}, u32[]{:S(2)}) %collective-permute-start.22) | collective-permute-done | bytes 49184 | tf_op jit(solution)/shard_map/ppermute | solution.py:307
  52.9 0.0 collective-permute-done.23.refs_7_
  53.0 0.7 %shard_map.118 = bf16[16,3072]{1,0:T(8,128)(2,1)} custom-call(f32[16,1536]{1,0:T(8,128)S(1)} %get-tuple-element.59.refs_0_, bf16[16,1536]{1,0:T(8,128)(2,1)S(1)} %collective-permute-done.15.refs_1_, bf16[16,1536]{1,0:T(8,128)(2,1)S(1)} %collective-permute-done.16.refs_2_, bf16[16,1536]{1,0:T(8,128)(2,1)S(1)} %collective-permute-done.17.refs_3_, ...), custom_call_target="tpu_custom_call" | custom-call | tf_op jit(solution)/shard_map/pallas_call | solution.py:433
  (10 shorter events, 0.0 us)
Async XLA Ops:
  4.0 19.4 %slice-start = ((s8[12582912]{0:T(1024)(128)(4,1)}), s8[4194304]{0:T(1024)(128)(4,1)S(1)}, s32[]{:S(2)}) async-start(s8[12582912]{0:T(1024)(128)(4,1)} %bitcast.8), calls=%async_computation | async-start | bytes 8388608
  4.0 19.4 %slice-start.3 = ((s8[12582912]{0:T(1024)(128)(4,1)}), s8[4194304]{0:T(1024)(128)(4,1)S(1)}, s32[]{:S(2)}) async-start(s8[12582912]{0:T(1024)(128)(4,1)} %bitcast.12), calls=%async_computation.3 | async-start | bytes 8388608
  4.0 19.4 %slice-start.1 = ((s8[12582912]{0:T(1024)(128)(4,1)}), s8[4194304]{0:T(1024)(128)(4,1)S(1)}, s32[]{:S(2)}) async-start(s8[12582912]{0:T(1024)(128)(4,1)} %bitcast.8), calls=%async_computation.1 | async-start | bytes 8388608
  4.0 19.4 %slice-start.2 = ((s8[12582912]{0:T(1024)(128)(4,1)}), s8[4194304]{0:T(1024)(128)(4,1)S(1)}, s32[]{:S(2)}) async-start(s8[12582912]{0:T(1024)(128)(4,1)} %bitcast.8), calls=%async_computation.2 | async-start | bytes 8388608
  4.0 19.4 %slice-start.4 = ((s8[12582912]{0:T(1024)(128)(4,1)}), s8[4194304]{0:T(1024)(128)(4,1)S(1)}, s32[]{:S(2)}) async-start(s8[12582912]{0:T(1024)(128)(4,1)} %bitcast.12), calls=%async_computation.4 | async-start | bytes 8388608
  4.1 19.4 %slice-start.5 = ((s8[12582912]{0:T(1024)(128)(4,1)}), s8[4194304]{0:T(1024)(128)(4,1)S(1)}, s32[]{:S(2)}) async-start(s8[12582912]{0:T(1024)(128)(4,1)} %bitcast.12), calls=%async_computation.5 | async-start | bytes 8388608
  4.1 9.5 %collective-permute-start.2 = (bf16[16,1664]{1,0:T(8,128)(2,1)S(1)}, bf16[16,1664]{1,0:T(8,128)(2,1)S(1)}, u32[]{:S(2)}, u32[]{:S(2)}) collective-permute-start(bf16[16,1664]{1,0:T(8,128)(2,1)S(1)} %get-tuple-element.41.refs_0_), channel_id=1, source_target_pairs={{0,12},{4,8},{8,4},{12,0},{1,13},{5,9},{9,5},{13,1},{2,14},{6,10},... | collective-permute-start | bytes 159752 | tf_op jit(solution)/shard_map/ppermute | solution.py:307
  9.2 6.4 %collective-permute-start.1 = (bf16[16,1664]{1,0:T(8,128)(2,1)S(1)}, bf16[16,1664]{1,0:T(8,128)(2,1)S(1)}, u32[]{:S(2)}, u32[]{:S(2)}) collective-permute-start(bf16[16,1664]{1,0:T(8,128)(2,1)S(1)} %get-tuple-element.41.refs_0_), channel_id=1, source_target_pairs={{0,8},{4,12},{8,0},{12,4},{1,9},{5,13},{9,1},{13,5},{2,10},{6,14},... | collective-permute-start | bytes 159752 | tf_op jit(solution)/shard_map/ppermute | solution.py:307
  9.2 6.4 %collective-permute-start = (bf16[16,1664]{1,0:T(8,128)(2,1)S(1)}, bf16[16,1664]{1,0:T(8,128)(2,1)S(1)}, u32[]{:S(2)}, u32[]{:S(2)}) collective-permute-start(bf16[16,1664]{1,0:T(8,128)(2,1)S(1)} %get-tuple-element.41.refs_0_), channel_id=1, source_target_pairs={{0,4},{4,0},{8,12},{12,8},{1,5},{5,1},{9,13},{13,9},{2,6},{6,2},{1... | collective-permute-start | bytes 159752 | tf_op jit(solution)/shard_map/ppermute | solution.py:307
  9.8 7.9 %collective-permute-start.5 = (bf16[16,1536]{1,0:T(8,128)(2,1)S(1)}, bf16[16,1536]{1,0:T(8,128)(2,1)S(1)}, u32[]{:S(2)}, u32[]{:S(2)}) collective-permute-start(bf16[16,1536]{1,0:T(8,128)(2,1)S(1)} %get-tuple-element.42.refs_4_), channel_id=1, source_target_pairs={{0,12},{4,8},{8,4},{12,0},{1,13},{5,9},{9,5},{13,1},{2,14},{6,10},... | collective-permute-start | bytes 147464 | tf_op jit(solution)/shard_map/ppermute | solution.py:307
  13.6 5.0 %collective-permute-start.4 = (bf16[16,1536]{1,0:T(8,128)(2,1)S(1)}, bf16[16,1536]{1,0:T(8,128)(2,1)S(1)}, u32[]{:S(2)}, u32[]{:S(2)}) collective-permute-start(bf16[16,1536]{1,0:T(8,128)(2,1)S(1)} %get-tuple-element.42.refs_4_), channel_id=1, source_target_pairs={{0,8},{4,12},{8,0},{12,4},{1,9},{5,13},{9,1},{13,5},{2,10},{6,14},... | collective-permute-start | bytes 147464 | tf_op jit(solution)/shard_map/ppermute | solution.py:307
  13.6 5.0 %collective-permute-start.3 = (bf16[16,1536]{1,0:T(8,128)(2,1)S(1)}, bf16[16,1536]{1,0:T(8,128)(2,1)S(1)}, u32[]{:S(2)}, u32[]{:S(2)}) collective-permute-start(bf16[16,1536]{1,0:T(8,128)(2,1)S(1)} %get-tuple-element.42.refs_4_), channel_id=1, source_target_pairs={{0,4},{4,0},{8,12},{12,8},{1,5},{5,1},{9,13},{13,9},{2,6},{6,2},{1... | collective-permute-start | bytes 147464 | tf_op jit(solution)/shard_map/ppermute | solution.py:307
  16.1 5.1 %collective-permute-start.9 = (bf16[32,1536]{1,0:T(8,128)(2,1)S(1)}, bf16[32,1536]{1,0:T(8,128)(2,1)S(1)}, u32[]{:S(2)}, u32[]{:S(2)}) collective-permute-start(bf16[32,1536]{1,0:T(8,128)(2,1)S(1)} %get-tuple-element.48), channel_id=1, source_target_pairs={{0,3},{1,2},{2,1},{3,0},{4,7},{5,6},{6,5},{7,4},{8,11},{9,10},{10,... | collective-permute-start | bytes 294920 | tf_op jit(solution)/shard_map/ppermute | solution.py:307
  16.2 7.2 %collective-permute-start.10 = (bf16[32,1536]{1,0:T(8,128)(2,1)S(1)}, bf16[32,1536]{1,0:T(8,128)(2,1)S(1)}, u32[]{:S(2)}, u32[]{:S(2)}) collective-permute-start(bf16[32,1536]{1,0:T(8,128)(2,1)S(1)} %get-tuple-element.49), channel_id=1, source_target_pairs={{0,2},{1,3},{2,0},{3,1},{4,6},{5,7},{6,4},{7,5},{8,10},{9,11},{10,... | collective-permute-start | bytes 294920 | tf_op jit(solution)/shard_map/ppermute | solution.py:307
  17.8 5.7 %collective-permute-start.11 = (bf16[32,1536]{1,0:T(8,128)(2,1)S(1)}, bf16[32,1536]{1,0:T(8,128)(2,1)S(1)}, u32[]{:S(2)}, u32[]{:S(2)}) collective-permute-start(bf16[32,1536]{1,0:T(8,128)(2,1)S(1)} %get-tuple-element.50), channel_id=1, source_target_pairs={{0,1},{1,0},{2,3},{3,2},{4,5},{5,4},{6,7},{7,6},{8,9},{9,8},{10,11... | collective-permute-start | bytes 294920 | tf_op jit(solution)/shard_map/ppermute | solution.py:307
  19.1 7.4 %collective-permute-start.6 = (bf16[32,1536]{1,0:T(8,128)(2,1)S(1)}, bf16[32,1536]{1,0:T(8,128)(2,1)S(1)}, u32[]{:S(2)}, u32[]{:S(2)}) collective-permute-start(bf16[32,1536]{1,0:T(8,128)(2,1)S(1)} %get-tuple-element.44), channel_id=1, source_target_pairs={{0,3},{1,2},{2,1},{3,0},{4,7},{5,6},{6,5},{7,4},{8,11},{9,10},{10,... | collective-permute-start | bytes 294920 | tf_op jit(solution)/shard_map/ppermute | solution.py:307
  19.7 7.9 %collective-permute-start.7 = (bf16[32,1536]{1,0:T(8,128)(2,1)S(1)}, bf16[32,1536]{1,0:T(8,128)(2,1)S(1)}, u32[]{:S(2)}, u32[]{:S(2)}) collective-permute-start(bf16[32,1536]{1,0:T(8,128)(2,1)S(1)} %get-tuple-element.45), channel_id=1, source_target_pairs={{0,2},{1,3},{2,0},{3,1},{4,6},{5,7},{6,4},{7,5},{8,10},{9,11},{10,... | collective-permute-start | bytes 294920 | tf_op jit(solution)/shard_map/ppermute | solution.py:307
  21.2 6.4 %collective-permute-start.8 = (bf16[32,1536]{1,0:T(8,128)(2,1)S(1)}, bf16[32,1536]{1,0:T(8,128)(2,1)S(1)}, u32[]{:S(2)}, u32[]{:S(2)}) collective-permute-start(bf16[32,1536]{1,0:T(8,128)(2,1)S(1)} %get-tuple-element.46), channel_id=1, source_target_pairs={{0,1},{1,0},{2,3},{3,2},{4,5},{5,4},{6,7},{7,6},{8,9},{9,8},{10,11... | collective-permute-start | bytes 294920 | tf_op jit(solution)/shard_map/ppermute | solution.py:307
  31.8 7.5 %copy-start = (bf16[3072,4]{0,1:T(4,128)(2,1)S(1)}, bf16[3072,4]{0,1:T(4,128)(2,1)}, u32[]{:S(2)}) copy-start(bf16[3072,4]{0,1:T(4,128)(2,1)} %param.18) | copy-start | bytes 73732
  31.8 5.4 %collective-permute-start.12 = (bf16[32,1536]{1,0:T(8,128)(2,1)S(1)}, bf16[32,1536]{1,0:T(8,128)(2,1)S(1)}, u32[]{:S(2)}, u32[]{:S(2)}) collective-permute-start(bf16[32,1536]{1,0:T(8,128)(2,1)S(1)} %get-tuple-element.55), channel_id=1, source_target_pairs={{0,3},{1,2},{2,1},{3,0},{4,7},{5,6},{6,5},{7,4},{8,11},{9,10},{10,... | collective-permute-start | bytes 294920 | tf_op jit(solution)/shard_map/ppermute | solution.py:307
  31.9 7.4 %collective-permute-start.13 = (bf16[32,1536]{1,0:T(8,128)(2,1)S(1)}, bf16[32,1536]{1,0:T(8,128)(2,1)S(1)}, u32[]{:S(2)}, u32[]{:S(2)}) collective-permute-start(bf16[32,1536]{1,0:T(8,128)(2,1)S(1)} %get-tuple-element.56), channel_id=1, source_target_pairs={{0,2},{1,3},{2,0},{3,1},{4,6},{5,7},{6,4},{7,5},{8,10},{9,11},{10,... | collective-permute-start | bytes 294920 | tf_op jit(solution)/shard_map/ppermute | solution.py:307
  33.6 5.8 %collective-permute-start.14 = (bf16[32,1536]{1,0:T(8,128)(2,1)S(1)}, bf16[32,1536]{1,0:T(8,128)(2,1)S(1)}, u32[]{:S(2)}, u32[]{:S(2)}) collective-permute-start(bf16[32,1536]{1,0:T(8,128)(2,1)S(1)} %get-tuple-element.57), channel_id=1, source_target_pairs={{0,1},{1,0},{2,3},{3,2},{4,5},{5,4},{6,7},{7,6},{8,9},{9,8},{10,11... | collective-permute-start | bytes 294920 | tf_op jit(solution)/shard_map/ppermute | solution.py:307
  35.1 7.7 %collective-permute-start.18 = (bf16[32,1536]{1,0:T(8,128)(2,1)S(1)}, bf16[32,1536]{1,0:T(8,128)(2,1)S(1)}, u32[]{:S(2)}, u32[]{:S(2)}) collective-permute-start(bf16[32,1536]{1,0:T(8,128)(2,1)S(1)} %get-tuple-element.66), channel_id=1, source_target_pairs={{0,3},{1,2},{2,1},{3,0},{4,7},{5,6},{6,5},{7,4},{8,11},{9,10},{10,... | collective-permute-start | bytes 294920 | tf_op jit(solution)/shard_map/ppermute | solution.py:307
  35.5 9.0 %collective-permute-start.19 = (bf16[32,1536]{1,0:T(8,128)(2,1)S(1)}, bf16[32,1536]{1,0:T(8,128)(2,1)S(1)}, u32[]{:S(2)}, u32[]{:S(2)}) collective-permute-start(bf16[32,1536]{1,0:T(8,128)(2,1)S(1)} %get-tuple-element.67), channel_id=1, source_target_pairs={{0,2},{1,3},{2,0},{3,1},{4,6},{5,7},{6,4},{7,5},{8,10},{9,11},{10,... | collective-permute-start | bytes 294920 | tf_op jit(solution)/shard_map/ppermute | solution.py:307
  37.2 7.4 %collective-permute-start.20 = (bf16[32,1536]{1,0:T(8,128)(2,1)S(1)}, bf16[32,1536]{1,0:T(8,128)(2,1)S(1)}, u32[]{:S(2)}, u32[]{:S(2)}) collective-permute-start(bf16[32,1536]{1,0:T(8,128)(2,1)S(1)} %get-tuple-element.68), channel_id=1, source_target_pairs={{0,1},{1,0},{2,3},{3,2},{4,5},{5,4},{6,7},{7,6},{8,9},{9,8},{10,11... | collective-permute-start | bytes 294920 | tf_op jit(solution)/shard_map/ppermute | solution.py:307
  40.1 7.9 %collective-permute-start.15 = (bf16[16,1536]{1,0:T(8,128)(2,1)S(1)}, bf16[16,1536]{1,0:T(8,128)(2,1)S(1)}, u32[]{:S(2)}, u32[]{:S(2)}) collective-permute-start(bf16[16,1536]{1,0:T(8,128)(2,1)S(1)} %get-tuple-element.60), channel_id=1, source_target_pairs={{0,12},{4,8},{8,4},{12,0},{1,13},{5,9},{9,5},{13,1},{2,14},{6,10},... | collective-permute-start | bytes 147464 | tf_op jit(solution)/shard_map/ppermute | solution.py:307
  42.8 7.0 %collective-permute-start.16 = (bf16[16,1536]{1,0:T(8,128)(2,1)S(1)}, bf16[16,1536]{1,0:T(8,128)(2,1)S(1)}, u32[]{:S(2)}, u32[]{:S(2)}) collective-permute-start(bf16[16,1536]{1,0:T(8,128)(2,1)S(1)} %get-tuple-element.61), channel_id=1, source_target_pairs={{0,8},{4,12},{8,0},{12,4},{1,9},{5,13},{9,1},{13,5},{2,10},{6,14},... | collective-permute-start | bytes 147464 | tf_op jit(solution)/shard_map/ppermute | solution.py:307
  42.8 7.0 %collective-permute-start.17 = (bf16[16,1536]{1,0:T(8,128)(2,1)S(1)}, bf16[16,1536]{1,0:T(8,128)(2,1)S(1)}, u32[]{:S(2)}, u32[]{:S(2)}) collective-permute-start(bf16[16,1536]{1,0:T(8,128)(2,1)S(1)} %get-tuple-element.62), channel_id=1, source_target_pairs={{0,4},{4,0},{8,12},{12,8},{1,5},{5,1},{9,13},{13,9},{2,6},{6,2},{1... | collective-permute-start | bytes 147464 | tf_op jit(solution)/shard_map/ppermute | solution.py:307
  45.3 6.1 %collective-permute-start.21 = (bf16[16,1536]{1,0:T(8,128)(2,1)S(1)}, bf16[16,1536]{1,0:T(8,128)(2,1)S(1)}, u32[]{:S(2)}, u32[]{:S(2)}) collective-permute-start(bf16[16,1536]{1,0:T(8,128)(2,1)S(1)} %get-tuple-element.70), channel_id=1, source_target_pairs={{0,12},{4,8},{8,4},{12,0},{1,13},{5,9},{9,5},{13,1},{2,14},{6,10},... | collective-permute-start | bytes 147464 | tf_op jit(solution)/shard_map/ppermute | solution.py:307
  48.0 5.0 %collective-permute-start.22 = (bf16[16,1536]{1,0:T(8,128)(2,1)S(1)}, bf16[16,1536]{1,0:T(8,128)(2,1)S(1)}, u32[]{:S(2)}, u32[]{:S(2)}) collective-permute-start(bf16[16,1536]{1,0:T(8,128)(2,1)S(1)} %get-tuple-element.71), channel_id=1, source_target_pairs={{0,8},{4,12},{8,0},{12,4},{1,9},{5,13},{9,1},{13,5},{2,10},{6,14},... | collective-permute-start | bytes 147464 | tf_op jit(solution)/shard_map/ppermute | solution.py:307
  48.0 5.0 %collective-permute-start.23 = (bf16[16,1536]{1,0:T(8,128)(2,1)S(1)}, bf16[16,1536]{1,0:T(8,128)(2,1)S(1)}, u32[]{:S(2)}, u32[]{:S(2)}) collective-permute-start(bf16[16,1536]{1,0:T(8,128)(2,1)S(1)} %get-tuple-element.72), channel_id=1, source_target_pairs={{0,4},{4,0},{8,12},{12,8},{1,5},{5,1},{9,13},{13,9},{2,6},{6,2},{1... | collective-permute-start | bytes 147464 | tf_op jit(solution)/shard_map/ppermute | solution.py:307

commit v12 on v11

--- a/solution.py
+++ b/solution.py
@@ -13,6 +13,7 @@
 CAP = 8
 LANES = 128
 PAIR = 2
+BLOCK = 4
 STRIPS = 3
 TILE = 256
 UNROLL = 2
@@ -57,26 +58,29 @@
     return dot(table.astype(BF16), rows, ((0,), (0,)))
 
 
-def combine(me, rows, named, router, returned, chunks, experts):
+def weigh_kernel(me_ref, router_ref, *refs, layers):
+    high_ref, low_ref = refs[-2:]
+    rows, named = gather(refs[:-2], layers)
     routes = named[:, 0:2].astype(F32).astype(jnp.int32)
-    logits = dot(rows, router, ((1,), (1,)))
+    logits = dot(rows, router_ref[...], ((1,), (1,)))
+    experts = logits.shape[1]
     lane = iota(logits.shape, 1)
     first = jnp.sum(jnp.where(lane == routes[:, 0:1], logits, 0.0), axis=1, keepdims=True)
     second = jnp.sum(jnp.where(lane == routes[:, 1:2], logits, 0.0), axis=1, keepdims=True)
     gate0 = 1.0 / (1.0 + jnp.exp(second - first))
     gate1 = 1.0 / (1.0 + jnp.exp(first - second))
-    owners = routes ^ me
-    table = slot_map(owners, chunks, rows.shape[0] // chunks, experts)
-    expert = iota(table.shape, 1) // (chunks * CAP)
+    owners = routes ^ me_ref[0]
+    table = slot_map(owners, layers, rows.shape[0] // layers, experts)
+    expert = iota(table.shape, 1) // (layers * CAP)
     gates = table * jnp.where(owners[:, 0:1] == expert, gate0, gate1)
     high = gates.astype(BF16)
-    low = (gates - high.astype(F32)).astype(BF16)
-    return dot(high, returned) + dot(low, returned)
+    high_ref[...] = high
+    low_ref[...] = (gates - high.astype(F32)).astype(BF16)
 
 
 def attend_kernel(
     _, lengths_hbm, queries_hbm, keys_hbm, values_hbm, routes_hbm, residual_hbm, gain_hbm,
-    stream_ref, first_ref, second_ref,
+    stream_ref, first_ref, second_ref, whole_ref,
     lengths_ref, queries_ref, keys_ref, values_ref, routes_ref, residual_ref, gain_ref, sems,
 ):
     batch, window, _ = keys_ref.shape
@@ -87,26 +91,30 @@
         (lengths_hbm, lengths_ref), (queries_hbm, queries_ref), (routes_hbm, routes_ref),
         (residual_hbm, residual_ref), (gain_hbm, gain_ref),
     ]
-    caches = [
-        pair
-        for part in parts
-        for pair in (
-            (keys_hbm.at[:, :, part], keys_ref.at[:, :, part]),
-            (values_hbm.at[:, :, part], values_ref.at[:, 0:window, part]),
-        )
+    blocks = [pl.ds(begin, BLOCK) for begin in range(0, batch, BLOCK)]
+    groups = [
+        small[:2],
+        [(keys_hbm.at[block], keys_ref.at[block]) for block in blocks],
+        [(values_hbm.at[block], values_ref.at[block, 0:window]) for block in blocks],
+        small[2:],
     ]
-    copies = [
-        pltpu.make_async_copy(source, target, sems.at[i])
-        for i, (source, target) in enumerate(small[:2] + caches + small[2:])
-    ]
-    for copy in copies:
-        copy.start()
+    at, copies = 0, []
+    for group in groups:
+        copies.append([])
+        for source, target in group:
+            copies[-1].append(pltpu.make_async_copy(source, target, sems.at[at]))
+            copies[-1][-1].start()
+            at += 1
+
+    def wait(group):
+        for copy in copies[group]:
+            copy.wait()
+
     padded = values_ref.shape[1]
     if padded > window:
         pad = (batch, padded - window, values_ref.shape[2])
         values_ref[:, window:, :] = jnp.zeros(pad, BF16)
-    copies[0].wait()
-    copies[1].wait()
+    wait(0)
     same = iota((batch, batch), 0) == iota((batch, batch), 1)
 
     def upright(row):
@@ -134,7 +142,8 @@
         if full > lanes:
             spread.append(jnp.zeros((full - lanes, PAIR * HS), BF16))
         spread = jnp.concatenate(spread, axis=0)
-        copies[2 + 2 * i].wait()
+        if i == 0:
+            wait(1)
         keys = keys_ref[:, :, part].reshape(batch * window, PAIR * HS)
         products = dot(keys, spread, ((1,), (1,)))
         scores = products[:window]
@@ -149,15 +158,15 @@
         weights = jnp.concatenate(
             [jnp.where(owner == r, weights, 0.0).astype(BF16) for r in range(batch)], axis=1
         )
-        copies[3 + 2 * i].wait()
+        if i == 0:
+            wait(2)
         values = values_ref[:, :, part].reshape(batch * padded, PAIR * HS)
         mixed = dot(weights, values)
         attended += [
             mixed[h * batch : (h + 1) * batch, h // GROUP * HS : (h // GROUP + 1) * HS]
             for h in range(PAIR * GROUP)
         ]
-    for copy in copies[2 + 2 * len(parts) :]:
-        copy.wait()
+    wait(3)
     stream = residual_ref[...].astype(F32) + jnp.concatenate(attended, axis=1)
     scale = lax.rsqrt(jnp.mean(stream * stream, axis=1, keepdims=True) + 1e-05)
     lane = iota((batch, LANES), 1)
@@ -169,6 +178,8 @@
     first_ref[:, :half] = normed[:, :half]
     first_ref[:, half:] = named.astype(BF16)
     second_ref[...] = normed[:, half:]
+    whole_ref[:, :width] = normed
+    whole_ref[:, width:] = named.astype(BF16)
 
 
 def pass_kernel(*_):
@@ -179,12 +190,30 @@
     return jnp.concatenate([ref[...] for ref in refs], axis=0)
 
 
+def first_half(refs):
+    half = refs[0].shape[1] - LANES
+    blocks = [ref[...] for ref in refs]
+    rows = [block[:, :half] for block in blocks]
+    named = [block[:, block.shape[1] - LANES :] for block in blocks]
+    return jnp.concatenate(rows, axis=0), jnp.concatenate(named, axis=0)
+
+
+def second_half(refs, neighbour):
+    half = refs[0].shape[1]
+    blocks = [refs[0][...], neighbour[:, half : 2 * half], *[ref[...] for ref in refs[1:]]]
+    return jnp.concatenate(blocks, axis=0)
+
+
+def gather(refs, layers):
+    rows, named = first_half(refs[:layers])
+    return jnp.concatenate([rows, second_half(refs[layers:], refs[1])], axis=1), named
+
+
 def split_kernel(me_ref, *refs, layers, part):
-    payload = stack(refs[:layers])
-    half = payload.shape[1] - LANES
-    named = payload[:, half:]
-    rows = stack(refs[layers : 2 * layers]) if part else payload[:, :half]
-    outs = refs[(1 + part) * layers :]
+    rows, named = first_half(refs[:layers])
+    outs = refs[layers:]
+    if part:
+        rows, outs = second_half(refs[layers : 2 * layers - 1], refs[1]), refs[2 * layers - 1 :]
     slots = dispatch(me_ref[0], rows, named, layers, len(outs))
     span = layers * CAP
     for e, ref in enumerate(outs):
@@ -222,7 +251,7 @@
 
 
 def begin_kernel(*refs, experts):
-    gate_ref, up_ref, down_hbm, gate_out, up_out, down_out, rows_ref, sems = refs[experts:]
+    _, gate_ref, up_ref, down_hbm, gate_out, up_out, down_out, rows_ref, sems = refs[experts:]
     half = rows_ref.shape[1]
     copies = strip_copies(down_hbm, 0, down_out, sems)
     rows_ref[...] = stack(refs[:experts])
@@ -268,17 +297,13 @@
         store_rows(outs, at, dot(hidden_ref[...], down_ref[:, at]))
 
 
-def mix_kernel(me_ref, router_ref, *refs, layers, part):
+def mix_kernel(high_ref, low_ref, *refs, layers, part):
     outs, stream_ref = refs[-layers:], refs[-layers - 1]
-    blocks = refs[2 * layers : -layers - 1]
-    experts = len(blocks)
-    order = farthest_first(experts)
+    blocks = refs[: -layers - 1]
+    order = farthest_first(len(blocks))
+    returned = stack([blocks[order.index(e)] for e in range(len(blocks))])
+    mixed = dot(high_ref[...], returned) + dot(low_ref[...], returned)
     batch, half = outs[0].shape
-    payload = stack(refs[:layers])
-    named = payload[:, half:]
-    rows = jnp.concatenate([payload[:, :half], stack(refs[layers : 2 * layers])], axis=1)
-    returned = stack([blocks[order.index(e)] for e in range(experts)])
-    mixed = combine(me_ref[0], rows, named, router_ref[...], returned, layers, experts)
     for j, ref in enumerate(outs):
         value = mixed[j * batch : (j + 1) * batch]
         if j == 0:
@@ -286,14 +311,16 @@
         ref[...] = value.astype(ref.dtype)
 
 
-def finish_kernel(*refs, parts):
+def add_kernel(*refs):
     out_ref = refs[-1]
-    span, count = out_ref.shape[1] // parts, len(refs[:-1]) // parts
-    for p in range(parts):
-        total = refs[p * count][...]
-        for ref in refs[p * count + 1 : (p + 1) * count]:
-            total = total + ref[...].astype(F32)
-        out_ref[:, p * span : (p + 1) * span] = total.astype(BF16)
+    span = refs[-2].shape[1]
+    if out_ref.shape[1] > span:
+        out_ref[:, :span] = refs[0][...]
+        refs = refs[1:]
+    total = refs[0][...]
+    for ref in refs[1:-1]:
+        total = total + ref[...].astype(F32)
+    out_ref[:, out_ref.shape[1] - span :] = total.astype(BF16)
 
 
 def in_hbm(value):
@@ -347,22 +374,21 @@
     stream, *payload = pl.pallas_call(
         attend_kernel,
         in_specs=[SCALAR] + [ANY] * len(operands),
-        out_specs=[WHOLE] * 3,
-        out_shape=[
-            shape((batch, width), F32), shape((batch, half + LANES), BF16), shape((batch, half), BF16)
-        ],
+        out_specs=[WHOLE] * 4,
+        out_shape=[shape((batch, width), F32)]
+        + [shape((batch, size), BF16) for size in (half + LANES, half, width + LANES)],
         scratch_shapes=[pltpu.VMEM(size, a.dtype) for size, a in zip(held, operands)]
-        + [pltpu.SemaphoreType.DMA((5 + 2 * (KVH // PAIR),))],
+        + [pltpu.SemaphoreType.DMA((5 + 2 * (batch // BLOCK),))],
         compiler_params=params(28 * batch * width),
         cost_estimate=LIGHT,
     )(me, *operands)
 
     payload = pl.pallas_call(
         pass_kernel,
-        in_specs=[ANY] * 2,
-        out_specs=[ANY] * 2,
+        in_specs=[ANY] * 3,
+        out_specs=[ANY] * 3,
         out_shape=[shape(block.shape, BF16) for block in payload],
-        input_output_aliases={0: 0, 1: 1},
+        input_output_aliases={i: i for i in range(3)},
         cost_estimate=BUSY,
         compiler_params=params(0),
     )(*payload)
@@ -370,8 +396,11 @@
     order = farthest_first(experts)
     chunks, arrived = [], []
     for part in range(2):
-        came = {j: swap(payload[part], "attn", j) for j in farthest_first(layers)}
-        chunks += [came[j] for j in range(layers)]
+        came = {0: payload[part]}
+        for j in farthest_first(layers)[1:]:
+            if j != 1 or part == 0:
+                came[j] = swap(payload[2 if j == 1 else part], "attn", j)
+        chunks += [came[j] for j in sorted(came)]
         slots = pl.pallas_call(
             functools.partial(split_kernel, layers=layers, part=part),
             in_specs=[SCALAR] + [WHOLE] * len(chunks),
@@ -381,6 +410,14 @@
             compiler_params=params(experts * layers * CAP * half),
         )(me, *chunks)
         arrived.append([swap(slots[e], "expert", e) for e in order])
+    gates = pl.pallas_call(
+        functools.partial(weigh_kernel, layers=layers),
+        in_specs=[SCALAR] + [WHOLE] * (1 + len(chunks)),
+        out_specs=[WHOLE] * 2,
+        out_shape=[shape((layers * batch, experts * layers * CAP), BF16)] * 2,
+        cost_estimate=LIGHT,
+        compiler_params=params(layers * batch * width),
+    )(me, router, *chunks)
 
     total_rows = experts * layers * CAP
     units = gate_proj.shape[2]
@@ -390,7 +427,7 @@
     halves = [shape((layers * CAP, half), BF16)] * experts
     *sums, down_first = pl.pallas_call(
         functools.partial(begin_kernel, experts=experts),
-        in_specs=[WHOLE] * (experts + 2) + [ANY],
+        in_specs=[WHOLE] * experts + [ANY] + [WHOLE] * 2 + [ANY],
         out_specs=[WHOLE] * 3,
         out_shape=[shape((total_rows, units), F32)] * 2 + [pltpu.VMEM((units, half), BF16)],
         scratch_shapes=[rows, strips],
@@ -398,7 +435,7 @@
             flops=4 * total_rows * half * units, bytes_accessed=0, transcendentals=0
         ),
         compiler_params=params(total_rows * width),
-    )(*arrived[0], gate, up, down)
+    )(*arrived[0], gates[0], gate, up, down)
     *first, hidden, down_second = pl.pallas_call(
         functools.partial(middle_kernel, experts=experts),
         in_specs=[WHOLE] * (experts + 5) + [ANY],
@@ -418,26 +455,29 @@
         compiler_params=params(total_rows * width),
     )(hidden, down_second)
 
-    sums = []
+    done = []
     for part, blocks in enumerate((first, second)):
         returned = [swap(block, "expert", e) for e, block in zip(order, blocks)]
         mixed = pl.pallas_call(
             functools.partial(mix_kernel, layers=layers, part=part),
-            in_specs=[SCALAR] + [WHOLE] * (2 + 2 * layers + experts),
+            in_specs=[WHOLE] * (3 + experts),
             out_specs=[WHOLE] * layers,
             out_shape=[shape((batch, half), BF16 if j else F32) for j in range(layers)],
             cost_estimate=LIGHT,
             compiler_params=params(experts * layers * CAP * half),
-        )(me, router, *chunks, *returned, stream)
-        sums += [swap(mixed[j], "attn", j) for j in farthest_first(layers)]
-    return pl.pallas_call(
-        functools.partial(finish_kernel, parts=2),
-        in_specs=[WHOLE] * len(sums),
-        out_specs=WHOLE,
-        out_shape=shape((batch, width), BF16),
-        cost_estimate=LIGHT,
-        compiler_params=params(2 * layers * batch * width),
-    )(*sums)
+        )(*gates, *returned, stream)
+        sums = [swap(mixed[j], "attn", j) for j in farthest_first(layers)]
+        done = [
+            pl.pallas_call(
+                add_kernel,
+                in_specs=[WHOLE] * (layers + len(done)),
+                out_specs=WHOLE,
+                out_shape=shape((batch, width if part else half), BF16),
+                cost_estimate=LIGHT,
+                compiler_params=params(layers * batch * width),
+            )(*done, *sums)
+        ]
+    return done[0]
 
 
 def solution(mesh):

time: 53.8 us -> 55 us (1.022)
  waiting for transfers between devices: 11.1 us -> 13.8 us
  starting transfers between devices: 26.7 us -> 25.8 us
  Pallas kernels: 15.6 us -> 15 us
    ppermute x24 -> x23, waiting for transfers between devices: 11.1 us -> 13.8 us  [swap(): return lax.ppermute(value, axis, [(i, i ^ step) for i in range(count)])]
    pallas_call x2, Pallas kernels: 1.46 us -> 0.51 us  [shards(): pl.pallas_call(functools.partial(mix_kernel, layers=layers, part=part), i...]
    ppermute x24 -> x23, starting transfers between devices: 26.7 us -> 25.8 us  [swap(): return lax.ppermute(value, axis, [(i, i ^ step) for i in range(count)])]
  transfers between devices with their start and end apart: 24 -> 23, of which waited for: 8 -> 8; matrix products, arithmetic and copies ran while one was open for 0% -> 0% of each run, Pallas kernels for 13% -> 11%
where the time goes in v12:
time: 55 us; the launch traced here: 54.8 us
  starting transfers between devices  25.8 us (47%)
  Pallas kernels  15 us (27%)
  waiting for transfers between devices  13.8 us (25%)
    ppermute x23, starting transfers between devices, swap(): return lax.ppermute(value, axis, [(i, i ^ step) for i in range(count)])  25.8 us
    ppermute x23, waiting for transfers between devices, swap(): return lax.ppermute(value, axis, [(i, i ^ step) for i in range(count)])  13.8 us
    pallas_call x1, Pallas kernels, shards(): pl.pallas_call(functools.partial(middle_kernel, experts=experts), in_spec...  4.18 us
    pallas_call x1, Pallas kernels, shards(): pl.pallas_call(attend_kernel, in_specs=[SCALAR] + [ANY] * len(operands),...  4.01 us
    pallas_call x1, Pallas kernels, shards(): pl.pallas_call(functools.partial(begin_kernel, experts=experts), in_specs...  2.92 us
    pallas_call x1, Pallas kernels, shards(): pl.pallas_call(end_kernel, in_specs=[WHOLE] * 2, out_specs=[WHOLE] * expe...  1.37 us
  transfers between devices with their start and end apart: 23, of which 8 were waited for; matrix products, arithmetic and copies ran while one was open for 0% of the time, Pallas kernels for 11%

profile of v12, /device:TPU:0, one launch (start us, length us, event | category | flops | bytes accessed | tf_op | source)
XLA Modules:
  0.0 54.8 jit_solution(6559997365837298317)
XLA Ops:
  0.0 4.0 %shard_map.109 = (f32[16,3072]{1,0:T(8,128)S(1)}, bf16[16,1664]{1,0:T(8,128)(2,1)S(1)}, bf16[16,1536]{1,0:T(8,128)(2,1)S(1)}, bf16[16,3200]{1,0:T(8,128)(2,1)S(1)}) custom-call(s32[1]{0:T(128)} %bitcast._.me_ref, s32[1,16]{1,0:T(1,128)} %bitcast.21, bf16[16,3072]{1,0:T(8,128)(2,1)} %queries_hbm.1, bf16[16,96,512]{2,1,0:T(8,128)(2,1)} %keys_hbm.1, ...), custom_call_target="tpu_custom_call" | custom-call | tf_op jit(solution)/shard_map/pallas_call | solution.py:374
  4.0 0.0 slice-start
  4.0 0.0 slice-start.3
  4.0 0.0 slice-start.1
  4.1 0.0 slice-start.2
  4.1 0.0 slice-start.4
  4.1 0.0 slice-start.5
  4.1 0.0 copy-start
  4.1 3.1 %collective-permute-start = (bf16[16,3200]{1,0:T(8,128)(2,1)S(1)}, bf16[16,3200]{1,0:T(8,128)(2,1)S(1)}, u32[]{:S(2)}, u32[]{:S(2)}) collective-permute-start(bf16[16,3200]{1,0:T(8,128)(2,1)S(1)} %get-tuple-element.47), channel_id=1, source_target_pairs={{0,4},{4,0},{8,12},{12,8},{1,5},{5,1},{9,13},{13,9},{2,6},{6,2},{1... | collective-permute-start | bytes 307208 | tf_op jit(solution)/shard_map/ppermute | solution.py:334
  7.2 2.5 %collective-permute-start.2 = (bf16[16,1664]{1,0:T(8,128)(2,1)S(1)}, bf16[16,1664]{1,0:T(8,128)(2,1)S(1)}, u32[]{:S(2)}, u32[]{:S(2)}) collective-permute-start(bf16[16,1664]{1,0:T(8,128)(2,1)S(1)} %get-tuple-element.46.refs_0_), channel_id=1, source_target_pairs={{0,12},{4,8},{8,4},{12,0},{1,13},{5,9},{9,5},{13,1},{2,14},{6,10},... | collective-permute-start | bytes 159752 | tf_op jit(solution)/shard_map/ppermute | solution.py:334
  9.7 0.1 collective-permute-start.1
  9.8 2.9 %collective-permute-start.4 = (bf16[16,1536]{1,0:T(8,128)(2,1)S(1)}, bf16[16,1536]{1,0:T(8,128)(2,1)S(1)}, u32[]{:S(2)}, u32[]{:S(2)}) collective-permute-start(bf16[16,1536]{1,0:T(8,128)(2,1)S(1)} %get-tuple-element.48.refs_4_), channel_id=1, source_target_pairs={{0,12},{4,8},{8,4},{12,0},{1,13},{5,9},{9,5},{13,1},{2,14},{6,10},... | collective-permute-start | bytes 147464 | tf_op jit(solution)/shard_map/ppermute | solution.py:334
  12.7 0.3 collective-permute-start.3
  13.0 1.3 %collective-permute-done.2.refs_3_ = bf16[16,1664]{1,0:T(8,128)(2,1)S(1)} collective-permute-done((bf16[16,1664]{1,0:T(8,128)(2,1)S(1)}, bf16[16,1664]{1,0:T(8,128)(2,1)S(1)}, u32[]{:S(2)}, u32[]{:S(2)}) %collective-permute-start.2) | collective-permute-done | bytes 53280 | tf_op jit(solution)/shard_map/ppermute | solution.py:334
  14.3 3.6 %collective-permute-done.1.refs_2_ = bf16[16,1664]{1,0:T(8,128)(2,1)S(1)} collective-permute-done((bf16[16,1664]{1,0:T(8,128)(2,1)S(1)}, bf16[16,1664]{1,0:T(8,128)(2,1)S(1)}, u32[]{:S(2)}, u32[]{:S(2)}) %collective-permute-start.1) | collective-permute-done | bytes 53280 | tf_op jit(solution)/shard_map/ppermute | solution.py:334
  18.0 0.0 collective-permute-done.refs_1_
  18.0 0.5 shard_map.113
  18.5 0.1 collective-permute-start.8
  18.6 1.6 %collective-permute-start.9 = (bf16[32,1536]{1,0:T(8,128)(2,1)S(1)}, bf16[32,1536]{1,0:T(8,128)(2,1)S(1)}, u32[]{:S(2)}, u32[]{:S(2)}) collective-permute-start(bf16[32,1536]{1,0:T(8,128)(2,1)S(1)} %get-tuple-element.57), channel_id=1, source_target_pairs={{0,2},{1,3},{2,0},{3,1},{4,6},{5,7},{6,4},{7,5},{8,10},{9,11},{10,... | collective-permute-start | bytes 294920 | tf_op jit(solution)/shard_map/ppermute | solution.py:334
  20.1 0.3 collective-permute-start.10
  20.4 0.0 collective-permute-done.4.refs_6_
  20.4 0.0 collective-permute-done.3.refs_5_
  20.4 0.5 shard_map.112
  20.9 1.2 %collective-permute-start.5 = (bf16[32,1536]{1,0:T(8,128)(2,1)S(1)}, bf16[32,1536]{1,0:T(8,128)(2,1)S(1)}, u32[]{:S(2)}, u32[]{:S(2)}) collective-permute-start(bf16[32,1536]{1,0:T(8,128)(2,1)S(1)} %get-tuple-element.52), channel_id=1, source_target_pairs={{0,3},{1,2},{2,1},{3,0},{4,7},{5,6},{6,5},{7,4},{8,11},{9,10},{10,... | collective-permute-start | bytes 294920 | tf_op jit(solution)/shard_map/ppermute | solution.py:334
  22.1 0.7 %collective-permute-start.6 = (bf16[32,1536]{1,0:T(8,128)(2,1)S(1)}, bf16[32,1536]{1,0:T(8,128)(2,1)S(1)}, u32[]{:S(2)}, u32[]{:S(2)}) collective-permute-start(bf16[32,1536]{1,0:T(8,128)(2,1)S(1)} %get-tuple-element.53), channel_id=1, source_target_pairs={{0,2},{1,3},{2,0},{3,1},{4,6},{5,7},{6,4},{7,5},{8,10},{9,11},{10,... | collective-permute-start | bytes 294920 | tf_op jit(solution)/shard_map/ppermute | solution.py:334
  22.8 0.0 copy-done
  22.8 0.3 shard_map.111
  23.2 0.4 collective-permute-done.8.refs_1_
  23.6 0.1 collective-permute-start.7
  23.7 2.1 %collective-permute-done.9.refs_2_ = bf16[32,1536]{1,0:T(8,128)(2,1)S(1)} collective-permute-done((bf16[32,1536]{1,0:T(8,128)(2,1)S(1)}, bf16[32,1536]{1,0:T(8,128)(2,1)S(1)}, u32[]{:S(2)}, u32[]{:S(2)}) %collective-permute-start.9) | collective-permute-done | bytes 98336 | tf_op jit(solution)/shard_map/ppermute | solution.py:334
  25.8 0.0 collective-permute-done.10.refs_3_
  25.9 2.9 %shard_map.114 = (f32[128,2048]{1,0:T(8,128)S(1)}, f32[128,2048]{1,0:T(8,128)S(1)}, bf16[2048,1536]{1,0:T(8,128)(2,1)S(1)}) custom-call(bf16[32,1536]{1,0:T(8,128)(2,1)S(1)} %get-tuple-element.55.refs_0_, bf16[32,1536]{1,0:T(8,128)(2,1)S(1)} %collective-permute-done.8.refs_1_, bf16[32,1536]{1,0:T(8,128)(2,1)S(1)} %collective-permute-done.9.refs_2_, ...), custom_call_target="tpu_custom_call" | custom-call | flops 1610612736 | tf_op jit(solution)/shard_map/pallas_call | solution.py:428
  28.8 0.0 collective-permute-done.5.refs_1_
  28.8 1.2 %collective-permute-done.6.refs_2_ = bf16[32,1536]{1,0:T(8,128)(2,1)S(1)} collective-permute-done((bf16[32,1536]{1,0:T(8,128)(2,1)S(1)}, bf16[32,1536]{1,0:T(8,128)(2,1)S(1)}, u32[]{:S(2)}, u32[]{:S(2)}) %collective-permute-start.6) | collective-permute-done | bytes 98336 | tf_op jit(solution)/shard_map/ppermute | solution.py:334
  30.0 0.0 collective-permute-done.7.refs_3_
  30.0 4.2 %shard_map.115 = (bf16[32,1536]{1,0:T(8,128)(2,1)S(1)}, bf16[32,1536]{1,0:T(8,128)(2,1)S(1)}, bf16[32,1536]{1,0:T(8,128)(2,1)S(1)}, bf16[32,1536]{1,0:T(8,128)(2...) custom-call(bf16[32,1536]{1,0:T(8,128)(2,1)S(1)} %get-tuple-element.51.refs_0_, ...), custom_call_target="tpu_custom_call" | custom-call | tf_op jit(solution)/shard_map/pallas_call | solution.py:439
  34.1 0.1 collective-permute-start.11
  34.2 1.7 %collective-permute-start.12 = (bf16[32,1536]{1,0:T(8,128)(2,1)S(1)}, bf16[32,1536]{1,0:T(8,128)(2,1)S(1)}, u32[]{:S(2)}, u32[]{:S(2)}) collective-permute-start(bf16[32,1536]{1,0:T(8,128)(2,1)S(1)} %get-tuple-element.64), channel_id=1, source_target_pairs={{0,2},{1,3},{2,0},{3,1},{4,6},{5,7},{6,4},{7,5},{8,10},{9,11},{10,... | collective-permute-start | bytes 294920 | tf_op jit(solution)/shard_map/ppermute | solution.py:334
  35.9 0.2 collective-permute-start.13
  36.1 1.4 %shard_map.118 = (bf16[32,1536]{1,0:T(8,128)(2,1)S(1)}, bf16[32,1536]{1,0:T(8,128)(2,1)S(1)}, bf16[32,1536]{1,0:T(8,128)(2,1)S(1)}, bf16[32,1536]{1,0:T(8,128)(2,1)S(1)}) custom-call(bf16[128,2048]{1,0:T(8,128)(2,1)S(1)} %get-tuple-element.71.hidden_ref, bf16[2048,1536]{1,0:T(8,128)(2,1)S(1)} %get-tuple-element.72.down_ref), custom_call_target="tpu_custom_call" | custom-call | flops 805306368 | tf_op jit(solution)/shard_map/pallas_call | solution.py:447
  37.5 0.4 collective-permute-start.17
  37.9 1.6 %collective-permute-start.18 = (bf16[32,1536]{1,0:T(8,128)(2,1)S(1)}, bf16[32,1536]{1,0:T(8,128)(2,1)S(1)}, u32[]{:S(2)}, u32[]{:S(2)}) collective-permute-start(bf16[32,1536]{1,0:T(8,128)(2,1)S(1)} %get-tuple-element.75), channel_id=1, source_target_pairs={{0,2},{1,3},{2,0},{3,1},{4,6},{5,7},{6,4},{7,5},{8,10},{9,11},{10,... | collective-permute-start | bytes 294920 | tf_op jit(solution)/shard_map/ppermute | solution.py:334
  39.5 0.0 collective-permute-done.11.refs_1_
  39.5 0.0 collective-permute-start.19
  39.5 2.2 %collective-permute-done.12.refs_2_ = bf16[32,1536]{1,0:T(8,128)(2,1)S(1)} collective-permute-done((bf16[32,1536]{1,0:T(8,128)(2,1)S(1)}, bf16[32,1536]{1,0:T(8,128)(2,1)S(1)}, u32[]{:S(2)}, u32[]{:S(2)}) %collective-permute-start.12) | collective-permute-done | bytes 98336 | tf_op jit(solution)/shard_map/ppermute | solution.py:334
  41.7 0.0 collective-permute-done.13.refs_3_
  41.7 0.3 shard_map.116
  41.9 2.5 %collective-permute-start.14 = (bf16[16,1536]{1,0:T(8,128)(2,1)S(1)}, bf16[16,1536]{1,0:T(8,128)(2,1)S(1)}, u32[]{:S(2)}, u32[]{:S(2)}) collective-permute-start(bf16[16,1536]{1,0:T(8,128)(2,1)S(1)} %get-tuple-element.68), channel_id=1, source_target_pairs={{0,12},{4,8},{8,4},{12,0},{1,13},{5,9},{9,5},{13,1},{2,14},{6,10},... | collective-permute-start | bytes 147464 | tf_op jit(solution)/shard_map/ppermute | solution.py:334
  44.4 0.0 collective-permute-start.15
  44.4 0.0 collective-permute-done.17.refs_1_
  44.4 2.0 %collective-permute-start.16 = (bf16[16,1536]{1,0:T(8,128)(2,1)S(1)}, bf16[16,1536]{1,0:T(8,128)(2,1)S(1)}, u32[]{:S(2)}, u32[]{:S(2)}) collective-permute-start(bf16[16,1536]{1,0:T(8,128)(2,1)S(1)} %get-tuple-element.70), channel_id=1, source_target_pairs={{0,4},{4,0},{8,12},{12,8},{1,5},{5,1},{9,13},{13,9},{2,6},{6,2},{1... | collective-permute-start | bytes 147464 | tf_op jit(solution)/shard_map/ppermute | solution.py:334
  46.4 0.0 collective-permute-done.18.refs_2_
  46.4 0.0 collective-permute-done.19.refs_3_
  46.4 0.3 shard_map.119
  46.6 2.5 %collective-permute-start.20 = (bf16[16,1536]{1,0:T(8,128)(2,1)S(1)}, bf16[16,1536]{1,0:T(8,128)(2,1)S(1)}, u32[]{:S(2)}, u32[]{:S(2)}) collective-permute-start(bf16[16,1536]{1,0:T(8,128)(2,1)S(1)} %get-tuple-element.78), channel_id=1, source_target_pairs={{0,12},{4,8},{8,4},{12,0},{1,13},{5,9},{9,5},{13,1},{2,14},{6,10},... | collective-permute-start | bytes 147464 | tf_op jit(solution)/shard_map/ppermute | solution.py:334
  49.1 0.0 collective-permute-start.21
  49.1 0.0 collective-permute-done.14.refs_1_
  49.1 2.0 %collective-permute-start.22 = (bf16[16,1536]{1,0:T(8,128)(2,1)S(1)}, bf16[16,1536]{1,0:T(8,128)(2,1)S(1)}, u32[]{:S(2)}, u32[]{:S(2)}) collective-permute-start(bf16[16,1536]{1,0:T(8,128)(2,1)S(1)} %get-tuple-element.80), channel_id=1, source_target_pairs={{0,4},{4,0},{8,12},{12,8},{1,5},{5,1},{9,13},{13,9},{2,6},{6,2},{1... | collective-permute-start | bytes 147464 | tf_op jit(solution)/shard_map/ppermute | solution.py:334
  51.1 0.0 collective-permute-done.15.refs_2_
  51.1 0.0 collective-permute-done.16.refs_3_
  51.1 1.5 %collective-permute-done.20.refs_2_ = bf16[16,1536]{1,0:T(8,128)(2,1)S(1)} collective-permute-done((bf16[16,1536]{1,0:T(8,128)(2,1)S(1)}, bf16[16,1536]{1,0:T(8,128)(2,1)S(1)}, u32[]{:S(2)}, u32[]{:S(2)}) %collective-permute-start.20) | collective-permute-done | bytes 49184 | tf_op jit(solution)/shard_map/ppermute | solution.py:334
  52.6 1.6 %collective-permute-done.21.refs_3_ = bf16[16,1536]{1,0:T(8,128)(2,1)S(1)} collective-permute-done((bf16[16,1536]{1,0:T(8,128)(2,1)S(1)}, bf16[16,1536]{1,0:T(8,128)(2,1)S(1)}, u32[]{:S(2)}, u32[]{:S(2)}) %collective-permute-start.21) | collective-permute-done | bytes 49184 | tf_op jit(solution)/shard_map/ppermute | solution.py:334
  54.2 0.0 collective-permute-done.22.refs_4_
  54.2 0.7 %shard_map.120 = bf16[16,3072]{1,0:T(8,128)(2,1)} custom-call(bf16[16,1536]{1,0:T(8,128)(2,1)S(1)} %shard_map.117.refs_0_, f32[16,1536]{1,0:T(8,128)S(1)} %get-tuple-element.77.refs_1_, bf16[16,1536]{1,0:T(8,128)(2,1)S(1)} %collective-permute-done.20.refs_2_, bf16[16,1536]{1,0:T(8,128)(2,1)S(1)} %collective-permute-done.21.refs_3_, ...), custom_call_target="tpu_custom_call" | custom-call | tf_op jit(solution)/shard_map/pallas_call | solution.py:471
  (10 shorter events, 0.0 us)
Async XLA Ops:
  4.0 21.8 %slice-start = ((s8[12582912]{0:T(1024)(128)(4,1)}), s8[4194304]{0:T(1024)(128)(4,1)S(1)}, s32[]{:S(2)}) async-start(s8[12582912]{0:T(1024)(128)(4,1)} %bitcast.8), calls=%async_computation | async-start | bytes 8388608
  4.0 21.8 %slice-start.3 = ((s8[12582912]{0:T(1024)(128)(4,1)}), s8[4194304]{0:T(1024)(128)(4,1)S(1)}, s32[]{:S(2)}) async-start(s8[12582912]{0:T(1024)(128)(4,1)} %bitcast.12), calls=%async_computation.3 | async-start | bytes 8388608
  4.0 21.8 %slice-start.1 = ((s8[12582912]{0:T(1024)(128)(4,1)}), s8[4194304]{0:T(1024)(128)(4,1)S(1)}, s32[]{:S(2)}) async-start(s8[12582912]{0:T(1024)(128)(4,1)} %bitcast.8), calls=%async_computation.1 | async-start | bytes 8388608
  4.1 21.8 %slice-start.2 = ((s8[12582912]{0:T(1024)(128)(4,1)}), s8[4194304]{0:T(1024)(128)(4,1)S(1)}, s32[]{:S(2)}) async-start(s8[12582912]{0:T(1024)(128)(4,1)} %bitcast.8), calls=%async_computation.2 | async-start | bytes 8388608
  4.1 21.8 %slice-start.4 = ((s8[12582912]{0:T(1024)(128)(4,1)}), s8[4194304]{0:T(1024)(128)(4,1)S(1)}, s32[]{:S(2)}) async-start(s8[12582912]{0:T(1024)(128)(4,1)} %bitcast.12), calls=%async_computation.4 | async-start | bytes 8388608
  4.1 21.8 %slice-start.5 = ((s8[12582912]{0:T(1024)(128)(4,1)}), s8[4194304]{0:T(1024)(128)(4,1)S(1)}, s32[]{:S(2)}) async-start(s8[12582912]{0:T(1024)(128)(4,1)} %bitcast.12), calls=%async_computation.5 | async-start | bytes 8388608
  4.1 18.7 %copy-start = (bf16[3072,4]{0,1:T(4,128)(2,1)S(1)}, bf16[3072,4]{0,1:T(4,128)(2,1)}, u32[]{:S(2)}) copy-start(bf16[3072,4]{0,1:T(4,128)(2,1)} %param.18) | copy-start | bytes 73732
  4.1 13.9 %collective-permute-start = (bf16[16,3200]{1,0:T(8,128)(2,1)S(1)}, bf16[16,3200]{1,0:T(8,128)(2,1)S(1)}, u32[]{:S(2)}, u32[]{:S(2)}) collective-permute-start(bf16[16,3200]{1,0:T(8,128)(2,1)S(1)} %get-tuple-element.47), channel_id=1, source_target_pairs={{0,4},{4,0},{8,12},{12,8},{1,5},{5,1},{9,13},{13,9},{2,6},{6,2},{1... | collective-permute-start | bytes 307208 | tf_op jit(solution)/shard_map/ppermute | solution.py:334
  7.2 7.1 %collective-permute-start.2 = (bf16[16,1664]{1,0:T(8,128)(2,1)S(1)}, bf16[16,1664]{1,0:T(8,128)(2,1)S(1)}, u32[]{:S(2)}, u32[]{:S(2)}) collective-permute-start(bf16[16,1664]{1,0:T(8,128)(2,1)S(1)} %get-tuple-element.46.refs_0_), channel_id=1, source_target_pairs={{0,12},{4,8},{8,4},{12,0},{1,13},{5,9},{9,5},{13,1},{2,14},{6,10},... | collective-permute-start | bytes 159752 | tf_op jit(solution)/shard_map/ppermute | solution.py:334
  9.7 8.3 %collective-permute-start.1 = (bf16[16,1664]{1,0:T(8,128)(2,1)S(1)}, bf16[16,1664]{1,0:T(8,128)(2,1)S(1)}, u32[]{:S(2)}, u32[]{:S(2)}) collective-permute-start(bf16[16,1664]{1,0:T(8,128)(2,1)S(1)} %get-tuple-element.46.refs_0_), channel_id=1, source_target_pairs={{0,8},{4,12},{8,0},{12,4},{1,9},{5,13},{9,1},{13,5},{2,10},{6,14},... | collective-permute-start | bytes 159752 | tf_op jit(solution)/shard_map/ppermute | solution.py:334
  9.8 10.6 %collective-permute-start.4 = (bf16[16,1536]{1,0:T(8,128)(2,1)S(1)}, bf16[16,1536]{1,0:T(8,128)(2,1)S(1)}, u32[]{:S(2)}, u32[]{:S(2)}) collective-permute-start(bf16[16,1536]{1,0:T(8,128)(2,1)S(1)} %get-tuple-element.48.refs_4_), channel_id=1, source_target_pairs={{0,12},{4,8},{8,4},{12,0},{1,13},{5,9},{9,5},{13,1},{2,14},{6,10},... | collective-permute-start | bytes 147464 | tf_op jit(solution)/shard_map/ppermute | solution.py:334
  12.7 7.7 %collective-permute-start.3 = (bf16[16,1536]{1,0:T(8,128)(2,1)S(1)}, bf16[16,1536]{1,0:T(8,128)(2,1)S(1)}, u32[]{:S(2)}, u32[]{:S(2)}) collective-permute-start(bf16[16,1536]{1,0:T(8,128)(2,1)S(1)} %get-tuple-element.48.refs_4_), channel_id=1, source_target_pairs={{0,8},{4,12},{8,0},{12,4},{1,9},{5,13},{9,1},{13,5},{2,10},{6,14},... | collective-permute-start | bytes 147464 | tf_op jit(solution)/shard_map/ppermute | solution.py:334
  18.5 5.1 %collective-permute-start.8 = (bf16[32,1536]{1,0:T(8,128)(2,1)S(1)}, bf16[32,1536]{1,0:T(8,128)(2,1)S(1)}, u32[]{:S(2)}, u32[]{:S(2)}) collective-permute-start(bf16[32,1536]{1,0:T(8,128)(2,1)S(1)} %get-tuple-element.56), channel_id=1, source_target_pairs={{0,3},{1,2},{2,1},{3,0},{4,7},{5,6},{6,5},{7,4},{8,11},{9,10},{10,... | collective-permute-start | bytes 294920 | tf_op jit(solution)/shard_map/ppermute | solution.py:334
  18.6 7.2 %collective-permute-start.9 = (bf16[32,1536]{1,0:T(8,128)(2,1)S(1)}, bf16[32,1536]{1,0:T(8,128)(2,1)S(1)}, u32[]{:S(2)}, u32[]{:S(2)}) collective-permute-start(bf16[32,1536]{1,0:T(8,128)(2,1)S(1)} %get-tuple-element.57), channel_id=1, source_target_pairs={{0,2},{1,3},{2,0},{3,1},{4,6},{5,7},{6,4},{7,5},{8,10},{9,11},{10,... | collective-permute-start | bytes 294920 | tf_op jit(solution)/shard_map/ppermute | solution.py:334
  20.1 5.7 %collective-permute-start.10 = (bf16[32,1536]{1,0:T(8,128)(2,1)S(1)}, bf16[32,1536]{1,0:T(8,128)(2,1)S(1)}, u32[]{:S(2)}, u32[]{:S(2)}) collective-permute-start(bf16[32,1536]{1,0:T(8,128)(2,1)S(1)} %get-tuple-element.58), channel_id=1, source_target_pairs={{0,1},{1,0},{2,3},{3,2},{4,5},{5,4},{6,7},{7,6},{8,9},{9,8},{10,11... | collective-permute-start | bytes 294920 | tf_op jit(solution)/shard_map/ppermute | solution.py:334
  20.9 7.9 %collective-permute-start.5 = (bf16[32,1536]{1,0:T(8,128)(2,1)S(1)}, bf16[32,1536]{1,0:T(8,128)(2,1)S(1)}, u32[]{:S(2)}, u32[]{:S(2)}) collective-permute-start(bf16[32,1536]{1,0:T(8,128)(2,1)S(1)} %get-tuple-element.52), channel_id=1, source_target_pairs={{0,3},{1,2},{2,1},{3,0},{4,7},{5,6},{6,5},{7,4},{8,11},{9,10},{10,... | collective-permute-start | bytes 294920 | tf_op jit(solution)/shard_map/ppermute | solution.py:334
  22.1 7.9 %collective-permute-start.6 = (bf16[32,1536]{1,0:T(8,128)(2,1)S(1)}, bf16[32,1536]{1,0:T(8,128)(2,1)S(1)}, u32[]{:S(2)}, u32[]{:S(2)}) collective-permute-start(bf16[32,1536]{1,0:T(8,128)(2,1)S(1)} %get-tuple-element.53), channel_id=1, source_target_pairs={{0,2},{1,3},{2,0},{3,1},{4,6},{5,7},{6,4},{7,5},{8,10},{9,11},{10,... | collective-permute-start | bytes 294920 | tf_op jit(solution)/shard_map/ppermute | solution.py:334
  23.6 6.4 %collective-permute-start.7 = (bf16[32,1536]{1,0:T(8,128)(2,1)S(1)}, bf16[32,1536]{1,0:T(8,128)(2,1)S(1)}, u32[]{:S(2)}, u32[]{:S(2)}) collective-permute-start(bf16[32,1536]{1,0:T(8,128)(2,1)S(1)} %get-tuple-element.54), channel_id=1, source_target_pairs={{0,1},{1,0},{2,3},{3,2},{4,5},{5,4},{6,7},{7,6},{8,9},{9,8},{10,11... | collective-permute-start | bytes 294920 | tf_op jit(solution)/shard_map/ppermute | solution.py:334
  34.1 5.4 %collective-permute-start.11 = (bf16[32,1536]{1,0:T(8,128)(2,1)S(1)}, bf16[32,1536]{1,0:T(8,128)(2,1)S(1)}, u32[]{:S(2)}, u32[]{:S(2)}) collective-permute-start(bf16[32,1536]{1,0:T(8,128)(2,1)S(1)} %get-tuple-element.63), channel_id=1, source_target_pairs={{0,3},{1,2},{2,1},{3,0},{4,7},{5,6},{6,5},{7,4},{8,11},{9,10},{10,... | collective-permute-start | bytes 294920 | tf_op jit(solution)/shard_map/ppermute | solution.py:334
  34.2 7.4 %collective-permute-start.12 = (bf16[32,1536]{1,0:T(8,128)(2,1)S(1)}, bf16[32,1536]{1,0:T(8,128)(2,1)S(1)}, u32[]{:S(2)}, u32[]{:S(2)}) collective-permute-start(bf16[32,1536]{1,0:T(8,128)(2,1)S(1)} %get-tuple-element.64), channel_id=1, source_target_pairs={{0,2},{1,3},{2,0},{3,1},{4,6},{5,7},{6,4},{7,5},{8,10},{9,11},{10,... | collective-permute-start | bytes 294920 | tf_op jit(solution)/shard_map/ppermute | solution.py:334
  35.9 5.7 %collective-permute-start.13 = (bf16[32,1536]{1,0:T(8,128)(2,1)S(1)}, bf16[32,1536]{1,0:T(8,128)(2,1)S(1)}, u32[]{:S(2)}, u32[]{:S(2)}) collective-permute-start(bf16[32,1536]{1,0:T(8,128)(2,1)S(1)} %get-tuple-element.65), channel_id=1, source_target_pairs={{0,1},{1,0},{2,3},{3,2},{4,5},{5,4},{6,7},{7,6},{8,9},{9,8},{10,11... | collective-permute-start | bytes 294920 | tf_op jit(solution)/shard_map/ppermute | solution.py:334
  37.5 6.9 %collective-permute-start.17 = (bf16[32,1536]{1,0:T(8,128)(2,1)S(1)}, bf16[32,1536]{1,0:T(8,128)(2,1)S(1)}, u32[]{:S(2)}, u32[]{:S(2)}) collective-permute-start(bf16[32,1536]{1,0:T(8,128)(2,1)S(1)} %get-tuple-element.74), channel_id=1, source_target_pairs={{0,3},{1,2},{2,1},{3,0},{4,7},{5,6},{6,5},{7,4},{8,11},{9,10},{10,... | collective-permute-start | bytes 294920 | tf_op jit(solution)/shard_map/ppermute | solution.py:334
  37.9 8.5 %collective-permute-start.18 = (bf16[32,1536]{1,0:T(8,128)(2,1)S(1)}, bf16[32,1536]{1,0:T(8,128)(2,1)S(1)}, u32[]{:S(2)}, u32[]{:S(2)}) collective-permute-start(bf16[32,1536]{1,0:T(8,128)(2,1)S(1)} %get-tuple-element.75), channel_id=1, source_target_pairs={{0,2},{1,3},{2,0},{3,1},{4,6},{5,7},{6,4},{7,5},{8,10},{9,11},{10,... | collective-permute-start | bytes 294920 | tf_op jit(solution)/shard_map/ppermute | solution.py:334
  39.5 6.9 %collective-permute-start.19 = (bf16[32,1536]{1,0:T(8,128)(2,1)S(1)}, bf16[32,1536]{1,0:T(8,128)(2,1)S(1)}, u32[]{:S(2)}, u32[]{:S(2)}) collective-permute-start(bf16[32,1536]{1,0:T(8,128)(2,1)S(1)} %get-tuple-element.76), channel_id=1, source_target_pairs={{0,1},{1,0},{2,3},{3,2},{4,5},{5,4},{6,7},{7,6},{8,9},{9,8},{10,11... | collective-permute-start | bytes 294920 | tf_op jit(solution)/shard_map/ppermute | solution.py:334
  41.9 7.2 %collective-permute-start.14 = (bf16[16,1536]{1,0:T(8,128)(2,1)S(1)}, bf16[16,1536]{1,0:T(8,128)(2,1)S(1)}, u32[]{:S(2)}, u32[]{:S(2)}) collective-permute-start(bf16[16,1536]{1,0:T(8,128)(2,1)S(1)} %get-tuple-element.68), channel_id=1, source_target_pairs={{0,12},{4,8},{8,4},{12,0},{1,13},{5,9},{9,5},{13,1},{2,14},{6,10},... | collective-permute-start | bytes 147464 | tf_op jit(solution)/shard_map/ppermute | solution.py:334
  44.4 6.7 %collective-permute-start.15 = (bf16[16,1536]{1,0:T(8,128)(2,1)S(1)}, bf16[16,1536]{1,0:T(8,128)(2,1)S(1)}, u32[]{:S(2)}, u32[]{:S(2)}) collective-permute-start(bf16[16,1536]{1,0:T(8,128)(2,1)S(1)} %get-tuple-element.69), channel_id=1, source_target_pairs={{0,8},{4,12},{8,0},{12,4},{1,9},{5,13},{9,1},{13,5},{2,10},{6,14},... | collective-permute-start | bytes 147464 | tf_op jit(solution)/shard_map/ppermute | solution.py:334
  44.4 6.7 %collective-permute-start.16 = (bf16[16,1536]{1,0:T(8,128)(2,1)S(1)}, bf16[16,1536]{1,0:T(8,128)(2,1)S(1)}, u32[]{:S(2)}, u32[]{:S(2)}) collective-permute-start(bf16[16,1536]{1,0:T(8,128)(2,1)S(1)} %get-tuple-element.70), channel_id=1, source_target_pairs={{0,4},{4,0},{8,12},{12,8},{1,5},{5,1},{9,13},{13,9},{2,6},{6,2},{1... | collective-permute-start | bytes 147464 | tf_op jit(solution)/shard_map/ppermute | solution.py:334
  46.6 6.0 %collective-permute-start.20 = (bf16[16,1536]{1,0:T(8,128)(2,1)S(1)}, bf16[16,1536]{1,0:T(8,128)(2,1)S(1)}, u32[]{:S(2)}, u32[]{:S(2)}) collective-permute-start(bf16[16,1536]{1,0:T(8,128)(2,1)S(1)} %get-tuple-element.78), channel_id=1, source_target_pairs={{0,12},{4,8},{8,4},{12,0},{1,13},{5,9},{9,5},{13,1},{2,14},{6,10},... | collective-permute-start | bytes 147464 | tf_op jit(solution)/shard_map/ppermute | solution.py:334
  49.1 5.1 %collective-permute-start.21 = (bf16[16,1536]{1,0:T(8,128)(2,1)S(1)}, bf16[16,1536]{1,0:T(8,128)(2,1)S(1)}, u32[]{:S(2)}, u32[]{:S(2)}) collective-permute-start(bf16[16,1536]{1,0:T(8,128)(2,1)S(1)} %get-tuple-element.79), channel_id=1, source_target_pairs={{0,8},{4,12},{8,0},{12,4},{1,9},{5,13},{9,1},{13,5},{2,10},{6,14},... | collective-permute-start | bytes 147464 | tf_op jit(solution)/shard_map/ppermute | solution.py:334
  49.1 5.1 %collective-permute-start.22 = (bf16[16,1536]{1,0:T(8,128)(2,1)S(1)}, bf16[16,1536]{1,0:T(8,128)(2,1)S(1)}, u32[]{:S(2)}, u32[]{:S(2)}) collective-permute-start(bf16[16,1536]{1,0:T(8,128)(2,1)S(1)} %get-tuple-element.80), channel_id=1, source_target_pairs={{0,4},{4,0},{8,12},{12,8},{1,5},{5,1},{9,13},{13,9},{2,6},{6,2},{1... | collective-permute-start | bytes 147464 | tf_op jit(solution)/shard_map/ppermute | solution.py:334

commit v13 on v12

--- a/solution.py
+++ b/solution.py
@@ -60,7 +60,8 @@
 
 def weigh_kernel(me_ref, router_ref, *refs, layers):
     high_ref, low_ref = refs[-2:]
-    rows, named = gather(refs[:-2], layers)
+    parts, named = gather(refs[:-2], layers)
+    rows = jnp.concatenate(parts, axis=1)
     routes = named[:, 0:2].astype(F32).astype(jnp.int32)
     logits = dot(rows, router_ref[...], ((1,), (1,)))
     experts = logits.shape[1]
@@ -80,7 +81,7 @@
 
 def attend_kernel(
     _, lengths_hbm, queries_hbm, keys_hbm, values_hbm, routes_hbm, residual_hbm, gain_hbm,
-    stream_ref, first_ref, second_ref, whole_ref,
+    stream_ref, first_ref, second_ref,
     lengths_ref, queries_ref, keys_ref, values_ref, routes_ref, residual_ref, gain_ref, sems,
 ):
     batch, window, _ = keys_ref.shape
@@ -178,8 +179,6 @@
     first_ref[:, :half] = normed[:, :half]
     first_ref[:, half:] = named.astype(BF16)
     second_ref[...] = normed[:, half:]
-    whole_ref[:, :width] = normed
-    whole_ref[:, width:] = named.astype(BF16)
 
 
 def pass_kernel(*_):
@@ -190,31 +189,17 @@
     return jnp.concatenate([ref[...] for ref in refs], axis=0)
 
 
-def first_half(refs):
-    half = refs[0].shape[1] - LANES
-    blocks = [ref[...] for ref in refs]
-    rows = [block[:, :half] for block in blocks]
-    named = [block[:, block.shape[1] - LANES :] for block in blocks]
-    return jnp.concatenate(rows, axis=0), jnp.concatenate(named, axis=0)
-
-
-def second_half(refs, neighbour):
-    half = refs[0].shape[1]
-    blocks = [refs[0][...], neighbour[:, half : 2 * half], *[ref[...] for ref in refs[1:]]]
-    return jnp.concatenate(blocks, axis=0)
-
-
 def gather(refs, layers):
-    rows, named = first_half(refs[:layers])
-    return jnp.concatenate([rows, second_half(refs[layers:], refs[1])], axis=1), named
+    first = stack(refs[:layers])
+    half = first.shape[1] - LANES
+    parts = [first[:, :half]] + [stack(refs[at : at + layers]) for at in range(layers, len(refs), layers)]
+    return parts, first[:, half:]
 
 
 def split_kernel(me_ref, *refs, layers, part):
-    rows, named = first_half(refs[:layers])
-    outs = refs[layers:]
-    if part:
-        rows, outs = second_half(refs[layers : 2 * layers - 1], refs[1]), refs[2 * layers - 1 :]
-    slots = dispatch(me_ref[0], rows, named, layers, len(outs))
+    parts, named = gather(refs[: (1 + part) * layers], layers)
+    outs = refs[(1 + part) * layers :]
+    slots = dispatch(me_ref[0], parts[part], named, layers, len(outs))
     span = layers * CAP
     for e, ref in enumerate(outs):
         ref[...] = slots[e * span : (e + 1) * span].astype(BF16)
@@ -374,9 +359,9 @@
     stream, *payload = pl.pallas_call(
         attend_kernel,
         in_specs=[SCALAR] + [ANY] * len(operands),
-        out_specs=[WHOLE] * 4,
+        out_specs=[WHOLE] * 3,
         out_shape=[shape((batch, width), F32)]
-        + [shape((batch, size), BF16) for size in (half + LANES, half, width + LANES)],
+        + [shape((batch, size), BF16) for size in (half + LANES, half)],
         scratch_shapes=[pltpu.VMEM(size, a.dtype) for size, a in zip(held, operands)]
         + [pltpu.SemaphoreType.DMA((5 + 2 * (batch // BLOCK),))],
         compiler_params=params(28 * batch * width),
@@ -385,10 +370,10 @@
 
     payload = pl.pallas_call(
         pass_kernel,
-        in_specs=[ANY] * 3,
-        out_specs=[ANY] * 3,
+        in_specs=[ANY] * 2,
+        out_specs=[ANY] * 2,
         out_shape=[shape(block.shape, BF16) for block in payload],
-        input_output_aliases={i: i for i in range(3)},
+        input_output_aliases={0: 0, 1: 1},
         cost_estimate=BUSY,
         compiler_params=params(0),
     )(*payload)
@@ -396,11 +381,8 @@
     order = farthest_first(experts)
     chunks, arrived = [], []
     for part in range(2):
-        came = {0: payload[part]}
-        for j in farthest_first(layers)[1:]:
-            if j != 1 or part == 0:
-                came[j] = swap(payload[2 if j == 1 else part], "attn", j)
-        chunks += [came[j] for j in sorted(came)]
+        came = {j: swap(payload[part], "attn", j) for j in farthest_first(layers)}
+        chunks += [came[j] for j in range(layers)]
         slots = pl.pallas_call(
             functools.partial(split_kernel, layers=layers, part=part),
             in_specs=[SCALAR] + [WHOLE] * len(chunks),

time: 55 us -> 52.8 us (0.960)
  waiting for transfers between devices: 13.8 us -> 10.6 us
  starting transfers between devices: 25.8 us -> 26.8 us
    ppermute x23 -> x24, waiting for transfers between devices: 13.8 us -> 10.6 us  [swap(): return lax.ppermute(value, axis, [(i, i ^ step) for i in range(count)])]
    ppermute x23 -> x24, starting transfers between devices: 25.8 us -> 26.8 us  [swap(): return lax.ppermute(value, axis, [(i, i ^ step) for i in range(count)])]
  transfers between devices with their start and end apart: 23 -> 24, of which waited for: 8 -> 8; matrix products, arithmetic and copies ran while one was open for 0% -> 0% of each run, Pallas kernels for 11% -> 12%
where the time goes in v13:
time: 52.8 us; the launch traced here: 52.7 us
  starting transfers between devices  26.8 us (51%)
  Pallas kernels  15 us (28%)
  waiting for transfers between devices  10.6 us (20%)
    ppermute x24, starting transfers between devices, swap(): return lax.ppermute(value, axis, [(i, i ^ step) for i in range(count)])  26.8 us
    ppermute x24, waiting for transfers between devices, swap(): return lax.ppermute(value, axis, [(i, i ^ step) for i in range(count)])  10.6 us
    pallas_call x1, Pallas kernels, shards(): pl.pallas_call(functools.partial(middle_kernel, experts=experts), in_spec...  4.17 us
    pallas_call x1, Pallas kernels, shards(): pl.pallas_call(attend_kernel, in_specs=[SCALAR] + [ANY] * len(operands),...  4.01 us
    pallas_call x1, Pallas kernels, shards(): pl.pallas_call(functools.partial(begin_kernel, experts=experts), in_specs...  2.92 us
    pallas_call x1, Pallas kernels, shards(): pl.pallas_call(end_kernel, in_specs=[WHOLE] * 2, out_specs=[WHOLE] * expe...  1.37 us
  transfers between devices with their start and end apart: 24, of which 8 were waited for; matrix products, arithmetic and copies ran while one was open for 0% of the time, Pallas kernels for 12%

profile of v13, /device:TPU:0, one launch (start us, length us, event | category | flops | bytes accessed | tf_op | source)
XLA Modules:
  0.0 52.7 jit_solution(16137568495320048962)
XLA Ops:
  0.0 4.0 %shard_map.109 = (f32[16,3072]{1,0:T(8,128)S(1)}, bf16[16,1664]{1,0:T(8,128)(2,1)S(1)}, bf16[16,1536]{1,0:T(8,128)(2,1)S(1)}) custom-call(s32[1]{0:T(128)} %bitcast._.me_ref, s32[1,16]{1,0:T(1,128)} %bitcast.21, bf16[16,3072]{1,0:T(8,128)(2,1)} %queries_hbm.1, bf16[16,96,512]{2,1,0:T(8,128)(2,1)} %keys_hbm.1, bf16[16,96,512]{2,1,0:T(8,128)(2,1)} %values_hbm.1, ...), custom_call_target="tpu_custom_call" | custom-call | tf_op jit(solution)/shard_map/pallas_call | solution.py:359
  4.0 0.0 slice-start
  4.0 0.0 slice-start.3
  4.0 0.0 slice-start.1
  4.1 0.0 slice-start.2
  4.1 0.0 slice-start.4
  4.1 0.0 slice-start.5
  4.1 0.0 copy-start
  4.1 5.1 %collective-permute-start.2 = (bf16[16,1664]{1,0:T(8,128)(2,1)S(1)}, bf16[16,1664]{1,0:T(8,128)(2,1)S(1)}, u32[]{:S(2)}, u32[]{:S(2)}) collective-permute-start(bf16[16,1664]{1,0:T(8,128)(2,1)S(1)} %get-tuple-element.43.refs_0_), channel_id=1, source_target_pairs={{0,12},{4,8},{8,4},{12,0},{1,13},{5,9},{9,5},{13,1},{2,14},{6,10},... | collective-permute-start | bytes 159752 | tf_op jit(solution)/shard_map/ppermute | solution.py:319
  9.2 0.0 collective-permute-start.1
  9.2 0.6 %collective-permute-start = (bf16[16,1664]{1,0:T(8,128)(2,1)S(1)}, bf16[16,1664]{1,0:T(8,128)(2,1)S(1)}, u32[]{:S(2)}, u32[]{:S(2)}) collective-permute-start(bf16[16,1664]{1,0:T(8,128)(2,1)S(1)} %get-tuple-element.43.refs_0_), channel_id=1, source_target_pairs={{0,4},{4,0},{8,12},{12,8},{1,5},{5,1},{9,13},{13,9},{2,6},{6,2},{1... | collective-permute-start | bytes 159752 | tf_op jit(solution)/shard_map/ppermute | solution.py:319
  9.9 3.7 %collective-permute-start.5 = (bf16[16,1536]{1,0:T(8,128)(2,1)S(1)}, bf16[16,1536]{1,0:T(8,128)(2,1)S(1)}, u32[]{:S(2)}, u32[]{:S(2)}) collective-permute-start(bf16[16,1536]{1,0:T(8,128)(2,1)S(1)} %get-tuple-element.44.refs_4_), channel_id=1, source_target_pairs={{0,12},{4,8},{8,4},{12,0},{1,13},{5,9},{9,5},{13,1},{2,14},{6,10},... | collective-permute-start | bytes 147464 | tf_op jit(solution)/shard_map/ppermute | solution.py:319
  13.6 0.0 collective-permute-start.4
  13.6 0.0 collective-permute-done.2.refs_3_
  13.6 0.6 %collective-permute-start.3 = (bf16[16,1536]{1,0:T(8,128)(2,1)S(1)}, bf16[16,1536]{1,0:T(8,128)(2,1)S(1)}, u32[]{:S(2)}, u32[]{:S(2)}) collective-permute-start(bf16[16,1536]{1,0:T(8,128)(2,1)S(1)} %get-tuple-element.44.refs_4_), channel_id=1, source_target_pairs={{0,4},{4,0},{8,12},{12,8},{1,5},{5,1},{9,13},{13,9},{2,6},{6,2},{1... | collective-permute-start | bytes 147464 | tf_op jit(solution)/shard_map/ppermute | solution.py:319
  14.3 1.4 %collective-permute-done.1.refs_2_ = bf16[16,1664]{1,0:T(8,128)(2,1)S(1)} collective-permute-done((bf16[16,1664]{1,0:T(8,128)(2,1)S(1)}, bf16[16,1664]{1,0:T(8,128)(2,1)S(1)}, u32[]{:S(2)}, u32[]{:S(2)}) %collective-permute-start.1) | collective-permute-done | bytes 53280 | tf_op jit(solution)/shard_map/ppermute | solution.py:319
  15.6 0.0 collective-permute-done.refs_1_
  15.7 0.5 shard_map.113
  16.2 0.1 collective-permute-start.9
  16.2 1.6 %collective-permute-start.10 = (bf16[32,1536]{1,0:T(8,128)(2,1)S(1)}, bf16[32,1536]{1,0:T(8,128)(2,1)S(1)}, u32[]{:S(2)}, u32[]{:S(2)}) collective-permute-start(bf16[32,1536]{1,0:T(8,128)(2,1)S(1)} %get-tuple-element.53), channel_id=1, source_target_pairs={{0,2},{1,3},{2,0},{3,1},{4,6},{5,7},{6,4},{7,5},{8,10},{9,11},{10,... | collective-permute-start | bytes 294920 | tf_op jit(solution)/shard_map/ppermute | solution.py:319
  17.8 0.0 collective-permute-done.5.refs_7_
  17.8 0.3 collective-permute-start.11
  18.1 0.5 collective-permute-done.4.refs_6_
  18.6 0.0 collective-permute-done.3.refs_5_
  18.6 0.5 shard_map.112
  19.1 0.7 %collective-permute-start.6 = (bf16[32,1536]{1,0:T(8,128)(2,1)S(1)}, bf16[32,1536]{1,0:T(8,128)(2,1)S(1)}, u32[]{:S(2)}, u32[]{:S(2)}) collective-permute-start(bf16[32,1536]{1,0:T(8,128)(2,1)S(1)} %get-tuple-element.48), channel_id=1, source_target_pairs={{0,3},{1,2},{2,1},{3,0},{4,7},{5,6},{6,5},{7,4},{8,11},{9,10},{10,... | collective-permute-start | bytes 294920 | tf_op jit(solution)/shard_map/ppermute | solution.py:319
  19.8 1.0 %collective-permute-start.7 = (bf16[32,1536]{1,0:T(8,128)(2,1)S(1)}, bf16[32,1536]{1,0:T(8,128)(2,1)S(1)}, u32[]{:S(2)}, u32[]{:S(2)}) collective-permute-start(bf16[32,1536]{1,0:T(8,128)(2,1)S(1)} %get-tuple-element.49), channel_id=1, source_target_pairs={{0,2},{1,3},{2,0},{3,1},{4,6},{5,7},{6,4},{7,5},{8,10},{9,11},{10,... | collective-permute-start | bytes 294920 | tf_op jit(solution)/shard_map/ppermute | solution.py:319
  20.7 0.3 shard_map.111
  21.1 0.2 collective-permute-done.9.refs_1_
  21.3 0.2 collective-permute-start.8
  21.5 2.0 %collective-permute-done.10.refs_2_ = bf16[32,1536]{1,0:T(8,128)(2,1)S(1)} collective-permute-done((bf16[32,1536]{1,0:T(8,128)(2,1)S(1)}, bf16[32,1536]{1,0:T(8,128)(2,1)S(1)}, u32[]{:S(2)}, u32[]{:S(2)}) %collective-permute-start.10) | collective-permute-done | bytes 98336 | tf_op jit(solution)/shard_map/ppermute | solution.py:319
  23.5 0.0 collective-permute-done.11.refs_3_
  23.5 2.9 %shard_map.114 = (f32[128,2048]{1,0:T(8,128)S(1)}, f32[128,2048]{1,0:T(8,128)S(1)}, bf16[2048,1536]{1,0:T(8,128)(2,1)S(1)}) custom-call(bf16[32,1536]{1,0:T(8,128)(2,1)S(1)} %get-tuple-element.51.refs_0_, bf16[32,1536]{1,0:T(8,128)(2,1)S(1)} %collective-permute-done.9.refs_1_, bf16[32,1536]{1,0:T(8,128)(2,1)S(1)} %collective-permute-done.10.refs_2_, ...), custom_call_target="tpu_custom_call" | custom-call | flops 1610612736 | tf_op jit(solution)/shard_map/pallas_call | solution.py:410
  26.5 0.0 collective-permute-done.6.refs_1_
  26.5 1.2 %collective-permute-done.7.refs_2_ = bf16[32,1536]{1,0:T(8,128)(2,1)S(1)} collective-permute-done((bf16[32,1536]{1,0:T(8,128)(2,1)S(1)}, bf16[32,1536]{1,0:T(8,128)(2,1)S(1)}, u32[]{:S(2)}, u32[]{:S(2)}) %collective-permute-start.7) | collective-permute-done | bytes 98336 | tf_op jit(solution)/shard_map/ppermute | solution.py:319
  27.6 0.0 collective-permute-done.8.refs_3_
  27.6 4.2 %shard_map.115 = (bf16[32,1536]{1,0:T(8,128)(2,1)S(1)}, bf16[32,1536]{1,0:T(8,128)(2,1)S(1)}, bf16[32,1536]{1,0:T(8,128)(2,1)S(1)}, bf16[32,1536]{1,0:T(8,128)(2...) custom-call(bf16[32,1536]{1,0:T(8,128)(2,1)S(1)} %get-tuple-element.47.refs_0_, ...), custom_call_target="tpu_custom_call" | custom-call | tf_op jit(solution)/shard_map/pallas_call | solution.py:421
  31.8 0.1 collective-permute-start.12
  31.9 1.7 %collective-permute-start.13 = (bf16[32,1536]{1,0:T(8,128)(2,1)S(1)}, bf16[32,1536]{1,0:T(8,128)(2,1)S(1)}, u32[]{:S(2)}, u32[]{:S(2)}) collective-permute-start(bf16[32,1536]{1,0:T(8,128)(2,1)S(1)} %get-tuple-element.60), channel_id=1, source_target_pairs={{0,2},{1,3},{2,0},{3,1},{4,6},{5,7},{6,4},{7,5},{8,10},{9,11},{10,... | collective-permute-start | bytes 294920 | tf_op jit(solution)/shard_map/ppermute | solution.py:319
  33.6 0.2 collective-permute-start.14
  33.8 1.4 %shard_map.118 = (bf16[32,1536]{1,0:T(8,128)(2,1)S(1)}, bf16[32,1536]{1,0:T(8,128)(2,1)S(1)}, bf16[32,1536]{1,0:T(8,128)(2,1)S(1)}, bf16[32,1536]{1,0:T(8,128)(2,1)S(1)}) custom-call(bf16[128,2048]{1,0:T(8,128)(2,1)S(1)} %get-tuple-element.67.hidden_ref, bf16[2048,1536]{1,0:T(8,128)(2,1)S(1)} %get-tuple-element.68.down_ref), custom_call_target="tpu_custom_call" | custom-call | flops 805306368 | tf_op jit(solution)/shard_map/pallas_call | solution.py:429
  35.1 0.4 collective-permute-start.18
  35.6 1.6 %collective-permute-start.19 = (bf16[32,1536]{1,0:T(8,128)(2,1)S(1)}, bf16[32,1536]{1,0:T(8,128)(2,1)S(1)}, u32[]{:S(2)}, u32[]{:S(2)}) collective-permute-start(bf16[32,1536]{1,0:T(8,128)(2,1)S(1)} %get-tuple-element.71), channel_id=1, source_target_pairs={{0,2},{1,3},{2,0},{3,1},{4,6},{5,7},{6,4},{7,5},{8,10},{9,11},{10,... | collective-permute-start | bytes 294920 | tf_op jit(solution)/shard_map/ppermute | solution.py:319
  37.2 0.0 collective-permute-done.12.refs_1_
  37.2 0.0 collective-permute-start.20
  37.2 2.1 %collective-permute-done.13.refs_2_ = bf16[32,1536]{1,0:T(8,128)(2,1)S(1)} collective-permute-done((bf16[32,1536]{1,0:T(8,128)(2,1)S(1)}, bf16[32,1536]{1,0:T(8,128)(2,1)S(1)}, u32[]{:S(2)}, u32[]{:S(2)}) %collective-permute-start.13) | collective-permute-done | bytes 98336 | tf_op jit(solution)/shard_map/ppermute | solution.py:319
  39.4 0.0 collective-permute-done.14.refs_3_
  39.4 0.3 shard_map.116
  39.6 2.7 %collective-permute-start.15 = (bf16[16,1536]{1,0:T(8,128)(2,1)S(1)}, bf16[16,1536]{1,0:T(8,128)(2,1)S(1)}, u32[]{:S(2)}, u32[]{:S(2)}) collective-permute-start(bf16[16,1536]{1,0:T(8,128)(2,1)S(1)} %get-tuple-element.64), channel_id=1, source_target_pairs={{0,12},{4,8},{8,4},{12,0},{1,13},{5,9},{9,5},{13,1},{2,14},{6,10},... | collective-permute-start | bytes 147464 | tf_op jit(solution)/shard_map/ppermute | solution.py:319
  42.3 0.0 collective-permute-start.16
  42.3 0.0 collective-permute-done.18.refs_1_
  42.3 1.8 %collective-permute-start.17 = (bf16[16,1536]{1,0:T(8,128)(2,1)S(1)}, bf16[16,1536]{1,0:T(8,128)(2,1)S(1)}, u32[]{:S(2)}, u32[]{:S(2)}) collective-permute-start(bf16[16,1536]{1,0:T(8,128)(2,1)S(1)} %get-tuple-element.66), channel_id=1, source_target_pairs={{0,4},{4,0},{8,12},{12,8},{1,5},{5,1},{9,13},{13,9},{2,6},{6,2},{1... | collective-permute-start | bytes 147464 | tf_op jit(solution)/shard_map/ppermute | solution.py:319
  44.1 0.0 collective-permute-done.19.refs_2_
  44.1 0.0 collective-permute-done.20.refs_3_
  44.1 0.3 shard_map.119
  44.3 2.7 %collective-permute-start.21 = (bf16[16,1536]{1,0:T(8,128)(2,1)S(1)}, bf16[16,1536]{1,0:T(8,128)(2,1)S(1)}, u32[]{:S(2)}, u32[]{:S(2)}) collective-permute-start(bf16[16,1536]{1,0:T(8,128)(2,1)S(1)} %get-tuple-element.74), channel_id=1, source_target_pairs={{0,12},{4,8},{8,4},{12,0},{1,13},{5,9},{9,5},{13,1},{2,14},{6,10},... | collective-permute-start | bytes 147464 | tf_op jit(solution)/shard_map/ppermute | solution.py:319
  47.0 0.0 collective-permute-start.22
  47.0 0.0 collective-permute-done.15.refs_1_
  47.0 1.8 %collective-permute-start.23 = (bf16[16,1536]{1,0:T(8,128)(2,1)S(1)}, bf16[16,1536]{1,0:T(8,128)(2,1)S(1)}, u32[]{:S(2)}, u32[]{:S(2)}) collective-permute-start(bf16[16,1536]{1,0:T(8,128)(2,1)S(1)} %get-tuple-element.76), channel_id=1, source_target_pairs={{0,4},{4,0},{8,12},{12,8},{1,5},{5,1},{9,13},{13,9},{2,6},{6,2},{1... | collective-permute-start | bytes 147464 | tf_op jit(solution)/shard_map/ppermute | solution.py:319
  48.8 0.0 collective-permute-done.17.refs_3_
  48.8 1.5 %collective-permute-done.21.refs_2_ = bf16[16,1536]{1,0:T(8,128)(2,1)S(1)} collective-permute-done((bf16[16,1536]{1,0:T(8,128)(2,1)S(1)}, bf16[16,1536]{1,0:T(8,128)(2,1)S(1)}, u32[]{:S(2)}, u32[]{:S(2)}) %collective-permute-start.21) | collective-permute-done | bytes 49184 | tf_op jit(solution)/shard_map/ppermute | solution.py:319
  50.3 1.7 %collective-permute-done.22.refs_3_ = bf16[16,1536]{1,0:T(8,128)(2,1)S(1)} collective-permute-done((bf16[16,1536]{1,0:T(8,128)(2,1)S(1)}, bf16[16,1536]{1,0:T(8,128)(2,1)S(1)}, u32[]{:S(2)}, u32[]{:S(2)}) %collective-permute-start.22) | collective-permute-done | bytes 49184 | tf_op jit(solution)/shard_map/ppermute | solution.py:319
  52.0 0.0 collective-permute-done.23.refs_4_
  52.0 0.7 %shard_map.120 = bf16[16,3072]{1,0:T(8,128)(2,1)} custom-call(bf16[16,1536]{1,0:T(8,128)(2,1)S(1)} %shard_map.117.refs_0_, f32[16,1536]{1,0:T(8,128)S(1)} %get-tuple-element.73.refs_1_, bf16[16,1536]{1,0:T(8,128)(2,1)S(1)} %collective-permute-done.21.refs_2_, bf16[16,1536]{1,0:T(8,128)(2,1)S(1)} %collective-permute-done.22.refs_3_, ...), custom_call_target="tpu_custom_call" | custom-call | tf_op jit(solution)/shard_map/pallas_call | solution.py:453
  (12 shorter events, 0.0 us)
Async XLA Ops:
  4.0 19.5 %slice-start = ((s8[12582912]{0:T(1024)(128)(4,1)}), s8[4194304]{0:T(1024)(128)(4,1)S(1)}, s32[]{:S(2)}) async-start(s8[12582912]{0:T(1024)(128)(4,1)} %bitcast.8), calls=%async_computation | async-start | bytes 8388608
  4.0 19.4 %slice-start.3 = ((s8[12582912]{0:T(1024)(128)(4,1)}), s8[4194304]{0:T(1024)(128)(4,1)S(1)}, s32[]{:S(2)}) async-start(s8[12582912]{0:T(1024)(128)(4,1)} %bitcast.12), calls=%async_computation.3 | async-start | bytes 8388608
  4.0 19.4 %slice-start.1 = ((s8[12582912]{0:T(1024)(128)(4,1)}), s8[4194304]{0:T(1024)(128)(4,1)S(1)}, s32[]{:S(2)}) async-start(s8[12582912]{0:T(1024)(128)(4,1)} %bitcast.8), calls=%async_computation.1 | async-start | bytes 8388608
  4.1 19.4 %slice-start.2 = ((s8[12582912]{0:T(1024)(128)(4,1)}), s8[4194304]{0:T(1024)(128)(4,1)S(1)}, s32[]{:S(2)}) async-start(s8[12582912]{0:T(1024)(128)(4,1)} %bitcast.8), calls=%async_computation.2 | async-start | bytes 8388608
  4.1 19.4 %slice-start.4 = ((s8[12582912]{0:T(1024)(128)(4,1)}), s8[4194304]{0:T(1024)(128)(4,1)S(1)}, s32[]{:S(2)}) async-start(s8[12582912]{0:T(1024)(128)(4,1)} %bitcast.12), calls=%async_computation.4 | async-start | bytes 8388608
  4.1 19.4 %slice-start.5 = ((s8[12582912]{0:T(1024)(128)(4,1)}), s8[4194304]{0:T(1024)(128)(4,1)S(1)}, s32[]{:S(2)}) async-start(s8[12582912]{0:T(1024)(128)(4,1)} %bitcast.12), calls=%async_computation.5 | async-start | bytes 8388608
  4.1 16.6 %copy-start = (bf16[3072,4]{0,1:T(4,128)(2,1)S(1)}, bf16[3072,4]{0,1:T(4,128)(2,1)}, u32[]{:S(2)}) copy-start(bf16[3072,4]{0,1:T(4,128)(2,1)} %param.18) | copy-start | bytes 73732
  4.1 9.5 %collective-permute-start.2 = (bf16[16,1664]{1,0:T(8,128)(2,1)S(1)}, bf16[16,1664]{1,0:T(8,128)(2,1)S(1)}, u32[]{:S(2)}, u32[]{:S(2)}) collective-permute-start(bf16[16,1664]{1,0:T(8,128)(2,1)S(1)} %get-tuple-element.43.refs_0_), channel_id=1, source_target_pairs={{0,12},{4,8},{8,4},{12,0},{1,13},{5,9},{9,5},{13,1},{2,14},{6,10},... | collective-permute-start | bytes 159752 | tf_op jit(solution)/shard_map/ppermute | solution.py:319
  9.2 6.4 %collective-permute-start.1 = (bf16[16,1664]{1,0:T(8,128)(2,1)S(1)}, bf16[16,1664]{1,0:T(8,128)(2,1)S(1)}, u32[]{:S(2)}, u32[]{:S(2)}) collective-permute-start(bf16[16,1664]{1,0:T(8,128)(2,1)S(1)} %get-tuple-element.43.refs_0_), channel_id=1, source_target_pairs={{0,8},{4,12},{8,0},{12,4},{1,9},{5,13},{9,1},{13,5},{2,10},{6,14},... | collective-permute-start | bytes 159752 | tf_op jit(solution)/shard_map/ppermute | solution.py:319
  9.2 6.4 %collective-permute-start = (bf16[16,1664]{1,0:T(8,128)(2,1)S(1)}, bf16[16,1664]{1,0:T(8,128)(2,1)S(1)}, u32[]{:S(2)}, u32[]{:S(2)}) collective-permute-start(bf16[16,1664]{1,0:T(8,128)(2,1)S(1)} %get-tuple-element.43.refs_0_), channel_id=1, source_target_pairs={{0,4},{4,0},{8,12},{12,8},{1,5},{5,1},{9,13},{13,9},{2,6},{6,2},{1... | collective-permute-start | bytes 159752 | tf_op jit(solution)/shard_map/ppermute | solution.py:319
  9.9 7.9 %collective-permute-start.5 = (bf16[16,1536]{1,0:T(8,128)(2,1)S(1)}, bf16[16,1536]{1,0:T(8,128)(2,1)S(1)}, u32[]{:S(2)}, u32[]{:S(2)}) collective-permute-start(bf16[16,1536]{1,0:T(8,128)(2,1)S(1)} %get-tuple-element.44.refs_4_), channel_id=1, source_target_pairs={{0,12},{4,8},{8,4},{12,0},{1,13},{5,9},{9,5},{13,1},{2,14},{6,10},... | collective-permute-start | bytes 147464 | tf_op jit(solution)/shard_map/ppermute | solution.py:319
  13.6 5.0 %collective-permute-start.4 = (bf16[16,1536]{1,0:T(8,128)(2,1)S(1)}, bf16[16,1536]{1,0:T(8,128)(2,1)S(1)}, u32[]{:S(2)}, u32[]{:S(2)}) collective-permute-start(bf16[16,1536]{1,0:T(8,128)(2,1)S(1)} %get-tuple-element.44.refs_4_), channel_id=1, source_target_pairs={{0,8},{4,12},{8,0},{12,4},{1,9},{5,13},{9,1},{13,5},{2,10},{6,14},... | collective-permute-start | bytes 147464 | tf_op jit(solution)/shard_map/ppermute | solution.py:319
  13.6 5.0 %collective-permute-start.3 = (bf16[16,1536]{1,0:T(8,128)(2,1)S(1)}, bf16[16,1536]{1,0:T(8,128)(2,1)S(1)}, u32[]{:S(2)}, u32[]{:S(2)}) collective-permute-start(bf16[16,1536]{1,0:T(8,128)(2,1)S(1)} %get-tuple-element.44.refs_4_), channel_id=1, source_target_pairs={{0,4},{4,0},{8,12},{12,8},{1,5},{5,1},{9,13},{13,9},{2,6},{6,2},{1... | collective-permute-start | bytes 147464 | tf_op jit(solution)/shard_map/ppermute | solution.py:319
  16.2 5.1 %collective-permute-start.9 = (bf16[32,1536]{1,0:T(8,128)(2,1)S(1)}, bf16[32,1536]{1,0:T(8,128)(2,1)S(1)}, u32[]{:S(2)}, u32[]{:S(2)}) collective-permute-start(bf16[32,1536]{1,0:T(8,128)(2,1)S(1)} %get-tuple-element.52), channel_id=1, source_target_pairs={{0,3},{1,2},{2,1},{3,0},{4,7},{5,6},{6,5},{7,4},{8,11},{9,10},{10,... | collective-permute-start | bytes 294920 | tf_op jit(solution)/shard_map/ppermute | solution.py:319
  16.2 7.2 %collective-permute-start.10 = (bf16[32,1536]{1,0:T(8,128)(2,1)S(1)}, bf16[32,1536]{1,0:T(8,128)(2,1)S(1)}, u32[]{:S(2)}, u32[]{:S(2)}) collective-permute-start(bf16[32,1536]{1,0:T(8,128)(2,1)S(1)} %get-tuple-element.53), channel_id=1, source_target_pairs={{0,2},{1,3},{2,0},{3,1},{4,6},{5,7},{6,4},{7,5},{8,10},{9,11},{10,... | collective-permute-start | bytes 294920 | tf_op jit(solution)/shard_map/ppermute | solution.py:319
  17.8 5.7 %collective-permute-start.11 = (bf16[32,1536]{1,0:T(8,128)(2,1)S(1)}, bf16[32,1536]{1,0:T(8,128)(2,1)S(1)}, u32[]{:S(2)}, u32[]{:S(2)}) collective-permute-start(bf16[32,1536]{1,0:T(8,128)(2,1)S(1)} %get-tuple-element.54), channel_id=1, source_target_pairs={{0,1},{1,0},{2,3},{3,2},{4,5},{5,4},{6,7},{7,6},{8,9},{9,8},{10,11... | collective-permute-start | bytes 294920 | tf_op jit(solution)/shard_map/ppermute | solution.py:319
  19.1 7.4 %collective-permute-start.6 = (bf16[32,1536]{1,0:T(8,128)(2,1)S(1)}, bf16[32,1536]{1,0:T(8,128)(2,1)S(1)}, u32[]{:S(2)}, u32[]{:S(2)}) collective-permute-start(bf16[32,1536]{1,0:T(8,128)(2,1)S(1)} %get-tuple-element.48), channel_id=1, source_target_pairs={{0,3},{1,2},{2,1},{3,0},{4,7},{5,6},{6,5},{7,4},{8,11},{9,10},{10,... | collective-permute-start | bytes 294920 | tf_op jit(solution)/shard_map/ppermute | solution.py:319
  19.8 7.9 %collective-permute-start.7 = (bf16[32,1536]{1,0:T(8,128)(2,1)S(1)}, bf16[32,1536]{1,0:T(8,128)(2,1)S(1)}, u32[]{:S(2)}, u32[]{:S(2)}) collective-permute-start(bf16[32,1536]{1,0:T(8,128)(2,1)S(1)} %get-tuple-element.49), channel_id=1, source_target_pairs={{0,2},{1,3},{2,0},{3,1},{4,6},{5,7},{6,4},{7,5},{8,10},{9,11},{10,... | collective-permute-start | bytes 294920 | tf_op jit(solution)/shard_map/ppermute | solution.py:319
  21.3 6.4 %collective-permute-start.8 = (bf16[32,1536]{1,0:T(8,128)(2,1)S(1)}, bf16[32,1536]{1,0:T(8,128)(2,1)S(1)}, u32[]{:S(2)}, u32[]{:S(2)}) collective-permute-start(bf16[32,1536]{1,0:T(8,128)(2,1)S(1)} %get-tuple-element.50), channel_id=1, source_target_pairs={{0,1},{1,0},{2,3},{3,2},{4,5},{5,4},{6,7},{7,6},{8,9},{9,8},{10,11... | collective-permute-start | bytes 294920 | tf_op jit(solution)/shard_map/ppermute | solution.py:319
  31.8 5.4 %collective-permute-start.12 = (bf16[32,1536]{1,0:T(8,128)(2,1)S(1)}, bf16[32,1536]{1,0:T(8,128)(2,1)S(1)}, u32[]{:S(2)}, u32[]{:S(2)}) collective-permute-start(bf16[32,1536]{1,0:T(8,128)(2,1)S(1)} %get-tuple-element.59), channel_id=1, source_target_pairs={{0,3},{1,2},{2,1},{3,0},{4,7},{5,6},{6,5},{7,4},{8,11},{9,10},{10,... | collective-permute-start | bytes 294920 | tf_op jit(solution)/shard_map/ppermute | solution.py:319
  31.9 7.4 %collective-permute-start.13 = (bf16[32,1536]{1,0:T(8,128)(2,1)S(1)}, bf16[32,1536]{1,0:T(8,128)(2,1)S(1)}, u32[]{:S(2)}, u32[]{:S(2)}) collective-permute-start(bf16[32,1536]{1,0:T(8,128)(2,1)S(1)} %get-tuple-element.60), channel_id=1, source_target_pairs={{0,2},{1,3},{2,0},{3,1},{4,6},{5,7},{6,4},{7,5},{8,10},{9,11},{10,... | collective-permute-start | bytes 294920 | tf_op jit(solution)/shard_map/ppermute | solution.py:319
  33.6 5.8 %collective-permute-start.14 = (bf16[32,1536]{1,0:T(8,128)(2,1)S(1)}, bf16[32,1536]{1,0:T(8,128)(2,1)S(1)}, u32[]{:S(2)}, u32[]{:S(2)}) collective-permute-start(bf16[32,1536]{1,0:T(8,128)(2,1)S(1)} %get-tuple-element.61), channel_id=1, source_target_pairs={{0,1},{1,0},{2,3},{3,2},{4,5},{5,4},{6,7},{7,6},{8,9},{9,8},{10,11... | collective-permute-start | bytes 294920 | tf_op jit(solution)/shard_map/ppermute | solution.py:319
  35.1 7.2 %collective-permute-start.18 = (bf16[32,1536]{1,0:T(8,128)(2,1)S(1)}, bf16[32,1536]{1,0:T(8,128)(2,1)S(1)}, u32[]{:S(2)}, u32[]{:S(2)}) collective-permute-start(bf16[32,1536]{1,0:T(8,128)(2,1)S(1)} %get-tuple-element.70), channel_id=1, source_target_pairs={{0,3},{1,2},{2,1},{3,0},{4,7},{5,6},{6,5},{7,4},{8,11},{9,10},{10,... | collective-permute-start | bytes 294920 | tf_op jit(solution)/shard_map/ppermute | solution.py:319
  35.6 8.5 %collective-permute-start.19 = (bf16[32,1536]{1,0:T(8,128)(2,1)S(1)}, bf16[32,1536]{1,0:T(8,128)(2,1)S(1)}, u32[]{:S(2)}, u32[]{:S(2)}) collective-permute-start(bf16[32,1536]{1,0:T(8,128)(2,1)S(1)} %get-tuple-element.71), channel_id=1, source_target_pairs={{0,2},{1,3},{2,0},{3,1},{4,6},{5,7},{6,4},{7,5},{8,10},{9,11},{10,... | collective-permute-start | bytes 294920 | tf_op jit(solution)/shard_map/ppermute | solution.py:319
  37.2 6.9 %collective-permute-start.20 = (bf16[32,1536]{1,0:T(8,128)(2,1)S(1)}, bf16[32,1536]{1,0:T(8,128)(2,1)S(1)}, u32[]{:S(2)}, u32[]{:S(2)}) collective-permute-start(bf16[32,1536]{1,0:T(8,128)(2,1)S(1)} %get-tuple-element.72), channel_id=1, source_target_pairs={{0,1},{1,0},{2,3},{3,2},{4,5},{5,4},{6,7},{7,6},{8,9},{9,8},{10,11... | collective-permute-start | bytes 294920 | tf_op jit(solution)/shard_map/ppermute | solution.py:319
  39.6 7.4 %collective-permute-start.15 = (bf16[16,1536]{1,0:T(8,128)(2,1)S(1)}, bf16[16,1536]{1,0:T(8,128)(2,1)S(1)}, u32[]{:S(2)}, u32[]{:S(2)}) collective-permute-start(bf16[16,1536]{1,0:T(8,128)(2,1)S(1)} %get-tuple-element.64), channel_id=1, source_target_pairs={{0,12},{4,8},{8,4},{12,0},{1,13},{5,9},{9,5},{13,1},{2,14},{6,10},... | collective-permute-start | bytes 147464 | tf_op jit(solution)/shard_map/ppermute | solution.py:319
  42.3 6.5 %collective-permute-start.16 = (bf16[16,1536]{1,0:T(8,128)(2,1)S(1)}, bf16[16,1536]{1,0:T(8,128)(2,1)S(1)}, u32[]{:S(2)}, u32[]{:S(2)}) collective-permute-start(bf16[16,1536]{1,0:T(8,128)(2,1)S(1)} %get-tuple-element.65), channel_id=1, source_target_pairs={{0,8},{4,12},{8,0},{12,4},{1,9},{5,13},{9,1},{13,5},{2,10},{6,14},... | collective-permute-start | bytes 147464 | tf_op jit(solution)/shard_map/ppermute | solution.py:319
  42.3 6.5 %collective-permute-start.17 = (bf16[16,1536]{1,0:T(8,128)(2,1)S(1)}, bf16[16,1536]{1,0:T(8,128)(2,1)S(1)}, u32[]{:S(2)}, u32[]{:S(2)}) collective-permute-start(bf16[16,1536]{1,0:T(8,128)(2,1)S(1)} %get-tuple-element.66), channel_id=1, source_target_pairs={{0,4},{4,0},{8,12},{12,8},{1,5},{5,1},{9,13},{13,9},{2,6},{6,2},{1... | collective-permute-start | bytes 147464 | tf_op jit(solution)/shard_map/ppermute | solution.py:319
  44.3 6.0 %collective-permute-start.21 = (bf16[16,1536]{1,0:T(8,128)(2,1)S(1)}, bf16[16,1536]{1,0:T(8,128)(2,1)S(1)}, u32[]{:S(2)}, u32[]{:S(2)}) collective-permute-start(bf16[16,1536]{1,0:T(8,128)(2,1)S(1)} %get-tuple-element.74), channel_id=1, source_target_pairs={{0,12},{4,8},{8,4},{12,0},{1,13},{5,9},{9,5},{13,1},{2,14},{6,10},... | collective-permute-start | bytes 147464 | tf_op jit(solution)/shard_map/ppermute | solution.py:319
  47.0 5.0 %collective-permute-start.22 = (bf16[16,1536]{1,0:T(8,128)(2,1)S(1)}, bf16[16,1536]{1,0:T(8,128)(2,1)S(1)}, u32[]{:S(2)}, u32[]{:S(2)}) collective-permute-start(bf16[16,1536]{1,0:T(8,128)(2,1)S(1)} %get-tuple-element.75), channel_id=1, source_target_pairs={{0,8},{4,12},{8,0},{12,4},{1,9},{5,13},{9,1},{13,5},{2,10},{6,14},... | collective-permute-start | bytes 147464 | tf_op jit(solution)/shard_map/ppermute | solution.py:319
  47.0 5.0 %collective-permute-start.23 = (bf16[16,1536]{1,0:T(8,128)(2,1)S(1)}, bf16[16,1536]{1,0:T(8,128)(2,1)S(1)}, u32[]{:S(2)}, u32[]{:S(2)}) collective-permute-start(bf16[16,1536]{1,0:T(8,128)(2,1)S(1)} %get-tuple-element.76), channel_id=1, source_target_pairs={{0,4},{4,0},{8,12},{12,8},{1,5},{5,1},{9,13},{13,9},{2,6},{6,2},{1... | collective-permute-start | bytes 147464 | tf_op jit(solution)/shard_map/ppermute | solution.py:319

commit v14 on v13

--- a/solution.py
+++ b/solution.py
@@ -36,20 +36,25 @@
     return lax.broadcasted_iota(jnp.int32, shape, dim)
 
 
+def split(index, size):
+    if size & (size - 1):
+        return lax.div(index, size), lax.rem(index, size)
+    return index >> (size.bit_length() - 1), index & (size - 1)
+
+
 def slot_map(owners, chunks, batch, experts):
     rows, slots = chunks * batch, experts * chunks * CAP
     slot = iota((rows, slots), 1)
     row = iota((rows, slots), 0)
-    expert = slot // (chunks * CAP)
-    chunk = (slot // CAP) % chunks
+    group, wanted = split(slot, CAP)
+    expert, chunk = split(group, chunks)
     named = (owners[:, 0:1] == expert) | (owners[:, 1:2] == expert)
-    named = named & (row // batch == chunk)
+    named = named & (split(row, batch)[0] == chunk)
     named = jnp.where(named, 1.0, 0.0)
     left, right = iota((rows, rows), 0), iota((rows, rows), 1)
     before = jnp.where(right < left, 1.0, 0.0).astype(BF16)
     place = dot(before, named.astype(BF16))
-    wanted = (slot % CAP).astype(F32)
-    return jnp.where(place == wanted, named, 0.0)
+    return jnp.where(place == wanted.astype(F32), named, 0.0)
 
 
 def dispatch(me, rows, named, chunks, experts):
@@ -72,7 +77,7 @@
     gate1 = 1.0 / (1.0 + jnp.exp(first - second))
     owners = routes ^ me_ref[0]
     table = slot_map(owners, layers, rows.shape[0] // layers, experts)
-    expert = iota(table.shape, 1) // (layers * CAP)
+    expert, _ = split(iota(table.shape, 1), layers * CAP)
     gates = table * jnp.where(owners[:, 0:1] == expert, gate0, gate1)
     high = gates.astype(BF16)
     high_ref[...] = high
@@ -124,12 +129,12 @@
     queries = queries_ref[...]
     lanes = PAIR * GROUP * batch
     full = -(-lanes // LANES) * LANES
-    request = iota((window, full), 1) % batch
+    _, request = split(iota((window, full), 1), batch)
     length = jnp.zeros((1, full), jnp.int32)
     for r in range(batch):
         length = jnp.where(request[0:1] == r, lengths_ref[0:1, r : r + 1], length)
     visible = iota((window, full), 0) < length
-    owner = iota((lanes, padded), 0) % batch
+    _, owner = split(iota((lanes, padded), 0), batch)
     attended = []
     for i, part in enumerate(parts):
         spread = []
@@ -185,6 +190,19 @@
     pass
 
 
+def pass_on(values, cost, after):
+    first = len(after)
+    return pl.pallas_call(
+        pass_kernel,
+        in_specs=[ANY] * (first + len(values)),
+        out_specs=[ANY] * len(values),
+        out_shape=[jax.ShapeDtypeStruct(value.shape, value.dtype) for value in values],
+        input_output_aliases={first + i: i for i in range(len(values))},
+        cost_estimate=cost,
+        compiler_params=params(0),
+    )(*after, *values)
+
+
 def stack(refs):
     return jnp.concatenate([ref[...] for ref in refs], axis=0)
 
@@ -368,15 +386,7 @@
         cost_estimate=LIGHT,
     )(me, *operands)
 
-    payload = pl.pallas_call(
-        pass_kernel,
-        in_specs=[ANY] * 2,
-        out_specs=[ANY] * 2,
-        out_shape=[shape(block.shape, BF16) for block in payload],
-        input_output_aliases={0: 0, 1: 1},
-        cost_estimate=BUSY,
-        compiler_params=params(0),
-    )(*payload)
+    payload = pass_on(payload, BUSY, [])
 
     order = farthest_first(experts)
     chunks, arrived = [], []
@@ -439,6 +449,8 @@
 
     done = []
     for part, blocks in enumerate((first, second)):
+        if part:
+            blocks = pass_on(blocks, LIGHT, returned[1:2])
         returned = [swap(block, "expert", e) for e, block in zip(order, blocks)]
         mixed = pl.pallas_call(
             functools.partial(mix_kernel, layers=layers, part=part),
@@ -448,7 +460,8 @@
             cost_estimate=LIGHT,
             compiler_params=params(experts * layers * CAP * half),
         )(*gates, *returned, stream)
-        sums = [swap(mixed[j], "attn", j) for j in farthest_first(layers)]
+        distances = [0, 1, *range(layers - 1, 1, -1)] if part else farthest_first(layers)
+        sums = [swap(mixed[j], "attn", j) for j in distances]
         done = [
             pl.pallas_call(
                 add_kernel,

time: 52.8 us -> 52.8 us (level)
  starting transfers between devices: 26.8 us -> 25.8 us
  waiting for transfers between devices: 10.6 us -> 11.5 us
    ppermute x24, starting transfers between devices: 26.8 us -> 25.8 us  [swap(): return lax.ppermute(value, axis, [(i, i ^ step) for i in range(count)])]
    ppermute x24, waiting for transfers between devices: 10.6 us -> 11.5 us  [swap(): return lax.ppermute(value, axis, [(i, i ^ step) for i in range(count)])]
  transfers between devices with their start and end apart: 24 -> 24, of which waited for: 8 -> 11; matrix products, arithmetic and copies ran while one was open for 0% -> 0% of each run, Pallas kernels for 12% -> 12%
where the time goes in v14:
time: 52.8 us; the launch traced here: 52.7 us
  starting transfers between devices  25.8 us (49%)
  Pallas kernels  15 us (28%)
  waiting for transfers between devices  11.5 us (22%)
    ppermute x24, starting transfers between devices, swap(): return lax.ppermute(value, axis, [(i, i ^ step) for i in range(count)])  25.8 us
    ppermute x24, waiting for transfers between devices, swap(): return lax.ppermute(value, axis, [(i, i ^ step) for i in range(count)])  11.5 us
    pallas_call x1, Pallas kernels, shards(): pl.pallas_call(functools.partial(middle_kernel, experts=experts), in_spec...  4.17 us
    pallas_call x1, Pallas kernels, shards(): pl.pallas_call(attend_kernel, in_specs=[SCALAR] + [ANY] * len(operands),...  4.01 us
    pallas_call x1, Pallas kernels, shards(): pl.pallas_call(functools.partial(begin_kernel, experts=experts), in_specs...  2.92 us
    pallas_call x1, Pallas kernels, shards(): pl.pallas_call(end_kernel, in_specs=[WHOLE] * 2, out_specs=[WHOLE] * expe...  1.37 us
  transfers between devices with their start and end apart: 24, of which 11 were waited for; matrix products, arithmetic and copies ran while one was open for 0% of the time, Pallas kernels for 12%

profile of v14, /device:TPU:0, one launch (start us, length us, event | category | flops | bytes accessed | tf_op | source)
XLA Modules:
  0.0 52.7 jit_solution(890165809478726306)
XLA Ops:
  0.0 4.0 %shard_map.109 = (f32[16,3072]{1,0:T(8,128)S(1)}, bf16[16,1664]{1,0:T(8,128)(2,1)S(1)}, bf16[16,1536]{1,0:T(8,128)(2,1)S(1)}) custom-call(s32[1]{0:T(128)} %bitcast._.me_ref, s32[1,16]{1,0:T(1,128)} %bitcast.21, bf16[16,3072]{1,0:T(8,128)(2,1)} %queries_hbm.1, bf16[16,96,512]{2,1,0:T(8,128)(2,1)} %keys_hbm.1, bf16[16,96,512]{2,1,0:T(8,128)(2,1)} %values_hbm.1, ...), custom_call_target="tpu_custom_call" | custom-call | tf_op jit(solution)/shard_map/pallas_call | solution.py:377
  4.0 0.0 slice-start
  4.0 0.0 slice-start.3
  4.0 0.0 slice-start.1
  4.1 0.0 slice-start.2
  4.1 0.0 slice-start.4
  4.1 0.0 slice-start.5
  4.1 0.0 copy-start
  4.1 5.1 %collective-permute-start.2 = (bf16[16,1664]{1,0:T(8,128)(2,1)S(1)}, bf16[16,1664]{1,0:T(8,128)(2,1)S(1)}, u32[]{:S(2)}, u32[]{:S(2)}) collective-permute-start(bf16[16,1664]{1,0:T(8,128)(2,1)S(1)} %get-tuple-element.47.refs_0_), channel_id=1, source_target_pairs={{0,12},{4,8},{8,4},{12,0},{1,13},{5,9},{9,5},{13,1},{2,14},{6,10},... | collective-permute-start | bytes 159752 | tf_op jit(solution)/shard_map/ppermute | solution.py:337
  9.2 0.0 collective-permute-start.1
  9.2 0.6 %collective-permute-start = (bf16[16,1664]{1,0:T(8,128)(2,1)S(1)}, bf16[16,1664]{1,0:T(8,128)(2,1)S(1)}, u32[]{:S(2)}, u32[]{:S(2)}) collective-permute-start(bf16[16,1664]{1,0:T(8,128)(2,1)S(1)} %get-tuple-element.47.refs_0_), channel_id=1, source_target_pairs={{0,4},{4,0},{8,12},{12,8},{1,5},{5,1},{9,13},{13,9},{2,6},{6,2},{1... | collective-permute-start | bytes 159752 | tf_op jit(solution)/shard_map/ppermute | solution.py:337
  9.9 3.7 %collective-permute-start.5 = (bf16[16,1536]{1,0:T(8,128)(2,1)S(1)}, bf16[16,1536]{1,0:T(8,128)(2,1)S(1)}, u32[]{:S(2)}, u32[]{:S(2)}) collective-permute-start(bf16[16,1536]{1,0:T(8,128)(2,1)S(1)} %get-tuple-element.48.refs_4_), channel_id=1, source_target_pairs={{0,12},{4,8},{8,4},{12,0},{1,13},{5,9},{9,5},{13,1},{2,14},{6,10},... | collective-permute-start | bytes 147464 | tf_op jit(solution)/shard_map/ppermute | solution.py:337
  13.6 0.0 collective-permute-start.4
  13.6 0.0 collective-permute-done.2.refs_3_
  13.6 0.6 %collective-permute-start.3 = (bf16[16,1536]{1,0:T(8,128)(2,1)S(1)}, bf16[16,1536]{1,0:T(8,128)(2,1)S(1)}, u32[]{:S(2)}, u32[]{:S(2)}) collective-permute-start(bf16[16,1536]{1,0:T(8,128)(2,1)S(1)} %get-tuple-element.48.refs_4_), channel_id=1, source_target_pairs={{0,4},{4,0},{8,12},{12,8},{1,5},{5,1},{9,13},{13,9},{2,6},{6,2},{1... | collective-permute-start | bytes 147464 | tf_op jit(solution)/shard_map/ppermute | solution.py:337
  14.3 1.4 %collective-permute-done.1.refs_2_ = bf16[16,1664]{1,0:T(8,128)(2,1)S(1)} collective-permute-done((bf16[16,1664]{1,0:T(8,128)(2,1)S(1)}, bf16[16,1664]{1,0:T(8,128)(2,1)S(1)}, u32[]{:S(2)}, u32[]{:S(2)}) %collective-permute-start.1) | collective-permute-done | bytes 53280 | tf_op jit(solution)/shard_map/ppermute | solution.py:337
  15.6 0.0 collective-permute-done.refs_1_
  15.7 0.5 shard_map.113
  16.2 0.1 collective-permute-start.9
  16.2 1.6 %collective-permute-start.10 = (bf16[32,1536]{1,0:T(8,128)(2,1)S(1)}, bf16[32,1536]{1,0:T(8,128)(2,1)S(1)}, u32[]{:S(2)}, u32[]{:S(2)}) collective-permute-start(bf16[32,1536]{1,0:T(8,128)(2,1)S(1)} %get-tuple-element.57), channel_id=1, source_target_pairs={{0,2},{1,3},{2,0},{3,1},{4,6},{5,7},{6,4},{7,5},{8,10},{9,11},{10,... | collective-permute-start | bytes 294920 | tf_op jit(solution)/shard_map/ppermute | solution.py:337
  17.8 0.0 collective-permute-done.5.refs_7_
  17.8 0.3 collective-permute-start.11
  18.1 0.5 collective-permute-done.4.refs_6_
  18.6 0.0 collective-permute-done.3.refs_5_
  18.6 0.5 shard_map.112
  19.1 0.7 %collective-permute-start.6 = (bf16[32,1536]{1,0:T(8,128)(2,1)S(1)}, bf16[32,1536]{1,0:T(8,128)(2,1)S(1)}, u32[]{:S(2)}, u32[]{:S(2)}) collective-permute-start(bf16[32,1536]{1,0:T(8,128)(2,1)S(1)} %get-tuple-element.52), channel_id=1, source_target_pairs={{0,3},{1,2},{2,1},{3,0},{4,7},{5,6},{6,5},{7,4},{8,11},{9,10},{10,... | collective-permute-start | bytes 294920 | tf_op jit(solution)/shard_map/ppermute | solution.py:337
  19.8 1.0 %collective-permute-start.7 = (bf16[32,1536]{1,0:T(8,128)(2,1)S(1)}, bf16[32,1536]{1,0:T(8,128)(2,1)S(1)}, u32[]{:S(2)}, u32[]{:S(2)}) collective-permute-start(bf16[32,1536]{1,0:T(8,128)(2,1)S(1)} %get-tuple-element.53), channel_id=1, source_target_pairs={{0,2},{1,3},{2,0},{3,1},{4,6},{5,7},{6,4},{7,5},{8,10},{9,11},{10,... | collective-permute-start | bytes 294920 | tf_op jit(solution)/shard_map/ppermute | solution.py:337
  20.8 0.3 shard_map.111
  21.1 0.2 collective-permute-done.9.refs_1_
  21.3 0.2 collective-permute-start.8
  21.5 2.0 %collective-permute-done.10.refs_2_ = bf16[32,1536]{1,0:T(8,128)(2,1)S(1)} collective-permute-done((bf16[32,1536]{1,0:T(8,128)(2,1)S(1)}, bf16[32,1536]{1,0:T(8,128)(2,1)S(1)}, u32[]{:S(2)}, u32[]{:S(2)}) %collective-permute-start.10) | collective-permute-done | bytes 98336 | tf_op jit(solution)/shard_map/ppermute | solution.py:337
  23.5 0.0 collective-permute-done.11.refs_3_
  23.5 2.9 %shard_map.114 = (f32[128,2048]{1,0:T(8,128)S(1)}, f32[128,2048]{1,0:T(8,128)S(1)}, bf16[2048,1536]{1,0:T(8,128)(2,1)S(1)}) custom-call(bf16[32,1536]{1,0:T(8,128)(2,1)S(1)} %get-tuple-element.55.refs_0_, bf16[32,1536]{1,0:T(8,128)(2,1)S(1)} %collective-permute-done.9.refs_1_, bf16[32,1536]{1,0:T(8,128)(2,1)S(1)} %collective-permute-done.10.refs_2_, ...), custom_call_target="tpu_custom_call" | custom-call | flops 1610612736 | tf_op jit(solution)/shard_map/pallas_call | solution.py:420
  26.5 0.0 collective-permute-done.6.refs_1_
  26.5 1.2 %collective-permute-done.7.refs_2_ = bf16[32,1536]{1,0:T(8,128)(2,1)S(1)} collective-permute-done((bf16[32,1536]{1,0:T(8,128)(2,1)S(1)}, bf16[32,1536]{1,0:T(8,128)(2,1)S(1)}, u32[]{:S(2)}, u32[]{:S(2)}) %collective-permute-start.7) | collective-permute-done | bytes 98336 | tf_op jit(solution)/shard_map/ppermute | solution.py:337
  27.6 0.0 collective-permute-done.8.refs_3_
  27.6 4.2 %shard_map.115 = (bf16[32,1536]{1,0:T(8,128)(2,1)S(1)}, bf16[32,1536]{1,0:T(8,128)(2,1)S(1)}, bf16[32,1536]{1,0:T(8,128)(2,1)S(1)}, bf16[32,1536]{1,0:T(8,128)(2...) custom-call(bf16[32,1536]{1,0:T(8,128)(2,1)S(1)} %get-tuple-element.51.refs_0_, ...), custom_call_target="tpu_custom_call" | custom-call | tf_op jit(solution)/shard_map/pallas_call | solution.py:431
  31.8 0.1 collective-permute-start.12
  31.9 1.7 %collective-permute-start.13 = (bf16[32,1536]{1,0:T(8,128)(2,1)S(1)}, bf16[32,1536]{1,0:T(8,128)(2,1)S(1)}, u32[]{:S(2)}, u32[]{:S(2)}) collective-permute-start(bf16[32,1536]{1,0:T(8,128)(2,1)S(1)} %get-tuple-element.64), channel_id=1, source_target_pairs={{0,2},{1,3},{2,0},{3,1},{4,6},{5,7},{6,4},{7,5},{8,10},{9,11},{10,... | collective-permute-start | bytes 294920 | tf_op jit(solution)/shard_map/ppermute | solution.py:337
  33.6 0.2 collective-permute-start.14
  33.8 1.4 %shard_map.118 = (bf16[32,1536]{1,0:T(8,128)(2,1)S(1)}, bf16[32,1536]{1,0:T(8,128)(2,1)S(1)}, bf16[32,1536]{1,0:T(8,128)(2,1)S(1)}, bf16[32,1536]{1,0:T(8,128)(2,1)S(1)}) custom-call(bf16[128,2048]{1,0:T(8,128)(2,1)S(1)} %get-tuple-element.71.hidden_ref, bf16[2048,1536]{1,0:T(8,128)(2,1)S(1)} %get-tuple-element.72.down_ref), custom_call_target="tpu_custom_call" | custom-call | flops 805306368 | tf_op jit(solution)/shard_map/pallas_call | solution.py:439
  35.1 1.6 %collective-permute-done.12.refs_1_.__0_ = bf16[32,1536]{1,0:T(8,128)(2,1)S(1)} collective-permute-done((bf16[32,1536]{1,0:T(8,128)(2,1)S(1)}, bf16[32,1536]{1,0:T(8,128)(2,1)S(1)}, u32[]{:S(2)}, u32[]{:S(2)}) %collective-permute-start.12) | collective-permute-done | bytes 98336 | tf_op jit(solution)/shard_map/ppermute | solution.py:337
  36.7 0.0 collective-permute-start.18
  36.7 2.0 %collective-permute-start.19 = (bf16[32,1536]{1,0:T(8,128)(2,1)S(1)}, bf16[32,1536]{1,0:T(8,128)(2,1)S(1)}, u32[]{:S(2)}, u32[]{:S(2)}) collective-permute-start(bf16[32,1536]{1,0:T(8,128)(2,1)S(1)} %get-tuple-element.79), channel_id=1, source_target_pairs={{0,2},{1,3},{2,0},{3,1},{4,6},{5,7},{6,4},{7,5},{8,10},{9,11},{10,... | collective-permute-start | bytes 294920 | tf_op jit(solution)/shard_map/ppermute | solution.py:337
  38.7 0.0 collective-permute-start.20
  38.7 0.4 collective-permute-done.13.refs_2_
  39.1 0.0 collective-permute-done.14.refs_3_
  39.1 0.3 shard_map.116
  39.4 2.7 %collective-permute-start.15 = (bf16[16,1536]{1,0:T(8,128)(2,1)S(1)}, bf16[16,1536]{1,0:T(8,128)(2,1)S(1)}, u32[]{:S(2)}, u32[]{:S(2)}) collective-permute-start(bf16[16,1536]{1,0:T(8,128)(2,1)S(1)} %get-tuple-element.68), channel_id=1, source_target_pairs={{0,12},{4,8},{8,4},{12,0},{1,13},{5,9},{9,5},{13,1},{2,14},{6,10},... | collective-permute-start | bytes 147464 | tf_op jit(solution)/shard_map/ppermute | solution.py:337
  42.1 0.0 collective-permute-start.16
  42.1 0.0 collective-permute-done.18.refs_1_
  42.1 1.7 %collective-permute-start.17 = (bf16[16,1536]{1,0:T(8,128)(2,1)S(1)}, bf16[16,1536]{1,0:T(8,128)(2,1)S(1)}, u32[]{:S(2)}, u32[]{:S(2)}) collective-permute-start(bf16[16,1536]{1,0:T(8,128)(2,1)S(1)} %get-tuple-element.70), channel_id=1, source_target_pairs={{0,4},{4,0},{8,12},{12,8},{1,5},{5,1},{9,13},{13,9},{2,6},{6,2},{1... | collective-permute-start | bytes 147464 | tf_op jit(solution)/shard_map/ppermute | solution.py:337
  43.8 0.1 collective-permute-done.19.refs_2_
  43.9 0.0 collective-permute-done.20.refs_3_
  43.9 0.3 shard_map.120
  44.2 0.2 collective-permute-start.21
  44.4 2.6 %collective-permute-start.22 = (bf16[16,1536]{1,0:T(8,128)(2,1)S(1)}, bf16[16,1536]{1,0:T(8,128)(2,1)S(1)}, u32[]{:S(2)}, u32[]{:S(2)}) collective-permute-start(bf16[16,1536]{1,0:T(8,128)(2,1)S(1)} %get-tuple-element.83), channel_id=1, source_target_pairs={{0,12},{4,8},{8,4},{12,0},{1,13},{5,9},{9,5},{13,1},{2,14},{6,10},... | collective-permute-start | bytes 147464 | tf_op jit(solution)/shard_map/ppermute | solution.py:337
  47.0 0.0 collective-permute-done.15.refs_1_
  47.0 0.8 %collective-permute-start.23 = (bf16[16,1536]{1,0:T(8,128)(2,1)S(1)}, bf16[16,1536]{1,0:T(8,128)(2,1)S(1)}, u32[]{:S(2)}, u32[]{:S(2)}) collective-permute-start(bf16[16,1536]{1,0:T(8,128)(2,1)S(1)} %get-tuple-element.84), channel_id=1, source_target_pairs={{0,8},{4,12},{8,0},{12,4},{1,9},{5,13},{9,1},{13,5},{2,10},{6,14},... | collective-permute-start | bytes 147464 | tf_op jit(solution)/shard_map/ppermute | solution.py:337
  47.8 0.0 collective-permute-done.16.refs_2_
  47.8 0.6 %collective-permute-done.21.refs_2_ = bf16[16,1536]{1,0:T(8,128)(2,1)S(1)} collective-permute-done((bf16[16,1536]{1,0:T(8,128)(2,1)S(1)}, bf16[16,1536]{1,0:T(8,128)(2,1)S(1)}, u32[]{:S(2)}, u32[]{:S(2)}) %collective-permute-start.21) | collective-permute-done | bytes 49184 | tf_op jit(solution)/shard_map/ppermute | solution.py:337
  48.4 2.2 %collective-permute-done.22.refs_3_ = bf16[16,1536]{1,0:T(8,128)(2,1)S(1)} collective-permute-done((bf16[16,1536]{1,0:T(8,128)(2,1)S(1)}, bf16[16,1536]{1,0:T(8,128)(2,1)S(1)}, u32[]{:S(2)}, u32[]{:S(2)}) %collective-permute-start.22) | collective-permute-done | bytes 49184 | tf_op jit(solution)/shard_map/ppermute | solution.py:337
  50.6 1.4 %collective-permute-done.23.refs_4_ = bf16[16,1536]{1,0:T(8,128)(2,1)S(1)} collective-permute-done((bf16[16,1536]{1,0:T(8,128)(2,1)S(1)}, bf16[16,1536]{1,0:T(8,128)(2,1)S(1)}, u32[]{:S(2)}, u32[]{:S(2)}) %collective-permute-start.23) | collective-permute-done | bytes 49184 | tf_op jit(solution)/shard_map/ppermute | solution.py:337
  52.0 0.7 %shard_map.121 = bf16[16,3072]{1,0:T(8,128)(2,1)} custom-call(bf16[16,1536]{1,0:T(8,128)(2,1)S(1)} %shard_map.117.refs_0_, f32[16,1536]{1,0:T(8,128)S(1)} %get-tuple-element.81.refs_1_, bf16[16,1536]{1,0:T(8,128)(2,1)S(1)} %collective-permute-done.21.refs_2_, bf16[16,1536]{1,0:T(8,128)(2,1)S(1)} %collective-permute-done.22.refs_3_, ...), custom_call_target="tpu_custom_call" | custom-call | tf_op jit(solution)/shard_map/pallas_call | solution.py:466
  (13 shorter events, 0.0 us)
Async XLA Ops:
  4.0 19.5 %slice-start = ((s8[12582912]{0:T(1024)(128)(4,1)}), s8[4194304]{0:T(1024)(128)(4,1)S(1)}, s32[]{:S(2)}) async-start(s8[12582912]{0:T(1024)(128)(4,1)} %bitcast.8), calls=%async_computation | async-start | bytes 8388608
  4.0 19.4 %slice-start.3 = ((s8[12582912]{0:T(1024)(128)(4,1)}), s8[4194304]{0:T(1024)(128)(4,1)S(1)}, s32[]{:S(2)}) async-start(s8[12582912]{0:T(1024)(128)(4,1)} %bitcast.12), calls=%async_computation.3 | async-start | bytes 8388608
  4.0 19.4 %slice-start.1 = ((s8[12582912]{0:T(1024)(128)(4,1)}), s8[4194304]{0:T(1024)(128)(4,1)S(1)}, s32[]{:S(2)}) async-start(s8[12582912]{0:T(1024)(128)(4,1)} %bitcast.8), calls=%async_computation.1 | async-start | bytes 8388608
  4.1 19.4 %slice-start.2 = ((s8[12582912]{0:T(1024)(128)(4,1)}), s8[4194304]{0:T(1024)(128)(4,1)S(1)}, s32[]{:S(2)}) async-start(s8[12582912]{0:T(1024)(128)(4,1)} %bitcast.8), calls=%async_computation.2 | async-start | bytes 8388608
  4.1 19.4 %slice-start.4 = ((s8[12582912]{0:T(1024)(128)(4,1)}), s8[4194304]{0:T(1024)(128)(4,1)S(1)}, s32[]{:S(2)}) async-start(s8[12582912]{0:T(1024)(128)(4,1)} %bitcast.12), calls=%async_computation.4 | async-start | bytes 8388608
  4.1 19.4 %slice-start.5 = ((s8[12582912]{0:T(1024)(128)(4,1)}), s8[4194304]{0:T(1024)(128)(4,1)S(1)}, s32[]{:S(2)}) async-start(s8[12582912]{0:T(1024)(128)(4,1)} %bitcast.12), calls=%async_computation.5 | async-start | bytes 8388608
  4.1 16.7 %copy-start = (bf16[3072,4]{0,1:T(4,128)(2,1)S(1)}, bf16[3072,4]{0,1:T(4,128)(2,1)}, u32[]{:S(2)}) copy-start(bf16[3072,4]{0,1:T(4,128)(2,1)} %param.18) | copy-start | bytes 73732
  4.1 9.5 %collective-permute-start.2 = (bf16[16,1664]{1,0:T(8,128)(2,1)S(1)}, bf16[16,1664]{1,0:T(8,128)(2,1)S(1)}, u32[]{:S(2)}, u32[]{:S(2)}) collective-permute-start(bf16[16,1664]{1,0:T(8,128)(2,1)S(1)} %get-tuple-element.47.refs_0_), channel_id=1, source_target_pairs={{0,12},{4,8},{8,4},{12,0},{1,13},{5,9},{9,5},{13,1},{2,14},{6,10},... | collective-permute-start | bytes 159752 | tf_op jit(solution)/shard_map/ppermute | solution.py:337
  9.2 6.4 %collective-permute-start.1 = (bf16[16,1664]{1,0:T(8,128)(2,1)S(1)}, bf16[16,1664]{1,0:T(8,128)(2,1)S(1)}, u32[]{:S(2)}, u32[]{:S(2)}) collective-permute-start(bf16[16,1664]{1,0:T(8,128)(2,1)S(1)} %get-tuple-element.47.refs_0_), channel_id=1, source_target_pairs={{0,8},{4,12},{8,0},{12,4},{1,9},{5,13},{9,1},{13,5},{2,10},{6,14},... | collective-permute-start | bytes 159752 | tf_op jit(solution)/shard_map/ppermute | solution.py:337
  9.2 6.4 %collective-permute-start = (bf16[16,1664]{1,0:T(8,128)(2,1)S(1)}, bf16[16,1664]{1,0:T(8,128)(2,1)S(1)}, u32[]{:S(2)}, u32[]{:S(2)}) collective-permute-start(bf16[16,1664]{1,0:T(8,128)(2,1)S(1)} %get-tuple-element.47.refs_0_), channel_id=1, source_target_pairs={{0,4},{4,0},{8,12},{12,8},{1,5},{5,1},{9,13},{13,9},{2,6},{6,2},{1... | collective-permute-start | bytes 159752 | tf_op jit(solution)/shard_map/ppermute | solution.py:337
  9.9 7.9 %collective-permute-start.5 = (bf16[16,1536]{1,0:T(8,128)(2,1)S(1)}, bf16[16,1536]{1,0:T(8,128)(2,1)S(1)}, u32[]{:S(2)}, u32[]{:S(2)}) collective-permute-start(bf16[16,1536]{1,0:T(8,128)(2,1)S(1)} %get-tuple-element.48.refs_4_), channel_id=1, source_target_pairs={{0,12},{4,8},{8,4},{12,0},{1,13},{5,9},{9,5},{13,1},{2,14},{6,10},... | collective-permute-start | bytes 147464 | tf_op jit(solution)/shard_map/ppermute | solution.py:337
  13.6 5.0 %collective-permute-start.4 = (bf16[16,1536]{1,0:T(8,128)(2,1)S(1)}, bf16[16,1536]{1,0:T(8,128)(2,1)S(1)}, u32[]{:S(2)}, u32[]{:S(2)}) collective-permute-start(bf16[16,1536]{1,0:T(8,128)(2,1)S(1)} %get-tuple-element.48.refs_4_), channel_id=1, source_target_pairs={{0,8},{4,12},{8,0},{12,4},{1,9},{5,13},{9,1},{13,5},{2,10},{6,14},... | collective-permute-start | bytes 147464 | tf_op jit(solution)/shard_map/ppermute | solution.py:337
  13.6 5.0 %collective-permute-start.3 = (bf16[16,1536]{1,0:T(8,128)(2,1)S(1)}, bf16[16,1536]{1,0:T(8,128)(2,1)S(1)}, u32[]{:S(2)}, u32[]{:S(2)}) collective-permute-start(bf16[16,1536]{1,0:T(8,128)(2,1)S(1)} %get-tuple-element.48.refs_4_), channel_id=1, source_target_pairs={{0,4},{4,0},{8,12},{12,8},{1,5},{5,1},{9,13},{13,9},{2,6},{6,2},{1... | collective-permute-start | bytes 147464 | tf_op jit(solution)/shard_map/ppermute | solution.py:337
  16.2 5.1 %collective-permute-start.9 = (bf16[32,1536]{1,0:T(8,128)(2,1)S(1)}, bf16[32,1536]{1,0:T(8,128)(2,1)S(1)}, u32[]{:S(2)}, u32[]{:S(2)}) collective-permute-start(bf16[32,1536]{1,0:T(8,128)(2,1)S(1)} %get-tuple-element.56), channel_id=1, source_target_pairs={{0,3},{1,2},{2,1},{3,0},{4,7},{5,6},{6,5},{7,4},{8,11},{9,10},{10,... | collective-permute-start | bytes 294920 | tf_op jit(solution)/shard_map/ppermute | solution.py:337
  16.2 7.2 %collective-permute-start.10 = (bf16[32,1536]{1,0:T(8,128)(2,1)S(1)}, bf16[32,1536]{1,0:T(8,128)(2,1)S(1)}, u32[]{:S(2)}, u32[]{:S(2)}) collective-permute-start(bf16[32,1536]{1,0:T(8,128)(2,1)S(1)} %get-tuple-element.57), channel_id=1, source_target_pairs={{0,2},{1,3},{2,0},{3,1},{4,6},{5,7},{6,4},{7,5},{8,10},{9,11},{10,... | collective-permute-start | bytes 294920 | tf_op jit(solution)/shard_map/ppermute | solution.py:337
  17.8 5.7 %collective-permute-start.11 = (bf16[32,1536]{1,0:T(8,128)(2,1)S(1)}, bf16[32,1536]{1,0:T(8,128)(2,1)S(1)}, u32[]{:S(2)}, u32[]{:S(2)}) collective-permute-start(bf16[32,1536]{1,0:T(8,128)(2,1)S(1)} %get-tuple-element.58), channel_id=1, source_target_pairs={{0,1},{1,0},{2,3},{3,2},{4,5},{5,4},{6,7},{7,6},{8,9},{9,8},{10,11... | collective-permute-start | bytes 294920 | tf_op jit(solution)/shard_map/ppermute | solution.py:337
  19.1 7.4 %collective-permute-start.6 = (bf16[32,1536]{1,0:T(8,128)(2,1)S(1)}, bf16[32,1536]{1,0:T(8,128)(2,1)S(1)}, u32[]{:S(2)}, u32[]{:S(2)}) collective-permute-start(bf16[32,1536]{1,0:T(8,128)(2,1)S(1)} %get-tuple-element.52), channel_id=1, source_target_pairs={{0,3},{1,2},{2,1},{3,0},{4,7},{5,6},{6,5},{7,4},{8,11},{9,10},{10,... | collective-permute-start | bytes 294920 | tf_op jit(solution)/shard_map/ppermute | solution.py:337
  19.8 7.9 %collective-permute-start.7 = (bf16[32,1536]{1,0:T(8,128)(2,1)S(1)}, bf16[32,1536]{1,0:T(8,128)(2,1)S(1)}, u32[]{:S(2)}, u32[]{:S(2)}) collective-permute-start(bf16[32,1536]{1,0:T(8,128)(2,1)S(1)} %get-tuple-element.53), channel_id=1, source_target_pairs={{0,2},{1,3},{2,0},{3,1},{4,6},{5,7},{6,4},{7,5},{8,10},{9,11},{10,... | collective-permute-start | bytes 294920 | tf_op jit(solution)/shard_map/ppermute | solution.py:337
  21.3 6.4 %collective-permute-start.8 = (bf16[32,1536]{1,0:T(8,128)(2,1)S(1)}, bf16[32,1536]{1,0:T(8,128)(2,1)S(1)}, u32[]{:S(2)}, u32[]{:S(2)}) collective-permute-start(bf16[32,1536]{1,0:T(8,128)(2,1)S(1)} %get-tuple-element.54), channel_id=1, source_target_pairs={{0,1},{1,0},{2,3},{3,2},{4,5},{5,4},{6,7},{7,6},{8,9},{9,8},{10,11... | collective-permute-start | bytes 294920 | tf_op jit(solution)/shard_map/ppermute | solution.py:337
  31.8 4.9 %collective-permute-start.12 = (bf16[32,1536]{1,0:T(8,128)(2,1)S(1)}, bf16[32,1536]{1,0:T(8,128)(2,1)S(1)}, u32[]{:S(2)}, u32[]{:S(2)}) collective-permute-start(bf16[32,1536]{1,0:T(8,128)(2,1)S(1)} %get-tuple-element.63), channel_id=1, source_target_pairs={{0,3},{1,2},{2,1},{3,0},{4,7},{5,6},{6,5},{7,4},{8,11},{9,10},{10,... | collective-permute-start | bytes 294920 | tf_op jit(solution)/shard_map/ppermute | solution.py:337
  31.9 7.2 %collective-permute-start.13 = (bf16[32,1536]{1,0:T(8,128)(2,1)S(1)}, bf16[32,1536]{1,0:T(8,128)(2,1)S(1)}, u32[]{:S(2)}, u32[]{:S(2)}) collective-permute-start(bf16[32,1536]{1,0:T(8,128)(2,1)S(1)} %get-tuple-element.64), channel_id=1, source_target_pairs={{0,2},{1,3},{2,0},{3,1},{4,6},{5,7},{6,4},{7,5},{8,10},{9,11},{10,... | collective-permute-start | bytes 294920 | tf_op jit(solution)/shard_map/ppermute | solution.py:337
  33.6 5.5 %collective-permute-start.14 = (bf16[32,1536]{1,0:T(8,128)(2,1)S(1)}, bf16[32,1536]{1,0:T(8,128)(2,1)S(1)}, u32[]{:S(2)}, u32[]{:S(2)}) collective-permute-start(bf16[32,1536]{1,0:T(8,128)(2,1)S(1)} %get-tuple-element.65), channel_id=1, source_target_pairs={{0,1},{1,0},{2,3},{3,2},{4,5},{5,4},{6,7},{7,6},{8,9},{9,8},{10,11... | collective-permute-start | bytes 294920 | tf_op jit(solution)/shard_map/ppermute | solution.py:337
  36.7 5.4 %collective-permute-start.18 = (bf16[32,1536]{1,0:T(8,128)(2,1)S(1)}, bf16[32,1536]{1,0:T(8,128)(2,1)S(1)}, u32[]{:S(2)}, u32[]{:S(2)}) collective-permute-start(bf16[32,1536]{1,0:T(8,128)(2,1)S(1)} %get-tuple-element.78), channel_id=1, source_target_pairs={{0,3},{1,2},{2,1},{3,0},{4,7},{5,6},{6,5},{7,4},{8,11},{9,10},{10,... | collective-permute-start | bytes 294920 | tf_op jit(solution)/shard_map/ppermute | solution.py:337
  36.7 7.2 %collective-permute-start.19 = (bf16[32,1536]{1,0:T(8,128)(2,1)S(1)}, bf16[32,1536]{1,0:T(8,128)(2,1)S(1)}, u32[]{:S(2)}, u32[]{:S(2)}) collective-permute-start(bf16[32,1536]{1,0:T(8,128)(2,1)S(1)} %get-tuple-element.79), channel_id=1, source_target_pairs={{0,2},{1,3},{2,0},{3,1},{4,6},{5,7},{6,4},{7,5},{8,10},{9,11},{10,... | collective-permute-start | bytes 294920 | tf_op jit(solution)/shard_map/ppermute | solution.py:337
  38.7 5.2 %collective-permute-start.20 = (bf16[32,1536]{1,0:T(8,128)(2,1)S(1)}, bf16[32,1536]{1,0:T(8,128)(2,1)S(1)}, u32[]{:S(2)}, u32[]{:S(2)}) collective-permute-start(bf16[32,1536]{1,0:T(8,128)(2,1)S(1)} %get-tuple-element.80), channel_id=1, source_target_pairs={{0,1},{1,0},{2,3},{3,2},{4,5},{5,4},{6,7},{7,6},{8,9},{9,8},{10,11... | collective-permute-start | bytes 294920 | tf_op jit(solution)/shard_map/ppermute | solution.py:337
  39.4 7.6 %collective-permute-start.15 = (bf16[16,1536]{1,0:T(8,128)(2,1)S(1)}, bf16[16,1536]{1,0:T(8,128)(2,1)S(1)}, u32[]{:S(2)}, u32[]{:S(2)}) collective-permute-start(bf16[16,1536]{1,0:T(8,128)(2,1)S(1)} %get-tuple-element.68), channel_id=1, source_target_pairs={{0,12},{4,8},{8,4},{12,0},{1,13},{5,9},{9,5},{13,1},{2,14},{6,10},... | collective-permute-start | bytes 147464 | tf_op jit(solution)/shard_map/ppermute | solution.py:337
  42.1 5.7 %collective-permute-start.16 = (bf16[16,1536]{1,0:T(8,128)(2,1)S(1)}, bf16[16,1536]{1,0:T(8,128)(2,1)S(1)}, u32[]{:S(2)}, u32[]{:S(2)}) collective-permute-start(bf16[16,1536]{1,0:T(8,128)(2,1)S(1)} %get-tuple-element.69), channel_id=1, source_target_pairs={{0,8},{4,12},{8,0},{12,4},{1,9},{5,13},{9,1},{13,5},{2,10},{6,14},... | collective-permute-start | bytes 147464 | tf_op jit(solution)/shard_map/ppermute | solution.py:337
  42.1 5.7 %collective-permute-start.17 = (bf16[16,1536]{1,0:T(8,128)(2,1)S(1)}, bf16[16,1536]{1,0:T(8,128)(2,1)S(1)}, u32[]{:S(2)}, u32[]{:S(2)}) collective-permute-start(bf16[16,1536]{1,0:T(8,128)(2,1)S(1)} %get-tuple-element.70), channel_id=1, source_target_pairs={{0,4},{4,0},{8,12},{12,8},{1,5},{5,1},{9,13},{13,9},{2,6},{6,2},{1... | collective-permute-start | bytes 147464 | tf_op jit(solution)/shard_map/ppermute | solution.py:337
  44.2 4.2 %collective-permute-start.21 = (bf16[16,1536]{1,0:T(8,128)(2,1)S(1)}, bf16[16,1536]{1,0:T(8,128)(2,1)S(1)}, u32[]{:S(2)}, u32[]{:S(2)}) collective-permute-start(bf16[16,1536]{1,0:T(8,128)(2,1)S(1)} %get-tuple-element.82), channel_id=1, source_target_pairs={{0,4},{4,0},{8,12},{12,8},{1,5},{5,1},{9,13},{13,9},{2,6},{6,2},{1... | collective-permute-start | bytes 147464 | tf_op jit(solution)/shard_map/ppermute | solution.py:337
  44.4 6.2 %collective-permute-start.22 = (bf16[16,1536]{1,0:T(8,128)(2,1)S(1)}, bf16[16,1536]{1,0:T(8,128)(2,1)S(1)}, u32[]{:S(2)}, u32[]{:S(2)}) collective-permute-start(bf16[16,1536]{1,0:T(8,128)(2,1)S(1)} %get-tuple-element.83), channel_id=1, source_target_pairs={{0,12},{4,8},{8,4},{12,0},{1,13},{5,9},{9,5},{13,1},{2,14},{6,10},... | collective-permute-start | bytes 147464 | tf_op jit(solution)/shard_map/ppermute | solution.py:337
  47.0 5.0 %collective-permute-start.23 = (bf16[16,1536]{1,0:T(8,128)(2,1)S(1)}, bf16[16,1536]{1,0:T(8,128)(2,1)S(1)}, u32[]{:S(2)}, u32[]{:S(2)}) collective-permute-start(bf16[16,1536]{1,0:T(8,128)(2,1)S(1)} %get-tuple-element.84), channel_id=1, source_target_pairs={{0,8},{4,12},{8,0},{12,4},{1,9},{5,13},{9,1},{13,5},{2,10},{6,14},... | collective-permute-start | bytes 147464 | tf_op jit(solution)/shard_map/ppermute | solution.py:337

commit v15 on v14

--- a/solution.py
+++ b/solution.py
@@ -135,8 +135,8 @@
         length = jnp.where(request[0:1] == r, lengths_ref[0:1, r : r + 1], length)
     visible = iota((window, full), 0) < length
     _, owner = split(iota((lanes, padded), 0), batch)
-    attended = []
-    for i, part in enumerate(parts):
+    spreads = []
+    for i in range(len(parts)):
         spread = []
         for k in range(PAIR):
             at = [(i * PAIR + k) * span + g * HS for g in range(GROUP)]
@@ -147,9 +147,10 @@
             )
         if full > lanes:
             spread.append(jnp.zeros((full - lanes, PAIR * HS), BF16))
-        spread = jnp.concatenate(spread, axis=0)
-        if i == 0:
-            wait(1)
+        spreads.append(jnp.concatenate(spread, axis=0))
+    wait(1)
+    weighted = []
+    for spread, part in zip(spreads, parts):
         keys = keys_ref[:, :, part].reshape(batch * window, PAIR * HS)
         products = dot(keys, spread, ((1,), (1,)))
         scores = products[:window]
@@ -161,11 +162,14 @@
         if padded > window:
             weights = jnp.concatenate([weights, jnp.zeros((padded - window, full), F32)], axis=0)
         weights = weights.T[:lanes]
-        weights = jnp.concatenate(
-            [jnp.where(owner == r, weights, 0.0).astype(BF16) for r in range(batch)], axis=1
+        weighted.append(
+            jnp.concatenate(
+                [jnp.where(owner == r, weights, 0.0).astype(BF16) for r in range(batch)], axis=1
+            )
         )
-        if i == 0:
-            wait(2)
+    wait(2)
+    attended = []
+    for weights, part in zip(weighted, parts):
         values = values_ref[:, :, part].reshape(batch * padded, PAIR * HS)
         mixed = dot(weights, values)
         attended += [
@@ -190,17 +194,16 @@
     pass
 
 
-def pass_on(values, cost, after):
-    first = len(after)
+def pass_on(values, cost):
     return pl.pallas_call(
         pass_kernel,
-        in_specs=[ANY] * (first + len(values)),
+        in_specs=[ANY] * len(values),
         out_specs=[ANY] * len(values),
         out_shape=[jax.ShapeDtypeStruct(value.shape, value.dtype) for value in values],
-        input_output_aliases={first + i: i for i in range(len(values))},
+        input_output_aliases={i: i for i in range(len(values))},
         cost_estimate=cost,
         compiler_params=params(0),
-    )(*after, *values)
+    )(*values)
 
 
 def stack(refs):
@@ -386,7 +389,7 @@
         cost_estimate=LIGHT,
     )(me, *operands)
 
-    payload = pass_on(payload, BUSY, [])
+    payload = pass_on(payload, BUSY)
 
     order = farthest_first(experts)
     chunks, arrived = [], []
@@ -449,8 +452,6 @@
 
     done = []
     for part, blocks in enumerate((first, second)):
-        if part:
-            blocks = pass_on(blocks, LIGHT, returned[1:2])
         returned = [swap(block, "expert", e) for e, block in zip(order, blocks)]
         mixed = pl.pallas_call(
             functools.partial(mix_kernel, layers=layers, part=part),
@@ -460,8 +461,7 @@
             cost_estimate=LIGHT,
             compiler_params=params(experts * layers * CAP * half),
         )(*gates, *returned, stream)
-        distances = [0, 1, *range(layers - 1, 1, -1)] if part else farthest_first(layers)
-        sums = [swap(mixed[j], "attn", j) for j in distances]
+        sums = [swap(mixed[j], "attn", j) for j in farthest_first(layers)]
         done = [
             pl.pallas_call(
                 add_kernel,

time: 52.8 us -> 51.9 us (0.983)
  Pallas kernels: 15 us -> 14 us
  starting transfers between devices: 25.8 us -> 26.8 us
  waiting for transfers between devices: 11.5 us -> 10.7 us
    pallas_call x1, Pallas kernels: 4.01 us -> 3.01 us  [shards(): pl.pallas_call(attend_kernel, in_specs=[SCALAR] + [ANY] * len(operands),...]
    ppermute x24, starting transfers between devices: 25.8 us -> 26.8 us  [swap(): return lax.ppermute(value, axis, [(i, i ^ step) for i in range(count)])]
    ppermute x24, waiting for transfers between devices: 11.5 us -> 10.7 us  [swap(): return lax.ppermute(value, axis, [(i, i ^ step) for i in range(count)])]
  transfers between devices with their start and end apart: 24 -> 24, of which waited for: 11 -> 8; matrix products, arithmetic and copies ran while one was open for 0% -> 0% of each run, Pallas kernels for 12% -> 12%
where the time goes in v15:
time: 51.9 us; the launch traced here: 51.7 us
  starting transfers between devices  26.8 us (52%)
  Pallas kernels  14 us (27%)
  waiting for transfers between devices  10.7 us (21%)
    ppermute x24, starting transfers between devices, swap(): return lax.ppermute(value, axis, [(i, i ^ step) for i in range(count)])  26.8 us
    ppermute x24, waiting for transfers between devices, swap(): return lax.ppermute(value, axis, [(i, i ^ step) for i in range(count)])  10.7 us
    pallas_call x1, Pallas kernels, shards(): pl.pallas_call(functools.partial(middle_kernel, experts=experts), in_spec...  4.18 us
    pallas_call x1, Pallas kernels, shards(): pl.pallas_call(attend_kernel, in_specs=[SCALAR] + [ANY] * len(operands),...  3.01 us
    pallas_call x1, Pallas kernels, shards(): pl.pallas_call(functools.partial(begin_kernel, experts=experts), in_specs...  2.92 us
    pallas_call x1, Pallas kernels, shards(): pl.pallas_call(end_kernel, in_specs=[WHOLE] * 2, out_specs=[WHOLE] * expe...  1.37 us
  transfers between devices with their start and end apart: 24, of which 8 were waited for; matrix products, arithmetic and copies ran while one was open for 0% of the time, Pallas kernels for 12%

profile of v15, /device:TPU:0, one launch (start us, length us, event | category | flops | bytes accessed | tf_op | source)
XLA Modules:
  0.0 51.7 jit_solution(3779457651523191700)
XLA Ops:
  0.0 3.0 %shard_map.109 = (f32[16,3072]{1,0:T(8,128)S(1)}, bf16[16,1664]{1,0:T(8,128)(2,1)S(1)}, bf16[16,1536]{1,0:T(8,128)(2,1)S(1)}) custom-call(s32[1]{0:T(128)} %bitcast._.me_ref, s32[1,16]{1,0:T(1,128)} %bitcast.21, bf16[16,3072]{1,0:T(8,128)(2,1)} %queries_hbm.1, bf16[16,96,512]{2,1,0:T(8,128)(2,1)} %keys_hbm.1, bf16[16,96,512]{2,1,0:T(8,128)(2,1)} %values_hbm.1, ...), custom_call_target="tpu_custom_call" | custom-call | tf_op jit(solution)/shard_map/pallas_call | solution.py:380
  3.0 0.0 slice-start
  3.0 0.0 slice-start.3
  3.0 0.0 slice-start.1
  3.1 0.0 slice-start.2
  3.1 0.0 slice-start.4
  3.1 0.0 slice-start.5
  3.1 0.0 copy-start
  3.1 5.1 %collective-permute-start.2 = (bf16[16,1664]{1,0:T(8,128)(2,1)S(1)}, bf16[16,1664]{1,0:T(8,128)(2,1)S(1)}, u32[]{:S(2)}, u32[]{:S(2)}) collective-permute-start(bf16[16,1664]{1,0:T(8,128)(2,1)S(1)} %get-tuple-element.43.refs_0_), channel_id=1, source_target_pairs={{0,12},{4,8},{8,4},{12,0},{1,13},{5,9},{9,5},{13,1},{2,14},{6,10},... | collective-permute-start | bytes 159752 | tf_op jit(solution)/shard_map/ppermute | solution.py:340
  8.2 0.0 collective-permute-start.1
  8.2 0.6 %collective-permute-start = (bf16[16,1664]{1,0:T(8,128)(2,1)S(1)}, bf16[16,1664]{1,0:T(8,128)(2,1)S(1)}, u32[]{:S(2)}, u32[]{:S(2)}) collective-permute-start(bf16[16,1664]{1,0:T(8,128)(2,1)S(1)} %get-tuple-element.43.refs_0_), channel_id=1, source_target_pairs={{0,4},{4,0},{8,12},{12,8},{1,5},{5,1},{9,13},{13,9},{2,6},{6,2},{1... | collective-permute-start | bytes 159752 | tf_op jit(solution)/shard_map/ppermute | solution.py:340
  8.9 3.7 %collective-permute-start.5 = (bf16[16,1536]{1,0:T(8,128)(2,1)S(1)}, bf16[16,1536]{1,0:T(8,128)(2,1)S(1)}, u32[]{:S(2)}, u32[]{:S(2)}) collective-permute-start(bf16[16,1536]{1,0:T(8,128)(2,1)S(1)} %get-tuple-element.44.refs_4_), channel_id=1, source_target_pairs={{0,12},{4,8},{8,4},{12,0},{1,13},{5,9},{9,5},{13,1},{2,14},{6,10},... | collective-permute-start | bytes 147464 | tf_op jit(solution)/shard_map/ppermute | solution.py:340
  12.6 0.0 collective-permute-start.4
  12.6 0.0 collective-permute-done.2.refs_3_
  12.6 0.6 %collective-permute-start.3 = (bf16[16,1536]{1,0:T(8,128)(2,1)S(1)}, bf16[16,1536]{1,0:T(8,128)(2,1)S(1)}, u32[]{:S(2)}, u32[]{:S(2)}) collective-permute-start(bf16[16,1536]{1,0:T(8,128)(2,1)S(1)} %get-tuple-element.44.refs_4_), channel_id=1, source_target_pairs={{0,4},{4,0},{8,12},{12,8},{1,5},{5,1},{9,13},{13,9},{2,6},{6,2},{1... | collective-permute-start | bytes 147464 | tf_op jit(solution)/shard_map/ppermute | solution.py:340
  13.3 1.4 %collective-permute-done.1.refs_2_ = bf16[16,1664]{1,0:T(8,128)(2,1)S(1)} collective-permute-done((bf16[16,1664]{1,0:T(8,128)(2,1)S(1)}, bf16[16,1664]{1,0:T(8,128)(2,1)S(1)}, u32[]{:S(2)}, u32[]{:S(2)}) %collective-permute-start.1) | collective-permute-done | bytes 53280 | tf_op jit(solution)/shard_map/ppermute | solution.py:340
  14.7 0.0 collective-permute-done.refs_1_
  14.7 0.5 shard_map.113
  15.2 0.1 collective-permute-start.9
  15.2 1.5 %collective-permute-start.10 = (bf16[32,1536]{1,0:T(8,128)(2,1)S(1)}, bf16[32,1536]{1,0:T(8,128)(2,1)S(1)}, u32[]{:S(2)}, u32[]{:S(2)}) collective-permute-start(bf16[32,1536]{1,0:T(8,128)(2,1)S(1)} %get-tuple-element.53), channel_id=1, source_target_pairs={{0,2},{1,3},{2,0},{3,1},{4,6},{5,7},{6,4},{7,5},{8,10},{9,11},{10,... | collective-permute-start | bytes 294920 | tf_op jit(solution)/shard_map/ppermute | solution.py:340
  16.8 0.0 collective-permute-done.5.refs_7_
  16.8 0.3 collective-permute-start.11
  17.1 0.5 collective-permute-done.4.refs_6_
  17.6 0.0 collective-permute-done.3.refs_5_
  17.6 0.5 shard_map.112
  18.1 0.7 %collective-permute-start.6 = (bf16[32,1536]{1,0:T(8,128)(2,1)S(1)}, bf16[32,1536]{1,0:T(8,128)(2,1)S(1)}, u32[]{:S(2)}, u32[]{:S(2)}) collective-permute-start(bf16[32,1536]{1,0:T(8,128)(2,1)S(1)} %get-tuple-element.48), channel_id=1, source_target_pairs={{0,3},{1,2},{2,1},{3,0},{4,7},{5,6},{6,5},{7,4},{8,11},{9,10},{10,... | collective-permute-start | bytes 294920 | tf_op jit(solution)/shard_map/ppermute | solution.py:340
  18.8 1.0 %collective-permute-start.7 = (bf16[32,1536]{1,0:T(8,128)(2,1)S(1)}, bf16[32,1536]{1,0:T(8,128)(2,1)S(1)}, u32[]{:S(2)}, u32[]{:S(2)}) collective-permute-start(bf16[32,1536]{1,0:T(8,128)(2,1)S(1)} %get-tuple-element.49), channel_id=1, source_target_pairs={{0,2},{1,3},{2,0},{3,1},{4,6},{5,7},{6,4},{7,5},{8,10},{9,11},{10,... | collective-permute-start | bytes 294920 | tf_op jit(solution)/shard_map/ppermute | solution.py:340
  19.7 0.3 shard_map.111
  20.1 0.2 collective-permute-done.9.refs_1_
  20.3 0.2 collective-permute-start.8
  20.5 2.0 %collective-permute-done.10.refs_2_ = bf16[32,1536]{1,0:T(8,128)(2,1)S(1)} collective-permute-done((bf16[32,1536]{1,0:T(8,128)(2,1)S(1)}, bf16[32,1536]{1,0:T(8,128)(2,1)S(1)}, u32[]{:S(2)}, u32[]{:S(2)}) %collective-permute-start.10) | collective-permute-done | bytes 98336 | tf_op jit(solution)/shard_map/ppermute | solution.py:340
  22.5 0.0 collective-permute-done.11.refs_3_
  22.5 2.9 %shard_map.114 = (f32[128,2048]{1,0:T(8,128)S(1)}, f32[128,2048]{1,0:T(8,128)S(1)}, bf16[2048,1536]{1,0:T(8,128)(2,1)S(1)}) custom-call(bf16[32,1536]{1,0:T(8,128)(2,1)S(1)} %get-tuple-element.51.refs_0_, bf16[32,1536]{1,0:T(8,128)(2,1)S(1)} %collective-permute-done.9.refs_1_, bf16[32,1536]{1,0:T(8,128)(2,1)S(1)} %collective-permute-done.10.refs_2_, ...), custom_call_target="tpu_custom_call" | custom-call | flops 1610612736 | tf_op jit(solution)/shard_map/pallas_call | solution.py:423
  25.5 0.0 collective-permute-done.6.refs_1_
  25.5 1.2 %collective-permute-done.7.refs_2_ = bf16[32,1536]{1,0:T(8,128)(2,1)S(1)} collective-permute-done((bf16[32,1536]{1,0:T(8,128)(2,1)S(1)}, bf16[32,1536]{1,0:T(8,128)(2,1)S(1)}, u32[]{:S(2)}, u32[]{:S(2)}) %collective-permute-start.7) | collective-permute-done | bytes 98336 | tf_op jit(solution)/shard_map/ppermute | solution.py:340
  26.6 0.0 collective-permute-done.8.refs_3_
  26.7 4.2 %shard_map.115 = (bf16[32,1536]{1,0:T(8,128)(2,1)S(1)}, bf16[32,1536]{1,0:T(8,128)(2,1)S(1)}, bf16[32,1536]{1,0:T(8,128)(2,1)S(1)}, bf16[32,1536]{1,0:T(8,128)(2...) custom-call(bf16[32,1536]{1,0:T(8,128)(2,1)S(1)} %get-tuple-element.47.refs_0_, ...), custom_call_target="tpu_custom_call" | custom-call | tf_op jit(solution)/shard_map/pallas_call | solution.py:434
  30.8 0.1 collective-permute-start.12
  30.9 1.7 %collective-permute-start.13 = (bf16[32,1536]{1,0:T(8,128)(2,1)S(1)}, bf16[32,1536]{1,0:T(8,128)(2,1)S(1)}, u32[]{:S(2)}, u32[]{:S(2)}) collective-permute-start(bf16[32,1536]{1,0:T(8,128)(2,1)S(1)} %get-tuple-element.60), channel_id=1, source_target_pairs={{0,2},{1,3},{2,0},{3,1},{4,6},{5,7},{6,4},{7,5},{8,10},{9,11},{10,... | collective-permute-start | bytes 294920 | tf_op jit(solution)/shard_map/ppermute | solution.py:340
  32.6 0.2 collective-permute-start.14
  32.8 1.4 %shard_map.118 = (bf16[32,1536]{1,0:T(8,128)(2,1)S(1)}, bf16[32,1536]{1,0:T(8,128)(2,1)S(1)}, bf16[32,1536]{1,0:T(8,128)(2,1)S(1)}, bf16[32,1536]{1,0:T(8,128)(2,1)S(1)}) custom-call(bf16[128,2048]{1,0:T(8,128)(2,1)S(1)} %get-tuple-element.67.hidden_ref, bf16[2048,1536]{1,0:T(8,128)(2,1)S(1)} %get-tuple-element.68.down_ref), custom_call_target="tpu_custom_call" | custom-call | flops 805306368 | tf_op jit(solution)/shard_map/pallas_call | solution.py:442
  34.2 0.4 collective-permute-start.18
  34.6 1.6 %collective-permute-start.19 = (bf16[32,1536]{1,0:T(8,128)(2,1)S(1)}, bf16[32,1536]{1,0:T(8,128)(2,1)S(1)}, u32[]{:S(2)}, u32[]{:S(2)}) collective-permute-start(bf16[32,1536]{1,0:T(8,128)(2,1)S(1)} %get-tuple-element.71), channel_id=1, source_target_pairs={{0,2},{1,3},{2,0},{3,1},{4,6},{5,7},{6,4},{7,5},{8,10},{9,11},{10,... | collective-permute-start | bytes 294920 | tf_op jit(solution)/shard_map/ppermute | solution.py:340
  36.2 0.0 collective-permute-done.12.refs_1_
  36.2 0.0 collective-permute-start.20
  36.2 2.1 %collective-permute-done.13.refs_2_ = bf16[32,1536]{1,0:T(8,128)(2,1)S(1)} collective-permute-done((bf16[32,1536]{1,0:T(8,128)(2,1)S(1)}, bf16[32,1536]{1,0:T(8,128)(2,1)S(1)}, u32[]{:S(2)}, u32[]{:S(2)}) %collective-permute-start.13) | collective-permute-done | bytes 98336 | tf_op jit(solution)/shard_map/ppermute | solution.py:340
  38.4 0.0 collective-permute-done.14.refs_3_
  38.4 0.3 shard_map.116
  38.6 2.7 %collective-permute-start.15 = (bf16[16,1536]{1,0:T(8,128)(2,1)S(1)}, bf16[16,1536]{1,0:T(8,128)(2,1)S(1)}, u32[]{:S(2)}, u32[]{:S(2)}) collective-permute-start(bf16[16,1536]{1,0:T(8,128)(2,1)S(1)} %get-tuple-element.64), channel_id=1, source_target_pairs={{0,12},{4,8},{8,4},{12,0},{1,13},{5,9},{9,5},{13,1},{2,14},{6,10},... | collective-permute-start | bytes 147464 | tf_op jit(solution)/shard_map/ppermute | solution.py:340
  41.3 0.0 collective-permute-start.16
  41.4 0.0 collective-permute-done.18.refs_1_
  41.4 1.7 %collective-permute-start.17 = (bf16[16,1536]{1,0:T(8,128)(2,1)S(1)}, bf16[16,1536]{1,0:T(8,128)(2,1)S(1)}, u32[]{:S(2)}, u32[]{:S(2)}) collective-permute-start(bf16[16,1536]{1,0:T(8,128)(2,1)S(1)} %get-tuple-element.66), channel_id=1, source_target_pairs={{0,4},{4,0},{8,12},{12,8},{1,5},{5,1},{9,13},{13,9},{2,6},{6,2},{1... | collective-permute-start | bytes 147464 | tf_op jit(solution)/shard_map/ppermute | solution.py:340
  43.1 0.0 collective-permute-done.19.refs_2_
  43.1 0.0 collective-permute-done.20.refs_3_
  43.1 0.3 shard_map.119
  43.4 2.7 %collective-permute-start.21 = (bf16[16,1536]{1,0:T(8,128)(2,1)S(1)}, bf16[16,1536]{1,0:T(8,128)(2,1)S(1)}, u32[]{:S(2)}, u32[]{:S(2)}) collective-permute-start(bf16[16,1536]{1,0:T(8,128)(2,1)S(1)} %get-tuple-element.74), channel_id=1, source_target_pairs={{0,12},{4,8},{8,4},{12,0},{1,13},{5,9},{9,5},{13,1},{2,14},{6,10},... | collective-permute-start | bytes 147464 | tf_op jit(solution)/shard_map/ppermute | solution.py:340
  46.1 0.0 collective-permute-start.22
  46.1 0.0 collective-permute-done.15.refs_1_
  46.1 1.7 %collective-permute-start.23 = (bf16[16,1536]{1,0:T(8,128)(2,1)S(1)}, bf16[16,1536]{1,0:T(8,128)(2,1)S(1)}, u32[]{:S(2)}, u32[]{:S(2)}) collective-permute-start(bf16[16,1536]{1,0:T(8,128)(2,1)S(1)} %get-tuple-element.76), channel_id=1, source_target_pairs={{0,4},{4,0},{8,12},{12,8},{1,5},{5,1},{9,13},{13,9},{2,6},{6,2},{1... | collective-permute-start | bytes 147464 | tf_op jit(solution)/shard_map/ppermute | solution.py:340
  47.8 0.0 collective-permute-done.16.refs_2_
  47.8 1.5 %collective-permute-done.21.refs_2_ = bf16[16,1536]{1,0:T(8,128)(2,1)S(1)} collective-permute-done((bf16[16,1536]{1,0:T(8,128)(2,1)S(1)}, bf16[16,1536]{1,0:T(8,128)(2,1)S(1)}, u32[]{:S(2)}, u32[]{:S(2)}) %collective-permute-start.21) | collective-permute-done | bytes 49184 | tf_op jit(solution)/shard_map/ppermute | solution.py:340
  49.3 1.7 %collective-permute-done.22.refs_3_ = bf16[16,1536]{1,0:T(8,128)(2,1)S(1)} collective-permute-done((bf16[16,1536]{1,0:T(8,128)(2,1)S(1)}, bf16[16,1536]{1,0:T(8,128)(2,1)S(1)}, u32[]{:S(2)}, u32[]{:S(2)}) %collective-permute-start.22) | collective-permute-done | bytes 49184 | tf_op jit(solution)/shard_map/ppermute | solution.py:340
  51.1 0.0 collective-permute-done.23.refs_4_
  51.1 0.7 %shard_map.120 = bf16[16,3072]{1,0:T(8,128)(2,1)} custom-call(bf16[16,1536]{1,0:T(8,128)(2,1)S(1)} %shard_map.117.refs_0_, f32[16,1536]{1,0:T(8,128)S(1)} %get-tuple-element.73.refs_1_, bf16[16,1536]{1,0:T(8,128)(2,1)S(1)} %collective-permute-done.21.refs_2_, bf16[16,1536]{1,0:T(8,128)(2,1)S(1)} %collective-permute-done.22.refs_3_, ...), custom_call_target="tpu_custom_call" | custom-call | tf_op jit(solution)/shard_map/pallas_call | solution.py:466
  (12 shorter events, 0.0 us)
Async XLA Ops:
  3.0 19.5 %slice-start = ((s8[12582912]{0:T(1024)(128)(4,1)}), s8[4194304]{0:T(1024)(128)(4,1)S(1)}, s32[]{:S(2)}) async-start(s8[12582912]{0:T(1024)(128)(4,1)} %bitcast.8), calls=%async_computation | async-start | bytes 8388608
  3.0 19.4 %slice-start.3 = ((s8[12582912]{0:T(1024)(128)(4,1)}), s8[4194304]{0:T(1024)(128)(4,1)S(1)}, s32[]{:S(2)}) async-start(s8[12582912]{0:T(1024)(128)(4,1)} %bitcast.12), calls=%async_computation.3 | async-start | bytes 8388608
  3.0 19.4 %slice-start.1 = ((s8[12582912]{0:T(1024)(128)(4,1)}), s8[4194304]{0:T(1024)(128)(4,1)S(1)}, s32[]{:S(2)}) async-start(s8[12582912]{0:T(1024)(128)(4,1)} %bitcast.8), calls=%async_computation.1 | async-start | bytes 8388608
  3.1 19.4 %slice-start.2 = ((s8[12582912]{0:T(1024)(128)(4,1)}), s8[4194304]{0:T(1024)(128)(4,1)S(1)}, s32[]{:S(2)}) async-start(s8[12582912]{0:T(1024)(128)(4,1)} %bitcast.8), calls=%async_computation.2 | async-start | bytes 8388608
  3.1 19.4 %slice-start.4 = ((s8[12582912]{0:T(1024)(128)(4,1)}), s8[4194304]{0:T(1024)(128)(4,1)S(1)}, s32[]{:S(2)}) async-start(s8[12582912]{0:T(1024)(128)(4,1)} %bitcast.12), calls=%async_computation.4 | async-start | bytes 8388608
  3.1 19.4 %slice-start.5 = ((s8[12582912]{0:T(1024)(128)(4,1)}), s8[4194304]{0:T(1024)(128)(4,1)S(1)}, s32[]{:S(2)}) async-start(s8[12582912]{0:T(1024)(128)(4,1)} %bitcast.12), calls=%async_computation.5 | async-start | bytes 8388608
  3.1 16.6 %copy-start = (bf16[3072,4]{0,1:T(4,128)(2,1)S(1)}, bf16[3072,4]{0,1:T(4,128)(2,1)}, u32[]{:S(2)}) copy-start(bf16[3072,4]{0,1:T(4,128)(2,1)} %param.18) | copy-start | bytes 73732
  3.1 9.5 %collective-permute-start.2 = (bf16[16,1664]{1,0:T(8,128)(2,1)S(1)}, bf16[16,1664]{1,0:T(8,128)(2,1)S(1)}, u32[]{:S(2)}, u32[]{:S(2)}) collective-permute-start(bf16[16,1664]{1,0:T(8,128)(2,1)S(1)} %get-tuple-element.43.refs_0_), channel_id=1, source_target_pairs={{0,12},{4,8},{8,4},{12,0},{1,13},{5,9},{9,5},{13,1},{2,14},{6,10},... | collective-permute-start | bytes 159752 | tf_op jit(solution)/shard_map/ppermute | solution.py:340
  8.2 6.4 %collective-permute-start.1 = (bf16[16,1664]{1,0:T(8,128)(2,1)S(1)}, bf16[16,1664]{1,0:T(8,128)(2,1)S(1)}, u32[]{:S(2)}, u32[]{:S(2)}) collective-permute-start(bf16[16,1664]{1,0:T(8,128)(2,1)S(1)} %get-tuple-element.43.refs_0_), channel_id=1, source_target_pairs={{0,8},{4,12},{8,0},{12,4},{1,9},{5,13},{9,1},{13,5},{2,10},{6,14},... | collective-permute-start | bytes 159752 | tf_op jit(solution)/shard_map/ppermute | solution.py:340
  8.2 6.4 %collective-permute-start = (bf16[16,1664]{1,0:T(8,128)(2,1)S(1)}, bf16[16,1664]{1,0:T(8,128)(2,1)S(1)}, u32[]{:S(2)}, u32[]{:S(2)}) collective-permute-start(bf16[16,1664]{1,0:T(8,128)(2,1)S(1)} %get-tuple-element.43.refs_0_), channel_id=1, source_target_pairs={{0,4},{4,0},{8,12},{12,8},{1,5},{5,1},{9,13},{13,9},{2,6},{6,2},{1... | collective-permute-start | bytes 159752 | tf_op jit(solution)/shard_map/ppermute | solution.py:340
  8.9 7.9 %collective-permute-start.5 = (bf16[16,1536]{1,0:T(8,128)(2,1)S(1)}, bf16[16,1536]{1,0:T(8,128)(2,1)S(1)}, u32[]{:S(2)}, u32[]{:S(2)}) collective-permute-start(bf16[16,1536]{1,0:T(8,128)(2,1)S(1)} %get-tuple-element.44.refs_4_), channel_id=1, source_target_pairs={{0,12},{4,8},{8,4},{12,0},{1,13},{5,9},{9,5},{13,1},{2,14},{6,10},... | collective-permute-start | bytes 147464 | tf_op jit(solution)/shard_map/ppermute | solution.py:340
  12.6 5.0 %collective-permute-start.4 = (bf16[16,1536]{1,0:T(8,128)(2,1)S(1)}, bf16[16,1536]{1,0:T(8,128)(2,1)S(1)}, u32[]{:S(2)}, u32[]{:S(2)}) collective-permute-start(bf16[16,1536]{1,0:T(8,128)(2,1)S(1)} %get-tuple-element.44.refs_4_), channel_id=1, source_target_pairs={{0,8},{4,12},{8,0},{12,4},{1,9},{5,13},{9,1},{13,5},{2,10},{6,14},... | collective-permute-start | bytes 147464 | tf_op jit(solution)/shard_map/ppermute | solution.py:340
  12.6 5.0 %collective-permute-start.3 = (bf16[16,1536]{1,0:T(8,128)(2,1)S(1)}, bf16[16,1536]{1,0:T(8,128)(2,1)S(1)}, u32[]{:S(2)}, u32[]{:S(2)}) collective-permute-start(bf16[16,1536]{1,0:T(8,128)(2,1)S(1)} %get-tuple-element.44.refs_4_), channel_id=1, source_target_pairs={{0,4},{4,0},{8,12},{12,8},{1,5},{5,1},{9,13},{13,9},{2,6},{6,2},{1... | collective-permute-start | bytes 147464 | tf_op jit(solution)/shard_map/ppermute | solution.py:340
  15.2 5.1 %collective-permute-start.9 = (bf16[32,1536]{1,0:T(8,128)(2,1)S(1)}, bf16[32,1536]{1,0:T(8,128)(2,1)S(1)}, u32[]{:S(2)}, u32[]{:S(2)}) collective-permute-start(bf16[32,1536]{1,0:T(8,128)(2,1)S(1)} %get-tuple-element.52), channel_id=1, source_target_pairs={{0,3},{1,2},{2,1},{3,0},{4,7},{5,6},{6,5},{7,4},{8,11},{9,10},{10,... | collective-permute-start | bytes 294920 | tf_op jit(solution)/shard_map/ppermute | solution.py:340
  15.2 7.2 %collective-permute-start.10 = (bf16[32,1536]{1,0:T(8,128)(2,1)S(1)}, bf16[32,1536]{1,0:T(8,128)(2,1)S(1)}, u32[]{:S(2)}, u32[]{:S(2)}) collective-permute-start(bf16[32,1536]{1,0:T(8,128)(2,1)S(1)} %get-tuple-element.53), channel_id=1, source_target_pairs={{0,2},{1,3},{2,0},{3,1},{4,6},{5,7},{6,4},{7,5},{8,10},{9,11},{10,... | collective-permute-start | bytes 294920 | tf_op jit(solution)/shard_map/ppermute | solution.py:340
  16.8 5.7 %collective-permute-start.11 = (bf16[32,1536]{1,0:T(8,128)(2,1)S(1)}, bf16[32,1536]{1,0:T(8,128)(2,1)S(1)}, u32[]{:S(2)}, u32[]{:S(2)}) collective-permute-start(bf16[32,1536]{1,0:T(8,128)(2,1)S(1)} %get-tuple-element.54), channel_id=1, source_target_pairs={{0,1},{1,0},{2,3},{3,2},{4,5},{5,4},{6,7},{7,6},{8,9},{9,8},{10,11... | collective-permute-start | bytes 294920 | tf_op jit(solution)/shard_map/ppermute | solution.py:340
  18.1 7.4 %collective-permute-start.6 = (bf16[32,1536]{1,0:T(8,128)(2,1)S(1)}, bf16[32,1536]{1,0:T(8,128)(2,1)S(1)}, u32[]{:S(2)}, u32[]{:S(2)}) collective-permute-start(bf16[32,1536]{1,0:T(8,128)(2,1)S(1)} %get-tuple-element.48), channel_id=1, source_target_pairs={{0,3},{1,2},{2,1},{3,0},{4,7},{5,6},{6,5},{7,4},{8,11},{9,10},{10,... | collective-permute-start | bytes 294920 | tf_op jit(solution)/shard_map/ppermute | solution.py:340
  18.8 7.9 %collective-permute-start.7 = (bf16[32,1536]{1,0:T(8,128)(2,1)S(1)}, bf16[32,1536]{1,0:T(8,128)(2,1)S(1)}, u32[]{:S(2)}, u32[]{:S(2)}) collective-permute-start(bf16[32,1536]{1,0:T(8,128)(2,1)S(1)} %get-tuple-element.49), channel_id=1, source_target_pairs={{0,2},{1,3},{2,0},{3,1},{4,6},{5,7},{6,4},{7,5},{8,10},{9,11},{10,... | collective-permute-start | bytes 294920 | tf_op jit(solution)/shard_map/ppermute | solution.py:340
  20.3 6.4 %collective-permute-start.8 = (bf16[32,1536]{1,0:T(8,128)(2,1)S(1)}, bf16[32,1536]{1,0:T(8,128)(2,1)S(1)}, u32[]{:S(2)}, u32[]{:S(2)}) collective-permute-start(bf16[32,1536]{1,0:T(8,128)(2,1)S(1)} %get-tuple-element.50), channel_id=1, source_target_pairs={{0,1},{1,0},{2,3},{3,2},{4,5},{5,4},{6,7},{7,6},{8,9},{9,8},{10,11... | collective-permute-start | bytes 294920 | tf_op jit(solution)/shard_map/ppermute | solution.py:340
  30.8 5.4 %collective-permute-start.12 = (bf16[32,1536]{1,0:T(8,128)(2,1)S(1)}, bf16[32,1536]{1,0:T(8,128)(2,1)S(1)}, u32[]{:S(2)}, u32[]{:S(2)}) collective-permute-start(bf16[32,1536]{1,0:T(8,128)(2,1)S(1)} %get-tuple-element.59), channel_id=1, source_target_pairs={{0,3},{1,2},{2,1},{3,0},{4,7},{5,6},{6,5},{7,4},{8,11},{9,10},{10,... | collective-permute-start | bytes 294920 | tf_op jit(solution)/shard_map/ppermute | solution.py:340
  30.9 7.4 %collective-permute-start.13 = (bf16[32,1536]{1,0:T(8,128)(2,1)S(1)}, bf16[32,1536]{1,0:T(8,128)(2,1)S(1)}, u32[]{:S(2)}, u32[]{:S(2)}) collective-permute-start(bf16[32,1536]{1,0:T(8,128)(2,1)S(1)} %get-tuple-element.60), channel_id=1, source_target_pairs={{0,2},{1,3},{2,0},{3,1},{4,6},{5,7},{6,4},{7,5},{8,10},{9,11},{10,... | collective-permute-start | bytes 294920 | tf_op jit(solution)/shard_map/ppermute | solution.py:340
  32.6 5.8 %collective-permute-start.14 = (bf16[32,1536]{1,0:T(8,128)(2,1)S(1)}, bf16[32,1536]{1,0:T(8,128)(2,1)S(1)}, u32[]{:S(2)}, u32[]{:S(2)}) collective-permute-start(bf16[32,1536]{1,0:T(8,128)(2,1)S(1)} %get-tuple-element.61), channel_id=1, source_target_pairs={{0,1},{1,0},{2,3},{3,2},{4,5},{5,4},{6,7},{7,6},{8,9},{9,8},{10,11... | collective-permute-start | bytes 294920 | tf_op jit(solution)/shard_map/ppermute | solution.py:340
  34.2 7.2 %collective-permute-start.18 = (bf16[32,1536]{1,0:T(8,128)(2,1)S(1)}, bf16[32,1536]{1,0:T(8,128)(2,1)S(1)}, u32[]{:S(2)}, u32[]{:S(2)}) collective-permute-start(bf16[32,1536]{1,0:T(8,128)(2,1)S(1)} %get-tuple-element.70), channel_id=1, source_target_pairs={{0,3},{1,2},{2,1},{3,0},{4,7},{5,6},{6,5},{7,4},{8,11},{9,10},{10,... | collective-permute-start | bytes 294920 | tf_op jit(solution)/shard_map/ppermute | solution.py:340
  34.6 8.5 %collective-permute-start.19 = (bf16[32,1536]{1,0:T(8,128)(2,1)S(1)}, bf16[32,1536]{1,0:T(8,128)(2,1)S(1)}, u32[]{:S(2)}, u32[]{:S(2)}) collective-permute-start(bf16[32,1536]{1,0:T(8,128)(2,1)S(1)} %get-tuple-element.71), channel_id=1, source_target_pairs={{0,2},{1,3},{2,0},{3,1},{4,6},{5,7},{6,4},{7,5},{8,10},{9,11},{10,... | collective-permute-start | bytes 294920 | tf_op jit(solution)/shard_map/ppermute | solution.py:340
  36.2 6.9 %collective-permute-start.20 = (bf16[32,1536]{1,0:T(8,128)(2,1)S(1)}, bf16[32,1536]{1,0:T(8,128)(2,1)S(1)}, u32[]{:S(2)}, u32[]{:S(2)}) collective-permute-start(bf16[32,1536]{1,0:T(8,128)(2,1)S(1)} %get-tuple-element.72), channel_id=1, source_target_pairs={{0,1},{1,0},{2,3},{3,2},{4,5},{5,4},{6,7},{7,6},{8,9},{9,8},{10,11... | collective-permute-start | bytes 294920 | tf_op jit(solution)/shard_map/ppermute | solution.py:340
  38.6 7.5 %collective-permute-start.15 = (bf16[16,1536]{1,0:T(8,128)(2,1)S(1)}, bf16[16,1536]{1,0:T(8,128)(2,1)S(1)}, u32[]{:S(2)}, u32[]{:S(2)}) collective-permute-start(bf16[16,1536]{1,0:T(8,128)(2,1)S(1)} %get-tuple-element.64), channel_id=1, source_target_pairs={{0,12},{4,8},{8,4},{12,0},{1,13},{5,9},{9,5},{13,1},{2,14},{6,10},... | collective-permute-start | bytes 147464 | tf_op jit(solution)/shard_map/ppermute | solution.py:340
  41.3 6.5 %collective-permute-start.16 = (bf16[16,1536]{1,0:T(8,128)(2,1)S(1)}, bf16[16,1536]{1,0:T(8,128)(2,1)S(1)}, u32[]{:S(2)}, u32[]{:S(2)}) collective-permute-start(bf16[16,1536]{1,0:T(8,128)(2,1)S(1)} %get-tuple-element.65), channel_id=1, source_target_pairs={{0,8},{4,12},{8,0},{12,4},{1,9},{5,13},{9,1},{13,5},{2,10},{6,14},... | collective-permute-start | bytes 147464 | tf_op jit(solution)/shard_map/ppermute | solution.py:340
  41.4 6.5 %collective-permute-start.17 = (bf16[16,1536]{1,0:T(8,128)(2,1)S(1)}, bf16[16,1536]{1,0:T(8,128)(2,1)S(1)}, u32[]{:S(2)}, u32[]{:S(2)}) collective-permute-start(bf16[16,1536]{1,0:T(8,128)(2,1)S(1)} %get-tuple-element.66), channel_id=1, source_target_pairs={{0,4},{4,0},{8,12},{12,8},{1,5},{5,1},{9,13},{13,9},{2,6},{6,2},{1... | collective-permute-start | bytes 147464 | tf_op jit(solution)/shard_map/ppermute | solution.py:340
  43.4 6.0 %collective-permute-start.21 = (bf16[16,1536]{1,0:T(8,128)(2,1)S(1)}, bf16[16,1536]{1,0:T(8,128)(2,1)S(1)}, u32[]{:S(2)}, u32[]{:S(2)}) collective-permute-start(bf16[16,1536]{1,0:T(8,128)(2,1)S(1)} %get-tuple-element.74), channel_id=1, source_target_pairs={{0,12},{4,8},{8,4},{12,0},{1,13},{5,9},{9,5},{13,1},{2,14},{6,10},... | collective-permute-start | bytes 147464 | tf_op jit(solution)/shard_map/ppermute | solution.py:340
  46.1 5.0 %collective-permute-start.22 = (bf16[16,1536]{1,0:T(8,128)(2,1)S(1)}, bf16[16,1536]{1,0:T(8,128)(2,1)S(1)}, u32[]{:S(2)}, u32[]{:S(2)}) collective-permute-start(bf16[16,1536]{1,0:T(8,128)(2,1)S(1)} %get-tuple-element.75), channel_id=1, source_target_pairs={{0,8},{4,12},{8,0},{12,4},{1,9},{5,13},{9,1},{13,5},{2,10},{6,14},... | collective-permute-start | bytes 147464 | tf_op jit(solution)/shard_map/ppermute | solution.py:340
  46.1 5.0 %collective-permute-start.23 = (bf16[16,1536]{1,0:T(8,128)(2,1)S(1)}, bf16[16,1536]{1,0:T(8,128)(2,1)S(1)}, u32[]{:S(2)}, u32[]{:S(2)}) collective-permute-start(bf16[16,1536]{1,0:T(8,128)(2,1)S(1)} %get-tuple-element.76), channel_id=1, source_target_pairs={{0,4},{4,0},{8,12},{12,8},{1,5},{5,1},{9,13},{13,9},{2,6},{6,2},{1... | collective-permute-start | bytes 147464 | tf_op jit(solution)/shard_map/ppermute | solution.py:340

commit v16 on v15

--- a/solution.py
+++ b/solution.py
@@ -13,7 +13,7 @@
 CAP = 8
 LANES = 128
 PAIR = 2
-BLOCK = 4
+BLOCK = 8
 STRIPS = 3
 TILE = 256
 UNROLL = 2
@@ -42,25 +42,21 @@
     return index >> (size.bit_length() - 1), index & (size - 1)
 
 
-def slot_map(owners, chunks, batch, experts):
-    rows, slots = chunks * batch, experts * chunks * CAP
-    slot = iota((rows, slots), 1)
-    row = iota((rows, slots), 0)
-    group, wanted = split(slot, CAP)
+def slot_map(me, named, chunks, experts):
+    named = named[:, 0:4].astype(F32).astype(jnp.int32)
+    owners, places = named[:, 0:2] ^ me, named[:, 2:4]
+    rows, slots = named.shape[0], experts * chunks * CAP
+    group, place = split(iota((rows, slots), 1), CAP)
     expert, chunk = split(group, chunks)
-    named = (owners[:, 0:1] == expert) | (owners[:, 1:2] == expert)
-    named = named & (split(row, batch)[0] == chunk)
-    named = jnp.where(named, 1.0, 0.0)
-    left, right = iota((rows, rows), 0), iota((rows, rows), 1)
-    before = jnp.where(right < left, 1.0, 0.0).astype(BF16)
-    place = dot(before, named.astype(BF16))
-    return jnp.where(place == wanted.astype(F32), named, 0.0)
+    taken = [(owners[:, k : k + 1] == expert) & (places[:, k : k + 1] == place) for k in range(2)]
+    here = split(iota((rows, slots), 0), rows // chunks)[0] == chunk
+    return taken[0] & here, taken[1] & here
 
 
 def dispatch(me, rows, named, chunks, experts):
-    owners = named[:, 0:2].astype(F32).astype(jnp.int32) ^ me
-    table = slot_map(owners, chunks, rows.shape[0] // chunks, experts)
-    return dot(table.astype(BF16), rows, ((0,), (0,)))
+    first, second = slot_map(me, named, chunks, experts)
+    table = jnp.where(first | second, 1.0, 0.0).astype(BF16)
+    return dot(table, rows, ((0,), (0,)))
 
 
 def weigh_kernel(me_ref, router_ref, *refs, layers):
@@ -75,10 +71,8 @@
     second = jnp.sum(jnp.where(lane == routes[:, 1:2], logits, 0.0), axis=1, keepdims=True)
     gate0 = 1.0 / (1.0 + jnp.exp(second - first))
     gate1 = 1.0 / (1.0 + jnp.exp(first - second))
-    owners = routes ^ me_ref[0]
-    table = slot_map(owners, layers, rows.shape[0] // layers, experts)
-    expert, _ = split(iota(table.shape, 1), layers * CAP)
-    gates = table * jnp.where(owners[:, 0:1] == expert, gate0, gate1)
+    taken = slot_map(me_ref[0], named, layers, experts)
+    gates = jnp.where(taken[0], gate0, jnp.where(taken[1], gate1, 0.0))
     high = gates.astype(BF16)
     high_ref[...] = high
     low_ref[...] = (gates - high.astype(F32)).astype(BF16)
@@ -99,10 +93,10 @@
     ]
     blocks = [pl.ds(begin, BLOCK) for begin in range(0, batch, BLOCK)]
     groups = [
-        small[:2],
-        [(keys_hbm.at[block], keys_ref.at[block]) for block in blocks],
+        small[:3],
+        *[[(keys_hbm.at[block], keys_ref.at[block])] for block in blocks],
         [(values_hbm.at[block], values_ref.at[block, 0:window]) for block in blocks],
-        small[2:],
+        small[3:],
     ]
     at, copies = 0, []
     for group in groups:
@@ -126,6 +120,15 @@
     def upright(row):
         return jnp.sum(jnp.where(same, row, 0), axis=1, keepdims=True)
 
+    named, lane = jnp.zeros((batch, LANES), jnp.int32), iota((batch, LANES), 1)
+    before = iota((batch, batch), 1) < iota((batch, batch), 0)
+    listed = [routes_ref[k : k + 1, :] for k in range(2)]
+    for k in range(2):
+        route = upright(listed[k])
+        earlier = before & ((listed[0] == route) | (listed[1] == route))
+        place = jnp.sum(jnp.where(earlier, 1, 0), axis=1, keepdims=True)
+        named = jnp.where(lane == k, route, jnp.where(lane == 2 + k, place, named))
+    named = named.astype(F32).astype(BF16)
     queries = queries_ref[...]
     lanes = PAIR * GROUP * batch
     full = -(-lanes // LANES) * LANES
@@ -148,14 +151,17 @@
         if full > lanes:
             spread.append(jnp.zeros((full - lanes, PAIR * HS), BF16))
         spreads.append(jnp.concatenate(spread, axis=0))
-    wait(1)
+    total = [jnp.zeros((window, full), F32) for _ in parts]
+    for b, block in enumerate(blocks):
+        wait(1 + b)
+        for i, part in enumerate(parts):
+            keys = keys_ref[block, :, part].reshape(BLOCK * window, PAIR * HS)
+            products = dot(keys, spreads[i], ((1,), (1,)))
+            for r in range(BLOCK):
+                mine = request == b * BLOCK + r
+                total[i] = jnp.where(mine, products[r * window : (r + 1) * window], total[i])
     weighted = []
-    for spread, part in zip(spreads, parts):
-        keys = keys_ref[:, :, part].reshape(batch * window, PAIR * HS)
-        products = dot(keys, spread, ((1,), (1,)))
-        scores = products[:window]
-        for r in range(1, batch):
-            scores = jnp.where(request == r, products[r * window : (r + 1) * window], scores)
+    for scores in total:
         scores = jnp.where(visible, scores * HS ** (-0.5), -1e30)
         powers = jnp.exp(scores - jnp.max(scores, axis=0, keepdims=True))
         weights = powers / jnp.sum(powers, axis=0, keepdims=True)
@@ -167,7 +173,7 @@
                 [jnp.where(owner == r, weights, 0.0).astype(BF16) for r in range(batch)], axis=1
             )
         )
-    wait(2)
+    wait(-2)
     attended = []
     for weights, part in zip(weighted, parts):
         values = values_ref[:, :, part].reshape(batch * padded, PAIR * HS)
@@ -176,17 +182,14 @@
             mixed[h * batch : (h + 1) * batch, h // GROUP * HS : (h // GROUP + 1) * HS]
             for h in range(PAIR * GROUP)
         ]
-    wait(3)
+    wait(-1)
     stream = residual_ref[...].astype(F32) + jnp.concatenate(attended, axis=1)
     scale = lax.rsqrt(jnp.mean(stream * stream, axis=1, keepdims=True) + 1e-05)
-    lane = iota((batch, LANES), 1)
-    routes = [upright(routes_ref[k : k + 1, :]).astype(F32) for k in range(2)]
-    named = jnp.where(lane == 0, routes[0], jnp.where(lane == 1, routes[1], 0.0))
     stream_ref[...] = stream
     half = width // 2
     normed = (stream * scale * gain_ref[...]).astype(BF16)
     first_ref[:, :half] = normed[:, :half]
-    first_ref[:, half:] = named.astype(BF16)
+    first_ref[:, half:] = named
     second_ref[...] = normed[:, half:]
 
 

time: 51.9 us -> 51.7 us (level)
  no operation moved by 1% of the time
where the time goes in v16:
time: 51.7 us; the launch traced here: 51.5 us
  starting transfers between devices  26.8 us (52%)
  Pallas kernels  13.8 us (27%)
  waiting for transfers between devices  10.7 us (21%)
    ppermute x24, starting transfers between devices, swap(): return lax.ppermute(value, axis, [(i, i ^ step) for i in range(count)])  26.8 us
    ppermute x24, waiting for transfers between devices, swap(): return lax.ppermute(value, axis, [(i, i ^ step) for i in range(count)])  10.7 us
    pallas_call x1, Pallas kernels, shards(): pl.pallas_call(functools.partial(middle_kernel, experts=experts), in_spec...  4.17 us
    pallas_call x1, Pallas kernels, shards(): pl.pallas_call(attend_kernel, in_specs=[SCALAR] + [ANY] * len(operands),...  2.95 us
    pallas_call x1, Pallas kernels, shards(): pl.pallas_call(functools.partial(begin_kernel, experts=experts), in_specs...  2.92 us
    pallas_call x1, Pallas kernels, shards(): pl.pallas_call(end_kernel, in_specs=[WHOLE] * 2, out_specs=[WHOLE] * expe...  1.37 us
  transfers between devices with their start and end apart: 24, of which 8 were waited for; matrix products, arithmetic and copies ran while one was open for 0% of the time, Pallas kernels for 12%

profile of v16, /device:TPU:0, one launch (start us, length us, event | category | flops | bytes accessed | tf_op | source)
XLA Modules:
  0.0 51.5 jit_solution(14410407067009628012)
XLA Ops:
  0.0 2.9 %shard_map.109 = (f32[16,3072]{1,0:T(8,128)S(1)}, bf16[16,1664]{1,0:T(8,128)(2,1)S(1)}, bf16[16,1536]{1,0:T(8,128)(2,1)S(1)}) custom-call(s32[1]{0:T(128)} %bitcast._.me_ref, s32[1,16]{1,0:T(1,128)} %bitcast.21, bf16[16,3072]{1,0:T(8,128)(2,1)} %queries_hbm.1, bf16[16,96,512]{2,1,0:T(8,128)(2,1)} %keys_hbm.1, bf16[16,96,512]{2,1,0:T(8,128)(2,1)} %values_hbm.1, ...), custom_call_target="tpu_custom_call" | custom-call | tf_op jit(solution)/shard_map/pallas_call | solution.py:383
  3.0 0.0 slice-start
  3.0 0.0 slice-start.3
  3.0 0.0 slice-start.1
  3.0 0.0 slice-start.2
  3.0 0.0 slice-start.4
  3.0 0.0 slice-start.5
  3.0 0.0 copy-start
  3.0 5.1 %collective-permute-start.2 = (bf16[16,1664]{1,0:T(8,128)(2,1)S(1)}, bf16[16,1664]{1,0:T(8,128)(2,1)S(1)}, u32[]{:S(2)}, u32[]{:S(2)}) collective-permute-start(bf16[16,1664]{1,0:T(8,128)(2,1)S(1)} %get-tuple-element.43.refs_0_), channel_id=1, source_target_pairs={{0,12},{4,8},{8,4},{12,0},{1,13},{5,9},{9,5},{13,1},{2,14},{6,10},... | collective-permute-start | bytes 159752 | tf_op jit(solution)/shard_map/ppermute | solution.py:343
  8.2 0.0 collective-permute-start.1
  8.2 0.6 %collective-permute-start = (bf16[16,1664]{1,0:T(8,128)(2,1)S(1)}, bf16[16,1664]{1,0:T(8,128)(2,1)S(1)}, u32[]{:S(2)}, u32[]{:S(2)}) collective-permute-start(bf16[16,1664]{1,0:T(8,128)(2,1)S(1)} %get-tuple-element.43.refs_0_), channel_id=1, source_target_pairs={{0,4},{4,0},{8,12},{12,8},{1,5},{5,1},{9,13},{13,9},{2,6},{6,2},{1... | collective-permute-start | bytes 159752 | tf_op jit(solution)/shard_map/ppermute | solution.py:343
  8.8 3.7 %collective-permute-start.5 = (bf16[16,1536]{1,0:T(8,128)(2,1)S(1)}, bf16[16,1536]{1,0:T(8,128)(2,1)S(1)}, u32[]{:S(2)}, u32[]{:S(2)}) collective-permute-start(bf16[16,1536]{1,0:T(8,128)(2,1)S(1)} %get-tuple-element.44.refs_4_), channel_id=1, source_target_pairs={{0,12},{4,8},{8,4},{12,0},{1,13},{5,9},{9,5},{13,1},{2,14},{6,10},... | collective-permute-start | bytes 147464 | tf_op jit(solution)/shard_map/ppermute | solution.py:343
  12.5 0.0 collective-permute-start.4
  12.5 0.0 collective-permute-done.2.refs_3_
  12.6 0.6 %collective-permute-start.3 = (bf16[16,1536]{1,0:T(8,128)(2,1)S(1)}, bf16[16,1536]{1,0:T(8,128)(2,1)S(1)}, u32[]{:S(2)}, u32[]{:S(2)}) collective-permute-start(bf16[16,1536]{1,0:T(8,128)(2,1)S(1)} %get-tuple-element.44.refs_4_), channel_id=1, source_target_pairs={{0,4},{4,0},{8,12},{12,8},{1,5},{5,1},{9,13},{13,9},{2,6},{6,2},{1... | collective-permute-start | bytes 147464 | tf_op jit(solution)/shard_map/ppermute | solution.py:343
  13.2 1.4 %collective-permute-done.1.refs_2_ = bf16[16,1664]{1,0:T(8,128)(2,1)S(1)} collective-permute-done((bf16[16,1664]{1,0:T(8,128)(2,1)S(1)}, bf16[16,1664]{1,0:T(8,128)(2,1)S(1)}, u32[]{:S(2)}, u32[]{:S(2)}) %collective-permute-start.1) | collective-permute-done | bytes 53280 | tf_op jit(solution)/shard_map/ppermute | solution.py:343
  14.6 0.0 collective-permute-done.refs_1_
  14.6 0.4 shard_map.113
  15.0 0.1 collective-permute-start.9
  15.1 1.6 %collective-permute-start.10 = (bf16[32,1536]{1,0:T(8,128)(2,1)S(1)}, bf16[32,1536]{1,0:T(8,128)(2,1)S(1)}, u32[]{:S(2)}, u32[]{:S(2)}) collective-permute-start(bf16[32,1536]{1,0:T(8,128)(2,1)S(1)} %get-tuple-element.53), channel_id=1, source_target_pairs={{0,2},{1,3},{2,0},{3,1},{4,6},{5,7},{6,4},{7,5},{8,10},{9,11},{10,... | collective-permute-start | bytes 294920 | tf_op jit(solution)/shard_map/ppermute | solution.py:343
  16.6 0.0 collective-permute-done.5.refs_7_
  16.6 0.3 collective-permute-start.11
  16.9 0.6 %collective-permute-done.4.refs_6_ = bf16[16,1536]{1,0:T(8,128)(2,1)S(1)} collective-permute-done((bf16[16,1536]{1,0:T(8,128)(2,1)S(1)}, bf16[16,1536]{1,0:T(8,128)(2,1)S(1)}, u32[]{:S(2)}, u32[]{:S(2)}) %collective-permute-start.4) | collective-permute-done | bytes 49184 | tf_op jit(solution)/shard_map/ppermute | solution.py:343
  17.5 0.0 collective-permute-done.3.refs_5_
  17.5 0.4 shard_map.112
  17.9 0.6 %collective-permute-start.6 = (bf16[32,1536]{1,0:T(8,128)(2,1)S(1)}, bf16[32,1536]{1,0:T(8,128)(2,1)S(1)}, u32[]{:S(2)}, u32[]{:S(2)}) collective-permute-start(bf16[32,1536]{1,0:T(8,128)(2,1)S(1)} %get-tuple-element.48), channel_id=1, source_target_pairs={{0,3},{1,2},{2,1},{3,0},{4,7},{5,6},{6,5},{7,4},{8,11},{9,10},{10,... | collective-permute-start | bytes 294920 | tf_op jit(solution)/shard_map/ppermute | solution.py:343
  18.5 1.1 %collective-permute-start.7 = (bf16[32,1536]{1,0:T(8,128)(2,1)S(1)}, bf16[32,1536]{1,0:T(8,128)(2,1)S(1)}, u32[]{:S(2)}, u32[]{:S(2)}) collective-permute-start(bf16[32,1536]{1,0:T(8,128)(2,1)S(1)} %get-tuple-element.49), channel_id=1, source_target_pairs={{0,2},{1,3},{2,0},{3,1},{4,6},{5,7},{6,4},{7,5},{8,10},{9,11},{10,... | collective-permute-start | bytes 294920 | tf_op jit(solution)/shard_map/ppermute | solution.py:343
  19.6 0.4 shard_map.111
  20.0 0.1 collective-permute-done.9.refs_1_
  20.1 0.2 collective-permute-start.8
  20.3 2.0 %collective-permute-done.10.refs_2_ = bf16[32,1536]{1,0:T(8,128)(2,1)S(1)} collective-permute-done((bf16[32,1536]{1,0:T(8,128)(2,1)S(1)}, bf16[32,1536]{1,0:T(8,128)(2,1)S(1)}, u32[]{:S(2)}, u32[]{:S(2)}) %collective-permute-start.10) | collective-permute-done | bytes 98336 | tf_op jit(solution)/shard_map/ppermute | solution.py:343
  22.3 0.0 collective-permute-done.11.refs_3_
  22.4 2.9 %shard_map.114 = (f32[128,2048]{1,0:T(8,128)S(1)}, f32[128,2048]{1,0:T(8,128)S(1)}, bf16[2048,1536]{1,0:T(8,128)(2,1)S(1)}) custom-call(bf16[32,1536]{1,0:T(8,128)(2,1)S(1)} %get-tuple-element.51.refs_0_, bf16[32,1536]{1,0:T(8,128)(2,1)S(1)} %collective-permute-done.9.refs_1_, bf16[32,1536]{1,0:T(8,128)(2,1)S(1)} %collective-permute-done.10.refs_2_, ...), custom_call_target="tpu_custom_call" | custom-call | flops 1610612736 | tf_op jit(solution)/shard_map/pallas_call | solution.py:426
  25.3 0.0 collective-permute-done.6.refs_1_
  25.3 1.2 %collective-permute-done.7.refs_2_ = bf16[32,1536]{1,0:T(8,128)(2,1)S(1)} collective-permute-done((bf16[32,1536]{1,0:T(8,128)(2,1)S(1)}, bf16[32,1536]{1,0:T(8,128)(2,1)S(1)}, u32[]{:S(2)}, u32[]{:S(2)}) %collective-permute-start.7) | collective-permute-done | bytes 98336 | tf_op jit(solution)/shard_map/ppermute | solution.py:343
  26.5 0.0 collective-permute-done.8.refs_3_
  26.5 4.2 %shard_map.115 = (bf16[32,1536]{1,0:T(8,128)(2,1)S(1)}, bf16[32,1536]{1,0:T(8,128)(2,1)S(1)}, bf16[32,1536]{1,0:T(8,128)(2,1)S(1)}, bf16[32,1536]{1,0:T(8,128)(2...) custom-call(bf16[32,1536]{1,0:T(8,128)(2,1)S(1)} %get-tuple-element.47.refs_0_, ...), custom_call_target="tpu_custom_call" | custom-call | tf_op jit(solution)/shard_map/pallas_call | solution.py:437
  30.7 0.1 collective-permute-start.12
  30.8 1.7 %collective-permute-start.13 = (bf16[32,1536]{1,0:T(8,128)(2,1)S(1)}, bf16[32,1536]{1,0:T(8,128)(2,1)S(1)}, u32[]{:S(2)}, u32[]{:S(2)}) collective-permute-start(bf16[32,1536]{1,0:T(8,128)(2,1)S(1)} %get-tuple-element.60), channel_id=1, source_target_pairs={{0,2},{1,3},{2,0},{3,1},{4,6},{5,7},{6,4},{7,5},{8,10},{9,11},{10,... | collective-permute-start | bytes 294920 | tf_op jit(solution)/shard_map/ppermute | solution.py:343
  32.4 0.2 collective-permute-start.14
  32.6 1.4 %shard_map.118 = (bf16[32,1536]{1,0:T(8,128)(2,1)S(1)}, bf16[32,1536]{1,0:T(8,128)(2,1)S(1)}, bf16[32,1536]{1,0:T(8,128)(2,1)S(1)}, bf16[32,1536]{1,0:T(8,128)(2,1)S(1)}) custom-call(bf16[128,2048]{1,0:T(8,128)(2,1)S(1)} %get-tuple-element.67.hidden_ref, bf16[2048,1536]{1,0:T(8,128)(2,1)S(1)} %get-tuple-element.68.down_ref), custom_call_target="tpu_custom_call" | custom-call | flops 805306368 | tf_op jit(solution)/shard_map/pallas_call | solution.py:445
  34.0 0.4 collective-permute-start.18
  34.4 1.6 %collective-permute-start.19 = (bf16[32,1536]{1,0:T(8,128)(2,1)S(1)}, bf16[32,1536]{1,0:T(8,128)(2,1)S(1)}, u32[]{:S(2)}, u32[]{:S(2)}) collective-permute-start(bf16[32,1536]{1,0:T(8,128)(2,1)S(1)} %get-tuple-element.71), channel_id=1, source_target_pairs={{0,2},{1,3},{2,0},{3,1},{4,6},{5,7},{6,4},{7,5},{8,10},{9,11},{10,... | collective-permute-start | bytes 294920 | tf_op jit(solution)/shard_map/ppermute | solution.py:343
  36.0 0.0 collective-permute-done.12.refs_1_
  36.0 0.0 collective-permute-start.20
  36.0 2.2 %collective-permute-done.13.refs_2_ = bf16[32,1536]{1,0:T(8,128)(2,1)S(1)} collective-permute-done((bf16[32,1536]{1,0:T(8,128)(2,1)S(1)}, bf16[32,1536]{1,0:T(8,128)(2,1)S(1)}, u32[]{:S(2)}, u32[]{:S(2)}) %collective-permute-start.13) | collective-permute-done | bytes 98336 | tf_op jit(solution)/shard_map/ppermute | solution.py:343
  38.2 0.0 collective-permute-done.14.refs_3_
  38.2 0.3 shard_map.116
  38.4 2.7 %collective-permute-start.15 = (bf16[16,1536]{1,0:T(8,128)(2,1)S(1)}, bf16[16,1536]{1,0:T(8,128)(2,1)S(1)}, u32[]{:S(2)}, u32[]{:S(2)}) collective-permute-start(bf16[16,1536]{1,0:T(8,128)(2,1)S(1)} %get-tuple-element.64), channel_id=1, source_target_pairs={{0,12},{4,8},{8,4},{12,0},{1,13},{5,9},{9,5},{13,1},{2,14},{6,10},... | collective-permute-start | bytes 147464 | tf_op jit(solution)/shard_map/ppermute | solution.py:343
  41.2 0.0 collective-permute-start.16
  41.2 0.0 collective-permute-done.18.refs_1_
  41.2 1.7 %collective-permute-start.17 = (bf16[16,1536]{1,0:T(8,128)(2,1)S(1)}, bf16[16,1536]{1,0:T(8,128)(2,1)S(1)}, u32[]{:S(2)}, u32[]{:S(2)}) collective-permute-start(bf16[16,1536]{1,0:T(8,128)(2,1)S(1)} %get-tuple-element.66), channel_id=1, source_target_pairs={{0,4},{4,0},{8,12},{12,8},{1,5},{5,1},{9,13},{13,9},{2,6},{6,2},{1... | collective-permute-start | bytes 147464 | tf_op jit(solution)/shard_map/ppermute | solution.py:343
  42.9 0.0 collective-permute-done.19.refs_2_
  42.9 0.0 collective-permute-done.20.refs_3_
  42.9 0.3 shard_map.119
  43.2 2.7 %collective-permute-start.21 = (bf16[16,1536]{1,0:T(8,128)(2,1)S(1)}, bf16[16,1536]{1,0:T(8,128)(2,1)S(1)}, u32[]{:S(2)}, u32[]{:S(2)}) collective-permute-start(bf16[16,1536]{1,0:T(8,128)(2,1)S(1)} %get-tuple-element.74), channel_id=1, source_target_pairs={{0,12},{4,8},{8,4},{12,0},{1,13},{5,9},{9,5},{13,1},{2,14},{6,10},... | collective-permute-start | bytes 147464 | tf_op jit(solution)/shard_map/ppermute | solution.py:343
  45.9 0.0 collective-permute-start.22
  45.9 0.0 collective-permute-done.15.refs_1_
  45.9 1.7 %collective-permute-start.23 = (bf16[16,1536]{1,0:T(8,128)(2,1)S(1)}, bf16[16,1536]{1,0:T(8,128)(2,1)S(1)}, u32[]{:S(2)}, u32[]{:S(2)}) collective-permute-start(bf16[16,1536]{1,0:T(8,128)(2,1)S(1)} %get-tuple-element.76), channel_id=1, source_target_pairs={{0,4},{4,0},{8,12},{12,8},{1,5},{5,1},{9,13},{13,9},{2,6},{6,2},{1... | collective-permute-start | bytes 147464 | tf_op jit(solution)/shard_map/ppermute | solution.py:343
  47.6 0.0 collective-permute-done.17.refs_3_
  47.7 1.5 %collective-permute-done.21.refs_2_ = bf16[16,1536]{1,0:T(8,128)(2,1)S(1)} collective-permute-done((bf16[16,1536]{1,0:T(8,128)(2,1)S(1)}, bf16[16,1536]{1,0:T(8,128)(2,1)S(1)}, u32[]{:S(2)}, u32[]{:S(2)}) %collective-permute-start.21) | collective-permute-done | bytes 49184 | tf_op jit(solution)/shard_map/ppermute | solution.py:343
  49.1 1.7 %collective-permute-done.22.refs_3_ = bf16[16,1536]{1,0:T(8,128)(2,1)S(1)} collective-permute-done((bf16[16,1536]{1,0:T(8,128)(2,1)S(1)}, bf16[16,1536]{1,0:T(8,128)(2,1)S(1)}, u32[]{:S(2)}, u32[]{:S(2)}) %collective-permute-start.22) | collective-permute-done | bytes 49184 | tf_op jit(solution)/shard_map/ppermute | solution.py:343
  50.9 0.0 collective-permute-done.23.refs_4_
  50.9 0.7 %shard_map.120 = bf16[16,3072]{1,0:T(8,128)(2,1)} custom-call(bf16[16,1536]{1,0:T(8,128)(2,1)S(1)} %shard_map.117.refs_0_, f32[16,1536]{1,0:T(8,128)S(1)} %get-tuple-element.73.refs_1_, bf16[16,1536]{1,0:T(8,128)(2,1)S(1)} %collective-permute-done.21.refs_2_, bf16[16,1536]{1,0:T(8,128)(2,1)S(1)} %collective-permute-done.22.refs_3_, ...), custom_call_target="tpu_custom_call" | custom-call | tf_op jit(solution)/shard_map/pallas_call | solution.py:469
  (12 shorter events, 0.0 us)
Async XLA Ops:
  3.0 19.4 %slice-start = ((s8[12582912]{0:T(1024)(128)(4,1)}), s8[4194304]{0:T(1024)(128)(4,1)S(1)}, s32[]{:S(2)}) async-start(s8[12582912]{0:T(1024)(128)(4,1)} %bitcast.8), calls=%async_computation | async-start | bytes 8388608
  3.0 19.4 %slice-start.3 = ((s8[12582912]{0:T(1024)(128)(4,1)}), s8[4194304]{0:T(1024)(128)(4,1)S(1)}, s32[]{:S(2)}) async-start(s8[12582912]{0:T(1024)(128)(4,1)} %bitcast.12), calls=%async_computation.3 | async-start | bytes 8388608
  3.0 19.3 %slice-start.1 = ((s8[12582912]{0:T(1024)(128)(4,1)}), s8[4194304]{0:T(1024)(128)(4,1)S(1)}, s32[]{:S(2)}) async-start(s8[12582912]{0:T(1024)(128)(4,1)} %bitcast.8), calls=%async_computation.1 | async-start | bytes 8388608
  3.0 19.3 %slice-start.2 = ((s8[12582912]{0:T(1024)(128)(4,1)}), s8[4194304]{0:T(1024)(128)(4,1)S(1)}, s32[]{:S(2)}) async-start(s8[12582912]{0:T(1024)(128)(4,1)} %bitcast.8), calls=%async_computation.2 | async-start | bytes 8388608
  3.0 19.3 %slice-start.4 = ((s8[12582912]{0:T(1024)(128)(4,1)}), s8[4194304]{0:T(1024)(128)(4,1)S(1)}, s32[]{:S(2)}) async-start(s8[12582912]{0:T(1024)(128)(4,1)} %bitcast.12), calls=%async_computation.4 | async-start | bytes 8388608
  3.0 19.3 %slice-start.5 = ((s8[12582912]{0:T(1024)(128)(4,1)}), s8[4194304]{0:T(1024)(128)(4,1)S(1)}, s32[]{:S(2)}) async-start(s8[12582912]{0:T(1024)(128)(4,1)} %bitcast.12), calls=%async_computation.5 | async-start | bytes 8388608
  3.0 16.6 %copy-start = (bf16[3072,4]{0,1:T(4,128)(2,1)S(1)}, bf16[3072,4]{0,1:T(4,128)(2,1)}, u32[]{:S(2)}) copy-start(bf16[3072,4]{0,1:T(4,128)(2,1)} %param.18) | copy-start | bytes 73732
  3.0 9.5 %collective-permute-start.2 = (bf16[16,1664]{1,0:T(8,128)(2,1)S(1)}, bf16[16,1664]{1,0:T(8,128)(2,1)S(1)}, u32[]{:S(2)}, u32[]{:S(2)}) collective-permute-start(bf16[16,1664]{1,0:T(8,128)(2,1)S(1)} %get-tuple-element.43.refs_0_), channel_id=1, source_target_pairs={{0,12},{4,8},{8,4},{12,0},{1,13},{5,9},{9,5},{13,1},{2,14},{6,10},... | collective-permute-start | bytes 159752 | tf_op jit(solution)/shard_map/ppermute | solution.py:343
  8.2 6.4 %collective-permute-start.1 = (bf16[16,1664]{1,0:T(8,128)(2,1)S(1)}, bf16[16,1664]{1,0:T(8,128)(2,1)S(1)}, u32[]{:S(2)}, u32[]{:S(2)}) collective-permute-start(bf16[16,1664]{1,0:T(8,128)(2,1)S(1)} %get-tuple-element.43.refs_0_), channel_id=1, source_target_pairs={{0,8},{4,12},{8,0},{12,4},{1,9},{5,13},{9,1},{13,5},{2,10},{6,14},... | collective-permute-start | bytes 159752 | tf_op jit(solution)/shard_map/ppermute | solution.py:343
  8.2 6.4 %collective-permute-start = (bf16[16,1664]{1,0:T(8,128)(2,1)S(1)}, bf16[16,1664]{1,0:T(8,128)(2,1)S(1)}, u32[]{:S(2)}, u32[]{:S(2)}) collective-permute-start(bf16[16,1664]{1,0:T(8,128)(2,1)S(1)} %get-tuple-element.43.refs_0_), channel_id=1, source_target_pairs={{0,4},{4,0},{8,12},{12,8},{1,5},{5,1},{9,13},{13,9},{2,6},{6,2},{1... | collective-permute-start | bytes 159752 | tf_op jit(solution)/shard_map/ppermute | solution.py:343
  8.8 7.8 %collective-permute-start.5 = (bf16[16,1536]{1,0:T(8,128)(2,1)S(1)}, bf16[16,1536]{1,0:T(8,128)(2,1)S(1)}, u32[]{:S(2)}, u32[]{:S(2)}) collective-permute-start(bf16[16,1536]{1,0:T(8,128)(2,1)S(1)} %get-tuple-element.44.refs_4_), channel_id=1, source_target_pairs={{0,12},{4,8},{8,4},{12,0},{1,13},{5,9},{9,5},{13,1},{2,14},{6,10},... | collective-permute-start | bytes 147464 | tf_op jit(solution)/shard_map/ppermute | solution.py:343
  12.5 5.0 %collective-permute-start.4 = (bf16[16,1536]{1,0:T(8,128)(2,1)S(1)}, bf16[16,1536]{1,0:T(8,128)(2,1)S(1)}, u32[]{:S(2)}, u32[]{:S(2)}) collective-permute-start(bf16[16,1536]{1,0:T(8,128)(2,1)S(1)} %get-tuple-element.44.refs_4_), channel_id=1, source_target_pairs={{0,8},{4,12},{8,0},{12,4},{1,9},{5,13},{9,1},{13,5},{2,10},{6,14},... | collective-permute-start | bytes 147464 | tf_op jit(solution)/shard_map/ppermute | solution.py:343
  12.6 5.0 %collective-permute-start.3 = (bf16[16,1536]{1,0:T(8,128)(2,1)S(1)}, bf16[16,1536]{1,0:T(8,128)(2,1)S(1)}, u32[]{:S(2)}, u32[]{:S(2)}) collective-permute-start(bf16[16,1536]{1,0:T(8,128)(2,1)S(1)} %get-tuple-element.44.refs_4_), channel_id=1, source_target_pairs={{0,4},{4,0},{8,12},{12,8},{1,5},{5,1},{9,13},{13,9},{2,6},{6,2},{1... | collective-permute-start | bytes 147464 | tf_op jit(solution)/shard_map/ppermute | solution.py:343
  15.0 5.1 %collective-permute-start.9 = (bf16[32,1536]{1,0:T(8,128)(2,1)S(1)}, bf16[32,1536]{1,0:T(8,128)(2,1)S(1)}, u32[]{:S(2)}, u32[]{:S(2)}) collective-permute-start(bf16[32,1536]{1,0:T(8,128)(2,1)S(1)} %get-tuple-element.52), channel_id=1, source_target_pairs={{0,3},{1,2},{2,1},{3,0},{4,7},{5,6},{6,5},{7,4},{8,11},{9,10},{10,... | collective-permute-start | bytes 294920 | tf_op jit(solution)/shard_map/ppermute | solution.py:343
  15.1 7.2 %collective-permute-start.10 = (bf16[32,1536]{1,0:T(8,128)(2,1)S(1)}, bf16[32,1536]{1,0:T(8,128)(2,1)S(1)}, u32[]{:S(2)}, u32[]{:S(2)}) collective-permute-start(bf16[32,1536]{1,0:T(8,128)(2,1)S(1)} %get-tuple-element.53), channel_id=1, source_target_pairs={{0,2},{1,3},{2,0},{3,1},{4,6},{5,7},{6,4},{7,5},{8,10},{9,11},{10,... | collective-permute-start | bytes 294920 | tf_op jit(solution)/shard_map/ppermute | solution.py:343
  16.6 5.7 %collective-permute-start.11 = (bf16[32,1536]{1,0:T(8,128)(2,1)S(1)}, bf16[32,1536]{1,0:T(8,128)(2,1)S(1)}, u32[]{:S(2)}, u32[]{:S(2)}) collective-permute-start(bf16[32,1536]{1,0:T(8,128)(2,1)S(1)} %get-tuple-element.54), channel_id=1, source_target_pairs={{0,1},{1,0},{2,3},{3,2},{4,5},{5,4},{6,7},{7,6},{8,9},{9,8},{10,11... | collective-permute-start | bytes 294920 | tf_op jit(solution)/shard_map/ppermute | solution.py:343
  17.9 7.4 %collective-permute-start.6 = (bf16[32,1536]{1,0:T(8,128)(2,1)S(1)}, bf16[32,1536]{1,0:T(8,128)(2,1)S(1)}, u32[]{:S(2)}, u32[]{:S(2)}) collective-permute-start(bf16[32,1536]{1,0:T(8,128)(2,1)S(1)} %get-tuple-element.48), channel_id=1, source_target_pairs={{0,3},{1,2},{2,1},{3,0},{4,7},{5,6},{6,5},{7,4},{8,11},{9,10},{10,... | collective-permute-start | bytes 294920 | tf_op jit(solution)/shard_map/ppermute | solution.py:343
  18.5 8.0 %collective-permute-start.7 = (bf16[32,1536]{1,0:T(8,128)(2,1)S(1)}, bf16[32,1536]{1,0:T(8,128)(2,1)S(1)}, u32[]{:S(2)}, u32[]{:S(2)}) collective-permute-start(bf16[32,1536]{1,0:T(8,128)(2,1)S(1)} %get-tuple-element.49), channel_id=1, source_target_pairs={{0,2},{1,3},{2,0},{3,1},{4,6},{5,7},{6,4},{7,5},{8,10},{9,11},{10,... | collective-permute-start | bytes 294920 | tf_op jit(solution)/shard_map/ppermute | solution.py:343
  20.1 6.4 %collective-permute-start.8 = (bf16[32,1536]{1,0:T(8,128)(2,1)S(1)}, bf16[32,1536]{1,0:T(8,128)(2,1)S(1)}, u32[]{:S(2)}, u32[]{:S(2)}) collective-permute-start(bf16[32,1536]{1,0:T(8,128)(2,1)S(1)} %get-tuple-element.50), channel_id=1, source_target_pairs={{0,1},{1,0},{2,3},{3,2},{4,5},{5,4},{6,7},{7,6},{8,9},{9,8},{10,11... | collective-permute-start | bytes 294920 | tf_op jit(solution)/shard_map/ppermute | solution.py:343
  30.7 5.4 %collective-permute-start.12 = (bf16[32,1536]{1,0:T(8,128)(2,1)S(1)}, bf16[32,1536]{1,0:T(8,128)(2,1)S(1)}, u32[]{:S(2)}, u32[]{:S(2)}) collective-permute-start(bf16[32,1536]{1,0:T(8,128)(2,1)S(1)} %get-tuple-element.59), channel_id=1, source_target_pairs={{0,3},{1,2},{2,1},{3,0},{4,7},{5,6},{6,5},{7,4},{8,11},{9,10},{10,... | collective-permute-start | bytes 294920 | tf_op jit(solution)/shard_map/ppermute | solution.py:343
  30.8 7.4 %collective-permute-start.13 = (bf16[32,1536]{1,0:T(8,128)(2,1)S(1)}, bf16[32,1536]{1,0:T(8,128)(2,1)S(1)}, u32[]{:S(2)}, u32[]{:S(2)}) collective-permute-start(bf16[32,1536]{1,0:T(8,128)(2,1)S(1)} %get-tuple-element.60), channel_id=1, source_target_pairs={{0,2},{1,3},{2,0},{3,1},{4,6},{5,7},{6,4},{7,5},{8,10},{9,11},{10,... | collective-permute-start | bytes 294920 | tf_op jit(solution)/shard_map/ppermute | solution.py:343
  32.4 5.7 %collective-permute-start.14 = (bf16[32,1536]{1,0:T(8,128)(2,1)S(1)}, bf16[32,1536]{1,0:T(8,128)(2,1)S(1)}, u32[]{:S(2)}, u32[]{:S(2)}) collective-permute-start(bf16[32,1536]{1,0:T(8,128)(2,1)S(1)} %get-tuple-element.61), channel_id=1, source_target_pairs={{0,1},{1,0},{2,3},{3,2},{4,5},{5,4},{6,7},{7,6},{8,9},{9,8},{10,11... | collective-permute-start | bytes 294920 | tf_op jit(solution)/shard_map/ppermute | solution.py:343
  34.0 7.2 %collective-permute-start.18 = (bf16[32,1536]{1,0:T(8,128)(2,1)S(1)}, bf16[32,1536]{1,0:T(8,128)(2,1)S(1)}, u32[]{:S(2)}, u32[]{:S(2)}) collective-permute-start(bf16[32,1536]{1,0:T(8,128)(2,1)S(1)} %get-tuple-element.70), channel_id=1, source_target_pairs={{0,3},{1,2},{2,1},{3,0},{4,7},{5,6},{6,5},{7,4},{8,11},{9,10},{10,... | collective-permute-start | bytes 294920 | tf_op jit(solution)/shard_map/ppermute | solution.py:343
  34.4 8.5 %collective-permute-start.19 = (bf16[32,1536]{1,0:T(8,128)(2,1)S(1)}, bf16[32,1536]{1,0:T(8,128)(2,1)S(1)}, u32[]{:S(2)}, u32[]{:S(2)}) collective-permute-start(bf16[32,1536]{1,0:T(8,128)(2,1)S(1)} %get-tuple-element.71), channel_id=1, source_target_pairs={{0,2},{1,3},{2,0},{3,1},{4,6},{5,7},{6,4},{7,5},{8,10},{9,11},{10,... | collective-permute-start | bytes 294920 | tf_op jit(solution)/shard_map/ppermute | solution.py:343
  36.0 6.9 %collective-permute-start.20 = (bf16[32,1536]{1,0:T(8,128)(2,1)S(1)}, bf16[32,1536]{1,0:T(8,128)(2,1)S(1)}, u32[]{:S(2)}, u32[]{:S(2)}) collective-permute-start(bf16[32,1536]{1,0:T(8,128)(2,1)S(1)} %get-tuple-element.72), channel_id=1, source_target_pairs={{0,1},{1,0},{2,3},{3,2},{4,5},{5,4},{6,7},{7,6},{8,9},{9,8},{10,11... | collective-permute-start | bytes 294920 | tf_op jit(solution)/shard_map/ppermute | solution.py:343
  38.4 7.4 %collective-permute-start.15 = (bf16[16,1536]{1,0:T(8,128)(2,1)S(1)}, bf16[16,1536]{1,0:T(8,128)(2,1)S(1)}, u32[]{:S(2)}, u32[]{:S(2)}) collective-permute-start(bf16[16,1536]{1,0:T(8,128)(2,1)S(1)} %get-tuple-element.64), channel_id=1, source_target_pairs={{0,12},{4,8},{8,4},{12,0},{1,13},{5,9},{9,5},{13,1},{2,14},{6,10},... | collective-permute-start | bytes 147464 | tf_op jit(solution)/shard_map/ppermute | solution.py:343
  41.2 6.5 %collective-permute-start.16 = (bf16[16,1536]{1,0:T(8,128)(2,1)S(1)}, bf16[16,1536]{1,0:T(8,128)(2,1)S(1)}, u32[]{:S(2)}, u32[]{:S(2)}) collective-permute-start(bf16[16,1536]{1,0:T(8,128)(2,1)S(1)} %get-tuple-element.65), channel_id=1, source_target_pairs={{0,8},{4,12},{8,0},{12,4},{1,9},{5,13},{9,1},{13,5},{2,10},{6,14},... | collective-permute-start | bytes 147464 | tf_op jit(solution)/shard_map/ppermute | solution.py:343
  41.2 6.5 %collective-permute-start.17 = (bf16[16,1536]{1,0:T(8,128)(2,1)S(1)}, bf16[16,1536]{1,0:T(8,128)(2,1)S(1)}, u32[]{:S(2)}, u32[]{:S(2)}) collective-permute-start(bf16[16,1536]{1,0:T(8,128)(2,1)S(1)} %get-tuple-element.66), channel_id=1, source_target_pairs={{0,4},{4,0},{8,12},{12,8},{1,5},{5,1},{9,13},{13,9},{2,6},{6,2},{1... | collective-permute-start | bytes 147464 | tf_op jit(solution)/shard_map/ppermute | solution.py:343
  43.2 6.0 %collective-permute-start.21 = (bf16[16,1536]{1,0:T(8,128)(2,1)S(1)}, bf16[16,1536]{1,0:T(8,128)(2,1)S(1)}, u32[]{:S(2)}, u32[]{:S(2)}) collective-permute-start(bf16[16,1536]{1,0:T(8,128)(2,1)S(1)} %get-tuple-element.74), channel_id=1, source_target_pairs={{0,12},{4,8},{8,4},{12,0},{1,13},{5,9},{9,5},{13,1},{2,14},{6,10},... | collective-permute-start | bytes 147464 | tf_op jit(solution)/shard_map/ppermute | solution.py:343
  45.9 5.0 %collective-permute-start.22 = (bf16[16,1536]{1,0:T(8,128)(2,1)S(1)}, bf16[16,1536]{1,0:T(8,128)(2,1)S(1)}, u32[]{:S(2)}, u32[]{:S(2)}) collective-permute-start(bf16[16,1536]{1,0:T(8,128)(2,1)S(1)} %get-tuple-element.75), channel_id=1, source_target_pairs={{0,8},{4,12},{8,0},{12,4},{1,9},{5,13},{9,1},{13,5},{2,10},{6,14},... | collective-permute-start | bytes 147464 | tf_op jit(solution)/shard_map/ppermute | solution.py:343
  45.9 5.0 %collective-permute-start.23 = (bf16[16,1536]{1,0:T(8,128)(2,1)S(1)}, bf16[16,1536]{1,0:T(8,128)(2,1)S(1)}, u32[]{:S(2)}, u32[]{:S(2)}) collective-permute-start(bf16[16,1536]{1,0:T(8,128)(2,1)S(1)} %get-tuple-element.76), channel_id=1, source_target_pairs={{0,4},{4,0},{8,12},{12,8},{1,5},{5,1},{9,13},{13,9},{2,6},{6,2},{1... | collective-permute-start | bytes 147464 | tf_op jit(solution)/shard_map/ppermute | solution.py:343

commit v17 on v16

--- a/solution.py
+++ b/solution.py
@@ -309,7 +309,7 @@
 def mix_kernel(high_ref, low_ref, *refs, layers, part):
     outs, stream_ref = refs[-layers:], refs[-layers - 1]
     blocks = refs[: -layers - 1]
-    order = farthest_first(len(blocks))
+    order = same_core_first(len(blocks))
     returned = stack([blocks[order.index(e)] for e in range(len(blocks))])
     mixed = dot(high_ref[...], returned) + dot(low_ref[...], returned)
     batch, half = outs[0].shape
@@ -345,6 +345,10 @@
 
 def farthest_first(count):
     return [0, *range(count - 1, 0, -1)]
+
+
+def same_core_first(count):
+    return [*range(0, count, 2), *range(count - 1, 0, -2)]
 
 
 def params(elements):
@@ -394,7 +398,7 @@
 
     payload = pass_on(payload, BUSY)
 
-    order = farthest_first(experts)
+    order = same_core_first(experts)
     chunks, arrived = [], []
     for part in range(2):
         came = {j: swap(payload[part], "attn", j) for j in farthest_first(layers)}

time: 51.7 us -> 50.1 us (0.969)
  waiting for transfers between devices: 10.7 us -> 9.36 us
    ppermute x24, waiting for transfers between devices: 10.7 us -> 9.36 us  [swap(): return lax.ppermute(value, axis, [(i, i ^ step) for i in range(count)])]
  transfers between devices with their start and end apart: 24 -> 24, of which waited for: 8 -> 9; matrix products, arithmetic and copies ran while one was open for 0% -> 0% of each run, Pallas kernels for 12% -> 12%
where the time goes in v17:
time: 50.1 us; the launch traced here: 50 us
  starting transfers between devices  26.6 us (53%)
  Pallas kernels  13.8 us (28%)
  waiting for transfers between devices  9.36 us (19%)
    ppermute x24, starting transfers between devices, swap(): return lax.ppermute(value, axis, [(i, i ^ step) for i in range(count)])  26.6 us
    ppermute x24, waiting for transfers between devices, swap(): return lax.ppermute(value, axis, [(i, i ^ step) for i in range(count)])  9.36 us
    pallas_call x1, Pallas kernels, shards(): pl.pallas_call(functools.partial(middle_kernel, experts=experts), in_spec...  4.18 us
    pallas_call x1, Pallas kernels, shards(): pl.pallas_call(attend_kernel, in_specs=[SCALAR] + [ANY] * len(operands),...  2.95 us
    pallas_call x1, Pallas kernels, shards(): pl.pallas_call(functools.partial(begin_kernel, experts=experts), in_specs...  2.92 us
    pallas_call x1, Pallas kernels, shards(): pl.pallas_call(end_kernel, in_specs=[WHOLE] * 2, out_specs=[WHOLE] * expe...  1.38 us
  transfers between devices with their start and end apart: 24, of which 9 were waited for; matrix products, arithmetic and copies ran while one was open for 0% of the time, Pallas kernels for 12%

profile of v17, /device:TPU:0, one launch (start us, length us, event | category | flops | bytes accessed | tf_op | source)
XLA Modules:
  0.0 50.0 jit_solution(6116777052829415489)
XLA Ops:
  0.0 2.9 %shard_map.109 = (f32[16,3072]{1,0:T(8,128)S(1)}, bf16[16,1664]{1,0:T(8,128)(2,1)S(1)}, bf16[16,1536]{1,0:T(8,128)(2,1)S(1)}) custom-call(s32[1]{0:T(128)} %bitcast._.me_ref, s32[1,16]{1,0:T(1,128)} %bitcast.21, bf16[16,3072]{1,0:T(8,128)(2,1)} %queries_hbm.1, bf16[16,96,512]{2,1,0:T(8,128)(2,1)} %keys_hbm.1, bf16[16,96,512]{2,1,0:T(8,128)(2,1)} %values_hbm.1, ...), custom_call_target="tpu_custom_call" | custom-call | tf_op jit(solution)/shard_map/pallas_call | solution.py:387
  3.0 0.0 slice-start
  3.0 0.0 slice-start.3
  3.0 0.0 slice-start.1
  3.0 0.0 slice-start.2
  3.0 0.0 slice-start.4
  3.0 0.0 slice-start.5
  3.0 0.0 copy-start
  3.0 5.1 %collective-permute-start.2 = (bf16[16,1664]{1,0:T(8,128)(2,1)S(1)}, bf16[16,1664]{1,0:T(8,128)(2,1)S(1)}, u32[]{:S(2)}, u32[]{:S(2)}) collective-permute-start(bf16[16,1664]{1,0:T(8,128)(2,1)S(1)} %get-tuple-element.43.refs_0_), channel_id=1, source_target_pairs={{0,12},{4,8},{8,4},{12,0},{1,13},{5,9},{9,5},{13,1},{2,14},{6,10},... | collective-permute-start | bytes 159752 | tf_op jit(solution)/shard_map/ppermute | solution.py:343
  8.2 0.0 collective-permute-start.1
  8.2 0.6 %collective-permute-start = (bf16[16,1664]{1,0:T(8,128)(2,1)S(1)}, bf16[16,1664]{1,0:T(8,128)(2,1)S(1)}, u32[]{:S(2)}, u32[]{:S(2)}) collective-permute-start(bf16[16,1664]{1,0:T(8,128)(2,1)S(1)} %get-tuple-element.43.refs_0_), channel_id=1, source_target_pairs={{0,4},{4,0},{8,12},{12,8},{1,5},{5,1},{9,13},{13,9},{2,6},{6,2},{1... | collective-permute-start | bytes 159752 | tf_op jit(solution)/shard_map/ppermute | solution.py:343
  8.8 3.7 %collective-permute-start.5 = (bf16[16,1536]{1,0:T(8,128)(2,1)S(1)}, bf16[16,1536]{1,0:T(8,128)(2,1)S(1)}, u32[]{:S(2)}, u32[]{:S(2)}) collective-permute-start(bf16[16,1536]{1,0:T(8,128)(2,1)S(1)} %get-tuple-element.44.refs_4_), channel_id=1, source_target_pairs={{0,12},{4,8},{8,4},{12,0},{1,13},{5,9},{9,5},{13,1},{2,14},{6,10},... | collective-permute-start | bytes 147464 | tf_op jit(solution)/shard_map/ppermute | solution.py:343
  12.5 0.0 collective-permute-start.4
  12.5 0.0 collective-permute-done.2.refs_3_
  12.6 0.6 %collective-permute-start.3 = (bf16[16,1536]{1,0:T(8,128)(2,1)S(1)}, bf16[16,1536]{1,0:T(8,128)(2,1)S(1)}, u32[]{:S(2)}, u32[]{:S(2)}) collective-permute-start(bf16[16,1536]{1,0:T(8,128)(2,1)S(1)} %get-tuple-element.44.refs_4_), channel_id=1, source_target_pairs={{0,4},{4,0},{8,12},{12,8},{1,5},{5,1},{9,13},{13,9},{2,6},{6,2},{1... | collective-permute-start | bytes 147464 | tf_op jit(solution)/shard_map/ppermute | solution.py:343
  13.2 1.4 %collective-permute-done.1.refs_2_ = bf16[16,1664]{1,0:T(8,128)(2,1)S(1)} collective-permute-done((bf16[16,1664]{1,0:T(8,128)(2,1)S(1)}, bf16[16,1664]{1,0:T(8,128)(2,1)S(1)}, u32[]{:S(2)}, u32[]{:S(2)}) %collective-permute-start.1) | collective-permute-done | bytes 53280 | tf_op jit(solution)/shard_map/ppermute | solution.py:343
  14.6 0.0 collective-permute-done.refs_1_
  14.6 0.4 shard_map.113
  15.0 1.6 %collective-permute-start.9 = (bf16[32,1536]{1,0:T(8,128)(2,1)S(1)}, bf16[32,1536]{1,0:T(8,128)(2,1)S(1)}, u32[]{:S(2)}, u32[]{:S(2)}) collective-permute-start(bf16[32,1536]{1,0:T(8,128)(2,1)S(1)} %get-tuple-element.52), channel_id=1, source_target_pairs={{0,2},{1,3},{2,0},{3,1},{4,6},{5,7},{6,4},{7,5},{8,10},{9,11},{10,... | collective-permute-start | bytes 294920 | tf_op jit(solution)/shard_map/ppermute | solution.py:343
  16.6 0.0 collective-permute-start.10
  16.6 0.0 collective-permute-done.5.refs_7_
  16.6 0.6 %collective-permute-start.11 = (bf16[32,1536]{1,0:T(8,128)(2,1)S(1)}, bf16[32,1536]{1,0:T(8,128)(2,1)S(1)}, u32[]{:S(2)}, u32[]{:S(2)}) collective-permute-start(bf16[32,1536]{1,0:T(8,128)(2,1)S(1)} %get-tuple-element.54), channel_id=1, source_target_pairs={{0,1},{1,0},{2,3},{3,2},{4,5},{5,4},{6,7},{7,6},{8,9},{9,8},{10,11... | collective-permute-start | bytes 294920 | tf_op jit(solution)/shard_map/ppermute | solution.py:343
  17.2 0.3 collective-permute-done.4.refs_6_
  17.5 0.0 collective-permute-done.3.refs_5_
  17.5 0.4 shard_map.112
  17.9 1.6 %collective-permute-start.6 = (bf16[32,1536]{1,0:T(8,128)(2,1)S(1)}, bf16[32,1536]{1,0:T(8,128)(2,1)S(1)}, u32[]{:S(2)}, u32[]{:S(2)}) collective-permute-start(bf16[32,1536]{1,0:T(8,128)(2,1)S(1)} %get-tuple-element.48), channel_id=1, source_target_pairs={{0,2},{1,3},{2,0},{3,1},{4,6},{5,7},{6,4},{7,5},{8,10},{9,11},{10,... | collective-permute-start | bytes 294920 | tf_op jit(solution)/shard_map/ppermute | solution.py:343
  19.5 0.0 collective-permute-start.7
  19.5 0.4 shard_map.111
  19.9 0.0 collective-permute-done.9.refs_1_
  19.9 0.7 %collective-permute-start.8 = (bf16[32,1536]{1,0:T(8,128)(2,1)S(1)}, bf16[32,1536]{1,0:T(8,128)(2,1)S(1)}, u32[]{:S(2)}, u32[]{:S(2)}) collective-permute-start(bf16[32,1536]{1,0:T(8,128)(2,1)S(1)} %get-tuple-element.50), channel_id=1, source_target_pairs={{0,1},{1,0},{2,3},{3,2},{4,5},{5,4},{6,7},{7,6},{8,9},{9,8},{10,11... | collective-permute-start | bytes 294920 | tf_op jit(solution)/shard_map/ppermute | solution.py:343
  20.6 1.3 %collective-permute-done.10.refs_2_ = bf16[32,1536]{1,0:T(8,128)(2,1)S(1)} collective-permute-done((bf16[32,1536]{1,0:T(8,128)(2,1)S(1)}, bf16[32,1536]{1,0:T(8,128)(2,1)S(1)}, u32[]{:S(2)}, u32[]{:S(2)}) %collective-permute-start.10) | collective-permute-done | bytes 98336 | tf_op jit(solution)/shard_map/ppermute | solution.py:343
  21.9 0.0 collective-permute-done.11.refs_3_
  21.9 2.9 %shard_map.114 = (f32[128,2048]{1,0:T(8,128)S(1)}, f32[128,2048]{1,0:T(8,128)S(1)}, bf16[2048,1536]{1,0:T(8,128)(2,1)S(1)}) custom-call(bf16[32,1536]{1,0:T(8,128)(2,1)S(1)} %get-tuple-element.51.refs_0_, bf16[32,1536]{1,0:T(8,128)(2,1)S(1)} %collective-permute-done.9.refs_1_, bf16[32,1536]{1,0:T(8,128)(2,1)S(1)} %collective-permute-done.10.refs_2_, ...), custom_call_target="tpu_custom_call" | custom-call | flops 1610612736 | tf_op jit(solution)/shard_map/pallas_call | solution.py:430
  24.8 0.0 collective-permute-done.6.refs_1_
  24.9 1.0 %collective-permute-done.7.refs_2_ = bf16[32,1536]{1,0:T(8,128)(2,1)S(1)} collective-permute-done((bf16[32,1536]{1,0:T(8,128)(2,1)S(1)}, bf16[32,1536]{1,0:T(8,128)(2,1)S(1)}, u32[]{:S(2)}, u32[]{:S(2)}) %collective-permute-start.7) | collective-permute-done | bytes 98336 | tf_op jit(solution)/shard_map/ppermute | solution.py:343
  25.9 0.0 collective-permute-done.8.refs_3_
  25.9 4.2 %shard_map.115 = (bf16[32,1536]{1,0:T(8,128)(2,1)S(1)}, bf16[32,1536]{1,0:T(8,128)(2,1)S(1)}, bf16[32,1536]{1,0:T(8,128)(2,1)S(1)}, bf16[32,1536]{1,0:T(8,128)(2...) custom-call(bf16[32,1536]{1,0:T(8,128)(2,1)S(1)} %get-tuple-element.47.refs_0_, ...), custom_call_target="tpu_custom_call" | custom-call | tf_op jit(solution)/shard_map/pallas_call | solution.py:441
  30.0 0.6 %collective-permute-start.12 = (bf16[32,1536]{1,0:T(8,128)(2,1)S(1)}, bf16[32,1536]{1,0:T(8,128)(2,1)S(1)}, u32[]{:S(2)}, u32[]{:S(2)}) collective-permute-start(bf16[32,1536]{1,0:T(8,128)(2,1)S(1)} %get-tuple-element.59), channel_id=1, source_target_pairs={{0,2},{1,3},{2,0},{3,1},{4,6},{5,7},{6,4},{7,5},{8,10},{9,11},{10,... | collective-permute-start | bytes 294920 | tf_op jit(solution)/shard_map/ppermute | solution.py:343
  30.6 0.9 %collective-permute-start.13 = (bf16[32,1536]{1,0:T(8,128)(2,1)S(1)}, bf16[32,1536]{1,0:T(8,128)(2,1)S(1)}, u32[]{:S(2)}, u32[]{:S(2)}) collective-permute-start(bf16[32,1536]{1,0:T(8,128)(2,1)S(1)} %get-tuple-element.60), channel_id=1, source_target_pairs={{0,3},{1,2},{2,1},{3,0},{4,7},{5,6},{6,5},{7,4},{8,11},{9,10},{10,... | collective-permute-start | bytes 294920 | tf_op jit(solution)/shard_map/ppermute | solution.py:343
  31.6 0.7 %collective-permute-start.14 = (bf16[32,1536]{1,0:T(8,128)(2,1)S(1)}, bf16[32,1536]{1,0:T(8,128)(2,1)S(1)}, u32[]{:S(2)}, u32[]{:S(2)}) collective-permute-start(bf16[32,1536]{1,0:T(8,128)(2,1)S(1)} %get-tuple-element.61), channel_id=1, source_target_pairs={{0,1},{1,0},{2,3},{3,2},{4,5},{5,4},{6,7},{7,6},{8,9},{9,8},{10,11... | collective-permute-start | bytes 294920 | tf_op jit(solution)/shard_map/ppermute | solution.py:343
  32.3 1.4 %shard_map.118 = (bf16[32,1536]{1,0:T(8,128)(2,1)S(1)}, bf16[32,1536]{1,0:T(8,128)(2,1)S(1)}, bf16[32,1536]{1,0:T(8,128)(2,1)S(1)}, bf16[32,1536]{1,0:T(8,128)(2,1)S(1)}) custom-call(bf16[128,2048]{1,0:T(8,128)(2,1)S(1)} %get-tuple-element.67.hidden_ref, bf16[2048,1536]{1,0:T(8,128)(2,1)S(1)} %get-tuple-element.68.down_ref), custom_call_target="tpu_custom_call" | custom-call | flops 805306368 | tf_op jit(solution)/shard_map/pallas_call | solution.py:449
  33.6 0.9 %collective-permute-start.18 = (bf16[32,1536]{1,0:T(8,128)(2,1)S(1)}, bf16[32,1536]{1,0:T(8,128)(2,1)S(1)}, u32[]{:S(2)}, u32[]{:S(2)}) collective-permute-start(bf16[32,1536]{1,0:T(8,128)(2,1)S(1)} %get-tuple-element.70), channel_id=1, source_target_pairs={{0,2},{1,3},{2,0},{3,1},{4,6},{5,7},{6,4},{7,5},{8,10},{9,11},{10,... | collective-permute-start | bytes 294920 | tf_op jit(solution)/shard_map/ppermute | solution.py:343
  34.5 0.5 %collective-permute-start.19 = (bf16[32,1536]{1,0:T(8,128)(2,1)S(1)}, bf16[32,1536]{1,0:T(8,128)(2,1)S(1)}, u32[]{:S(2)}, u32[]{:S(2)}) collective-permute-start(bf16[32,1536]{1,0:T(8,128)(2,1)S(1)} %get-tuple-element.71), channel_id=1, source_target_pairs={{0,3},{1,2},{2,1},{3,0},{4,7},{5,6},{6,5},{7,4},{8,11},{9,10},{10,... | collective-permute-start | bytes 294920 | tf_op jit(solution)/shard_map/ppermute | solution.py:343
  35.1 0.7 %collective-permute-done.12.refs_1_ = bf16[32,1536]{1,0:T(8,128)(2,1)S(1)} collective-permute-done((bf16[32,1536]{1,0:T(8,128)(2,1)S(1)}, bf16[32,1536]{1,0:T(8,128)(2,1)S(1)}, u32[]{:S(2)}, u32[]{:S(2)}) %collective-permute-start.12) | collective-permute-done | bytes 98336 | tf_op jit(solution)/shard_map/ppermute | solution.py:343
  35.8 0.1 collective-permute-start.20
  35.9 0.4 collective-permute-done.13.refs_2_
  36.2 0.0 collective-permute-done.14.refs_3_
  36.2 0.3 shard_map.116
  36.5 2.7 %collective-permute-start.15 = (bf16[16,1536]{1,0:T(8,128)(2,1)S(1)}, bf16[16,1536]{1,0:T(8,128)(2,1)S(1)}, u32[]{:S(2)}, u32[]{:S(2)}) collective-permute-start(bf16[16,1536]{1,0:T(8,128)(2,1)S(1)} %get-tuple-element.64), channel_id=1, source_target_pairs={{0,12},{4,8},{8,4},{12,0},{1,13},{5,9},{9,5},{13,1},{2,14},{6,10},... | collective-permute-start | bytes 147464 | tf_op jit(solution)/shard_map/ppermute | solution.py:343
  39.2 0.0 collective-permute-start.16
  39.2 0.7 %collective-permute-done.18.refs_1_ = bf16[32,1536]{1,0:T(8,128)(2,1)S(1)} collective-permute-done((bf16[32,1536]{1,0:T(8,128)(2,1)S(1)}, bf16[32,1536]{1,0:T(8,128)(2,1)S(1)}, u32[]{:S(2)}, u32[]{:S(2)}) %collective-permute-start.18) | collective-permute-done | bytes 98336 | tf_op jit(solution)/shard_map/ppermute | solution.py:343
  39.8 1.1 %collective-permute-start.17 = (bf16[16,1536]{1,0:T(8,128)(2,1)S(1)}, bf16[16,1536]{1,0:T(8,128)(2,1)S(1)}, u32[]{:S(2)}, u32[]{:S(2)}) collective-permute-start(bf16[16,1536]{1,0:T(8,128)(2,1)S(1)} %get-tuple-element.66), channel_id=1, source_target_pairs={{0,4},{4,0},{8,12},{12,8},{1,5},{5,1},{9,13},{13,9},{2,6},{6,2},{1... | collective-permute-start | bytes 147464 | tf_op jit(solution)/shard_map/ppermute | solution.py:343
  40.9 0.0 collective-permute-done.19.refs_2_
  40.9 0.3 shard_map.119
  41.2 2.7 %collective-permute-start.21 = (bf16[16,1536]{1,0:T(8,128)(2,1)S(1)}, bf16[16,1536]{1,0:T(8,128)(2,1)S(1)}, u32[]{:S(2)}, u32[]{:S(2)}) collective-permute-start(bf16[16,1536]{1,0:T(8,128)(2,1)S(1)} %get-tuple-element.74), channel_id=1, source_target_pairs={{0,12},{4,8},{8,4},{12,0},{1,13},{5,9},{9,5},{13,1},{2,14},{6,10},... | collective-permute-start | bytes 147464 | tf_op jit(solution)/shard_map/ppermute | solution.py:343
  43.9 0.0 collective-permute-start.22
  43.9 0.0 collective-permute-done.15.refs_1_
  43.9 1.8 %collective-permute-start.23 = (bf16[16,1536]{1,0:T(8,128)(2,1)S(1)}, bf16[16,1536]{1,0:T(8,128)(2,1)S(1)}, u32[]{:S(2)}, u32[]{:S(2)}) collective-permute-start(bf16[16,1536]{1,0:T(8,128)(2,1)S(1)} %get-tuple-element.76), channel_id=1, source_target_pairs={{0,4},{4,0},{8,12},{12,8},{1,5},{5,1},{9,13},{13,9},{2,6},{6,2},{1... | collective-permute-start | bytes 147464 | tf_op jit(solution)/shard_map/ppermute | solution.py:343
  45.7 0.0 collective-permute-done.16.refs_2_
  45.7 0.0 collective-permute-done.17.refs_3_
  45.7 1.9 %collective-permute-done.21.refs_2_ = bf16[16,1536]{1,0:T(8,128)(2,1)S(1)} collective-permute-done((bf16[16,1536]{1,0:T(8,128)(2,1)S(1)}, bf16[16,1536]{1,0:T(8,128)(2,1)S(1)}, u32[]{:S(2)}, u32[]{:S(2)}) %collective-permute-start.21) | collective-permute-done | bytes 49184 | tf_op jit(solution)/shard_map/ppermute | solution.py:343
  47.6 1.7 %collective-permute-done.22.refs_3_ = bf16[16,1536]{1,0:T(8,128)(2,1)S(1)} collective-permute-done((bf16[16,1536]{1,0:T(8,128)(2,1)S(1)}, bf16[16,1536]{1,0:T(8,128)(2,1)S(1)}, u32[]{:S(2)}, u32[]{:S(2)}) %collective-permute-start.22) | collective-permute-done | bytes 49184 | tf_op jit(solution)/shard_map/ppermute | solution.py:343
  49.3 0.0 collective-permute-done.23.refs_4_
  49.3 0.7 %shard_map.120 = bf16[16,3072]{1,0:T(8,128)(2,1)} custom-call(bf16[16,1536]{1,0:T(8,128)(2,1)S(1)} %shard_map.117.refs_0_, f32[16,1536]{1,0:T(8,128)S(1)} %get-tuple-element.73.refs_1_, bf16[16,1536]{1,0:T(8,128)(2,1)S(1)} %collective-permute-done.21.refs_2_, bf16[16,1536]{1,0:T(8,128)(2,1)S(1)} %collective-permute-done.22.refs_3_, ...), custom_call_target="tpu_custom_call" | custom-call | tf_op jit(solution)/shard_map/pallas_call | solution.py:473
  (12 shorter events, 0.0 us)
Async XLA Ops:
  3.0 18.9 %slice-start = ((s8[12582912]{0:T(1024)(128)(4,1)}), s8[4194304]{0:T(1024)(128)(4,1)S(1)}, s32[]{:S(2)}) async-start(s8[12582912]{0:T(1024)(128)(4,1)} %bitcast.8), calls=%async_computation | async-start | bytes 8388608
  3.0 18.9 %slice-start.3 = ((s8[12582912]{0:T(1024)(128)(4,1)}), s8[4194304]{0:T(1024)(128)(4,1)S(1)}, s32[]{:S(2)}) async-start(s8[12582912]{0:T(1024)(128)(4,1)} %bitcast.12), calls=%async_computation.3 | async-start | bytes 8388608
  3.0 18.9 %slice-start.1 = ((s8[12582912]{0:T(1024)(128)(4,1)}), s8[4194304]{0:T(1024)(128)(4,1)S(1)}, s32[]{:S(2)}) async-start(s8[12582912]{0:T(1024)(128)(4,1)} %bitcast.8), calls=%async_computation.1 | async-start | bytes 8388608
  3.0 18.9 %slice-start.2 = ((s8[12582912]{0:T(1024)(128)(4,1)}), s8[4194304]{0:T(1024)(128)(4,1)S(1)}, s32[]{:S(2)}) async-start(s8[12582912]{0:T(1024)(128)(4,1)} %bitcast.8), calls=%async_computation.2 | async-start | bytes 8388608
  3.0 18.9 %slice-start.4 = ((s8[12582912]{0:T(1024)(128)(4,1)}), s8[4194304]{0:T(1024)(128)(4,1)S(1)}, s32[]{:S(2)}) async-start(s8[12582912]{0:T(1024)(128)(4,1)} %bitcast.12), calls=%async_computation.4 | async-start | bytes 8388608
  3.0 18.9 %slice-start.5 = ((s8[12582912]{0:T(1024)(128)(4,1)}), s8[4194304]{0:T(1024)(128)(4,1)S(1)}, s32[]{:S(2)}) async-start(s8[12582912]{0:T(1024)(128)(4,1)} %bitcast.12), calls=%async_computation.5 | async-start | bytes 8388608
  3.0 16.5 %copy-start = (bf16[3072,4]{0,1:T(4,128)(2,1)S(1)}, bf16[3072,4]{0,1:T(4,128)(2,1)}, u32[]{:S(2)}) copy-start(bf16[3072,4]{0,1:T(4,128)(2,1)} %param.18) | copy-start | bytes 73732
  3.0 9.5 %collective-permute-start.2 = (bf16[16,1664]{1,0:T(8,128)(2,1)S(1)}, bf16[16,1664]{1,0:T(8,128)(2,1)S(1)}, u32[]{:S(2)}, u32[]{:S(2)}) collective-permute-start(bf16[16,1664]{1,0:T(8,128)(2,1)S(1)} %get-tuple-element.43.refs_0_), channel_id=1, source_target_pairs={{0,12},{4,8},{8,4},{12,0},{1,13},{5,9},{9,5},{13,1},{2,14},{6,10},... | collective-permute-start | bytes 159752 | tf_op jit(solution)/shard_map/ppermute | solution.py:343
  8.2 6.4 %collective-permute-start.1 = (bf16[16,1664]{1,0:T(8,128)(2,1)S(1)}, bf16[16,1664]{1,0:T(8,128)(2,1)S(1)}, u32[]{:S(2)}, u32[]{:S(2)}) collective-permute-start(bf16[16,1664]{1,0:T(8,128)(2,1)S(1)} %get-tuple-element.43.refs_0_), channel_id=1, source_target_pairs={{0,8},{4,12},{8,0},{12,4},{1,9},{5,13},{9,1},{13,5},{2,10},{6,14},... | collective-permute-start | bytes 159752 | tf_op jit(solution)/shard_map/ppermute | solution.py:343
  8.2 6.4 %collective-permute-start = (bf16[16,1664]{1,0:T(8,128)(2,1)S(1)}, bf16[16,1664]{1,0:T(8,128)(2,1)S(1)}, u32[]{:S(2)}, u32[]{:S(2)}) collective-permute-start(bf16[16,1664]{1,0:T(8,128)(2,1)S(1)} %get-tuple-element.43.refs_0_), channel_id=1, source_target_pairs={{0,4},{4,0},{8,12},{12,8},{1,5},{5,1},{9,13},{13,9},{2,6},{6,2},{1... | collective-permute-start | bytes 159752 | tf_op jit(solution)/shard_map/ppermute | solution.py:343
  8.8 7.8 %collective-permute-start.5 = (bf16[16,1536]{1,0:T(8,128)(2,1)S(1)}, bf16[16,1536]{1,0:T(8,128)(2,1)S(1)}, u32[]{:S(2)}, u32[]{:S(2)}) collective-permute-start(bf16[16,1536]{1,0:T(8,128)(2,1)S(1)} %get-tuple-element.44.refs_4_), channel_id=1, source_target_pairs={{0,12},{4,8},{8,4},{12,0},{1,13},{5,9},{9,5},{13,1},{2,14},{6,10},... | collective-permute-start | bytes 147464 | tf_op jit(solution)/shard_map/ppermute | solution.py:343
  12.5 5.0 %collective-permute-start.4 = (bf16[16,1536]{1,0:T(8,128)(2,1)S(1)}, bf16[16,1536]{1,0:T(8,128)(2,1)S(1)}, u32[]{:S(2)}, u32[]{:S(2)}) collective-permute-start(bf16[16,1536]{1,0:T(8,128)(2,1)S(1)} %get-tuple-element.44.refs_4_), channel_id=1, source_target_pairs={{0,8},{4,12},{8,0},{12,4},{1,9},{5,13},{9,1},{13,5},{2,10},{6,14},... | collective-permute-start | bytes 147464 | tf_op jit(solution)/shard_map/ppermute | solution.py:343
  12.6 5.0 %collective-permute-start.3 = (bf16[16,1536]{1,0:T(8,128)(2,1)S(1)}, bf16[16,1536]{1,0:T(8,128)(2,1)S(1)}, u32[]{:S(2)}, u32[]{:S(2)}) collective-permute-start(bf16[16,1536]{1,0:T(8,128)(2,1)S(1)} %get-tuple-element.44.refs_4_), channel_id=1, source_target_pairs={{0,4},{4,0},{8,12},{12,8},{1,5},{5,1},{9,13},{13,9},{2,6},{6,2},{1... | collective-permute-start | bytes 147464 | tf_op jit(solution)/shard_map/ppermute | solution.py:343
  15.0 4.9 %collective-permute-start.9 = (bf16[32,1536]{1,0:T(8,128)(2,1)S(1)}, bf16[32,1536]{1,0:T(8,128)(2,1)S(1)}, u32[]{:S(2)}, u32[]{:S(2)}) collective-permute-start(bf16[32,1536]{1,0:T(8,128)(2,1)S(1)} %get-tuple-element.52), channel_id=1, source_target_pairs={{0,2},{1,3},{2,0},{3,1},{4,6},{5,7},{6,4},{7,5},{8,10},{9,11},{10,... | collective-permute-start | bytes 294920 | tf_op jit(solution)/shard_map/ppermute | solution.py:343
  16.6 5.3 %collective-permute-start.10 = (bf16[32,1536]{1,0:T(8,128)(2,1)S(1)}, bf16[32,1536]{1,0:T(8,128)(2,1)S(1)}, u32[]{:S(2)}, u32[]{:S(2)}) collective-permute-start(bf16[32,1536]{1,0:T(8,128)(2,1)S(1)} %get-tuple-element.53), channel_id=1, source_target_pairs={{0,3},{1,2},{2,1},{3,0},{4,7},{5,6},{6,5},{7,4},{8,11},{9,10},{10,... | collective-permute-start | bytes 294920 | tf_op jit(solution)/shard_map/ppermute | solution.py:343
  16.6 5.3 %collective-permute-start.11 = (bf16[32,1536]{1,0:T(8,128)(2,1)S(1)}, bf16[32,1536]{1,0:T(8,128)(2,1)S(1)}, u32[]{:S(2)}, u32[]{:S(2)}) collective-permute-start(bf16[32,1536]{1,0:T(8,128)(2,1)S(1)} %get-tuple-element.54), channel_id=1, source_target_pairs={{0,1},{1,0},{2,3},{3,2},{4,5},{5,4},{6,7},{7,6},{8,9},{9,8},{10,11... | collective-permute-start | bytes 294920 | tf_op jit(solution)/shard_map/ppermute | solution.py:343
  17.9 6.9 %collective-permute-start.6 = (bf16[32,1536]{1,0:T(8,128)(2,1)S(1)}, bf16[32,1536]{1,0:T(8,128)(2,1)S(1)}, u32[]{:S(2)}, u32[]{:S(2)}) collective-permute-start(bf16[32,1536]{1,0:T(8,128)(2,1)S(1)} %get-tuple-element.48), channel_id=1, source_target_pairs={{0,2},{1,3},{2,0},{3,1},{4,6},{5,7},{6,4},{7,5},{8,10},{9,11},{10,... | collective-permute-start | bytes 294920 | tf_op jit(solution)/shard_map/ppermute | solution.py:343
  19.5 6.3 %collective-permute-start.7 = (bf16[32,1536]{1,0:T(8,128)(2,1)S(1)}, bf16[32,1536]{1,0:T(8,128)(2,1)S(1)}, u32[]{:S(2)}, u32[]{:S(2)}) collective-permute-start(bf16[32,1536]{1,0:T(8,128)(2,1)S(1)} %get-tuple-element.49), channel_id=1, source_target_pairs={{0,3},{1,2},{2,1},{3,0},{4,7},{5,6},{6,5},{7,4},{8,11},{9,10},{10,... | collective-permute-start | bytes 294920 | tf_op jit(solution)/shard_map/ppermute | solution.py:343
  19.9 6.0 %collective-permute-start.8 = (bf16[32,1536]{1,0:T(8,128)(2,1)S(1)}, bf16[32,1536]{1,0:T(8,128)(2,1)S(1)}, u32[]{:S(2)}, u32[]{:S(2)}) collective-permute-start(bf16[32,1536]{1,0:T(8,128)(2,1)S(1)} %get-tuple-element.50), channel_id=1, source_target_pairs={{0,1},{1,0},{2,3},{3,2},{4,5},{5,4},{6,7},{7,6},{8,9},{9,8},{10,11... | collective-permute-start | bytes 294920 | tf_op jit(solution)/shard_map/ppermute | solution.py:343
  30.0 5.7 %collective-permute-start.12 = (bf16[32,1536]{1,0:T(8,128)(2,1)S(1)}, bf16[32,1536]{1,0:T(8,128)(2,1)S(1)}, u32[]{:S(2)}, u32[]{:S(2)}) collective-permute-start(bf16[32,1536]{1,0:T(8,128)(2,1)S(1)} %get-tuple-element.59), channel_id=1, source_target_pairs={{0,2},{1,3},{2,0},{3,1},{4,6},{5,7},{6,4},{7,5},{8,10},{9,11},{10,... | collective-permute-start | bytes 294920 | tf_op jit(solution)/shard_map/ppermute | solution.py:343
  30.6 5.6 %collective-permute-start.13 = (bf16[32,1536]{1,0:T(8,128)(2,1)S(1)}, bf16[32,1536]{1,0:T(8,128)(2,1)S(1)}, u32[]{:S(2)}, u32[]{:S(2)}) collective-permute-start(bf16[32,1536]{1,0:T(8,128)(2,1)S(1)} %get-tuple-element.60), channel_id=1, source_target_pairs={{0,3},{1,2},{2,1},{3,0},{4,7},{5,6},{6,5},{7,4},{8,11},{9,10},{10,... | collective-permute-start | bytes 294920 | tf_op jit(solution)/shard_map/ppermute | solution.py:343
  31.6 4.6 %collective-permute-start.14 = (bf16[32,1536]{1,0:T(8,128)(2,1)S(1)}, bf16[32,1536]{1,0:T(8,128)(2,1)S(1)}, u32[]{:S(2)}, u32[]{:S(2)}) collective-permute-start(bf16[32,1536]{1,0:T(8,128)(2,1)S(1)} %get-tuple-element.61), channel_id=1, source_target_pairs={{0,1},{1,0},{2,3},{3,2},{4,5},{5,4},{6,7},{7,6},{8,9},{9,8},{10,11... | collective-permute-start | bytes 294920 | tf_op jit(solution)/shard_map/ppermute | solution.py:343
  33.6 6.2 %collective-permute-start.18 = (bf16[32,1536]{1,0:T(8,128)(2,1)S(1)}, bf16[32,1536]{1,0:T(8,128)(2,1)S(1)}, u32[]{:S(2)}, u32[]{:S(2)}) collective-permute-start(bf16[32,1536]{1,0:T(8,128)(2,1)S(1)} %get-tuple-element.70), channel_id=1, source_target_pairs={{0,2},{1,3},{2,0},{3,1},{4,6},{5,7},{6,4},{7,5},{8,10},{9,11},{10,... | collective-permute-start | bytes 294920 | tf_op jit(solution)/shard_map/ppermute | solution.py:343
  34.5 6.4 %collective-permute-start.19 = (bf16[32,1536]{1,0:T(8,128)(2,1)S(1)}, bf16[32,1536]{1,0:T(8,128)(2,1)S(1)}, u32[]{:S(2)}, u32[]{:S(2)}) collective-permute-start(bf16[32,1536]{1,0:T(8,128)(2,1)S(1)} %get-tuple-element.71), channel_id=1, source_target_pairs={{0,3},{1,2},{2,1},{3,0},{4,7},{5,6},{6,5},{7,4},{8,11},{9,10},{10,... | collective-permute-start | bytes 294920 | tf_op jit(solution)/shard_map/ppermute | solution.py:343
  35.8 5.2 %collective-permute-start.20 = (bf16[32,1536]{1,0:T(8,128)(2,1)S(1)}, bf16[32,1536]{1,0:T(8,128)(2,1)S(1)}, u32[]{:S(2)}, u32[]{:S(2)}) collective-permute-start(bf16[32,1536]{1,0:T(8,128)(2,1)S(1)} %get-tuple-element.72), channel_id=1, source_target_pairs={{0,1},{1,0},{2,3},{3,2},{4,5},{5,4},{6,7},{7,6},{8,9},{9,8},{10,11... | collective-permute-start | bytes 294920 | tf_op jit(solution)/shard_map/ppermute | solution.py:343
  36.5 7.4 %collective-permute-start.15 = (bf16[16,1536]{1,0:T(8,128)(2,1)S(1)}, bf16[16,1536]{1,0:T(8,128)(2,1)S(1)}, u32[]{:S(2)}, u32[]{:S(2)}) collective-permute-start(bf16[16,1536]{1,0:T(8,128)(2,1)S(1)} %get-tuple-element.64), channel_id=1, source_target_pairs={{0,12},{4,8},{8,4},{12,0},{1,13},{5,9},{9,5},{13,1},{2,14},{6,10},... | collective-permute-start | bytes 147464 | tf_op jit(solution)/shard_map/ppermute | solution.py:343
  39.2 6.5 %collective-permute-start.16 = (bf16[16,1536]{1,0:T(8,128)(2,1)S(1)}, bf16[16,1536]{1,0:T(8,128)(2,1)S(1)}, u32[]{:S(2)}, u32[]{:S(2)}) collective-permute-start(bf16[16,1536]{1,0:T(8,128)(2,1)S(1)} %get-tuple-element.65), channel_id=1, source_target_pairs={{0,8},{4,12},{8,0},{12,4},{1,9},{5,13},{9,1},{13,5},{2,10},{6,14},... | collective-permute-start | bytes 147464 | tf_op jit(solution)/shard_map/ppermute | solution.py:343
  39.8 5.8 %collective-permute-start.17 = (bf16[16,1536]{1,0:T(8,128)(2,1)S(1)}, bf16[16,1536]{1,0:T(8,128)(2,1)S(1)}, u32[]{:S(2)}, u32[]{:S(2)}) collective-permute-start(bf16[16,1536]{1,0:T(8,128)(2,1)S(1)} %get-tuple-element.66), channel_id=1, source_target_pairs={{0,4},{4,0},{8,12},{12,8},{1,5},{5,1},{9,13},{13,9},{2,6},{6,2},{1... | collective-permute-start | bytes 147464 | tf_op jit(solution)/shard_map/ppermute | solution.py:343
  41.2 6.4 %collective-permute-start.21 = (bf16[16,1536]{1,0:T(8,128)(2,1)S(1)}, bf16[16,1536]{1,0:T(8,128)(2,1)S(1)}, u32[]{:S(2)}, u32[]{:S(2)}) collective-permute-start(bf16[16,1536]{1,0:T(8,128)(2,1)S(1)} %get-tuple-element.74), channel_id=1, source_target_pairs={{0,12},{4,8},{8,4},{12,0},{1,13},{5,9},{9,5},{13,1},{2,14},{6,10},... | collective-permute-start | bytes 147464 | tf_op jit(solution)/shard_map/ppermute | solution.py:343
  43.9 5.4 %collective-permute-start.22 = (bf16[16,1536]{1,0:T(8,128)(2,1)S(1)}, bf16[16,1536]{1,0:T(8,128)(2,1)S(1)}, u32[]{:S(2)}, u32[]{:S(2)}) collective-permute-start(bf16[16,1536]{1,0:T(8,128)(2,1)S(1)} %get-tuple-element.75), channel_id=1, source_target_pairs={{0,8},{4,12},{8,0},{12,4},{1,9},{5,13},{9,1},{13,5},{2,10},{6,14},... | collective-permute-start | bytes 147464 | tf_op jit(solution)/shard_map/ppermute | solution.py:343
  43.9 5.4 %collective-permute-start.23 = (bf16[16,1536]{1,0:T(8,128)(2,1)S(1)}, bf16[16,1536]{1,0:T(8,128)(2,1)S(1)}, u32[]{:S(2)}, u32[]{:S(2)}) collective-permute-start(bf16[16,1536]{1,0:T(8,128)(2,1)S(1)} %get-tuple-element.76), channel_id=1, source_target_pairs={{0,4},{4,0},{8,12},{12,8},{1,5},{5,1},{9,13},{13,9},{2,6},{6,2},{1... | collective-permute-start | bytes 147464 | tf_op jit(solution)/shard_map/ppermute | solution.py:343

commit v18 on v17

--- a/solution.py
+++ b/solution.py
@@ -95,7 +95,7 @@
     groups = [
         small[:3],
         *[[(keys_hbm.at[block], keys_ref.at[block])] for block in blocks],
-        [(values_hbm.at[block], values_ref.at[block, 0:window]) for block in blocks],
+        *[[(values_hbm.at[block], values_ref.at[block, 0:window])] for block in blocks],
         small[3:],
     ]
     at, copies = 0, []
@@ -173,15 +173,18 @@
                 [jnp.where(owner == r, weights, 0.0).astype(BF16) for r in range(batch)], axis=1
             )
         )
-    wait(-2)
-    attended = []
-    for weights, part in zip(weighted, parts):
-        values = values_ref[:, :, part].reshape(batch * padded, PAIR * HS)
-        mixed = dot(weights, values)
-        attended += [
-            mixed[h * batch : (h + 1) * batch, h // GROUP * HS : (h // GROUP + 1) * HS]
-            for h in range(PAIR * GROUP)
-        ]
+    mixed = [0.0] * len(parts)
+    reach = BLOCK * padded
+    for b, block in enumerate(blocks):
+        wait(1 + len(blocks) + b)
+        for i, part in enumerate(parts):
+            values = values_ref[block, :, part].reshape(reach, PAIR * HS)
+            mixed[i] = mixed[i] + dot(weighted[i][:, b * reach : (b + 1) * reach], values)
+    attended = [
+        block[h * batch : (h + 1) * batch, h // GROUP * HS : (h // GROUP + 1) * HS]
+        for block in mixed
+        for h in range(PAIR * GROUP)
+    ]
     wait(-1)
     stream = residual_ref[...].astype(F32) + jnp.concatenate(attended, axis=1)
     scale = lax.rsqrt(jnp.mean(stream * stream, axis=1, keepdims=True) + 1e-05)
@@ -309,7 +312,7 @@
 def mix_kernel(high_ref, low_ref, *refs, layers, part):
     outs, stream_ref = refs[-layers:], refs[-layers - 1]
     blocks = refs[: -layers - 1]
-    order = same_core_first(len(blocks))
+    order = even_first(len(blocks))
     returned = stack([blocks[order.index(e)] for e in range(len(blocks))])
     mixed = dot(high_ref[...], returned) + dot(low_ref[...], returned)
     batch, half = outs[0].shape
@@ -343,11 +346,7 @@
     return lax.ppermute(value, axis, [(i, i ^ step) for i in range(count)])
 
 
-def farthest_first(count):
-    return [0, *range(count - 1, 0, -1)]
-
-
-def same_core_first(count):
+def even_first(count):
     return [*range(0, count, 2), *range(count - 1, 0, -2)]
 
 
@@ -398,10 +397,10 @@
 
     payload = pass_on(payload, BUSY)
 
-    order = same_core_first(experts)
+    order = even_first(experts)
     chunks, arrived = [], []
     for part in range(2):
-        came = {j: swap(payload[part], "attn", j) for j in farthest_first(layers)}
+        came = {j: swap(payload[part], "attn", j) for j in even_first(layers)}
         chunks += [came[j] for j in range(layers)]
         slots = pl.pallas_call(
             functools.partial(split_kernel, layers=layers, part=part),
@@ -468,7 +467,7 @@
             cost_estimate=LIGHT,
             compiler_params=params(experts * layers * CAP * half),
         )(*gates, *returned, stream)
-        sums = [swap(mixed[j], "attn", j) for j in farthest_first(layers)]
+        sums = [swap(mixed[j], "attn", j) for j in even_first(layers)]
         done = [
             pl.pallas_call(
                 add_kernel,

time: 50.1 us -> 50.3 us (level)
  waiting for transfers between devices: 9.36 us -> 11 us
  starting transfers between devices: 26.6 us -> 25 us
    ppermute x24, waiting for transfers between devices: 9.36 us -> 11 us  [swap(): return lax.ppermute(value, axis, [(i, i ^ step) for i in range(count)])]
    ppermute x24, starting transfers between devices: 26.6 us -> 25 us  [swap(): return lax.ppermute(value, axis, [(i, i ^ step) for i in range(count)])]
  transfers between devices with their start and end apart: 24 -> 24, of which waited for: 9 -> 11; matrix products, arithmetic and copies ran while one was open for 0% -> 0% of each run, Pallas kernels for 12% -> 12%
where the time goes in v18:
time: 50.3 us; the launch traced here: 50.1 us
  starting transfers between devices  25 us (50%)
  Pallas kernels  13.9 us (28%)
  waiting for transfers between devices  11 us (22%)
    ppermute x24, starting transfers between devices, swap(): return lax.ppermute(value, axis, [(i, i ^ step) for i in range(count)])  25 us
    ppermute x24, waiting for transfers between devices, swap(): return lax.ppermute(value, axis, [(i, i ^ step) for i in range(count)])  11 us
    pallas_call x1, Pallas kernels, shards(): pl.pallas_call(functools.partial(middle_kernel, experts=experts), in_spec...  4.18 us
    pallas_call x1, Pallas kernels, shards(): pl.pallas_call(attend_kernel, in_specs=[SCALAR] + [ANY] * len(operands),...  3.02 us
    pallas_call x1, Pallas kernels, shards(): pl.pallas_call(functools.partial(begin_kernel, experts=experts), in_specs...  2.92 us
    pallas_call x1, Pallas kernels, shards(): pl.pallas_call(end_kernel, in_specs=[WHOLE] * 2, out_specs=[WHOLE] * expe...  1.38 us
  transfers between devices with their start and end apart: 24, of which 11 were waited for; matrix products, arithmetic and copies ran while one was open for 0% of the time, Pallas kernels for 12%

profile of v18, /device:TPU:0, one launch (start us, length us, event | category | flops | bytes accessed | tf_op | source)
XLA Modules:
  0.0 50.1 jit_solution(10067265783652023882)
XLA Ops:
  0.0 3.0 %shard_map.109 = (f32[16,3072]{1,0:T(8,128)S(1)}, bf16[16,1664]{1,0:T(8,128)(2,1)S(1)}, bf16[16,1536]{1,0:T(8,128)(2,1)S(1)}) custom-call(s32[1]{0:T(128)} %bitcast._.me_ref, s32[1,16]{1,0:T(1,128)} %bitcast.21, bf16[16,3072]{1,0:T(8,128)(2,1)} %queries_hbm.1, bf16[16,96,512]{2,1,0:T(8,128)(2,1)} %keys_hbm.1, bf16[16,96,512]{2,1,0:T(8,128)(2,1)} %values_hbm.1, ...), custom_call_target="tpu_custom_call" | custom-call | tf_op jit(solution)/shard_map/pallas_call | solution.py:386
  3.0 0.0 slice-start
  3.0 0.0 slice-start.3
  3.1 0.0 slice-start.1
  3.1 0.0 slice-start.2
  3.1 0.0 slice-start.4
  3.1 0.0 slice-start.5
  3.1 0.0 copy-start
  3.1 5.1 %collective-permute-start.2 = (bf16[16,1664]{1,0:T(8,128)(2,1)S(1)}, bf16[16,1664]{1,0:T(8,128)(2,1)S(1)}, u32[]{:S(2)}, u32[]{:S(2)}) collective-permute-start(bf16[16,1664]{1,0:T(8,128)(2,1)S(1)} %get-tuple-element.43.refs_0_), channel_id=1, source_target_pairs={{0,12},{4,8},{8,4},{12,0},{1,13},{5,9},{9,5},{13,1},{2,14},{6,10},... | collective-permute-start | bytes 159752 | tf_op jit(solution)/shard_map/ppermute | solution.py:346
  8.2 0.0 collective-permute-start.1
  8.2 0.6 %collective-permute-start = (bf16[16,1664]{1,0:T(8,128)(2,1)S(1)}, bf16[16,1664]{1,0:T(8,128)(2,1)S(1)}, u32[]{:S(2)}, u32[]{:S(2)}) collective-permute-start(bf16[16,1664]{1,0:T(8,128)(2,1)S(1)} %get-tuple-element.43.refs_0_), channel_id=1, source_target_pairs={{0,4},{4,0},{8,12},{12,8},{1,5},{5,1},{9,13},{13,9},{2,6},{6,2},{1... | collective-permute-start | bytes 159752 | tf_op jit(solution)/shard_map/ppermute | solution.py:346
  8.9 3.7 %collective-permute-start.5 = (bf16[16,1536]{1,0:T(8,128)(2,1)S(1)}, bf16[16,1536]{1,0:T(8,128)(2,1)S(1)}, u32[]{:S(2)}, u32[]{:S(2)}) collective-permute-start(bf16[16,1536]{1,0:T(8,128)(2,1)S(1)} %get-tuple-element.44.refs_4_), channel_id=1, source_target_pairs={{0,12},{4,8},{8,4},{12,0},{1,13},{5,9},{9,5},{13,1},{2,14},{6,10},... | collective-permute-start | bytes 147464 | tf_op jit(solution)/shard_map/ppermute | solution.py:346
  12.6 0.0 collective-permute-start.4
  12.6 0.0 collective-permute-done.2.refs_3_
  12.6 0.6 %collective-permute-start.3 = (bf16[16,1536]{1,0:T(8,128)(2,1)S(1)}, bf16[16,1536]{1,0:T(8,128)(2,1)S(1)}, u32[]{:S(2)}, u32[]{:S(2)}) collective-permute-start(bf16[16,1536]{1,0:T(8,128)(2,1)S(1)} %get-tuple-element.44.refs_4_), channel_id=1, source_target_pairs={{0,4},{4,0},{8,12},{12,8},{1,5},{5,1},{9,13},{13,9},{2,6},{6,2},{1... | collective-permute-start | bytes 147464 | tf_op jit(solution)/shard_map/ppermute | solution.py:346
  13.3 1.4 %collective-permute-done.1.refs_2_ = bf16[16,1664]{1,0:T(8,128)(2,1)S(1)} collective-permute-done((bf16[16,1664]{1,0:T(8,128)(2,1)S(1)}, bf16[16,1664]{1,0:T(8,128)(2,1)S(1)}, u32[]{:S(2)}, u32[]{:S(2)}) %collective-permute-start.1) | collective-permute-done | bytes 53280 | tf_op jit(solution)/shard_map/ppermute | solution.py:346
  14.7 0.0 collective-permute-done.refs_1_
  14.7 0.4 shard_map.113
  15.1 1.6 %collective-permute-start.9 = (bf16[32,1536]{1,0:T(8,128)(2,1)S(1)}, bf16[32,1536]{1,0:T(8,128)(2,1)S(1)}, u32[]{:S(2)}, u32[]{:S(2)}) collective-permute-start(bf16[32,1536]{1,0:T(8,128)(2,1)S(1)} %get-tuple-element.52), channel_id=1, source_target_pairs={{0,2},{1,3},{2,0},{3,1},{4,6},{5,7},{6,4},{7,5},{8,10},{9,11},{10,... | collective-permute-start | bytes 294920 | tf_op jit(solution)/shard_map/ppermute | solution.py:346
  16.6 0.0 collective-permute-start.10
  16.6 0.0 collective-permute-done.5.refs_7_
  16.6 0.7 %collective-permute-start.11 = (bf16[32,1536]{1,0:T(8,128)(2,1)S(1)}, bf16[32,1536]{1,0:T(8,128)(2,1)S(1)}, u32[]{:S(2)}, u32[]{:S(2)}) collective-permute-start(bf16[32,1536]{1,0:T(8,128)(2,1)S(1)} %get-tuple-element.54), channel_id=1, source_target_pairs={{0,1},{1,0},{2,3},{3,2},{4,5},{5,4},{6,7},{7,6},{8,9},{9,8},{10,11... | collective-permute-start | bytes 294920 | tf_op jit(solution)/shard_map/ppermute | solution.py:346
  17.3 0.3 collective-permute-done.4.refs_6_
  17.6 0.0 collective-permute-done.3.refs_5_
  17.6 0.4 shard_map.112
  18.0 1.6 %collective-permute-start.6 = (bf16[32,1536]{1,0:T(8,128)(2,1)S(1)}, bf16[32,1536]{1,0:T(8,128)(2,1)S(1)}, u32[]{:S(2)}, u32[]{:S(2)}) collective-permute-start(bf16[32,1536]{1,0:T(8,128)(2,1)S(1)} %get-tuple-element.48), channel_id=1, source_target_pairs={{0,2},{1,3},{2,0},{3,1},{4,6},{5,7},{6,4},{7,5},{8,10},{9,11},{10,... | collective-permute-start | bytes 294920 | tf_op jit(solution)/shard_map/ppermute | solution.py:346
  19.6 0.0 collective-permute-start.7
  19.6 0.4 shard_map.111
  20.0 0.0 collective-permute-done.9.refs_1_
  20.0 0.7 %collective-permute-start.8 = (bf16[32,1536]{1,0:T(8,128)(2,1)S(1)}, bf16[32,1536]{1,0:T(8,128)(2,1)S(1)}, u32[]{:S(2)}, u32[]{:S(2)}) collective-permute-start(bf16[32,1536]{1,0:T(8,128)(2,1)S(1)} %get-tuple-element.50), channel_id=1, source_target_pairs={{0,1},{1,0},{2,3},{3,2},{4,5},{5,4},{6,7},{7,6},{8,9},{9,8},{10,11... | collective-permute-start | bytes 294920 | tf_op jit(solution)/shard_map/ppermute | solution.py:346
  20.7 1.3 %collective-permute-done.10.refs_2_ = bf16[32,1536]{1,0:T(8,128)(2,1)S(1)} collective-permute-done((bf16[32,1536]{1,0:T(8,128)(2,1)S(1)}, bf16[32,1536]{1,0:T(8,128)(2,1)S(1)}, u32[]{:S(2)}, u32[]{:S(2)}) %collective-permute-start.10) | collective-permute-done | bytes 98336 | tf_op jit(solution)/shard_map/ppermute | solution.py:346
  21.9 0.0 collective-permute-done.11.refs_3_
  22.0 2.9 %shard_map.114 = (f32[128,2048]{1,0:T(8,128)S(1)}, f32[128,2048]{1,0:T(8,128)S(1)}, bf16[2048,1536]{1,0:T(8,128)(2,1)S(1)}) custom-call(bf16[32,1536]{1,0:T(8,128)(2,1)S(1)} %get-tuple-element.51.refs_0_, bf16[32,1536]{1,0:T(8,128)(2,1)S(1)} %collective-permute-done.9.refs_1_, bf16[32,1536]{1,0:T(8,128)(2,1)S(1)} %collective-permute-done.10.refs_2_, ...), custom_call_target="tpu_custom_call" | custom-call | flops 1610612736 | tf_op jit(solution)/shard_map/pallas_call | solution.py:429
  24.9 0.0 collective-permute-done.6.refs_1_
  24.9 1.0 %collective-permute-done.7.refs_2_ = bf16[32,1536]{1,0:T(8,128)(2,1)S(1)} collective-permute-done((bf16[32,1536]{1,0:T(8,128)(2,1)S(1)}, bf16[32,1536]{1,0:T(8,128)(2,1)S(1)}, u32[]{:S(2)}, u32[]{:S(2)}) %collective-permute-start.7) | collective-permute-done | bytes 98336 | tf_op jit(solution)/shard_map/ppermute | solution.py:346
  25.9 0.0 collective-permute-done.8.refs_3_
  25.9 4.2 %shard_map.115 = (bf16[32,1536]{1,0:T(8,128)(2,1)S(1)}, bf16[32,1536]{1,0:T(8,128)(2,1)S(1)}, bf16[32,1536]{1,0:T(8,128)(2,1)S(1)}, bf16[32,1536]{1,0:T(8,128)(2...) custom-call(bf16[32,1536]{1,0:T(8,128)(2,1)S(1)} %get-tuple-element.47.refs_0_, ...), custom_call_target="tpu_custom_call" | custom-call | tf_op jit(solution)/shard_map/pallas_call | solution.py:440
  30.1 0.6 %collective-permute-start.12 = (bf16[32,1536]{1,0:T(8,128)(2,1)S(1)}, bf16[32,1536]{1,0:T(8,128)(2,1)S(1)}, u32[]{:S(2)}, u32[]{:S(2)}) collective-permute-start(bf16[32,1536]{1,0:T(8,128)(2,1)S(1)} %get-tuple-element.59), channel_id=1, source_target_pairs={{0,2},{1,3},{2,0},{3,1},{4,6},{5,7},{6,4},{7,5},{8,10},{9,11},{10,... | collective-permute-start | bytes 294920 | tf_op jit(solution)/shard_map/ppermute | solution.py:346
  30.7 0.9 %collective-permute-start.13 = (bf16[32,1536]{1,0:T(8,128)(2,1)S(1)}, bf16[32,1536]{1,0:T(8,128)(2,1)S(1)}, u32[]{:S(2)}, u32[]{:S(2)}) collective-permute-start(bf16[32,1536]{1,0:T(8,128)(2,1)S(1)} %get-tuple-element.60), channel_id=1, source_target_pairs={{0,3},{1,2},{2,1},{3,0},{4,7},{5,6},{6,5},{7,4},{8,11},{9,10},{10,... | collective-permute-start | bytes 294920 | tf_op jit(solution)/shard_map/ppermute | solution.py:346
  31.7 0.7 %collective-permute-start.14 = (bf16[32,1536]{1,0:T(8,128)(2,1)S(1)}, bf16[32,1536]{1,0:T(8,128)(2,1)S(1)}, u32[]{:S(2)}, u32[]{:S(2)}) collective-permute-start(bf16[32,1536]{1,0:T(8,128)(2,1)S(1)} %get-tuple-element.61), channel_id=1, source_target_pairs={{0,1},{1,0},{2,3},{3,2},{4,5},{5,4},{6,7},{7,6},{8,9},{9,8},{10,11... | collective-permute-start | bytes 294920 | tf_op jit(solution)/shard_map/ppermute | solution.py:346
  32.3 1.4 %shard_map.118 = (bf16[32,1536]{1,0:T(8,128)(2,1)S(1)}, bf16[32,1536]{1,0:T(8,128)(2,1)S(1)}, bf16[32,1536]{1,0:T(8,128)(2,1)S(1)}, bf16[32,1536]{1,0:T(8,128)(2,1)S(1)}) custom-call(bf16[128,2048]{1,0:T(8,128)(2,1)S(1)} %get-tuple-element.67.hidden_ref, bf16[2048,1536]{1,0:T(8,128)(2,1)S(1)} %get-tuple-element.68.down_ref), custom_call_target="tpu_custom_call" | custom-call | flops 805306368 | tf_op jit(solution)/shard_map/pallas_call | solution.py:448
  33.7 0.9 %collective-permute-start.18 = (bf16[32,1536]{1,0:T(8,128)(2,1)S(1)}, bf16[32,1536]{1,0:T(8,128)(2,1)S(1)}, u32[]{:S(2)}, u32[]{:S(2)}) collective-permute-start(bf16[32,1536]{1,0:T(8,128)(2,1)S(1)} %get-tuple-element.70), channel_id=1, source_target_pairs={{0,2},{1,3},{2,0},{3,1},{4,6},{5,7},{6,4},{7,5},{8,10},{9,11},{10,... | collective-permute-start | bytes 294920 | tf_op jit(solution)/shard_map/ppermute | solution.py:346
  34.6 0.5 %collective-permute-start.19 = (bf16[32,1536]{1,0:T(8,128)(2,1)S(1)}, bf16[32,1536]{1,0:T(8,128)(2,1)S(1)}, u32[]{:S(2)}, u32[]{:S(2)}) collective-permute-start(bf16[32,1536]{1,0:T(8,128)(2,1)S(1)} %get-tuple-element.71), channel_id=1, source_target_pairs={{0,3},{1,2},{2,1},{3,0},{4,7},{5,6},{6,5},{7,4},{8,11},{9,10},{10,... | collective-permute-start | bytes 294920 | tf_op jit(solution)/shard_map/ppermute | solution.py:346
  35.1 0.7 %collective-permute-done.12.refs_1_ = bf16[32,1536]{1,0:T(8,128)(2,1)S(1)} collective-permute-done((bf16[32,1536]{1,0:T(8,128)(2,1)S(1)}, bf16[32,1536]{1,0:T(8,128)(2,1)S(1)}, u32[]{:S(2)}, u32[]{:S(2)}) %collective-permute-start.12) | collective-permute-done | bytes 98336 | tf_op jit(solution)/shard_map/ppermute | solution.py:346
  35.8 0.1 collective-permute-start.20
  35.9 0.4 collective-permute-done.13.refs_2_
  36.3 0.0 collective-permute-done.14.refs_3_
  36.3 0.3 shard_map.116
  36.6 0.8 %collective-permute-start.15 = (bf16[16,1536]{1,0:T(8,128)(2,1)S(1)}, bf16[16,1536]{1,0:T(8,128)(2,1)S(1)}, u32[]{:S(2)}, u32[]{:S(2)}) collective-permute-start(bf16[16,1536]{1,0:T(8,128)(2,1)S(1)} %get-tuple-element.64), channel_id=1, source_target_pairs={{0,8},{4,12},{8,0},{12,4},{1,9},{5,13},{9,1},{13,5},{2,10},{6,14},... | collective-permute-start | bytes 147464 | tf_op jit(solution)/shard_map/ppermute | solution.py:346
  37.4 1.9 %collective-permute-start.16 = (bf16[16,1536]{1,0:T(8,128)(2,1)S(1)}, bf16[16,1536]{1,0:T(8,128)(2,1)S(1)}, u32[]{:S(2)}, u32[]{:S(2)}) collective-permute-start(bf16[16,1536]{1,0:T(8,128)(2,1)S(1)} %get-tuple-element.65), channel_id=1, source_target_pairs={{0,12},{4,8},{8,4},{12,0},{1,13},{5,9},{9,5},{13,1},{2,14},{6,10},... | collective-permute-start | bytes 147464 | tf_op jit(solution)/shard_map/ppermute | solution.py:346
  39.3 0.6 %collective-permute-done.18.refs_1_ = bf16[32,1536]{1,0:T(8,128)(2,1)S(1)} collective-permute-done((bf16[32,1536]{1,0:T(8,128)(2,1)S(1)}, bf16[32,1536]{1,0:T(8,128)(2,1)S(1)}, u32[]{:S(2)}, u32[]{:S(2)}) %collective-permute-start.18) | collective-permute-done | bytes 98336 | tf_op jit(solution)/shard_map/ppermute | solution.py:346
  39.9 0.2 collective-permute-start.17
  40.1 0.5 %collective-permute-done.19.refs_2_ = bf16[32,1536]{1,0:T(8,128)(2,1)S(1)} collective-permute-done((bf16[32,1536]{1,0:T(8,128)(2,1)S(1)}, bf16[32,1536]{1,0:T(8,128)(2,1)S(1)}, u32[]{:S(2)}, u32[]{:S(2)}) %collective-permute-start.19) | collective-permute-done | bytes 98336 | tf_op jit(solution)/shard_map/ppermute | solution.py:346
  40.6 0.3 shard_map.119
  40.9 2.5 %collective-permute-start.21 = (bf16[16,1536]{1,0:T(8,128)(2,1)S(1)}, bf16[16,1536]{1,0:T(8,128)(2,1)S(1)}, u32[]{:S(2)}, u32[]{:S(2)}) collective-permute-start(bf16[16,1536]{1,0:T(8,128)(2,1)S(1)} %get-tuple-element.74), channel_id=1, source_target_pairs={{0,8},{4,12},{8,0},{12,4},{1,9},{5,13},{9,1},{13,5},{2,10},{6,14},... | collective-permute-start | bytes 147464 | tf_op jit(solution)/shard_map/ppermute | solution.py:346
  43.4 1.2 %collective-permute-start.22 = (bf16[16,1536]{1,0:T(8,128)(2,1)S(1)}, bf16[16,1536]{1,0:T(8,128)(2,1)S(1)}, u32[]{:S(2)}, u32[]{:S(2)}) collective-permute-start(bf16[16,1536]{1,0:T(8,128)(2,1)S(1)} %get-tuple-element.75), channel_id=1, source_target_pairs={{0,12},{4,8},{8,4},{12,0},{1,13},{5,9},{9,5},{13,1},{2,14},{6,10},... | collective-permute-start | bytes 147464 | tf_op jit(solution)/shard_map/ppermute | solution.py:346
  44.6 0.0 collective-permute-done.15.refs_1_
  44.6 0.0 collective-permute-start.23
  44.6 0.0 collective-permute-done.16.refs_2_
  44.6 0.4 collective-permute-done.17.refs_3_
  45.0 3.0 %collective-permute-done.21.refs_2_ = bf16[16,1536]{1,0:T(8,128)(2,1)S(1)} collective-permute-done((bf16[16,1536]{1,0:T(8,128)(2,1)S(1)}, bf16[16,1536]{1,0:T(8,128)(2,1)S(1)}, u32[]{:S(2)}, u32[]{:S(2)}) %collective-permute-start.21) | collective-permute-done | bytes 49184 | tf_op jit(solution)/shard_map/ppermute | solution.py:346
  48.1 1.4 %collective-permute-done.22.refs_3_ = bf16[16,1536]{1,0:T(8,128)(2,1)S(1)} collective-permute-done((bf16[16,1536]{1,0:T(8,128)(2,1)S(1)}, bf16[16,1536]{1,0:T(8,128)(2,1)S(1)}, u32[]{:S(2)}, u32[]{:S(2)}) %collective-permute-start.22) | collective-permute-done | bytes 49184 | tf_op jit(solution)/shard_map/ppermute | solution.py:346
  49.4 0.0 collective-permute-done.23.refs_4_
  49.5 0.7 %shard_map.120 = bf16[16,3072]{1,0:T(8,128)(2,1)} custom-call(bf16[16,1536]{1,0:T(8,128)(2,1)S(1)} %shard_map.117.refs_0_, f32[16,1536]{1,0:T(8,128)S(1)} %get-tuple-element.73.refs_1_, bf16[16,1536]{1,0:T(8,128)(2,1)S(1)} %collective-permute-done.21.refs_2_, bf16[16,1536]{1,0:T(8,128)(2,1)S(1)} %collective-permute-done.22.refs_3_, ...), custom_call_target="tpu_custom_call" | custom-call | tf_op jit(solution)/shard_map/pallas_call | solution.py:472
  (12 shorter events, 0.0 us)
Async XLA Ops:
  3.0 18.9 %slice-start = ((s8[12582912]{0:T(1024)(128)(4,1)}), s8[4194304]{0:T(1024)(128)(4,1)S(1)}, s32[]{:S(2)}) async-start(s8[12582912]{0:T(1024)(128)(4,1)} %bitcast.8), calls=%async_computation | async-start | bytes 8388608
  3.0 18.9 %slice-start.3 = ((s8[12582912]{0:T(1024)(128)(4,1)}), s8[4194304]{0:T(1024)(128)(4,1)S(1)}, s32[]{:S(2)}) async-start(s8[12582912]{0:T(1024)(128)(4,1)} %bitcast.12), calls=%async_computation.3 | async-start | bytes 8388608
  3.1 18.9 %slice-start.1 = ((s8[12582912]{0:T(1024)(128)(4,1)}), s8[4194304]{0:T(1024)(128)(4,1)S(1)}, s32[]{:S(2)}) async-start(s8[12582912]{0:T(1024)(128)(4,1)} %bitcast.8), calls=%async_computation.1 | async-start | bytes 8388608
  3.1 18.9 %slice-start.2 = ((s8[12582912]{0:T(1024)(128)(4,1)}), s8[4194304]{0:T(1024)(128)(4,1)S(1)}, s32[]{:S(2)}) async-start(s8[12582912]{0:T(1024)(128)(4,1)} %bitcast.8), calls=%async_computation.2 | async-start | bytes 8388608
  3.1 18.9 %slice-start.4 = ((s8[12582912]{0:T(1024)(128)(4,1)}), s8[4194304]{0:T(1024)(128)(4,1)S(1)}, s32[]{:S(2)}) async-start(s8[12582912]{0:T(1024)(128)(4,1)} %bitcast.12), calls=%async_computation.4 | async-start | bytes 8388608
  3.1 18.9 %slice-start.5 = ((s8[12582912]{0:T(1024)(128)(4,1)}), s8[4194304]{0:T(1024)(128)(4,1)S(1)}, s32[]{:S(2)}) async-start(s8[12582912]{0:T(1024)(128)(4,1)} %bitcast.12), calls=%async_computation.5 | async-start | bytes 8388608
  3.1 16.5 %copy-start = (bf16[3072,4]{0,1:T(4,128)(2,1)S(1)}, bf16[3072,4]{0,1:T(4,128)(2,1)}, u32[]{:S(2)}) copy-start(bf16[3072,4]{0,1:T(4,128)(2,1)} %param.18) | copy-start | bytes 73732
  3.1 9.5 %collective-permute-start.2 = (bf16[16,1664]{1,0:T(8,128)(2,1)S(1)}, bf16[16,1664]{1,0:T(8,128)(2,1)S(1)}, u32[]{:S(2)}, u32[]{:S(2)}) collective-permute-start(bf16[16,1664]{1,0:T(8,128)(2,1)S(1)} %get-tuple-element.43.refs_0_), channel_id=1, source_target_pairs={{0,12},{4,8},{8,4},{12,0},{1,13},{5,9},{9,5},{13,1},{2,14},{6,10},... | collective-permute-start | bytes 159752 | tf_op jit(solution)/shard_map/ppermute | solution.py:346
  8.2 6.4 %collective-permute-start.1 = (bf16[16,1664]{1,0:T(8,128)(2,1)S(1)}, bf16[16,1664]{1,0:T(8,128)(2,1)S(1)}, u32[]{:S(2)}, u32[]{:S(2)}) collective-permute-start(bf16[16,1664]{1,0:T(8,128)(2,1)S(1)} %get-tuple-element.43.refs_0_), channel_id=1, source_target_pairs={{0,8},{4,12},{8,0},{12,4},{1,9},{5,13},{9,1},{13,5},{2,10},{6,14},... | collective-permute-start | bytes 159752 | tf_op jit(solution)/shard_map/ppermute | solution.py:346
  8.2 6.4 %collective-permute-start = (bf16[16,1664]{1,0:T(8,128)(2,1)S(1)}, bf16[16,1664]{1,0:T(8,128)(2,1)S(1)}, u32[]{:S(2)}, u32[]{:S(2)}) collective-permute-start(bf16[16,1664]{1,0:T(8,128)(2,1)S(1)} %get-tuple-element.43.refs_0_), channel_id=1, source_target_pairs={{0,4},{4,0},{8,12},{12,8},{1,5},{5,1},{9,13},{13,9},{2,6},{6,2},{1... | collective-permute-start | bytes 159752 | tf_op jit(solution)/shard_map/ppermute | solution.py:346
  8.9 7.8 %collective-permute-start.5 = (bf16[16,1536]{1,0:T(8,128)(2,1)S(1)}, bf16[16,1536]{1,0:T(8,128)(2,1)S(1)}, u32[]{:S(2)}, u32[]{:S(2)}) collective-permute-start(bf16[16,1536]{1,0:T(8,128)(2,1)S(1)} %get-tuple-element.44.refs_4_), channel_id=1, source_target_pairs={{0,12},{4,8},{8,4},{12,0},{1,13},{5,9},{9,5},{13,1},{2,14},{6,10},... | collective-permute-start | bytes 147464 | tf_op jit(solution)/shard_map/ppermute | solution.py:346
  12.6 5.0 %collective-permute-start.4 = (bf16[16,1536]{1,0:T(8,128)(2,1)S(1)}, bf16[16,1536]{1,0:T(8,128)(2,1)S(1)}, u32[]{:S(2)}, u32[]{:S(2)}) collective-permute-start(bf16[16,1536]{1,0:T(8,128)(2,1)S(1)} %get-tuple-element.44.refs_4_), channel_id=1, source_target_pairs={{0,8},{4,12},{8,0},{12,4},{1,9},{5,13},{9,1},{13,5},{2,10},{6,14},... | collective-permute-start | bytes 147464 | tf_op jit(solution)/shard_map/ppermute | solution.py:346
  12.6 5.0 %collective-permute-start.3 = (bf16[16,1536]{1,0:T(8,128)(2,1)S(1)}, bf16[16,1536]{1,0:T(8,128)(2,1)S(1)}, u32[]{:S(2)}, u32[]{:S(2)}) collective-permute-start(bf16[16,1536]{1,0:T(8,128)(2,1)S(1)} %get-tuple-element.44.refs_4_), channel_id=1, source_target_pairs={{0,4},{4,0},{8,12},{12,8},{1,5},{5,1},{9,13},{13,9},{2,6},{6,2},{1... | collective-permute-start | bytes 147464 | tf_op jit(solution)/shard_map/ppermute | solution.py:346
  15.1 4.9 %collective-permute-start.9 = (bf16[32,1536]{1,0:T(8,128)(2,1)S(1)}, bf16[32,1536]{1,0:T(8,128)(2,1)S(1)}, u32[]{:S(2)}, u32[]{:S(2)}) collective-permute-start(bf16[32,1536]{1,0:T(8,128)(2,1)S(1)} %get-tuple-element.52), channel_id=1, source_target_pairs={{0,2},{1,3},{2,0},{3,1},{4,6},{5,7},{6,4},{7,5},{8,10},{9,11},{10,... | collective-permute-start | bytes 294920 | tf_op jit(solution)/shard_map/ppermute | solution.py:346
  16.6 5.3 %collective-permute-start.10 = (bf16[32,1536]{1,0:T(8,128)(2,1)S(1)}, bf16[32,1536]{1,0:T(8,128)(2,1)S(1)}, u32[]{:S(2)}, u32[]{:S(2)}) collective-permute-start(bf16[32,1536]{1,0:T(8,128)(2,1)S(1)} %get-tuple-element.53), channel_id=1, source_target_pairs={{0,3},{1,2},{2,1},{3,0},{4,7},{5,6},{6,5},{7,4},{8,11},{9,10},{10,... | collective-permute-start | bytes 294920 | tf_op jit(solution)/shard_map/ppermute | solution.py:346
  16.6 5.3 %collective-permute-start.11 = (bf16[32,1536]{1,0:T(8,128)(2,1)S(1)}, bf16[32,1536]{1,0:T(8,128)(2,1)S(1)}, u32[]{:S(2)}, u32[]{:S(2)}) collective-permute-start(bf16[32,1536]{1,0:T(8,128)(2,1)S(1)} %get-tuple-element.54), channel_id=1, source_target_pairs={{0,1},{1,0},{2,3},{3,2},{4,5},{5,4},{6,7},{7,6},{8,9},{9,8},{10,11... | collective-permute-start | bytes 294920 | tf_op jit(solution)/shard_map/ppermute | solution.py:346
  18.0 6.9 %collective-permute-start.6 = (bf16[32,1536]{1,0:T(8,128)(2,1)S(1)}, bf16[32,1536]{1,0:T(8,128)(2,1)S(1)}, u32[]{:S(2)}, u32[]{:S(2)}) collective-permute-start(bf16[32,1536]{1,0:T(8,128)(2,1)S(1)} %get-tuple-element.48), channel_id=1, source_target_pairs={{0,2},{1,3},{2,0},{3,1},{4,6},{5,7},{6,4},{7,5},{8,10},{9,11},{10,... | collective-permute-start | bytes 294920 | tf_op jit(solution)/shard_map/ppermute | solution.py:346
  19.6 6.3 %collective-permute-start.7 = (bf16[32,1536]{1,0:T(8,128)(2,1)S(1)}, bf16[32,1536]{1,0:T(8,128)(2,1)S(1)}, u32[]{:S(2)}, u32[]{:S(2)}) collective-permute-start(bf16[32,1536]{1,0:T(8,128)(2,1)S(1)} %get-tuple-element.49), channel_id=1, source_target_pairs={{0,3},{1,2},{2,1},{3,0},{4,7},{5,6},{6,5},{7,4},{8,11},{9,10},{10,... | collective-permute-start | bytes 294920 | tf_op jit(solution)/shard_map/ppermute | solution.py:346
  20.0 6.0 %collective-permute-start.8 = (bf16[32,1536]{1,0:T(8,128)(2,1)S(1)}, bf16[32,1536]{1,0:T(8,128)(2,1)S(1)}, u32[]{:S(2)}, u32[]{:S(2)}) collective-permute-start(bf16[32,1536]{1,0:T(8,128)(2,1)S(1)} %get-tuple-element.50), channel_id=1, source_target_pairs={{0,1},{1,0},{2,3},{3,2},{4,5},{5,4},{6,7},{7,6},{8,9},{9,8},{10,11... | collective-permute-start | bytes 294920 | tf_op jit(solution)/shard_map/ppermute | solution.py:346
  30.1 5.7 %collective-permute-start.12 = (bf16[32,1536]{1,0:T(8,128)(2,1)S(1)}, bf16[32,1536]{1,0:T(8,128)(2,1)S(1)}, u32[]{:S(2)}, u32[]{:S(2)}) collective-permute-start(bf16[32,1536]{1,0:T(8,128)(2,1)S(1)} %get-tuple-element.59), channel_id=1, source_target_pairs={{0,2},{1,3},{2,0},{3,1},{4,6},{5,7},{6,4},{7,5},{8,10},{9,11},{10,... | collective-permute-start | bytes 294920 | tf_op jit(solution)/shard_map/ppermute | solution.py:346
  30.7 5.6 %collective-permute-start.13 = (bf16[32,1536]{1,0:T(8,128)(2,1)S(1)}, bf16[32,1536]{1,0:T(8,128)(2,1)S(1)}, u32[]{:S(2)}, u32[]{:S(2)}) collective-permute-start(bf16[32,1536]{1,0:T(8,128)(2,1)S(1)} %get-tuple-element.60), channel_id=1, source_target_pairs={{0,3},{1,2},{2,1},{3,0},{4,7},{5,6},{6,5},{7,4},{8,11},{9,10},{10,... | collective-permute-start | bytes 294920 | tf_op jit(solution)/shard_map/ppermute | solution.py:346
  31.7 4.6 %collective-permute-start.14 = (bf16[32,1536]{1,0:T(8,128)(2,1)S(1)}, bf16[32,1536]{1,0:T(8,128)(2,1)S(1)}, u32[]{:S(2)}, u32[]{:S(2)}) collective-permute-start(bf16[32,1536]{1,0:T(8,128)(2,1)S(1)} %get-tuple-element.61), channel_id=1, source_target_pairs={{0,1},{1,0},{2,3},{3,2},{4,5},{5,4},{6,7},{7,6},{8,9},{9,8},{10,11... | collective-permute-start | bytes 294920 | tf_op jit(solution)/shard_map/ppermute | solution.py:346
  33.7 6.2 %collective-permute-start.18 = (bf16[32,1536]{1,0:T(8,128)(2,1)S(1)}, bf16[32,1536]{1,0:T(8,128)(2,1)S(1)}, u32[]{:S(2)}, u32[]{:S(2)}) collective-permute-start(bf16[32,1536]{1,0:T(8,128)(2,1)S(1)} %get-tuple-element.70), channel_id=1, source_target_pairs={{0,2},{1,3},{2,0},{3,1},{4,6},{5,7},{6,4},{7,5},{8,10},{9,11},{10,... | collective-permute-start | bytes 294920 | tf_op jit(solution)/shard_map/ppermute | solution.py:346
  34.6 6.0 %collective-permute-start.19 = (bf16[32,1536]{1,0:T(8,128)(2,1)S(1)}, bf16[32,1536]{1,0:T(8,128)(2,1)S(1)}, u32[]{:S(2)}, u32[]{:S(2)}) collective-permute-start(bf16[32,1536]{1,0:T(8,128)(2,1)S(1)} %get-tuple-element.71), channel_id=1, source_target_pairs={{0,3},{1,2},{2,1},{3,0},{4,7},{5,6},{6,5},{7,4},{8,11},{9,10},{10,... | collective-permute-start | bytes 294920 | tf_op jit(solution)/shard_map/ppermute | solution.py:346
  35.8 4.8 %collective-permute-start.20 = (bf16[32,1536]{1,0:T(8,128)(2,1)S(1)}, bf16[32,1536]{1,0:T(8,128)(2,1)S(1)}, u32[]{:S(2)}, u32[]{:S(2)}) collective-permute-start(bf16[32,1536]{1,0:T(8,128)(2,1)S(1)} %get-tuple-element.72), channel_id=1, source_target_pairs={{0,1},{1,0},{2,3},{3,2},{4,5},{5,4},{6,7},{7,6},{8,9},{9,8},{10,11... | collective-permute-start | bytes 294920 | tf_op jit(solution)/shard_map/ppermute | solution.py:346
  36.6 8.1 %collective-permute-start.15 = (bf16[16,1536]{1,0:T(8,128)(2,1)S(1)}, bf16[16,1536]{1,0:T(8,128)(2,1)S(1)}, u32[]{:S(2)}, u32[]{:S(2)}) collective-permute-start(bf16[16,1536]{1,0:T(8,128)(2,1)S(1)} %get-tuple-element.64), channel_id=1, source_target_pairs={{0,8},{4,12},{8,0},{12,4},{1,9},{5,13},{9,1},{13,5},{2,10},{6,14},... | collective-permute-start | bytes 147464 | tf_op jit(solution)/shard_map/ppermute | solution.py:346
  37.4 7.2 %collective-permute-start.16 = (bf16[16,1536]{1,0:T(8,128)(2,1)S(1)}, bf16[16,1536]{1,0:T(8,128)(2,1)S(1)}, u32[]{:S(2)}, u32[]{:S(2)}) collective-permute-start(bf16[16,1536]{1,0:T(8,128)(2,1)S(1)} %get-tuple-element.65), channel_id=1, source_target_pairs={{0,12},{4,8},{8,4},{12,0},{1,13},{5,9},{9,5},{13,1},{2,14},{6,10},... | collective-permute-start | bytes 147464 | tf_op jit(solution)/shard_map/ppermute | solution.py:346
  39.9 5.1 %collective-permute-start.17 = (bf16[16,1536]{1,0:T(8,128)(2,1)S(1)}, bf16[16,1536]{1,0:T(8,128)(2,1)S(1)}, u32[]{:S(2)}, u32[]{:S(2)}) collective-permute-start(bf16[16,1536]{1,0:T(8,128)(2,1)S(1)} %get-tuple-element.66), channel_id=1, source_target_pairs={{0,4},{4,0},{8,12},{12,8},{1,5},{5,1},{9,13},{13,9},{2,6},{6,2},{1... | collective-permute-start | bytes 147464 | tf_op jit(solution)/shard_map/ppermute | solution.py:346
  40.9 7.1 %collective-permute-start.21 = (bf16[16,1536]{1,0:T(8,128)(2,1)S(1)}, bf16[16,1536]{1,0:T(8,128)(2,1)S(1)}, u32[]{:S(2)}, u32[]{:S(2)}) collective-permute-start(bf16[16,1536]{1,0:T(8,128)(2,1)S(1)} %get-tuple-element.74), channel_id=1, source_target_pairs={{0,8},{4,12},{8,0},{12,4},{1,9},{5,13},{9,1},{13,5},{2,10},{6,14},... | collective-permute-start | bytes 147464 | tf_op jit(solution)/shard_map/ppermute | solution.py:346
  43.4 6.0 %collective-permute-start.22 = (bf16[16,1536]{1,0:T(8,128)(2,1)S(1)}, bf16[16,1536]{1,0:T(8,128)(2,1)S(1)}, u32[]{:S(2)}, u32[]{:S(2)}) collective-permute-start(bf16[16,1536]{1,0:T(8,128)(2,1)S(1)} %get-tuple-element.75), channel_id=1, source_target_pairs={{0,12},{4,8},{8,4},{12,0},{1,13},{5,9},{9,5},{13,1},{2,14},{6,10},... | collective-permute-start | bytes 147464 | tf_op jit(solution)/shard_map/ppermute | solution.py:346
  44.6 4.9 %collective-permute-start.23 = (bf16[16,1536]{1,0:T(8,128)(2,1)S(1)}, bf16[16,1536]{1,0:T(8,128)(2,1)S(1)}, u32[]{:S(2)}, u32[]{:S(2)}) collective-permute-start(bf16[16,1536]{1,0:T(8,128)(2,1)S(1)} %get-tuple-element.76), channel_id=1, source_target_pairs={{0,4},{4,0},{8,12},{12,8},{1,5},{5,1},{9,13},{13,9},{2,6},{6,2},{1... | collective-permute-start | bytes 147464 | tf_op jit(solution)/shard_map/ppermute | solution.py:346

commit v19 on v18

--- a/solution.py
+++ b/solution.py
@@ -398,10 +398,11 @@
     payload = pass_on(payload, BUSY)
 
     order = even_first(experts)
+    placed = [0, *even_first(layers)[:0:-1]]
     chunks, arrived = [], []
     for part in range(2):
         came = {j: swap(payload[part], "attn", j) for j in even_first(layers)}
-        chunks += [came[j] for j in range(layers)]
+        chunks += [came[j] for j in placed]
         slots = pl.pallas_call(
             functools.partial(split_kernel, layers=layers, part=part),
             in_specs=[SCALAR] + [WHOLE] * len(chunks),
@@ -467,7 +468,7 @@
             cost_estimate=LIGHT,
             compiler_params=params(experts * layers * CAP * half),
         )(*gates, *returned, stream)
-        sums = [swap(mixed[j], "attn", j) for j in even_first(layers)]
+        sums = [swap(mixed[placed.index(j)], "attn", j) for j in even_first(layers)]
         done = [
             pl.pallas_call(
                 add_kernel,

time: 50.3 us -> 51 us (1.014)
  starting transfers between devices: 25 us -> 26.6 us
  waiting for transfers between devices: 11 us -> 10.1 us
    ppermute x24, starting transfers between devices: 25 us -> 26.6 us  [swap(): return lax.ppermute(value, axis, [(i, i ^ step) for i in range(count)])]
    ppermute x24, waiting for transfers between devices: 11 us -> 10.1 us  [swap(): return lax.ppermute(value, axis, [(i, i ^ step) for i in range(count)])]
  transfers between devices with their start and end apart: 24 -> 24, of which waited for: 11 -> 10; matrix products, arithmetic and copies ran while one was open for 0% -> 0% of each run, Pallas kernels for 12% -> 12%
where the time goes in v19:
time: 51 us; the launch traced here: 50.8 us
  starting transfers between devices  26.6 us (52%)
  Pallas kernels  13.8 us (27%)
  waiting for transfers between devices  10.1 us (20%)
    ppermute x24, starting transfers between devices, swap(): return lax.ppermute(value, axis, [(i, i ^ step) for i in range(count)])  26.6 us
    ppermute x24, waiting for transfers between devices, swap(): return lax.ppermute(value, axis, [(i, i ^ step) for i in range(count)])  10.1 us
    pallas_call x1, Pallas kernels, shards(): pl.pallas_call(functools.partial(middle_kernel, experts=experts), in_spec...  4.17 us
    pallas_call x1, Pallas kernels, shards(): pl.pallas_call(attend_kernel, in_specs=[SCALAR] + [ANY] * len(operands),...  3.02 us
    pallas_call x1, Pallas kernels, shards(): pl.pallas_call(functools.partial(begin_kernel, experts=experts), in_specs...  2.92 us
    pallas_call x1, Pallas kernels, shards(): pl.pallas_call(end_kernel, in_specs=[WHOLE] * 2, out_specs=[WHOLE] * expe...  1.37 us
  transfers between devices with their start and end apart: 24, of which 10 were waited for; matrix products, arithmetic and copies ran while one was open for 0% of the time, Pallas kernels for 12%

profile of v19, /device:TPU:0, one launch (start us, length us, event | category | flops | bytes accessed | tf_op | source)
XLA Modules:
  0.0 50.8 jit_solution(15376615456185893122)
XLA Ops:
  0.0 3.0 %shard_map.109 = (f32[16,3072]{1,0:T(8,128)S(1)}, bf16[16,1664]{1,0:T(8,128)(2,1)S(1)}, bf16[16,1536]{1,0:T(8,128)(2,1)S(1)}) custom-call(s32[1]{0:T(128)} %bitcast._.me_ref, s32[1,16]{1,0:T(1,128)} %bitcast.21, bf16[16,3072]{1,0:T(8,128)(2,1)} %queries_hbm.1, bf16[16,96,512]{2,1,0:T(8,128)(2,1)} %keys_hbm.1, bf16[16,96,512]{2,1,0:T(8,128)(2,1)} %values_hbm.1, ...), custom_call_target="tpu_custom_call" | custom-call | tf_op jit(solution)/shard_map/pallas_call | solution.py:386
  3.0 0.0 slice-start
  3.0 0.0 slice-start.3
  3.1 0.0 slice-start.1
  3.1 0.0 slice-start.2
  3.1 0.0 slice-start.4
  3.1 0.0 slice-start.5
  3.1 0.0 copy-start
  3.1 4.1 %collective-permute-start.2 = (bf16[16,1664]{1,0:T(8,128)(2,1)S(1)}, bf16[16,1664]{1,0:T(8,128)(2,1)S(1)}, u32[]{:S(2)}, u32[]{:S(2)}) collective-permute-start(bf16[16,1664]{1,0:T(8,128)(2,1)S(1)} %get-tuple-element.43.refs_0_), channel_id=1, source_target_pairs={{0,8},{4,12},{8,0},{12,4},{1,9},{5,13},{9,1},{13,5},{2,10},{6,14},... | collective-permute-start | bytes 159752 | tf_op jit(solution)/shard_map/ppermute | solution.py:346
  7.2 1.4 %collective-permute-start.1 = (bf16[16,1664]{1,0:T(8,128)(2,1)S(1)}, bf16[16,1664]{1,0:T(8,128)(2,1)S(1)}, u32[]{:S(2)}, u32[]{:S(2)}) collective-permute-start(bf16[16,1664]{1,0:T(8,128)(2,1)S(1)} %get-tuple-element.43.refs_0_), channel_id=1, source_target_pairs={{0,12},{4,8},{8,4},{12,0},{1,13},{5,9},{9,5},{13,1},{2,14},{6,10},... | collective-permute-start | bytes 159752 | tf_op jit(solution)/shard_map/ppermute | solution.py:346
  8.6 0.2 collective-permute-start
  8.8 2.8 %collective-permute-start.5 = (bf16[16,1536]{1,0:T(8,128)(2,1)S(1)}, bf16[16,1536]{1,0:T(8,128)(2,1)S(1)}, u32[]{:S(2)}, u32[]{:S(2)}) collective-permute-start(bf16[16,1536]{1,0:T(8,128)(2,1)S(1)} %get-tuple-element.44.refs_4_), channel_id=1, source_target_pairs={{0,8},{4,12},{8,0},{12,4},{1,9},{5,13},{9,1},{13,5},{2,10},{6,14},... | collective-permute-start | bytes 147464 | tf_op jit(solution)/shard_map/ppermute | solution.py:346
  11.6 1.3 %collective-permute-start.4 = (bf16[16,1536]{1,0:T(8,128)(2,1)S(1)}, bf16[16,1536]{1,0:T(8,128)(2,1)S(1)}, u32[]{:S(2)}, u32[]{:S(2)}) collective-permute-start(bf16[16,1536]{1,0:T(8,128)(2,1)S(1)} %get-tuple-element.44.refs_4_), channel_id=1, source_target_pairs={{0,12},{4,8},{8,4},{12,0},{1,13},{5,9},{9,5},{13,1},{2,14},{6,10},... | collective-permute-start | bytes 147464 | tf_op jit(solution)/shard_map/ppermute | solution.py:346
  13.0 0.0 collective-permute-done.2.refs_3_
  13.0 0.0 collective-permute-start.3
  13.0 0.8 %collective-permute-done.1.refs_2_ = bf16[16,1664]{1,0:T(8,128)(2,1)S(1)} collective-permute-done((bf16[16,1664]{1,0:T(8,128)(2,1)S(1)}, bf16[16,1664]{1,0:T(8,128)(2,1)S(1)}, u32[]{:S(2)}, u32[]{:S(2)}) %collective-permute-start.1) | collective-permute-done | bytes 53280 | tf_op jit(solution)/shard_map/ppermute | solution.py:346
  13.7 0.0 collective-permute-done.refs_1_
  13.7 0.4 shard_map.113
  14.1 1.6 %collective-permute-start.9 = (bf16[32,1536]{1,0:T(8,128)(2,1)S(1)}, bf16[32,1536]{1,0:T(8,128)(2,1)S(1)}, u32[]{:S(2)}, u32[]{:S(2)}) collective-permute-start(bf16[32,1536]{1,0:T(8,128)(2,1)S(1)} %get-tuple-element.52), channel_id=1, source_target_pairs={{0,2},{1,3},{2,0},{3,1},{4,6},{5,7},{6,4},{7,5},{8,10},{9,11},{10,... | collective-permute-start | bytes 294920 | tf_op jit(solution)/shard_map/ppermute | solution.py:346
  15.7 0.0 collective-permute-start.10
  15.7 0.4 collective-permute-done.5.refs_7_
  16.1 0.2 collective-permute-start.11
  16.4 1.2 %collective-permute-done.4.refs_6_ = bf16[16,1536]{1,0:T(8,128)(2,1)S(1)} collective-permute-done((bf16[16,1536]{1,0:T(8,128)(2,1)S(1)}, bf16[16,1536]{1,0:T(8,128)(2,1)S(1)}, u32[]{:S(2)}, u32[]{:S(2)}) %collective-permute-start.4) | collective-permute-done | bytes 49184 | tf_op jit(solution)/shard_map/ppermute | solution.py:346
  17.6 0.0 collective-permute-done.3.refs_5_
  17.6 0.4 shard_map.112
  18.0 1.5 %collective-permute-start.6 = (bf16[32,1536]{1,0:T(8,128)(2,1)S(1)}, bf16[32,1536]{1,0:T(8,128)(2,1)S(1)}, u32[]{:S(2)}, u32[]{:S(2)}) collective-permute-start(bf16[32,1536]{1,0:T(8,128)(2,1)S(1)} %get-tuple-element.48), channel_id=1, source_target_pairs={{0,2},{1,3},{2,0},{3,1},{4,6},{5,7},{6,4},{7,5},{8,10},{9,11},{10,... | collective-permute-start | bytes 294920 | tf_op jit(solution)/shard_map/ppermute | solution.py:346
  19.5 0.0 collective-permute-start.7
  19.5 0.4 shard_map.111
  19.9 0.0 collective-permute-done.9.refs_1_
  19.9 0.7 %collective-permute-start.8 = (bf16[32,1536]{1,0:T(8,128)(2,1)S(1)}, bf16[32,1536]{1,0:T(8,128)(2,1)S(1)}, u32[]{:S(2)}, u32[]{:S(2)}) collective-permute-start(bf16[32,1536]{1,0:T(8,128)(2,1)S(1)} %get-tuple-element.50), channel_id=1, source_target_pairs={{0,1},{1,0},{2,3},{3,2},{4,5},{5,4},{6,7},{7,6},{8,9},{9,8},{10,11... | collective-permute-start | bytes 294920 | tf_op jit(solution)/shard_map/ppermute | solution.py:346
  20.6 0.4 collective-permute-done.10.refs_2_
  21.0 0.0 collective-permute-done.11.refs_3_
  21.1 2.9 %shard_map.114 = (f32[128,2048]{1,0:T(8,128)S(1)}, f32[128,2048]{1,0:T(8,128)S(1)}, bf16[2048,1536]{1,0:T(8,128)(2,1)S(1)}) custom-call(bf16[32,1536]{1,0:T(8,128)(2,1)S(1)} %get-tuple-element.51.refs_0_, bf16[32,1536]{1,0:T(8,128)(2,1)S(1)} %collective-permute-done.9.refs_1_, bf16[32,1536]{1,0:T(8,128)(2,1)S(1)} %collective-permute-done.10.refs_2_, ...), custom_call_target="tpu_custom_call" | custom-call | flops 1610612736 | tf_op jit(solution)/shard_map/pallas_call | solution.py:430
  24.0 0.0 collective-permute-done.6.refs_1_
  24.0 0.6 %collective-permute-done.7.refs_2_ = bf16[32,1536]{1,0:T(8,128)(2,1)S(1)} collective-permute-done((bf16[32,1536]{1,0:T(8,128)(2,1)S(1)}, bf16[32,1536]{1,0:T(8,128)(2,1)S(1)}, u32[]{:S(2)}, u32[]{:S(2)}) %collective-permute-start.7) | collective-permute-done | bytes 98336 | tf_op jit(solution)/shard_map/ppermute | solution.py:346
  24.6 0.0 collective-permute-done.8.refs_3_
  24.6 4.2 %shard_map.115 = (bf16[32,1536]{1,0:T(8,128)(2,1)S(1)}, bf16[32,1536]{1,0:T(8,128)(2,1)S(1)}, bf16[32,1536]{1,0:T(8,128)(2,1)S(1)}, bf16[32,1536]{1,0:T(8,128)(2...) custom-call(bf16[32,1536]{1,0:T(8,128)(2,1)S(1)} %get-tuple-element.47.refs_0_, ...), custom_call_target="tpu_custom_call" | custom-call | tf_op jit(solution)/shard_map/pallas_call | solution.py:441
  28.8 1.0 %collective-permute-start.12 = (bf16[32,1536]{1,0:T(8,128)(2,1)S(1)}, bf16[32,1536]{1,0:T(8,128)(2,1)S(1)}, u32[]{:S(2)}, u32[]{:S(2)}) collective-permute-start(bf16[32,1536]{1,0:T(8,128)(2,1)S(1)} %get-tuple-element.59), channel_id=1, source_target_pairs={{0,2},{1,3},{2,0},{3,1},{4,6},{5,7},{6,4},{7,5},{8,10},{9,11},{10,... | collective-permute-start | bytes 294920 | tf_op jit(solution)/shard_map/ppermute | solution.py:346
  29.8 0.8 %collective-permute-start.13 = (bf16[32,1536]{1,0:T(8,128)(2,1)S(1)}, bf16[32,1536]{1,0:T(8,128)(2,1)S(1)}, u32[]{:S(2)}, u32[]{:S(2)}) collective-permute-start(bf16[32,1536]{1,0:T(8,128)(2,1)S(1)} %get-tuple-element.60), channel_id=1, source_target_pairs={{0,3},{1,2},{2,1},{3,0},{4,7},{5,6},{6,5},{7,4},{8,11},{9,10},{10,... | collective-permute-start | bytes 294920 | tf_op jit(solution)/shard_map/ppermute | solution.py:346
  30.6 0.4 collective-permute-start.14
  31.0 1.4 %shard_map.118 = (bf16[32,1536]{1,0:T(8,128)(2,1)S(1)}, bf16[32,1536]{1,0:T(8,128)(2,1)S(1)}, bf16[32,1536]{1,0:T(8,128)(2,1)S(1)}, bf16[32,1536]{1,0:T(8,128)(2,1)S(1)}) custom-call(bf16[128,2048]{1,0:T(8,128)(2,1)S(1)} %get-tuple-element.67.hidden_ref, bf16[2048,1536]{1,0:T(8,128)(2,1)S(1)} %get-tuple-element.68.down_ref), custom_call_target="tpu_custom_call" | custom-call | flops 805306368 | tf_op jit(solution)/shard_map/pallas_call | solution.py:449
  32.4 1.3 %collective-permute-start.18 = (bf16[32,1536]{1,0:T(8,128)(2,1)S(1)}, bf16[32,1536]{1,0:T(8,128)(2,1)S(1)}, u32[]{:S(2)}, u32[]{:S(2)}) collective-permute-start(bf16[32,1536]{1,0:T(8,128)(2,1)S(1)} %get-tuple-element.70), channel_id=1, source_target_pairs={{0,2},{1,3},{2,0},{3,1},{4,6},{5,7},{6,4},{7,5},{8,10},{9,11},{10,... | collective-permute-start | bytes 294920 | tf_op jit(solution)/shard_map/ppermute | solution.py:346
  33.7 0.2 collective-permute-start.19
  33.9 0.6 %collective-permute-done.12.refs_1_ = bf16[32,1536]{1,0:T(8,128)(2,1)S(1)} collective-permute-done((bf16[32,1536]{1,0:T(8,128)(2,1)S(1)}, bf16[32,1536]{1,0:T(8,128)(2,1)S(1)}, u32[]{:S(2)}, u32[]{:S(2)}) %collective-permute-start.12) | collective-permute-done | bytes 98336 | tf_op jit(solution)/shard_map/ppermute | solution.py:346
  34.5 0.1 collective-permute-start.20
  34.6 0.9 %collective-permute-done.13.refs_2_ = bf16[32,1536]{1,0:T(8,128)(2,1)S(1)} collective-permute-done((bf16[32,1536]{1,0:T(8,128)(2,1)S(1)}, bf16[32,1536]{1,0:T(8,128)(2,1)S(1)}, u32[]{:S(2)}, u32[]{:S(2)}) %collective-permute-start.13) | collective-permute-done | bytes 98336 | tf_op jit(solution)/shard_map/ppermute | solution.py:346
  35.5 0.0 collective-permute-done.14.refs_3_
  35.5 0.3 shard_map.116
  35.7 3.5 %collective-permute-start.15 = (bf16[16,1536]{1,0:T(8,128)(2,1)S(1)}, bf16[16,1536]{1,0:T(8,128)(2,1)S(1)}, u32[]{:S(2)}, u32[]{:S(2)}) collective-permute-start(bf16[16,1536]{1,0:T(8,128)(2,1)S(1)} %get-tuple-element.64), channel_id=1, source_target_pairs={{0,8},{4,12},{8,0},{12,4},{1,9},{5,13},{9,1},{13,5},{2,10},{6,14},... | collective-permute-start | bytes 147464 | tf_op jit(solution)/shard_map/ppermute | solution.py:346
  39.3 0.3 collective-permute-start.16
  39.6 0.0 collective-permute-done.18.refs_1_
  39.6 0.9 %collective-permute-start.17 = (bf16[16,1536]{1,0:T(8,128)(2,1)S(1)}, bf16[16,1536]{1,0:T(8,128)(2,1)S(1)}, u32[]{:S(2)}, u32[]{:S(2)}) collective-permute-start(bf16[16,1536]{1,0:T(8,128)(2,1)S(1)} %get-tuple-element.66), channel_id=1, source_target_pairs={{0,4},{4,0},{8,12},{12,8},{1,5},{5,1},{9,13},{13,9},{2,6},{6,2},{1... | collective-permute-start | bytes 147464 | tf_op jit(solution)/shard_map/ppermute | solution.py:346
  40.5 0.0 collective-permute-done.19.refs_2_
  40.5 0.0 collective-permute-done.20.refs_3_
  40.5 0.3 shard_map.119
  40.8 3.2 %collective-permute-start.21 = (bf16[16,1536]{1,0:T(8,128)(2,1)S(1)}, bf16[16,1536]{1,0:T(8,128)(2,1)S(1)}, u32[]{:S(2)}, u32[]{:S(2)}) collective-permute-start(bf16[16,1536]{1,0:T(8,128)(2,1)S(1)} %get-tuple-element.74), channel_id=1, source_target_pairs={{0,8},{4,12},{8,0},{12,4},{1,9},{5,13},{9,1},{13,5},{2,10},{6,14},... | collective-permute-start | bytes 147464 | tf_op jit(solution)/shard_map/ppermute | solution.py:346
  44.0 0.4 collective-permute-start.22
  44.4 0.0 collective-permute-done.15.refs_1_
  44.4 0.5 collective-permute-start.23
  44.9 0.7 %collective-permute-done.16.refs_2_ = bf16[16,1536]{1,0:T(8,128)(2,1)S(1)} collective-permute-done((bf16[16,1536]{1,0:T(8,128)(2,1)S(1)}, bf16[16,1536]{1,0:T(8,128)(2,1)S(1)}, u32[]{:S(2)}, u32[]{:S(2)}) %collective-permute-start.16) | collective-permute-done | bytes 49184 | tf_op jit(solution)/shard_map/ppermute | solution.py:346
  45.6 1.2 %collective-permute-done.21.refs_2_ = bf16[16,1536]{1,0:T(8,128)(2,1)S(1)} collective-permute-done((bf16[16,1536]{1,0:T(8,128)(2,1)S(1)}, bf16[16,1536]{1,0:T(8,128)(2,1)S(1)}, u32[]{:S(2)}, u32[]{:S(2)}) %collective-permute-start.21) | collective-permute-done | bytes 49184 | tf_op jit(solution)/shard_map/ppermute | solution.py:346
  46.8 3.3 %collective-permute-done.22.refs_3_ = bf16[16,1536]{1,0:T(8,128)(2,1)S(1)} collective-permute-done((bf16[16,1536]{1,0:T(8,128)(2,1)S(1)}, bf16[16,1536]{1,0:T(8,128)(2,1)S(1)}, u32[]{:S(2)}, u32[]{:S(2)}) %collective-permute-start.22) | collective-permute-done | bytes 49184 | tf_op jit(solution)/shard_map/ppermute | solution.py:346
  50.2 0.0 collective-permute-done.23.refs_4_
  50.2 0.7 %shard_map.120 = bf16[16,3072]{1,0:T(8,128)(2,1)} custom-call(bf16[16,1536]{1,0:T(8,128)(2,1)S(1)} %shard_map.117.refs_0_, f32[16,1536]{1,0:T(8,128)S(1)} %get-tuple-element.73.refs_1_, bf16[16,1536]{1,0:T(8,128)(2,1)S(1)} %collective-permute-done.21.refs_2_, bf16[16,1536]{1,0:T(8,128)(2,1)S(1)} %collective-permute-done.22.refs_3_, ...), custom_call_target="tpu_custom_call" | custom-call | tf_op jit(solution)/shard_map/pallas_call | solution.py:473
  (12 shorter events, 0.0 us)
Async XLA Ops:
  3.0 18.0 %slice-start = ((s8[12582912]{0:T(1024)(128)(4,1)}), s8[4194304]{0:T(1024)(128)(4,1)S(1)}, s32[]{:S(2)}) async-start(s8[12582912]{0:T(1024)(128)(4,1)} %bitcast.8), calls=%async_computation | async-start | bytes 8388608
  3.0 18.0 %slice-start.3 = ((s8[12582912]{0:T(1024)(128)(4,1)}), s8[4194304]{0:T(1024)(128)(4,1)S(1)}, s32[]{:S(2)}) async-start(s8[12582912]{0:T(1024)(128)(4,1)} %bitcast.12), calls=%async_computation.3 | async-start | bytes 8388608
  3.1 17.9 %slice-start.1 = ((s8[12582912]{0:T(1024)(128)(4,1)}), s8[4194304]{0:T(1024)(128)(4,1)S(1)}, s32[]{:S(2)}) async-start(s8[12582912]{0:T(1024)(128)(4,1)} %bitcast.8), calls=%async_computation.1 | async-start | bytes 8388608
  3.1 17.9 %slice-start.2 = ((s8[12582912]{0:T(1024)(128)(4,1)}), s8[4194304]{0:T(1024)(128)(4,1)S(1)}, s32[]{:S(2)}) async-start(s8[12582912]{0:T(1024)(128)(4,1)} %bitcast.8), calls=%async_computation.2 | async-start | bytes 8388608
  3.1 17.9 %slice-start.4 = ((s8[12582912]{0:T(1024)(128)(4,1)}), s8[4194304]{0:T(1024)(128)(4,1)S(1)}, s32[]{:S(2)}) async-start(s8[12582912]{0:T(1024)(128)(4,1)} %bitcast.12), calls=%async_computation.4 | async-start | bytes 8388608
  3.1 17.9 %slice-start.5 = ((s8[12582912]{0:T(1024)(128)(4,1)}), s8[4194304]{0:T(1024)(128)(4,1)S(1)}, s32[]{:S(2)}) async-start(s8[12582912]{0:T(1024)(128)(4,1)} %bitcast.12), calls=%async_computation.5 | async-start | bytes 8388608
  3.1 16.4 %copy-start = (bf16[3072,4]{0,1:T(4,128)(2,1)S(1)}, bf16[3072,4]{0,1:T(4,128)(2,1)}, u32[]{:S(2)}) copy-start(bf16[3072,4]{0,1:T(4,128)(2,1)} %param.18) | copy-start | bytes 73732
  3.1 9.8 %collective-permute-start.2 = (bf16[16,1664]{1,0:T(8,128)(2,1)S(1)}, bf16[16,1664]{1,0:T(8,128)(2,1)S(1)}, u32[]{:S(2)}, u32[]{:S(2)}) collective-permute-start(bf16[16,1664]{1,0:T(8,128)(2,1)S(1)} %get-tuple-element.43.refs_0_), channel_id=1, source_target_pairs={{0,8},{4,12},{8,0},{12,4},{1,9},{5,13},{9,1},{13,5},{2,10},{6,14},... | collective-permute-start | bytes 159752 | tf_op jit(solution)/shard_map/ppermute | solution.py:346
  7.2 6.5 %collective-permute-start.1 = (bf16[16,1664]{1,0:T(8,128)(2,1)S(1)}, bf16[16,1664]{1,0:T(8,128)(2,1)S(1)}, u32[]{:S(2)}, u32[]{:S(2)}) collective-permute-start(bf16[16,1664]{1,0:T(8,128)(2,1)S(1)} %get-tuple-element.43.refs_0_), channel_id=1, source_target_pairs={{0,12},{4,8},{8,4},{12,0},{1,13},{5,9},{9,5},{13,1},{2,14},{6,10},... | collective-permute-start | bytes 159752 | tf_op jit(solution)/shard_map/ppermute | solution.py:346
  8.6 5.2 %collective-permute-start = (bf16[16,1664]{1,0:T(8,128)(2,1)S(1)}, bf16[16,1664]{1,0:T(8,128)(2,1)S(1)}, u32[]{:S(2)}, u32[]{:S(2)}) collective-permute-start(bf16[16,1664]{1,0:T(8,128)(2,1)S(1)} %get-tuple-element.43.refs_0_), channel_id=1, source_target_pairs={{0,4},{4,0},{8,12},{12,8},{1,5},{5,1},{9,13},{13,9},{2,6},{6,2},{1... | collective-permute-start | bytes 159752 | tf_op jit(solution)/shard_map/ppermute | solution.py:346
  8.8 7.3 %collective-permute-start.5 = (bf16[16,1536]{1,0:T(8,128)(2,1)S(1)}, bf16[16,1536]{1,0:T(8,128)(2,1)S(1)}, u32[]{:S(2)}, u32[]{:S(2)}) collective-permute-start(bf16[16,1536]{1,0:T(8,128)(2,1)S(1)} %get-tuple-element.44.refs_4_), channel_id=1, source_target_pairs={{0,8},{4,12},{8,0},{12,4},{1,9},{5,13},{9,1},{13,5},{2,10},{6,14},... | collective-permute-start | bytes 147464 | tf_op jit(solution)/shard_map/ppermute | solution.py:346
  11.6 6.0 %collective-permute-start.4 = (bf16[16,1536]{1,0:T(8,128)(2,1)S(1)}, bf16[16,1536]{1,0:T(8,128)(2,1)S(1)}, u32[]{:S(2)}, u32[]{:S(2)}) collective-permute-start(bf16[16,1536]{1,0:T(8,128)(2,1)S(1)} %get-tuple-element.44.refs_4_), channel_id=1, source_target_pairs={{0,12},{4,8},{8,4},{12,0},{1,13},{5,9},{9,5},{13,1},{2,14},{6,10},... | collective-permute-start | bytes 147464 | tf_op jit(solution)/shard_map/ppermute | solution.py:346
  13.0 4.6 %collective-permute-start.3 = (bf16[16,1536]{1,0:T(8,128)(2,1)S(1)}, bf16[16,1536]{1,0:T(8,128)(2,1)S(1)}, u32[]{:S(2)}, u32[]{:S(2)}) collective-permute-start(bf16[16,1536]{1,0:T(8,128)(2,1)S(1)} %get-tuple-element.44.refs_4_), channel_id=1, source_target_pairs={{0,4},{4,0},{8,12},{12,8},{1,5},{5,1},{9,13},{13,9},{2,6},{6,2},{1... | collective-permute-start | bytes 147464 | tf_op jit(solution)/shard_map/ppermute | solution.py:346
  14.1 5.8 %collective-permute-start.9 = (bf16[32,1536]{1,0:T(8,128)(2,1)S(1)}, bf16[32,1536]{1,0:T(8,128)(2,1)S(1)}, u32[]{:S(2)}, u32[]{:S(2)}) collective-permute-start(bf16[32,1536]{1,0:T(8,128)(2,1)S(1)} %get-tuple-element.52), channel_id=1, source_target_pairs={{0,2},{1,3},{2,0},{3,1},{4,6},{5,7},{6,4},{7,5},{8,10},{9,11},{10,... | collective-permute-start | bytes 294920 | tf_op jit(solution)/shard_map/ppermute | solution.py:346
  15.7 5.3 %collective-permute-start.10 = (bf16[32,1536]{1,0:T(8,128)(2,1)S(1)}, bf16[32,1536]{1,0:T(8,128)(2,1)S(1)}, u32[]{:S(2)}, u32[]{:S(2)}) collective-permute-start(bf16[32,1536]{1,0:T(8,128)(2,1)S(1)} %get-tuple-element.53), channel_id=1, source_target_pairs={{0,3},{1,2},{2,1},{3,0},{4,7},{5,6},{6,5},{7,4},{8,11},{9,10},{10,... | collective-permute-start | bytes 294920 | tf_op jit(solution)/shard_map/ppermute | solution.py:346
  16.1 4.9 %collective-permute-start.11 = (bf16[32,1536]{1,0:T(8,128)(2,1)S(1)}, bf16[32,1536]{1,0:T(8,128)(2,1)S(1)}, u32[]{:S(2)}, u32[]{:S(2)}) collective-permute-start(bf16[32,1536]{1,0:T(8,128)(2,1)S(1)} %get-tuple-element.54), channel_id=1, source_target_pairs={{0,1},{1,0},{2,3},{3,2},{4,5},{5,4},{6,7},{7,6},{8,9},{9,8},{10,11... | collective-permute-start | bytes 294920 | tf_op jit(solution)/shard_map/ppermute | solution.py:346
  18.0 6.0 %collective-permute-start.6 = (bf16[32,1536]{1,0:T(8,128)(2,1)S(1)}, bf16[32,1536]{1,0:T(8,128)(2,1)S(1)}, u32[]{:S(2)}, u32[]{:S(2)}) collective-permute-start(bf16[32,1536]{1,0:T(8,128)(2,1)S(1)} %get-tuple-element.48), channel_id=1, source_target_pairs={{0,2},{1,3},{2,0},{3,1},{4,6},{5,7},{6,4},{7,5},{8,10},{9,11},{10,... | collective-permute-start | bytes 294920 | tf_op jit(solution)/shard_map/ppermute | solution.py:346
  19.5 5.1 %collective-permute-start.7 = (bf16[32,1536]{1,0:T(8,128)(2,1)S(1)}, bf16[32,1536]{1,0:T(8,128)(2,1)S(1)}, u32[]{:S(2)}, u32[]{:S(2)}) collective-permute-start(bf16[32,1536]{1,0:T(8,128)(2,1)S(1)} %get-tuple-element.49), channel_id=1, source_target_pairs={{0,3},{1,2},{2,1},{3,0},{4,7},{5,6},{6,5},{7,4},{8,11},{9,10},{10,... | collective-permute-start | bytes 294920 | tf_op jit(solution)/shard_map/ppermute | solution.py:346
  19.9 4.7 %collective-permute-start.8 = (bf16[32,1536]{1,0:T(8,128)(2,1)S(1)}, bf16[32,1536]{1,0:T(8,128)(2,1)S(1)}, u32[]{:S(2)}, u32[]{:S(2)}) collective-permute-start(bf16[32,1536]{1,0:T(8,128)(2,1)S(1)} %get-tuple-element.50), channel_id=1, source_target_pairs={{0,1},{1,0},{2,3},{3,2},{4,5},{5,4},{6,7},{7,6},{8,9},{9,8},{10,11... | collective-permute-start | bytes 294920 | tf_op jit(solution)/shard_map/ppermute | solution.py:346
  28.8 5.7 %collective-permute-start.12 = (bf16[32,1536]{1,0:T(8,128)(2,1)S(1)}, bf16[32,1536]{1,0:T(8,128)(2,1)S(1)}, u32[]{:S(2)}, u32[]{:S(2)}) collective-permute-start(bf16[32,1536]{1,0:T(8,128)(2,1)S(1)} %get-tuple-element.59), channel_id=1, source_target_pairs={{0,2},{1,3},{2,0},{3,1},{4,6},{5,7},{6,4},{7,5},{8,10},{9,11},{10,... | collective-permute-start | bytes 294920 | tf_op jit(solution)/shard_map/ppermute | solution.py:346
  29.8 5.7 %collective-permute-start.13 = (bf16[32,1536]{1,0:T(8,128)(2,1)S(1)}, bf16[32,1536]{1,0:T(8,128)(2,1)S(1)}, u32[]{:S(2)}, u32[]{:S(2)}) collective-permute-start(bf16[32,1536]{1,0:T(8,128)(2,1)S(1)} %get-tuple-element.60), channel_id=1, source_target_pairs={{0,3},{1,2},{2,1},{3,0},{4,7},{5,6},{6,5},{7,4},{8,11},{9,10},{10,... | collective-permute-start | bytes 294920 | tf_op jit(solution)/shard_map/ppermute | solution.py:346
  30.6 4.9 %collective-permute-start.14 = (bf16[32,1536]{1,0:T(8,128)(2,1)S(1)}, bf16[32,1536]{1,0:T(8,128)(2,1)S(1)}, u32[]{:S(2)}, u32[]{:S(2)}) collective-permute-start(bf16[32,1536]{1,0:T(8,128)(2,1)S(1)} %get-tuple-element.61), channel_id=1, source_target_pairs={{0,1},{1,0},{2,3},{3,2},{4,5},{5,4},{6,7},{7,6},{8,9},{9,8},{10,11... | collective-permute-start | bytes 294920 | tf_op jit(solution)/shard_map/ppermute | solution.py:346
  32.4 7.2 %collective-permute-start.18 = (bf16[32,1536]{1,0:T(8,128)(2,1)S(1)}, bf16[32,1536]{1,0:T(8,128)(2,1)S(1)}, u32[]{:S(2)}, u32[]{:S(2)}) collective-permute-start(bf16[32,1536]{1,0:T(8,128)(2,1)S(1)} %get-tuple-element.70), channel_id=1, source_target_pairs={{0,2},{1,3},{2,0},{3,1},{4,6},{5,7},{6,4},{7,5},{8,10},{9,11},{10,... | collective-permute-start | bytes 294920 | tf_op jit(solution)/shard_map/ppermute | solution.py:346
  33.7 6.8 %collective-permute-start.19 = (bf16[32,1536]{1,0:T(8,128)(2,1)S(1)}, bf16[32,1536]{1,0:T(8,128)(2,1)S(1)}, u32[]{:S(2)}, u32[]{:S(2)}) collective-permute-start(bf16[32,1536]{1,0:T(8,128)(2,1)S(1)} %get-tuple-element.71), channel_id=1, source_target_pairs={{0,3},{1,2},{2,1},{3,0},{4,7},{5,6},{6,5},{7,4},{8,11},{9,10},{10,... | collective-permute-start | bytes 294920 | tf_op jit(solution)/shard_map/ppermute | solution.py:346
  34.5 6.0 %collective-permute-start.20 = (bf16[32,1536]{1,0:T(8,128)(2,1)S(1)}, bf16[32,1536]{1,0:T(8,128)(2,1)S(1)}, u32[]{:S(2)}, u32[]{:S(2)}) collective-permute-start(bf16[32,1536]{1,0:T(8,128)(2,1)S(1)} %get-tuple-element.72), channel_id=1, source_target_pairs={{0,1},{1,0},{2,3},{3,2},{4,5},{5,4},{6,7},{7,6},{8,9},{9,8},{10,11... | collective-permute-start | bytes 294920 | tf_op jit(solution)/shard_map/ppermute | solution.py:346
  35.7 8.7 %collective-permute-start.15 = (bf16[16,1536]{1,0:T(8,128)(2,1)S(1)}, bf16[16,1536]{1,0:T(8,128)(2,1)S(1)}, u32[]{:S(2)}, u32[]{:S(2)}) collective-permute-start(bf16[16,1536]{1,0:T(8,128)(2,1)S(1)} %get-tuple-element.64), channel_id=1, source_target_pairs={{0,8},{4,12},{8,0},{12,4},{1,9},{5,13},{9,1},{13,5},{2,10},{6,14},... | collective-permute-start | bytes 147464 | tf_op jit(solution)/shard_map/ppermute | solution.py:346
  39.3 6.4 %collective-permute-start.16 = (bf16[16,1536]{1,0:T(8,128)(2,1)S(1)}, bf16[16,1536]{1,0:T(8,128)(2,1)S(1)}, u32[]{:S(2)}, u32[]{:S(2)}) collective-permute-start(bf16[16,1536]{1,0:T(8,128)(2,1)S(1)} %get-tuple-element.65), channel_id=1, source_target_pairs={{0,12},{4,8},{8,4},{12,0},{1,13},{5,9},{9,5},{13,1},{2,14},{6,10},... | collective-permute-start | bytes 147464 | tf_op jit(solution)/shard_map/ppermute | solution.py:346
  39.6 6.0 %collective-permute-start.17 = (bf16[16,1536]{1,0:T(8,128)(2,1)S(1)}, bf16[16,1536]{1,0:T(8,128)(2,1)S(1)}, u32[]{:S(2)}, u32[]{:S(2)}) collective-permute-start(bf16[16,1536]{1,0:T(8,128)(2,1)S(1)} %get-tuple-element.66), channel_id=1, source_target_pairs={{0,4},{4,0},{8,12},{12,8},{1,5},{5,1},{9,13},{13,9},{2,6},{6,2},{1... | collective-permute-start | bytes 147464 | tf_op jit(solution)/shard_map/ppermute | solution.py:346
  40.8 6.1 %collective-permute-start.21 = (bf16[16,1536]{1,0:T(8,128)(2,1)S(1)}, bf16[16,1536]{1,0:T(8,128)(2,1)S(1)}, u32[]{:S(2)}, u32[]{:S(2)}) collective-permute-start(bf16[16,1536]{1,0:T(8,128)(2,1)S(1)} %get-tuple-element.74), channel_id=1, source_target_pairs={{0,8},{4,12},{8,0},{12,4},{1,9},{5,13},{9,1},{13,5},{2,10},{6,14},... | collective-permute-start | bytes 147464 | tf_op jit(solution)/shard_map/ppermute | solution.py:346
  44.0 6.2 %collective-permute-start.22 = (bf16[16,1536]{1,0:T(8,128)(2,1)S(1)}, bf16[16,1536]{1,0:T(8,128)(2,1)S(1)}, u32[]{:S(2)}, u32[]{:S(2)}) collective-permute-start(bf16[16,1536]{1,0:T(8,128)(2,1)S(1)} %get-tuple-element.75), channel_id=1, source_target_pairs={{0,12},{4,8},{8,4},{12,0},{1,13},{5,9},{9,5},{13,1},{2,14},{6,10},... | collective-permute-start | bytes 147464 | tf_op jit(solution)/shard_map/ppermute | solution.py:346
  44.4 5.7 %collective-permute-start.23 = (bf16[16,1536]{1,0:T(8,128)(2,1)S(1)}, bf16[16,1536]{1,0:T(8,128)(2,1)S(1)}, u32[]{:S(2)}, u32[]{:S(2)}) collective-permute-start(bf16[16,1536]{1,0:T(8,128)(2,1)S(1)} %get-tuple-element.76), channel_id=1, source_target_pairs={{0,4},{4,0},{8,12},{12,8},{1,5},{5,1},{9,13},{13,9},{2,6},{6,2},{1... | collective-permute-start | bytes 147464 | tf_op jit(solution)/shard_map/ppermute | solution.py:346

commit v20 on v19

--- a/solution.py
+++ b/solution.py
@@ -468,7 +468,7 @@
             cost_estimate=LIGHT,
             compiler_params=params(experts * layers * CAP * half),
         )(*gates, *returned, stream)
-        sums = [swap(mixed[placed.index(j)], "attn", j) for j in even_first(layers)]
+        sums = [swap(mixed[placed.index(j)], "attn", j) for j in [0, *range(layers - 1, 0, -1)]]
         done = [
             pl.pallas_call(
                 add_kernel,

time: 51 us -> 50.3 us (0.986)
  waiting for transfers between devices: 10.1 us -> 9.06 us
    ppermute x24, waiting for transfers between devices: 10.1 us -> 9.06 us  [swap(): return lax.ppermute(value, axis, [(i, i ^ step) for i in range(count)])]
  transfers between devices with their start and end apart: 24 -> 24, of which waited for: 10 -> 9; matrix products, arithmetic and copies ran while one was open for 0% -> 0% of each run, Pallas kernels for 12% -> 12%
where the time goes in v20:
time: 50.3 us; the launch traced here: 50.1 us
  starting transfers between devices  27 us (54%)
  Pallas kernels  13.8 us (27%)
  waiting for transfers between devices  9.06 us (18%)
    ppermute x24, starting transfers between devices, swap(): return lax.ppermute(value, axis, [(i, i ^ step) for i in range(count)])  27 us
    ppermute x24, waiting for transfers between devices, swap(): return lax.ppermute(value, axis, [(i, i ^ step) for i in range(count)])  9.06 us
    pallas_call x1, Pallas kernels, shards(): pl.pallas_call(functools.partial(middle_kernel, experts=experts), in_spec...  4.17 us
    pallas_call x1, Pallas kernels, shards(): pl.pallas_call(attend_kernel, in_specs=[SCALAR] + [ANY] * len(operands),...  3.02 us
    pallas_call x1, Pallas kernels, shards(): pl.pallas_call(functools.partial(begin_kernel, experts=experts), in_specs...  2.92 us
    pallas_call x1, Pallas kernels, shards(): pl.pallas_call(end_kernel, in_specs=[WHOLE] * 2, out_specs=[WHOLE] * expe...  1.37 us
  transfers between devices with their start and end apart: 24, of which 9 were waited for; matrix products, arithmetic and copies ran while one was open for 0% of the time, Pallas kernels for 12%

profile of v20, /device:TPU:0, one launch (start us, length us, event | category | flops | bytes accessed | tf_op | source)
XLA Modules:
  0.0 50.1 jit_solution(5729207793381909665)
XLA Ops:
  0.0 3.0 %shard_map.109 = (f32[16,3072]{1,0:T(8,128)S(1)}, bf16[16,1664]{1,0:T(8,128)(2,1)S(1)}, bf16[16,1536]{1,0:T(8,128)(2,1)S(1)}) custom-call(s32[1]{0:T(128)} %bitcast._.me_ref, s32[1,16]{1,0:T(1,128)} %bitcast.21, bf16[16,3072]{1,0:T(8,128)(2,1)} %queries_hbm.1, bf16[16,96,512]{2,1,0:T(8,128)(2,1)} %keys_hbm.1, bf16[16,96,512]{2,1,0:T(8,128)(2,1)} %values_hbm.1, ...), custom_call_target="tpu_custom_call" | custom-call | tf_op jit(solution)/shard_map/pallas_call | solution.py:386
  3.0 0.0 slice-start
  3.0 0.0 slice-start.3
  3.1 0.0 slice-start.1
  3.1 0.0 slice-start.2
  3.1 0.0 slice-start.4
  3.1 0.0 slice-start.5
  3.1 0.0 copy-start
  3.1 4.1 %collective-permute-start.2 = (bf16[16,1664]{1,0:T(8,128)(2,1)S(1)}, bf16[16,1664]{1,0:T(8,128)(2,1)S(1)}, u32[]{:S(2)}, u32[]{:S(2)}) collective-permute-start(bf16[16,1664]{1,0:T(8,128)(2,1)S(1)} %get-tuple-element.43.refs_0_), channel_id=1, source_target_pairs={{0,8},{4,12},{8,0},{12,4},{1,9},{5,13},{9,1},{13,5},{2,10},{6,14},... | collective-permute-start | bytes 159752 | tf_op jit(solution)/shard_map/ppermute | solution.py:346
  7.2 1.4 %collective-permute-start.1 = (bf16[16,1664]{1,0:T(8,128)(2,1)S(1)}, bf16[16,1664]{1,0:T(8,128)(2,1)S(1)}, u32[]{:S(2)}, u32[]{:S(2)}) collective-permute-start(bf16[16,1664]{1,0:T(8,128)(2,1)S(1)} %get-tuple-element.43.refs_0_), channel_id=1, source_target_pairs={{0,12},{4,8},{8,4},{12,0},{1,13},{5,9},{9,5},{13,1},{2,14},{6,10},... | collective-permute-start | bytes 159752 | tf_op jit(solution)/shard_map/ppermute | solution.py:346
  8.6 0.2 collective-permute-start
  8.8 2.8 %collective-permute-start.5 = (bf16[16,1536]{1,0:T(8,128)(2,1)S(1)}, bf16[16,1536]{1,0:T(8,128)(2,1)S(1)}, u32[]{:S(2)}, u32[]{:S(2)}) collective-permute-start(bf16[16,1536]{1,0:T(8,128)(2,1)S(1)} %get-tuple-element.44.refs_4_), channel_id=1, source_target_pairs={{0,8},{4,12},{8,0},{12,4},{1,9},{5,13},{9,1},{13,5},{2,10},{6,14},... | collective-permute-start | bytes 147464 | tf_op jit(solution)/shard_map/ppermute | solution.py:346
  11.6 1.3 %collective-permute-start.4 = (bf16[16,1536]{1,0:T(8,128)(2,1)S(1)}, bf16[16,1536]{1,0:T(8,128)(2,1)S(1)}, u32[]{:S(2)}, u32[]{:S(2)}) collective-permute-start(bf16[16,1536]{1,0:T(8,128)(2,1)S(1)} %get-tuple-element.44.refs_4_), channel_id=1, source_target_pairs={{0,12},{4,8},{8,4},{12,0},{1,13},{5,9},{9,5},{13,1},{2,14},{6,10},... | collective-permute-start | bytes 147464 | tf_op jit(solution)/shard_map/ppermute | solution.py:346
  13.0 0.0 collective-permute-done.2.refs_3_
  13.0 0.0 collective-permute-start.3
  13.0 0.8 %collective-permute-done.1.refs_2_ = bf16[16,1664]{1,0:T(8,128)(2,1)S(1)} collective-permute-done((bf16[16,1664]{1,0:T(8,128)(2,1)S(1)}, bf16[16,1664]{1,0:T(8,128)(2,1)S(1)}, u32[]{:S(2)}, u32[]{:S(2)}) %collective-permute-start.1) | collective-permute-done | bytes 53280 | tf_op jit(solution)/shard_map/ppermute | solution.py:346
  13.7 0.0 collective-permute-done.refs_1_
  13.7 0.4 shard_map.113
  14.1 1.6 %collective-permute-start.9 = (bf16[32,1536]{1,0:T(8,128)(2,1)S(1)}, bf16[32,1536]{1,0:T(8,128)(2,1)S(1)}, u32[]{:S(2)}, u32[]{:S(2)}) collective-permute-start(bf16[32,1536]{1,0:T(8,128)(2,1)S(1)} %get-tuple-element.52), channel_id=1, source_target_pairs={{0,2},{1,3},{2,0},{3,1},{4,6},{5,7},{6,4},{7,5},{8,10},{9,11},{10,... | collective-permute-start | bytes 294920 | tf_op jit(solution)/shard_map/ppermute | solution.py:346
  15.7 0.0 collective-permute-start.10
  15.7 0.4 collective-permute-done.5.refs_7_
  16.1 0.2 collective-permute-start.11
  16.4 1.2 %collective-permute-done.4.refs_6_ = bf16[16,1536]{1,0:T(8,128)(2,1)S(1)} collective-permute-done((bf16[16,1536]{1,0:T(8,128)(2,1)S(1)}, bf16[16,1536]{1,0:T(8,128)(2,1)S(1)}, u32[]{:S(2)}, u32[]{:S(2)}) %collective-permute-start.4) | collective-permute-done | bytes 49184 | tf_op jit(solution)/shard_map/ppermute | solution.py:346
  17.6 0.0 collective-permute-done.3.refs_5_
  17.6 0.4 shard_map.112
  18.0 1.5 %collective-permute-start.6 = (bf16[32,1536]{1,0:T(8,128)(2,1)S(1)}, bf16[32,1536]{1,0:T(8,128)(2,1)S(1)}, u32[]{:S(2)}, u32[]{:S(2)}) collective-permute-start(bf16[32,1536]{1,0:T(8,128)(2,1)S(1)} %get-tuple-element.48), channel_id=1, source_target_pairs={{0,2},{1,3},{2,0},{3,1},{4,6},{5,7},{6,4},{7,5},{8,10},{9,11},{10,... | collective-permute-start | bytes 294920 | tf_op jit(solution)/shard_map/ppermute | solution.py:346
  19.5 0.0 collective-permute-start.7
  19.5 0.4 shard_map.111
  19.9 0.0 collective-permute-done.9.refs_1_
  19.9 0.7 %collective-permute-start.8 = (bf16[32,1536]{1,0:T(8,128)(2,1)S(1)}, bf16[32,1536]{1,0:T(8,128)(2,1)S(1)}, u32[]{:S(2)}, u32[]{:S(2)}) collective-permute-start(bf16[32,1536]{1,0:T(8,128)(2,1)S(1)} %get-tuple-element.50), channel_id=1, source_target_pairs={{0,1},{1,0},{2,3},{3,2},{4,5},{5,4},{6,7},{7,6},{8,9},{9,8},{10,11... | collective-permute-start | bytes 294920 | tf_op jit(solution)/shard_map/ppermute | solution.py:346
  20.6 0.4 collective-permute-done.10.refs_2_
  21.0 0.0 collective-permute-done.11.refs_3_
  21.1 2.9 %shard_map.114 = (f32[128,2048]{1,0:T(8,128)S(1)}, f32[128,2048]{1,0:T(8,128)S(1)}, bf16[2048,1536]{1,0:T(8,128)(2,1)S(1)}) custom-call(bf16[32,1536]{1,0:T(8,128)(2,1)S(1)} %get-tuple-element.51.refs_0_, bf16[32,1536]{1,0:T(8,128)(2,1)S(1)} %collective-permute-done.9.refs_1_, bf16[32,1536]{1,0:T(8,128)(2,1)S(1)} %collective-permute-done.10.refs_2_, ...), custom_call_target="tpu_custom_call" | custom-call | flops 1610612736 | tf_op jit(solution)/shard_map/pallas_call | solution.py:430
  24.0 0.0 collective-permute-done.6.refs_1_
  24.0 0.6 %collective-permute-done.7.refs_2_ = bf16[32,1536]{1,0:T(8,128)(2,1)S(1)} collective-permute-done((bf16[32,1536]{1,0:T(8,128)(2,1)S(1)}, bf16[32,1536]{1,0:T(8,128)(2,1)S(1)}, u32[]{:S(2)}, u32[]{:S(2)}) %collective-permute-start.7) | collective-permute-done | bytes 98336 | tf_op jit(solution)/shard_map/ppermute | solution.py:346
  24.6 0.0 collective-permute-done.8.refs_3_
  24.6 4.2 %shard_map.115 = (bf16[32,1536]{1,0:T(8,128)(2,1)S(1)}, bf16[32,1536]{1,0:T(8,128)(2,1)S(1)}, bf16[32,1536]{1,0:T(8,128)(2,1)S(1)}, bf16[32,1536]{1,0:T(8,128)(2...) custom-call(bf16[32,1536]{1,0:T(8,128)(2,1)S(1)} %get-tuple-element.47.refs_0_, ...), custom_call_target="tpu_custom_call" | custom-call | tf_op jit(solution)/shard_map/pallas_call | solution.py:441
  28.8 1.0 %collective-permute-start.12 = (bf16[32,1536]{1,0:T(8,128)(2,1)S(1)}, bf16[32,1536]{1,0:T(8,128)(2,1)S(1)}, u32[]{:S(2)}, u32[]{:S(2)}) collective-permute-start(bf16[32,1536]{1,0:T(8,128)(2,1)S(1)} %get-tuple-element.59), channel_id=1, source_target_pairs={{0,2},{1,3},{2,0},{3,1},{4,6},{5,7},{6,4},{7,5},{8,10},{9,11},{10,... | collective-permute-start | bytes 294920 | tf_op jit(solution)/shard_map/ppermute | solution.py:346
  29.8 0.8 %collective-permute-start.13 = (bf16[32,1536]{1,0:T(8,128)(2,1)S(1)}, bf16[32,1536]{1,0:T(8,128)(2,1)S(1)}, u32[]{:S(2)}, u32[]{:S(2)}) collective-permute-start(bf16[32,1536]{1,0:T(8,128)(2,1)S(1)} %get-tuple-element.60), channel_id=1, source_target_pairs={{0,3},{1,2},{2,1},{3,0},{4,7},{5,6},{6,5},{7,4},{8,11},{9,10},{10,... | collective-permute-start | bytes 294920 | tf_op jit(solution)/shard_map/ppermute | solution.py:346
  30.6 0.4 collective-permute-start.14
  31.0 1.4 %shard_map.118 = (bf16[32,1536]{1,0:T(8,128)(2,1)S(1)}, bf16[32,1536]{1,0:T(8,128)(2,1)S(1)}, bf16[32,1536]{1,0:T(8,128)(2,1)S(1)}, bf16[32,1536]{1,0:T(8,128)(2,1)S(1)}) custom-call(bf16[128,2048]{1,0:T(8,128)(2,1)S(1)} %get-tuple-element.67.hidden_ref, bf16[2048,1536]{1,0:T(8,128)(2,1)S(1)} %get-tuple-element.68.down_ref), custom_call_target="tpu_custom_call" | custom-call | flops 805306368 | tf_op jit(solution)/shard_map/pallas_call | solution.py:449
  32.4 1.3 %collective-permute-start.18 = (bf16[32,1536]{1,0:T(8,128)(2,1)S(1)}, bf16[32,1536]{1,0:T(8,128)(2,1)S(1)}, u32[]{:S(2)}, u32[]{:S(2)}) collective-permute-start(bf16[32,1536]{1,0:T(8,128)(2,1)S(1)} %get-tuple-element.70), channel_id=1, source_target_pairs={{0,2},{1,3},{2,0},{3,1},{4,6},{5,7},{6,4},{7,5},{8,10},{9,11},{10,... | collective-permute-start | bytes 294920 | tf_op jit(solution)/shard_map/ppermute | solution.py:346
  33.7 0.2 collective-permute-start.19
  33.9 0.6 %collective-permute-done.12.refs_1_ = bf16[32,1536]{1,0:T(8,128)(2,1)S(1)} collective-permute-done((bf16[32,1536]{1,0:T(8,128)(2,1)S(1)}, bf16[32,1536]{1,0:T(8,128)(2,1)S(1)}, u32[]{:S(2)}, u32[]{:S(2)}) %collective-permute-start.12) | collective-permute-done | bytes 98336 | tf_op jit(solution)/shard_map/ppermute | solution.py:346
  34.5 0.1 collective-permute-start.20
  34.6 0.9 %collective-permute-done.13.refs_2_ = bf16[32,1536]{1,0:T(8,128)(2,1)S(1)} collective-permute-done((bf16[32,1536]{1,0:T(8,128)(2,1)S(1)}, bf16[32,1536]{1,0:T(8,128)(2,1)S(1)}, u32[]{:S(2)}, u32[]{:S(2)}) %collective-permute-start.13) | collective-permute-done | bytes 98336 | tf_op jit(solution)/shard_map/ppermute | solution.py:346
  35.5 0.0 collective-permute-done.14.refs_3_
  35.5 0.3 shard_map.116
  35.7 2.2 %collective-permute-start.15 = (bf16[16,1536]{1,0:T(8,128)(2,1)S(1)}, bf16[16,1536]{1,0:T(8,128)(2,1)S(1)}, u32[]{:S(2)}, u32[]{:S(2)}) collective-permute-start(bf16[16,1536]{1,0:T(8,128)(2,1)S(1)} %get-tuple-element.64), channel_id=1, source_target_pairs={{0,12},{4,8},{8,4},{12,0},{1,13},{5,9},{9,5},{13,1},{2,14},{6,10},... | collective-permute-start | bytes 147464 | tf_op jit(solution)/shard_map/ppermute | solution.py:346
  37.9 1.4 %collective-permute-start.16 = (bf16[16,1536]{1,0:T(8,128)(2,1)S(1)}, bf16[16,1536]{1,0:T(8,128)(2,1)S(1)}, u32[]{:S(2)}, u32[]{:S(2)}) collective-permute-start(bf16[16,1536]{1,0:T(8,128)(2,1)S(1)} %get-tuple-element.65), channel_id=1, source_target_pairs={{0,8},{4,12},{8,0},{12,4},{1,9},{5,13},{9,1},{13,5},{2,10},{6,14},... | collective-permute-start | bytes 147464 | tf_op jit(solution)/shard_map/ppermute | solution.py:346
  39.3 0.0 collective-permute-done.18.refs_1_
  39.3 1.2 %collective-permute-start.17 = (bf16[16,1536]{1,0:T(8,128)(2,1)S(1)}, bf16[16,1536]{1,0:T(8,128)(2,1)S(1)}, u32[]{:S(2)}, u32[]{:S(2)}) collective-permute-start(bf16[16,1536]{1,0:T(8,128)(2,1)S(1)} %get-tuple-element.66), channel_id=1, source_target_pairs={{0,4},{4,0},{8,12},{12,8},{1,5},{5,1},{9,13},{13,9},{2,6},{6,2},{1... | collective-permute-start | bytes 147464 | tf_op jit(solution)/shard_map/ppermute | solution.py:346
  40.5 0.0 collective-permute-done.19.refs_2_
  40.5 0.3 shard_map.119
  40.8 3.5 %collective-permute-start.21 = (bf16[16,1536]{1,0:T(8,128)(2,1)S(1)}, bf16[16,1536]{1,0:T(8,128)(2,1)S(1)}, u32[]{:S(2)}, u32[]{:S(2)}) collective-permute-start(bf16[16,1536]{1,0:T(8,128)(2,1)S(1)} %get-tuple-element.74), channel_id=1, source_target_pairs={{0,12},{4,8},{8,4},{12,0},{1,13},{5,9},{9,5},{13,1},{2,14},{6,10},... | collective-permute-start | bytes 147464 | tf_op jit(solution)/shard_map/ppermute | solution.py:346
  44.3 0.0 collective-permute-start.22
  44.3 0.0 collective-permute-done.15.refs_1_
  44.3 0.9 %collective-permute-start.23 = (bf16[16,1536]{1,0:T(8,128)(2,1)S(1)}, bf16[16,1536]{1,0:T(8,128)(2,1)S(1)}, u32[]{:S(2)}, u32[]{:S(2)}) collective-permute-start(bf16[16,1536]{1,0:T(8,128)(2,1)S(1)} %get-tuple-element.76), channel_id=1, source_target_pairs={{0,4},{4,0},{8,12},{12,8},{1,5},{5,1},{9,13},{13,9},{2,6},{6,2},{1... | collective-permute-start | bytes 147464 | tf_op jit(solution)/shard_map/ppermute | solution.py:346
  45.2 0.0 collective-permute-done.16.refs_2_
  45.2 0.0 collective-permute-done.17.refs_3_
  45.3 1.7 %collective-permute-done.21.refs_2_ = bf16[16,1536]{1,0:T(8,128)(2,1)S(1)} collective-permute-done((bf16[16,1536]{1,0:T(8,128)(2,1)S(1)}, bf16[16,1536]{1,0:T(8,128)(2,1)S(1)}, u32[]{:S(2)}, u32[]{:S(2)}) %collective-permute-start.21) | collective-permute-done | bytes 49184 | tf_op jit(solution)/shard_map/ppermute | solution.py:346
  47.0 2.5 %collective-permute-done.22.refs_3_ = bf16[16,1536]{1,0:T(8,128)(2,1)S(1)} collective-permute-done((bf16[16,1536]{1,0:T(8,128)(2,1)S(1)}, bf16[16,1536]{1,0:T(8,128)(2,1)S(1)}, u32[]{:S(2)}, u32[]{:S(2)}) %collective-permute-start.22) | collective-permute-done | bytes 49184 | tf_op jit(solution)/shard_map/ppermute | solution.py:346
  49.5 0.0 collective-permute-done.23.refs_4_
  49.5 0.7 %shard_map.120 = bf16[16,3072]{1,0:T(8,128)(2,1)} custom-call(bf16[16,1536]{1,0:T(8,128)(2,1)S(1)} %shard_map.117.refs_0_, f32[16,1536]{1,0:T(8,128)S(1)} %get-tuple-element.73.refs_1_, bf16[16,1536]{1,0:T(8,128)(2,1)S(1)} %collective-permute-done.21.refs_2_, bf16[16,1536]{1,0:T(8,128)(2,1)S(1)} %collective-permute-done.22.refs_3_, ...), custom_call_target="tpu_custom_call" | custom-call | tf_op jit(solution)/shard_map/pallas_call | solution.py:473
  (12 shorter events, 0.0 us)
Async XLA Ops:
  3.0 18.0 %slice-start = ((s8[12582912]{0:T(1024)(128)(4,1)}), s8[4194304]{0:T(1024)(128)(4,1)S(1)}, s32[]{:S(2)}) async-start(s8[12582912]{0:T(1024)(128)(4,1)} %bitcast.8), calls=%async_computation | async-start | bytes 8388608
  3.0 18.0 %slice-start.3 = ((s8[12582912]{0:T(1024)(128)(4,1)}), s8[4194304]{0:T(1024)(128)(4,1)S(1)}, s32[]{:S(2)}) async-start(s8[12582912]{0:T(1024)(128)(4,1)} %bitcast.12), calls=%async_computation.3 | async-start | bytes 8388608
  3.1 17.9 %slice-start.1 = ((s8[12582912]{0:T(1024)(128)(4,1)}), s8[4194304]{0:T(1024)(128)(4,1)S(1)}, s32[]{:S(2)}) async-start(s8[12582912]{0:T(1024)(128)(4,1)} %bitcast.8), calls=%async_computation.1 | async-start | bytes 8388608
  3.1 17.9 %slice-start.2 = ((s8[12582912]{0:T(1024)(128)(4,1)}), s8[4194304]{0:T(1024)(128)(4,1)S(1)}, s32[]{:S(2)}) async-start(s8[12582912]{0:T(1024)(128)(4,1)} %bitcast.8), calls=%async_computation.2 | async-start | bytes 8388608
  3.1 17.9 %slice-start.4 = ((s8[12582912]{0:T(1024)(128)(4,1)}), s8[4194304]{0:T(1024)(128)(4,1)S(1)}, s32[]{:S(2)}) async-start(s8[12582912]{0:T(1024)(128)(4,1)} %bitcast.12), calls=%async_computation.4 | async-start | bytes 8388608
  3.1 17.9 %slice-start.5 = ((s8[12582912]{0:T(1024)(128)(4,1)}), s8[4194304]{0:T(1024)(128)(4,1)S(1)}, s32[]{:S(2)}) async-start(s8[12582912]{0:T(1024)(128)(4,1)} %bitcast.12), calls=%async_computation.5 | async-start | bytes 8388608
  3.1 16.4 %copy-start = (bf16[3072,4]{0,1:T(4,128)(2,1)S(1)}, bf16[3072,4]{0,1:T(4,128)(2,1)}, u32[]{:S(2)}) copy-start(bf16[3072,4]{0,1:T(4,128)(2,1)} %param.18) | copy-start | bytes 73732
  3.1 9.8 %collective-permute-start.2 = (bf16[16,1664]{1,0:T(8,128)(2,1)S(1)}, bf16[16,1664]{1,0:T(8,128)(2,1)S(1)}, u32[]{:S(2)}, u32[]{:S(2)}) collective-permute-start(bf16[16,1664]{1,0:T(8,128)(2,1)S(1)} %get-tuple-element.43.refs_0_), channel_id=1, source_target_pairs={{0,8},{4,12},{8,0},{12,4},{1,9},{5,13},{9,1},{13,5},{2,10},{6,14},... | collective-permute-start | bytes 159752 | tf_op jit(solution)/shard_map/ppermute | solution.py:346
  7.2 6.5 %collective-permute-start.1 = (bf16[16,1664]{1,0:T(8,128)(2,1)S(1)}, bf16[16,1664]{1,0:T(8,128)(2,1)S(1)}, u32[]{:S(2)}, u32[]{:S(2)}) collective-permute-start(bf16[16,1664]{1,0:T(8,128)(2,1)S(1)} %get-tuple-element.43.refs_0_), channel_id=1, source_target_pairs={{0,12},{4,8},{8,4},{12,0},{1,13},{5,9},{9,5},{13,1},{2,14},{6,10},... | collective-permute-start | bytes 159752 | tf_op jit(solution)/shard_map/ppermute | solution.py:346
  8.6 5.2 %collective-permute-start = (bf16[16,1664]{1,0:T(8,128)(2,1)S(1)}, bf16[16,1664]{1,0:T(8,128)(2,1)S(1)}, u32[]{:S(2)}, u32[]{:S(2)}) collective-permute-start(bf16[16,1664]{1,0:T(8,128)(2,1)S(1)} %get-tuple-element.43.refs_0_), channel_id=1, source_target_pairs={{0,4},{4,0},{8,12},{12,8},{1,5},{5,1},{9,13},{13,9},{2,6},{6,2},{1... | collective-permute-start | bytes 159752 | tf_op jit(solution)/shard_map/ppermute | solution.py:346
  8.8 7.3 %collective-permute-start.5 = (bf16[16,1536]{1,0:T(8,128)(2,1)S(1)}, bf16[16,1536]{1,0:T(8,128)(2,1)S(1)}, u32[]{:S(2)}, u32[]{:S(2)}) collective-permute-start(bf16[16,1536]{1,0:T(8,128)(2,1)S(1)} %get-tuple-element.44.refs_4_), channel_id=1, source_target_pairs={{0,8},{4,12},{8,0},{12,4},{1,9},{5,13},{9,1},{13,5},{2,10},{6,14},... | collective-permute-start | bytes 147464 | tf_op jit(solution)/shard_map/ppermute | solution.py:346
  11.6 6.0 %collective-permute-start.4 = (bf16[16,1536]{1,0:T(8,128)(2,1)S(1)}, bf16[16,1536]{1,0:T(8,128)(2,1)S(1)}, u32[]{:S(2)}, u32[]{:S(2)}) collective-permute-start(bf16[16,1536]{1,0:T(8,128)(2,1)S(1)} %get-tuple-element.44.refs_4_), channel_id=1, source_target_pairs={{0,12},{4,8},{8,4},{12,0},{1,13},{5,9},{9,5},{13,1},{2,14},{6,10},... | collective-permute-start | bytes 147464 | tf_op jit(solution)/shard_map/ppermute | solution.py:346
  13.0 4.6 %collective-permute-start.3 = (bf16[16,1536]{1,0:T(8,128)(2,1)S(1)}, bf16[16,1536]{1,0:T(8,128)(2,1)S(1)}, u32[]{:S(2)}, u32[]{:S(2)}) collective-permute-start(bf16[16,1536]{1,0:T(8,128)(2,1)S(1)} %get-tuple-element.44.refs_4_), channel_id=1, source_target_pairs={{0,4},{4,0},{8,12},{12,8},{1,5},{5,1},{9,13},{13,9},{2,6},{6,2},{1... | collective-permute-start | bytes 147464 | tf_op jit(solution)/shard_map/ppermute | solution.py:346
  14.1 5.8 %collective-permute-start.9 = (bf16[32,1536]{1,0:T(8,128)(2,1)S(1)}, bf16[32,1536]{1,0:T(8,128)(2,1)S(1)}, u32[]{:S(2)}, u32[]{:S(2)}) collective-permute-start(bf16[32,1536]{1,0:T(8,128)(2,1)S(1)} %get-tuple-element.52), channel_id=1, source_target_pairs={{0,2},{1,3},{2,0},{3,1},{4,6},{5,7},{6,4},{7,5},{8,10},{9,11},{10,... | collective-permute-start | bytes 294920 | tf_op jit(solution)/shard_map/ppermute | solution.py:346
  15.7 5.3 %collective-permute-start.10 = (bf16[32,1536]{1,0:T(8,128)(2,1)S(1)}, bf16[32,1536]{1,0:T(8,128)(2,1)S(1)}, u32[]{:S(2)}, u32[]{:S(2)}) collective-permute-start(bf16[32,1536]{1,0:T(8,128)(2,1)S(1)} %get-tuple-element.53), channel_id=1, source_target_pairs={{0,3},{1,2},{2,1},{3,0},{4,7},{5,6},{6,5},{7,4},{8,11},{9,10},{10,... | collective-permute-start | bytes 294920 | tf_op jit(solution)/shard_map/ppermute | solution.py:346
  16.1 4.9 %collective-permute-start.11 = (bf16[32,1536]{1,0:T(8,128)(2,1)S(1)}, bf16[32,1536]{1,0:T(8,128)(2,1)S(1)}, u32[]{:S(2)}, u32[]{:S(2)}) collective-permute-start(bf16[32,1536]{1,0:T(8,128)(2,1)S(1)} %get-tuple-element.54), channel_id=1, source_target_pairs={{0,1},{1,0},{2,3},{3,2},{4,5},{5,4},{6,7},{7,6},{8,9},{9,8},{10,11... | collective-permute-start | bytes 294920 | tf_op jit(solution)/shard_map/ppermute | solution.py:346
  18.0 6.0 %collective-permute-start.6 = (bf16[32,1536]{1,0:T(8,128)(2,1)S(1)}, bf16[32,1536]{1,0:T(8,128)(2,1)S(1)}, u32[]{:S(2)}, u32[]{:S(2)}) collective-permute-start(bf16[32,1536]{1,0:T(8,128)(2,1)S(1)} %get-tuple-element.48), channel_id=1, source_target_pairs={{0,2},{1,3},{2,0},{3,1},{4,6},{5,7},{6,4},{7,5},{8,10},{9,11},{10,... | collective-permute-start | bytes 294920 | tf_op jit(solution)/shard_map/ppermute | solution.py:346
  19.5 5.1 %collective-permute-start.7 = (bf16[32,1536]{1,0:T(8,128)(2,1)S(1)}, bf16[32,1536]{1,0:T(8,128)(2,1)S(1)}, u32[]{:S(2)}, u32[]{:S(2)}) collective-permute-start(bf16[32,1536]{1,0:T(8,128)(2,1)S(1)} %get-tuple-element.49), channel_id=1, source_target_pairs={{0,3},{1,2},{2,1},{3,0},{4,7},{5,6},{6,5},{7,4},{8,11},{9,10},{10,... | collective-permute-start | bytes 294920 | tf_op jit(solution)/shard_map/ppermute | solution.py:346
  19.9 4.7 %collective-permute-start.8 = (bf16[32,1536]{1,0:T(8,128)(2,1)S(1)}, bf16[32,1536]{1,0:T(8,128)(2,1)S(1)}, u32[]{:S(2)}, u32[]{:S(2)}) collective-permute-start(bf16[32,1536]{1,0:T(8,128)(2,1)S(1)} %get-tuple-element.50), channel_id=1, source_target_pairs={{0,1},{1,0},{2,3},{3,2},{4,5},{5,4},{6,7},{7,6},{8,9},{9,8},{10,11... | collective-permute-start | bytes 294920 | tf_op jit(solution)/shard_map/ppermute | solution.py:346
  28.8 5.7 %collective-permute-start.12 = (bf16[32,1536]{1,0:T(8,128)(2,1)S(1)}, bf16[32,1536]{1,0:T(8,128)(2,1)S(1)}, u32[]{:S(2)}, u32[]{:S(2)}) collective-permute-start(bf16[32,1536]{1,0:T(8,128)(2,1)S(1)} %get-tuple-element.59), channel_id=1, source_target_pairs={{0,2},{1,3},{2,0},{3,1},{4,6},{5,7},{6,4},{7,5},{8,10},{9,11},{10,... | collective-permute-start | bytes 294920 | tf_op jit(solution)/shard_map/ppermute | solution.py:346
  29.8 5.7 %collective-permute-start.13 = (bf16[32,1536]{1,0:T(8,128)(2,1)S(1)}, bf16[32,1536]{1,0:T(8,128)(2,1)S(1)}, u32[]{:S(2)}, u32[]{:S(2)}) collective-permute-start(bf16[32,1536]{1,0:T(8,128)(2,1)S(1)} %get-tuple-element.60), channel_id=1, source_target_pairs={{0,3},{1,2},{2,1},{3,0},{4,7},{5,6},{6,5},{7,4},{8,11},{9,10},{10,... | collective-permute-start | bytes 294920 | tf_op jit(solution)/shard_map/ppermute | solution.py:346
  30.6 4.9 %collective-permute-start.14 = (bf16[32,1536]{1,0:T(8,128)(2,1)S(1)}, bf16[32,1536]{1,0:T(8,128)(2,1)S(1)}, u32[]{:S(2)}, u32[]{:S(2)}) collective-permute-start(bf16[32,1536]{1,0:T(8,128)(2,1)S(1)} %get-tuple-element.61), channel_id=1, source_target_pairs={{0,1},{1,0},{2,3},{3,2},{4,5},{5,4},{6,7},{7,6},{8,9},{9,8},{10,11... | collective-permute-start | bytes 294920 | tf_op jit(solution)/shard_map/ppermute | solution.py:346
  32.4 6.9 %collective-permute-start.18 = (bf16[32,1536]{1,0:T(8,128)(2,1)S(1)}, bf16[32,1536]{1,0:T(8,128)(2,1)S(1)}, u32[]{:S(2)}, u32[]{:S(2)}) collective-permute-start(bf16[32,1536]{1,0:T(8,128)(2,1)S(1)} %get-tuple-element.70), channel_id=1, source_target_pairs={{0,2},{1,3},{2,0},{3,1},{4,6},{5,7},{6,4},{7,5},{8,10},{9,11},{10,... | collective-permute-start | bytes 294920 | tf_op jit(solution)/shard_map/ppermute | solution.py:346
  33.7 6.8 %collective-permute-start.19 = (bf16[32,1536]{1,0:T(8,128)(2,1)S(1)}, bf16[32,1536]{1,0:T(8,128)(2,1)S(1)}, u32[]{:S(2)}, u32[]{:S(2)}) collective-permute-start(bf16[32,1536]{1,0:T(8,128)(2,1)S(1)} %get-tuple-element.71), channel_id=1, source_target_pairs={{0,3},{1,2},{2,1},{3,0},{4,7},{5,6},{6,5},{7,4},{8,11},{9,10},{10,... | collective-permute-start | bytes 294920 | tf_op jit(solution)/shard_map/ppermute | solution.py:346
  34.5 6.0 %collective-permute-start.20 = (bf16[32,1536]{1,0:T(8,128)(2,1)S(1)}, bf16[32,1536]{1,0:T(8,128)(2,1)S(1)}, u32[]{:S(2)}, u32[]{:S(2)}) collective-permute-start(bf16[32,1536]{1,0:T(8,128)(2,1)S(1)} %get-tuple-element.72), channel_id=1, source_target_pairs={{0,1},{1,0},{2,3},{3,2},{4,5},{5,4},{6,7},{7,6},{8,9},{9,8},{10,11... | collective-permute-start | bytes 294920 | tf_op jit(solution)/shard_map/ppermute | solution.py:346
  35.7 8.6 %collective-permute-start.15 = (bf16[16,1536]{1,0:T(8,128)(2,1)S(1)}, bf16[16,1536]{1,0:T(8,128)(2,1)S(1)}, u32[]{:S(2)}, u32[]{:S(2)}) collective-permute-start(bf16[16,1536]{1,0:T(8,128)(2,1)S(1)} %get-tuple-element.64), channel_id=1, source_target_pairs={{0,12},{4,8},{8,4},{12,0},{1,13},{5,9},{9,5},{13,1},{2,14},{6,10},... | collective-permute-start | bytes 147464 | tf_op jit(solution)/shard_map/ppermute | solution.py:346
  37.9 7.3 %collective-permute-start.16 = (bf16[16,1536]{1,0:T(8,128)(2,1)S(1)}, bf16[16,1536]{1,0:T(8,128)(2,1)S(1)}, u32[]{:S(2)}, u32[]{:S(2)}) collective-permute-start(bf16[16,1536]{1,0:T(8,128)(2,1)S(1)} %get-tuple-element.65), channel_id=1, source_target_pairs={{0,8},{4,12},{8,0},{12,4},{1,9},{5,13},{9,1},{13,5},{2,10},{6,14},... | collective-permute-start | bytes 147464 | tf_op jit(solution)/shard_map/ppermute | solution.py:346
  39.3 5.9 %collective-permute-start.17 = (bf16[16,1536]{1,0:T(8,128)(2,1)S(1)}, bf16[16,1536]{1,0:T(8,128)(2,1)S(1)}, u32[]{:S(2)}, u32[]{:S(2)}) collective-permute-start(bf16[16,1536]{1,0:T(8,128)(2,1)S(1)} %get-tuple-element.66), channel_id=1, source_target_pairs={{0,4},{4,0},{8,12},{12,8},{1,5},{5,1},{9,13},{13,9},{2,6},{6,2},{1... | collective-permute-start | bytes 147464 | tf_op jit(solution)/shard_map/ppermute | solution.py:346
  40.8 6.2 %collective-permute-start.21 = (bf16[16,1536]{1,0:T(8,128)(2,1)S(1)}, bf16[16,1536]{1,0:T(8,128)(2,1)S(1)}, u32[]{:S(2)}, u32[]{:S(2)}) collective-permute-start(bf16[16,1536]{1,0:T(8,128)(2,1)S(1)} %get-tuple-element.74), channel_id=1, source_target_pairs={{0,12},{4,8},{8,4},{12,0},{1,13},{5,9},{9,5},{13,1},{2,14},{6,10},... | collective-permute-start | bytes 147464 | tf_op jit(solution)/shard_map/ppermute | solution.py:346
  44.3 5.1 %collective-permute-start.22 = (bf16[16,1536]{1,0:T(8,128)(2,1)S(1)}, bf16[16,1536]{1,0:T(8,128)(2,1)S(1)}, u32[]{:S(2)}, u32[]{:S(2)}) collective-permute-start(bf16[16,1536]{1,0:T(8,128)(2,1)S(1)} %get-tuple-element.75), channel_id=1, source_target_pairs={{0,8},{4,12},{8,0},{12,4},{1,9},{5,13},{9,1},{13,5},{2,10},{6,14},... | collective-permute-start | bytes 147464 | tf_op jit(solution)/shard_map/ppermute | solution.py:346
  44.3 5.1 %collective-permute-start.23 = (bf16[16,1536]{1,0:T(8,128)(2,1)S(1)}, bf16[16,1536]{1,0:T(8,128)(2,1)S(1)}, u32[]{:S(2)}, u32[]{:S(2)}) collective-permute-start(bf16[16,1536]{1,0:T(8,128)(2,1)S(1)} %get-tuple-element.76), channel_id=1, source_target_pairs={{0,4},{4,0},{8,12},{12,8},{1,5},{5,1},{9,13},{13,9},{2,6},{6,2},{1... | collective-permute-start | bytes 147464 | tf_op jit(solution)/shard_map/ppermute | solution.py:346

commit v21 on v20

--- a/solution.py
+++ b/solution.py
@@ -310,6 +310,7 @@
 
 
 def mix_kernel(high_ref, low_ref, *refs, layers, part):
+    refs = refs[part : len(refs) - part]
     outs, stream_ref = refs[-layers:], refs[-layers - 1]
     blocks = refs[: -layers - 1]
     order = even_first(len(blocks))
@@ -324,15 +325,13 @@
 
 
 def add_kernel(*refs):
-    out_ref = refs[-1]
-    span = refs[-2].shape[1]
-    if out_ref.shape[1] > span:
-        out_ref[:, :span] = refs[0][...]
-        refs = refs[1:]
-    total = refs[0][...]
-    for ref in refs[1:-1]:
-        total = total + ref[...].astype(F32)
-    out_ref[:, out_ref.shape[1] - span :] = total.astype(BF16)
+    out_ref, count = refs[-1], len(refs) // 2
+    half = refs[0].shape[1]
+    for begin, blocks in ((half, refs[:count]), (0, refs[count:-1])):
+        total = blocks[0][...]
+        for ref in blocks[1:]:
+            total = total + ref[...].astype(F32)
+        out_ref[:, begin : begin + half] = total.astype(BF16)
 
 
 def in_hbm(value):
@@ -344,6 +343,10 @@
         return value
     count = lax.axis_size(axis)
     return lax.ppermute(value, axis, [(i, i ^ step) for i in range(count)])
+
+
+def farthest_first(count):
+    return [0, *range(count - 1, 0, -1)]
 
 
 def even_first(count):
@@ -457,29 +460,36 @@
         compiler_params=params(total_rows * width),
     )(hidden, down_second)
 
-    done = []
+    mixed, near = [], placed.index(1)
     for part, blocks in enumerate((first, second)):
         returned = [swap(block, "expert", e) for e, block in zip(order, blocks)]
-        mixed = pl.pallas_call(
+        held = [mixed[0][near]] if part else []
+        sizes = [shape((batch, half), BF16 if j else F32) for j in range(layers)]
+        outs = pl.pallas_call(
             functools.partial(mix_kernel, layers=layers, part=part),
-            in_specs=[WHOLE] * (3 + experts),
-            out_specs=[WHOLE] * layers,
-            out_shape=[shape((batch, half), BF16 if j else F32) for j in range(layers)],
+            in_specs=[WHOLE] * 2 + [ANY] * part + [WHOLE] * (1 + experts),
+            out_specs=[WHOLE] * layers + [ANY] * part,
+            out_shape=sizes + [shape((batch, half), BF16)] * part,
+            input_output_aliases={2: layers} if part else {},
             cost_estimate=LIGHT,
             compiler_params=params(experts * layers * CAP * half),
-        )(*gates, *returned, stream)
-        sums = [swap(mixed[placed.index(j)], "attn", j) for j in [0, *range(layers - 1, 0, -1)]]
-        done = [
-            pl.pallas_call(
-                add_kernel,
-                in_specs=[WHOLE] * (layers + len(done)),
-                out_specs=WHOLE,
-                out_shape=shape((batch, width if part else half), BF16),
-                cost_estimate=LIGHT,
-                compiler_params=params(layers * batch * width),
-            )(*done, *sums)
-        ]
-    return done[0]
+        )(*gates, *held, *returned, stream)
+        mixed.append(list(outs[:layers]))
+        if part:
+            mixed[0][near] = outs[layers]
+    came = [
+        swap(sums[placed.index(j)], "attn", j)
+        for sums in mixed[::-1]
+        for j in farthest_first(layers)
+    ]
+    return pl.pallas_call(
+        add_kernel,
+        in_specs=[WHOLE] * (2 * layers),
+        out_specs=WHOLE,
+        out_shape=shape((batch, width), BF16),
+        cost_estimate=LIGHT,
+        compiler_params=params(2 * layers * batch * width),
+    )(*came)
 
 
 def solution(mesh):

time: 50.3 us -> 50.8 us (level)
  transfers between devices with their start and end apart: 24 -> 24, of which waited for: 9 -> 11; matrix products, arithmetic and copies ran while one was open for 0% -> 0% of each run, Pallas kernels for 12% -> 12%
where the time goes in v21:
time: 50.8 us; the launch traced here: 50.7 us
  starting transfers between devices  27.1 us (53%)
  Pallas kernels  13.8 us (27%)
  waiting for transfers between devices  9.45 us (19%)
    ppermute x24, starting transfers between devices, swap(): return lax.ppermute(value, axis, [(i, i ^ step) for i in range(count)])  27.1 us
    ppermute x24, waiting for transfers between devices, swap(): return lax.ppermute(value, axis, [(i, i ^ step) for i in range(count)])  9.45 us
    pallas_call x1, Pallas kernels, shards(): pl.pallas_call(functools.partial(middle_kernel, experts=experts), in_spec...  4.17 us
    pallas_call x1, Pallas kernels, shards(): pl.pallas_call(attend_kernel, in_specs=[SCALAR] + [ANY] * len(operands),...  3.02 us
    pallas_call x1, Pallas kernels, shards(): pl.pallas_call(functools.partial(begin_kernel, experts=experts), in_specs...  2.92 us
    pallas_call x1, Pallas kernels, shards(): pl.pallas_call(end_kernel, in_specs=[WHOLE] * 2, out_specs=[WHOLE] * expe...  1.37 us
  transfers between devices with their start and end apart: 24, of which 11 were waited for; matrix products, arithmetic and copies ran while one was open for 0% of the time, Pallas kernels for 12%

profile of v21, /device:TPU:0, one launch (start us, length us, event | category | flops | bytes accessed | tf_op | source)
XLA Modules:
  0.0 50.7 jit_solution(14882276477017319797)
XLA Ops:
  0.0 3.0 %shard_map.109 = (f32[16,3072]{1,0:T(8,128)S(1)}, bf16[16,1664]{1,0:T(8,128)(2,1)S(1)}, bf16[16,1536]{1,0:T(8,128)(2,1)S(1)}) custom-call(s32[1]{0:T(128)} %bitcast._.me_ref, s32[1,16]{1,0:T(1,128)} %bitcast.21, bf16[16,3072]{1,0:T(8,128)(2,1)} %queries_hbm.1, bf16[16,96,512]{2,1,0:T(8,128)(2,1)} %keys_hbm.1, bf16[16,96,512]{2,1,0:T(8,128)(2,1)} %values_hbm.1, ...), custom_call_target="tpu_custom_call" | custom-call | tf_op jit(solution)/shard_map/pallas_call | solution.py:389
  3.0 0.0 slice-start
  3.0 0.0 slice-start.3
  3.1 0.0 slice-start.1
  3.1 0.0 slice-start.2
  3.1 0.0 slice-start.4
  3.1 0.0 slice-start.5
  3.1 0.0 copy-start
  3.1 4.1 %collective-permute-start.2 = (bf16[16,1664]{1,0:T(8,128)(2,1)S(1)}, bf16[16,1664]{1,0:T(8,128)(2,1)S(1)}, u32[]{:S(2)}, u32[]{:S(2)}) collective-permute-start(bf16[16,1664]{1,0:T(8,128)(2,1)S(1)} %get-tuple-element.44.refs_0_), channel_id=1, source_target_pairs={{0,8},{4,12},{8,0},{12,4},{1,9},{5,13},{9,1},{13,5},{2,10},{6,14},... | collective-permute-start | bytes 159752 | tf_op jit(solution)/shard_map/ppermute | solution.py:345
  7.2 1.4 %collective-permute-start.1 = (bf16[16,1664]{1,0:T(8,128)(2,1)S(1)}, bf16[16,1664]{1,0:T(8,128)(2,1)S(1)}, u32[]{:S(2)}, u32[]{:S(2)}) collective-permute-start(bf16[16,1664]{1,0:T(8,128)(2,1)S(1)} %get-tuple-element.44.refs_0_), channel_id=1, source_target_pairs={{0,12},{4,8},{8,4},{12,0},{1,13},{5,9},{9,5},{13,1},{2,14},{6,10},... | collective-permute-start | bytes 159752 | tf_op jit(solution)/shard_map/ppermute | solution.py:345
  8.6 0.2 collective-permute-start
  8.8 2.8 %collective-permute-start.5 = (bf16[16,1536]{1,0:T(8,128)(2,1)S(1)}, bf16[16,1536]{1,0:T(8,128)(2,1)S(1)}, u32[]{:S(2)}, u32[]{:S(2)}) collective-permute-start(bf16[16,1536]{1,0:T(8,128)(2,1)S(1)} %get-tuple-element.45.refs_4_), channel_id=1, source_target_pairs={{0,8},{4,12},{8,0},{12,4},{1,9},{5,13},{9,1},{13,5},{2,10},{6,14},... | collective-permute-start | bytes 147464 | tf_op jit(solution)/shard_map/ppermute | solution.py:345
  11.6 1.3 %collective-permute-start.4 = (bf16[16,1536]{1,0:T(8,128)(2,1)S(1)}, bf16[16,1536]{1,0:T(8,128)(2,1)S(1)}, u32[]{:S(2)}, u32[]{:S(2)}) collective-permute-start(bf16[16,1536]{1,0:T(8,128)(2,1)S(1)} %get-tuple-element.45.refs_4_), channel_id=1, source_target_pairs={{0,12},{4,8},{8,4},{12,0},{1,13},{5,9},{9,5},{13,1},{2,14},{6,10},... | collective-permute-start | bytes 147464 | tf_op jit(solution)/shard_map/ppermute | solution.py:345
  13.0 0.0 collective-permute-done.2.refs_3_
  13.0 0.0 collective-permute-start.3
  13.0 0.8 %collective-permute-done.1.refs_2_ = bf16[16,1664]{1,0:T(8,128)(2,1)S(1)} collective-permute-done((bf16[16,1664]{1,0:T(8,128)(2,1)S(1)}, bf16[16,1664]{1,0:T(8,128)(2,1)S(1)}, u32[]{:S(2)}, u32[]{:S(2)}) %collective-permute-start.1) | collective-permute-done | bytes 53280 | tf_op jit(solution)/shard_map/ppermute | solution.py:345
  13.7 0.0 collective-permute-done.refs_1_
  13.7 0.4 shard_map.113
  14.1 1.6 %collective-permute-start.9 = (bf16[32,1536]{1,0:T(8,128)(2,1)S(1)}, bf16[32,1536]{1,0:T(8,128)(2,1)S(1)}, u32[]{:S(2)}, u32[]{:S(2)}) collective-permute-start(bf16[32,1536]{1,0:T(8,128)(2,1)S(1)} %get-tuple-element.53), channel_id=1, source_target_pairs={{0,2},{1,3},{2,0},{3,1},{4,6},{5,7},{6,4},{7,5},{8,10},{9,11},{10,... | collective-permute-start | bytes 294920 | tf_op jit(solution)/shard_map/ppermute | solution.py:345
  15.7 0.0 collective-permute-start.10
  15.7 0.4 collective-permute-done.5.refs_7_
  16.1 0.2 collective-permute-start.11
  16.4 1.2 %collective-permute-done.4.refs_6_ = bf16[16,1536]{1,0:T(8,128)(2,1)S(1)} collective-permute-done((bf16[16,1536]{1,0:T(8,128)(2,1)S(1)}, bf16[16,1536]{1,0:T(8,128)(2,1)S(1)}, u32[]{:S(2)}, u32[]{:S(2)}) %collective-permute-start.4) | collective-permute-done | bytes 49184 | tf_op jit(solution)/shard_map/ppermute | solution.py:345
  17.6 0.0 collective-permute-done.3.refs_5_
  17.6 0.4 shard_map.112
  18.0 1.5 %collective-permute-start.6 = (bf16[32,1536]{1,0:T(8,128)(2,1)S(1)}, bf16[32,1536]{1,0:T(8,128)(2,1)S(1)}, u32[]{:S(2)}, u32[]{:S(2)}) collective-permute-start(bf16[32,1536]{1,0:T(8,128)(2,1)S(1)} %get-tuple-element.49), channel_id=1, source_target_pairs={{0,2},{1,3},{2,0},{3,1},{4,6},{5,7},{6,4},{7,5},{8,10},{9,11},{10,... | collective-permute-start | bytes 294920 | tf_op jit(solution)/shard_map/ppermute | solution.py:345
  19.5 0.0 collective-permute-start.7
  19.5 0.4 shard_map.111
  19.9 0.0 collective-permute-done.9.refs_1_
  19.9 0.7 %collective-permute-start.8 = (bf16[32,1536]{1,0:T(8,128)(2,1)S(1)}, bf16[32,1536]{1,0:T(8,128)(2,1)S(1)}, u32[]{:S(2)}, u32[]{:S(2)}) collective-permute-start(bf16[32,1536]{1,0:T(8,128)(2,1)S(1)} %get-tuple-element.51), channel_id=1, source_target_pairs={{0,1},{1,0},{2,3},{3,2},{4,5},{5,4},{6,7},{7,6},{8,9},{9,8},{10,11... | collective-permute-start | bytes 294920 | tf_op jit(solution)/shard_map/ppermute | solution.py:345
  20.6 0.4 collective-permute-done.10.refs_2_
  21.0 0.0 collective-permute-done.11.refs_3_
  21.1 2.9 %shard_map.114 = (f32[128,2048]{1,0:T(8,128)S(1)}, f32[128,2048]{1,0:T(8,128)S(1)}, bf16[2048,1536]{1,0:T(8,128)(2,1)S(1)}) custom-call(bf16[32,1536]{1,0:T(8,128)(2,1)S(1)} %get-tuple-element.52.refs_0_, bf16[32,1536]{1,0:T(8,128)(2,1)S(1)} %collective-permute-done.9.refs_1_, bf16[32,1536]{1,0:T(8,128)(2,1)S(1)} %collective-permute-done.10.refs_2_, ...), custom_call_target="tpu_custom_call" | custom-call | flops 1610612736 | tf_op jit(solution)/shard_map/pallas_call | solution.py:433
  24.0 0.0 collective-permute-done.6.refs_1_
  24.0 0.6 %collective-permute-done.7.refs_2_ = bf16[32,1536]{1,0:T(8,128)(2,1)S(1)} collective-permute-done((bf16[32,1536]{1,0:T(8,128)(2,1)S(1)}, bf16[32,1536]{1,0:T(8,128)(2,1)S(1)}, u32[]{:S(2)}, u32[]{:S(2)}) %collective-permute-start.7) | collective-permute-done | bytes 98336 | tf_op jit(solution)/shard_map/ppermute | solution.py:345
  24.6 0.0 collective-permute-done.8.refs_3_
  24.6 4.2 %shard_map.115 = (bf16[32,1536]{1,0:T(8,128)(2,1)S(1)}, bf16[32,1536]{1,0:T(8,128)(2,1)S(1)}, bf16[32,1536]{1,0:T(8,128)(2,1)S(1)}, bf16[32,1536]{1,0:T(8,128)(2...) custom-call(bf16[32,1536]{1,0:T(8,128)(2,1)S(1)} %get-tuple-element.48.refs_0_, ...), custom_call_target="tpu_custom_call" | custom-call | tf_op jit(solution)/shard_map/pallas_call | solution.py:444
  28.8 1.0 %collective-permute-start.12 = (bf16[32,1536]{1,0:T(8,128)(2,1)S(1)}, bf16[32,1536]{1,0:T(8,128)(2,1)S(1)}, u32[]{:S(2)}, u32[]{:S(2)}) collective-permute-start(bf16[32,1536]{1,0:T(8,128)(2,1)S(1)} %get-tuple-element.60), channel_id=1, source_target_pairs={{0,2},{1,3},{2,0},{3,1},{4,6},{5,7},{6,4},{7,5},{8,10},{9,11},{10,... | collective-permute-start | bytes 294920 | tf_op jit(solution)/shard_map/ppermute | solution.py:345
  29.8 0.8 %collective-permute-start.13 = (bf16[32,1536]{1,0:T(8,128)(2,1)S(1)}, bf16[32,1536]{1,0:T(8,128)(2,1)S(1)}, u32[]{:S(2)}, u32[]{:S(2)}) collective-permute-start(bf16[32,1536]{1,0:T(8,128)(2,1)S(1)} %get-tuple-element.61), channel_id=1, source_target_pairs={{0,3},{1,2},{2,1},{3,0},{4,7},{5,6},{6,5},{7,4},{8,11},{9,10},{10,... | collective-permute-start | bytes 294920 | tf_op jit(solution)/shard_map/ppermute | solution.py:345
  30.6 0.4 collective-permute-start.14
  31.0 1.4 %shard_map.117 = (bf16[32,1536]{1,0:T(8,128)(2,1)S(1)}, bf16[32,1536]{1,0:T(8,128)(2,1)S(1)}, bf16[32,1536]{1,0:T(8,128)(2,1)S(1)}, bf16[32,1536]{1,0:T(8,128)(2,1)S(1)}) custom-call(bf16[128,2048]{1,0:T(8,128)(2,1)S(1)} %get-tuple-element.65.hidden_ref, bf16[2048,1536]{1,0:T(8,128)(2,1)S(1)} %get-tuple-element.66.down_ref), custom_call_target="tpu_custom_call" | custom-call | flops 805306368 | tf_op jit(solution)/shard_map/pallas_call | solution.py:452
  32.4 1.3 %collective-permute-start.15 = (bf16[32,1536]{1,0:T(8,128)(2,1)S(1)}, bf16[32,1536]{1,0:T(8,128)(2,1)S(1)}, u32[]{:S(2)}, u32[]{:S(2)}) collective-permute-start(bf16[32,1536]{1,0:T(8,128)(2,1)S(1)} %get-tuple-element.68), channel_id=1, source_target_pairs={{0,2},{1,3},{2,0},{3,1},{4,6},{5,7},{6,4},{7,5},{8,10},{9,11},{10,... | collective-permute-start | bytes 294920 | tf_op jit(solution)/shard_map/ppermute | solution.py:345
  33.7 0.2 collective-permute-start.16
  33.9 0.6 %collective-permute-done.12.refs_1_ = bf16[32,1536]{1,0:T(8,128)(2,1)S(1)} collective-permute-done((bf16[32,1536]{1,0:T(8,128)(2,1)S(1)}, bf16[32,1536]{1,0:T(8,128)(2,1)S(1)}, u32[]{:S(2)}, u32[]{:S(2)}) %collective-permute-start.12) | collective-permute-done | bytes 98336 | tf_op jit(solution)/shard_map/ppermute | solution.py:345
  34.5 0.1 collective-permute-start.17
  34.6 0.9 %collective-permute-done.13.refs_2_ = bf16[32,1536]{1,0:T(8,128)(2,1)S(1)} collective-permute-done((bf16[32,1536]{1,0:T(8,128)(2,1)S(1)}, bf16[32,1536]{1,0:T(8,128)(2,1)S(1)}, u32[]{:S(2)}, u32[]{:S(2)}) %collective-permute-start.13) | collective-permute-done | bytes 98336 | tf_op jit(solution)/shard_map/ppermute | solution.py:345
  35.5 0.0 collective-permute-done.14.refs_3_
  35.5 0.3 shard_map.116
  35.7 2.2 %collective-permute-start.21 = (bf16[16,1536]{1,0:T(8,128)(2,1)S(1)}, bf16[16,1536]{1,0:T(8,128)(2,1)S(1)}, u32[]{:S(2)}, u32[]{:S(2)}) collective-permute-start(bf16[16,1536]{1,0:T(8,128)(2,1)S(1)} %get-tuple-element.76), channel_id=1, source_target_pairs={{0,12},{4,8},{8,4},{12,0},{1,13},{5,9},{9,5},{13,1},{2,14},{6,10},... | collective-permute-start | bytes 147464 | tf_op jit(solution)/shard_map/ppermute | solution.py:345
  37.9 1.4 %collective-permute-start.22 = (bf16[16,1536]{1,0:T(8,128)(2,1)S(1)}, bf16[16,1536]{1,0:T(8,128)(2,1)S(1)}, u32[]{:S(2)}, u32[]{:S(2)}) collective-permute-start(bf16[16,1536]{1,0:T(8,128)(2,1)S(1)} %get-tuple-element.77), channel_id=1, source_target_pairs={{0,8},{4,12},{8,0},{12,4},{1,9},{5,13},{9,1},{13,5},{2,10},{6,14},... | collective-permute-start | bytes 147464 | tf_op jit(solution)/shard_map/ppermute | solution.py:345
  39.3 0.0 collective-permute-done.15.refs_2_
  39.3 0.3 collective-permute-done.16.refs_3_
  39.7 0.0 collective-permute-done.17.refs_4_
  39.7 0.3 shard_map.118
  39.9 2.6 %collective-permute-start.18 = (bf16[16,1536]{1,0:T(8,128)(2,1)S(1)}, bf16[16,1536]{1,0:T(8,128)(2,1)S(1)}, u32[]{:S(2)}, u32[]{:S(2)}) collective-permute-start(bf16[16,1536]{1,0:T(8,128)(2,1)S(1)} %get-tuple-element.72), channel_id=1, source_target_pairs={{0,12},{4,8},{8,4},{12,0},{1,13},{5,9},{9,5},{13,1},{2,14},{6,10},... | collective-permute-start | bytes 147464 | tf_op jit(solution)/shard_map/ppermute | solution.py:345
  42.5 1.2 %collective-permute-start.19 = (bf16[16,1536]{1,0:T(8,128)(2,1)S(1)}, bf16[16,1536]{1,0:T(8,128)(2,1)S(1)}, u32[]{:S(2)}, u32[]{:S(2)}) collective-permute-start(bf16[16,1536]{1,0:T(8,128)(2,1)S(1)} %get-tuple-element.73), channel_id=1, source_target_pairs={{0,8},{4,12},{8,0},{12,4},{1,9},{5,13},{9,1},{13,5},{2,10},{6,14},... | collective-permute-start | bytes 147464 | tf_op jit(solution)/shard_map/ppermute | solution.py:345
  43.7 0.7 %collective-permute-start.20 = (bf16[16,1536]{1,0:T(8,128)(2,1)S(1)}, bf16[16,1536]{1,0:T(8,128)(2,1)S(1)}, u32[]{:S(2)}, u32[]{:S(2)}) collective-permute-start(bf16[16,1536]{1,0:T(8,128)(2,1)S(1)} %get-tuple-element.74), channel_id=1, source_target_pairs={{0,4},{4,0},{8,12},{12,8},{1,5},{5,1},{9,13},{13,9},{2,6},{6,2},{1... | collective-permute-start | bytes 147464 | tf_op jit(solution)/shard_map/ppermute | solution.py:345
  44.4 0.0 collective-permute-done.21.refs_5_
  44.4 1.3 %collective-permute-start.23 = (bf16[16,1536]{1,0:T(8,128)(2,1)S(1)}, bf16[16,1536]{1,0:T(8,128)(2,1)S(1)}, u32[]{:S(2)}, u32[]{:S(2)}) collective-permute-start(bf16[16,1536]{1,0:T(8,128)(2,1)S(1)} %get-tuple-element.78), channel_id=1, source_target_pairs={{0,4},{4,0},{8,12},{12,8},{1,5},{5,1},{9,13},{13,9},{2,6},{6,2},{1... | collective-permute-start | bytes 147464 | tf_op jit(solution)/shard_map/ppermute | solution.py:345
  45.7 0.0 collective-permute-done.22.refs_6_
  45.7 0.5 collective-permute-done.18.refs_1_
  46.2 3.2 %collective-permute-done.19.refs_2_ = bf16[16,1536]{1,0:T(8,128)(2,1)S(1)} collective-permute-done((bf16[16,1536]{1,0:T(8,128)(2,1)S(1)}, bf16[16,1536]{1,0:T(8,128)(2,1)S(1)}, u32[]{:S(2)}, u32[]{:S(2)}) %collective-permute-start.19) | collective-permute-done | bytes 49184 | tf_op jit(solution)/shard_map/ppermute | solution.py:345
  49.4 0.5 %collective-permute-done.23.refs_7_ = bf16[16,1536]{1,0:T(8,128)(2,1)S(1)} collective-permute-done((bf16[16,1536]{1,0:T(8,128)(2,1)S(1)}, bf16[16,1536]{1,0:T(8,128)(2,1)S(1)}, u32[]{:S(2)}, u32[]{:S(2)}) %collective-permute-start.23) | collective-permute-done | bytes 49184 | tf_op jit(solution)/shard_map/ppermute | solution.py:345
  50.0 0.7 %shard_map.119 = bf16[16,3072]{1,0:T(8,128)(2,1)} custom-call(f32[16,1536]{1,0:T(8,128)S(1)} %get-tuple-element.71.refs_0_, bf16[16,1536]{1,0:T(8,128)(2,1)S(1)} %collective-permute-done.18.refs_1_, bf16[16,1536]{1,0:T(8,128)(2,1)S(1)} %collective-permute-done.19.refs_2_, bf16[16,1536]{1,0:T(8,128)(2,1)S(1)} %collective-permute-done.20.refs_3_, ...), custom_call_target="tpu_custom_call" | custom-call | tf_op jit(solution)/shard_map/pallas_call | solution.py:485
  (11 shorter events, 0.0 us)
Async XLA Ops:
  3.0 18.0 %slice-start = ((s8[12582912]{0:T(1024)(128)(4,1)}), s8[4194304]{0:T(1024)(128)(4,1)S(1)}, s32[]{:S(2)}) async-start(s8[12582912]{0:T(1024)(128)(4,1)} %bitcast.8), calls=%async_computation | async-start | bytes 8388608
  3.0 18.0 %slice-start.3 = ((s8[12582912]{0:T(1024)(128)(4,1)}), s8[4194304]{0:T(1024)(128)(4,1)S(1)}, s32[]{:S(2)}) async-start(s8[12582912]{0:T(1024)(128)(4,1)} %bitcast.12), calls=%async_computation.3 | async-start | bytes 8388608
  3.1 17.9 %slice-start.1 = ((s8[12582912]{0:T(1024)(128)(4,1)}), s8[4194304]{0:T(1024)(128)(4,1)S(1)}, s32[]{:S(2)}) async-start(s8[12582912]{0:T(1024)(128)(4,1)} %bitcast.8), calls=%async_computation.1 | async-start | bytes 8388608
  3.1 17.9 %slice-start.2 = ((s8[12582912]{0:T(1024)(128)(4,1)}), s8[4194304]{0:T(1024)(128)(4,1)S(1)}, s32[]{:S(2)}) async-start(s8[12582912]{0:T(1024)(128)(4,1)} %bitcast.8), calls=%async_computation.2 | async-start | bytes 8388608
  3.1 17.9 %slice-start.4 = ((s8[12582912]{0:T(1024)(128)(4,1)}), s8[4194304]{0:T(1024)(128)(4,1)S(1)}, s32[]{:S(2)}) async-start(s8[12582912]{0:T(1024)(128)(4,1)} %bitcast.12), calls=%async_computation.4 | async-start | bytes 8388608
  3.1 17.9 %slice-start.5 = ((s8[12582912]{0:T(1024)(128)(4,1)}), s8[4194304]{0:T(1024)(128)(4,1)S(1)}, s32[]{:S(2)}) async-start(s8[12582912]{0:T(1024)(128)(4,1)} %bitcast.12), calls=%async_computation.5 | async-start | bytes 8388608
  3.1 16.4 %copy-start = (bf16[3072,4]{0,1:T(4,128)(2,1)S(1)}, bf16[3072,4]{0,1:T(4,128)(2,1)}, u32[]{:S(2)}) copy-start(bf16[3072,4]{0,1:T(4,128)(2,1)} %param.18) | copy-start | bytes 73732
  3.1 9.8 %collective-permute-start.2 = (bf16[16,1664]{1,0:T(8,128)(2,1)S(1)}, bf16[16,1664]{1,0:T(8,128)(2,1)S(1)}, u32[]{:S(2)}, u32[]{:S(2)}) collective-permute-start(bf16[16,1664]{1,0:T(8,128)(2,1)S(1)} %get-tuple-element.44.refs_0_), channel_id=1, source_target_pairs={{0,8},{4,12},{8,0},{12,4},{1,9},{5,13},{9,1},{13,5},{2,10},{6,14},... | collective-permute-start | bytes 159752 | tf_op jit(solution)/shard_map/ppermute | solution.py:345
  7.2 6.5 %collective-permute-start.1 = (bf16[16,1664]{1,0:T(8,128)(2,1)S(1)}, bf16[16,1664]{1,0:T(8,128)(2,1)S(1)}, u32[]{:S(2)}, u32[]{:S(2)}) collective-permute-start(bf16[16,1664]{1,0:T(8,128)(2,1)S(1)} %get-tuple-element.44.refs_0_), channel_id=1, source_target_pairs={{0,12},{4,8},{8,4},{12,0},{1,13},{5,9},{9,5},{13,1},{2,14},{6,10},... | collective-permute-start | bytes 159752 | tf_op jit(solution)/shard_map/ppermute | solution.py:345
  8.6 5.2 %collective-permute-start = (bf16[16,1664]{1,0:T(8,128)(2,1)S(1)}, bf16[16,1664]{1,0:T(8,128)(2,1)S(1)}, u32[]{:S(2)}, u32[]{:S(2)}) collective-permute-start(bf16[16,1664]{1,0:T(8,128)(2,1)S(1)} %get-tuple-element.44.refs_0_), channel_id=1, source_target_pairs={{0,4},{4,0},{8,12},{12,8},{1,5},{5,1},{9,13},{13,9},{2,6},{6,2},{1... | collective-permute-start | bytes 159752 | tf_op jit(solution)/shard_map/ppermute | solution.py:345
  8.8 7.3 %collective-permute-start.5 = (bf16[16,1536]{1,0:T(8,128)(2,1)S(1)}, bf16[16,1536]{1,0:T(8,128)(2,1)S(1)}, u32[]{:S(2)}, u32[]{:S(2)}) collective-permute-start(bf16[16,1536]{1,0:T(8,128)(2,1)S(1)} %get-tuple-element.45.refs_4_), channel_id=1, source_target_pairs={{0,8},{4,12},{8,0},{12,4},{1,9},{5,13},{9,1},{13,5},{2,10},{6,14},... | collective-permute-start | bytes 147464 | tf_op jit(solution)/shard_map/ppermute | solution.py:345
  11.6 6.0 %collective-permute-start.4 = (bf16[16,1536]{1,0:T(8,128)(2,1)S(1)}, bf16[16,1536]{1,0:T(8,128)(2,1)S(1)}, u32[]{:S(2)}, u32[]{:S(2)}) collective-permute-start(bf16[16,1536]{1,0:T(8,128)(2,1)S(1)} %get-tuple-element.45.refs_4_), channel_id=1, source_target_pairs={{0,12},{4,8},{8,4},{12,0},{1,13},{5,9},{9,5},{13,1},{2,14},{6,10},... | collective-permute-start | bytes 147464 | tf_op jit(solution)/shard_map/ppermute | solution.py:345
  13.0 4.6 %collective-permute-start.3 = (bf16[16,1536]{1,0:T(8,128)(2,1)S(1)}, bf16[16,1536]{1,0:T(8,128)(2,1)S(1)}, u32[]{:S(2)}, u32[]{:S(2)}) collective-permute-start(bf16[16,1536]{1,0:T(8,128)(2,1)S(1)} %get-tuple-element.45.refs_4_), channel_id=1, source_target_pairs={{0,4},{4,0},{8,12},{12,8},{1,5},{5,1},{9,13},{13,9},{2,6},{6,2},{1... | collective-permute-start | bytes 147464 | tf_op jit(solution)/shard_map/ppermute | solution.py:345
  14.1 5.8 %collective-permute-start.9 = (bf16[32,1536]{1,0:T(8,128)(2,1)S(1)}, bf16[32,1536]{1,0:T(8,128)(2,1)S(1)}, u32[]{:S(2)}, u32[]{:S(2)}) collective-permute-start(bf16[32,1536]{1,0:T(8,128)(2,1)S(1)} %get-tuple-element.53), channel_id=1, source_target_pairs={{0,2},{1,3},{2,0},{3,1},{4,6},{5,7},{6,4},{7,5},{8,10},{9,11},{10,... | collective-permute-start | bytes 294920 | tf_op jit(solution)/shard_map/ppermute | solution.py:345
  15.7 5.3 %collective-permute-start.10 = (bf16[32,1536]{1,0:T(8,128)(2,1)S(1)}, bf16[32,1536]{1,0:T(8,128)(2,1)S(1)}, u32[]{:S(2)}, u32[]{:S(2)}) collective-permute-start(bf16[32,1536]{1,0:T(8,128)(2,1)S(1)} %get-tuple-element.54), channel_id=1, source_target_pairs={{0,3},{1,2},{2,1},{3,0},{4,7},{5,6},{6,5},{7,4},{8,11},{9,10},{10,... | collective-permute-start | bytes 294920 | tf_op jit(solution)/shard_map/ppermute | solution.py:345
  16.1 4.9 %collective-permute-start.11 = (bf16[32,1536]{1,0:T(8,128)(2,1)S(1)}, bf16[32,1536]{1,0:T(8,128)(2,1)S(1)}, u32[]{:S(2)}, u32[]{:S(2)}) collective-permute-start(bf16[32,1536]{1,0:T(8,128)(2,1)S(1)} %get-tuple-element.55), channel_id=1, source_target_pairs={{0,1},{1,0},{2,3},{3,2},{4,5},{5,4},{6,7},{7,6},{8,9},{9,8},{10,11... | collective-permute-start | bytes 294920 | tf_op jit(solution)/shard_map/ppermute | solution.py:345
  18.0 6.0 %collective-permute-start.6 = (bf16[32,1536]{1,0:T(8,128)(2,1)S(1)}, bf16[32,1536]{1,0:T(8,128)(2,1)S(1)}, u32[]{:S(2)}, u32[]{:S(2)}) collective-permute-start(bf16[32,1536]{1,0:T(8,128)(2,1)S(1)} %get-tuple-element.49), channel_id=1, source_target_pairs={{0,2},{1,3},{2,0},{3,1},{4,6},{5,7},{6,4},{7,5},{8,10},{9,11},{10,... | collective-permute-start | bytes 294920 | tf_op jit(solution)/shard_map/ppermute | solution.py:345
  19.5 5.1 %collective-permute-start.7 = (bf16[32,1536]{1,0:T(8,128)(2,1)S(1)}, bf16[32,1536]{1,0:T(8,128)(2,1)S(1)}, u32[]{:S(2)}, u32[]{:S(2)}) collective-permute-start(bf16[32,1536]{1,0:T(8,128)(2,1)S(1)} %get-tuple-element.50), channel_id=1, source_target_pairs={{0,3},{1,2},{2,1},{3,0},{4,7},{5,6},{6,5},{7,4},{8,11},{9,10},{10,... | collective-permute-start | bytes 294920 | tf_op jit(solution)/shard_map/ppermute | solution.py:345
  19.9 4.7 %collective-permute-start.8 = (bf16[32,1536]{1,0:T(8,128)(2,1)S(1)}, bf16[32,1536]{1,0:T(8,128)(2,1)S(1)}, u32[]{:S(2)}, u32[]{:S(2)}) collective-permute-start(bf16[32,1536]{1,0:T(8,128)(2,1)S(1)} %get-tuple-element.51), channel_id=1, source_target_pairs={{0,1},{1,0},{2,3},{3,2},{4,5},{5,4},{6,7},{7,6},{8,9},{9,8},{10,11... | collective-permute-start | bytes 294920 | tf_op jit(solution)/shard_map/ppermute | solution.py:345
  28.8 5.7 %collective-permute-start.12 = (bf16[32,1536]{1,0:T(8,128)(2,1)S(1)}, bf16[32,1536]{1,0:T(8,128)(2,1)S(1)}, u32[]{:S(2)}, u32[]{:S(2)}) collective-permute-start(bf16[32,1536]{1,0:T(8,128)(2,1)S(1)} %get-tuple-element.60), channel_id=1, source_target_pairs={{0,2},{1,3},{2,0},{3,1},{4,6},{5,7},{6,4},{7,5},{8,10},{9,11},{10,... | collective-permute-start | bytes 294920 | tf_op jit(solution)/shard_map/ppermute | solution.py:345
  29.8 5.7 %collective-permute-start.13 = (bf16[32,1536]{1,0:T(8,128)(2,1)S(1)}, bf16[32,1536]{1,0:T(8,128)(2,1)S(1)}, u32[]{:S(2)}, u32[]{:S(2)}) collective-permute-start(bf16[32,1536]{1,0:T(8,128)(2,1)S(1)} %get-tuple-element.61), channel_id=1, source_target_pairs={{0,3},{1,2},{2,1},{3,0},{4,7},{5,6},{6,5},{7,4},{8,11},{9,10},{10,... | collective-permute-start | bytes 294920 | tf_op jit(solution)/shard_map/ppermute | solution.py:345
  30.6 4.9 %collective-permute-start.14 = (bf16[32,1536]{1,0:T(8,128)(2,1)S(1)}, bf16[32,1536]{1,0:T(8,128)(2,1)S(1)}, u32[]{:S(2)}, u32[]{:S(2)}) collective-permute-start(bf16[32,1536]{1,0:T(8,128)(2,1)S(1)} %get-tuple-element.62), channel_id=1, source_target_pairs={{0,1},{1,0},{2,3},{3,2},{4,5},{5,4},{6,7},{7,6},{8,9},{9,8},{10,11... | collective-permute-start | bytes 294920 | tf_op jit(solution)/shard_map/ppermute | solution.py:345
  32.4 6.9 %collective-permute-start.15 = (bf16[32,1536]{1,0:T(8,128)(2,1)S(1)}, bf16[32,1536]{1,0:T(8,128)(2,1)S(1)}, u32[]{:S(2)}, u32[]{:S(2)}) collective-permute-start(bf16[32,1536]{1,0:T(8,128)(2,1)S(1)} %get-tuple-element.68), channel_id=1, source_target_pairs={{0,2},{1,3},{2,0},{3,1},{4,6},{5,7},{6,4},{7,5},{8,10},{9,11},{10,... | collective-permute-start | bytes 294920 | tf_op jit(solution)/shard_map/ppermute | solution.py:345
  33.7 6.0 %collective-permute-start.16 = (bf16[32,1536]{1,0:T(8,128)(2,1)S(1)}, bf16[32,1536]{1,0:T(8,128)(2,1)S(1)}, u32[]{:S(2)}, u32[]{:S(2)}) collective-permute-start(bf16[32,1536]{1,0:T(8,128)(2,1)S(1)} %get-tuple-element.69), channel_id=1, source_target_pairs={{0,3},{1,2},{2,1},{3,0},{4,7},{5,6},{6,5},{7,4},{8,11},{9,10},{10,... | collective-permute-start | bytes 294920 | tf_op jit(solution)/shard_map/ppermute | solution.py:345
  34.5 5.2 %collective-permute-start.17 = (bf16[32,1536]{1,0:T(8,128)(2,1)S(1)}, bf16[32,1536]{1,0:T(8,128)(2,1)S(1)}, u32[]{:S(2)}, u32[]{:S(2)}) collective-permute-start(bf16[32,1536]{1,0:T(8,128)(2,1)S(1)} %get-tuple-element.70), channel_id=1, source_target_pairs={{0,1},{1,0},{2,3},{3,2},{4,5},{5,4},{6,7},{7,6},{8,9},{9,8},{10,11... | collective-permute-start | bytes 294920 | tf_op jit(solution)/shard_map/ppermute | solution.py:345
  35.7 8.7 %collective-permute-start.21 = (bf16[16,1536]{1,0:T(8,128)(2,1)S(1)}, bf16[16,1536]{1,0:T(8,128)(2,1)S(1)}, u32[]{:S(2)}, u32[]{:S(2)}) collective-permute-start(bf16[16,1536]{1,0:T(8,128)(2,1)S(1)} %get-tuple-element.76), channel_id=1, source_target_pairs={{0,12},{4,8},{8,4},{12,0},{1,13},{5,9},{9,5},{13,1},{2,14},{6,10},... | collective-permute-start | bytes 147464 | tf_op jit(solution)/shard_map/ppermute | solution.py:345
  37.9 7.8 %collective-permute-start.22 = (bf16[16,1536]{1,0:T(8,128)(2,1)S(1)}, bf16[16,1536]{1,0:T(8,128)(2,1)S(1)}, u32[]{:S(2)}, u32[]{:S(2)}) collective-permute-start(bf16[16,1536]{1,0:T(8,128)(2,1)S(1)} %get-tuple-element.77), channel_id=1, source_target_pairs={{0,8},{4,12},{8,0},{12,4},{1,9},{5,13},{9,1},{13,5},{2,10},{6,14},... | collective-permute-start | bytes 147464 | tf_op jit(solution)/shard_map/ppermute | solution.py:345
  39.9 6.3 %collective-permute-start.18 = (bf16[16,1536]{1,0:T(8,128)(2,1)S(1)}, bf16[16,1536]{1,0:T(8,128)(2,1)S(1)}, u32[]{:S(2)}, u32[]{:S(2)}) collective-permute-start(bf16[16,1536]{1,0:T(8,128)(2,1)S(1)} %get-tuple-element.72), channel_id=1, source_target_pairs={{0,12},{4,8},{8,4},{12,0},{1,13},{5,9},{9,5},{13,1},{2,14},{6,10},... | collective-permute-start | bytes 147464 | tf_op jit(solution)/shard_map/ppermute | solution.py:345
  42.5 6.9 %collective-permute-start.19 = (bf16[16,1536]{1,0:T(8,128)(2,1)S(1)}, bf16[16,1536]{1,0:T(8,128)(2,1)S(1)}, u32[]{:S(2)}, u32[]{:S(2)}) collective-permute-start(bf16[16,1536]{1,0:T(8,128)(2,1)S(1)} %get-tuple-element.73), channel_id=1, source_target_pairs={{0,8},{4,12},{8,0},{12,4},{1,9},{5,13},{9,1},{13,5},{2,10},{6,14},... | collective-permute-start | bytes 147464 | tf_op jit(solution)/shard_map/ppermute | solution.py:345
  43.7 5.7 %collective-permute-start.20 = (bf16[16,1536]{1,0:T(8,128)(2,1)S(1)}, bf16[16,1536]{1,0:T(8,128)(2,1)S(1)}, u32[]{:S(2)}, u32[]{:S(2)}) collective-permute-start(bf16[16,1536]{1,0:T(8,128)(2,1)S(1)} %get-tuple-element.74), channel_id=1, source_target_pairs={{0,4},{4,0},{8,12},{12,8},{1,5},{5,1},{9,13},{13,9},{2,6},{6,2},{1... | collective-permute-start | bytes 147464 | tf_op jit(solution)/shard_map/ppermute | solution.py:345
  44.4 5.6 %collective-permute-start.23 = (bf16[16,1536]{1,0:T(8,128)(2,1)S(1)}, bf16[16,1536]{1,0:T(8,128)(2,1)S(1)}, u32[]{:S(2)}, u32[]{:S(2)}) collective-permute-start(bf16[16,1536]{1,0:T(8,128)(2,1)S(1)} %get-tuple-element.78), channel_id=1, source_target_pairs={{0,4},{4,0},{8,12},{12,8},{1,5},{5,1},{9,13},{13,9},{2,6},{6,2},{1... | collective-permute-start | bytes 147464 | tf_op jit(solution)/shard_map/ppermute | solution.py:345

commit v22 on v21

--- a/solution.py
+++ b/solution.py
@@ -401,7 +401,7 @@
     payload = pass_on(payload, BUSY)
 
     order = even_first(experts)
-    placed = [0, *even_first(layers)[:0:-1]]
+    placed = list(range(layers))
     chunks, arrived = [], []
     for part in range(2):
         came = {j: swap(payload[part], "attn", j) for j in even_first(layers)}

time: 50.8 us -> 51 us (level)
  waiting for transfers between devices: 9.45 us -> 11 us
  starting transfers between devices: 27.1 us -> 25.7 us
    ppermute x24, waiting for transfers between devices: 9.45 us -> 11 us  [swap(): return lax.ppermute(value, axis, [(i, i ^ step) for i in range(count)])]
    ppermute x24, starting transfers between devices: 27.1 us -> 25.7 us  [swap(): return lax.ppermute(value, axis, [(i, i ^ step) for i in range(count)])]
where the time goes in v22:
time: 51 us; the launch traced here: 50.9 us
  starting transfers between devices  25.7 us (50%)
  Pallas kernels  13.9 us (27%)
  waiting for transfers between devices  11 us (22%)
    ppermute x24, starting transfers between devices, swap(): return lax.ppermute(value, axis, [(i, i ^ step) for i in range(count)])  25.7 us
    ppermute x24, waiting for transfers between devices, swap(): return lax.ppermute(value, axis, [(i, i ^ step) for i in range(count)])  11 us
    pallas_call x1, Pallas kernels, shards(): pl.pallas_call(functools.partial(middle_kernel, experts=experts), in_spec...  4.18 us
    pallas_call x1, Pallas kernels, shards(): pl.pallas_call(attend_kernel, in_specs=[SCALAR] + [ANY] * len(operands),...  3.02 us
    pallas_call x1, Pallas kernels, shards(): pl.pallas_call(functools.partial(begin_kernel, experts=experts), in_specs...  2.92 us
    pallas_call x1, Pallas kernels, shards(): pl.pallas_call(end_kernel, in_specs=[WHOLE] * 2, out_specs=[WHOLE] * expe...  1.38 us
  transfers between devices with their start and end apart: 24, of which 11 were waited for; matrix products, arithmetic and copies ran while one was open for 0% of the time, Pallas kernels for 12%

profile of v22, /device:TPU:0, one launch (start us, length us, event | category | flops | bytes accessed | tf_op | source)
XLA Modules:
  0.0 50.9 jit_solution(4776512220373519550)
XLA Ops:
  0.0 3.0 %shard_map.109 = (f32[16,3072]{1,0:T(8,128)S(1)}, bf16[16,1664]{1,0:T(8,128)(2,1)S(1)}, bf16[16,1536]{1,0:T(8,128)(2,1)S(1)}) custom-call(s32[1]{0:T(128)} %bitcast._.me_ref, s32[1,16]{1,0:T(1,128)} %bitcast.21, bf16[16,3072]{1,0:T(8,128)(2,1)} %queries_hbm.1, bf16[16,96,512]{2,1,0:T(8,128)(2,1)} %keys_hbm.1, bf16[16,96,512]{2,1,0:T(8,128)(2,1)} %values_hbm.1, ...), custom_call_target="tpu_custom_call" | custom-call | tf_op jit(solution)/shard_map/pallas_call | solution.py:389
  3.0 0.0 slice-start
  3.0 0.0 slice-start.3
  3.1 0.0 slice-start.1
  3.1 0.0 slice-start.2
  3.1 0.0 slice-start.4
  3.1 0.0 slice-start.5
  3.1 0.0 copy-start
  3.1 5.1 %collective-permute-start.2 = (bf16[16,1664]{1,0:T(8,128)(2,1)S(1)}, bf16[16,1664]{1,0:T(8,128)(2,1)S(1)}, u32[]{:S(2)}, u32[]{:S(2)}) collective-permute-start(bf16[16,1664]{1,0:T(8,128)(2,1)S(1)} %get-tuple-element.44.refs_0_), channel_id=1, source_target_pairs={{0,12},{4,8},{8,4},{12,0},{1,13},{5,9},{9,5},{13,1},{2,14},{6,10},... | collective-permute-start | bytes 159752 | tf_op jit(solution)/shard_map/ppermute | solution.py:345
  8.2 0.0 collective-permute-start.1
  8.2 0.6 %collective-permute-start = (bf16[16,1664]{1,0:T(8,128)(2,1)S(1)}, bf16[16,1664]{1,0:T(8,128)(2,1)S(1)}, u32[]{:S(2)}, u32[]{:S(2)}) collective-permute-start(bf16[16,1664]{1,0:T(8,128)(2,1)S(1)} %get-tuple-element.44.refs_0_), channel_id=1, source_target_pairs={{0,4},{4,0},{8,12},{12,8},{1,5},{5,1},{9,13},{13,9},{2,6},{6,2},{1... | collective-permute-start | bytes 159752 | tf_op jit(solution)/shard_map/ppermute | solution.py:345
  8.9 3.7 %collective-permute-start.5 = (bf16[16,1536]{1,0:T(8,128)(2,1)S(1)}, bf16[16,1536]{1,0:T(8,128)(2,1)S(1)}, u32[]{:S(2)}, u32[]{:S(2)}) collective-permute-start(bf16[16,1536]{1,0:T(8,128)(2,1)S(1)} %get-tuple-element.45.refs_4_), channel_id=1, source_target_pairs={{0,12},{4,8},{8,4},{12,0},{1,13},{5,9},{9,5},{13,1},{2,14},{6,10},... | collective-permute-start | bytes 147464 | tf_op jit(solution)/shard_map/ppermute | solution.py:345
  12.6 0.0 collective-permute-start.4
  12.6 0.0 collective-permute-done.2.refs_3_
  12.6 0.6 %collective-permute-start.3 = (bf16[16,1536]{1,0:T(8,128)(2,1)S(1)}, bf16[16,1536]{1,0:T(8,128)(2,1)S(1)}, u32[]{:S(2)}, u32[]{:S(2)}) collective-permute-start(bf16[16,1536]{1,0:T(8,128)(2,1)S(1)} %get-tuple-element.45.refs_4_), channel_id=1, source_target_pairs={{0,4},{4,0},{8,12},{12,8},{1,5},{5,1},{9,13},{13,9},{2,6},{6,2},{1... | collective-permute-start | bytes 147464 | tf_op jit(solution)/shard_map/ppermute | solution.py:345
  13.3 1.4 %collective-permute-done.1.refs_2_ = bf16[16,1664]{1,0:T(8,128)(2,1)S(1)} collective-permute-done((bf16[16,1664]{1,0:T(8,128)(2,1)S(1)}, bf16[16,1664]{1,0:T(8,128)(2,1)S(1)}, u32[]{:S(2)}, u32[]{:S(2)}) %collective-permute-start.1) | collective-permute-done | bytes 53280 | tf_op jit(solution)/shard_map/ppermute | solution.py:345
  14.7 0.0 collective-permute-done.refs_1_
  14.7 0.4 shard_map.113
  15.1 1.6 %collective-permute-start.9 = (bf16[32,1536]{1,0:T(8,128)(2,1)S(1)}, bf16[32,1536]{1,0:T(8,128)(2,1)S(1)}, u32[]{:S(2)}, u32[]{:S(2)}) collective-permute-start(bf16[32,1536]{1,0:T(8,128)(2,1)S(1)} %get-tuple-element.53), channel_id=1, source_target_pairs={{0,2},{1,3},{2,0},{3,1},{4,6},{5,7},{6,4},{7,5},{8,10},{9,11},{10,... | collective-permute-start | bytes 294920 | tf_op jit(solution)/shard_map/ppermute | solution.py:345
  16.6 0.0 collective-permute-start.10
  16.6 0.0 collective-permute-done.5.refs_7_
  16.6 0.7 %collective-permute-start.11 = (bf16[32,1536]{1,0:T(8,128)(2,1)S(1)}, bf16[32,1536]{1,0:T(8,128)(2,1)S(1)}, u32[]{:S(2)}, u32[]{:S(2)}) collective-permute-start(bf16[32,1536]{1,0:T(8,128)(2,1)S(1)} %get-tuple-element.55), channel_id=1, source_target_pairs={{0,1},{1,0},{2,3},{3,2},{4,5},{5,4},{6,7},{7,6},{8,9},{9,8},{10,11... | collective-permute-start | bytes 294920 | tf_op jit(solution)/shard_map/ppermute | solution.py:345
  17.3 0.3 collective-permute-done.4.refs_6_
  17.6 0.0 collective-permute-done.3.refs_5_
  17.6 0.4 shard_map.112
  18.0 1.6 %collective-permute-start.6 = (bf16[32,1536]{1,0:T(8,128)(2,1)S(1)}, bf16[32,1536]{1,0:T(8,128)(2,1)S(1)}, u32[]{:S(2)}, u32[]{:S(2)}) collective-permute-start(bf16[32,1536]{1,0:T(8,128)(2,1)S(1)} %get-tuple-element.49), channel_id=1, source_target_pairs={{0,2},{1,3},{2,0},{3,1},{4,6},{5,7},{6,4},{7,5},{8,10},{9,11},{10,... | collective-permute-start | bytes 294920 | tf_op jit(solution)/shard_map/ppermute | solution.py:345
  19.6 0.0 collective-permute-start.7
  19.6 0.4 shard_map.111
  20.0 0.0 collective-permute-done.9.refs_1_
  20.0 0.7 %collective-permute-start.8 = (bf16[32,1536]{1,0:T(8,128)(2,1)S(1)}, bf16[32,1536]{1,0:T(8,128)(2,1)S(1)}, u32[]{:S(2)}, u32[]{:S(2)}) collective-permute-start(bf16[32,1536]{1,0:T(8,128)(2,1)S(1)} %get-tuple-element.51), channel_id=1, source_target_pairs={{0,1},{1,0},{2,3},{3,2},{4,5},{5,4},{6,7},{7,6},{8,9},{9,8},{10,11... | collective-permute-start | bytes 294920 | tf_op jit(solution)/shard_map/ppermute | solution.py:345
  20.7 1.3 %collective-permute-done.10.refs_2_ = bf16[32,1536]{1,0:T(8,128)(2,1)S(1)} collective-permute-done((bf16[32,1536]{1,0:T(8,128)(2,1)S(1)}, bf16[32,1536]{1,0:T(8,128)(2,1)S(1)}, u32[]{:S(2)}, u32[]{:S(2)}) %collective-permute-start.10) | collective-permute-done | bytes 98336 | tf_op jit(solution)/shard_map/ppermute | solution.py:345
  21.9 0.0 collective-permute-done.11.refs_3_
  22.0 2.9 %shard_map.114 = (f32[128,2048]{1,0:T(8,128)S(1)}, f32[128,2048]{1,0:T(8,128)S(1)}, bf16[2048,1536]{1,0:T(8,128)(2,1)S(1)}) custom-call(bf16[32,1536]{1,0:T(8,128)(2,1)S(1)} %get-tuple-element.52.refs_0_, bf16[32,1536]{1,0:T(8,128)(2,1)S(1)} %collective-permute-done.9.refs_1_, bf16[32,1536]{1,0:T(8,128)(2,1)S(1)} %collective-permute-done.10.refs_2_, ...), custom_call_target="tpu_custom_call" | custom-call | flops 1610612736 | tf_op jit(solution)/shard_map/pallas_call | solution.py:433
  24.9 0.0 collective-permute-done.6.refs_1_
  24.9 1.0 %collective-permute-done.7.refs_2_ = bf16[32,1536]{1,0:T(8,128)(2,1)S(1)} collective-permute-done((bf16[32,1536]{1,0:T(8,128)(2,1)S(1)}, bf16[32,1536]{1,0:T(8,128)(2,1)S(1)}, u32[]{:S(2)}, u32[]{:S(2)}) %collective-permute-start.7) | collective-permute-done | bytes 98336 | tf_op jit(solution)/shard_map/ppermute | solution.py:345
  25.9 0.0 collective-permute-done.8.refs_3_
  25.9 4.2 %shard_map.115 = (bf16[32,1536]{1,0:T(8,128)(2,1)S(1)}, bf16[32,1536]{1,0:T(8,128)(2,1)S(1)}, bf16[32,1536]{1,0:T(8,128)(2,1)S(1)}, bf16[32,1536]{1,0:T(8,128)(2...) custom-call(bf16[32,1536]{1,0:T(8,128)(2,1)S(1)} %get-tuple-element.48.refs_0_, ...), custom_call_target="tpu_custom_call" | custom-call | tf_op jit(solution)/shard_map/pallas_call | solution.py:444
  30.1 0.6 %collective-permute-start.12 = (bf16[32,1536]{1,0:T(8,128)(2,1)S(1)}, bf16[32,1536]{1,0:T(8,128)(2,1)S(1)}, u32[]{:S(2)}, u32[]{:S(2)}) collective-permute-start(bf16[32,1536]{1,0:T(8,128)(2,1)S(1)} %get-tuple-element.60), channel_id=1, source_target_pairs={{0,2},{1,3},{2,0},{3,1},{4,6},{5,7},{6,4},{7,5},{8,10},{9,11},{10,... | collective-permute-start | bytes 294920 | tf_op jit(solution)/shard_map/ppermute | solution.py:345
  30.7 0.9 %collective-permute-start.13 = (bf16[32,1536]{1,0:T(8,128)(2,1)S(1)}, bf16[32,1536]{1,0:T(8,128)(2,1)S(1)}, u32[]{:S(2)}, u32[]{:S(2)}) collective-permute-start(bf16[32,1536]{1,0:T(8,128)(2,1)S(1)} %get-tuple-element.61), channel_id=1, source_target_pairs={{0,3},{1,2},{2,1},{3,0},{4,7},{5,6},{6,5},{7,4},{8,11},{9,10},{10,... | collective-permute-start | bytes 294920 | tf_op jit(solution)/shard_map/ppermute | solution.py:345
  31.7 0.7 %collective-permute-start.14 = (bf16[32,1536]{1,0:T(8,128)(2,1)S(1)}, bf16[32,1536]{1,0:T(8,128)(2,1)S(1)}, u32[]{:S(2)}, u32[]{:S(2)}) collective-permute-start(bf16[32,1536]{1,0:T(8,128)(2,1)S(1)} %get-tuple-element.62), channel_id=1, source_target_pairs={{0,1},{1,0},{2,3},{3,2},{4,5},{5,4},{6,7},{7,6},{8,9},{9,8},{10,11... | collective-permute-start | bytes 294920 | tf_op jit(solution)/shard_map/ppermute | solution.py:345
  32.3 1.4 %shard_map.117 = (bf16[32,1536]{1,0:T(8,128)(2,1)S(1)}, bf16[32,1536]{1,0:T(8,128)(2,1)S(1)}, bf16[32,1536]{1,0:T(8,128)(2,1)S(1)}, bf16[32,1536]{1,0:T(8,128)(2,1)S(1)}) custom-call(bf16[128,2048]{1,0:T(8,128)(2,1)S(1)} %get-tuple-element.65.hidden_ref, bf16[2048,1536]{1,0:T(8,128)(2,1)S(1)} %get-tuple-element.66.down_ref), custom_call_target="tpu_custom_call" | custom-call | flops 805306368 | tf_op jit(solution)/shard_map/pallas_call | solution.py:452
  33.7 0.9 %collective-permute-start.15 = (bf16[32,1536]{1,0:T(8,128)(2,1)S(1)}, bf16[32,1536]{1,0:T(8,128)(2,1)S(1)}, u32[]{:S(2)}, u32[]{:S(2)}) collective-permute-start(bf16[32,1536]{1,0:T(8,128)(2,1)S(1)} %get-tuple-element.68), channel_id=1, source_target_pairs={{0,2},{1,3},{2,0},{3,1},{4,6},{5,7},{6,4},{7,5},{8,10},{9,11},{10,... | collective-permute-start | bytes 294920 | tf_op jit(solution)/shard_map/ppermute | solution.py:345
  34.6 0.5 collective-permute-start.16
  35.1 0.7 %collective-permute-done.12.refs_1_ = bf16[32,1536]{1,0:T(8,128)(2,1)S(1)} collective-permute-done((bf16[32,1536]{1,0:T(8,128)(2,1)S(1)}, bf16[32,1536]{1,0:T(8,128)(2,1)S(1)}, u32[]{:S(2)}, u32[]{:S(2)}) %collective-permute-start.12) | collective-permute-done | bytes 98336 | tf_op jit(solution)/shard_map/ppermute | solution.py:345
  35.8 0.1 collective-permute-start.17
  35.9 0.4 collective-permute-done.13.refs_2_
  36.3 0.0 collective-permute-done.14.refs_3_
  36.3 0.3 shard_map.116
  36.6 2.7 %collective-permute-start.21 = (bf16[16,1536]{1,0:T(8,128)(2,1)S(1)}, bf16[16,1536]{1,0:T(8,128)(2,1)S(1)}, u32[]{:S(2)}, u32[]{:S(2)}) collective-permute-start(bf16[16,1536]{1,0:T(8,128)(2,1)S(1)} %get-tuple-element.76), channel_id=1, source_target_pairs={{0,12},{4,8},{8,4},{12,0},{1,13},{5,9},{9,5},{13,1},{2,14},{6,10},... | collective-permute-start | bytes 147464 | tf_op jit(solution)/shard_map/ppermute | solution.py:345
  39.2 0.0 collective-permute-start.22
  39.2 0.7 %collective-permute-done.15.refs_2_ = bf16[32,1536]{1,0:T(8,128)(2,1)S(1)} collective-permute-done((bf16[32,1536]{1,0:T(8,128)(2,1)S(1)}, bf16[32,1536]{1,0:T(8,128)(2,1)S(1)}, u32[]{:S(2)}, u32[]{:S(2)}) %collective-permute-start.15) | collective-permute-done | bytes 98336 | tf_op jit(solution)/shard_map/ppermute | solution.py:345
  39.9 0.8 %collective-permute-done.16.refs_3_ = bf16[32,1536]{1,0:T(8,128)(2,1)S(1)} collective-permute-done((bf16[32,1536]{1,0:T(8,128)(2,1)S(1)}, bf16[32,1536]{1,0:T(8,128)(2,1)S(1)}, u32[]{:S(2)}, u32[]{:S(2)}) %collective-permute-start.16) | collective-permute-done | bytes 98336 | tf_op jit(solution)/shard_map/ppermute | solution.py:345
  40.6 0.0 collective-permute-done.17.refs_4_
  40.6 0.3 shard_map.118
  40.9 2.7 %collective-permute-start.18 = (bf16[16,1536]{1,0:T(8,128)(2,1)S(1)}, bf16[16,1536]{1,0:T(8,128)(2,1)S(1)}, u32[]{:S(2)}, u32[]{:S(2)}) collective-permute-start(bf16[16,1536]{1,0:T(8,128)(2,1)S(1)} %get-tuple-element.72), channel_id=1, source_target_pairs={{0,12},{4,8},{8,4},{12,0},{1,13},{5,9},{9,5},{13,1},{2,14},{6,10},... | collective-permute-start | bytes 147464 | tf_op jit(solution)/shard_map/ppermute | solution.py:345
  43.6 0.0 collective-permute-start.19
  43.6 1.8 %collective-permute-start.20 = (bf16[16,1536]{1,0:T(8,128)(2,1)S(1)}, bf16[16,1536]{1,0:T(8,128)(2,1)S(1)}, u32[]{:S(2)}, u32[]{:S(2)}) collective-permute-start(bf16[16,1536]{1,0:T(8,128)(2,1)S(1)} %get-tuple-element.74), channel_id=1, source_target_pairs={{0,4},{4,0},{8,12},{12,8},{1,5},{5,1},{9,13},{13,9},{2,6},{6,2},{1... | collective-permute-start | bytes 147464 | tf_op jit(solution)/shard_map/ppermute | solution.py:345
  45.4 0.0 collective-permute-done.21.refs_5_
  45.4 0.3 collective-permute-start.23
  45.6 1.8 %collective-permute-done.18.refs_1_ = bf16[16,1536]{1,0:T(8,128)(2,1)S(1)} collective-permute-done((bf16[16,1536]{1,0:T(8,128)(2,1)S(1)}, bf16[16,1536]{1,0:T(8,128)(2,1)S(1)}, u32[]{:S(2)}, u32[]{:S(2)}) %collective-permute-start.18) | collective-permute-done | bytes 49184 | tf_op jit(solution)/shard_map/ppermute | solution.py:345
  47.4 2.0 %collective-permute-done.19.refs_2_ = bf16[16,1536]{1,0:T(8,128)(2,1)S(1)} collective-permute-done((bf16[16,1536]{1,0:T(8,128)(2,1)S(1)}, bf16[16,1536]{1,0:T(8,128)(2,1)S(1)}, u32[]{:S(2)}, u32[]{:S(2)}) %collective-permute-start.19) | collective-permute-done | bytes 49184 | tf_op jit(solution)/shard_map/ppermute | solution.py:345
  49.4 0.0 collective-permute-done.20.refs_3_
  49.4 0.7 %collective-permute-done.23.refs_7_ = bf16[16,1536]{1,0:T(8,128)(2,1)S(1)} collective-permute-done((bf16[16,1536]{1,0:T(8,128)(2,1)S(1)}, bf16[16,1536]{1,0:T(8,128)(2,1)S(1)}, u32[]{:S(2)}, u32[]{:S(2)}) %collective-permute-start.23) | collective-permute-done | bytes 49184 | tf_op jit(solution)/shard_map/ppermute | solution.py:345
  50.2 0.7 %shard_map.119 = bf16[16,3072]{1,0:T(8,128)(2,1)} custom-call(f32[16,1536]{1,0:T(8,128)S(1)} %get-tuple-element.71.refs_0_, bf16[16,1536]{1,0:T(8,128)(2,1)S(1)} %collective-permute-done.18.refs_1_, bf16[16,1536]{1,0:T(8,128)(2,1)S(1)} %collective-permute-done.19.refs_2_, bf16[16,1536]{1,0:T(8,128)(2,1)S(1)} %collective-permute-done.20.refs_3_, ...), custom_call_target="tpu_custom_call" | custom-call | tf_op jit(solution)/shard_map/pallas_call | solution.py:485
  (11 shorter events, 0.0 us)
Async XLA Ops:
  3.0 18.9 %slice-start = ((s8[12582912]{0:T(1024)(128)(4,1)}), s8[4194304]{0:T(1024)(128)(4,1)S(1)}, s32[]{:S(2)}) async-start(s8[12582912]{0:T(1024)(128)(4,1)} %bitcast.8), calls=%async_computation | async-start | bytes 8388608
  3.0 18.9 %slice-start.3 = ((s8[12582912]{0:T(1024)(128)(4,1)}), s8[4194304]{0:T(1024)(128)(4,1)S(1)}, s32[]{:S(2)}) async-start(s8[12582912]{0:T(1024)(128)(4,1)} %bitcast.12), calls=%async_computation.3 | async-start | bytes 8388608
  3.1 18.9 %slice-start.1 = ((s8[12582912]{0:T(1024)(128)(4,1)}), s8[4194304]{0:T(1024)(128)(4,1)S(1)}, s32[]{:S(2)}) async-start(s8[12582912]{0:T(1024)(128)(4,1)} %bitcast.8), calls=%async_computation.1 | async-start | bytes 8388608
  3.1 18.9 %slice-start.2 = ((s8[12582912]{0:T(1024)(128)(4,1)}), s8[4194304]{0:T(1024)(128)(4,1)S(1)}, s32[]{:S(2)}) async-start(s8[12582912]{0:T(1024)(128)(4,1)} %bitcast.8), calls=%async_computation.2 | async-start | bytes 8388608
  3.1 18.9 %slice-start.4 = ((s8[12582912]{0:T(1024)(128)(4,1)}), s8[4194304]{0:T(1024)(128)(4,1)S(1)}, s32[]{:S(2)}) async-start(s8[12582912]{0:T(1024)(128)(4,1)} %bitcast.12), calls=%async_computation.4 | async-start | bytes 8388608
  3.1 18.9 %slice-start.5 = ((s8[12582912]{0:T(1024)(128)(4,1)}), s8[4194304]{0:T(1024)(128)(4,1)S(1)}, s32[]{:S(2)}) async-start(s8[12582912]{0:T(1024)(128)(4,1)} %bitcast.12), calls=%async_computation.5 | async-start | bytes 8388608
  3.1 16.5 %copy-start = (bf16[3072,4]{0,1:T(4,128)(2,1)S(1)}, bf16[3072,4]{0,1:T(4,128)(2,1)}, u32[]{:S(2)}) copy-start(bf16[3072,4]{0,1:T(4,128)(2,1)} %param.18) | copy-start | bytes 73732
  3.1 9.5 %collective-permute-start.2 = (bf16[16,1664]{1,0:T(8,128)(2,1)S(1)}, bf16[16,1664]{1,0:T(8,128)(2,1)S(1)}, u32[]{:S(2)}, u32[]{:S(2)}) collective-permute-start(bf16[16,1664]{1,0:T(8,128)(2,1)S(1)} %get-tuple-element.44.refs_0_), channel_id=1, source_target_pairs={{0,12},{4,8},{8,4},{12,0},{1,13},{5,9},{9,5},{13,1},{2,14},{6,10},... | collective-permute-start | bytes 159752 | tf_op jit(solution)/shard_map/ppermute | solution.py:345
  8.2 6.4 %collective-permute-start.1 = (bf16[16,1664]{1,0:T(8,128)(2,1)S(1)}, bf16[16,1664]{1,0:T(8,128)(2,1)S(1)}, u32[]{:S(2)}, u32[]{:S(2)}) collective-permute-start(bf16[16,1664]{1,0:T(8,128)(2,1)S(1)} %get-tuple-element.44.refs_0_), channel_id=1, source_target_pairs={{0,8},{4,12},{8,0},{12,4},{1,9},{5,13},{9,1},{13,5},{2,10},{6,14},... | collective-permute-start | bytes 159752 | tf_op jit(solution)/shard_map/ppermute | solution.py:345
  8.2 6.4 %collective-permute-start = (bf16[16,1664]{1,0:T(8,128)(2,1)S(1)}, bf16[16,1664]{1,0:T(8,128)(2,1)S(1)}, u32[]{:S(2)}, u32[]{:S(2)}) collective-permute-start(bf16[16,1664]{1,0:T(8,128)(2,1)S(1)} %get-tuple-element.44.refs_0_), channel_id=1, source_target_pairs={{0,4},{4,0},{8,12},{12,8},{1,5},{5,1},{9,13},{13,9},{2,6},{6,2},{1... | collective-permute-start | bytes 159752 | tf_op jit(solution)/shard_map/ppermute | solution.py:345
  8.9 7.8 %collective-permute-start.5 = (bf16[16,1536]{1,0:T(8,128)(2,1)S(1)}, bf16[16,1536]{1,0:T(8,128)(2,1)S(1)}, u32[]{:S(2)}, u32[]{:S(2)}) collective-permute-start(bf16[16,1536]{1,0:T(8,128)(2,1)S(1)} %get-tuple-element.45.refs_4_), channel_id=1, source_target_pairs={{0,12},{4,8},{8,4},{12,0},{1,13},{5,9},{9,5},{13,1},{2,14},{6,10},... | collective-permute-start | bytes 147464 | tf_op jit(solution)/shard_map/ppermute | solution.py:345
  12.6 5.0 %collective-permute-start.4 = (bf16[16,1536]{1,0:T(8,128)(2,1)S(1)}, bf16[16,1536]{1,0:T(8,128)(2,1)S(1)}, u32[]{:S(2)}, u32[]{:S(2)}) collective-permute-start(bf16[16,1536]{1,0:T(8,128)(2,1)S(1)} %get-tuple-element.45.refs_4_), channel_id=1, source_target_pairs={{0,8},{4,12},{8,0},{12,4},{1,9},{5,13},{9,1},{13,5},{2,10},{6,14},... | collective-permute-start | bytes 147464 | tf_op jit(solution)/shard_map/ppermute | solution.py:345
  12.6 5.0 %collective-permute-start.3 = (bf16[16,1536]{1,0:T(8,128)(2,1)S(1)}, bf16[16,1536]{1,0:T(8,128)(2,1)S(1)}, u32[]{:S(2)}, u32[]{:S(2)}) collective-permute-start(bf16[16,1536]{1,0:T(8,128)(2,1)S(1)} %get-tuple-element.45.refs_4_), channel_id=1, source_target_pairs={{0,4},{4,0},{8,12},{12,8},{1,5},{5,1},{9,13},{13,9},{2,6},{6,2},{1... | collective-permute-start | bytes 147464 | tf_op jit(solution)/shard_map/ppermute | solution.py:345
  15.1 4.9 %collective-permute-start.9 = (bf16[32,1536]{1,0:T(8,128)(2,1)S(1)}, bf16[32,1536]{1,0:T(8,128)(2,1)S(1)}, u32[]{:S(2)}, u32[]{:S(2)}) collective-permute-start(bf16[32,1536]{1,0:T(8,128)(2,1)S(1)} %get-tuple-element.53), channel_id=1, source_target_pairs={{0,2},{1,3},{2,0},{3,1},{4,6},{5,7},{6,4},{7,5},{8,10},{9,11},{10,... | collective-permute-start | bytes 294920 | tf_op jit(solution)/shard_map/ppermute | solution.py:345
  16.6 5.3 %collective-permute-start.10 = (bf16[32,1536]{1,0:T(8,128)(2,1)S(1)}, bf16[32,1536]{1,0:T(8,128)(2,1)S(1)}, u32[]{:S(2)}, u32[]{:S(2)}) collective-permute-start(bf16[32,1536]{1,0:T(8,128)(2,1)S(1)} %get-tuple-element.54), channel_id=1, source_target_pairs={{0,3},{1,2},{2,1},{3,0},{4,7},{5,6},{6,5},{7,4},{8,11},{9,10},{10,... | collective-permute-start | bytes 294920 | tf_op jit(solution)/shard_map/ppermute | solution.py:345
  16.6 5.3 %collective-permute-start.11 = (bf16[32,1536]{1,0:T(8,128)(2,1)S(1)}, bf16[32,1536]{1,0:T(8,128)(2,1)S(1)}, u32[]{:S(2)}, u32[]{:S(2)}) collective-permute-start(bf16[32,1536]{1,0:T(8,128)(2,1)S(1)} %get-tuple-element.55), channel_id=1, source_target_pairs={{0,1},{1,0},{2,3},{3,2},{4,5},{5,4},{6,7},{7,6},{8,9},{9,8},{10,11... | collective-permute-start | bytes 294920 | tf_op jit(solution)/shard_map/ppermute | solution.py:345
  18.0 6.9 %collective-permute-start.6 = (bf16[32,1536]{1,0:T(8,128)(2,1)S(1)}, bf16[32,1536]{1,0:T(8,128)(2,1)S(1)}, u32[]{:S(2)}, u32[]{:S(2)}) collective-permute-start(bf16[32,1536]{1,0:T(8,128)(2,1)S(1)} %get-tuple-element.49), channel_id=1, source_target_pairs={{0,2},{1,3},{2,0},{3,1},{4,6},{5,7},{6,4},{7,5},{8,10},{9,11},{10,... | collective-permute-start | bytes 294920 | tf_op jit(solution)/shard_map/ppermute | solution.py:345
  19.6 6.3 %collective-permute-start.7 = (bf16[32,1536]{1,0:T(8,128)(2,1)S(1)}, bf16[32,1536]{1,0:T(8,128)(2,1)S(1)}, u32[]{:S(2)}, u32[]{:S(2)}) collective-permute-start(bf16[32,1536]{1,0:T(8,128)(2,1)S(1)} %get-tuple-element.50), channel_id=1, source_target_pairs={{0,3},{1,2},{2,1},{3,0},{4,7},{5,6},{6,5},{7,4},{8,11},{9,10},{10,... | collective-permute-start | bytes 294920 | tf_op jit(solution)/shard_map/ppermute | solution.py:345
  20.0 6.0 %collective-permute-start.8 = (bf16[32,1536]{1,0:T(8,128)(2,1)S(1)}, bf16[32,1536]{1,0:T(8,128)(2,1)S(1)}, u32[]{:S(2)}, u32[]{:S(2)}) collective-permute-start(bf16[32,1536]{1,0:T(8,128)(2,1)S(1)} %get-tuple-element.51), channel_id=1, source_target_pairs={{0,1},{1,0},{2,3},{3,2},{4,5},{5,4},{6,7},{7,6},{8,9},{9,8},{10,11... | collective-permute-start | bytes 294920 | tf_op jit(solution)/shard_map/ppermute | solution.py:345
  30.1 5.7 %collective-permute-start.12 = (bf16[32,1536]{1,0:T(8,128)(2,1)S(1)}, bf16[32,1536]{1,0:T(8,128)(2,1)S(1)}, u32[]{:S(2)}, u32[]{:S(2)}) collective-permute-start(bf16[32,1536]{1,0:T(8,128)(2,1)S(1)} %get-tuple-element.60), channel_id=1, source_target_pairs={{0,2},{1,3},{2,0},{3,1},{4,6},{5,7},{6,4},{7,5},{8,10},{9,11},{10,... | collective-permute-start | bytes 294920 | tf_op jit(solution)/shard_map/ppermute | solution.py:345
  30.7 5.6 %collective-permute-start.13 = (bf16[32,1536]{1,0:T(8,128)(2,1)S(1)}, bf16[32,1536]{1,0:T(8,128)(2,1)S(1)}, u32[]{:S(2)}, u32[]{:S(2)}) collective-permute-start(bf16[32,1536]{1,0:T(8,128)(2,1)S(1)} %get-tuple-element.61), channel_id=1, source_target_pairs={{0,3},{1,2},{2,1},{3,0},{4,7},{5,6},{6,5},{7,4},{8,11},{9,10},{10,... | collective-permute-start | bytes 294920 | tf_op jit(solution)/shard_map/ppermute | solution.py:345
  31.7 4.6 %collective-permute-start.14 = (bf16[32,1536]{1,0:T(8,128)(2,1)S(1)}, bf16[32,1536]{1,0:T(8,128)(2,1)S(1)}, u32[]{:S(2)}, u32[]{:S(2)}) collective-permute-start(bf16[32,1536]{1,0:T(8,128)(2,1)S(1)} %get-tuple-element.62), channel_id=1, source_target_pairs={{0,1},{1,0},{2,3},{3,2},{4,5},{5,4},{6,7},{7,6},{8,9},{9,8},{10,11... | collective-permute-start | bytes 294920 | tf_op jit(solution)/shard_map/ppermute | solution.py:345
  33.7 6.2 %collective-permute-start.15 = (bf16[32,1536]{1,0:T(8,128)(2,1)S(1)}, bf16[32,1536]{1,0:T(8,128)(2,1)S(1)}, u32[]{:S(2)}, u32[]{:S(2)}) collective-permute-start(bf16[32,1536]{1,0:T(8,128)(2,1)S(1)} %get-tuple-element.68), channel_id=1, source_target_pairs={{0,2},{1,3},{2,0},{3,1},{4,6},{5,7},{6,4},{7,5},{8,10},{9,11},{10,... | collective-permute-start | bytes 294920 | tf_op jit(solution)/shard_map/ppermute | solution.py:345
  34.6 6.0 %collective-permute-start.16 = (bf16[32,1536]{1,0:T(8,128)(2,1)S(1)}, bf16[32,1536]{1,0:T(8,128)(2,1)S(1)}, u32[]{:S(2)}, u32[]{:S(2)}) collective-permute-start(bf16[32,1536]{1,0:T(8,128)(2,1)S(1)} %get-tuple-element.69), channel_id=1, source_target_pairs={{0,3},{1,2},{2,1},{3,0},{4,7},{5,6},{6,5},{7,4},{8,11},{9,10},{10,... | collective-permute-start | bytes 294920 | tf_op jit(solution)/shard_map/ppermute | solution.py:345
  35.8 4.8 %collective-permute-start.17 = (bf16[32,1536]{1,0:T(8,128)(2,1)S(1)}, bf16[32,1536]{1,0:T(8,128)(2,1)S(1)}, u32[]{:S(2)}, u32[]{:S(2)}) collective-permute-start(bf16[32,1536]{1,0:T(8,128)(2,1)S(1)} %get-tuple-element.70), channel_id=1, source_target_pairs={{0,1},{1,0},{2,3},{3,2},{4,5},{5,4},{6,7},{7,6},{8,9},{9,8},{10,11... | collective-permute-start | bytes 294920 | tf_op jit(solution)/shard_map/ppermute | solution.py:345
  36.6 8.8 %collective-permute-start.21 = (bf16[16,1536]{1,0:T(8,128)(2,1)S(1)}, bf16[16,1536]{1,0:T(8,128)(2,1)S(1)}, u32[]{:S(2)}, u32[]{:S(2)}) collective-permute-start(bf16[16,1536]{1,0:T(8,128)(2,1)S(1)} %get-tuple-element.76), channel_id=1, source_target_pairs={{0,12},{4,8},{8,4},{12,0},{1,13},{5,9},{9,5},{13,1},{2,14},{6,10},... | collective-permute-start | bytes 147464 | tf_op jit(solution)/shard_map/ppermute | solution.py:345
  39.2 6.4 %collective-permute-start.22 = (bf16[16,1536]{1,0:T(8,128)(2,1)S(1)}, bf16[16,1536]{1,0:T(8,128)(2,1)S(1)}, u32[]{:S(2)}, u32[]{:S(2)}) collective-permute-start(bf16[16,1536]{1,0:T(8,128)(2,1)S(1)} %get-tuple-element.77), channel_id=1, source_target_pairs={{0,8},{4,12},{8,0},{12,4},{1,9},{5,13},{9,1},{13,5},{2,10},{6,14},... | collective-permute-start | bytes 147464 | tf_op jit(solution)/shard_map/ppermute | solution.py:345
  40.9 6.5 %collective-permute-start.18 = (bf16[16,1536]{1,0:T(8,128)(2,1)S(1)}, bf16[16,1536]{1,0:T(8,128)(2,1)S(1)}, u32[]{:S(2)}, u32[]{:S(2)}) collective-permute-start(bf16[16,1536]{1,0:T(8,128)(2,1)S(1)} %get-tuple-element.72), channel_id=1, source_target_pairs={{0,12},{4,8},{8,4},{12,0},{1,13},{5,9},{9,5},{13,1},{2,14},{6,10},... | collective-permute-start | bytes 147464 | tf_op jit(solution)/shard_map/ppermute | solution.py:345
  43.6 5.8 %collective-permute-start.19 = (bf16[16,1536]{1,0:T(8,128)(2,1)S(1)}, bf16[16,1536]{1,0:T(8,128)(2,1)S(1)}, u32[]{:S(2)}, u32[]{:S(2)}) collective-permute-start(bf16[16,1536]{1,0:T(8,128)(2,1)S(1)} %get-tuple-element.73), channel_id=1, source_target_pairs={{0,8},{4,12},{8,0},{12,4},{1,9},{5,13},{9,1},{13,5},{2,10},{6,14},... | collective-permute-start | bytes 147464 | tf_op jit(solution)/shard_map/ppermute | solution.py:345
  43.6 5.8 %collective-permute-start.20 = (bf16[16,1536]{1,0:T(8,128)(2,1)S(1)}, bf16[16,1536]{1,0:T(8,128)(2,1)S(1)}, u32[]{:S(2)}, u32[]{:S(2)}) collective-permute-start(bf16[16,1536]{1,0:T(8,128)(2,1)S(1)} %get-tuple-element.74), channel_id=1, source_target_pairs={{0,4},{4,0},{8,12},{12,8},{1,5},{5,1},{9,13},{13,9},{2,6},{6,2},{1... | collective-permute-start | bytes 147464 | tf_op jit(solution)/shard_map/ppermute | solution.py:345
  45.4 4.8 %collective-permute-start.23 = (bf16[16,1536]{1,0:T(8,128)(2,1)S(1)}, bf16[16,1536]{1,0:T(8,128)(2,1)S(1)}, u32[]{:S(2)}, u32[]{:S(2)}) collective-permute-start(bf16[16,1536]{1,0:T(8,128)(2,1)S(1)} %get-tuple-element.78), channel_id=1, source_target_pairs={{0,4},{4,0},{8,12},{12,8},{1,5},{5,1},{9,13},{13,9},{2,6},{6,2},{1... | collective-permute-start | bytes 147464 | tf_op jit(solution)/shard_map/ppermute | solution.py:345

commit v23 on v17

--- a/solution.py
+++ b/solution.py
@@ -16,7 +16,7 @@
 BLOCK = 8
 STRIPS = 3
 TILE = 256
-UNROLL = 2
+UNROLL = 4
 MIB = 1 << 20
 F32 = jnp.float32
 BF16 = jnp.bfloat16
@@ -245,8 +245,11 @@
 
 
 def tiles(count, tile):
+    steps = count // tile
+    unroll = max(u for u in range(1, UNROLL + 1) if steps % u == 0)
+
     def run(body):
-        @pl.loop(0, count // tile, unroll=UNROLL)
+        @pl.loop(0, steps, unroll=unroll)
         def _(i):
             body(pl.ds(pl.multiple_of(i * tile, tile), tile))
 

time: 50.1 us -> 49.8 us (level)
  Pallas kernels: 13.8 us -> 13.1 us
where the time goes in v23:
time: 49.8 us; the launch traced here: 49.6 us
  starting transfers between devices  26.4 us (53%)
  Pallas kernels  13.1 us (26%)
  waiting for transfers between devices  9.86 us (20%)
    ppermute x24, starting transfers between devices, swap(): return lax.ppermute(value, axis, [(i, i ^ step) for i in range(count)])  26.4 us
    ppermute x24, waiting for transfers between devices, swap(): return lax.ppermute(value, axis, [(i, i ^ step) for i in range(count)])  9.86 us
    pallas_call x1, Pallas kernels, shards(): pl.pallas_call(functools.partial(middle_kernel, experts=experts), in_spec...  3.7 us
    pallas_call x1, Pallas kernels, shards(): pl.pallas_call(attend_kernel, in_specs=[SCALAR] + [ANY] * len(operands),...  2.95 us
    pallas_call x1, Pallas kernels, shards(): pl.pallas_call(functools.partial(begin_kernel, experts=experts), in_specs...  2.92 us
    pallas_call x1, Pallas kernels, shards(): pl.pallas_call(end_kernel, in_specs=[WHOLE] * 2, out_specs=[WHOLE] * expe...  1.22 us
  transfers between devices with their start and end apart: 24, of which 9 were waited for; matrix products, arithmetic and copies ran while one was open for 0% of the time, Pallas kernels for 12%

profile of v23, /device:TPU:0, one launch (start us, length us, event | category | flops | bytes accessed | tf_op | source)
XLA Modules:
  0.0 49.6 jit_solution(17391812082283896692)
XLA Ops:
  0.0 2.9 %shard_map.109 = (f32[16,3072]{1,0:T(8,128)S(1)}, bf16[16,1664]{1,0:T(8,128)(2,1)S(1)}, bf16[16,1536]{1,0:T(8,128)(2,1)S(1)}) custom-call(s32[1]{0:T(128)} %bitcast._.me_ref, s32[1,16]{1,0:T(1,128)} %bitcast.21, bf16[16,3072]{1,0:T(8,128)(2,1)} %queries_hbm.1, bf16[16,96,512]{2,1,0:T(8,128)(2,1)} %keys_hbm.1, bf16[16,96,512]{2,1,0:T(8,128)(2,1)} %values_hbm.1, ...), custom_call_target="tpu_custom_call" | custom-call | tf_op jit(solution)/shard_map/pallas_call | solution.py:390
  3.0 0.0 slice-start
  3.0 0.0 slice-start.3
  3.0 0.0 slice-start.1
  3.0 0.0 slice-start.2
  3.0 0.0 slice-start.4
  3.0 0.0 slice-start.5
  3.0 0.0 copy-start
  3.0 5.1 %collective-permute-start.2 = (bf16[16,1664]{1,0:T(8,128)(2,1)S(1)}, bf16[16,1664]{1,0:T(8,128)(2,1)S(1)}, u32[]{:S(2)}, u32[]{:S(2)}) collective-permute-start(bf16[16,1664]{1,0:T(8,128)(2,1)S(1)} %get-tuple-element.43.refs_0_), channel_id=1, source_target_pairs={{0,12},{4,8},{8,4},{12,0},{1,13},{5,9},{9,5},{13,1},{2,14},{6,10},... | collective-permute-start | bytes 159752 | tf_op jit(solution)/shard_map/ppermute | solution.py:346
  8.2 0.0 collective-permute-start.1
  8.2 0.6 %collective-permute-start = (bf16[16,1664]{1,0:T(8,128)(2,1)S(1)}, bf16[16,1664]{1,0:T(8,128)(2,1)S(1)}, u32[]{:S(2)}, u32[]{:S(2)}) collective-permute-start(bf16[16,1664]{1,0:T(8,128)(2,1)S(1)} %get-tuple-element.43.refs_0_), channel_id=1, source_target_pairs={{0,4},{4,0},{8,12},{12,8},{1,5},{5,1},{9,13},{13,9},{2,6},{6,2},{1... | collective-permute-start | bytes 159752 | tf_op jit(solution)/shard_map/ppermute | solution.py:346
  8.8 3.7 %collective-permute-start.5 = (bf16[16,1536]{1,0:T(8,128)(2,1)S(1)}, bf16[16,1536]{1,0:T(8,128)(2,1)S(1)}, u32[]{:S(2)}, u32[]{:S(2)}) collective-permute-start(bf16[16,1536]{1,0:T(8,128)(2,1)S(1)} %get-tuple-element.44.refs_4_), channel_id=1, source_target_pairs={{0,12},{4,8},{8,4},{12,0},{1,13},{5,9},{9,5},{13,1},{2,14},{6,10},... | collective-permute-start | bytes 147464 | tf_op jit(solution)/shard_map/ppermute | solution.py:346
  12.5 0.0 collective-permute-start.4
  12.5 0.0 collective-permute-done.2.refs_3_
  12.6 0.6 %collective-permute-start.3 = (bf16[16,1536]{1,0:T(8,128)(2,1)S(1)}, bf16[16,1536]{1,0:T(8,128)(2,1)S(1)}, u32[]{:S(2)}, u32[]{:S(2)}) collective-permute-start(bf16[16,1536]{1,0:T(8,128)(2,1)S(1)} %get-tuple-element.44.refs_4_), channel_id=1, source_target_pairs={{0,4},{4,0},{8,12},{12,8},{1,5},{5,1},{9,13},{13,9},{2,6},{6,2},{1... | collective-permute-start | bytes 147464 | tf_op jit(solution)/shard_map/ppermute | solution.py:346
  13.2 1.4 %collective-permute-done.1.refs_2_ = bf16[16,1664]{1,0:T(8,128)(2,1)S(1)} collective-permute-done((bf16[16,1664]{1,0:T(8,128)(2,1)S(1)}, bf16[16,1664]{1,0:T(8,128)(2,1)S(1)}, u32[]{:S(2)}, u32[]{:S(2)}) %collective-permute-start.1) | collective-permute-done | bytes 53280 | tf_op jit(solution)/shard_map/ppermute | solution.py:346
  14.6 0.0 collective-permute-done.refs_1_
  14.6 0.4 shard_map.113
  15.0 1.6 %collective-permute-start.9 = (bf16[32,1536]{1,0:T(8,128)(2,1)S(1)}, bf16[32,1536]{1,0:T(8,128)(2,1)S(1)}, u32[]{:S(2)}, u32[]{:S(2)}) collective-permute-start(bf16[32,1536]{1,0:T(8,128)(2,1)S(1)} %get-tuple-element.52), channel_id=1, source_target_pairs={{0,2},{1,3},{2,0},{3,1},{4,6},{5,7},{6,4},{7,5},{8,10},{9,11},{10,... | collective-permute-start | bytes 294920 | tf_op jit(solution)/shard_map/ppermute | solution.py:346
  16.6 0.0 collective-permute-start.10
  16.6 0.0 collective-permute-done.5.refs_7_
  16.6 0.6 %collective-permute-start.11 = (bf16[32,1536]{1,0:T(8,128)(2,1)S(1)}, bf16[32,1536]{1,0:T(8,128)(2,1)S(1)}, u32[]{:S(2)}, u32[]{:S(2)}) collective-permute-start(bf16[32,1536]{1,0:T(8,128)(2,1)S(1)} %get-tuple-element.54), channel_id=1, source_target_pairs={{0,1},{1,0},{2,3},{3,2},{4,5},{5,4},{6,7},{7,6},{8,9},{9,8},{10,11... | collective-permute-start | bytes 294920 | tf_op jit(solution)/shard_map/ppermute | solution.py:346
  17.2 0.3 collective-permute-done.4.refs_6_
  17.5 0.0 collective-permute-done.3.refs_5_
  17.5 0.4 shard_map.112
  17.9 1.6 %collective-permute-start.6 = (bf16[32,1536]{1,0:T(8,128)(2,1)S(1)}, bf16[32,1536]{1,0:T(8,128)(2,1)S(1)}, u32[]{:S(2)}, u32[]{:S(2)}) collective-permute-start(bf16[32,1536]{1,0:T(8,128)(2,1)S(1)} %get-tuple-element.48), channel_id=1, source_target_pairs={{0,2},{1,3},{2,0},{3,1},{4,6},{5,7},{6,4},{7,5},{8,10},{9,11},{10,... | collective-permute-start | bytes 294920 | tf_op jit(solution)/shard_map/ppermute | solution.py:346
  19.5 0.0 collective-permute-start.7
  19.5 0.4 shard_map.111
  19.9 0.0 collective-permute-done.9.refs_1_
  19.9 0.7 %collective-permute-start.8 = (bf16[32,1536]{1,0:T(8,128)(2,1)S(1)}, bf16[32,1536]{1,0:T(8,128)(2,1)S(1)}, u32[]{:S(2)}, u32[]{:S(2)}) collective-permute-start(bf16[32,1536]{1,0:T(8,128)(2,1)S(1)} %get-tuple-element.50), channel_id=1, source_target_pairs={{0,1},{1,0},{2,3},{3,2},{4,5},{5,4},{6,7},{7,6},{8,9},{9,8},{10,11... | collective-permute-start | bytes 294920 | tf_op jit(solution)/shard_map/ppermute | solution.py:346
  20.6 1.3 %collective-permute-done.10.refs_2_ = bf16[32,1536]{1,0:T(8,128)(2,1)S(1)} collective-permute-done((bf16[32,1536]{1,0:T(8,128)(2,1)S(1)}, bf16[32,1536]{1,0:T(8,128)(2,1)S(1)}, u32[]{:S(2)}, u32[]{:S(2)}) %collective-permute-start.10) | collective-permute-done | bytes 98336 | tf_op jit(solution)/shard_map/ppermute | solution.py:346
  21.9 0.0 collective-permute-done.11.refs_3_
  21.9 2.9 %shard_map.114 = (f32[128,2048]{1,0:T(8,128)S(1)}, f32[128,2048]{1,0:T(8,128)S(1)}, bf16[2048,1536]{1,0:T(8,128)(2,1)S(1)}) custom-call(bf16[32,1536]{1,0:T(8,128)(2,1)S(1)} %get-tuple-element.51.refs_0_, bf16[32,1536]{1,0:T(8,128)(2,1)S(1)} %collective-permute-done.9.refs_1_, bf16[32,1536]{1,0:T(8,128)(2,1)S(1)} %collective-permute-done.10.refs_2_, ...), custom_call_target="tpu_custom_call" | custom-call | flops 1610612736 | tf_op jit(solution)/shard_map/pallas_call | solution.py:433
  24.8 0.0 collective-permute-done.6.refs_1_
  24.9 1.0 %collective-permute-done.7.refs_2_ = bf16[32,1536]{1,0:T(8,128)(2,1)S(1)} collective-permute-done((bf16[32,1536]{1,0:T(8,128)(2,1)S(1)}, bf16[32,1536]{1,0:T(8,128)(2,1)S(1)}, u32[]{:S(2)}, u32[]{:S(2)}) %collective-permute-start.7) | collective-permute-done | bytes 98336 | tf_op jit(solution)/shard_map/ppermute | solution.py:346
  25.9 0.0 collective-permute-done.8.refs_3_
  25.9 3.7 %shard_map.115 = (bf16[32,1536]{1,0:T(8,128)(2,1)S(1)}, bf16[32,1536]{1,0:T(8,128)(2,1)S(1)}, bf16[32,1536]{1,0:T(8,128)(2,1)S(1)}, bf16[32,1536]{1,0:T(8,128)(2...) custom-call(bf16[32,1536]{1,0:T(8,128)(2,1)S(1)} %get-tuple-element.47.refs_0_, ...), custom_call_target="tpu_custom_call" | custom-call | tf_op jit(solution)/shard_map/pallas_call | solution.py:444
  29.6 0.6 %collective-permute-start.12 = (bf16[32,1536]{1,0:T(8,128)(2,1)S(1)}, bf16[32,1536]{1,0:T(8,128)(2,1)S(1)}, u32[]{:S(2)}, u32[]{:S(2)}) collective-permute-start(bf16[32,1536]{1,0:T(8,128)(2,1)S(1)} %get-tuple-element.59), channel_id=1, source_target_pairs={{0,2},{1,3},{2,0},{3,1},{4,6},{5,7},{6,4},{7,5},{8,10},{9,11},{10,... | collective-permute-start | bytes 294920 | tf_op jit(solution)/shard_map/ppermute | solution.py:346
  30.2 0.9 %collective-permute-start.13 = (bf16[32,1536]{1,0:T(8,128)(2,1)S(1)}, bf16[32,1536]{1,0:T(8,128)(2,1)S(1)}, u32[]{:S(2)}, u32[]{:S(2)}) collective-permute-start(bf16[32,1536]{1,0:T(8,128)(2,1)S(1)} %get-tuple-element.60), channel_id=1, source_target_pairs={{0,3},{1,2},{2,1},{3,0},{4,7},{5,6},{6,5},{7,4},{8,11},{9,10},{10,... | collective-permute-start | bytes 294920 | tf_op jit(solution)/shard_map/ppermute | solution.py:346
  31.1 0.7 %collective-permute-start.14 = (bf16[32,1536]{1,0:T(8,128)(2,1)S(1)}, bf16[32,1536]{1,0:T(8,128)(2,1)S(1)}, u32[]{:S(2)}, u32[]{:S(2)}) collective-permute-start(bf16[32,1536]{1,0:T(8,128)(2,1)S(1)} %get-tuple-element.61), channel_id=1, source_target_pairs={{0,1},{1,0},{2,3},{3,2},{4,5},{5,4},{6,7},{7,6},{8,9},{9,8},{10,11... | collective-permute-start | bytes 294920 | tf_op jit(solution)/shard_map/ppermute | solution.py:346
  31.8 1.2 %shard_map.118 = (bf16[32,1536]{1,0:T(8,128)(2,1)S(1)}, bf16[32,1536]{1,0:T(8,128)(2,1)S(1)}, bf16[32,1536]{1,0:T(8,128)(2,1)S(1)}, bf16[32,1536]{1,0:T(8,128)(2,1)S(1)}) custom-call(bf16[128,2048]{1,0:T(8,128)(2,1)S(1)} %get-tuple-element.67.hidden_ref, bf16[2048,1536]{1,0:T(8,128)(2,1)S(1)} %get-tuple-element.68.down_ref), custom_call_target="tpu_custom_call" | custom-call | flops 805306368 | tf_op jit(solution)/shard_map/pallas_call | solution.py:452
  33.0 0.9 %collective-permute-start.18 = (bf16[32,1536]{1,0:T(8,128)(2,1)S(1)}, bf16[32,1536]{1,0:T(8,128)(2,1)S(1)}, u32[]{:S(2)}, u32[]{:S(2)}) collective-permute-start(bf16[32,1536]{1,0:T(8,128)(2,1)S(1)} %get-tuple-element.70), channel_id=1, source_target_pairs={{0,2},{1,3},{2,0},{3,1},{4,6},{5,7},{6,4},{7,5},{8,10},{9,11},{10,... | collective-permute-start | bytes 294920 | tf_op jit(solution)/shard_map/ppermute | solution.py:346
  33.9 0.5 %collective-permute-start.19 = (bf16[32,1536]{1,0:T(8,128)(2,1)S(1)}, bf16[32,1536]{1,0:T(8,128)(2,1)S(1)}, u32[]{:S(2)}, u32[]{:S(2)}) collective-permute-start(bf16[32,1536]{1,0:T(8,128)(2,1)S(1)} %get-tuple-element.71), channel_id=1, source_target_pairs={{0,3},{1,2},{2,1},{3,0},{4,7},{5,6},{6,5},{7,4},{8,11},{9,10},{10,... | collective-permute-start | bytes 294920 | tf_op jit(solution)/shard_map/ppermute | solution.py:346
  34.4 0.8 %collective-permute-done.12.refs_1_ = bf16[32,1536]{1,0:T(8,128)(2,1)S(1)} collective-permute-done((bf16[32,1536]{1,0:T(8,128)(2,1)S(1)}, bf16[32,1536]{1,0:T(8,128)(2,1)S(1)}, u32[]{:S(2)}, u32[]{:S(2)}) %collective-permute-start.12) | collective-permute-done | bytes 98336 | tf_op jit(solution)/shard_map/ppermute | solution.py:346
  35.3 0.0 collective-permute-start.20
  35.3 0.4 collective-permute-done.13.refs_2_
  35.7 0.0 collective-permute-done.14.refs_3_
  35.7 0.3 shard_map.116
  36.0 2.7 %collective-permute-start.15 = (bf16[16,1536]{1,0:T(8,128)(2,1)S(1)}, bf16[16,1536]{1,0:T(8,128)(2,1)S(1)}, u32[]{:S(2)}, u32[]{:S(2)}) collective-permute-start(bf16[16,1536]{1,0:T(8,128)(2,1)S(1)} %get-tuple-element.64), channel_id=1, source_target_pairs={{0,12},{4,8},{8,4},{12,0},{1,13},{5,9},{9,5},{13,1},{2,14},{6,10},... | collective-permute-start | bytes 147464 | tf_op jit(solution)/shard_map/ppermute | solution.py:346
  38.7 0.0 collective-permute-start.16
  38.7 0.8 %collective-permute-done.18.refs_1_ = bf16[32,1536]{1,0:T(8,128)(2,1)S(1)} collective-permute-done((bf16[32,1536]{1,0:T(8,128)(2,1)S(1)}, bf16[32,1536]{1,0:T(8,128)(2,1)S(1)}, u32[]{:S(2)}, u32[]{:S(2)}) %collective-permute-start.18) | collective-permute-done | bytes 98336 | tf_op jit(solution)/shard_map/ppermute | solution.py:346
  39.5 1.0 %collective-permute-start.17 = (bf16[16,1536]{1,0:T(8,128)(2,1)S(1)}, bf16[16,1536]{1,0:T(8,128)(2,1)S(1)}, u32[]{:S(2)}, u32[]{:S(2)}) collective-permute-start(bf16[16,1536]{1,0:T(8,128)(2,1)S(1)} %get-tuple-element.66), channel_id=1, source_target_pairs={{0,4},{4,0},{8,12},{12,8},{1,5},{5,1},{9,13},{13,9},{2,6},{6,2},{1... | collective-permute-start | bytes 147464 | tf_op jit(solution)/shard_map/ppermute | solution.py:346
  40.4 0.0 collective-permute-done.19.refs_2_
  40.4 0.0 collective-permute-done.20.refs_3_
  40.5 0.3 shard_map.119
  40.7 2.7 %collective-permute-start.21 = (bf16[16,1536]{1,0:T(8,128)(2,1)S(1)}, bf16[16,1536]{1,0:T(8,128)(2,1)S(1)}, u32[]{:S(2)}, u32[]{:S(2)}) collective-permute-start(bf16[16,1536]{1,0:T(8,128)(2,1)S(1)} %get-tuple-element.74), channel_id=1, source_target_pairs={{0,12},{4,8},{8,4},{12,0},{1,13},{5,9},{9,5},{13,1},{2,14},{6,10},... | collective-permute-start | bytes 147464 | tf_op jit(solution)/shard_map/ppermute | solution.py:346
  43.4 0.0 collective-permute-start.22
  43.4 0.0 collective-permute-done.15.refs_1_
  43.4 1.8 %collective-permute-start.23 = (bf16[16,1536]{1,0:T(8,128)(2,1)S(1)}, bf16[16,1536]{1,0:T(8,128)(2,1)S(1)}, u32[]{:S(2)}, u32[]{:S(2)}) collective-permute-start(bf16[16,1536]{1,0:T(8,128)(2,1)S(1)} %get-tuple-element.76), channel_id=1, source_target_pairs={{0,4},{4,0},{8,12},{12,8},{1,5},{5,1},{9,13},{13,9},{2,6},{6,2},{1... | collective-permute-start | bytes 147464 | tf_op jit(solution)/shard_map/ppermute | solution.py:346
  45.2 0.0 collective-permute-done.16.refs_2_
  45.2 0.0 collective-permute-done.17.refs_3_
  45.2 2.0 %collective-permute-done.21.refs_2_ = bf16[16,1536]{1,0:T(8,128)(2,1)S(1)} collective-permute-done((bf16[16,1536]{1,0:T(8,128)(2,1)S(1)}, bf16[16,1536]{1,0:T(8,128)(2,1)S(1)}, u32[]{:S(2)}, u32[]{:S(2)}) %collective-permute-start.21) | collective-permute-done | bytes 49184 | tf_op jit(solution)/shard_map/ppermute | solution.py:346
  47.2 1.8 %collective-permute-done.22.refs_3_ = bf16[16,1536]{1,0:T(8,128)(2,1)S(1)} collective-permute-done((bf16[16,1536]{1,0:T(8,128)(2,1)S(1)}, bf16[16,1536]{1,0:T(8,128)(2,1)S(1)}, u32[]{:S(2)}, u32[]{:S(2)}) %collective-permute-start.22) | collective-permute-done | bytes 49184 | tf_op jit(solution)/shard_map/ppermute | solution.py:346
  49.0 0.7 %shard_map.120 = bf16[16,3072]{1,0:T(8,128)(2,1)} custom-call(bf16[16,1536]{1,0:T(8,128)(2,1)S(1)} %shard_map.117.refs_0_, f32[16,1536]{1,0:T(8,128)S(1)} %get-tuple-element.73.refs_1_, bf16[16,1536]{1,0:T(8,128)(2,1)S(1)} %collective-permute-done.21.refs_2_, bf16[16,1536]{1,0:T(8,128)(2,1)S(1)} %collective-permute-done.22.refs_3_, ...), custom_call_target="tpu_custom_call" | custom-call | tf_op jit(solution)/shard_map/pallas_call | solution.py:476
  (12 shorter events, 0.0 us)
Async XLA Ops:
  3.0 18.9 %slice-start = ((s8[12582912]{0:T(1024)(128)(4,1)}), s8[4194304]{0:T(1024)(128)(4,1)S(1)}, s32[]{:S(2)}) async-start(s8[12582912]{0:T(1024)(128)(4,1)} %bitcast.8), calls=%async_computation | async-start | bytes 8388608
  3.0 18.9 %slice-start.3 = ((s8[12582912]{0:T(1024)(128)(4,1)}), s8[4194304]{0:T(1024)(128)(4,1)S(1)}, s32[]{:S(2)}) async-start(s8[12582912]{0:T(1024)(128)(4,1)} %bitcast.12), calls=%async_computation.3 | async-start | bytes 8388608
  3.0 18.9 %slice-start.1 = ((s8[12582912]{0:T(1024)(128)(4,1)}), s8[4194304]{0:T(1024)(128)(4,1)S(1)}, s32[]{:S(2)}) async-start(s8[12582912]{0:T(1024)(128)(4,1)} %bitcast.8), calls=%async_computation.1 | async-start | bytes 8388608
  3.0 18.9 %slice-start.2 = ((s8[12582912]{0:T(1024)(128)(4,1)}), s8[4194304]{0:T(1024)(128)(4,1)S(1)}, s32[]{:S(2)}) async-start(s8[12582912]{0:T(1024)(128)(4,1)} %bitcast.8), calls=%async_computation.2 | async-start | bytes 8388608
  3.0 18.9 %slice-start.4 = ((s8[12582912]{0:T(1024)(128)(4,1)}), s8[4194304]{0:T(1024)(128)(4,1)S(1)}, s32[]{:S(2)}) async-start(s8[12582912]{0:T(1024)(128)(4,1)} %bitcast.12), calls=%async_computation.4 | async-start | bytes 8388608
  3.0 18.9 %slice-start.5 = ((s8[12582912]{0:T(1024)(128)(4,1)}), s8[4194304]{0:T(1024)(128)(4,1)S(1)}, s32[]{:S(2)}) async-start(s8[12582912]{0:T(1024)(128)(4,1)} %bitcast.12), calls=%async_computation.5 | async-start | bytes 8388608
  3.0 16.5 %copy-start = (bf16[3072,4]{0,1:T(4,128)(2,1)S(1)}, bf16[3072,4]{0,1:T(4,128)(2,1)}, u32[]{:S(2)}) copy-start(bf16[3072,4]{0,1:T(4,128)(2,1)} %param.18) | copy-start | bytes 73732
  3.0 9.5 %collective-permute-start.2 = (bf16[16,1664]{1,0:T(8,128)(2,1)S(1)}, bf16[16,1664]{1,0:T(8,128)(2,1)S(1)}, u32[]{:S(2)}, u32[]{:S(2)}) collective-permute-start(bf16[16,1664]{1,0:T(8,128)(2,1)S(1)} %get-tuple-element.43.refs_0_), channel_id=1, source_target_pairs={{0,12},{4,8},{8,4},{12,0},{1,13},{5,9},{9,5},{13,1},{2,14},{6,10},... | collective-permute-start | bytes 159752 | tf_op jit(solution)/shard_map/ppermute | solution.py:346
  8.2 6.4 %collective-permute-start.1 = (bf16[16,1664]{1,0:T(8,128)(2,1)S(1)}, bf16[16,1664]{1,0:T(8,128)(2,1)S(1)}, u32[]{:S(2)}, u32[]{:S(2)}) collective-permute-start(bf16[16,1664]{1,0:T(8,128)(2,1)S(1)} %get-tuple-element.43.refs_0_), channel_id=1, source_target_pairs={{0,8},{4,12},{8,0},{12,4},{1,9},{5,13},{9,1},{13,5},{2,10},{6,14},... | collective-permute-start | bytes 159752 | tf_op jit(solution)/shard_map/ppermute | solution.py:346
  8.2 6.4 %collective-permute-start = (bf16[16,1664]{1,0:T(8,128)(2,1)S(1)}, bf16[16,1664]{1,0:T(8,128)(2,1)S(1)}, u32[]{:S(2)}, u32[]{:S(2)}) collective-permute-start(bf16[16,1664]{1,0:T(8,128)(2,1)S(1)} %get-tuple-element.43.refs_0_), channel_id=1, source_target_pairs={{0,4},{4,0},{8,12},{12,8},{1,5},{5,1},{9,13},{13,9},{2,6},{6,2},{1... | collective-permute-start | bytes 159752 | tf_op jit(solution)/shard_map/ppermute | solution.py:346
  8.8 7.8 %collective-permute-start.5 = (bf16[16,1536]{1,0:T(8,128)(2,1)S(1)}, bf16[16,1536]{1,0:T(8,128)(2,1)S(1)}, u32[]{:S(2)}, u32[]{:S(2)}) collective-permute-start(bf16[16,1536]{1,0:T(8,128)(2,1)S(1)} %get-tuple-element.44.refs_4_), channel_id=1, source_target_pairs={{0,12},{4,8},{8,4},{12,0},{1,13},{5,9},{9,5},{13,1},{2,14},{6,10},... | collective-permute-start | bytes 147464 | tf_op jit(solution)/shard_map/ppermute | solution.py:346
  12.5 5.0 %collective-permute-start.4 = (bf16[16,1536]{1,0:T(8,128)(2,1)S(1)}, bf16[16,1536]{1,0:T(8,128)(2,1)S(1)}, u32[]{:S(2)}, u32[]{:S(2)}) collective-permute-start(bf16[16,1536]{1,0:T(8,128)(2,1)S(1)} %get-tuple-element.44.refs_4_), channel_id=1, source_target_pairs={{0,8},{4,12},{8,0},{12,4},{1,9},{5,13},{9,1},{13,5},{2,10},{6,14},... | collective-permute-start | bytes 147464 | tf_op jit(solution)/shard_map/ppermute | solution.py:346
  12.6 5.0 %collective-permute-start.3 = (bf16[16,1536]{1,0:T(8,128)(2,1)S(1)}, bf16[16,1536]{1,0:T(8,128)(2,1)S(1)}, u32[]{:S(2)}, u32[]{:S(2)}) collective-permute-start(bf16[16,1536]{1,0:T(8,128)(2,1)S(1)} %get-tuple-element.44.refs_4_), channel_id=1, source_target_pairs={{0,4},{4,0},{8,12},{12,8},{1,5},{5,1},{9,13},{13,9},{2,6},{6,2},{1... | collective-permute-start | bytes 147464 | tf_op jit(solution)/shard_map/ppermute | solution.py:346
  15.0 4.9 %collective-permute-start.9 = (bf16[32,1536]{1,0:T(8,128)(2,1)S(1)}, bf16[32,1536]{1,0:T(8,128)(2,1)S(1)}, u32[]{:S(2)}, u32[]{:S(2)}) collective-permute-start(bf16[32,1536]{1,0:T(8,128)(2,1)S(1)} %get-tuple-element.52), channel_id=1, source_target_pairs={{0,2},{1,3},{2,0},{3,1},{4,6},{5,7},{6,4},{7,5},{8,10},{9,11},{10,... | collective-permute-start | bytes 294920 | tf_op jit(solution)/shard_map/ppermute | solution.py:346
  16.6 5.3 %collective-permute-start.10 = (bf16[32,1536]{1,0:T(8,128)(2,1)S(1)}, bf16[32,1536]{1,0:T(8,128)(2,1)S(1)}, u32[]{:S(2)}, u32[]{:S(2)}) collective-permute-start(bf16[32,1536]{1,0:T(8,128)(2,1)S(1)} %get-tuple-element.53), channel_id=1, source_target_pairs={{0,3},{1,2},{2,1},{3,0},{4,7},{5,6},{6,5},{7,4},{8,11},{9,10},{10,... | collective-permute-start | bytes 294920 | tf_op jit(solution)/shard_map/ppermute | solution.py:346
  16.6 5.3 %collective-permute-start.11 = (bf16[32,1536]{1,0:T(8,128)(2,1)S(1)}, bf16[32,1536]{1,0:T(8,128)(2,1)S(1)}, u32[]{:S(2)}, u32[]{:S(2)}) collective-permute-start(bf16[32,1536]{1,0:T(8,128)(2,1)S(1)} %get-tuple-element.54), channel_id=1, source_target_pairs={{0,1},{1,0},{2,3},{3,2},{4,5},{5,4},{6,7},{7,6},{8,9},{9,8},{10,11... | collective-permute-start | bytes 294920 | tf_op jit(solution)/shard_map/ppermute | solution.py:346
  17.9 6.9 %collective-permute-start.6 = (bf16[32,1536]{1,0:T(8,128)(2,1)S(1)}, bf16[32,1536]{1,0:T(8,128)(2,1)S(1)}, u32[]{:S(2)}, u32[]{:S(2)}) collective-permute-start(bf16[32,1536]{1,0:T(8,128)(2,1)S(1)} %get-tuple-element.48), channel_id=1, source_target_pairs={{0,2},{1,3},{2,0},{3,1},{4,6},{5,7},{6,4},{7,5},{8,10},{9,11},{10,... | collective-permute-start | bytes 294920 | tf_op jit(solution)/shard_map/ppermute | solution.py:346
  19.5 6.3 %collective-permute-start.7 = (bf16[32,1536]{1,0:T(8,128)(2,1)S(1)}, bf16[32,1536]{1,0:T(8,128)(2,1)S(1)}, u32[]{:S(2)}, u32[]{:S(2)}) collective-permute-start(bf16[32,1536]{1,0:T(8,128)(2,1)S(1)} %get-tuple-element.49), channel_id=1, source_target_pairs={{0,3},{1,2},{2,1},{3,0},{4,7},{5,6},{6,5},{7,4},{8,11},{9,10},{10,... | collective-permute-start | bytes 294920 | tf_op jit(solution)/shard_map/ppermute | solution.py:346
  19.9 6.0 %collective-permute-start.8 = (bf16[32,1536]{1,0:T(8,128)(2,1)S(1)}, bf16[32,1536]{1,0:T(8,128)(2,1)S(1)}, u32[]{:S(2)}, u32[]{:S(2)}) collective-permute-start(bf16[32,1536]{1,0:T(8,128)(2,1)S(1)} %get-tuple-element.50), channel_id=1, source_target_pairs={{0,1},{1,0},{2,3},{3,2},{4,5},{5,4},{6,7},{7,6},{8,9},{9,8},{10,11... | collective-permute-start | bytes 294920 | tf_op jit(solution)/shard_map/ppermute | solution.py:346
  29.6 5.7 %collective-permute-start.12 = (bf16[32,1536]{1,0:T(8,128)(2,1)S(1)}, bf16[32,1536]{1,0:T(8,128)(2,1)S(1)}, u32[]{:S(2)}, u32[]{:S(2)}) collective-permute-start(bf16[32,1536]{1,0:T(8,128)(2,1)S(1)} %get-tuple-element.59), channel_id=1, source_target_pairs={{0,2},{1,3},{2,0},{3,1},{4,6},{5,7},{6,4},{7,5},{8,10},{9,11},{10,... | collective-permute-start | bytes 294920 | tf_op jit(solution)/shard_map/ppermute | solution.py:346
  30.2 5.5 %collective-permute-start.13 = (bf16[32,1536]{1,0:T(8,128)(2,1)S(1)}, bf16[32,1536]{1,0:T(8,128)(2,1)S(1)}, u32[]{:S(2)}, u32[]{:S(2)}) collective-permute-start(bf16[32,1536]{1,0:T(8,128)(2,1)S(1)} %get-tuple-element.60), channel_id=1, source_target_pairs={{0,3},{1,2},{2,1},{3,0},{4,7},{5,6},{6,5},{7,4},{8,11},{9,10},{10,... | collective-permute-start | bytes 294920 | tf_op jit(solution)/shard_map/ppermute | solution.py:346
  31.1 4.6 %collective-permute-start.14 = (bf16[32,1536]{1,0:T(8,128)(2,1)S(1)}, bf16[32,1536]{1,0:T(8,128)(2,1)S(1)}, u32[]{:S(2)}, u32[]{:S(2)}) collective-permute-start(bf16[32,1536]{1,0:T(8,128)(2,1)S(1)} %get-tuple-element.61), channel_id=1, source_target_pairs={{0,1},{1,0},{2,3},{3,2},{4,5},{5,4},{6,7},{7,6},{8,9},{9,8},{10,11... | collective-permute-start | bytes 294920 | tf_op jit(solution)/shard_map/ppermute | solution.py:346
  33.0 6.5 %collective-permute-start.18 = (bf16[32,1536]{1,0:T(8,128)(2,1)S(1)}, bf16[32,1536]{1,0:T(8,128)(2,1)S(1)}, u32[]{:S(2)}, u32[]{:S(2)}) collective-permute-start(bf16[32,1536]{1,0:T(8,128)(2,1)S(1)} %get-tuple-element.70), channel_id=1, source_target_pairs={{0,2},{1,3},{2,0},{3,1},{4,6},{5,7},{6,4},{7,5},{8,10},{9,11},{10,... | collective-permute-start | bytes 294920 | tf_op jit(solution)/shard_map/ppermute | solution.py:346
  33.9 6.5 %collective-permute-start.19 = (bf16[32,1536]{1,0:T(8,128)(2,1)S(1)}, bf16[32,1536]{1,0:T(8,128)(2,1)S(1)}, u32[]{:S(2)}, u32[]{:S(2)}) collective-permute-start(bf16[32,1536]{1,0:T(8,128)(2,1)S(1)} %get-tuple-element.71), channel_id=1, source_target_pairs={{0,3},{1,2},{2,1},{3,0},{4,7},{5,6},{6,5},{7,4},{8,11},{9,10},{10,... | collective-permute-start | bytes 294920 | tf_op jit(solution)/shard_map/ppermute | solution.py:346
  35.3 5.2 %collective-permute-start.20 = (bf16[32,1536]{1,0:T(8,128)(2,1)S(1)}, bf16[32,1536]{1,0:T(8,128)(2,1)S(1)}, u32[]{:S(2)}, u32[]{:S(2)}) collective-permute-start(bf16[32,1536]{1,0:T(8,128)(2,1)S(1)} %get-tuple-element.72), channel_id=1, source_target_pairs={{0,1},{1,0},{2,3},{3,2},{4,5},{5,4},{6,7},{7,6},{8,9},{9,8},{10,11... | collective-permute-start | bytes 294920 | tf_op jit(solution)/shard_map/ppermute | solution.py:346
  36.0 7.4 %collective-permute-start.15 = (bf16[16,1536]{1,0:T(8,128)(2,1)S(1)}, bf16[16,1536]{1,0:T(8,128)(2,1)S(1)}, u32[]{:S(2)}, u32[]{:S(2)}) collective-permute-start(bf16[16,1536]{1,0:T(8,128)(2,1)S(1)} %get-tuple-element.64), channel_id=1, source_target_pairs={{0,12},{4,8},{8,4},{12,0},{1,13},{5,9},{9,5},{13,1},{2,14},{6,10},... | collective-permute-start | bytes 147464 | tf_op jit(solution)/shard_map/ppermute | solution.py:346
  38.7 6.5 %collective-permute-start.16 = (bf16[16,1536]{1,0:T(8,128)(2,1)S(1)}, bf16[16,1536]{1,0:T(8,128)(2,1)S(1)}, u32[]{:S(2)}, u32[]{:S(2)}) collective-permute-start(bf16[16,1536]{1,0:T(8,128)(2,1)S(1)} %get-tuple-element.65), channel_id=1, source_target_pairs={{0,8},{4,12},{8,0},{12,4},{1,9},{5,13},{9,1},{13,5},{2,10},{6,14},... | collective-permute-start | bytes 147464 | tf_op jit(solution)/shard_map/ppermute | solution.py:346
  39.5 5.7 %collective-permute-start.17 = (bf16[16,1536]{1,0:T(8,128)(2,1)S(1)}, bf16[16,1536]{1,0:T(8,128)(2,1)S(1)}, u32[]{:S(2)}, u32[]{:S(2)}) collective-permute-start(bf16[16,1536]{1,0:T(8,128)(2,1)S(1)} %get-tuple-element.66), channel_id=1, source_target_pairs={{0,4},{4,0},{8,12},{12,8},{1,5},{5,1},{9,13},{13,9},{2,6},{6,2},{1... | collective-permute-start | bytes 147464 | tf_op jit(solution)/shard_map/ppermute | solution.py:346
  40.7 6.5 %collective-permute-start.21 = (bf16[16,1536]{1,0:T(8,128)(2,1)S(1)}, bf16[16,1536]{1,0:T(8,128)(2,1)S(1)}, u32[]{:S(2)}, u32[]{:S(2)}) collective-permute-start(bf16[16,1536]{1,0:T(8,128)(2,1)S(1)} %get-tuple-element.74), channel_id=1, source_target_pairs={{0,12},{4,8},{8,4},{12,0},{1,13},{5,9},{9,5},{13,1},{2,14},{6,10},... | collective-permute-start | bytes 147464 | tf_op jit(solution)/shard_map/ppermute | solution.py:346
  43.4 5.6 %collective-permute-start.22 = (bf16[16,1536]{1,0:T(8,128)(2,1)S(1)}, bf16[16,1536]{1,0:T(8,128)(2,1)S(1)}, u32[]{:S(2)}, u32[]{:S(2)}) collective-permute-start(bf16[16,1536]{1,0:T(8,128)(2,1)S(1)} %get-tuple-element.75), channel_id=1, source_target_pairs={{0,8},{4,12},{8,0},{12,4},{1,9},{5,13},{9,1},{13,5},{2,10},{6,14},... | collective-permute-start | bytes 147464 | tf_op jit(solution)/shard_map/ppermute | solution.py:346
  43.4 5.6 %collective-permute-start.23 = (bf16[16,1536]{1,0:T(8,128)(2,1)S(1)}, bf16[16,1536]{1,0:T(8,128)(2,1)S(1)}, u32[]{:S(2)}, u32[]{:S(2)}) collective-permute-start(bf16[16,1536]{1,0:T(8,128)(2,1)S(1)} %get-tuple-element.76), channel_id=1, source_target_pairs={{0,4},{4,0},{8,12},{12,8},{1,5},{5,1},{9,13},{13,9},{2,6},{6,2},{1... | collective-permute-start | bytes 147464 | tf_op jit(solution)/shard_map/ppermute | solution.py:346

commit v24 on v23

--- a/solution.py
+++ b/solution.py
@@ -16,7 +16,7 @@
 BLOCK = 8
 STRIPS = 3
 TILE = 256
-UNROLL = 4
+UNROLL = 8
 MIB = 1 << 20
 F32 = jnp.float32
 BF16 = jnp.bfloat16

time: 49.8 us -> 53.3 us (1.070)
  Pallas kernels: 13.1 us -> 16.4 us
  starting transfers between devices: 26.4 us -> 27.8 us
  waiting for transfers between devices: 9.86 us -> 8.65 us
    pallas_call x1, Pallas kernels: 3.7 us -> 5.54 us  [shards(): pl.pallas_call(functools.partial(middle_kernel, experts=experts), in_spec...]
    pallas_call x1, Pallas kernels: 2.92 us -> 4.59 us  [shards(): pl.pallas_call(functools.partial(begin_kernel, experts=experts), in_specs...]
    ppermute x24, starting transfers between devices: 26.4 us -> 27.8 us  [swap(): return lax.ppermute(value, axis, [(i, i ^ step) for i in range(count)])]
    ppermute x24, waiting for transfers between devices: 9.86 us -> 8.65 us  [swap(): return lax.ppermute(value, axis, [(i, i ^ step) for i in range(count)])]
  transfers between devices with their start and end apart: 24 -> 24, of which waited for: 9 -> 7; matrix products, arithmetic and copies ran while one was open for 0% -> 0% of each run, Pallas kernels for 12% -> 14%
where the time goes in v24:
time: 53.3 us; the launch traced here: 53.1 us
  starting transfers between devices  27.8 us (52%)
  Pallas kernels  16.4 us (31%)
  waiting for transfers between devices  8.65 us (16%)
    ppermute x24, starting transfers between devices, swap(): return lax.ppermute(value, axis, [(i, i ^ step) for i in range(count)])  27.8 us
    ppermute x24, waiting for transfers between devices, swap(): return lax.ppermute(value, axis, [(i, i ^ step) for i in range(count)])  8.65 us
    pallas_call x1, Pallas kernels, shards(): pl.pallas_call(functools.partial(middle_kernel, experts=experts), in_spec...  5.54 us
    pallas_call x1, Pallas kernels, shards(): pl.pallas_call(functools.partial(begin_kernel, experts=experts), in_specs...  4.59 us
    pallas_call x1, Pallas kernels, shards(): pl.pallas_call(attend_kernel, in_specs=[SCALAR] + [ANY] * len(operands),...  2.95 us
  transfers between devices with their start and end apart: 24, of which 7 were waited for; matrix products, arithmetic and copies ran while one was open for 0% of the time, Pallas kernels for 14%

profile of v24, /device:TPU:0, one launch (start us, length us, event | category | flops | bytes accessed | tf_op | source)
XLA Modules:
  0.0 53.1 jit_solution(17160715814552573715)
XLA Ops:
  0.0 2.9 %shard_map.109 = (f32[16,3072]{1,0:T(8,128)S(1)}, bf16[16,1664]{1,0:T(8,128)(2,1)S(1)}, bf16[16,1536]{1,0:T(8,128)(2,1)S(1)}) custom-call(s32[1]{0:T(128)} %bitcast._.me_ref, s32[1,16]{1,0:T(1,128)} %bitcast.21, bf16[16,3072]{1,0:T(8,128)(2,1)} %queries_hbm.1, bf16[16,96,512]{2,1,0:T(8,128)(2,1)} %keys_hbm.1, bf16[16,96,512]{2,1,0:T(8,128)(2,1)} %values_hbm.1, ...), custom_call_target="tpu_custom_call" | custom-call | tf_op jit(solution)/shard_map/pallas_call | solution.py:390
  3.0 0.0 slice-start
  3.0 0.0 slice-start.3
  3.0 0.0 slice-start.1
  3.0 0.0 slice-start.2
  3.0 0.0 slice-start.4
  3.0 0.0 slice-start.5
  3.0 0.0 copy-start
  3.0 5.1 %collective-permute-start.2 = (bf16[16,1664]{1,0:T(8,128)(2,1)S(1)}, bf16[16,1664]{1,0:T(8,128)(2,1)S(1)}, u32[]{:S(2)}, u32[]{:S(2)}) collective-permute-start(bf16[16,1664]{1,0:T(8,128)(2,1)S(1)} %get-tuple-element.43.refs_0_), channel_id=1, source_target_pairs={{0,12},{4,8},{8,4},{12,0},{1,13},{5,9},{9,5},{13,1},{2,14},{6,10},... | collective-permute-start | bytes 159752 | tf_op jit(solution)/shard_map/ppermute | solution.py:346
  8.2 0.0 collective-permute-start.1
  8.2 0.6 %collective-permute-start = (bf16[16,1664]{1,0:T(8,128)(2,1)S(1)}, bf16[16,1664]{1,0:T(8,128)(2,1)S(1)}, u32[]{:S(2)}, u32[]{:S(2)}) collective-permute-start(bf16[16,1664]{1,0:T(8,128)(2,1)S(1)} %get-tuple-element.43.refs_0_), channel_id=1, source_target_pairs={{0,4},{4,0},{8,12},{12,8},{1,5},{5,1},{9,13},{13,9},{2,6},{6,2},{1... | collective-permute-start | bytes 159752 | tf_op jit(solution)/shard_map/ppermute | solution.py:346
  8.8 3.7 %collective-permute-start.5 = (bf16[16,1536]{1,0:T(8,128)(2,1)S(1)}, bf16[16,1536]{1,0:T(8,128)(2,1)S(1)}, u32[]{:S(2)}, u32[]{:S(2)}) collective-permute-start(bf16[16,1536]{1,0:T(8,128)(2,1)S(1)} %get-tuple-element.44.refs_4_), channel_id=1, source_target_pairs={{0,12},{4,8},{8,4},{12,0},{1,13},{5,9},{9,5},{13,1},{2,14},{6,10},... | collective-permute-start | bytes 147464 | tf_op jit(solution)/shard_map/ppermute | solution.py:346
  12.5 0.0 collective-permute-start.4
  12.5 0.0 collective-permute-done.2.refs_3_
  12.6 0.6 %collective-permute-start.3 = (bf16[16,1536]{1,0:T(8,128)(2,1)S(1)}, bf16[16,1536]{1,0:T(8,128)(2,1)S(1)}, u32[]{:S(2)}, u32[]{:S(2)}) collective-permute-start(bf16[16,1536]{1,0:T(8,128)(2,1)S(1)} %get-tuple-element.44.refs_4_), channel_id=1, source_target_pairs={{0,4},{4,0},{8,12},{12,8},{1,5},{5,1},{9,13},{13,9},{2,6},{6,2},{1... | collective-permute-start | bytes 147464 | tf_op jit(solution)/shard_map/ppermute | solution.py:346
  13.2 1.4 %collective-permute-done.1.refs_2_ = bf16[16,1664]{1,0:T(8,128)(2,1)S(1)} collective-permute-done((bf16[16,1664]{1,0:T(8,128)(2,1)S(1)}, bf16[16,1664]{1,0:T(8,128)(2,1)S(1)}, u32[]{:S(2)}, u32[]{:S(2)}) %collective-permute-start.1) | collective-permute-done | bytes 53280 | tf_op jit(solution)/shard_map/ppermute | solution.py:346
  14.6 0.0 collective-permute-done.refs_1_
  14.6 0.4 shard_map.113
  15.0 1.6 %collective-permute-start.9 = (bf16[32,1536]{1,0:T(8,128)(2,1)S(1)}, bf16[32,1536]{1,0:T(8,128)(2,1)S(1)}, u32[]{:S(2)}, u32[]{:S(2)}) collective-permute-start(bf16[32,1536]{1,0:T(8,128)(2,1)S(1)} %get-tuple-element.52), channel_id=1, source_target_pairs={{0,2},{1,3},{2,0},{3,1},{4,6},{5,7},{6,4},{7,5},{8,10},{9,11},{10,... | collective-permute-start | bytes 294920 | tf_op jit(solution)/shard_map/ppermute | solution.py:346
  16.6 0.0 collective-permute-start.10
  16.6 0.0 collective-permute-done.5.refs_7_
  16.6 0.6 %collective-permute-start.11 = (bf16[32,1536]{1,0:T(8,128)(2,1)S(1)}, bf16[32,1536]{1,0:T(8,128)(2,1)S(1)}, u32[]{:S(2)}, u32[]{:S(2)}) collective-permute-start(bf16[32,1536]{1,0:T(8,128)(2,1)S(1)} %get-tuple-element.54), channel_id=1, source_target_pairs={{0,1},{1,0},{2,3},{3,2},{4,5},{5,4},{6,7},{7,6},{8,9},{9,8},{10,11... | collective-permute-start | bytes 294920 | tf_op jit(solution)/shard_map/ppermute | solution.py:346
  17.2 0.3 collective-permute-done.4.refs_6_
  17.5 0.0 collective-permute-done.3.refs_5_
  17.5 0.4 shard_map.112
  17.9 1.6 %collective-permute-start.6 = (bf16[32,1536]{1,0:T(8,128)(2,1)S(1)}, bf16[32,1536]{1,0:T(8,128)(2,1)S(1)}, u32[]{:S(2)}, u32[]{:S(2)}) collective-permute-start(bf16[32,1536]{1,0:T(8,128)(2,1)S(1)} %get-tuple-element.48), channel_id=1, source_target_pairs={{0,2},{1,3},{2,0},{3,1},{4,6},{5,7},{6,4},{7,5},{8,10},{9,11},{10,... | collective-permute-start | bytes 294920 | tf_op jit(solution)/shard_map/ppermute | solution.py:346
  19.5 0.0 collective-permute-start.7
  19.5 0.4 shard_map.111
  19.9 0.0 collective-permute-done.9.refs_1_
  19.9 0.7 %collective-permute-start.8 = (bf16[32,1536]{1,0:T(8,128)(2,1)S(1)}, bf16[32,1536]{1,0:T(8,128)(2,1)S(1)}, u32[]{:S(2)}, u32[]{:S(2)}) collective-permute-start(bf16[32,1536]{1,0:T(8,128)(2,1)S(1)} %get-tuple-element.50), channel_id=1, source_target_pairs={{0,1},{1,0},{2,3},{3,2},{4,5},{5,4},{6,7},{7,6},{8,9},{9,8},{10,11... | collective-permute-start | bytes 294920 | tf_op jit(solution)/shard_map/ppermute | solution.py:346
  20.6 1.3 %collective-permute-done.10.refs_2_ = bf16[32,1536]{1,0:T(8,128)(2,1)S(1)} collective-permute-done((bf16[32,1536]{1,0:T(8,128)(2,1)S(1)}, bf16[32,1536]{1,0:T(8,128)(2,1)S(1)}, u32[]{:S(2)}, u32[]{:S(2)}) %collective-permute-start.10) | collective-permute-done | bytes 98336 | tf_op jit(solution)/shard_map/ppermute | solution.py:346
  21.9 0.0 collective-permute-done.11.refs_3_
  21.9 4.6 %shard_map.114 = (f32[128,2048]{1,0:T(8,128)S(1)}, f32[128,2048]{1,0:T(8,128)S(1)}, bf16[2048,1536]{1,0:T(8,128)(2,1)S(1)}) custom-call(bf16[32,1536]{1,0:T(8,128)(2,1)S(1)} %get-tuple-element.51.refs_0_, bf16[32,1536]{1,0:T(8,128)(2,1)S(1)} %collective-permute-done.9.refs_1_, bf16[32,1536]{1,0:T(8,128)(2,1)S(1)} %collective-permute-done.10.refs_2_, ...), custom_call_target="tpu_custom_call" | custom-call | flops 1610612736 | tf_op jit(solution)/shard_map/pallas_call | solution.py:433
  26.5 0.0 collective-permute-done.6.refs_1_
  26.5 0.0 collective-permute-done.7.refs_2_
  26.5 0.0 collective-permute-done.8.refs_3_
  26.5 5.5 %shard_map.115 = (bf16[32,1536]{1,0:T(8,128)(2,1)S(1)}, bf16[32,1536]{1,0:T(8,128)(2,1)S(1)}, bf16[32,1536]{1,0:T(8,128)(2,1)S(1)}, bf16[32,1536]{1,0:T(8,128)(2...) custom-call(bf16[32,1536]{1,0:T(8,128)(2,1)S(1)} %get-tuple-element.47.refs_0_, ...), custom_call_target="tpu_custom_call" | custom-call | tf_op jit(solution)/shard_map/pallas_call | solution.py:444
  32.1 0.5 collective-permute-start.12
  32.6 1.9 %collective-permute-start.13 = (bf16[32,1536]{1,0:T(8,128)(2,1)S(1)}, bf16[32,1536]{1,0:T(8,128)(2,1)S(1)}, u32[]{:S(2)}, u32[]{:S(2)}) collective-permute-start(bf16[32,1536]{1,0:T(8,128)(2,1)S(1)} %get-tuple-element.60), channel_id=1, source_target_pairs={{0,3},{1,2},{2,1},{3,0},{4,7},{5,6},{6,5},{7,4},{8,11},{9,10},{10,... | collective-permute-start | bytes 294920 | tf_op jit(solution)/shard_map/ppermute | solution.py:346
  34.4 0.0 collective-permute-start.14
  34.5 1.0 %shard_map.118 = (bf16[32,1536]{1,0:T(8,128)(2,1)S(1)}, bf16[32,1536]{1,0:T(8,128)(2,1)S(1)}, bf16[32,1536]{1,0:T(8,128)(2,1)S(1)}, bf16[32,1536]{1,0:T(8,128)(2,1)S(1)}) custom-call(bf16[128,2048]{1,0:T(8,128)(2,1)S(1)} %get-tuple-element.67.hidden_ref, bf16[2048,1536]{1,0:T(8,128)(2,1)S(1)} %get-tuple-element.68.down_ref), custom_call_target="tpu_custom_call" | custom-call | flops 805306368 | tf_op jit(solution)/shard_map/pallas_call | solution.py:452
  35.5 1.7 %collective-permute-start.18 = (bf16[32,1536]{1,0:T(8,128)(2,1)S(1)}, bf16[32,1536]{1,0:T(8,128)(2,1)S(1)}, u32[]{:S(2)}, u32[]{:S(2)}) collective-permute-start(bf16[32,1536]{1,0:T(8,128)(2,1)S(1)} %get-tuple-element.70), channel_id=1, source_target_pairs={{0,2},{1,3},{2,0},{3,1},{4,6},{5,7},{6,4},{7,5},{8,10},{9,11},{10,... | collective-permute-start | bytes 294920 | tf_op jit(solution)/shard_map/ppermute | solution.py:346
  37.2 0.2 collective-permute-start.19
  37.4 0.5 collective-permute-done.12.refs_1_
  37.8 0.0 collective-permute-start.20
  37.8 1.9 %collective-permute-done.13.refs_2_ = bf16[32,1536]{1,0:T(8,128)(2,1)S(1)} collective-permute-done((bf16[32,1536]{1,0:T(8,128)(2,1)S(1)}, bf16[32,1536]{1,0:T(8,128)(2,1)S(1)}, u32[]{:S(2)}, u32[]{:S(2)}) %collective-permute-start.13) | collective-permute-done | bytes 98336 | tf_op jit(solution)/shard_map/ppermute | solution.py:346
  39.7 0.0 collective-permute-done.14.refs_3_
  39.7 0.3 shard_map.116
  40.0 2.7 %collective-permute-start.15 = (bf16[16,1536]{1,0:T(8,128)(2,1)S(1)}, bf16[16,1536]{1,0:T(8,128)(2,1)S(1)}, u32[]{:S(2)}, u32[]{:S(2)}) collective-permute-start(bf16[16,1536]{1,0:T(8,128)(2,1)S(1)} %get-tuple-element.64), channel_id=1, source_target_pairs={{0,12},{4,8},{8,4},{12,0},{1,13},{5,9},{9,5},{13,1},{2,14},{6,10},... | collective-permute-start | bytes 147464 | tf_op jit(solution)/shard_map/ppermute | solution.py:346
  42.7 0.0 collective-permute-start.16
  42.7 0.0 collective-permute-done.18.refs_1_
  42.7 1.8 %collective-permute-start.17 = (bf16[16,1536]{1,0:T(8,128)(2,1)S(1)}, bf16[16,1536]{1,0:T(8,128)(2,1)S(1)}, u32[]{:S(2)}, u32[]{:S(2)}) collective-permute-start(bf16[16,1536]{1,0:T(8,128)(2,1)S(1)} %get-tuple-element.66), channel_id=1, source_target_pairs={{0,4},{4,0},{8,12},{12,8},{1,5},{5,1},{9,13},{13,9},{2,6},{6,2},{1... | collective-permute-start | bytes 147464 | tf_op jit(solution)/shard_map/ppermute | solution.py:346
  44.4 0.0 collective-permute-done.19.refs_2_
  44.4 0.3 shard_map.119
  44.7 2.7 %collective-permute-start.21 = (bf16[16,1536]{1,0:T(8,128)(2,1)S(1)}, bf16[16,1536]{1,0:T(8,128)(2,1)S(1)}, u32[]{:S(2)}, u32[]{:S(2)}) collective-permute-start(bf16[16,1536]{1,0:T(8,128)(2,1)S(1)} %get-tuple-element.74), channel_id=1, source_target_pairs={{0,12},{4,8},{8,4},{12,0},{1,13},{5,9},{9,5},{13,1},{2,14},{6,10},... | collective-permute-start | bytes 147464 | tf_op jit(solution)/shard_map/ppermute | solution.py:346
  47.4 0.0 collective-permute-start.22
  47.4 0.0 collective-permute-done.15.refs_1_
  47.4 1.8 %collective-permute-start.23 = (bf16[16,1536]{1,0:T(8,128)(2,1)S(1)}, bf16[16,1536]{1,0:T(8,128)(2,1)S(1)}, u32[]{:S(2)}, u32[]{:S(2)}) collective-permute-start(bf16[16,1536]{1,0:T(8,128)(2,1)S(1)} %get-tuple-element.76), channel_id=1, source_target_pairs={{0,4},{4,0},{8,12},{12,8},{1,5},{5,1},{9,13},{13,9},{2,6},{6,2},{1... | collective-permute-start | bytes 147464 | tf_op jit(solution)/shard_map/ppermute | solution.py:346
  49.2 0.0 collective-permute-done.16.refs_2_
  49.2 0.0 collective-permute-done.17.refs_3_
  49.2 1.6 %collective-permute-done.21.refs_2_ = bf16[16,1536]{1,0:T(8,128)(2,1)S(1)} collective-permute-done((bf16[16,1536]{1,0:T(8,128)(2,1)S(1)}, bf16[16,1536]{1,0:T(8,128)(2,1)S(1)}, u32[]{:S(2)}, u32[]{:S(2)}) %collective-permute-start.21) | collective-permute-done | bytes 49184 | tf_op jit(solution)/shard_map/ppermute | solution.py:346
  50.8 1.7 %collective-permute-done.22.refs_3_ = bf16[16,1536]{1,0:T(8,128)(2,1)S(1)} collective-permute-done((bf16[16,1536]{1,0:T(8,128)(2,1)S(1)}, bf16[16,1536]{1,0:T(8,128)(2,1)S(1)}, u32[]{:S(2)}, u32[]{:S(2)}) %collective-permute-start.22) | collective-permute-done | bytes 49184 | tf_op jit(solution)/shard_map/ppermute | solution.py:346
  52.4 0.0 collective-permute-done.23.refs_4_
  52.5 0.7 %shard_map.120 = bf16[16,3072]{1,0:T(8,128)(2,1)} custom-call(bf16[16,1536]{1,0:T(8,128)(2,1)S(1)} %shard_map.117.refs_0_, f32[16,1536]{1,0:T(8,128)S(1)} %get-tuple-element.73.refs_1_, bf16[16,1536]{1,0:T(8,128)(2,1)S(1)} %collective-permute-done.21.refs_2_, bf16[16,1536]{1,0:T(8,128)(2,1)S(1)} %collective-permute-done.22.refs_3_, ...), custom_call_target="tpu_custom_call" | custom-call | tf_op jit(solution)/shard_map/pallas_call | solution.py:476
  (12 shorter events, 0.0 us)
Async XLA Ops:
  3.0 18.9 %slice-start = ((s8[12582912]{0:T(1024)(128)(4,1)}), s8[4194304]{0:T(1024)(128)(4,1)S(1)}, s32[]{:S(2)}) async-start(s8[12582912]{0:T(1024)(128)(4,1)} %bitcast.8), calls=%async_computation | async-start | bytes 8388608
  3.0 18.9 %slice-start.3 = ((s8[12582912]{0:T(1024)(128)(4,1)}), s8[4194304]{0:T(1024)(128)(4,1)S(1)}, s32[]{:S(2)}) async-start(s8[12582912]{0:T(1024)(128)(4,1)} %bitcast.12), calls=%async_computation.3 | async-start | bytes 8388608
  3.0 18.9 %slice-start.1 = ((s8[12582912]{0:T(1024)(128)(4,1)}), s8[4194304]{0:T(1024)(128)(4,1)S(1)}, s32[]{:S(2)}) async-start(s8[12582912]{0:T(1024)(128)(4,1)} %bitcast.8), calls=%async_computation.1 | async-start | bytes 8388608
  3.0 18.9 %slice-start.2 = ((s8[12582912]{0:T(1024)(128)(4,1)}), s8[4194304]{0:T(1024)(128)(4,1)S(1)}, s32[]{:S(2)}) async-start(s8[12582912]{0:T(1024)(128)(4,1)} %bitcast.8), calls=%async_computation.2 | async-start | bytes 8388608
  3.0 18.9 %slice-start.4 = ((s8[12582912]{0:T(1024)(128)(4,1)}), s8[4194304]{0:T(1024)(128)(4,1)S(1)}, s32[]{:S(2)}) async-start(s8[12582912]{0:T(1024)(128)(4,1)} %bitcast.12), calls=%async_computation.4 | async-start | bytes 8388608
  3.0 18.9 %slice-start.5 = ((s8[12582912]{0:T(1024)(128)(4,1)}), s8[4194304]{0:T(1024)(128)(4,1)S(1)}, s32[]{:S(2)}) async-start(s8[12582912]{0:T(1024)(128)(4,1)} %bitcast.12), calls=%async_computation.5 | async-start | bytes 8388608
  3.0 16.5 %copy-start = (bf16[3072,4]{0,1:T(4,128)(2,1)S(1)}, bf16[3072,4]{0,1:T(4,128)(2,1)}, u32[]{:S(2)}) copy-start(bf16[3072,4]{0,1:T(4,128)(2,1)} %param.18) | copy-start | bytes 73732
  3.0 9.5 %collective-permute-start.2 = (bf16[16,1664]{1,0:T(8,128)(2,1)S(1)}, bf16[16,1664]{1,0:T(8,128)(2,1)S(1)}, u32[]{:S(2)}, u32[]{:S(2)}) collective-permute-start(bf16[16,1664]{1,0:T(8,128)(2,1)S(1)} %get-tuple-element.43.refs_0_), channel_id=1, source_target_pairs={{0,12},{4,8},{8,4},{12,0},{1,13},{5,9},{9,5},{13,1},{2,14},{6,10},... | collective-permute-start | bytes 159752 | tf_op jit(solution)/shard_map/ppermute | solution.py:346
  8.2 6.4 %collective-permute-start.1 = (bf16[16,1664]{1,0:T(8,128)(2,1)S(1)}, bf16[16,1664]{1,0:T(8,128)(2,1)S(1)}, u32[]{:S(2)}, u32[]{:S(2)}) collective-permute-start(bf16[16,1664]{1,0:T(8,128)(2,1)S(1)} %get-tuple-element.43.refs_0_), channel_id=1, source_target_pairs={{0,8},{4,12},{8,0},{12,4},{1,9},{5,13},{9,1},{13,5},{2,10},{6,14},... | collective-permute-start | bytes 159752 | tf_op jit(solution)/shard_map/ppermute | solution.py:346
  8.2 6.4 %collective-permute-start = (bf16[16,1664]{1,0:T(8,128)(2,1)S(1)}, bf16[16,1664]{1,0:T(8,128)(2,1)S(1)}, u32[]{:S(2)}, u32[]{:S(2)}) collective-permute-start(bf16[16,1664]{1,0:T(8,128)(2,1)S(1)} %get-tuple-element.43.refs_0_), channel_id=1, source_target_pairs={{0,4},{4,0},{8,12},{12,8},{1,5},{5,1},{9,13},{13,9},{2,6},{6,2},{1... | collective-permute-start | bytes 159752 | tf_op jit(solution)/shard_map/ppermute | solution.py:346
  8.8 7.8 %collective-permute-start.5 = (bf16[16,1536]{1,0:T(8,128)(2,1)S(1)}, bf16[16,1536]{1,0:T(8,128)(2,1)S(1)}, u32[]{:S(2)}, u32[]{:S(2)}) collective-permute-start(bf16[16,1536]{1,0:T(8,128)(2,1)S(1)} %get-tuple-element.44.refs_4_), channel_id=1, source_target_pairs={{0,12},{4,8},{8,4},{12,0},{1,13},{5,9},{9,5},{13,1},{2,14},{6,10},... | collective-permute-start | bytes 147464 | tf_op jit(solution)/shard_map/ppermute | solution.py:346
  12.5 5.0 %collective-permute-start.4 = (bf16[16,1536]{1,0:T(8,128)(2,1)S(1)}, bf16[16,1536]{1,0:T(8,128)(2,1)S(1)}, u32[]{:S(2)}, u32[]{:S(2)}) collective-permute-start(bf16[16,1536]{1,0:T(8,128)(2,1)S(1)} %get-tuple-element.44.refs_4_), channel_id=1, source_target_pairs={{0,8},{4,12},{8,0},{12,4},{1,9},{5,13},{9,1},{13,5},{2,10},{6,14},... | collective-permute-start | bytes 147464 | tf_op jit(solution)/shard_map/ppermute | solution.py:346
  12.6 5.0 %collective-permute-start.3 = (bf16[16,1536]{1,0:T(8,128)(2,1)S(1)}, bf16[16,1536]{1,0:T(8,128)(2,1)S(1)}, u32[]{:S(2)}, u32[]{:S(2)}) collective-permute-start(bf16[16,1536]{1,0:T(8,128)(2,1)S(1)} %get-tuple-element.44.refs_4_), channel_id=1, source_target_pairs={{0,4},{4,0},{8,12},{12,8},{1,5},{5,1},{9,13},{13,9},{2,6},{6,2},{1... | collective-permute-start | bytes 147464 | tf_op jit(solution)/shard_map/ppermute | solution.py:346
  15.0 4.9 %collective-permute-start.9 = (bf16[32,1536]{1,0:T(8,128)(2,1)S(1)}, bf16[32,1536]{1,0:T(8,128)(2,1)S(1)}, u32[]{:S(2)}, u32[]{:S(2)}) collective-permute-start(bf16[32,1536]{1,0:T(8,128)(2,1)S(1)} %get-tuple-element.52), channel_id=1, source_target_pairs={{0,2},{1,3},{2,0},{3,1},{4,6},{5,7},{6,4},{7,5},{8,10},{9,11},{10,... | collective-permute-start | bytes 294920 | tf_op jit(solution)/shard_map/ppermute | solution.py:346
  16.6 5.3 %collective-permute-start.10 = (bf16[32,1536]{1,0:T(8,128)(2,1)S(1)}, bf16[32,1536]{1,0:T(8,128)(2,1)S(1)}, u32[]{:S(2)}, u32[]{:S(2)}) collective-permute-start(bf16[32,1536]{1,0:T(8,128)(2,1)S(1)} %get-tuple-element.53), channel_id=1, source_target_pairs={{0,3},{1,2},{2,1},{3,0},{4,7},{5,6},{6,5},{7,4},{8,11},{9,10},{10,... | collective-permute-start | bytes 294920 | tf_op jit(solution)/shard_map/ppermute | solution.py:346
  16.6 5.3 %collective-permute-start.11 = (bf16[32,1536]{1,0:T(8,128)(2,1)S(1)}, bf16[32,1536]{1,0:T(8,128)(2,1)S(1)}, u32[]{:S(2)}, u32[]{:S(2)}) collective-permute-start(bf16[32,1536]{1,0:T(8,128)(2,1)S(1)} %get-tuple-element.54), channel_id=1, source_target_pairs={{0,1},{1,0},{2,3},{3,2},{4,5},{5,4},{6,7},{7,6},{8,9},{9,8},{10,11... | collective-permute-start | bytes 294920 | tf_op jit(solution)/shard_map/ppermute | solution.py:346
  17.9 8.6 %collective-permute-start.6 = (bf16[32,1536]{1,0:T(8,128)(2,1)S(1)}, bf16[32,1536]{1,0:T(8,128)(2,1)S(1)}, u32[]{:S(2)}, u32[]{:S(2)}) collective-permute-start(bf16[32,1536]{1,0:T(8,128)(2,1)S(1)} %get-tuple-element.48), channel_id=1, source_target_pairs={{0,2},{1,3},{2,0},{3,1},{4,6},{5,7},{6,4},{7,5},{8,10},{9,11},{10,... | collective-permute-start | bytes 294920 | tf_op jit(solution)/shard_map/ppermute | solution.py:346
  19.5 7.0 %collective-permute-start.7 = (bf16[32,1536]{1,0:T(8,128)(2,1)S(1)}, bf16[32,1536]{1,0:T(8,128)(2,1)S(1)}, u32[]{:S(2)}, u32[]{:S(2)}) collective-permute-start(bf16[32,1536]{1,0:T(8,128)(2,1)S(1)} %get-tuple-element.49), channel_id=1, source_target_pairs={{0,3},{1,2},{2,1},{3,0},{4,7},{5,6},{6,5},{7,4},{8,11},{9,10},{10,... | collective-permute-start | bytes 294920 | tf_op jit(solution)/shard_map/ppermute | solution.py:346
  19.9 6.7 %collective-permute-start.8 = (bf16[32,1536]{1,0:T(8,128)(2,1)S(1)}, bf16[32,1536]{1,0:T(8,128)(2,1)S(1)}, u32[]{:S(2)}, u32[]{:S(2)}) collective-permute-start(bf16[32,1536]{1,0:T(8,128)(2,1)S(1)} %get-tuple-element.50), channel_id=1, source_target_pairs={{0,1},{1,0},{2,3},{3,2},{4,5},{5,4},{6,7},{7,6},{8,9},{9,8},{10,11... | collective-permute-start | bytes 294920 | tf_op jit(solution)/shard_map/ppermute | solution.py:346
  32.1 5.7 %collective-permute-start.12 = (bf16[32,1536]{1,0:T(8,128)(2,1)S(1)}, bf16[32,1536]{1,0:T(8,128)(2,1)S(1)}, u32[]{:S(2)}, u32[]{:S(2)}) collective-permute-start(bf16[32,1536]{1,0:T(8,128)(2,1)S(1)} %get-tuple-element.59), channel_id=1, source_target_pairs={{0,2},{1,3},{2,0},{3,1},{4,6},{5,7},{6,4},{7,5},{8,10},{9,11},{10,... | collective-permute-start | bytes 294920 | tf_op jit(solution)/shard_map/ppermute | solution.py:346
  32.6 7.1 %collective-permute-start.13 = (bf16[32,1536]{1,0:T(8,128)(2,1)S(1)}, bf16[32,1536]{1,0:T(8,128)(2,1)S(1)}, u32[]{:S(2)}, u32[]{:S(2)}) collective-permute-start(bf16[32,1536]{1,0:T(8,128)(2,1)S(1)} %get-tuple-element.60), channel_id=1, source_target_pairs={{0,3},{1,2},{2,1},{3,0},{4,7},{5,6},{6,5},{7,4},{8,11},{9,10},{10,... | collective-permute-start | bytes 294920 | tf_op jit(solution)/shard_map/ppermute | solution.py:346
  34.4 5.3 %collective-permute-start.14 = (bf16[32,1536]{1,0:T(8,128)(2,1)S(1)}, bf16[32,1536]{1,0:T(8,128)(2,1)S(1)}, u32[]{:S(2)}, u32[]{:S(2)}) collective-permute-start(bf16[32,1536]{1,0:T(8,128)(2,1)S(1)} %get-tuple-element.61), channel_id=1, source_target_pairs={{0,1},{1,0},{2,3},{3,2},{4,5},{5,4},{6,7},{7,6},{8,9},{9,8},{10,11... | collective-permute-start | bytes 294920 | tf_op jit(solution)/shard_map/ppermute | solution.py:346
  35.5 7.2 %collective-permute-start.18 = (bf16[32,1536]{1,0:T(8,128)(2,1)S(1)}, bf16[32,1536]{1,0:T(8,128)(2,1)S(1)}, u32[]{:S(2)}, u32[]{:S(2)}) collective-permute-start(bf16[32,1536]{1,0:T(8,128)(2,1)S(1)} %get-tuple-element.70), channel_id=1, source_target_pairs={{0,2},{1,3},{2,0},{3,1},{4,6},{5,7},{6,4},{7,5},{8,10},{9,11},{10,... | collective-permute-start | bytes 294920 | tf_op jit(solution)/shard_map/ppermute | solution.py:346
  37.2 7.3 %collective-permute-start.19 = (bf16[32,1536]{1,0:T(8,128)(2,1)S(1)}, bf16[32,1536]{1,0:T(8,128)(2,1)S(1)}, u32[]{:S(2)}, u32[]{:S(2)}) collective-permute-start(bf16[32,1536]{1,0:T(8,128)(2,1)S(1)} %get-tuple-element.71), channel_id=1, source_target_pairs={{0,3},{1,2},{2,1},{3,0},{4,7},{5,6},{6,5},{7,4},{8,11},{9,10},{10,... | collective-permute-start | bytes 294920 | tf_op jit(solution)/shard_map/ppermute | solution.py:346
  37.8 6.6 %collective-permute-start.20 = (bf16[32,1536]{1,0:T(8,128)(2,1)S(1)}, bf16[32,1536]{1,0:T(8,128)(2,1)S(1)}, u32[]{:S(2)}, u32[]{:S(2)}) collective-permute-start(bf16[32,1536]{1,0:T(8,128)(2,1)S(1)} %get-tuple-element.72), channel_id=1, source_target_pairs={{0,1},{1,0},{2,3},{3,2},{4,5},{5,4},{6,7},{7,6},{8,9},{9,8},{10,11... | collective-permute-start | bytes 294920 | tf_op jit(solution)/shard_map/ppermute | solution.py:346
  40.0 7.4 %collective-permute-start.15 = (bf16[16,1536]{1,0:T(8,128)(2,1)S(1)}, bf16[16,1536]{1,0:T(8,128)(2,1)S(1)}, u32[]{:S(2)}, u32[]{:S(2)}) collective-permute-start(bf16[16,1536]{1,0:T(8,128)(2,1)S(1)} %get-tuple-element.64), channel_id=1, source_target_pairs={{0,12},{4,8},{8,4},{12,0},{1,13},{5,9},{9,5},{13,1},{2,14},{6,10},... | collective-permute-start | bytes 147464 | tf_op jit(solution)/shard_map/ppermute | solution.py:346
  42.7 6.5 %collective-permute-start.16 = (bf16[16,1536]{1,0:T(8,128)(2,1)S(1)}, bf16[16,1536]{1,0:T(8,128)(2,1)S(1)}, u32[]{:S(2)}, u32[]{:S(2)}) collective-permute-start(bf16[16,1536]{1,0:T(8,128)(2,1)S(1)} %get-tuple-element.65), channel_id=1, source_target_pairs={{0,8},{4,12},{8,0},{12,4},{1,9},{5,13},{9,1},{13,5},{2,10},{6,14},... | collective-permute-start | bytes 147464 | tf_op jit(solution)/shard_map/ppermute | solution.py:346
  42.7 6.5 %collective-permute-start.17 = (bf16[16,1536]{1,0:T(8,128)(2,1)S(1)}, bf16[16,1536]{1,0:T(8,128)(2,1)S(1)}, u32[]{:S(2)}, u32[]{:S(2)}) collective-permute-start(bf16[16,1536]{1,0:T(8,128)(2,1)S(1)} %get-tuple-element.66), channel_id=1, source_target_pairs={{0,4},{4,0},{8,12},{12,8},{1,5},{5,1},{9,13},{13,9},{2,6},{6,2},{1... | collective-permute-start | bytes 147464 | tf_op jit(solution)/shard_map/ppermute | solution.py:346
  44.7 6.1 %collective-permute-start.21 = (bf16[16,1536]{1,0:T(8,128)(2,1)S(1)}, bf16[16,1536]{1,0:T(8,128)(2,1)S(1)}, u32[]{:S(2)}, u32[]{:S(2)}) collective-permute-start(bf16[16,1536]{1,0:T(8,128)(2,1)S(1)} %get-tuple-element.74), channel_id=1, source_target_pairs={{0,12},{4,8},{8,4},{12,0},{1,13},{5,9},{9,5},{13,1},{2,14},{6,10},... | collective-permute-start | bytes 147464 | tf_op jit(solution)/shard_map/ppermute | solution.py:346
  47.4 5.0 %collective-permute-start.22 = (bf16[16,1536]{1,0:T(8,128)(2,1)S(1)}, bf16[16,1536]{1,0:T(8,128)(2,1)S(1)}, u32[]{:S(2)}, u32[]{:S(2)}) collective-permute-start(bf16[16,1536]{1,0:T(8,128)(2,1)S(1)} %get-tuple-element.75), channel_id=1, source_target_pairs={{0,8},{4,12},{8,0},{12,4},{1,9},{5,13},{9,1},{13,5},{2,10},{6,14},... | collective-permute-start | bytes 147464 | tf_op jit(solution)/shard_map/ppermute | solution.py:346
  47.4 5.1 %collective-permute-start.23 = (bf16[16,1536]{1,0:T(8,128)(2,1)S(1)}, bf16[16,1536]{1,0:T(8,128)(2,1)S(1)}, u32[]{:S(2)}, u32[]{:S(2)}) collective-permute-start(bf16[16,1536]{1,0:T(8,128)(2,1)S(1)} %get-tuple-element.76), channel_id=1, source_target_pairs={{0,4},{4,0},{8,12},{12,8},{1,5},{5,1},{9,13},{13,9},{2,6},{6,2},{1... | collective-permute-start | bytes 147464 | tf_op jit(solution)/shard_map/ppermute | solution.py:346

commit v25 on v24

--- a/solution.py
+++ b/solution.py
@@ -16,7 +16,7 @@
 BLOCK = 8
 STRIPS = 3
 TILE = 256
-UNROLL = 8
+UNROLL = 6
 MIB = 1 << 20
 F32 = jnp.float32
 BF16 = jnp.bfloat16

time: 53.3 us -> 49.5 us (0.929)
  Pallas kernels: 16.4 us -> 12.7 us
  starting transfers between devices: 27.8 us -> 26.3 us
  waiting for transfers between devices: 8.65 us -> 10.1 us
    pallas_call x1, Pallas kernels: 5.54 us -> 3.45 us  [shards(): pl.pallas_call(functools.partial(middle_kernel, experts=experts), in_spec...]
    pallas_call x1, Pallas kernels: 4.59 us -> 2.92 us  [shards(): pl.pallas_call(functools.partial(begin_kernel, experts=experts), in_specs...]
    ppermute x24, waiting for transfers between devices: 8.65 us -> 10.1 us  [swap(): return lax.ppermute(value, axis, [(i, i ^ step) for i in range(count)])]
    ppermute x24, starting transfers between devices: 27.8 us -> 26.3 us  [swap(): return lax.ppermute(value, axis, [(i, i ^ step) for i in range(count)])]
  transfers between devices with their start and end apart: 24 -> 24, of which waited for: 7 -> 9; matrix products, arithmetic and copies ran while one was open for 0% -> 0% of each run, Pallas kernels for 14% -> 11%
where the time goes in v25:
time: 49.5 us; the launch traced here: 49.4 us
  starting transfers between devices  26.3 us (53%)
  Pallas kernels  12.7 us (26%)
  waiting for transfers between devices  10.1 us (20%)
    ppermute x24, starting transfers between devices, swap(): return lax.ppermute(value, axis, [(i, i ^ step) for i in range(count)])  26.3 us
    ppermute x24, waiting for transfers between devices, swap(): return lax.ppermute(value, axis, [(i, i ^ step) for i in range(count)])  10.1 us
    pallas_call x1, Pallas kernels, shards(): pl.pallas_call(functools.partial(middle_kernel, experts=experts), in_spec...  3.45 us
    pallas_call x1, Pallas kernels, shards(): pl.pallas_call(attend_kernel, in_specs=[SCALAR] + [ANY] * len(operands),...  2.95 us
    pallas_call x1, Pallas kernels, shards(): pl.pallas_call(functools.partial(begin_kernel, experts=experts), in_specs...  2.92 us
  transfers between devices with their start and end apart: 24, of which 9 were waited for; matrix products, arithmetic and copies ran while one was open for 0% of the time, Pallas kernels for 11%

profile of v25, /device:TPU:0, one launch (start us, length us, event | category | flops | bytes accessed | tf_op | source)
XLA Modules:
  0.0 49.4 jit_solution(135847999053159677)
XLA Ops:
  0.0 2.9 %shard_map.109 = (f32[16,3072]{1,0:T(8,128)S(1)}, bf16[16,1664]{1,0:T(8,128)(2,1)S(1)}, bf16[16,1536]{1,0:T(8,128)(2,1)S(1)}) custom-call(s32[1]{0:T(128)} %bitcast._.me_ref, s32[1,16]{1,0:T(1,128)} %bitcast.21, bf16[16,3072]{1,0:T(8,128)(2,1)} %queries_hbm.1, bf16[16,96,512]{2,1,0:T(8,128)(2,1)} %keys_hbm.1, bf16[16,96,512]{2,1,0:T(8,128)(2,1)} %values_hbm.1, ...), custom_call_target="tpu_custom_call" | custom-call | tf_op jit(solution)/shard_map/pallas_call | solution.py:390
  3.0 0.0 slice-start
  3.0 0.0 slice-start.3
  3.0 0.0 slice-start.1
  3.0 0.0 slice-start.2
  3.0 0.0 slice-start.4
  3.0 0.0 slice-start.5
  3.0 0.0 copy-start
  3.0 5.1 %collective-permute-start.2 = (bf16[16,1664]{1,0:T(8,128)(2,1)S(1)}, bf16[16,1664]{1,0:T(8,128)(2,1)S(1)}, u32[]{:S(2)}, u32[]{:S(2)}) collective-permute-start(bf16[16,1664]{1,0:T(8,128)(2,1)S(1)} %get-tuple-element.43.refs_0_), channel_id=1, source_target_pairs={{0,12},{4,8},{8,4},{12,0},{1,13},{5,9},{9,5},{13,1},{2,14},{6,10},... | collective-permute-start | bytes 159752 | tf_op jit(solution)/shard_map/ppermute | solution.py:346
  8.2 0.0 collective-permute-start.1
  8.2 0.6 %collective-permute-start = (bf16[16,1664]{1,0:T(8,128)(2,1)S(1)}, bf16[16,1664]{1,0:T(8,128)(2,1)S(1)}, u32[]{:S(2)}, u32[]{:S(2)}) collective-permute-start(bf16[16,1664]{1,0:T(8,128)(2,1)S(1)} %get-tuple-element.43.refs_0_), channel_id=1, source_target_pairs={{0,4},{4,0},{8,12},{12,8},{1,5},{5,1},{9,13},{13,9},{2,6},{6,2},{1... | collective-permute-start | bytes 159752 | tf_op jit(solution)/shard_map/ppermute | solution.py:346
  8.8 3.7 %collective-permute-start.5 = (bf16[16,1536]{1,0:T(8,128)(2,1)S(1)}, bf16[16,1536]{1,0:T(8,128)(2,1)S(1)}, u32[]{:S(2)}, u32[]{:S(2)}) collective-permute-start(bf16[16,1536]{1,0:T(8,128)(2,1)S(1)} %get-tuple-element.44.refs_4_), channel_id=1, source_target_pairs={{0,12},{4,8},{8,4},{12,0},{1,13},{5,9},{9,5},{13,1},{2,14},{6,10},... | collective-permute-start | bytes 147464 | tf_op jit(solution)/shard_map/ppermute | solution.py:346
  12.5 0.0 collective-permute-start.4
  12.5 0.0 collective-permute-done.2.refs_3_
  12.6 0.6 %collective-permute-start.3 = (bf16[16,1536]{1,0:T(8,128)(2,1)S(1)}, bf16[16,1536]{1,0:T(8,128)(2,1)S(1)}, u32[]{:S(2)}, u32[]{:S(2)}) collective-permute-start(bf16[16,1536]{1,0:T(8,128)(2,1)S(1)} %get-tuple-element.44.refs_4_), channel_id=1, source_target_pairs={{0,4},{4,0},{8,12},{12,8},{1,5},{5,1},{9,13},{13,9},{2,6},{6,2},{1... | collective-permute-start | bytes 147464 | tf_op jit(solution)/shard_map/ppermute | solution.py:346
  13.2 1.4 %collective-permute-done.1.refs_2_ = bf16[16,1664]{1,0:T(8,128)(2,1)S(1)} collective-permute-done((bf16[16,1664]{1,0:T(8,128)(2,1)S(1)}, bf16[16,1664]{1,0:T(8,128)(2,1)S(1)}, u32[]{:S(2)}, u32[]{:S(2)}) %collective-permute-start.1) | collective-permute-done | bytes 53280 | tf_op jit(solution)/shard_map/ppermute | solution.py:346
  14.6 0.0 collective-permute-done.refs_1_
  14.6 0.4 shard_map.113
  15.0 1.6 %collective-permute-start.9 = (bf16[32,1536]{1,0:T(8,128)(2,1)S(1)}, bf16[32,1536]{1,0:T(8,128)(2,1)S(1)}, u32[]{:S(2)}, u32[]{:S(2)}) collective-permute-start(bf16[32,1536]{1,0:T(8,128)(2,1)S(1)} %get-tuple-element.52), channel_id=1, source_target_pairs={{0,2},{1,3},{2,0},{3,1},{4,6},{5,7},{6,4},{7,5},{8,10},{9,11},{10,... | collective-permute-start | bytes 294920 | tf_op jit(solution)/shard_map/ppermute | solution.py:346
  16.6 0.0 collective-permute-start.10
  16.6 0.0 collective-permute-done.5.refs_7_
  16.6 0.6 %collective-permute-start.11 = (bf16[32,1536]{1,0:T(8,128)(2,1)S(1)}, bf16[32,1536]{1,0:T(8,128)(2,1)S(1)}, u32[]{:S(2)}, u32[]{:S(2)}) collective-permute-start(bf16[32,1536]{1,0:T(8,128)(2,1)S(1)} %get-tuple-element.54), channel_id=1, source_target_pairs={{0,1},{1,0},{2,3},{3,2},{4,5},{5,4},{6,7},{7,6},{8,9},{9,8},{10,11... | collective-permute-start | bytes 294920 | tf_op jit(solution)/shard_map/ppermute | solution.py:346
  17.2 0.3 collective-permute-done.4.refs_6_
  17.5 0.0 collective-permute-done.3.refs_5_
  17.5 0.4 shard_map.112
  17.9 1.6 %collective-permute-start.6 = (bf16[32,1536]{1,0:T(8,128)(2,1)S(1)}, bf16[32,1536]{1,0:T(8,128)(2,1)S(1)}, u32[]{:S(2)}, u32[]{:S(2)}) collective-permute-start(bf16[32,1536]{1,0:T(8,128)(2,1)S(1)} %get-tuple-element.48), channel_id=1, source_target_pairs={{0,2},{1,3},{2,0},{3,1},{4,6},{5,7},{6,4},{7,5},{8,10},{9,11},{10,... | collective-permute-start | bytes 294920 | tf_op jit(solution)/shard_map/ppermute | solution.py:346
  19.5 0.0 collective-permute-start.7
  19.5 0.4 shard_map.111
  19.9 0.0 collective-permute-done.9.refs_1_
  19.9 0.7 %collective-permute-start.8 = (bf16[32,1536]{1,0:T(8,128)(2,1)S(1)}, bf16[32,1536]{1,0:T(8,128)(2,1)S(1)}, u32[]{:S(2)}, u32[]{:S(2)}) collective-permute-start(bf16[32,1536]{1,0:T(8,128)(2,1)S(1)} %get-tuple-element.50), channel_id=1, source_target_pairs={{0,1},{1,0},{2,3},{3,2},{4,5},{5,4},{6,7},{7,6},{8,9},{9,8},{10,11... | collective-permute-start | bytes 294920 | tf_op jit(solution)/shard_map/ppermute | solution.py:346
  20.6 1.3 %collective-permute-done.10.refs_2_ = bf16[32,1536]{1,0:T(8,128)(2,1)S(1)} collective-permute-done((bf16[32,1536]{1,0:T(8,128)(2,1)S(1)}, bf16[32,1536]{1,0:T(8,128)(2,1)S(1)}, u32[]{:S(2)}, u32[]{:S(2)}) %collective-permute-start.10) | collective-permute-done | bytes 98336 | tf_op jit(solution)/shard_map/ppermute | solution.py:346
  21.9 0.0 collective-permute-done.11.refs_3_
  21.9 2.9 %shard_map.114 = (f32[128,2048]{1,0:T(8,128)S(1)}, f32[128,2048]{1,0:T(8,128)S(1)}, bf16[2048,1536]{1,0:T(8,128)(2,1)S(1)}) custom-call(bf16[32,1536]{1,0:T(8,128)(2,1)S(1)} %get-tuple-element.51.refs_0_, bf16[32,1536]{1,0:T(8,128)(2,1)S(1)} %collective-permute-done.9.refs_1_, bf16[32,1536]{1,0:T(8,128)(2,1)S(1)} %collective-permute-done.10.refs_2_, ...), custom_call_target="tpu_custom_call" | custom-call | flops 1610612736 | tf_op jit(solution)/shard_map/pallas_call | solution.py:433
  24.8 0.0 collective-permute-done.6.refs_1_
  24.9 1.0 %collective-permute-done.7.refs_2_ = bf16[32,1536]{1,0:T(8,128)(2,1)S(1)} collective-permute-done((bf16[32,1536]{1,0:T(8,128)(2,1)S(1)}, bf16[32,1536]{1,0:T(8,128)(2,1)S(1)}, u32[]{:S(2)}, u32[]{:S(2)}) %collective-permute-start.7) | collective-permute-done | bytes 98336 | tf_op jit(solution)/shard_map/ppermute | solution.py:346
  25.9 0.0 collective-permute-done.8.refs_3_
  25.9 3.5 %shard_map.115 = (bf16[32,1536]{1,0:T(8,128)(2,1)S(1)}, bf16[32,1536]{1,0:T(8,128)(2,1)S(1)}, bf16[32,1536]{1,0:T(8,128)(2,1)S(1)}, bf16[32,1536]{1,0:T(8,128)(2...) custom-call(bf16[32,1536]{1,0:T(8,128)(2,1)S(1)} %get-tuple-element.47.refs_0_, ...), custom_call_target="tpu_custom_call" | custom-call | tf_op jit(solution)/shard_map/pallas_call | solution.py:444
  29.3 0.6 %collective-permute-start.12 = (bf16[32,1536]{1,0:T(8,128)(2,1)S(1)}, bf16[32,1536]{1,0:T(8,128)(2,1)S(1)}, u32[]{:S(2)}, u32[]{:S(2)}) collective-permute-start(bf16[32,1536]{1,0:T(8,128)(2,1)S(1)} %get-tuple-element.59), channel_id=1, source_target_pairs={{0,2},{1,3},{2,0},{3,1},{4,6},{5,7},{6,4},{7,5},{8,10},{9,11},{10,... | collective-permute-start | bytes 294920 | tf_op jit(solution)/shard_map/ppermute | solution.py:346
  29.9 0.9 %collective-permute-start.13 = (bf16[32,1536]{1,0:T(8,128)(2,1)S(1)}, bf16[32,1536]{1,0:T(8,128)(2,1)S(1)}, u32[]{:S(2)}, u32[]{:S(2)}) collective-permute-start(bf16[32,1536]{1,0:T(8,128)(2,1)S(1)} %get-tuple-element.60), channel_id=1, source_target_pairs={{0,3},{1,2},{2,1},{3,0},{4,7},{5,6},{6,5},{7,4},{8,11},{9,10},{10,... | collective-permute-start | bytes 294920 | tf_op jit(solution)/shard_map/ppermute | solution.py:346
  30.9 0.7 %collective-permute-start.14 = (bf16[32,1536]{1,0:T(8,128)(2,1)S(1)}, bf16[32,1536]{1,0:T(8,128)(2,1)S(1)}, u32[]{:S(2)}, u32[]{:S(2)}) collective-permute-start(bf16[32,1536]{1,0:T(8,128)(2,1)S(1)} %get-tuple-element.61), channel_id=1, source_target_pairs={{0,1},{1,0},{2,3},{3,2},{4,5},{5,4},{6,7},{7,6},{8,9},{9,8},{10,11... | collective-permute-start | bytes 294920 | tf_op jit(solution)/shard_map/ppermute | solution.py:346
  31.5 1.0 %shard_map.118 = (bf16[32,1536]{1,0:T(8,128)(2,1)S(1)}, bf16[32,1536]{1,0:T(8,128)(2,1)S(1)}, bf16[32,1536]{1,0:T(8,128)(2,1)S(1)}, bf16[32,1536]{1,0:T(8,128)(2,1)S(1)}) custom-call(bf16[128,2048]{1,0:T(8,128)(2,1)S(1)} %get-tuple-element.67.hidden_ref, bf16[2048,1536]{1,0:T(8,128)(2,1)S(1)} %get-tuple-element.68.down_ref), custom_call_target="tpu_custom_call" | custom-call | flops 805306368 | tf_op jit(solution)/shard_map/pallas_call | solution.py:452
  32.5 0.9 %collective-permute-start.18 = (bf16[32,1536]{1,0:T(8,128)(2,1)S(1)}, bf16[32,1536]{1,0:T(8,128)(2,1)S(1)}, u32[]{:S(2)}, u32[]{:S(2)}) collective-permute-start(bf16[32,1536]{1,0:T(8,128)(2,1)S(1)} %get-tuple-element.70), channel_id=1, source_target_pairs={{0,2},{1,3},{2,0},{3,1},{4,6},{5,7},{6,4},{7,5},{8,10},{9,11},{10,... | collective-permute-start | bytes 294920 | tf_op jit(solution)/shard_map/ppermute | solution.py:346
  33.4 0.5 %collective-permute-start.19 = (bf16[32,1536]{1,0:T(8,128)(2,1)S(1)}, bf16[32,1536]{1,0:T(8,128)(2,1)S(1)}, u32[]{:S(2)}, u32[]{:S(2)}) collective-permute-start(bf16[32,1536]{1,0:T(8,128)(2,1)S(1)} %get-tuple-element.71), channel_id=1, source_target_pairs={{0,3},{1,2},{2,1},{3,0},{4,7},{5,6},{6,5},{7,4},{8,11},{9,10},{10,... | collective-permute-start | bytes 294920 | tf_op jit(solution)/shard_map/ppermute | solution.py:346
  33.9 1.1 %collective-permute-done.12.refs_1_ = bf16[32,1536]{1,0:T(8,128)(2,1)S(1)} collective-permute-done((bf16[32,1536]{1,0:T(8,128)(2,1)S(1)}, bf16[32,1536]{1,0:T(8,128)(2,1)S(1)}, u32[]{:S(2)}, u32[]{:S(2)}) %collective-permute-start.12) | collective-permute-done | bytes 98336 | tf_op jit(solution)/shard_map/ppermute | solution.py:346
  35.0 0.0 collective-permute-start.20
  35.0 0.5 collective-permute-done.13.refs_2_
  35.5 0.0 collective-permute-done.14.refs_3_
  35.5 0.3 shard_map.116
  35.7 2.7 %collective-permute-start.15 = (bf16[16,1536]{1,0:T(8,128)(2,1)S(1)}, bf16[16,1536]{1,0:T(8,128)(2,1)S(1)}, u32[]{:S(2)}, u32[]{:S(2)}) collective-permute-start(bf16[16,1536]{1,0:T(8,128)(2,1)S(1)} %get-tuple-element.64), channel_id=1, source_target_pairs={{0,12},{4,8},{8,4},{12,0},{1,13},{5,9},{9,5},{13,1},{2,14},{6,10},... | collective-permute-start | bytes 147464 | tf_op jit(solution)/shard_map/ppermute | solution.py:346
  38.4 0.0 collective-permute-start.16
  38.4 0.8 %collective-permute-done.18.refs_1_ = bf16[32,1536]{1,0:T(8,128)(2,1)S(1)} collective-permute-done((bf16[32,1536]{1,0:T(8,128)(2,1)S(1)}, bf16[32,1536]{1,0:T(8,128)(2,1)S(1)}, u32[]{:S(2)}, u32[]{:S(2)}) %collective-permute-start.18) | collective-permute-done | bytes 98336 | tf_op jit(solution)/shard_map/ppermute | solution.py:346
  39.2 1.0 %collective-permute-start.17 = (bf16[16,1536]{1,0:T(8,128)(2,1)S(1)}, bf16[16,1536]{1,0:T(8,128)(2,1)S(1)}, u32[]{:S(2)}, u32[]{:S(2)}) collective-permute-start(bf16[16,1536]{1,0:T(8,128)(2,1)S(1)} %get-tuple-element.66), channel_id=1, source_target_pairs={{0,4},{4,0},{8,12},{12,8},{1,5},{5,1},{9,13},{13,9},{2,6},{6,2},{1... | collective-permute-start | bytes 147464 | tf_op jit(solution)/shard_map/ppermute | solution.py:346
  40.2 0.0 collective-permute-done.19.refs_2_
  40.2 0.0 collective-permute-done.20.refs_3_
  40.2 0.3 shard_map.119
  40.5 2.7 %collective-permute-start.21 = (bf16[16,1536]{1,0:T(8,128)(2,1)S(1)}, bf16[16,1536]{1,0:T(8,128)(2,1)S(1)}, u32[]{:S(2)}, u32[]{:S(2)}) collective-permute-start(bf16[16,1536]{1,0:T(8,128)(2,1)S(1)} %get-tuple-element.74), channel_id=1, source_target_pairs={{0,12},{4,8},{8,4},{12,0},{1,13},{5,9},{9,5},{13,1},{2,14},{6,10},... | collective-permute-start | bytes 147464 | tf_op jit(solution)/shard_map/ppermute | solution.py:346
  43.2 0.0 collective-permute-start.22
  43.2 0.0 collective-permute-done.15.refs_1_
  43.2 1.8 %collective-permute-start.23 = (bf16[16,1536]{1,0:T(8,128)(2,1)S(1)}, bf16[16,1536]{1,0:T(8,128)(2,1)S(1)}, u32[]{:S(2)}, u32[]{:S(2)}) collective-permute-start(bf16[16,1536]{1,0:T(8,128)(2,1)S(1)} %get-tuple-element.76), channel_id=1, source_target_pairs={{0,4},{4,0},{8,12},{12,8},{1,5},{5,1},{9,13},{13,9},{2,6},{6,2},{1... | collective-permute-start | bytes 147464 | tf_op jit(solution)/shard_map/ppermute | solution.py:346
  44.9 0.0 collective-permute-done.16.refs_2_
  44.9 0.0 collective-permute-done.17.refs_3_
  45.0 2.0 %collective-permute-done.21.refs_2_ = bf16[16,1536]{1,0:T(8,128)(2,1)S(1)} collective-permute-done((bf16[16,1536]{1,0:T(8,128)(2,1)S(1)}, bf16[16,1536]{1,0:T(8,128)(2,1)S(1)}, u32[]{:S(2)}, u32[]{:S(2)}) %collective-permute-start.21) | collective-permute-done | bytes 49184 | tf_op jit(solution)/shard_map/ppermute | solution.py:346
  47.0 1.8 %collective-permute-done.22.refs_3_ = bf16[16,1536]{1,0:T(8,128)(2,1)S(1)} collective-permute-done((bf16[16,1536]{1,0:T(8,128)(2,1)S(1)}, bf16[16,1536]{1,0:T(8,128)(2,1)S(1)}, u32[]{:S(2)}, u32[]{:S(2)}) %collective-permute-start.22) | collective-permute-done | bytes 49184 | tf_op jit(solution)/shard_map/ppermute | solution.py:346
  48.7 0.7 %shard_map.120 = bf16[16,3072]{1,0:T(8,128)(2,1)} custom-call(bf16[16,1536]{1,0:T(8,128)(2,1)S(1)} %shard_map.117.refs_0_, f32[16,1536]{1,0:T(8,128)S(1)} %get-tuple-element.73.refs_1_, bf16[16,1536]{1,0:T(8,128)(2,1)S(1)} %collective-permute-done.21.refs_2_, bf16[16,1536]{1,0:T(8,128)(2,1)S(1)} %collective-permute-done.22.refs_3_, ...), custom_call_target="tpu_custom_call" | custom-call | tf_op jit(solution)/shard_map/pallas_call | solution.py:476
  (12 shorter events, 0.0 us)
Async XLA Ops:
  3.0 18.9 %slice-start = ((s8[12582912]{0:T(1024)(128)(4,1)}), s8[4194304]{0:T(1024)(128)(4,1)S(1)}, s32[]{:S(2)}) async-start(s8[12582912]{0:T(1024)(128)(4,1)} %bitcast.8), calls=%async_computation | async-start | bytes 8388608
  3.0 18.9 %slice-start.3 = ((s8[12582912]{0:T(1024)(128)(4,1)}), s8[4194304]{0:T(1024)(128)(4,1)S(1)}, s32[]{:S(2)}) async-start(s8[12582912]{0:T(1024)(128)(4,1)} %bitcast.12), calls=%async_computation.3 | async-start | bytes 8388608
  3.0 18.9 %slice-start.1 = ((s8[12582912]{0:T(1024)(128)(4,1)}), s8[4194304]{0:T(1024)(128)(4,1)S(1)}, s32[]{:S(2)}) async-start(s8[12582912]{0:T(1024)(128)(4,1)} %bitcast.8), calls=%async_computation.1 | async-start | bytes 8388608
  3.0 18.9 %slice-start.2 = ((s8[12582912]{0:T(1024)(128)(4,1)}), s8[4194304]{0:T(1024)(128)(4,1)S(1)}, s32[]{:S(2)}) async-start(s8[12582912]{0:T(1024)(128)(4,1)} %bitcast.8), calls=%async_computation.2 | async-start | bytes 8388608
  3.0 18.9 %slice-start.4 = ((s8[12582912]{0:T(1024)(128)(4,1)}), s8[4194304]{0:T(1024)(128)(4,1)S(1)}, s32[]{:S(2)}) async-start(s8[12582912]{0:T(1024)(128)(4,1)} %bitcast.12), calls=%async_computation.4 | async-start | bytes 8388608
  3.0 18.9 %slice-start.5 = ((s8[12582912]{0:T(1024)(128)(4,1)}), s8[4194304]{0:T(1024)(128)(4,1)S(1)}, s32[]{:S(2)}) async-start(s8[12582912]{0:T(1024)(128)(4,1)} %bitcast.12), calls=%async_computation.5 | async-start | bytes 8388608
  3.0 16.5 %copy-start = (bf16[3072,4]{0,1:T(4,128)(2,1)S(1)}, bf16[3072,4]{0,1:T(4,128)(2,1)}, u32[]{:S(2)}) copy-start(bf16[3072,4]{0,1:T(4,128)(2,1)} %param.18) | copy-start | bytes 73732
  3.0 9.5 %collective-permute-start.2 = (bf16[16,1664]{1,0:T(8,128)(2,1)S(1)}, bf16[16,1664]{1,0:T(8,128)(2,1)S(1)}, u32[]{:S(2)}, u32[]{:S(2)}) collective-permute-start(bf16[16,1664]{1,0:T(8,128)(2,1)S(1)} %get-tuple-element.43.refs_0_), channel_id=1, source_target_pairs={{0,12},{4,8},{8,4},{12,0},{1,13},{5,9},{9,5},{13,1},{2,14},{6,10},... | collective-permute-start | bytes 159752 | tf_op jit(solution)/shard_map/ppermute | solution.py:346
  8.2 6.4 %collective-permute-start.1 = (bf16[16,1664]{1,0:T(8,128)(2,1)S(1)}, bf16[16,1664]{1,0:T(8,128)(2,1)S(1)}, u32[]{:S(2)}, u32[]{:S(2)}) collective-permute-start(bf16[16,1664]{1,0:T(8,128)(2,1)S(1)} %get-tuple-element.43.refs_0_), channel_id=1, source_target_pairs={{0,8},{4,12},{8,0},{12,4},{1,9},{5,13},{9,1},{13,5},{2,10},{6,14},... | collective-permute-start | bytes 159752 | tf_op jit(solution)/shard_map/ppermute | solution.py:346
  8.2 6.4 %collective-permute-start = (bf16[16,1664]{1,0:T(8,128)(2,1)S(1)}, bf16[16,1664]{1,0:T(8,128)(2,1)S(1)}, u32[]{:S(2)}, u32[]{:S(2)}) collective-permute-start(bf16[16,1664]{1,0:T(8,128)(2,1)S(1)} %get-tuple-element.43.refs_0_), channel_id=1, source_target_pairs={{0,4},{4,0},{8,12},{12,8},{1,5},{5,1},{9,13},{13,9},{2,6},{6,2},{1... | collective-permute-start | bytes 159752 | tf_op jit(solution)/shard_map/ppermute | solution.py:346
  8.8 7.8 %collective-permute-start.5 = (bf16[16,1536]{1,0:T(8,128)(2,1)S(1)}, bf16[16,1536]{1,0:T(8,128)(2,1)S(1)}, u32[]{:S(2)}, u32[]{:S(2)}) collective-permute-start(bf16[16,1536]{1,0:T(8,128)(2,1)S(1)} %get-tuple-element.44.refs_4_), channel_id=1, source_target_pairs={{0,12},{4,8},{8,4},{12,0},{1,13},{5,9},{9,5},{13,1},{2,14},{6,10},... | collective-permute-start | bytes 147464 | tf_op jit(solution)/shard_map/ppermute | solution.py:346
  12.5 5.0 %collective-permute-start.4 = (bf16[16,1536]{1,0:T(8,128)(2,1)S(1)}, bf16[16,1536]{1,0:T(8,128)(2,1)S(1)}, u32[]{:S(2)}, u32[]{:S(2)}) collective-permute-start(bf16[16,1536]{1,0:T(8,128)(2,1)S(1)} %get-tuple-element.44.refs_4_), channel_id=1, source_target_pairs={{0,8},{4,12},{8,0},{12,4},{1,9},{5,13},{9,1},{13,5},{2,10},{6,14},... | collective-permute-start | bytes 147464 | tf_op jit(solution)/shard_map/ppermute | solution.py:346
  12.6 5.0 %collective-permute-start.3 = (bf16[16,1536]{1,0:T(8,128)(2,1)S(1)}, bf16[16,1536]{1,0:T(8,128)(2,1)S(1)}, u32[]{:S(2)}, u32[]{:S(2)}) collective-permute-start(bf16[16,1536]{1,0:T(8,128)(2,1)S(1)} %get-tuple-element.44.refs_4_), channel_id=1, source_target_pairs={{0,4},{4,0},{8,12},{12,8},{1,5},{5,1},{9,13},{13,9},{2,6},{6,2},{1... | collective-permute-start | bytes 147464 | tf_op jit(solution)/shard_map/ppermute | solution.py:346
  15.0 4.9 %collective-permute-start.9 = (bf16[32,1536]{1,0:T(8,128)(2,1)S(1)}, bf16[32,1536]{1,0:T(8,128)(2,1)S(1)}, u32[]{:S(2)}, u32[]{:S(2)}) collective-permute-start(bf16[32,1536]{1,0:T(8,128)(2,1)S(1)} %get-tuple-element.52), channel_id=1, source_target_pairs={{0,2},{1,3},{2,0},{3,1},{4,6},{5,7},{6,4},{7,5},{8,10},{9,11},{10,... | collective-permute-start | bytes 294920 | tf_op jit(solution)/shard_map/ppermute | solution.py:346
  16.6 5.3 %collective-permute-start.10 = (bf16[32,1536]{1,0:T(8,128)(2,1)S(1)}, bf16[32,1536]{1,0:T(8,128)(2,1)S(1)}, u32[]{:S(2)}, u32[]{:S(2)}) collective-permute-start(bf16[32,1536]{1,0:T(8,128)(2,1)S(1)} %get-tuple-element.53), channel_id=1, source_target_pairs={{0,3},{1,2},{2,1},{3,0},{4,7},{5,6},{6,5},{7,4},{8,11},{9,10},{10,... | collective-permute-start | bytes 294920 | tf_op jit(solution)/shard_map/ppermute | solution.py:346
  16.6 5.3 %collective-permute-start.11 = (bf16[32,1536]{1,0:T(8,128)(2,1)S(1)}, bf16[32,1536]{1,0:T(8,128)(2,1)S(1)}, u32[]{:S(2)}, u32[]{:S(2)}) collective-permute-start(bf16[32,1536]{1,0:T(8,128)(2,1)S(1)} %get-tuple-element.54), channel_id=1, source_target_pairs={{0,1},{1,0},{2,3},{3,2},{4,5},{5,4},{6,7},{7,6},{8,9},{9,8},{10,11... | collective-permute-start | bytes 294920 | tf_op jit(solution)/shard_map/ppermute | solution.py:346
  17.9 6.9 %collective-permute-start.6 = (bf16[32,1536]{1,0:T(8,128)(2,1)S(1)}, bf16[32,1536]{1,0:T(8,128)(2,1)S(1)}, u32[]{:S(2)}, u32[]{:S(2)}) collective-permute-start(bf16[32,1536]{1,0:T(8,128)(2,1)S(1)} %get-tuple-element.48), channel_id=1, source_target_pairs={{0,2},{1,3},{2,0},{3,1},{4,6},{5,7},{6,4},{7,5},{8,10},{9,11},{10,... | collective-permute-start | bytes 294920 | tf_op jit(solution)/shard_map/ppermute | solution.py:346
  19.5 6.3 %collective-permute-start.7 = (bf16[32,1536]{1,0:T(8,128)(2,1)S(1)}, bf16[32,1536]{1,0:T(8,128)(2,1)S(1)}, u32[]{:S(2)}, u32[]{:S(2)}) collective-permute-start(bf16[32,1536]{1,0:T(8,128)(2,1)S(1)} %get-tuple-element.49), channel_id=1, source_target_pairs={{0,3},{1,2},{2,1},{3,0},{4,7},{5,6},{6,5},{7,4},{8,11},{9,10},{10,... | collective-permute-start | bytes 294920 | tf_op jit(solution)/shard_map/ppermute | solution.py:346
  19.9 6.0 %collective-permute-start.8 = (bf16[32,1536]{1,0:T(8,128)(2,1)S(1)}, bf16[32,1536]{1,0:T(8,128)(2,1)S(1)}, u32[]{:S(2)}, u32[]{:S(2)}) collective-permute-start(bf16[32,1536]{1,0:T(8,128)(2,1)S(1)} %get-tuple-element.50), channel_id=1, source_target_pairs={{0,1},{1,0},{2,3},{3,2},{4,5},{5,4},{6,7},{7,6},{8,9},{9,8},{10,11... | collective-permute-start | bytes 294920 | tf_op jit(solution)/shard_map/ppermute | solution.py:346
  29.3 5.7 %collective-permute-start.12 = (bf16[32,1536]{1,0:T(8,128)(2,1)S(1)}, bf16[32,1536]{1,0:T(8,128)(2,1)S(1)}, u32[]{:S(2)}, u32[]{:S(2)}) collective-permute-start(bf16[32,1536]{1,0:T(8,128)(2,1)S(1)} %get-tuple-element.59), channel_id=1, source_target_pairs={{0,2},{1,3},{2,0},{3,1},{4,6},{5,7},{6,4},{7,5},{8,10},{9,11},{10,... | collective-permute-start | bytes 294920 | tf_op jit(solution)/shard_map/ppermute | solution.py:346
  29.9 5.6 %collective-permute-start.13 = (bf16[32,1536]{1,0:T(8,128)(2,1)S(1)}, bf16[32,1536]{1,0:T(8,128)(2,1)S(1)}, u32[]{:S(2)}, u32[]{:S(2)}) collective-permute-start(bf16[32,1536]{1,0:T(8,128)(2,1)S(1)} %get-tuple-element.60), channel_id=1, source_target_pairs={{0,3},{1,2},{2,1},{3,0},{4,7},{5,6},{6,5},{7,4},{8,11},{9,10},{10,... | collective-permute-start | bytes 294920 | tf_op jit(solution)/shard_map/ppermute | solution.py:346
  30.9 4.6 %collective-permute-start.14 = (bf16[32,1536]{1,0:T(8,128)(2,1)S(1)}, bf16[32,1536]{1,0:T(8,128)(2,1)S(1)}, u32[]{:S(2)}, u32[]{:S(2)}) collective-permute-start(bf16[32,1536]{1,0:T(8,128)(2,1)S(1)} %get-tuple-element.61), channel_id=1, source_target_pairs={{0,1},{1,0},{2,3},{3,2},{4,5},{5,4},{6,7},{7,6},{8,9},{9,8},{10,11... | collective-permute-start | bytes 294920 | tf_op jit(solution)/shard_map/ppermute | solution.py:346
  32.5 6.7 %collective-permute-start.18 = (bf16[32,1536]{1,0:T(8,128)(2,1)S(1)}, bf16[32,1536]{1,0:T(8,128)(2,1)S(1)}, u32[]{:S(2)}, u32[]{:S(2)}) collective-permute-start(bf16[32,1536]{1,0:T(8,128)(2,1)S(1)} %get-tuple-element.70), channel_id=1, source_target_pairs={{0,2},{1,3},{2,0},{3,1},{4,6},{5,7},{6,4},{7,5},{8,10},{9,11},{10,... | collective-permute-start | bytes 294920 | tf_op jit(solution)/shard_map/ppermute | solution.py:346
  33.4 6.8 %collective-permute-start.19 = (bf16[32,1536]{1,0:T(8,128)(2,1)S(1)}, bf16[32,1536]{1,0:T(8,128)(2,1)S(1)}, u32[]{:S(2)}, u32[]{:S(2)}) collective-permute-start(bf16[32,1536]{1,0:T(8,128)(2,1)S(1)} %get-tuple-element.71), channel_id=1, source_target_pairs={{0,3},{1,2},{2,1},{3,0},{4,7},{5,6},{6,5},{7,4},{8,11},{9,10},{10,... | collective-permute-start | bytes 294920 | tf_op jit(solution)/shard_map/ppermute | solution.py:346
  35.0 5.2 %collective-permute-start.20 = (bf16[32,1536]{1,0:T(8,128)(2,1)S(1)}, bf16[32,1536]{1,0:T(8,128)(2,1)S(1)}, u32[]{:S(2)}, u32[]{:S(2)}) collective-permute-start(bf16[32,1536]{1,0:T(8,128)(2,1)S(1)} %get-tuple-element.72), channel_id=1, source_target_pairs={{0,1},{1,0},{2,3},{3,2},{4,5},{5,4},{6,7},{7,6},{8,9},{9,8},{10,11... | collective-permute-start | bytes 294920 | tf_op jit(solution)/shard_map/ppermute | solution.py:346
  35.7 7.4 %collective-permute-start.15 = (bf16[16,1536]{1,0:T(8,128)(2,1)S(1)}, bf16[16,1536]{1,0:T(8,128)(2,1)S(1)}, u32[]{:S(2)}, u32[]{:S(2)}) collective-permute-start(bf16[16,1536]{1,0:T(8,128)(2,1)S(1)} %get-tuple-element.64), channel_id=1, source_target_pairs={{0,12},{4,8},{8,4},{12,0},{1,13},{5,9},{9,5},{13,1},{2,14},{6,10},... | collective-permute-start | bytes 147464 | tf_op jit(solution)/shard_map/ppermute | solution.py:346
  38.4 6.5 %collective-permute-start.16 = (bf16[16,1536]{1,0:T(8,128)(2,1)S(1)}, bf16[16,1536]{1,0:T(8,128)(2,1)S(1)}, u32[]{:S(2)}, u32[]{:S(2)}) collective-permute-start(bf16[16,1536]{1,0:T(8,128)(2,1)S(1)} %get-tuple-element.65), channel_id=1, source_target_pairs={{0,8},{4,12},{8,0},{12,4},{1,9},{5,13},{9,1},{13,5},{2,10},{6,14},... | collective-permute-start | bytes 147464 | tf_op jit(solution)/shard_map/ppermute | solution.py:346
  39.2 5.7 %collective-permute-start.17 = (bf16[16,1536]{1,0:T(8,128)(2,1)S(1)}, bf16[16,1536]{1,0:T(8,128)(2,1)S(1)}, u32[]{:S(2)}, u32[]{:S(2)}) collective-permute-start(bf16[16,1536]{1,0:T(8,128)(2,1)S(1)} %get-tuple-element.66), channel_id=1, source_target_pairs={{0,4},{4,0},{8,12},{12,8},{1,5},{5,1},{9,13},{13,9},{2,6},{6,2},{1... | collective-permute-start | bytes 147464 | tf_op jit(solution)/shard_map/ppermute | solution.py:346
  40.5 6.5 %collective-permute-start.21 = (bf16[16,1536]{1,0:T(8,128)(2,1)S(1)}, bf16[16,1536]{1,0:T(8,128)(2,1)S(1)}, u32[]{:S(2)}, u32[]{:S(2)}) collective-permute-start(bf16[16,1536]{1,0:T(8,128)(2,1)S(1)} %get-tuple-element.74), channel_id=1, source_target_pairs={{0,12},{4,8},{8,4},{12,0},{1,13},{5,9},{9,5},{13,1},{2,14},{6,10},... | collective-permute-start | bytes 147464 | tf_op jit(solution)/shard_map/ppermute | solution.py:346
  43.2 5.6 %collective-permute-start.22 = (bf16[16,1536]{1,0:T(8,128)(2,1)S(1)}, bf16[16,1536]{1,0:T(8,128)(2,1)S(1)}, u32[]{:S(2)}, u32[]{:S(2)}) collective-permute-start(bf16[16,1536]{1,0:T(8,128)(2,1)S(1)} %get-tuple-element.75), channel_id=1, source_target_pairs={{0,8},{4,12},{8,0},{12,4},{1,9},{5,13},{9,1},{13,5},{2,10},{6,14},... | collective-permute-start | bytes 147464 | tf_op jit(solution)/shard_map/ppermute | solution.py:346
  43.2 5.5 %collective-permute-start.23 = (bf16[16,1536]{1,0:T(8,128)(2,1)S(1)}, bf16[16,1536]{1,0:T(8,128)(2,1)S(1)}, u32[]{:S(2)}, u32[]{:S(2)}) collective-permute-start(bf16[16,1536]{1,0:T(8,128)(2,1)S(1)} %get-tuple-element.76), channel_id=1, source_target_pairs={{0,4},{4,0},{8,12},{12,8},{1,5},{5,1},{9,13},{13,9},{2,6},{6,2},{1... | collective-permute-start | bytes 147464 | tf_op jit(solution)/shard_map/ppermute | solution.py:346
